TPU v7x, 32 devices: a whole 2x2x4 slice. The times are simulated.
32 devices in a mesh: expert: 16 (over z, y, x), tensor: 2 (over core).
Axes of the slice: x: 2, y: 2, z: 4, core: 2. Of those that a mesh axis runs over, the one named last changes fastest.
Arguments:
- attn_out: bfloat16 [512, 4096], P('expert', 'tensor'), may hold values from -6 to 6
- out_weight: bfloat16 [4096, 2048], P('tensor'), may hold values from -0.09375 to 0.09375
- residual: bfloat16 [512, 2048], P(('expert', 'tensor')), may hold values from -6 to 6
- attn_gain: float32 [2048], replicated, may hold values from 0.1 to 1.9
- expert_ids: int32 [512, 8], P('expert'), may hold values from 0 to 31, all different within a row; in each aligned block of 32 rows (0 to 31, 32 to 63, ...) at most 12 rows name the same one
- route_weights: float32 [512, 8], P('expert'), may hold values from 0.05 to 0.3
- w_gate: bfloat16 [16, 2048, 1536], P('expert', None, 'tensor'), may hold values from -0.125 to 0.125
- w_up: bfloat16 [16, 2048, 1536], P('expert', None, 'tensor'), may hold values from -0.125 to 0.125
- w_down: bfloat16 [16, 1536, 2048], P('expert', 'tensor'), may hold values from -0.21875 to 0.21875
- input_gain: float32 [2048], replicated, may hold values from 0.1 to 1.9
- q_weight: bfloat16 [2048, 4096], P('expert', 'tensor'), may hold values from -0.125 to 0.125
- kv_weight: bfloat16 [2048, 1024], P('expert', 'tensor'), may hold values from -0.125 to 0.125
- q_gain: float32 [128], replicated, may hold values from 0.1 to 1.9
- k_gain: float32 [128], replicated, may hold values from 0.1 to 1.9
Outputs:
- next_residual: bfloat16 [512, 2048], P(('expert', 'tensor'))
- queries: bfloat16 [512, 4096], P('expert', 'tensor')
- keys_values: bfloat16 [512, 1024], P('expert', 'tensor')
Inputs may be any that keep to these rules, and one draw needn't show every extreme that they name: `expert_ids`: each row names 8 different experts. In each aligned block of 32 rows no expert is named by more than 12 rows, and in some block one expert is named by exactly 12 rows.
All inputs are finite; a program needn't handle non-finite values.
Results may differ from a plain program's by a relative error of at most 0.012.
Values may be sent and summed in bfloat16 or wider, within the bound.
No kernel may reach another device: no remote copies, remote signals or barrier semaphores. Data moves between devices by JAX's collectives and lax.ppermute only.
A program may use at most 64 MiB of HBM per device.

v0:
```python
import jax
import jax.numpy as jnp
from jax import lax
from jax.sharding import PartitionSpec as P

KV_HEADS = 4
TOP = 8


EPSILON = 1e-06


def normalize(values, gain):
    return values * lax.rsqrt(jnp.mean(values * values, axis=-1, keepdims=True) + EPSILON) * gain


def per_device(
    attn_out,
    out_weight,
    residual,
    attn_gain,
    expert_ids,
    route_weights,
    w_gate,
    w_up,
    w_down,
    input_gain,
    q_weight,
    kv_weight,
    q_gain,
    k_gain,
):
    n_expert = lax.axis_size("expert")
    n_tensor = lax.axis_size("tensor")
    share = n_tensor // 2
    tensor_index = lax.axis_index("tensor")
    group_rows = attn_out.shape[0]
    width = residual.shape[1]
    half = tensor_index // share
    capacity = 3 * group_rows * TOP // (4 * n_expert)
    all_experts = 2 * n_expert
    attn_rows = lax.psum_scatter(
        jnp.dot(attn_out, out_weight, preferred_element_type=jnp.float32),
        "tensor",
        scatter_dimension=0,
        tiled=True,
    )
    first_residual = (residual.astype(jnp.float32) + attn_rows).astype(jnp.bfloat16)
    normed = normalize(first_residual.astype(jnp.float32), attn_gain).astype(jnp.bfloat16)
    group_normed = lax.all_gather(normed, "tensor", axis=0, tiled=True)
    flat_ids = expert_ids.reshape(-1)
    onehot = (flat_ids[:, None] == jnp.arange(all_experts, dtype=jnp.int32)[None, :]).astype(
        jnp.int32
    )
    earlier = jnp.cumsum(onehot, axis=0) - onehot
    rank = jnp.sum(earlier * onehot, axis=1)
    dest = flat_ids * capacity + rank
    row_owner = jnp.arange(flat_ids.shape[0], dtype=jnp.int32) // TOP
    slot_row = jnp.full((all_experts * capacity,), group_rows, jnp.int32).at[dest].set(row_owner)
    slot_weight = (
        jnp.zeros((all_experts * capacity,), jnp.float32).at[dest].set(route_weights.reshape(-1))
    )
    own_slots = lax.dynamic_index_in_dim(
        slot_row.reshape(n_expert, 2, capacity), half, 1, keepdims=False
    )
    own_weights = lax.dynamic_index_in_dim(
        slot_weight.reshape(n_expert, 2, capacity), half, 1, keepdims=False
    )
    padded_rows = jnp.concatenate([group_normed, jnp.zeros((1, width), jnp.bfloat16)], axis=0)
    gate_w = w_gate[0]
    up_w = w_up[0]
    down_w = w_down[0]
    outgoing = jnp.take(padded_rows, own_slots, axis=0)
    arrived = lax.all_to_all(outgoing, "expert", split_axis=0, concat_axis=0, tiled=True)
    flat = arrived.reshape(-1, width)
    gate = jnp.dot(flat, gate_w, preferred_element_type=jnp.float32)
    up = jnp.dot(flat, up_w, preferred_element_type=jnp.float32)
    act = (jax.nn.silu(gate) * up).astype(jnp.bfloat16)
    part = jnp.dot(act, down_w, preferred_element_type=jnp.float32).astype(jnp.bfloat16)
    send_part = part.reshape(arrived.shape)
    returned = lax.all_to_all(send_part, "expert", split_axis=0, concat_axis=0, tiled=True)
    weighted = own_weights.reshape(-1)[:, None] * returned.reshape(-1, width).astype(jnp.float32)
    term = (
        jnp.zeros((group_rows + 1, width), jnp.float32)
        .at[own_slots.reshape(-1)]
        .add(weighted)[:group_rows]
    )
    expert_sum = lax.psum_scatter(
        term.astype(jnp.bfloat16), "tensor", scatter_dimension=0, tiled=True
    ).astype(jnp.float32)
    next_residual = (first_residual.astype(jnp.float32) + expert_sum).astype(jnp.bfloat16)
    own_normed = normalize(next_residual.astype(jnp.float32), input_gain).astype(jnp.bfloat16)
    next_normed = lax.all_gather(own_normed, "tensor", axis=0, tiled=True)
    query_cols = q_weight.shape[1]
    kv_cols = kv_weight.shape[1]
    query_raw = jnp.dot(
        next_normed,
        lax.all_gather(q_weight, "expert", axis=0, tiled=True),
        preferred_element_type=jnp.float32,
    )
    kv_raw = jnp.dot(
        next_normed,
        lax.all_gather(kv_weight, "expert", axis=0, tiled=True),
        preferred_element_type=jnp.float32,
    )
    head_size = q_gain.shape[0]
    queries = (
        normalize(query_raw.reshape(group_rows, -1, head_size), q_gain)
        .reshape(group_rows, query_cols)
        .astype(jnp.bfloat16)
    )
    heads_here = kv_cols // head_size
    head_number = tensor_index * heads_here + jnp.arange(heads_here, dtype=jnp.int32)
    is_key = head_number < KV_HEADS
    kv_shaped = kv_raw.reshape(group_rows, heads_here, head_size)
    keys_values = (
        jnp.where(is_key[None, :, None], normalize(kv_shaped, k_gain), kv_shaped)
        .reshape(group_rows, kv_cols)
        .astype(jnp.bfloat16)
    )
    return (next_residual, queries, keys_values)


def solution(mesh):
    return jax.shard_map(
        per_device,
        mesh=mesh,
        in_specs=(
            P("expert", "tensor"),
            P("tensor", None),
            P(("expert", "tensor"), None),
            P(),
            P("expert", None),
            P("expert", None),
            P("expert", None, "tensor"),
            P("expert", None, "tensor"),
            P("expert", "tensor", None),
            P(),
            P("expert", "tensor"),
            P("expert", "tensor"),
            P(),
            P(),
        ),
        out_specs=(P(("expert", "tensor"), None), P("expert", "tensor"), P("expert", "tensor")),
        check_vma=False,
    )
```

profile of v0, /device:TPU:0, one launch (start us, length us, event | category | flops | bytes accessed | tf_op | source)
XLA Modules:
  0.0 308.6 jit_solution(10205566362595522143)
XLA Ops:
  8.1 5.8 %fusion.51 = f32[32,2048]{1,0:T(8,128)} fusion(bf16[32,2048]{1,0:T(8,128)(2,1)} %param.14, bf16[2048,2048]{1,0:T(8,128)(2,1)} %param.15), kind=kOutput, calls=%fused_computation.83 | convolution fusion | flops 268435456 | bytes 8781824 | tf_op jit(solution)/shard_map/dot_general | solution.py:43
  15.4 1.4 scatter_custom_fusion
  18.2 6.3 %reduce-scatter.3.cloned.1.call-done = f32[16,2048]{1,0:T(8,128)} async-done(((f32[32,2048]{1,0:T(8,128)}), f32[16,2048]{1,0:T(8,128)}) %reduce-scatter.3.cloned.1.call-update) | async-done | bytes 131088 | tf_op jit(solution)/shard_map/reduce_scatter | solution.py:42
  25.6 1.9 all_gather.12
  27.5 2.1 gather_fusion
  29.6 2.1 reshape.199
  31.7 1.4 broadcast_select_fusion
  33.1 33.4 %all_to_all.10 = bf16[16,12,2048]{2,1,0:T(8,128)(2,1)} all-to-all(bf16[16,12,2048]{2,1,0:T(8,128)(2,1)S(1)} %broadcast_select_fusion), channel_id=1, replica_groups=mesh['expert'=16,'tensor'=2] {'expert'}, dimensions={0} | all-to-all | bytes 1572864 | tf_op jit(solution)/shard_map/all_to_all | solution.py:74
  66.5 2.1 reshape.195
  68.7 3.7 %fusion.4 = f32[192,768]{1,0:T(8,128)} fusion(bf16[192,2048]{1,0:T(8,128)(2,1)} %reshape.195, bf16[1,2048,768]{2,1,0:T(8,128)(2,1)} %param.20), kind=kOutput, calls=%fused_computation.8 | convolution fusion | flops 603979776 | bytes 4521984 | tf_op jit(solution)/shard_map/dot_general | solution.py:76
  72.4 4.8 %fusion.6 = bf16[192,2048]{1,0:T(8,128)(2,1)} fusion(bf16[1,768,2048]{2,1,0:T(8,128)(2,1)S(1)} %copy-done, bf16[192,2048]{1,0:T(8,128)(2,1)} %reshape.195, bf16[1,2048,768]{2,1,0:T(8,128)(2,1)} %param.21, f32[192,768]{1,0:T(8,128)} %fusion.4), kind=kOutput, calls=%fused_computation.10 | convolution fusion | flops 1209237504 | bytes 8454144 | tf_op jit(solution)/shard_map/dot_general | solution.py:79
  77.2 2.1 reshape.196
  79.3 4.3 %all-to-all-start.1 = ((bf16[16,12,2048]{2,1,0:T(8,128)(2,1)}), bf16[16,12,2048]{2,1,0:T(8,128)(2,1)}, u32[]{:S(2)}, u32[]{:S(2)}) async-start(bf16[16,12,2048]{2,1,0:T(8,128)(2,1)} %reshape.196), calls=%async_computation.2 | async-start | bytes 2097152 | tf_op jit(solution)/shard_map/all_to_all | solution.py:81
  84.0 1.4 scatter_custom_fusion.1
  86.2 21.0 %all-to-all-done.1 = bf16[16,12,2048]{2,1,0:T(8,128)(2,1)} async-done(((bf16[16,12,2048]{2,1,0:T(8,128)(2,1)}), bf16[16,12,2048]{2,1,0:T(8,128)(2,1)}, u32[]{:S(2)}, u32[]{:S(2)}) %all-to-all-start.1) | async-done | bytes 786464 | tf_op jit(solution)/shard_map/all_to_all | solution.py:81
  107.2 2.3 reshape.197
  109.6 4.0 %scatter_custom_fusion.2 = f32[33,2048]{1,0:T(8,128)S(1)} fusion(s32[192]{0:T(256)} %bitcast.84, f32[192,2048]{1,0:T(8,128)} %reshape.197, f32[192]{0:T(256)S(1)} %mul.141, f32[]{:T(128)} %constant.46.clone.1), kind=kCustom, calls=%fused_computation.11 | custom fusion | flops 786432 | bytes 1844480 | tf_op jit(solution)/shard_map/scatter-add | solution.py:86
  117.9 4.2 %reduce-scatter.5.cloned.1.call-done = bf16[16,2048]{1,0:T(8,128)(2,1)} async-done(((bf16[32,2048]{1,0:T(8,128)(2,1)}), bf16[16,2048]{1,0:T(8,128)(2,1)}) %reduce-scatter.5.cloned.1.call-update) | async-done | bytes 65552 | tf_op jit(solution)/shard_map/reduce_scatter | solution.py:88
  123.8 1.9 all_gather.13
  125.7 53.1 %all-gather.5.cloned.1.call-done = bf16[2048,512]{1,0:T(8,128)(2,1)} async-done(((bf16[128,512]{1,0:T(8,128)(2,1)}), bf16[2048,512]{1,0:T(8,128)(2,1)}) %all-gather.5.cloned.1.call-update) | async-done | bytes 2097168 | tf_op jit(solution)/shard_map/all_gather | solution.py:103
  178.8 2.0 fusion.50
  181.1 1.3 fusion.38
  182.4 111.0 %all-gather.3.cloned.1.call-done = bf16[2048,2048]{1,0:T(8,128)(2,1)} async-done(((bf16[128,2048]{1,0:T(8,128)(2,1)}), bf16[2048,2048]{1,0:T(8,128)(2,1)}) %all-gather.3.cloned.1.call-update) | async-done | bytes 8388624 | tf_op jit(solution)/shard_map/all_gather | solution.py:98
  293.4 4.9 %fusion.52 = f32[32,2048]{1,0:T(8,128)S(1)} fusion(bf16[32,2048]{1,0:T(8,128)(2,1)S(1)} %all_gather.13, bf16[2048,2048]{1,0:T(8,128)(2,1)} %all-gather.3.cloned.1.call-done), kind=kOutput, calls=%fused_computation.84 | convolution fusion | flops 268435456 | bytes 8781824 | tf_op jit(solution)/shard_map/dot_general | solution.py:96
  (72 shorter events, 14.0 us)
Async XLA Ops:
  8.0 64.4 %copy-start = (bf16[1,768,2048]{2,1,0:T(8,128)(2,1)S(1)}, bf16[1,768,2048]{2,1,0:T(8,128)(2,1)}, u32[]{:S(2)}) copy-start(bf16[1,768,2048]{2,1,0:T(8,128)(2,1)} %param.22) | copy-start | bytes 9437188
  8.0 5.9 %copy-start.3 = (s32[32,8]{0,1:T(8,128)S(1)}, s32[32,8]{0,1:T(8,128)}, u32[]{:S(2)}) copy-start(s32[32,8]{0,1:T(8,128)} %param.18) | copy-start | bytes 3076
  8.0 16.5 %copy-start.2 = (bf16[16,2048]{1,0:T(8,128)(2,1)S(1)}, bf16[16,2048]{1,0:T(8,128)(2,1)}, u32[]{:S(2)}) copy-start(bf16[16,2048]{1,0:T(8,128)(2,1)} %param.16) | copy-start | bytes 196612
  8.0 17.5 %copy-start.4 = (f32[2048]{0:T(1024)S(1)}, f32[2048]{0:T(1024)}, u32[]{:S(2)}) copy-start(f32[2048]{0:T(1024)} %param.17) | copy-start | bytes 24580
  8.0 16.4 %reduce-scatter.3.cloned.1.call-start = ((), (), s32[]{:S(2)}) async-start(), calls=%async_computation.4 | async-start | bytes 393216 | tf_op jit(solution)/shard_map/reduce_scatter | solution.py:42
  77.2 6.6 %copy-start.6 = (f32[32,8]{0,1:T(8,128)S(1)}, f32[32,8]{0,1:T(8,128)}, u32[]{:S(2)}) copy-start(f32[32,8]{0,1:T(8,128)} %param.19) | copy-start | bytes 3076
  79.3 27.9 %all-to-all-start.1 = ((bf16[16,12,2048]{2,1,0:T(8,128)(2,1)}), bf16[16,12,2048]{2,1,0:T(8,128)(2,1)}, u32[]{:S(2)}, u32[]{:S(2)}) async-start(bf16[16,12,2048]{2,1,0:T(8,128)(2,1)} %reshape.196), calls=%async_computation.2 | async-start | bytes 2097152 | tf_op jit(solution)/shard_map/all_to_all | solution.py:81
  83.7 40.1 %copy-start.5 = (f32[2048]{0:T(1024)S(1)}, f32[2048]{0:T(1024)}, u32[]{:S(2)}) copy-start(f32[2048]{0:T(1024)} %param.23) | copy-start | bytes 24580
  83.7 38.4 %reduce-scatter.5.cloned.1.call-start = ((), (), s32[]{:S(2)}) async-start(), calls=%async_computation.5 | async-start | bytes 196608 | tf_op jit(solution)/shard_map/reduce_scatter | solution.py:88
  114.3 64.5 %all-gather.5.cloned.1.call-start = ((), (), s32[]{:S(2)}) async-start(), calls=%async_computation.7 | async-start | bytes 2228224 | tf_op jit(solution)/shard_map/all_gather | solution.py:103
  114.9 178.5 %all-gather.3.cloned.1.call-start = ((), (), s32[]{:S(2)}) async-start(), calls=%async_computation.6 | async-start | bytes 8912896 | tf_op jit(solution)/shard_map/all_gather | solution.py:98
  123.1 0.6 copy-start.1
Sparse Core Ops, SparseCore 0:
  14.1 10.3 reduce-scatter.2
  114.4 7.6 reduce-scatter.4
Sparse Core Ops, SparseCore 1:
  117.9 60.8 all-gather.4
  181.9 111.5 all-gather.2
where the time goes:
time: 309 us
  waiting for transfers between devices  197 us (64%)
  blocking collectives  37.2 us (12%)
  matrix products  21.3 us (7%)
  local copies, waits for them, and re-layouts  20.8 us (7%)
  between operations  15.8 us (5%)
  other arithmetic  12.2 us (4%)
  starting transfers between devices  4.5 us (1%)
    all_gather x1, waiting for transfers between devices, per_device(): lax.all_gather(q_weight, 'expert', axis=0, tiled=True)  111 us
    all_gather x1, waiting for transfers between devices, per_device(): lax.all_gather(kv_weight, 'expert', axis=0, tiled=True)  53.1 us
    all_to_all x1, blocking collectives, per_device(): lax.all_to_all(outgoing, 'expert', split_axis=0, concat_axis=0, tiled=True)  33.4 us
    all_to_all x1, waiting for transfers between devices, per_device(): lax.all_to_all(send_part, 'expert', split_axis=0, concat_axis=0, tiled=True)  21 us
    reduce_scatter x1, waiting for transfers between devices, per_device(): lax.psum_scatter(jnp.dot(attn_out, out_weight, preferred_element_type=jnp...  6.26 us
  transfers between devices with their start and end apart: 5, of which 5 were waited for; matrix products, arithmetic and copies ran while one was open for 4% of the time, Pallas kernels for 0%

commit v1 on v0

--- a/solution.py
+++ b/solution.py
@@ -1,10 +1,16 @@
+import functools
+
 import jax
 import jax.numpy as jnp
 from jax import lax
+from jax.experimental import pallas as pl
+from jax.experimental.pallas import tpu as pltpu
 from jax.sharding import PartitionSpec as P
 
 KV_HEADS = 4
 TOP = 8
+PLANE = 4
+META = 128
 
 
 EPSILON = 1e-06
@@ -12,6 +18,444 @@
 
 def normalize(values, gain):
     return values * lax.rsqrt(jnp.mean(values * values, axis=-1, keepdims=True) + EPSILON) * gain
+
+
+def out_projection_kernel(chunk, pos_ref, a_ref, w_ref, mine_ref, theirs_ref, w_buf, sems):
+    depth, width = w_buf.shape
+    count = width // chunk
+    half = mine_ref.shape[0]
+    copies = []
+    for i in range(count):
+        cols = pl.ds(i * chunk, chunk)
+        copies.append(pltpu.make_async_copy(w_ref.at[:, cols], w_buf.at[:, cols], sems.at[i]))
+    for copy in copies:
+        copy.start()
+    tensor = pos_ref[1]
+    own_rows = pl.ds(pl.multiple_of(tensor * half, half), half)
+    other_rows = pl.ds(pl.multiple_of((1 - tensor) * half, half), half)
+    own = a_ref[own_rows, :]
+    other = a_ref[other_rows, :]
+    both = jnp.concatenate([own, other], axis=0)
+    for i in range(count):
+        copies[i].wait()
+        cols = pl.ds(i * chunk, chunk)
+        product = jnp.dot(both, w_buf[:, cols], preferred_element_type=jnp.float32)
+        mine_ref[:, cols] = product[:half]
+        theirs_ref[:, cols] = product[half:]
+
+
+def out_projection(pos, attn_out, out_weight):
+    rows, depth = attn_out.shape
+    width = out_weight.shape[1]
+    chunk = 256
+    half = jax.ShapeDtypeStruct((rows // 2, width), jnp.float32)
+    return pl.pallas_call(
+        functools.partial(out_projection_kernel, chunk),
+        out_shape=(half, half),
+        in_specs=[
+            pl.BlockSpec(memory_space=pltpu.SMEM),
+            pl.BlockSpec(memory_space=pltpu.VMEM),
+            pl.BlockSpec(memory_space=pl.ANY),
+        ],
+        out_specs=(pl.BlockSpec(memory_space=pltpu.VMEM), pl.BlockSpec(memory_space=pltpu.VMEM)),
+        scratch_shapes=[
+            pltpu.VMEM((depth, width), jnp.bfloat16),
+            pltpu.SemaphoreType.DMA((width // chunk,)),
+        ],
+        compiler_params=pltpu.CompilerParams(vmem_limit_bytes=24 << 20),
+        cost_estimate=pl.CostEstimate(
+            flops=2 * rows * depth * width, bytes_accessed=2 * depth * width, transcendentals=0
+        ),
+        name="out_projection",
+    )(pos, attn_out, out_weight)
+
+
+def first_norm_kernel(
+    slices, pos_ref, mine_ref, theirs_ref, residual_ref, gain_ref, meta_ref, tokens_ref, *slice_refs
+):
+    width = residual_ref.shape[1]
+    part = width // slices
+    first = (residual_ref[...].astype(jnp.float32) + (mine_ref[...] + theirs_ref[...])).astype(
+        jnp.bfloat16
+    )
+    tokens_ref[:, :width] = normalize(first.astype(jnp.float32), gain_ref[...]).astype(jnp.bfloat16)
+    tokens_ref[:, width:] = meta_ref[...]
+    for d in range(slices):
+        for j in range(slices):
+
+            @pl.when((pos_ref[0] ^ d) == j)
+            def _(d=d, j=j):
+                slice_refs[d][...] = first[:, j * part : (j + 1) * part]
+
+
+def first_norm(pos, mine, theirs, residual, gain, meta, slices):
+    rows, width = residual.shape
+    vmem = pl.BlockSpec(memory_space=pltpu.VMEM)
+    return pl.pallas_call(
+        functools.partial(first_norm_kernel, slices),
+        out_shape=(jax.ShapeDtypeStruct((rows, width + META), jnp.bfloat16),)
+        + (jax.ShapeDtypeStruct((rows, width // slices), jnp.bfloat16),) * slices,
+        in_specs=[pl.BlockSpec(memory_space=pltpu.SMEM)] + [vmem] * 5,
+        out_specs=(vmem,) * (1 + slices),
+        name="first_norm",
+    )(pos, mine, theirs, residual, gain, meta)
+
+
+def expert_kernel(blocks, chunk, pos_ref, *refs):
+    block_refs = refs[:blocks]
+    weight_refs = refs[blocks : blocks + 6]
+    rest = refs[blocks + 6 :]
+    out_refs, (x_buf, gate_buf, up_buf, down_buf, act_buf, sems) = rest[:PLANE], rest[PLANE:]
+    width, hidden = gate_buf.shape[1], gate_buf.shape[2]
+    rows = block_refs[0].shape[0]
+    per = hidden // chunk
+    gate_copies, down_copies = [], []
+    for side in range(2):
+        gate_ref, up_ref, down_ref = weight_refs[3 * side : 3 * side + 3]
+        for i in range(per):
+            cols = pl.ds(i * chunk, chunk)
+            at = side * per + i
+            pair = (
+                pltpu.make_async_copy(
+                    gate_ref.at[0, :, cols], gate_buf.at[side, :, cols], sems.at[0, at]
+                ),
+                pltpu.make_async_copy(
+                    up_ref.at[0, :, cols], up_buf.at[side, :, cols], sems.at[1, at]
+                ),
+            )
+            gate_copies.append(pair)
+    for side in range(2):
+        down_ref = weight_refs[3 * side + 2]
+        for i in range(per):
+            at = side * per + i
+            down_copies.append(
+                pltpu.make_async_copy(
+                    down_ref.at[0, pl.ds(i * chunk, chunk), :],
+                    down_buf.at[pl.ds(at * chunk, chunk), :],
+                    sems.at[2, at],
+                )
+            )
+    for pair in gate_copies:
+        pair[0].start()
+        pair[1].start()
+    for copy in down_copies:
+        copy.start()
+    for i in range(blocks):
+        x_buf[i * rows : (i + 1) * rows, :] = block_refs[i][...]
+    meta = x_buf[:, width:].astype(jnp.float32)
+    lane = lax.broadcasted_iota(jnp.int32, meta.shape, 1)
+    for side in range(2):
+        expert = pos_ref[2 + side]
+        chosen = (lane == expert) | (lane == expert + META // 2)
+        route = jnp.sum(jnp.where(chosen, meta, 0.0), axis=1, keepdims=True)
+        for i in range(per):
+            at = side * per + i
+            gate_copies[at][0].wait()
+            gate_copies[at][1].wait()
+            cols = pl.ds(i * chunk, chunk)
+            x = x_buf[:, :width]
+            gate = jnp.dot(x, gate_buf[side, :, cols], preferred_element_type=jnp.float32)
+            up = jnp.dot(x, up_buf[side, :, cols], preferred_element_type=jnp.float32)
+            act = gate / (1.0 + jnp.exp(-gate)) * up * route
+            act_buf[:, at * chunk : (at + 1) * chunk] = act.astype(jnp.bfloat16)
+    for copy in down_copies:
+        copy.wait()
+    step = width // 4
+    group = blocks // PLANE * rows
+    for j in range(4):
+        cols = pl.ds(j * step, step)
+        out = jnp.dot(act_buf[...], down_buf[:, cols], preferred_element_type=jnp.float32)
+        for k in range(PLANE):
+            out_refs[k][:, cols] = out[k * group : (k + 1) * group].astype(jnp.bfloat16)
+
+
+def experts(pos, blocks, weights):
+    rows, extended = blocks[0].shape
+    width, hidden = weights[0].shape[1:]
+    chunk = 256
+    total = rows * len(blocks)
+    vmem = pl.BlockSpec(memory_space=pltpu.VMEM)
+    return pl.pallas_call(
+        functools.partial(expert_kernel, len(blocks), chunk),
+        out_shape=(jax.ShapeDtypeStruct((total // PLANE, width), jnp.bfloat16),) * PLANE,
+        in_specs=[pl.BlockSpec(memory_space=pltpu.SMEM)]
+        + [vmem] * len(blocks)
+        + [pl.BlockSpec(memory_space=pl.ANY)] * 6,
+        out_specs=(vmem,) * PLANE,
+        scratch_shapes=[
+            pltpu.VMEM((total, extended), jnp.bfloat16),
+            pltpu.VMEM((2, width, hidden), jnp.bfloat16),
+            pltpu.VMEM((2, width, hidden), jnp.bfloat16),
+            pltpu.VMEM((2 * hidden, width), jnp.bfloat16),
+            pltpu.VMEM((total, 2 * hidden), jnp.bfloat16),
+            pltpu.SemaphoreType.DMA((3, 2 * (hidden // chunk))),
+        ],
+        compiler_params=pltpu.CompilerParams(vmem_limit_bytes=40 << 20),
+        cost_estimate=pl.CostEstimate(
+            flops=12 * total * width * hidden,
+            bytes_accessed=12 * width * hidden,
+            transcendentals=2 * total * hidden,
+        ),
+        name="experts",
+    )(pos, *blocks, *weights)
+
+
+def plane_sum_kernel(slices, pos_ref, *refs):
+    in_refs, out_refs = refs[:PLANE], refs[PLANE:]
+    rows, width = in_refs[0].shape
+    part = width // slices
+    block = rows // slices
+    total = in_refs[0][...].astype(jnp.float32)
+    for ref in in_refs[1:]:
+        total = total + ref[...].astype(jnp.float32)
+    total = total.astype(jnp.bfloat16)
+    for d in range(slices):
+        for j in range(slices):
+
+            @pl.when((pos_ref[0] ^ d) == j)
+            def _(d=d, j=j):
+                for i in range(slices):
+                    out_refs[d][i * block : (i + 1) * block, :] = total[
+                        (d ^ i) * block : ((d ^ i) + 1) * block, j * part : (j + 1) * part
+                    ]
+
+
+def plane_sum(pos, parts, slices):
+    rows, width = parts[0].shape
+    vmem = pl.BlockSpec(memory_space=pltpu.VMEM)
+    return pl.pallas_call(
+        functools.partial(plane_sum_kernel, slices),
+        out_shape=(jax.ShapeDtypeStruct((rows, width // slices), jnp.bfloat16),) * slices,
+        in_specs=[pl.BlockSpec(memory_space=pltpu.SMEM)] + [vmem] * PLANE,
+        out_specs=(vmem,) * slices,
+        name="plane_sum",
+    )(pos, *parts)
+
+
+def second_norm_kernel(slices, *refs):
+    parts, firsts, gain_ref = refs[:slices], refs[slices : 2 * slices], refs[2 * slices]
+    scaled_ref, next_refs = refs[2 * slices + 1], refs[2 * slices + 2 :]
+    rows, part = firsts[0].shape
+    total = parts[0][...].astype(jnp.float32)
+    for ref in parts[1:]:
+        total = total + ref[...].astype(jnp.float32)
+    lane = lax.broadcasted_iota(jnp.int32, (rows, META), 1)
+    for d in range(slices):
+        at = slice(d * rows, (d + 1) * rows)
+        following = (firsts[d][...].astype(jnp.float32) + total[at]).astype(jnp.bfloat16)
+        next_refs[d][...] = following
+        wide = following.astype(jnp.float32)
+        scaled_ref[at, :part] = (wide * gain_ref[...]).astype(jnp.bfloat16)
+        squares = jnp.sum(wide * wide, axis=1, keepdims=True)
+        high = squares.astype(jnp.bfloat16).astype(jnp.float32)
+        low = squares - high
+        scaled_ref[at, part:] = jnp.where(
+            lane == 0, high, jnp.where(lane == 1, low, 0.0)
+        ).astype(jnp.bfloat16)
+
+
+def second_norm(parts, firsts, gain):
+    slices = len(parts)
+    rows, part = firsts[0].shape
+    vmem = pl.BlockSpec(memory_space=pltpu.VMEM)
+    return pl.pallas_call(
+        functools.partial(second_norm_kernel, slices),
+        out_shape=(jax.ShapeDtypeStruct((slices * rows, part + META), jnp.bfloat16),)
+        + (jax.ShapeDtypeStruct((rows, part), jnp.bfloat16),) * slices,
+        in_specs=[vmem] * (2 * slices + 1),
+        out_specs=(vmem,) * (1 + slices),
+        name="second_norm",
+    )(*parts, *firsts, gain)
+
+
+def projection_kernel(slices, pos_ref, mine_ref, theirs_ref, q_ref, kv_ref, *out_refs):
+    rows, extended = mine_ref.shape
+    part = extended - META
+    block = rows // slices
+    q_cols, kv_cols = q_ref.shape[1], kv_ref.shape[1]
+    both = jnp.concatenate([mine_ref[:, :part], theirs_ref[:, :part]], axis=0)
+    starts = [(q_ref, i, i) for i in range(0, q_cols, kv_cols)] + [(kv_ref, 0, q_cols)]
+    tensor = pos_ref[1]
+    own = pl.ds(pl.multiple_of(tensor * block, block), block)
+    other = pl.ds(pl.multiple_of((1 - tensor) * block, block), block)
+    for weight_ref, source, target in starts:
+        product = jnp.dot(
+            both, weight_ref[:, source : source + kv_cols], preferred_element_type=jnp.float32
+        ).astype(jnp.bfloat16)
+        for d in range(slices):
+            cols = slice(target, target + kv_cols)
+            out_refs[d][own, cols] = product[d * block : (d + 1) * block]
+            out_refs[d][other, cols] = product[rows + d * block : rows + (d + 1) * block]
+    for d in range(slices):
+        out_refs[d][own, q_cols + kv_cols :] = mine_ref[d * block : (d + 1) * block, part:]
+        out_refs[d][other, q_cols + kv_cols :] = theirs_ref[d * block : (d + 1) * block, part:]
+
+
+def projection(pos, mine, theirs, q_weight, kv_weight, slices):
+    rows = mine.shape[0]
+    cols = q_weight.shape[1] + kv_weight.shape[1]
+    vmem = pl.BlockSpec(memory_space=pltpu.VMEM)
+    return pl.pallas_call(
+        functools.partial(projection_kernel, slices),
+        out_shape=(jax.ShapeDtypeStruct((2 * rows // slices, cols + META), jnp.bfloat16),) * slices,
+        in_specs=[pl.BlockSpec(memory_space=pltpu.SMEM)] + [vmem] * 4,
+        out_specs=(vmem,) * slices,
+        compiler_params=pltpu.CompilerParams(vmem_limit_bytes=24 << 20),
+        cost_estimate=pl.CostEstimate(
+            flops=4 * rows * q_weight.shape[0] * cols,
+            bytes_accessed=2 * q_weight.shape[0] * cols,
+            transcendentals=0,
+        ),
+        name="qkv_projection",
+    )(pos, mine, theirs, q_weight, kv_weight)
+
+
+def head_norm_kernel(slices, width, pos_ref, *refs):
+    parts, q_gain_ref, k_gain_ref = refs[:slices], refs[slices], refs[slices + 1]
+    q_ref, kv_ref = refs[slices + 2 :]
+    q_cols, kv_cols = q_ref.shape[1], kv_ref.shape[1]
+    head = q_gain_ref.shape[1]
+
+    def total(cols):
+        value = parts[0][:, cols].astype(jnp.float32)
+        for ref in parts[1:]:
+            value = value + ref[:, cols].astype(jnp.float32)
+        return value
+
+    squares = jnp.sum(total(slice(q_cols + kv_cols, None)), axis=1, keepdims=True)
+    scale = lax.rsqrt(squares / width + EPSILON)
+    for h in range(q_cols // head):
+        cols = slice(h * head, (h + 1) * head)
+        q_ref[:, cols] = normalize(total(cols) * scale, q_gain_ref[...]).astype(jnp.bfloat16)
+    for h in range(kv_cols // head):
+        cols = slice(h * head, (h + 1) * head)
+        raw = total(slice(q_cols + h * head, q_cols + (h + 1) * head)) * scale
+        is_key = pos_ref[1] * (kv_cols // head) + h < KV_HEADS
+        kv_ref[:, cols] = jnp.where(is_key, normalize(raw, k_gain_ref[...]), raw).astype(
+            jnp.bfloat16
+        )
+
+
+def head_norm(pos, parts, q_gain, k_gain, q_cols, kv_cols, width):
+    slices = len(parts)
+    rows = parts[0].shape[0]
+    vmem = pl.BlockSpec(memory_space=pltpu.VMEM)
+    return pl.pallas_call(
+        functools.partial(head_norm_kernel, slices, width),
+        out_shape=(
+            jax.ShapeDtypeStruct((rows, q_cols), jnp.bfloat16),
+            jax.ShapeDtypeStruct((rows, kv_cols), jnp.bfloat16),
+        ),
+        in_specs=[pl.BlockSpec(memory_space=pltpu.SMEM)] + [vmem] * (slices + 2),
+        out_specs=(vmem, vmem),
+        name="head_norm",
+    )(pos, *parts, q_gain, k_gain)
+
+
+def assemble_kernel(slices, pos_ref, *refs):
+    out_ref = refs[slices]
+    part = refs[0].shape[1]
+    for d in range(slices):
+        at = pl.multiple_of((pos_ref[0] ^ d) * part, part)
+        out_ref[:, pl.ds(at, part)] = refs[d][...]
+
+
+def assemble(pos, parts):
+    slices = len(parts)
+    rows, part = parts[0].shape
+    vmem = pl.BlockSpec(memory_space=pltpu.VMEM)
+    return pl.pallas_call(
+        functools.partial(assemble_kernel, slices),
+        out_shape=jax.ShapeDtypeStruct((rows, slices * part), jnp.bfloat16),
+        in_specs=[pl.BlockSpec(memory_space=pltpu.SMEM)] + [vmem] * slices,
+        out_specs=vmem,
+        name="assemble_residual",
+    )(pos, *parts)
+
+
+def per_device_dense(
+    attn_out,
+    out_weight,
+    residual,
+    attn_gain,
+    expert_ids,
+    route_weights,
+    w_gate,
+    w_up,
+    w_down,
+    input_gain,
+    q_weight,
+    kv_weight,
+    q_gain,
+    k_gain,
+):
+    n_expert = lax.axis_size("expert")
+    depth = n_expert // PLANE
+    all_experts = 2 * n_expert
+    width = residual.shape[1]
+    rows = residual.shape[0]
+    expert_index = lax.axis_index("expert").astype(jnp.int32)
+    tensor_index = lax.axis_index("tensor").astype(jnp.int32)
+    z_index = expert_index // PLANE
+    pos = jnp.stack(
+        [
+            z_index,
+            tensor_index,
+            2 * expert_index + tensor_index,
+            2 * expert_index + 1 - tensor_index,
+        ]
+    )
+
+    def to_core(value):
+        return lax.ppermute(value, "tensor", [(0, 1), (1, 0)])
+
+    def to_expert(value, offset):
+        return lax.ppermute(value, "expert", [(i, i ^ offset) for i in range(n_expert)])
+
+    def to_z(value, d):
+        return to_expert(value, d * PLANE) if d else value
+
+    def to_plane(value, d):
+        return to_expert(value, d) if d else value
+
+    planes = [list(range(i, i + PLANE)) for i in range(0, n_expert, PLANE)]
+    q_rows = lax.all_gather(q_weight, "expert", axis=0, tiled=True, axis_index_groups=planes)
+    kv_rows = lax.all_gather(kv_weight, "expert", axis=0, tiled=True, axis_index_groups=planes)
+    weights = (w_gate, w_up, w_down, to_core(w_gate), to_core(w_up), to_core(w_down))
+
+    own_ids = lax.dynamic_slice_in_dim(expert_ids, tensor_index * rows, rows, 0)
+    own_route = lax.dynamic_slice_in_dim(route_weights, tensor_index * rows, rows, 0)
+    chosen = own_ids[:, :, None] == jnp.arange(META // 2, dtype=jnp.int32)[None, None, :]
+    dense = jnp.sum(jnp.where(chosen, own_route[:, :, None], 0.0), axis=1)
+    high = lax.reduce_precision(dense, 8, 7)
+    meta = jnp.concatenate([high, dense - high], axis=1).astype(jnp.bfloat16)
+
+    mine, theirs = out_projection(pos, attn_out, out_weight)
+    tokens, *firsts = first_norm(
+        pos, mine, to_core(theirs), residual, attn_gain[None, :], meta, depth
+    )
+    firsts = [to_z(firsts[d], d) for d in range(depth)]
+    line = [to_z(tokens, d) for d in range(depth)]
+    blocks = [to_plane(block, d) for d in range(PLANE) for block in line]
+    outs = experts(pos, blocks, weights)
+    outs = [to_plane(outs[d], d) for d in range(PLANE)]
+    parts = plane_sum(pos, outs, depth)
+    parts = [to_z(parts[d], d) for d in range(depth)]
+    own_gain = lax.dynamic_slice_in_dim(input_gain, z_index * (width // depth), width // depth, 0)
+    scaled, *following = second_norm(parts, firsts, own_gain[None, :])
+    products = projection(pos, scaled, to_core(scaled), q_rows, kv_rows, depth)
+    next_residual = assemble(pos, [to_z(following[d], d) for d in range(depth)])
+    products = [to_z(products[d], d) for d in range(depth)]
+    queries, keys_values = head_norm(
+        pos,
+        products,
+        q_gain[None, :],
+        k_gain[None, :],
+        q_weight.shape[1],
+        kv_weight.shape[1],
+        width,
+    )
+    return (next_residual, queries, keys_values)
 
 
 def per_device(
@@ -122,8 +566,9 @@
 
 
 def solution(mesh):
+    small = mesh.shape["tensor"] == 2 and mesh.shape["expert"] == 4 * PLANE
     return jax.shard_map(
-        per_device,
+        per_device_dense if small else per_device,
         mesh=mesh,
         in_specs=(
             P("expert", "tensor"),

time: 309 us -> 162 us (0.52)
  waiting for transfers between devices: 197 us -> 39 us
  starting transfers between devices: 4.5 us -> 54.6 us
  blocking collectives: 37.2 us -> 9.96 us
  Pallas kernels: 0 us -> 23 us
  matrix products: 21.3 us -> 0 us
  other arithmetic: 12.2 us -> 0.86 us
    all_gather x2 -> x1, waiting for transfers between devices: 164 us -> 0.01 us  [per_device_dense(): lax.all_gather(q_weight, 'expert', axis=0, tiled=True, axis_index_groups=...]
    ppermute x0 -> x35, starting transfers between devices: none -> 54.6 us  [the longest x30 53.4 us: to_expert(): lax.ppermute(value, 'expert', [(i, i ^ offset) for i in range(n_expert)])]
    ppermute x0 -> x35, waiting for transfers between devices: none -> 38.9 us  [the longest x30 36.1 us: to_expert(): lax.ppermute(value, 'expert', [(i, i ^ offset) for i in range(n_expert)])]
    all_to_all x1 -> x0, blocking collectives: 33.4 us -> none  [per_device(): lax.all_to_all(outgoing, 'expert', split_axis=0, concat_axis=0, tiled=True)]
    pallas_call x0 -> x8, Pallas kernels: none -> 23 us  [the longest x1 7.65 us: experts(): pl.pallas_call(functools.partial(expert_kernel, len(blocks), chunk), out_...]
    dot_general x5 -> x0, matrix products: 21.3 us -> none  [the longest x1 5.84 us: per_device(): jnp.dot(attn_out, out_weight, preferred_element_type=jnp.float32)]
    all_to_all x1 -> x0, waiting for transfers between devices: 21 us -> none  [per_device(): lax.all_to_all(send_part, 'expert', split_axis=0, concat_axis=0, tiled=True)]
    unnamed x17 -> x78, local copies, waits for them, and re-layouts: 1.54 us -> 17.6 us
  transfers between devices with their start and end apart: 5 -> 36, of which waited for: 5 -> 19; matrix products, arithmetic and copies ran while one was open for 4% -> 2% of each run, Pallas kernels for 0% -> 12%
where the time goes in v1:
time: 162 us; the launch traced here: 161 us
  starting transfers between devices  54.6 us (34%)
  waiting for transfers between devices  39 us (24%)
  Pallas kernels  23 us (14%)
  local copies, waits for them, and re-layouts  19.3 us (12%)
  between operations  14.3 us (9%)
  blocking collectives  9.96 us (6%)
    ppermute x30, starting transfers between devices, to_expert(): lax.ppermute(value, 'expert', [(i, i ^ offset) for i in range(n_expert)])  53.4 us
    ppermute x30, waiting for transfers between devices, to_expert(): lax.ppermute(value, 'expert', [(i, i ^ offset) for i in range(n_expert)])  36.1 us
    unnamed x78, local copies, waits for them, and re-layouts  17.6 us
    all_gather x1, blocking collectives, per_device_dense(): lax.all_gather(kv_weight, 'expert', axis=0, tiled=True, axis_index_groups...  9.96 us
    pallas_call x1, Pallas kernels, experts(): pl.pallas_call(functools.partial(expert_kernel, len(blocks), chunk), out_...  7.65 us
    pallas_call x1, Pallas kernels, out_projection(): pl.pallas_call(functools.partial(out_projection_kernel, chunk), out_shape...  4.89 us
  transfers between devices with their start and end apart: 36, of which 19 were waited for; matrix products, arithmetic and copies ran while one was open for 2% of the time, Pallas kernels for 12%

profile of v1, /device:TPU:0, one launch (start us, length us, event | category | flops | bytes accessed | tf_op | source)
XLA Modules:
  0.0 161.0 jit_solution(17942542654936763770)
XLA Ops:
  8.4 3.4 %copy-done.1 = bf16[2048,2048]{1,0:T(8,128)(2,1)S(1)} copy-done((bf16[2048,2048]{1,0:T(8,128)(2,1)S(1)}, bf16[2048,2048]{1,0:T(8,128)(2,1)}, u32[]{:S(2)}) %copy-start.1) | copy-done | bytes 8388632
  12.7 4.9 %out_projection.1 = (f32[16,2048]{1,0:T(8,128)S(1)}, f32[16,2048]{1,0:T(8,128)S(1)}) custom-call(s32[4]{0:T(128)S(1)} %pad_add_fusion.pos_ref, bf16[32,2048]{1,0:T(8,128)(2,1)S(1)} %copy-done.8, bf16[2048,2048]{1,0:T(8,128)(2,1)S(1)} %copy-done.1), custom_call_target="tpu_custom_call" | custom-call | flops 268435456 | bytes 8388608 | tf_op jit(solution)/shard_map/out_projection/pallas_call | solution.py:52
  19.4 2.8 %collective-permute-done.theirs_ref = f32[16,2048]{1,0:T(8,128)S(1)} collective-permute-done((f32[16,2048]{1,0:T(8,128)S(1)}, f32[16,2048]{1,0:T(8,128)S(1)}, u32[]{:S(2)}, u32[]{:S(2)}) %collective-permute-start) | collective-permute-done | bytes 131104 | tf_op jit(solution)/shard_map/ppermute | solution.py:410
  24.8 4.0 %collective-permute-start.2 = (bf16[16,2176]{1,0:T(8,128)(2,1)}, bf16[16,2176]{1,0:T(8,128)(2,1)S(1)}, u32[]{:S(2)}, u32[]{:S(2)}) collective-permute-start(bf16[16,2176]{1,0:T(8,128)(2,1)} %get-tuple-element.31.refs_0_), channel_id=1, source_target_pairs={{0,16},{2,18},{4,20},{6,22},{8,24},{10,26},{12,28},{14,30},{16,0},... | collective-permute-start | bytes 208904 | tf_op jit(solution)/shard_map/ppermute | solution.py:413
  30.1 3.1 %collective-permute-done.2.refs_2_ = bf16[16,2176]{1,0:T(8,128)(2,1)S(1)} collective-permute-done((bf16[16,2176]{1,0:T(8,128)(2,1)}, bf16[16,2176]{1,0:T(8,128)(2,1)S(1)}, u32[]{:S(2)}, u32[]{:S(2)}) %collective-permute-start.2) | collective-permute-done | bytes 69664 | tf_op jit(solution)/shard_map/ppermute | solution.py:413
  33.2 2.2 %collective-permute-start.1 = (bf16[16,2176]{1,0:T(8,128)(2,1)}, bf16[16,2176]{1,0:T(8,128)(2,1)S(1)}, u32[]{:S(2)}, u32[]{:S(2)}) collective-permute-start(bf16[16,2176]{1,0:T(8,128)(2,1)} %get-tuple-element.31.refs_0_), channel_id=1, source_target_pairs={{0,8},{2,10},{4,12},{6,14},{8,0},{10,2},{12,4},{14,6},{16,24},{18,... | collective-permute-start | bytes 208904 | tf_op jit(solution)/shard_map/ppermute | solution.py:413
  35.4 2.4 %collective-permute-start.12 = (bf16[16,2176]{1,0:T(8,128)(2,1)}, bf16[16,2176]{1,0:T(8,128)(2,1)S(1)}, u32[]{:S(2)}, u32[]{:S(2)}) collective-permute-start(bf16[16,2176]{1,0:T(8,128)(2,1)} %get-tuple-element.31.refs_0_), channel_id=1, source_target_pairs={{0,6},{2,4},{4,2},{6,0},{8,14},{10,12},{12,10},{14,8},{16,22},{18,... | collective-permute-start | bytes 208904 | tf_op jit(solution)/shard_map/ppermute | solution.py:413
  37.8 2.5 %collective-permute-start.4 = (bf16[16,2176]{1,0:T(8,128)(2,1)}, bf16[16,2176]{1,0:T(8,128)(2,1)S(1)}, u32[]{:S(2)}, u32[]{:S(2)}) collective-permute-start(bf16[16,2176]{1,0:T(8,128)(2,1)} %get-tuple-element.31.refs_0_), channel_id=1, source_target_pairs={{0,2},{2,0},{4,6},{6,4},{8,10},{10,8},{12,14},{14,12},{16,18},{18,... | collective-permute-start | bytes 208904 | tf_op jit(solution)/shard_map/ppermute | solution.py:413
  40.3 2.7 %collective-permute-done.12.refs_12_ = bf16[16,2176]{1,0:T(8,128)(2,1)S(1)} collective-permute-done((bf16[16,2176]{1,0:T(8,128)(2,1)}, bf16[16,2176]{1,0:T(8,128)(2,1)S(1)}, u32[]{:S(2)}, u32[]{:S(2)}) %collective-permute-start.12) | collective-permute-done | bytes 69664 | tf_op jit(solution)/shard_map/ppermute | solution.py:413
  46.4 3.2 %collective-permute-done.8.refs_8_ = bf16[16,2176]{1,0:T(8,128)(2,1)S(1)} collective-permute-done((bf16[16,2176]{1,0:T(8,128)(2,1)}, bf16[16,2176]{1,0:T(8,128)(2,1)S(1)}, u32[]{:S(2)}, u32[]{:S(2)}) %collective-permute-start.8) | collective-permute-done | bytes 69664 | tf_op jit(solution)/shard_map/ppermute | solution.py:413
  54.6 2.2 %collective-permute-start.14 = (bf16[16,2176]{1,0:T(8,128)(2,1)S(1)}, bf16[16,2176]{1,0:T(8,128)(2,1)S(1)}, u32[]{:S(2)}, u32[]{:S(2)}) collective-permute-start(bf16[16,2176]{1,0:T(8,128)(2,1)S(1)} %collective-permute-done.2.refs_2_), channel_id=1, source_target_pairs={{0,6},{2,4},{4,2},{6,0},{8,14},{10,12},{12,10},{14,8},{16,22},{18,... | collective-permute-start | bytes 208904 | tf_op jit(solution)/shard_map/ppermute | solution.py:413
  69.2 2.7 %collective-permute-done.9.refs_9_ = bf16[16,2176]{1,0:T(8,128)(2,1)S(1)} collective-permute-done((bf16[16,2176]{1,0:T(8,128)(2,1)S(1)}, bf16[16,2176]{1,0:T(8,128)(2,1)S(1)}, u32[]{:S(2)}, u32[]{:S(2)}) %collective-permute-start.9) | collective-permute-done | bytes 69664 | tf_op jit(solution)/shard_map/ppermute | solution.py:413
  77.2 7.7 %experts.1 = (bf16[64,2048]{1,0:T(8,128)(2,1)S(1)}, bf16[64,2048]{1,0:T(8,128)(2,1)S(1)}, bf16[64,2048]{1,0:T(8,128)(2,1)S(1)}, bf16[64,2048]{1,0:T(8,128)(2,1)S(1)}) custom-call(s32[4]{0:T(128)S(1)} %copy-done.13, bf16[16,2176]{1,0:T(8,128)(2,1)S(1)} %copy-done.11, bf16[16,2176]{1,0:T(8,128)(2,1)S(1)} %collective-permute-done.1.refs_1_, ...), custom_call_target="tpu_custom_call" | custom-call | flops 4831838208 | bytes 18874368 | tf_op jit(solution)/shard_map/experts/pallas_call | solution.py:178
  89.0 2.9 %collective-permute-done.19.refs_1_ = bf16[64,2048]{1,0:T(8,128)(2,1)S(1)} collective-permute-done((bf16[64,2048]{1,0:T(8,128)(2,1)S(1)}, bf16[64,2048]{1,0:T(8,128)(2,1)S(1)}, u32[]{:S(2)}, u32[]{:S(2)}) %collective-permute-start.19) | collective-permute-done | bytes 262176 | tf_op jit(solution)/shard_map/ppermute | solution.py:413
  91.9 4.3 %collective-permute-done.20.refs_2_ = bf16[64,2048]{1,0:T(8,128)(2,1)S(1)} collective-permute-done((bf16[64,2048]{1,0:T(8,128)(2,1)S(1)}, bf16[64,2048]{1,0:T(8,128)(2,1)S(1)}, u32[]{:S(2)}, u32[]{:S(2)}) %collective-permute-start.20) | collective-permute-done | bytes 262176 | tf_op jit(solution)/shard_map/ppermute | solution.py:413
  97.0 2.2 %plane_sum.1 = (bf16[64,512]{1,0:T(8,128)(2,1)}, bf16[64,512]{1,0:T(8,128)(2,1)}, bf16[64,512]{1,0:T(8,128)(2,1)}, bf16[64,512]{1,0:T(8,128)(2,1)}) custom-call(s32[4]{0:T(128)} %copy-done.12, bf16[64,2048]{1,0:T(8,128)(2,1)} %copy-done.6, bf16[64,2048]{1,0:T(8,128)(2,1)} %copy-done.15, bf16[64,2048]{1,0:T(8,128)(2,1)} %copy-done.16, bf16[64,2048]{1,0:T(8,128)(2,1)} %copy-done.17), custom_call_target="tpu_custom_call" | custom-call | tf_op jit(solution)/shard_map/plane_sum/pallas_call | solution.py:226
  104.5 3.0 %collective-permute-start.26 = (bf16[16,512]{1,0:T(8,128)(2,1)S(1)}, bf16[16,512]{1,0:T(8,128)(2,1)S(1)}, u32[]{:S(2)}, u32[]{:S(2)}) collective-permute-start(bf16[16,512]{1,0:T(8,128)(2,1)S(1)} %copy-done.34), channel_id=1, source_target_pairs={{0,16},{2,18},{4,20},{6,22},{8,24},{10,26},{12,28},{14,30},{16,0},... | collective-permute-start | bytes 49160 | tf_op jit(solution)/shard_map/ppermute | solution.py:413
  107.5 3.2 %collective-permute-start.27 = (bf16[16,512]{1,0:T(8,128)(2,1)S(1)}, bf16[16,512]{1,0:T(8,128)(2,1)S(1)}, u32[]{:S(2)}, u32[]{:S(2)}) collective-permute-start(bf16[16,512]{1,0:T(8,128)(2,1)S(1)} %copy-done.33), channel_id=1, source_target_pairs={{0,24},{2,26},{4,28},{6,30},{8,16},{10,18},{12,20},{14,22},{16,8},... | collective-permute-start | bytes 49160 | tf_op jit(solution)/shard_map/ppermute | solution.py:413
  115.6 10.0 %all_gather.7.kv_ref = bf16[512,512]{1,0:T(8,128)(2,1)S(1)} all-gather(bf16[128,512]{1,0:T(8,128)(2,1)S(1)} %copy-done.21), channel_id=1, replica_groups={{0,2,4,6},{8,10,12,14},{16,18,20,22},{24,26,28,30},{1,3,5,7},{9,11,13,1..., dimensions={0}, use_global_device_ids=true | all-gather | bytes 655360 | tf_op jit(solution)/shard_map/all_gather | solution.py:423
  129.9 3.7 %collective-permute-start.33 = (bf16[32,2688]{1,0:T(8,128)(2,1)S(1)}, bf16[32,2688]{1,0:T(8,128)(2,1)S(1)}, u32[]{:S(2)}, u32[]{:S(2)}) collective-permute-start(bf16[32,2688]{1,0:T(8,128)(2,1)S(1)} %get-tuple-element.51), channel_id=1, source_target_pairs={{0,16},{2,18},{4,20},{6,22},{8,24},{10,26},{12,28},{14,30},{16,0},... | collective-permute-start | bytes 516104 | tf_op jit(solution)/shard_map/ppermute | solution.py:413
  134.3 3.7 %collective-permute-start.29 = (bf16[16,512]{1,0:T(8,128)(2,1)S(1)}, bf16[16,512]{1,0:T(8,128)(2,1)S(1)}, u32[]{:S(2)}, u32[]{:S(2)}) collective-permute-start(bf16[16,512]{1,0:T(8,128)(2,1)S(1)} %copy-done.37), channel_id=1, source_target_pairs={{0,16},{2,18},{4,20},{6,22},{8,24},{10,26},{12,28},{14,30},{16,0},... | collective-permute-start | bytes 49160 | tf_op jit(solution)/shard_map/ppermute | solution.py:413
  137.9 3.1 %collective-permute-done.28.refs_1_ = bf16[16,512]{1,0:T(8,128)(2,1)S(1)} collective-permute-done((bf16[16,512]{1,0:T(8,128)(2,1)S(1)}, bf16[16,512]{1,0:T(8,128)(2,1)S(1)}, u32[]{:S(2)}, u32[]{:S(2)}) %collective-permute-start.28) | collective-permute-done | bytes 16416 | tf_op jit(solution)/shard_map/ppermute | solution.py:413
  141.0 3.3 %collective-permute-start.30 = (bf16[16,512]{1,0:T(8,128)(2,1)S(1)}, bf16[16,512]{1,0:T(8,128)(2,1)S(1)}, u32[]{:S(2)}, u32[]{:S(2)}) collective-permute-start(bf16[16,512]{1,0:T(8,128)(2,1)S(1)} %copy-done.36), channel_id=1, source_target_pairs={{0,24},{2,26},{4,28},{6,30},{8,16},{10,18},{12,20},{14,22},{16,8},... | collective-permute-start | bytes 49160 | tf_op jit(solution)/shard_map/ppermute | solution.py:413
  144.3 4.9 %collective-permute-done.29.refs_2_ = bf16[16,512]{1,0:T(8,128)(2,1)S(1)} collective-permute-done((bf16[16,512]{1,0:T(8,128)(2,1)S(1)}, bf16[16,512]{1,0:T(8,128)(2,1)S(1)}, u32[]{:S(2)}, u32[]{:S(2)}) %collective-permute-start.29) | collective-permute-done | bytes 16416 | tf_op jit(solution)/shard_map/ppermute | solution.py:413
  (145 shorter events, 59.0 us)
Async XLA Ops:
  7.2 118.4 %all-gather.2.cloned.1.call-start = ((), (), s32[]{:S(2)}) async-start(), calls=%async_computation | async-start | bytes 2621440 | tf_op jit(solution)/shard_map/all_gather | solution.py:422
  7.2 64.6 %collective-permute-start.16 = (bf16[1,2048,768]{2,1,0:T(8,128)(2,1)}, bf16[1,2048,768]{2,1,0:T(8,128)(2,1)}, u32[]{:S(2)}, u32[]{:S(2)}) collective-permute-start(bf16[1,2048,768]{2,1,0:T(8,128)(2,1)} %refs_16_.1), channel_id=1, source_target_pairs={{0,1},{1,0},{2,3},{3,2},{4,5},{5,4},{6,7},{7,6},{8,9},{9,8},{10,11... | collective-permute-start | bytes 9437192 | tf_op jit(solution)/shard_map/ppermute | solution.py:410
  7.7 64.1 %collective-permute-start.17 = (bf16[1,2048,768]{2,1,0:T(8,128)(2,1)}, bf16[1,2048,768]{2,1,0:T(8,128)(2,1)}, u32[]{:S(2)}, u32[]{:S(2)}) collective-permute-start(bf16[1,2048,768]{2,1,0:T(8,128)(2,1)} %refs_17_.1), channel_id=1, source_target_pairs={{0,1},{1,0},{2,3},{3,2},{4,5},{5,4},{6,7},{7,6},{8,9},{9,8},{10,11... | collective-permute-start | bytes 9437192 | tf_op jit(solution)/shard_map/ppermute | solution.py:410
  7.8 64.0 %collective-permute-start.18 = (bf16[1,768,2048]{2,1,0:T(8,128)(2,1)}, bf16[1,768,2048]{2,1,0:T(8,128)(2,1)}, u32[]{:S(2)}, u32[]{:S(2)}) collective-permute-start(bf16[1,768,2048]{2,1,0:T(8,128)(2,1)} %refs_18_.1), channel_id=1, source_target_pairs={{0,1},{1,0},{2,3},{3,2},{4,5},{5,4},{6,7},{7,6},{8,9},{9,8},{10,11... | collective-permute-start | bytes 9437192 | tf_op jit(solution)/shard_map/ppermute | solution.py:410
  24.8 8.4 %collective-permute-start.2 = (bf16[16,2176]{1,0:T(8,128)(2,1)}, bf16[16,2176]{1,0:T(8,128)(2,1)S(1)}, u32[]{:S(2)}, u32[]{:S(2)}) collective-permute-start(bf16[16,2176]{1,0:T(8,128)(2,1)} %get-tuple-element.31.refs_0_), channel_id=1, source_target_pairs={{0,16},{2,18},{4,20},{6,22},{8,24},{10,26},{12,28},{14,30},{16,0},... | collective-permute-start | bytes 208904 | tf_op jit(solution)/shard_map/ppermute | solution.py:413
  28.8 6.6 %collective-permute-start.3 = (bf16[16,2176]{1,0:T(8,128)(2,1)}, bf16[16,2176]{1,0:T(8,128)(2,1)S(1)}, u32[]{:S(2)}, u32[]{:S(2)}) collective-permute-start(bf16[16,2176]{1,0:T(8,128)(2,1)} %get-tuple-element.31.refs_0_), channel_id=1, source_target_pairs={{0,24},{2,26},{4,28},{6,30},{8,16},{10,18},{12,20},{14,22},{16,8},... | collective-permute-start | bytes 208904 | tf_op jit(solution)/shard_map/ppermute | solution.py:413
  35.4 7.6 %collective-permute-start.12 = (bf16[16,2176]{1,0:T(8,128)(2,1)}, bf16[16,2176]{1,0:T(8,128)(2,1)S(1)}, u32[]{:S(2)}, u32[]{:S(2)}) collective-permute-start(bf16[16,2176]{1,0:T(8,128)(2,1)} %get-tuple-element.31.refs_0_), channel_id=1, source_target_pairs={{0,6},{2,4},{4,2},{6,0},{8,14},{10,12},{12,10},{14,8},{16,22},{18,... | collective-permute-start | bytes 208904 | tf_op jit(solution)/shard_map/ppermute | solution.py:413
  37.8 7.7 %collective-permute-start.4 = (bf16[16,2176]{1,0:T(8,128)(2,1)}, bf16[16,2176]{1,0:T(8,128)(2,1)S(1)}, u32[]{:S(2)}, u32[]{:S(2)}) collective-permute-start(bf16[16,2176]{1,0:T(8,128)(2,1)} %get-tuple-element.31.refs_0_), channel_id=1, source_target_pairs={{0,2},{2,0},{4,6},{6,4},{8,10},{10,8},{12,14},{14,12},{16,18},{18,... | collective-permute-start | bytes 208904 | tf_op jit(solution)/shard_map/ppermute | solution.py:413
  43.0 6.6 %collective-permute-start.8 = (bf16[16,2176]{1,0:T(8,128)(2,1)}, bf16[16,2176]{1,0:T(8,128)(2,1)S(1)}, u32[]{:S(2)}, u32[]{:S(2)}) collective-permute-start(bf16[16,2176]{1,0:T(8,128)(2,1)} %get-tuple-element.31.refs_0_), channel_id=1, source_target_pairs={{0,4},{2,6},{4,0},{6,2},{8,12},{10,14},{12,8},{14,10},{16,20},{18,... | collective-permute-start | bytes 208904 | tf_op jit(solution)/shard_map/ppermute | solution.py:413
  45.6 6.9 %collective-permute-start.10 = (bf16[16,2176]{1,0:T(8,128)(2,1)S(1)}, bf16[16,2176]{1,0:T(8,128)(2,1)S(1)}, u32[]{:S(2)}, u32[]{:S(2)}) collective-permute-start(bf16[16,2176]{1,0:T(8,128)(2,1)S(1)} %collective-permute-done.2.refs_2_), channel_id=1, source_target_pairs={{0,4},{2,6},{4,0},{6,2},{8,12},{10,14},{12,8},{14,10},{16,20},{18,... | collective-permute-start | bytes 208904 | tf_op jit(solution)/shard_map/ppermute | solution.py:413
  85.6 6.4 %collective-permute-start.19 = (bf16[64,2048]{1,0:T(8,128)(2,1)S(1)}, bf16[64,2048]{1,0:T(8,128)(2,1)S(1)}, u32[]{:S(2)}, u32[]{:S(2)}) collective-permute-start(bf16[64,2048]{1,0:T(8,128)(2,1)S(1)} %get-tuple-element.33), channel_id=1, source_target_pairs={{0,2},{2,0},{4,6},{6,4},{8,10},{10,8},{12,14},{14,12},{16,18},{18,... | collective-permute-start | bytes 786440 | tf_op jit(solution)/shard_map/ppermute | solution.py:413
  87.0 9.2 %collective-permute-start.20 = (bf16[64,2048]{1,0:T(8,128)(2,1)S(1)}, bf16[64,2048]{1,0:T(8,128)(2,1)S(1)}, u32[]{:S(2)}, u32[]{:S(2)}) collective-permute-start(bf16[64,2048]{1,0:T(8,128)(2,1)S(1)} %get-tuple-element.34), channel_id=1, source_target_pairs={{0,4},{2,6},{4,0},{6,2},{8,12},{10,14},{12,8},{14,10},{16,20},{18,... | collective-permute-start | bytes 786440 | tf_op jit(solution)/shard_map/ppermute | solution.py:413
  87.9 8.3 %collective-permute-start.21 = (bf16[64,2048]{1,0:T(8,128)(2,1)S(1)}, bf16[64,2048]{1,0:T(8,128)(2,1)S(1)}, u32[]{:S(2)}, u32[]{:S(2)}) collective-permute-start(bf16[64,2048]{1,0:T(8,128)(2,1)S(1)} %get-tuple-element.35), channel_id=1, source_target_pairs={{0,6},{2,4},{4,2},{6,0},{8,14},{10,12},{12,10},{14,8},{16,22},{18,... | collective-permute-start | bytes 786440 | tf_op jit(solution)/shard_map/ppermute | solution.py:413
  99.3 13.8 %collective-permute-start.22 = (bf16[64,512]{1,0:T(8,128)(2,1)}, bf16[64,512]{1,0:T(8,128)(2,1)S(1)}, u32[]{:S(2)}, u32[]{:S(2)}) collective-permute-start(bf16[64,512]{1,0:T(8,128)(2,1)} %get-tuple-element.37), channel_id=1, source_target_pairs={{0,8},{2,10},{4,12},{6,14},{8,0},{10,2},{12,4},{14,6},{16,24},{18,... | collective-permute-start | bytes 196616 | tf_op jit(solution)/shard_map/ppermute | solution.py:413
  101.0 12.1 %collective-permute-start.23 = (bf16[64,512]{1,0:T(8,128)(2,1)}, bf16[64,512]{1,0:T(8,128)(2,1)S(1)}, u32[]{:S(2)}, u32[]{:S(2)}) collective-permute-start(bf16[64,512]{1,0:T(8,128)(2,1)} %get-tuple-element.38), channel_id=1, source_target_pairs={{0,16},{2,18},{4,20},{6,22},{8,24},{10,26},{12,28},{14,30},{16,0},... | collective-permute-start | bytes 196616 | tf_op jit(solution)/shard_map/ppermute | solution.py:413
  103.1 10.0 %collective-permute-start.24 = (bf16[64,512]{1,0:T(8,128)(2,1)}, bf16[64,512]{1,0:T(8,128)(2,1)S(1)}, u32[]{:S(2)}, u32[]{:S(2)}) collective-permute-start(bf16[64,512]{1,0:T(8,128)(2,1)} %get-tuple-element.39), channel_id=1, source_target_pairs={{0,24},{2,26},{4,28},{6,30},{8,16},{10,18},{12,20},{14,22},{16,8},... | collective-permute-start | bytes 196616 | tf_op jit(solution)/shard_map/ppermute | solution.py:413
  104.5 7.5 %collective-permute-start.26 = (bf16[16,512]{1,0:T(8,128)(2,1)S(1)}, bf16[16,512]{1,0:T(8,128)(2,1)S(1)}, u32[]{:S(2)}, u32[]{:S(2)}) collective-permute-start(bf16[16,512]{1,0:T(8,128)(2,1)S(1)} %copy-done.34), channel_id=1, source_target_pairs={{0,16},{2,18},{4,20},{6,22},{8,24},{10,26},{12,28},{14,30},{16,0},... | collective-permute-start | bytes 49160 | tf_op jit(solution)/shard_map/ppermute | solution.py:413
  115.6 10.1 %collective-permute-start.31 = (bf16[64,640]{1,0:T(8,128)(2,1)}, bf16[64,640]{1,0:T(8,128)(2,1)S(1)}, u32[]{:S(2)}, u32[]{:S(2)}) collective-permute-start(bf16[64,640]{1,0:T(8,128)(2,1)} %get-tuple-element.48.mine_ref), channel_id=1, source_target_pairs={{0,1},{1,0},{2,3},{3,2},{4,5},{5,4},{6,7},{7,6},{8,9},{9,8},{10,11... | collective-permute-start | bytes 245768 | tf_op jit(solution)/shard_map/ppermute | solution.py:410
  129.9 21.4 %collective-permute-start.32 = (bf16[32,2688]{1,0:T(8,128)(2,1)S(1)}, bf16[32,2688]{1,0:T(8,128)(2,1)S(1)}, u32[]{:S(2)}, u32[]{:S(2)}) collective-permute-start(bf16[32,2688]{1,0:T(8,128)(2,1)S(1)} %get-tuple-element.50), channel_id=1, source_target_pairs={{0,8},{2,10},{4,12},{6,14},{8,0},{10,2},{12,4},{14,6},{16,24},{18,... | collective-permute-start | bytes 516104 | tf_op jit(solution)/shard_map/ppermute | solution.py:413
  129.9 21.4 %collective-permute-start.33 = (bf16[32,2688]{1,0:T(8,128)(2,1)S(1)}, bf16[32,2688]{1,0:T(8,128)(2,1)S(1)}, u32[]{:S(2)}, u32[]{:S(2)}) collective-permute-start(bf16[32,2688]{1,0:T(8,128)(2,1)S(1)} %get-tuple-element.51), channel_id=1, source_target_pairs={{0,16},{2,18},{4,20},{6,22},{8,24},{10,26},{12,28},{14,30},{16,0},... | collective-permute-start | bytes 516104 | tf_op jit(solution)/shard_map/ppermute | solution.py:413
  133.5 17.8 %collective-permute-start.34 = (bf16[32,2688]{1,0:T(8,128)(2,1)S(1)}, bf16[32,2688]{1,0:T(8,128)(2,1)S(1)}, u32[]{:S(2)}, u32[]{:S(2)}) collective-permute-start(bf16[32,2688]{1,0:T(8,128)(2,1)S(1)} %get-tuple-element.52), channel_id=1, source_target_pairs={{0,24},{2,26},{4,28},{6,30},{8,16},{10,18},{12,20},{14,22},{16,8},... | collective-permute-start | bytes 516104 | tf_op jit(solution)/shard_map/ppermute | solution.py:413
  134.2 6.7 %collective-permute-start.28 = (bf16[16,512]{1,0:T(8,128)(2,1)S(1)}, bf16[16,512]{1,0:T(8,128)(2,1)S(1)}, u32[]{:S(2)}, u32[]{:S(2)}) collective-permute-start(bf16[16,512]{1,0:T(8,128)(2,1)S(1)} %copy-done.38), channel_id=1, source_target_pairs={{0,8},{2,10},{4,12},{6,14},{8,0},{10,2},{12,4},{14,6},{16,24},{18,... | collective-permute-start | bytes 49160 | tf_op jit(solution)/shard_map/ppermute | solution.py:413
  134.3 15.0 %collective-permute-start.29 = (bf16[16,512]{1,0:T(8,128)(2,1)S(1)}, bf16[16,512]{1,0:T(8,128)(2,1)S(1)}, u32[]{:S(2)}, u32[]{:S(2)}) collective-permute-start(bf16[16,512]{1,0:T(8,128)(2,1)S(1)} %copy-done.37), channel_id=1, source_target_pairs={{0,16},{2,18},{4,20},{6,22},{8,24},{10,26},{12,28},{14,30},{16,0},... | collective-permute-start | bytes 49160 | tf_op jit(solution)/shard_map/ppermute | solution.py:413
  141.0 8.2 %collective-permute-start.30 = (bf16[16,512]{1,0:T(8,128)(2,1)S(1)}, bf16[16,512]{1,0:T(8,128)(2,1)S(1)}, u32[]{:S(2)}, u32[]{:S(2)}) collective-permute-start(bf16[16,512]{1,0:T(8,128)(2,1)S(1)} %copy-done.36), channel_id=1, source_target_pairs={{0,24},{2,26},{4,28},{6,30},{8,16},{10,18},{12,20},{14,22},{16,8},... | collective-permute-start | bytes 49160 | tf_op jit(solution)/shard_map/ppermute | solution.py:413
  (51 other events, 520.1 us)
Sparse Core Ops, SparseCore 0:
  9.9 43.2 all-gather.1

commit v2 on v0

--- a/solution.py
+++ b/solution.py
@@ -1,17 +1,502 @@
+import functools
+
 import jax
 import jax.numpy as jnp
 from jax import lax
+from jax.experimental import pallas as pl
+from jax.experimental.pallas import tpu as pltpu
 from jax.sharding import PartitionSpec as P
 
 KV_HEADS = 4
 TOP = 8
+PLANE = 4
+META = 128
 
 
 EPSILON = 1e-06
+
+VMEM = pl.BlockSpec(memory_space=pltpu.VMEM)
+HBM = pl.BlockSpec(memory_space=pltpu.HBM)
 
 
 def normalize(values, gain):
     return values * lax.rsqrt(jnp.mean(values * values, axis=-1, keepdims=True) + EPSILON) * gain
+
+
+def params(mebibytes):
+    return pltpu.CompilerParams(vmem_limit_bytes=mebibytes << 20)
+
+
+def lanes(start, size):
+    return pl.ds(pl.multiple_of(start, size), size)
+
+
+def out_projection_kernel(chunk, a_hbm, w_hbm, mine_ref, theirs_ref, a_buf, w_buf, a_sem, sems):
+    width = w_buf.shape[1]
+    count = width // chunk
+    half = mine_ref.shape[0]
+    a_copy = pltpu.make_async_copy(a_hbm, a_buf, a_sem)
+    a_copy.start()
+    copies = []
+    for i in range(count):
+        cols = pl.ds(i * chunk, chunk)
+        copies.append(pltpu.make_async_copy(w_hbm.at[:, cols], w_buf.at[:, cols], sems.at[i]))
+    for copy in copies:
+        copy.start()
+    tensor = lax.axis_index("tensor")
+    a_copy.wait()
+    own = a_buf[lanes(tensor * half, half), :]
+    other = a_buf[lanes((1 - tensor) * half, half), :]
+    both = jnp.concatenate([own, other], axis=0)
+    for i in range(count):
+        copies[i].wait()
+        cols = pl.ds(i * chunk, chunk)
+        product = jnp.dot(both, w_buf[:, cols], preferred_element_type=jnp.float32)
+        mine_ref[:, cols] = product[:half]
+        theirs_ref[:, cols] = product[half:]
+
+
+def out_projection(attn_out, out_weight):
+    rows, depth = attn_out.shape
+    width = out_weight.shape[1]
+    chunk = 256
+    half = jax.ShapeDtypeStruct((rows // 2, width), jnp.float32)
+    return pl.pallas_call(
+        functools.partial(out_projection_kernel, chunk),
+        out_shape=(half, half),
+        in_specs=[HBM, HBM],
+        out_specs=(VMEM, VMEM),
+        scratch_shapes=[
+            pltpu.VMEM((rows, depth), jnp.bfloat16),
+            pltpu.VMEM((depth, width), jnp.bfloat16),
+            pltpu.SemaphoreType.DMA,
+            pltpu.SemaphoreType.DMA((width // chunk,)),
+        ],
+        compiler_params=params(14),
+        cost_estimate=pl.CostEstimate(
+            flops=2 * rows * depth * width, bytes_accessed=2 * depth * width, transcendentals=0
+        ),
+        name="out_projection",
+    )(attn_out, out_weight)
+
+
+def first_norm_kernel(
+    depth, mine_ref, theirs_ref, residual_ref, gain_ref, meta_ref, tokens_ref, *refs
+):
+    slice_refs, first_ref = refs[:PLANE], refs[PLANE]
+    rows, width = residual_ref.shape
+    sub = width // (PLANE * depth)
+    first = (residual_ref[...].astype(jnp.float32) + (mine_ref[...] + theirs_ref[...])).astype(
+        jnp.bfloat16
+    )
+    first_ref[...] = first
+    tokens_ref[:, :width] = normalize(first.astype(jnp.float32), gain_ref[...]).astype(jnp.bfloat16)
+    tokens_ref[:, width:] = meta_ref[...]
+    plane = lax.axis_index("expert") % PLANE
+    for d in range(PLANE):
+        for z in range(depth):
+            slice_refs[d][z * rows : (z + 1) * rows, :] = first_ref[
+                :, lanes((z * PLANE + (plane ^ d)) * sub, sub)
+            ]
+
+
+def first_norm(mine, theirs, residual, gain, meta, depth):
+    rows, width = residual.shape
+    piece = jax.ShapeDtypeStruct((depth * rows, width // (PLANE * depth)), jnp.bfloat16)
+    return pl.pallas_call(
+        functools.partial(first_norm_kernel, depth),
+        out_shape=(jax.ShapeDtypeStruct((rows, width + META), jnp.bfloat16),) + (piece,) * PLANE,
+        in_specs=[VMEM] * 5,
+        out_specs=(VMEM,) * (1 + PLANE),
+        scratch_shapes=[pltpu.VMEM((rows, width), jnp.bfloat16)],
+        compiler_params=params(2),
+        name="first_norm",
+    )(mine, theirs, residual, gain, meta)
+
+
+def pack_kernel(depth, *refs):
+    line, pieces, out_refs = refs[:depth], refs[depth : depth + PLANE - 1], refs[depth + PLANE - 1 :]
+    rows, extended = line[0].shape
+    for ref, piece in zip(out_refs, pieces):
+        for z in range(depth):
+            ref[z * rows : (z + 1) * rows, :extended] = line[z][...]
+        ref[:, extended:] = piece[...]
+
+
+def pack(line, pieces):
+    depth = len(line)
+    rows, extended = line[0].shape
+    shape = jax.ShapeDtypeStruct((depth * rows, extended + pieces[0].shape[1]), jnp.bfloat16)
+    return pl.pallas_call(
+        functools.partial(pack_kernel, depth),
+        out_shape=(shape,) * (PLANE - 1),
+        in_specs=[VMEM] * (depth + PLANE - 1),
+        out_specs=(VMEM,) * (PLANE - 1),
+        compiler_params=params(2),
+        name="pack_tokens",
+    )(*line, *pieces)
+
+
+def expert_kernel(depth, chunk, *refs):
+    line, packed = refs[:depth], refs[depth : depth + PLANE - 1]
+    at = depth + PLANE - 1
+    weight_refs, out_refs = refs[at : at + 6], refs[at + 6 : at + 6 + PLANE]
+    x_buf, gate_buf, up_buf, down_buf, act_buf, sems = refs[at + 6 + PLANE :]
+    width, hidden = gate_buf.shape[1], gate_buf.shape[2]
+    rows, extended = line[0].shape
+    per = hidden // chunk
+    gate_copies, down_copies = [], []
+    for side in range(2):
+        gate_ref, up_ref, down_ref = weight_refs[3 * side : 3 * side + 3]
+        for i in range(per):
+            cols = pl.ds(i * chunk, chunk)
+            j = side * per + i
+            gate_copies.append(
+                (
+                    pltpu.make_async_copy(
+                        gate_ref.at[0, :, cols], gate_buf.at[side, :, cols], sems.at[0, j]
+                    ),
+                    pltpu.make_async_copy(
+                        up_ref.at[0, :, cols], up_buf.at[side, :, cols], sems.at[1, j]
+                    ),
+                )
+            )
+            down_copies.append(
+                pltpu.make_async_copy(
+                    down_ref.at[0, pl.ds(i * chunk, chunk), :],
+                    down_buf.at[pl.ds(j * chunk, chunk), :],
+                    sems.at[2, j],
+                )
+            )
+    for pair in gate_copies:
+        pair[0].start()
+        pair[1].start()
+    for copy in down_copies:
+        copy.start()
+    group = depth * rows
+    for z in range(depth):
+        x_buf[z * rows : (z + 1) * rows, :] = line[z][...]
+    for d in range(1, PLANE):
+        x_buf[d * group : (d + 1) * group, :] = packed[d - 1][:, :extended]
+    meta = x_buf[:, width:].astype(jnp.float32)
+    lane = lax.broadcasted_iota(jnp.int32, meta.shape, 1)
+    chip = lax.axis_index("expert")
+    tensor = lax.axis_index("tensor")
+    for side in range(2):
+        expert = 2 * chip + (tensor if side == 0 else 1 - tensor)
+        chosen = (lane == expert) | (lane == expert + META // 2)
+        route = jnp.sum(jnp.where(chosen, meta, 0.0), axis=1, keepdims=True)
+        for i in range(per):
+            j = side * per + i
+            gate_copies[j][0].wait()
+            gate_copies[j][1].wait()
+            cols = pl.ds(i * chunk, chunk)
+            x = x_buf[:, :width]
+            gate = jnp.dot(x, gate_buf[side, :, cols], preferred_element_type=jnp.float32)
+            up = jnp.dot(x, up_buf[side, :, cols], preferred_element_type=jnp.float32)
+            act = gate / (1.0 + jnp.exp(-gate)) * up * route
+            act_buf[:, j * chunk : (j + 1) * chunk] = act.astype(jnp.bfloat16)
+    for copy in down_copies:
+        copy.wait()
+    sub = width // (PLANE * depth)
+    plane = chip % PLANE
+    for d in range(PLANE):
+        weight = jnp.concatenate(
+            [
+                down_buf[:, lanes((z * PLANE + (plane ^ d)) * sub, sub)]
+                for z in range(depth)
+            ],
+            axis=1,
+        )
+        out = jnp.dot(act_buf[...], weight, preferred_element_type=jnp.float32)
+        for k in range(PLANE):
+            out_refs[d][k * group : (k + 1) * group, :] = out[
+                (d ^ k) * group : ((d ^ k) + 1) * group
+            ].astype(jnp.bfloat16)
+
+
+def experts(line, packed, weights):
+    depth = len(line)
+    rows, extended = line[0].shape
+    width, hidden = weights[0].shape[1:]
+    chunk = 256
+    total = rows * depth * PLANE
+    return pl.pallas_call(
+        functools.partial(expert_kernel, depth, chunk),
+        out_shape=(jax.ShapeDtypeStruct((total, width // PLANE), jnp.bfloat16),) * PLANE,
+        in_specs=[VMEM] * (depth + PLANE - 1) + [HBM] * 6,
+        out_specs=(VMEM,) * PLANE,
+        scratch_shapes=[
+            pltpu.VMEM((total, extended), jnp.bfloat16),
+            pltpu.VMEM((2, width, hidden), jnp.bfloat16),
+            pltpu.VMEM((2, width, hidden), jnp.bfloat16),
+            pltpu.VMEM((2 * hidden, width), jnp.bfloat16),
+            pltpu.VMEM((total, 2 * hidden), jnp.bfloat16),
+            pltpu.SemaphoreType.DMA((3, 2 * (hidden // chunk))),
+        ],
+        compiler_params=params(32),
+        cost_estimate=pl.CostEstimate(
+            flops=12 * total * width * hidden,
+            bytes_accessed=12 * width * hidden,
+            transcendentals=2 * total * hidden,
+        ),
+        name="experts",
+    )(*line, *packed, *weights)
+
+
+def plane_sum_kernel(depth, *refs):
+    in_refs, out_refs = refs[:PLANE], refs[PLANE:]
+    rows = in_refs[0].shape[0] // (PLANE * depth)
+    for d in range(PLANE):
+        for z in range(depth):
+            start = (d * depth + z) * rows
+            at = slice(start, start + rows)
+            total = in_refs[0][at, :].astype(jnp.float32)
+            for ref in in_refs[1:]:
+                total = total + ref[at, :].astype(jnp.float32)
+            out_refs[z][d * rows : (d + 1) * rows, :] = total.astype(jnp.bfloat16)
+
+
+def plane_sum(parts, depth):
+    rows, part = parts[0].shape
+    return pl.pallas_call(
+        functools.partial(plane_sum_kernel, depth),
+        out_shape=(jax.ShapeDtypeStruct((rows // depth, part), jnp.bfloat16),) * depth,
+        in_specs=[VMEM] * PLANE,
+        out_specs=(VMEM,) * depth,
+        compiler_params=params(4),
+        name="plane_sum",
+    )(*parts)
+
+
+def second_norm_kernel(depth, *refs):
+    parts, first_ref, packed = refs[:depth], refs[depth], refs[depth + 1 : depth + PLANE]
+    gain_ref, scaled_ref, next_ref = refs[depth + PLANE :]
+    rows = first_ref.shape[0] // depth
+    sub = first_ref.shape[1]
+    part = depth * sub
+    lane = lax.broadcasted_iota(jnp.int32, (rows, META), 1)
+    plane = lax.axis_index("expert") % PLANE
+    gain = jnp.concatenate(
+        [gain_ref[:, lanes((z * PLANE + plane) * sub, sub)] for z in range(depth)], axis=1
+    )
+    for d in range(PLANE):
+        at = slice(d * rows, (d + 1) * rows)
+        total = parts[0][at, :].astype(jnp.float32)
+        for ref in parts[1:]:
+            total = total + ref[at, :].astype(jnp.float32)
+        source = first_ref if d == 0 else packed[d - 1]
+        skip = source.shape[1] - sub
+        first = jnp.concatenate(
+            [source[z * rows : (z + 1) * rows, skip:] for z in range(depth)], axis=1
+        )
+        following = (first.astype(jnp.float32) + total).astype(jnp.bfloat16)
+        next_ref[at, :] = following
+        wide = following.astype(jnp.float32)
+        scaled_ref[at, :part] = (wide * gain).astype(jnp.bfloat16)
+        squares = jnp.sum(wide * wide, axis=1, keepdims=True)
+        high = squares.astype(jnp.bfloat16).astype(jnp.float32)
+        low = squares - high
+        scaled_ref[at, part:] = jnp.where(
+            lane == 0, high, jnp.where(lane == 1, low, 0.0)
+        ).astype(jnp.bfloat16)
+
+
+def second_norm(parts, first, packed, gain):
+    depth = len(parts)
+    rows, part = parts[0].shape
+    return pl.pallas_call(
+        functools.partial(second_norm_kernel, depth),
+        out_shape=(
+            jax.ShapeDtypeStruct((rows, part + META), jnp.bfloat16),
+            jax.ShapeDtypeStruct((rows, part), jnp.bfloat16),
+        ),
+        in_specs=[VMEM] * (depth + PLANE + 1),
+        out_specs=(VMEM, VMEM),
+        compiler_params=params(4),
+        name="second_norm",
+    )(*parts, first, *packed, gain)
+
+
+def projection_kernel(chunk, mine_ref, theirs_ref, next_ref, w_hbm, *refs):
+    out_refs, (w_buf, sems) = refs[:PLANE], refs[PLANE:]
+    cols = w_buf.shape[1]
+    copies = []
+    for i in range(cols // chunk):
+        at = pl.ds(i * chunk, chunk)
+        copies.append(pltpu.make_async_copy(w_hbm.at[:, at], w_buf.at[:, at], sems.at[i]))
+    for copy in copies:
+        copy.start()
+    rows, extended = mine_ref.shape
+    part = extended - META
+    block = rows // PLANE
+    tensor = lax.axis_index("tensor")
+    own = lanes(tensor * block, block)
+    other = lanes((1 - tensor) * block, block)
+    for d in range(PLANE):
+        at = slice(d * block, (d + 1) * block)
+        out_refs[d][own, cols : cols + META] = mine_ref[at, part:]
+        out_refs[d][other, cols : cols + META] = theirs_ref[at, part:]
+        out_refs[d][:block, cols + META :] = next_ref[at, : part // 2]
+        out_refs[d][block:, cols + META :] = next_ref[at, part // 2 :]
+    both = jnp.concatenate([mine_ref[:, :part], theirs_ref[:, :part]], axis=0)
+    for i in range(cols // chunk):
+        copies[i].wait()
+        at = slice(i * chunk, (i + 1) * chunk)
+        product = jnp.dot(both, w_buf[:, at], preferred_element_type=jnp.float32).astype(
+            jnp.bfloat16
+        )
+        for d in range(PLANE):
+            out_refs[d][own, at] = product[d * block : (d + 1) * block]
+            out_refs[d][other, at] = product[rows + d * block : rows + (d + 1) * block]
+
+
+def projection(mine, theirs, following, weight):
+    rows, part = following.shape
+    cols = weight.shape[1]
+    chunk = 512
+    shape = jax.ShapeDtypeStruct((2 * rows // PLANE, cols + META + part // 2), jnp.bfloat16)
+    return pl.pallas_call(
+        functools.partial(projection_kernel, chunk),
+        out_shape=(shape,) * PLANE,
+        in_specs=[VMEM] * 3 + [HBM],
+        out_specs=(VMEM,) * PLANE,
+        scratch_shapes=[
+            pltpu.VMEM((part, cols), jnp.bfloat16),
+            pltpu.SemaphoreType.DMA((cols // chunk,)),
+        ],
+        compiler_params=params(8),
+        cost_estimate=pl.CostEstimate(
+            flops=4 * rows * part * cols, bytes_accessed=2 * part * cols, transcendentals=0
+        ),
+        name="qkv_projection",
+    )(mine, theirs, following, weight)
+
+
+def head_norm_kernel(depth, *refs):
+    parts, q_gain_ref, k_gain_ref = refs[:PLANE], refs[PLANE], refs[PLANE + 1]
+    next_ref, q_ref, kv_ref = refs[PLANE + 2 :]
+    width = next_ref.shape[1]
+    q_cols, kv_cols = q_ref.shape[1], kv_ref.shape[1]
+    cols = q_cols + kv_cols
+    head = q_gain_ref.shape[1]
+
+    def total(at):
+        value = parts[0][:, at].astype(jnp.float32)
+        for ref in parts[1:]:
+            value = value + ref[:, at].astype(jnp.float32)
+        return value
+
+    squares = jnp.sum(total(slice(cols, cols + META)), axis=1, keepdims=True)
+    scale = lax.rsqrt(squares / width + EPSILON)
+    for h in range(q_cols // head):
+        at = slice(h * head, (h + 1) * head)
+        q_ref[:, at] = normalize(total(at) * scale, q_gain_ref[...]).astype(jnp.bfloat16)
+    tensor = lax.axis_index("tensor")
+    for h in range(kv_cols // head):
+        at = slice(h * head, (h + 1) * head)
+        raw = total(slice(q_cols + h * head, q_cols + (h + 1) * head)) * scale
+        is_key = tensor * (kv_cols // head) + h < KV_HEADS
+        kv_ref[:, at] = jnp.where(is_key, normalize(raw, k_gain_ref[...]), raw).astype(
+            jnp.bfloat16
+        )
+    plane = lax.axis_index("expert") % PLANE
+    rows = next_ref.shape[0]
+    sub = width // (PLANE * depth)
+    for d in range(PLANE):
+        for z in range(depth):
+            top = z * sub * 2 // (depth * sub)
+            start = cols + META + z * sub - top * (depth * sub // 2)
+            next_ref[:, lanes((z * PLANE + (plane ^ d)) * sub, sub)] = parts[d][
+                top * rows : (top + 1) * rows, start : start + sub
+            ]
+
+
+def head_norm(parts, q_gain, k_gain, q_cols, kv_cols, rows, width, depth):
+    both = parts[0].shape[0]
+    return pl.pallas_call(
+        functools.partial(head_norm_kernel, depth),
+        out_shape=(
+            jax.ShapeDtypeStruct((rows, width), jnp.bfloat16),
+            jax.ShapeDtypeStruct((both, q_cols), jnp.bfloat16),
+            jax.ShapeDtypeStruct((both, kv_cols), jnp.bfloat16),
+        ),
+        in_specs=[VMEM] * (PLANE + 2),
+        out_specs=(VMEM, VMEM, VMEM),
+        compiler_params=params(4),
+        name="head_norm",
+    )(*parts, q_gain, k_gain)
+
+
+def per_device_dense(
+    attn_out,
+    out_weight,
+    residual,
+    attn_gain,
+    expert_ids,
+    route_weights,
+    w_gate,
+    w_up,
+    w_down,
+    input_gain,
+    q_weight,
+    kv_weight,
+    q_gain,
+    k_gain,
+):
+    n_expert = lax.axis_size("expert")
+    depth = n_expert // PLANE
+    rows, width = residual.shape
+    tensor_index = lax.axis_index("tensor").astype(jnp.int32)
+
+    def to_core(value):
+        return lax.ppermute(value, "tensor", [(0, 1), (1, 0)])
+
+    def to_expert(value, offset):
+        return lax.ppermute(value, "expert", [(i, i ^ offset) for i in range(n_expert)])
+
+    def to_z(values):
+        return [to_expert(v, d * PLANE) if d else v for d, v in enumerate(values)]
+
+    def to_plane(values):
+        return [to_expert(v, d) if d else v for d, v in enumerate(values)]
+
+    lines = [list(range(i, n_expert, PLANE)) for i in range(PLANE)]
+    qkv = lax.all_gather(
+        jnp.concatenate([q_weight, kv_weight], axis=1),
+        "expert",
+        axis=0,
+        tiled=True,
+        axis_index_groups=lines,
+    )
+    weights = (w_gate, w_up, w_down, to_core(w_gate), to_core(w_up), to_core(w_down))
+
+    own_ids = lax.dynamic_slice_in_dim(expert_ids, tensor_index * rows, rows, 0)
+    own_route = lax.dynamic_slice_in_dim(route_weights, tensor_index * rows, rows, 0)
+    chosen = own_ids[:, :, None] == jnp.arange(META // 2, dtype=jnp.int32)[None, None, :]
+    dense = jnp.sum(jnp.where(chosen, own_route[:, :, None], 0.0), axis=1)
+    high = lax.reduce_precision(dense, 8, 7)
+    meta = jnp.concatenate([high, dense - high], axis=1).astype(jnp.bfloat16)
+
+    mine, theirs = out_projection(attn_out, out_weight)
+    tokens, *firsts = first_norm(
+        mine, to_core(theirs), residual, attn_gain[None, :], meta, depth
+    )
+    line = to_z([tokens] * depth)
+    packed = to_plane([None, *pack(line, firsts[1:])])[1:]
+    parts = plane_sum(to_plane(experts(line, packed, weights)), depth)
+    scaled, following = second_norm(to_z(parts), firsts[0], packed, input_gain[None, :])
+    products = to_plane(projection(scaled, to_core(scaled), following, qkv))
+    return head_norm(
+        products,
+        q_gain[None, :],
+        k_gain[None, :],
+        q_weight.shape[1],
+        kv_weight.shape[1],
+        rows,
+        width,
+        depth,
+    )
 
 
 def per_device(
@@ -122,8 +607,9 @@
 
 
 def solution(mesh):
+    small = mesh.shape["tensor"] == 2 and mesh.shape["expert"] == 4 * PLANE
     return jax.shard_map(
-        per_device,
+        per_device_dense if small else per_device,
         mesh=mesh,
         in_specs=(
             P("expert", "tensor"),

time: 309 us -> 117 us (0.38)
  waiting for transfers between devices: 197 us -> 42.4 us
  blocking collectives: 37.2 us -> 0 us
  starting transfers between devices: 4.5 us -> 31.1 us
  matrix products: 21.3 us -> 0 us
  Pallas kernels: 0 us -> 16.7 us
  local copies, waits for them, and re-layouts: 20.8 us -> 10.1 us
  other arithmetic: 12.2 us -> 2.23 us
    all_gather x2 -> x1, waiting for transfers between devices: 164 us -> 0.01 us  [per_device_dense(): lax.all_gather(jnp.concatenate([q_weight, kv_weight], axis=1), 'expert',...]
    ppermute x0 -> x20, waiting for transfers between devices: none -> 42.4 us  [the longest x15 40.1 us: to_expert(): lax.ppermute(value, 'expert', [(i, i ^ offset) for i in range(n_expert)])]
    all_to_all x1 -> x0, blocking collectives: 33.4 us -> none  [per_device(): lax.all_to_all(outgoing, 'expert', split_axis=0, concat_axis=0, tiled=True)]
    ppermute x0 -> x20, starting transfers between devices: none -> 31.1 us  [the longest x15 29.8 us: to_expert(): lax.ppermute(value, 'expert', [(i, i ^ offset) for i in range(n_expert)])]
    dot_general x5 -> x0, matrix products: 21.3 us -> none  [the longest x1 5.84 us: per_device(): jnp.dot(attn_out, out_weight, preferred_element_type=jnp.float32)]
    all_to_all x1 -> x0, waiting for transfers between devices: 21 us -> none  [per_device(): lax.all_to_all(send_part, 'expert', split_axis=0, concat_axis=0, tiled=True)]
    pallas_call x0 -> x8, Pallas kernels: none -> 16.7 us  [the longest x1 7.78 us: experts(): pl.pallas_call(functools.partial(expert_kernel, depth, chunk), out_shape=...]
    reduce_scatter x2 -> x0, waiting for transfers between devices: 10.5 us -> none  [the longest x1 6.26 us: per_device(): lax.psum_scatter(jnp.dot(attn_out, out_weight, preferred_element_type=jnp...]
  transfers between devices with their start and end apart: 5 -> 21, of which waited for: 5 -> 14; matrix products, arithmetic and copies ran while one was open for 4% -> 2% of each run, Pallas kernels for 0% -> 12%
where the time goes in v2:
time: 117 us
  waiting for transfers between devices  42.4 us (36%)
  starting transfers between devices  31.1 us (27%)
  Pallas kernels  16.7 us (14%)
  between operations  14.2 us (12%)
  local copies, waits for them, and re-layouts  10.1 us (9%)
  other arithmetic  2.23 us (2%)
    ppermute x15, waiting for transfers between devices, to_expert(): lax.ppermute(value, 'expert', [(i, i ^ offset) for i in range(n_expert)])  40.1 us
    ppermute x15, starting transfers between devices, to_expert(): lax.ppermute(value, 'expert', [(i, i ^ offset) for i in range(n_expert)])  29.8 us
    unnamed x26, local copies, waits for them, and re-layouts  9.84 us
    pallas_call x1, Pallas kernels, experts(): pl.pallas_call(functools.partial(expert_kernel, depth, chunk), out_shape=...  7.78 us
    pallas_call x1, Pallas kernels, out_projection(): pl.pallas_call(functools.partial(out_projection_kernel, chunk), out_shape...  6.17 us
  transfers between devices with their start and end apart: 21, of which 14 were waited for; matrix products, arithmetic and copies ran while one was open for 2% of the time, Pallas kernels for 12%

profile of v2, /device:TPU:0, one launch (start us, length us, event | category | flops | bytes accessed | tf_op | source)
XLA Modules:
  0.0 116.8 jit_solution(8108039662685953577)
XLA Ops:
  8.3 2.0 %pad_maximum_fusion = bf16[128,2560]{1,0:T(8,128)(2,1)} fusion(bf16[128,512]{1,0:T(8,128)(2,1)} %param.25, bf16[128,2048]{1,0:T(8,128)(2,1)} %param.24), kind=kLoop, calls=%fused_computation | loop fusion | flops 1310720 | bytes 1310720 | tf_op jit(solution)/shard_map/concatenate | solution.py:466
  10.3 3.4 %copy-done.1 = bf16[2048,2048]{1,0:T(8,128)(2,1)S(1)} copy-done((bf16[2048,2048]{1,0:T(8,128)(2,1)S(1)}, bf16[2048,2048]{1,0:T(8,128)(2,1)}, u32[]{:S(2)}) %copy-start.1) | copy-done | bytes 8388632
  14.6 6.2 %out_projection.1 = (f32[16,2048]{1,0:T(8,128)S(1)}, f32[16,2048]{1,0:T(8,128)}) custom-call(bf16[32,2048]{1,0:T(8,128)(2,1)S(1)} %copy-done.6, bf16[2048,2048]{1,0:T(8,128)(2,1)S(1)} %copy-done.1), custom_call_target="tpu_custom_call" | custom-call | flops 268435456 | bytes 8388608 | tf_op jit(solution)/shard_map/out_projection/pallas_call | solution.py:64
  22.6 3.0 %collective-permute-start.1 = (bf16[16,2176]{1,0:T(8,128)(2,1)S(1)}, bf16[16,2176]{1,0:T(8,128)(2,1)S(1)}, u32[]{:S(2)}, u32[]{:S(2)}) collective-permute-start(bf16[16,2176]{1,0:T(8,128)(2,1)S(1)} %get-tuple-element.29.refs_0_), channel_id=1, source_target_pairs={{0,8},{2,10},{4,12},{6,14},{8,0},{10,2},{12,4},{14,6},{16,24},{18,... | collective-permute-start | bytes 208904 | tf_op jit(solution)/shard_map/ppermute | solution.py:456
  25.6 2.6 %collective-permute-start.2 = (bf16[16,2176]{1,0:T(8,128)(2,1)S(1)}, bf16[16,2176]{1,0:T(8,128)(2,1)S(1)}, u32[]{:S(2)}, u32[]{:S(2)}) collective-permute-start(bf16[16,2176]{1,0:T(8,128)(2,1)S(1)} %get-tuple-element.29.refs_0_), channel_id=1, source_target_pairs={{0,16},{2,18},{4,20},{6,22},{8,24},{10,26},{12,28},{14,30},{16,0},... | collective-permute-start | bytes 208904 | tf_op jit(solution)/shard_map/ppermute | solution.py:456
  28.2 5.6 %collective-permute-done.1.refs_1_ = bf16[16,2176]{1,0:T(8,128)(2,1)S(1)} collective-permute-done((bf16[16,2176]{1,0:T(8,128)(2,1)S(1)}, bf16[16,2176]{1,0:T(8,128)(2,1)S(1)}, u32[]{:S(2)}, u32[]{:S(2)}) %collective-permute-start.1) | collective-permute-done | bytes 69664 | tf_op jit(solution)/shard_map/ppermute | solution.py:456
  33.7 3.1 %collective-permute-start.3 = (bf16[16,2176]{1,0:T(8,128)(2,1)S(1)}, bf16[16,2176]{1,0:T(8,128)(2,1)S(1)}, u32[]{:S(2)}, u32[]{:S(2)}) collective-permute-start(bf16[16,2176]{1,0:T(8,128)(2,1)S(1)} %get-tuple-element.29.refs_0_), channel_id=1, source_target_pairs={{0,24},{2,26},{4,28},{6,30},{8,16},{10,18},{12,20},{14,22},{16,8},... | collective-permute-start | bytes 208904 | tf_op jit(solution)/shard_map/ppermute | solution.py:456
  36.9 4.6 %collective-permute-done.3.refs_3_ = bf16[16,2176]{1,0:T(8,128)(2,1)S(1)} collective-permute-done((bf16[16,2176]{1,0:T(8,128)(2,1)S(1)}, bf16[16,2176]{1,0:T(8,128)(2,1)S(1)}, u32[]{:S(2)}, u32[]{:S(2)}) %collective-permute-start.3) | collective-permute-done | bytes 69664 | tf_op jit(solution)/shard_map/ppermute | solution.py:456
  41.6 2.0 %collective-permute-start.4 = (bf16[64,2304]{1,0:T(8,128)(2,1)S(1)}, bf16[64,2304]{1,0:T(8,128)(2,1)S(1)}, u32[]{:S(2)}, u32[]{:S(2)}) collective-permute-start(bf16[64,2304]{1,0:T(8,128)(2,1)S(1)} %get-tuple-element.33), channel_id=1, source_target_pairs={{0,2},{2,0},{4,6},{6,4},{8,10},{10,8},{12,14},{14,12},{16,18},{18,... | collective-permute-start | bytes 884744 | tf_op jit(solution)/shard_map/ppermute | solution.py:456
  45.1 4.0 %collective-permute-done.4.refs_4_.refs_5_ = bf16[64,2304]{1,0:T(8,128)(2,1)S(1)} collective-permute-done((bf16[64,2304]{1,0:T(8,128)(2,1)S(1)}, bf16[64,2304]{1,0:T(8,128)(2,1)S(1)}, u32[]{:S(2)}, u32[]{:S(2)}) %collective-permute-start.4) | collective-permute-done | bytes 294944 | tf_op jit(solution)/shard_map/ppermute | solution.py:456
  49.1 2.9 %collective-permute-start.6 = (bf16[64,2304]{1,0:T(8,128)(2,1)S(1)}, bf16[64,2304]{1,0:T(8,128)(2,1)S(1)}, u32[]{:S(2)}, u32[]{:S(2)}) collective-permute-start(bf16[64,2304]{1,0:T(8,128)(2,1)S(1)} %get-tuple-element.35), channel_id=1, source_target_pairs={{0,6},{2,4},{4,2},{6,0},{8,14},{10,12},{12,10},{14,8},{16,22},{18,... | collective-permute-start | bytes 884744 | tf_op jit(solution)/shard_map/ppermute | solution.py:456
  52.0 4.9 %collective-permute-done.6.refs_6_.refs_7_ = bf16[64,2304]{1,0:T(8,128)(2,1)S(1)} collective-permute-done((bf16[64,2304]{1,0:T(8,128)(2,1)S(1)}, bf16[64,2304]{1,0:T(8,128)(2,1)S(1)}, u32[]{:S(2)}, u32[]{:S(2)}) %collective-permute-start.6) | collective-permute-done | bytes 294944 | tf_op jit(solution)/shard_map/ppermute | solution.py:456
  56.9 1.9 %copy-done.3 = bf16[1,2048,768]{2,1,0:T(8,128)(2,1)S(1)} copy-done((bf16[1,2048,768]{2,1,0:T(8,128)(2,1)S(1)}, bf16[1,2048,768]{2,1,0:T(8,128)(2,1)}, u32[]{:S(2)}) %copy-start.3) | copy-done | bytes 3145752
  58.8 1.9 %copy-done.4 = bf16[1,768,2048]{2,1,0:T(8,128)(2,1)S(1)} copy-done((bf16[1,768,2048]{2,1,0:T(8,128)(2,1)S(1)}, bf16[1,768,2048]{2,1,0:T(8,128)(2,1)}, u32[]{:S(2)}) %copy-start.4) | copy-done | bytes 3145752
  60.7 7.8 %experts.1 = (bf16[256,512]{1,0:T(8,128)(2,1)S(1)}, bf16[256,512]{1,0:T(8,128)(2,1)S(1)}, bf16[256,512]{1,0:T(8,128)(2,1)S(1)}, bf16[256,512]{1,0:T(8,128)(2,1)S(1)}) custom-call(bf16[16,2176]{1,0:T(8,128)(2,1)S(1)} %get-tuple-element.29.refs_0_, bf16[16,2176]{1,0:T(8,128)(2,1)S(1)} %collective-permute-done.1.refs_1_, ...), custom_call_target="tpu_custom_call" | custom-call | flops 4831838208 | bytes 18874368 | tf_op jit(solution)/shard_map/experts/pallas_call | solution.py:224
  72.1 4.7 %collective-permute-done.10.refs_1_ = bf16[256,512]{1,0:T(8,128)(2,1)S(1)} collective-permute-done((bf16[256,512]{1,0:T(8,128)(2,1)S(1)}, bf16[256,512]{1,0:T(8,128)(2,1)S(1)}, u32[]{:S(2)}, u32[]{:S(2)}) %collective-permute-start.10) | collective-permute-done | bytes 262176 | tf_op jit(solution)/shard_map/ppermute | solution.py:456
  76.8 4.0 %collective-permute-done.11.refs_2_ = bf16[256,512]{1,0:T(8,128)(2,1)S(1)} collective-permute-done((bf16[256,512]{1,0:T(8,128)(2,1)S(1)}, bf16[256,512]{1,0:T(8,128)(2,1)S(1)}, u32[]{:S(2)}, u32[]{:S(2)}) %collective-permute-start.11) | collective-permute-done | bytes 262176 | tf_op jit(solution)/shard_map/ppermute | solution.py:456
  80.9 5.2 %collective-permute-start.13 = (bf16[64,512]{1,0:T(8,128)(2,1)S(1)}, bf16[64,512]{1,0:T(8,128)(2,1)S(1)}, u32[]{:S(2)}, u32[]{:S(2)}) collective-permute-start(bf16[64,512]{1,0:T(8,128)(2,1)S(1)} %get-tuple-element.41), channel_id=1, source_target_pairs={{0,8},{2,10},{4,12},{6,14},{8,0},{10,2},{12,4},{14,6},{16,24},{18,... | collective-permute-start | bytes 196616 | tf_op jit(solution)/shard_map/ppermute | solution.py:456
  86.2 2.4 %collective-permute-start.15 = (bf16[64,512]{1,0:T(8,128)(2,1)S(1)}, bf16[64,512]{1,0:T(8,128)(2,1)S(1)}, u32[]{:S(2)}, u32[]{:S(2)}) collective-permute-start(bf16[64,512]{1,0:T(8,128)(2,1)S(1)} %get-tuple-element.43), channel_id=1, source_target_pairs={{0,24},{2,26},{4,28},{6,30},{8,16},{10,18},{12,20},{14,22},{16,8},... | collective-permute-start | bytes 196616 | tf_op jit(solution)/shard_map/ppermute | solution.py:456
  88.6 2.9 %collective-permute-done.14.refs_2_ = bf16[64,512]{1,0:T(8,128)(2,1)S(1)} collective-permute-done((bf16[64,512]{1,0:T(8,128)(2,1)S(1)}, bf16[64,512]{1,0:T(8,128)(2,1)S(1)}, u32[]{:S(2)}, u32[]{:S(2)}) %collective-permute-start.14) | collective-permute-done | bytes 65568 | tf_op jit(solution)/shard_map/ppermute | solution.py:456
  93.8 1.7 %copy-done.5 = bf16[512,2560]{1,0:T(8,128)(2,1)S(1)} copy-done((bf16[512,2560]{1,0:T(8,128)(2,1)S(1)}, bf16[512,2560]{1,0:T(8,128)(2,1)}, u32[]{:S(2)}) %copy-start.5) | copy-done | bytes 2621464
  100.6 4.1 %collective-permute-done.17.refs_1_ = bf16[32,2944]{1,0:T(8,128)(2,1)S(1)} collective-permute-done((bf16[32,2944]{1,0:T(8,128)(2,1)S(1)}, bf16[32,2944]{1,0:T(8,128)(2,1)S(1)}, u32[]{:S(2)}, u32[]{:S(2)}) %collective-permute-start.17) | collective-permute-done | bytes 188448 | tf_op jit(solution)/shard_map/ppermute | solution.py:456
  104.6 2.6 %collective-permute-done.18.refs_2_ = bf16[32,2944]{1,0:T(8,128)(2,1)S(1)} collective-permute-done((bf16[32,2944]{1,0:T(8,128)(2,1)S(1)}, bf16[32,2944]{1,0:T(8,128)(2,1)S(1)}, u32[]{:S(2)}, u32[]{:S(2)}) %collective-permute-start.18) | collective-permute-done | bytes 188448 | tf_op jit(solution)/shard_map/ppermute | solution.py:456
  107.3 1.8 %collective-permute-done.19.refs_3_ = bf16[32,2944]{1,0:T(8,128)(2,1)S(1)} collective-permute-done((bf16[32,2944]{1,0:T(8,128)(2,1)S(1)}, bf16[32,2944]{1,0:T(8,128)(2,1)S(1)}, u32[]{:S(2)}, u32[]{:S(2)}) %collective-permute-start.19) | collective-permute-done | bytes 188448 | tf_op jit(solution)/shard_map/ppermute | solution.py:456
  (61 shorter events, 17.4 us)
Async XLA Ops:
  7.2 86.7 %all-gather.2.cloned.1.call-start = ((), (), s32[]{:S(2)}) async-start(), calls=%async_computation | async-start | bytes 3276800 | tf_op jit(solution)/shard_map/all_gather | solution.py:465
  7.2 49.7 %collective-permute-start.7 = (bf16[1,2048,768]{2,1,0:T(8,128)(2,1)}, bf16[1,2048,768]{2,1,0:T(8,128)(2,1)}, u32[]{:S(2)}, u32[]{:S(2)}) collective-permute-start(bf16[1,2048,768]{2,1,0:T(8,128)(2,1)} %refs_7_.1), channel_id=1, source_target_pairs={{0,1},{1,0},{2,3},{3,2},{4,5},{5,4},{6,7},{7,6},{8,9},{9,8},{10,11... | collective-permute-start | bytes 9437192 | tf_op jit(solution)/shard_map/ppermute | solution.py:453
  7.7 49.2 %collective-permute-start.8 = (bf16[1,2048,768]{2,1,0:T(8,128)(2,1)}, bf16[1,2048,768]{2,1,0:T(8,128)(2,1)}, u32[]{:S(2)}, u32[]{:S(2)}) collective-permute-start(bf16[1,2048,768]{2,1,0:T(8,128)(2,1)} %refs_8_.1), channel_id=1, source_target_pairs={{0,1},{1,0},{2,3},{3,2},{4,5},{5,4},{6,7},{7,6},{8,9},{9,8},{10,11... | collective-permute-start | bytes 9437192 | tf_op jit(solution)/shard_map/ppermute | solution.py:453
  7.8 49.1 %collective-permute-start.9 = (bf16[1,768,2048]{2,1,0:T(8,128)(2,1)}, bf16[1,768,2048]{2,1,0:T(8,128)(2,1)}, u32[]{:S(2)}, u32[]{:S(2)}) collective-permute-start(bf16[1,768,2048]{2,1,0:T(8,128)(2,1)} %refs_9_.1), channel_id=1, source_target_pairs={{0,1},{1,0},{2,3},{3,2},{4,5},{5,4},{6,7},{7,6},{8,9},{9,8},{10,11... | collective-permute-start | bytes 9437192 | tf_op jit(solution)/shard_map/ppermute | solution.py:453
  14.6 42.3 %copy-start.2 = (bf16[1,2048,768]{2,1,0:T(8,128)(2,1)S(1)}, bf16[1,2048,768]{2,1,0:T(8,128)(2,1)}, u32[]{:S(2)}) copy-start(bf16[1,2048,768]{2,1,0:T(8,128)(2,1)} %refs_7_.1) | copy-start | bytes 9437188
  20.8 1.6 %collective-permute-start = (f32[16,2048]{1,0:T(8,128)}, f32[16,2048]{1,0:T(8,128)S(1)}, u32[]{:S(2)}, u32[]{:S(2)}) collective-permute-start(f32[16,2048]{1,0:T(8,128)} %get-tuple-element.28), channel_id=1, source_target_pairs={{0,1},{1,0},{2,3},{3,2},{4,5},{5,4},{6,7},{7,6},{8,9},{9,8},{10,11... | collective-permute-start | bytes 393224 | tf_op jit(solution)/shard_map/ppermute | solution.py:453
  22.6 11.2 %collective-permute-start.1 = (bf16[16,2176]{1,0:T(8,128)(2,1)S(1)}, bf16[16,2176]{1,0:T(8,128)(2,1)S(1)}, u32[]{:S(2)}, u32[]{:S(2)}) collective-permute-start(bf16[16,2176]{1,0:T(8,128)(2,1)S(1)} %get-tuple-element.29.refs_0_), channel_id=1, source_target_pairs={{0,8},{2,10},{4,12},{6,14},{8,0},{10,2},{12,4},{14,6},{16,24},{18,... | collective-permute-start | bytes 208904 | tf_op jit(solution)/shard_map/ppermute | solution.py:456
  25.6 11.3 %collective-permute-start.2 = (bf16[16,2176]{1,0:T(8,128)(2,1)S(1)}, bf16[16,2176]{1,0:T(8,128)(2,1)S(1)}, u32[]{:S(2)}, u32[]{:S(2)}) collective-permute-start(bf16[16,2176]{1,0:T(8,128)(2,1)S(1)} %get-tuple-element.29.refs_0_), channel_id=1, source_target_pairs={{0,16},{2,18},{4,20},{6,22},{8,24},{10,26},{12,28},{14,30},{16,0},... | collective-permute-start | bytes 208904 | tf_op jit(solution)/shard_map/ppermute | solution.py:456
  33.7 7.8 %collective-permute-start.3 = (bf16[16,2176]{1,0:T(8,128)(2,1)S(1)}, bf16[16,2176]{1,0:T(8,128)(2,1)S(1)}, u32[]{:S(2)}, u32[]{:S(2)}) collective-permute-start(bf16[16,2176]{1,0:T(8,128)(2,1)S(1)} %get-tuple-element.29.refs_0_), channel_id=1, source_target_pairs={{0,24},{2,26},{4,28},{6,30},{8,16},{10,18},{12,20},{14,22},{16,8},... | collective-permute-start | bytes 208904 | tf_op jit(solution)/shard_map/ppermute | solution.py:456
  41.6 7.6 %collective-permute-start.4 = (bf16[64,2304]{1,0:T(8,128)(2,1)S(1)}, bf16[64,2304]{1,0:T(8,128)(2,1)S(1)}, u32[]{:S(2)}, u32[]{:S(2)}) collective-permute-start(bf16[64,2304]{1,0:T(8,128)(2,1)S(1)} %get-tuple-element.33), channel_id=1, source_target_pairs={{0,2},{2,0},{4,6},{6,4},{8,10},{10,8},{12,14},{14,12},{16,18},{18,... | collective-permute-start | bytes 884744 | tf_op jit(solution)/shard_map/ppermute | solution.py:456
  43.5 8.5 %collective-permute-start.5 = (bf16[64,2304]{1,0:T(8,128)(2,1)S(1)}, bf16[64,2304]{1,0:T(8,128)(2,1)S(1)}, u32[]{:S(2)}, u32[]{:S(2)}) collective-permute-start(bf16[64,2304]{1,0:T(8,128)(2,1)S(1)} %get-tuple-element.34), channel_id=1, source_target_pairs={{0,4},{2,6},{4,0},{6,2},{8,12},{10,14},{12,8},{14,10},{16,20},{18,... | collective-permute-start | bytes 884744 | tf_op jit(solution)/shard_map/ppermute | solution.py:456
  49.1 7.8 %collective-permute-start.6 = (bf16[64,2304]{1,0:T(8,128)(2,1)S(1)}, bf16[64,2304]{1,0:T(8,128)(2,1)S(1)}, u32[]{:S(2)}, u32[]{:S(2)}) collective-permute-start(bf16[64,2304]{1,0:T(8,128)(2,1)S(1)} %get-tuple-element.35), channel_id=1, source_target_pairs={{0,6},{2,4},{4,2},{6,0},{8,14},{10,12},{12,10},{14,8},{16,22},{18,... | collective-permute-start | bytes 884744 | tf_op jit(solution)/shard_map/ppermute | solution.py:456
  68.5 40.5 %copy-start.10 = (f32[128]{0:T(128)S(1)}, f32[128]{0:T(128)}, u32[]{:S(2)}) copy-start(f32[128]{0:T(128)} %param.26) | copy-start | bytes 1540
  68.5 40.5 %copy-start.11 = (f32[128]{0:T(128)S(1)}, f32[128]{0:T(128)}, u32[]{:S(2)}) copy-start(f32[128]{0:T(128)} %param.27) | copy-start | bytes 1540
  68.5 8.3 %collective-permute-start.10 = (bf16[256,512]{1,0:T(8,128)(2,1)S(1)}, bf16[256,512]{1,0:T(8,128)(2,1)S(1)}, u32[]{:S(2)}, u32[]{:S(2)}) collective-permute-start(bf16[256,512]{1,0:T(8,128)(2,1)S(1)} %get-tuple-element.37), channel_id=1, source_target_pairs={{0,2},{2,0},{4,6},{6,4},{8,10},{10,8},{12,14},{14,12},{16,18},{18,... | collective-permute-start | bytes 786440 | tf_op jit(solution)/shard_map/ppermute | solution.py:456
  70.2 10.6 %collective-permute-start.11 = (bf16[256,512]{1,0:T(8,128)(2,1)S(1)}, bf16[256,512]{1,0:T(8,128)(2,1)S(1)}, u32[]{:S(2)}, u32[]{:S(2)}) collective-permute-start(bf16[256,512]{1,0:T(8,128)(2,1)S(1)} %get-tuple-element.38), channel_id=1, source_target_pairs={{0,4},{2,6},{4,0},{6,2},{8,12},{10,14},{12,8},{14,10},{16,20},{18,... | collective-permute-start | bytes 786440 | tf_op jit(solution)/shard_map/ppermute | solution.py:456
  71.9 8.9 %collective-permute-start.12 = (bf16[256,512]{1,0:T(8,128)(2,1)S(1)}, bf16[256,512]{1,0:T(8,128)(2,1)S(1)}, u32[]{:S(2)}, u32[]{:S(2)}) collective-permute-start(bf16[256,512]{1,0:T(8,128)(2,1)S(1)} %get-tuple-element.39), channel_id=1, source_target_pairs={{0,6},{2,4},{4,2},{6,0},{8,14},{10,12},{12,10},{14,8},{16,22},{18,... | collective-permute-start | bytes 786440 | tf_op jit(solution)/shard_map/ppermute | solution.py:456
  80.9 7.7 %collective-permute-start.13 = (bf16[64,512]{1,0:T(8,128)(2,1)S(1)}, bf16[64,512]{1,0:T(8,128)(2,1)S(1)}, u32[]{:S(2)}, u32[]{:S(2)}) collective-permute-start(bf16[64,512]{1,0:T(8,128)(2,1)S(1)} %get-tuple-element.41), channel_id=1, source_target_pairs={{0,8},{2,10},{4,12},{6,14},{8,0},{10,2},{12,4},{14,6},{16,24},{18,... | collective-permute-start | bytes 196616 | tf_op jit(solution)/shard_map/ppermute | solution.py:456
  86.2 5.4 %collective-permute-start.14 = (bf16[64,512]{1,0:T(8,128)(2,1)S(1)}, bf16[64,512]{1,0:T(8,128)(2,1)S(1)}, u32[]{:S(2)}, u32[]{:S(2)}) collective-permute-start(bf16[64,512]{1,0:T(8,128)(2,1)S(1)} %get-tuple-element.42), channel_id=1, source_target_pairs={{0,16},{2,18},{4,20},{6,22},{8,24},{10,26},{12,28},{14,30},{16,0},... | collective-permute-start | bytes 196616 | tf_op jit(solution)/shard_map/ppermute | solution.py:456
  86.2 6.2 %collective-permute-start.15 = (bf16[64,512]{1,0:T(8,128)(2,1)S(1)}, bf16[64,512]{1,0:T(8,128)(2,1)S(1)}, u32[]{:S(2)}, u32[]{:S(2)}) collective-permute-start(bf16[64,512]{1,0:T(8,128)(2,1)S(1)} %get-tuple-element.43), channel_id=1, source_target_pairs={{0,24},{2,26},{4,28},{6,30},{8,16},{10,18},{12,20},{14,22},{16,8},... | collective-permute-start | bytes 196616 | tf_op jit(solution)/shard_map/ppermute | solution.py:456
  92.5 1.3 %collective-permute-start.16 = (bf16[64,640]{1,0:T(8,128)(2,1)S(1)}, bf16[64,640]{1,0:T(8,128)(2,1)S(1)}, u32[]{:S(2)}, u32[]{:S(2)}) collective-permute-start(bf16[64,640]{1,0:T(8,128)(2,1)S(1)} %get-tuple-element.45.mine_ref), channel_id=1, source_target_pairs={{0,1},{1,0},{2,3},{3,2},{4,5},{5,4},{6,7},{7,6},{8,9},{9,8},{10,11... | collective-permute-start | bytes 245768 | tf_op jit(solution)/shard_map/ppermute | solution.py:453
  97.0 7.6 %collective-permute-start.17 = (bf16[32,2944]{1,0:T(8,128)(2,1)S(1)}, bf16[32,2944]{1,0:T(8,128)(2,1)S(1)}, u32[]{:S(2)}, u32[]{:S(2)}) collective-permute-start(bf16[32,2944]{1,0:T(8,128)(2,1)S(1)} %get-tuple-element.48), channel_id=1, source_target_pairs={{0,2},{2,0},{4,6},{6,4},{8,10},{10,8},{12,14},{14,12},{16,18},{18,... | collective-permute-start | bytes 565256 | tf_op jit(solution)/shard_map/ppermute | solution.py:456
  98.5 8.8 %collective-permute-start.18 = (bf16[32,2944]{1,0:T(8,128)(2,1)S(1)}, bf16[32,2944]{1,0:T(8,128)(2,1)S(1)}, u32[]{:S(2)}, u32[]{:S(2)}) collective-permute-start(bf16[32,2944]{1,0:T(8,128)(2,1)S(1)} %get-tuple-element.49), channel_id=1, source_target_pairs={{0,4},{2,6},{4,0},{6,2},{8,12},{10,14},{12,8},{14,10},{16,20},{18,... | collective-permute-start | bytes 565256 | tf_op jit(solution)/shard_map/ppermute | solution.py:456
  99.2 9.9 %collective-permute-start.19 = (bf16[32,2944]{1,0:T(8,128)(2,1)S(1)}, bf16[32,2944]{1,0:T(8,128)(2,1)S(1)}, u32[]{:S(2)}, u32[]{:S(2)}) collective-permute-start(bf16[32,2944]{1,0:T(8,128)(2,1)S(1)} %get-tuple-element.50), channel_id=1, source_target_pairs={{0,6},{2,4},{4,2},{6,0},{8,14},{10,12},{12,10},{14,8},{16,22},{18,... | collective-permute-start | bytes 565256 | tf_op jit(solution)/shard_map/ppermute | solution.py:456
  (10 other events, 77.4 us)
Sparse Core Ops, SparseCore 0:
  10.4 63.0 all-gather.1

commit v3 on v2

--- a/solution.py
+++ b/solution.py
@@ -31,7 +31,12 @@
     return pl.ds(pl.multiple_of(start, size), size)
 
 
-def out_projection_kernel(chunk, a_hbm, w_hbm, mine_ref, theirs_ref, a_buf, w_buf, a_sem, sems):
+def out_projection_kernel(
+    chunk, start, side_count, a_hbm, w_hbm, *refs
+):
+    side_refs, (mine_ref, theirs_ref) = refs[:side_count], refs[side_count : side_count + 2]
+    joined = refs[side_count + 2 : -5]
+    a_buf, w_buf, a_sem, sems, side_sems = refs[-5:]
     width = w_buf.shape[1]
     count = width // chunk
     half = mine_ref.shape[0]
@@ -39,9 +44,23 @@
     a_copy.start()
     copies = []
     for i in range(count):
-        cols = pl.ds(i * chunk, chunk)
-        copies.append(pltpu.make_async_copy(w_hbm.at[:, cols], w_buf.at[:, cols], sems.at[i]))
+        copies.append(
+            pltpu.make_async_copy(
+                w_hbm.at[:, pl.ds(start + i * chunk, chunk)],
+                w_buf.at[:, pl.ds(i * chunk, chunk)],
+                sems.at[i],
+            )
+        )
     for copy in copies:
+        copy.start()
+    side_copies, at = [], 0
+    for i, ref in enumerate(side_refs):
+        cols = ref.shape[1]
+        side_copies.append(
+            pltpu.make_async_copy(ref, joined[0].at[:, pl.ds(at, cols)], side_sems.at[i])
+        )
+        at += cols
+    for copy in side_copies:
         copy.start()
     tensor = lax.axis_index("tensor")
     a_copy.wait()
@@ -54,42 +73,52 @@
         product = jnp.dot(both, w_buf[:, cols], preferred_element_type=jnp.float32)
         mine_ref[:, cols] = product[:half]
         theirs_ref[:, cols] = product[half:]
-
-
-def out_projection(attn_out, out_weight):
+    for copy in side_copies:
+        copy.wait()
+
+
+def out_projection(attn_out, out_weight, start, width, side=()):
     rows, depth = attn_out.shape
-    width = out_weight.shape[1]
     chunk = 256
     half = jax.ShapeDtypeStruct((rows // 2, width), jnp.float32)
-    return pl.pallas_call(
-        functools.partial(out_projection_kernel, chunk),
-        out_shape=(half, half),
-        in_specs=[HBM, HBM],
-        out_specs=(VMEM, VMEM),
+    joined = ()
+    if side:
+        cols = sum(array.shape[1] for array in side)
+        joined = (jax.ShapeDtypeStruct((side[0].shape[0], cols), side[0].dtype),)
+    return pl.pallas_call(
+        functools.partial(out_projection_kernel, chunk, start, len(side)),
+        out_shape=(half, half) + joined,
+        in_specs=[HBM, HBM] + [HBM] * len(side),
+        out_specs=(VMEM, VMEM) + (HBM,) * len(joined),
         scratch_shapes=[
             pltpu.VMEM((rows, depth), jnp.bfloat16),
             pltpu.VMEM((depth, width), jnp.bfloat16),
             pltpu.SemaphoreType.DMA,
             pltpu.SemaphoreType.DMA((width // chunk,)),
+            pltpu.SemaphoreType.DMA((2,)),
         ],
-        compiler_params=params(14),
+        compiler_params=params(60),
         cost_estimate=pl.CostEstimate(
             flops=2 * rows * depth * width, bytes_accessed=2 * depth * width, transcendentals=0
         ),
         name="out_projection",
-    )(attn_out, out_weight)
-
-
-def first_norm_kernel(
-    depth, mine_ref, theirs_ref, residual_ref, gain_ref, meta_ref, tokens_ref, *refs
-):
-    slice_refs, first_ref = refs[:PLANE], refs[PLANE]
+    )(attn_out, out_weight, *side)
+
+
+def first_norm_kernel(depth, count, *refs):
+    mine, theirs = refs[:count], refs[count : 2 * count]
+    residual_ref, gain_ref, meta_ref, tokens_ref = refs[2 * count : 2 * count + 4]
+    slice_refs, first_ref = refs[2 * count + 4 : -1], refs[-1]
     rows, width = residual_ref.shape
     sub = width // (PLANE * depth)
-    first = (residual_ref[...].astype(jnp.float32) + (mine_ref[...] + theirs_ref[...])).astype(
-        jnp.bfloat16
-    )
-    first_ref[...] = first
+    start = 0
+    for mine_ref, theirs_ref in zip(mine, theirs):
+        cols = slice(start, start + mine_ref.shape[1])
+        start += mine_ref.shape[1]
+        first_ref[:, cols] = (
+            residual_ref[:, cols].astype(jnp.float32) + (mine_ref[...] + theirs_ref[...])
+        ).astype(jnp.bfloat16)
+    first = first_ref[...]
     tokens_ref[:, :width] = normalize(first.astype(jnp.float32), gain_ref[...]).astype(jnp.bfloat16)
     tokens_ref[:, width:] = meta_ref[...]
     plane = lax.axis_index("expert") % PLANE
@@ -104,14 +133,14 @@
     rows, width = residual.shape
     piece = jax.ShapeDtypeStruct((depth * rows, width // (PLANE * depth)), jnp.bfloat16)
     return pl.pallas_call(
-        functools.partial(first_norm_kernel, depth),
+        functools.partial(first_norm_kernel, depth, len(mine)),
         out_shape=(jax.ShapeDtypeStruct((rows, width + META), jnp.bfloat16),) + (piece,) * PLANE,
-        in_specs=[VMEM] * 5,
+        in_specs=[VMEM] * (2 * len(mine) + 3),
         out_specs=(VMEM,) * (1 + PLANE),
         scratch_shapes=[pltpu.VMEM((rows, width), jnp.bfloat16)],
         compiler_params=params(2),
         name="first_norm",
-    )(mine, theirs, residual, gain, meta)
+    )(*mine, *theirs, residual, gain, meta)
 
 
 def pack_kernel(depth, *refs):
@@ -137,42 +166,59 @@
     )(*line, *pieces)
 
 
+def load_kernel(*refs):
+    sources, targets, sems = refs[:3], refs[-4:-1], refs[-1]
+    copies = [
+        pltpu.make_async_copy(source, target, sems.at[i])
+        for i, (source, target) in enumerate(zip(sources, targets))
+    ]
+    for copy in copies:
+        copy.start()
+    for copy in copies:
+        copy.wait()
+
+
+def load(weights, after):
+    size = sum(w.size for w in weights)
+    return pl.pallas_call(
+        load_kernel,
+        out_shape=tuple(jax.ShapeDtypeStruct(w.shape, w.dtype) for w in weights),
+        in_specs=[HBM] * 3 + [pl.BlockSpec(memory_space=pl.ANY)] * len(after),
+        out_specs=(VMEM,) * 3,
+        scratch_shapes=[pltpu.SemaphoreType.DMA((3,))],
+        compiler_params=params(46),
+        cost_estimate=pl.CostEstimate(flops=0, bytes_accessed=4 * size, transcendentals=0),
+        name="load_weights",
+    )(*weights, *after)
+
+
 def expert_kernel(depth, chunk, *refs):
     line, packed = refs[:depth], refs[depth : depth + PLANE - 1]
     at = depth + PLANE - 1
-    weight_refs, out_refs = refs[at : at + 6], refs[at + 6 : at + 6 + PLANE]
+    own_gate, own_up, own_down, gate_hbm, up_hbm, down_hbm = refs[at : at + 6]
+    out_refs = refs[at + 6 : at + 6 + PLANE]
     x_buf, gate_buf, up_buf, down_buf, act_buf, sems = refs[at + 6 + PLANE :]
-    width, hidden = gate_buf.shape[1], gate_buf.shape[2]
+    width, hidden = gate_buf.shape[1:]
     rows, extended = line[0].shape
     per = hidden // chunk
-    gate_copies, down_copies = [], []
-    for side in range(2):
-        gate_ref, up_ref, down_ref = weight_refs[3 * side : 3 * side + 3]
-        for i in range(per):
-            cols = pl.ds(i * chunk, chunk)
-            j = side * per + i
-            gate_copies.append(
-                (
-                    pltpu.make_async_copy(
-                        gate_ref.at[0, :, cols], gate_buf.at[side, :, cols], sems.at[0, j]
-                    ),
-                    pltpu.make_async_copy(
-                        up_ref.at[0, :, cols], up_buf.at[side, :, cols], sems.at[1, j]
-                    ),
-                )
+    gate_copies = []
+    for i in range(per):
+        cols = pl.ds(i * chunk, chunk)
+        gate_copies.append(
+            (
+                pltpu.make_async_copy(
+                    gate_hbm.at[:, :, cols], gate_buf.at[:, :, cols], sems.at[i]
+                ),
+                pltpu.make_async_copy(
+                    up_hbm.at[:, :, cols], up_buf.at[:, :, cols], sems.at[per + i]
+                ),
             )
-            down_copies.append(
-                pltpu.make_async_copy(
-                    down_ref.at[0, pl.ds(i * chunk, chunk), :],
-                    down_buf.at[pl.ds(j * chunk, chunk), :],
-                    sems.at[2, j],
-                )
-            )
+        )
+    down_copy = pltpu.make_async_copy(down_hbm, down_buf, sems.at[2 * per])
     for pair in gate_copies:
         pair[0].start()
         pair[1].start()
-    for copy in down_copies:
-        copy.start()
+    down_copy.start()
     group = depth * rows
     for z in range(depth):
         x_buf[z * rows : (z + 1) * rows, :] = line[z][...]
@@ -186,62 +232,66 @@
         expert = 2 * chip + (tensor if side == 0 else 1 - tensor)
         chosen = (lane == expert) | (lane == expert + META // 2)
         route = jnp.sum(jnp.where(chosen, meta, 0.0), axis=1, keepdims=True)
+        gate_ref, up_ref = (own_gate, own_up) if side == 0 else (gate_buf, up_buf)
         for i in range(per):
-            j = side * per + i
-            gate_copies[j][0].wait()
-            gate_copies[j][1].wait()
+            if side == 1:
+                gate_copies[i][0].wait()
+                gate_copies[i][1].wait()
             cols = pl.ds(i * chunk, chunk)
             x = x_buf[:, :width]
-            gate = jnp.dot(x, gate_buf[side, :, cols], preferred_element_type=jnp.float32)
-            up = jnp.dot(x, up_buf[side, :, cols], preferred_element_type=jnp.float32)
+            gate = jnp.dot(x, gate_ref[0, :, cols], preferred_element_type=jnp.float32)
+            up = jnp.dot(x, up_ref[0, :, cols], preferred_element_type=jnp.float32)
             act = gate / (1.0 + jnp.exp(-gate)) * up * route
-            act_buf[:, j * chunk : (j + 1) * chunk] = act.astype(jnp.bfloat16)
-    for copy in down_copies:
-        copy.wait()
+            start = side * hidden + i * chunk
+            act_buf[:, start : start + chunk] = act.astype(jnp.bfloat16)
+    down_copy.wait()
     sub = width // (PLANE * depth)
     plane = chip % PLANE
     for d in range(PLANE):
-        weight = jnp.concatenate(
-            [
-                down_buf[:, lanes((z * PLANE + (plane ^ d)) * sub, sub)]
-                for z in range(depth)
-            ],
-            axis=1,
-        )
-        out = jnp.dot(act_buf[...], weight, preferred_element_type=jnp.float32)
+        out = 0.0
+        for side, ref in enumerate((own_down, down_buf)):
+            weight = jnp.concatenate(
+                [ref[0, :, lanes((z * PLANE + (plane ^ d)) * sub, sub)] for z in range(depth)],
+                axis=1,
+            )
+            out = out + jnp.dot(
+                act_buf[:, side * hidden : (side + 1) * hidden],
+                weight,
+                preferred_element_type=jnp.float32,
+            )
         for k in range(PLANE):
             out_refs[d][k * group : (k + 1) * group, :] = out[
                 (d ^ k) * group : ((d ^ k) + 1) * group
             ].astype(jnp.bfloat16)
 
 
-def experts(line, packed, weights):
+def experts(line, packed, own, other):
     depth = len(line)
     rows, extended = line[0].shape
-    width, hidden = weights[0].shape[1:]
+    width, hidden = own[0].shape[1:]
     chunk = 256
     total = rows * depth * PLANE
     return pl.pallas_call(
         functools.partial(expert_kernel, depth, chunk),
         out_shape=(jax.ShapeDtypeStruct((total, width // PLANE), jnp.bfloat16),) * PLANE,
-        in_specs=[VMEM] * (depth + PLANE - 1) + [HBM] * 6,
+        in_specs=[VMEM] * (depth + PLANE + 2) + [HBM] * 3,
         out_specs=(VMEM,) * PLANE,
         scratch_shapes=[
             pltpu.VMEM((total, extended), jnp.bfloat16),
-            pltpu.VMEM((2, width, hidden), jnp.bfloat16),
-            pltpu.VMEM((2, width, hidden), jnp.bfloat16),
-            pltpu.VMEM((2 * hidden, width), jnp.bfloat16),
+            pltpu.VMEM((1, width, hidden), jnp.bfloat16),
+            pltpu.VMEM((1, width, hidden), jnp.bfloat16),
+            pltpu.VMEM((1, hidden, width), jnp.bfloat16),
             pltpu.VMEM((total, 2 * hidden), jnp.bfloat16),
-            pltpu.SemaphoreType.DMA((3, 2 * (hidden // chunk))),
+            pltpu.SemaphoreType.DMA((2 * (hidden // chunk) + 1,)),
         ],
-        compiler_params=params(32),
+        compiler_params=params(46),
         cost_estimate=pl.CostEstimate(
             flops=12 * total * width * hidden,
             bytes_accessed=12 * width * hidden,
             transcendentals=2 * total * hidden,
         ),
         name="experts",
-    )(*line, *packed, *weights)
+    )(*line, *packed, *own, *other)
 
 
 def plane_sum_kernel(depth, *refs):
@@ -365,7 +415,7 @@
             pltpu.VMEM((part, cols), jnp.bfloat16),
             pltpu.SemaphoreType.DMA((cols // chunk,)),
         ],
-        compiler_params=params(8),
+        compiler_params=params(58),
         cost_estimate=pl.CostEstimate(
             flops=4 * rows * part * cols, bytes_accessed=2 * part * cols, transcendentals=0
         ),
@@ -461,16 +511,6 @@
     def to_plane(values):
         return [to_expert(v, d) if d else v for d, v in enumerate(values)]
 
-    lines = [list(range(i, n_expert, PLANE)) for i in range(PLANE)]
-    qkv = lax.all_gather(
-        jnp.concatenate([q_weight, kv_weight], axis=1),
-        "expert",
-        axis=0,
-        tiled=True,
-        axis_index_groups=lines,
-    )
-    weights = (w_gate, w_up, w_down, to_core(w_gate), to_core(w_up), to_core(w_down))
-
     own_ids = lax.dynamic_slice_in_dim(expert_ids, tensor_index * rows, rows, 0)
     own_route = lax.dynamic_slice_in_dim(route_weights, tensor_index * rows, rows, 0)
     chosen = own_ids[:, :, None] == jnp.arange(META // 2, dtype=jnp.int32)[None, None, :]
@@ -478,13 +518,24 @@
     high = lax.reduce_precision(dense, 8, 7)
     meta = jnp.concatenate([high, dense - high], axis=1).astype(jnp.bfloat16)
 
-    mine, theirs = out_projection(attn_out, out_weight)
+    first_cols = width // 4
+    mine_a, theirs_a, qkv_rows = out_projection(
+        attn_out, out_weight, 0, first_cols, (q_weight, kv_weight)
+    )
+    lines = [list(range(i, n_expert, PLANE)) for i in range(PLANE)]
+    qkv = lax.all_gather(qkv_rows, "expert", axis=0, tiled=True, axis_index_groups=lines)
+    mine_b, theirs_b = out_projection(attn_out, out_weight, first_cols, width - first_cols)
+    theirs = (to_core(theirs_a), to_core(theirs_b))
     tokens, *firsts = first_norm(
-        mine, to_core(theirs), residual, attn_gain[None, :], meta, depth
-    )
+        (mine_a, mine_b), theirs, residual, attn_gain[None, :], meta, depth
+    )
+    own = (w_gate, w_up, w_down)
+    other = [to_core(w) for w in lax.optimization_barrier((*own, tokens))[:3]]
     line = to_z([tokens] * depth)
-    packed = to_plane([None, *pack(line, firsts[1:])])[1:]
-    parts = plane_sum(to_plane(experts(line, packed, weights)), depth)
+    sent = pack(line, firsts[1:])
+    packed = to_plane([None, *sent])[1:]
+    own = load(own, sent)
+    parts = plane_sum(to_plane(experts(line, packed, own, other)), depth)
     scaled, following = second_norm(to_z(parts), firsts[0], packed, input_gain[None, :])
     products = to_plane(projection(scaled, to_core(scaled), following, qkv))
     return head_norm(

time: 117 us -> 131 us (1.12)
  Pallas kernels: 16.7 us -> 49.5 us
  waiting for transfers between devices: 42.4 us -> 31 us
  local copies, waits for them, and re-layouts: 10.1 us -> 5.03 us
  other arithmetic: 2.23 us -> 0.19 us
    pallas_call x2 -> x4, Pallas kernels: 6.29 us -> 33.2 us  [the longest x2 27.6 us: out_projection(): pl.pallas_call(functools.partial(out_projection_kernel, chunk, start, len...]
    ppermute x15, waiting for transfers between devices: 40.1 us -> 28.7 us  [to_expert(): lax.ppermute(value, 'expert', [(i, i ^ offset) for i in range(n_expert)])]
    unnamed x26 -> x30, local copies, waits for them, and re-layouts: 9.84 us -> 4.74 us
    pallas_call x1, Pallas kernels: 7.78 us -> 11 us  [experts(): pl.pallas_call(functools.partial(expert_kernel, depth, chunk), out_shape=...]
    pallas_call x1, Pallas kernels: 1.42 us -> 4.07 us  [projection(): pl.pallas_call(functools.partial(projection_kernel, chunk), out_shape=(sh...]
    concatenate x1 -> x0, other arithmetic: 2.03 us -> none  [per_device_dense(): jnp.concatenate([q_weight, kv_weight], axis=1)]
  transfers between devices with their start and end apart: 21 -> 22, of which waited for: 14 -> 11; matrix products, arithmetic and copies ran while one was open for 2% -> 0% of each run, Pallas kernels for 12% -> 17%
where the time goes in v3:
time: 131 us; the launch traced here: 130 us
  Pallas kernels  49.5 us (38%)
  waiting for transfers between devices  31 us (24%)
  starting transfers between devices  30.5 us (23%)
  between operations  14.3 us (11%)
  local copies, waits for them, and re-layouts  5.03 us (4%)
    ppermute x15, starting transfers between devices, to_expert(): lax.ppermute(value, 'expert', [(i, i ^ offset) for i in range(n_expert)])  29.1 us
    ppermute x15, waiting for transfers between devices, to_expert(): lax.ppermute(value, 'expert', [(i, i ^ offset) for i in range(n_expert)])  28.7 us
    pallas_call x2, Pallas kernels, out_projection(): pl.pallas_call(functools.partial(out_projection_kernel, chunk, start, len...  27.6 us
    pallas_call x1, Pallas kernels, experts(): pl.pallas_call(functools.partial(expert_kernel, depth, chunk), out_shape=...  11 us
    pallas_call x1, Pallas kernels, load(): pl.pallas_call(load_kernel, out_shape=tuple((jax.ShapeDtypeStruct(w.shape...  5.54 us
    unnamed x30, local copies, waits for them, and re-layouts  4.74 us
    pallas_call x1, Pallas kernels, projection(): pl.pallas_call(functools.partial(projection_kernel, chunk), out_shape=(sh...  4.07 us
  transfers between devices with their start and end apart: 22, of which 11 were waited for; matrix products, arithmetic and copies ran while one was open for 0% of the time, Pallas kernels for 17%

profile of v3, /device:TPU:0, one launch (start us, length us, event | category | flops | bytes accessed | tf_op | source)
XLA Modules:
  0.0 130.5 jit_solution(5388103025095486450)
XLA Ops:
  7.2 21.6 %out_projection.2 = (f32[16,512]{1,0:T(8,128)}, f32[16,512]{1,0:T(8,128)}, bf16[128,2560]{1,0:T(8,128)(2,1)}) custom-call(bf16[32,2048]{1,0:T(8,128)(2,1)} %a_hbm.3, bf16[2048,2048]{1,0:T(8,128)(2,1)} %w_hbm.3, bf16[128,2048]{1,0:T(8,128)(2,1)} %refs_0_.2, bf16[128,512]{1,0:T(8,128)(2,1)} %refs_1_.2), custom_call_target="tpu_custom_call" | custom-call | flops 67108864 | bytes 2097152 | tf_op jit(solution)/shard_map/out_projection/pallas_call | solution.py:88
  29.4 5.9 %out_projection.3 = (f32[16,1536]{1,0:T(8,128)}, f32[16,1536]{1,0:T(8,128)}) custom-call(bf16[32,2048]{1,0:T(8,128)(2,1)} %a_hbm.3, bf16[2048,2048]{1,0:T(8,128)(2,1)} %w_hbm.3), custom_call_target="tpu_custom_call" | custom-call | flops 201326592 | bytes 6291456 | tf_op jit(solution)/shard_map/out_projection/pallas_call | solution.py:88
  38.8 2.9 %collective-permute-start.2 = (bf16[16,2176]{1,0:T(8,128)(2,1)S(1)}, bf16[16,2176]{1,0:T(8,128)(2,1)S(1)}, u32[]{:S(2)}, u32[]{:S(2)}) collective-permute-start(bf16[16,2176]{1,0:T(8,128)(2,1)S(1)} %get-tuple-element.40.refs_0_), channel_id=1, source_target_pairs={{0,8},{2,10},{4,12},{6,14},{8,0},{10,2},{12,4},{14,6},{16,24},{18,... | collective-permute-start | bytes 208904 | tf_op jit(solution)/shard_map/ppermute | solution.py:506
  41.7 2.6 %collective-permute-start.3 = (bf16[16,2176]{1,0:T(8,128)(2,1)S(1)}, bf16[16,2176]{1,0:T(8,128)(2,1)S(1)}, u32[]{:S(2)}, u32[]{:S(2)}) collective-permute-start(bf16[16,2176]{1,0:T(8,128)(2,1)S(1)} %get-tuple-element.40.refs_0_), channel_id=1, source_target_pairs={{0,16},{2,18},{4,20},{6,22},{8,24},{10,26},{12,28},{14,30},{16,0},... | collective-permute-start | bytes 208904 | tf_op jit(solution)/shard_map/ppermute | solution.py:506
  44.3 4.5 %collective-permute-start.4 = (bf16[16,2176]{1,0:T(8,128)(2,1)S(1)}, bf16[16,2176]{1,0:T(8,128)(2,1)S(1)}, u32[]{:S(2)}, u32[]{:S(2)}) collective-permute-start(bf16[16,2176]{1,0:T(8,128)(2,1)S(1)} %get-tuple-element.40.refs_0_), channel_id=1, source_target_pairs={{0,24},{2,26},{4,28},{6,30},{8,16},{10,18},{12,20},{14,22},{16,8},... | collective-permute-start | bytes 208904 | tf_op jit(solution)/shard_map/ppermute | solution.py:506
  49.2 2.9 %collective-permute-done.4.refs_3_ = bf16[16,2176]{1,0:T(8,128)(2,1)S(1)} collective-permute-done((bf16[16,2176]{1,0:T(8,128)(2,1)S(1)}, bf16[16,2176]{1,0:T(8,128)(2,1)S(1)}, u32[]{:S(2)}, u32[]{:S(2)}) %collective-permute-start.4) | collective-permute-done | bytes 69664 | tf_op jit(solution)/shard_map/ppermute | solution.py:506
  53.4 1.6 %collective-permute-start.6 = (bf16[64,2304]{1,0:T(8,128)(2,1)S(1)}, bf16[64,2304]{1,0:T(8,128)(2,1)S(1)}, u32[]{:S(2)}, u32[]{:S(2)}) collective-permute-start(bf16[64,2304]{1,0:T(8,128)(2,1)S(1)} %get-tuple-element.45.refs_4_), channel_id=1, source_target_pairs={{0,4},{2,6},{4,0},{6,2},{8,12},{10,14},{12,8},{14,10},{16,20},{18,... | collective-permute-start | bytes 884744 | tf_op jit(solution)/shard_map/ppermute | solution.py:506
  55.0 4.3 %collective-permute-done.5.refs_4_.refs_5_ = bf16[64,2304]{1,0:T(8,128)(2,1)S(1)} collective-permute-done((bf16[64,2304]{1,0:T(8,128)(2,1)S(1)}, bf16[64,2304]{1,0:T(8,128)(2,1)S(1)}, u32[]{:S(2)}, u32[]{:S(2)}) %collective-permute-start.5) | collective-permute-done | bytes 294944 | tf_op jit(solution)/shard_map/ppermute | solution.py:506
  59.3 3.0 %collective-permute-start.7 = (bf16[64,2304]{1,0:T(8,128)(2,1)S(1)}, bf16[64,2304]{1,0:T(8,128)(2,1)S(1)}, u32[]{:S(2)}, u32[]{:S(2)}) collective-permute-start(bf16[64,2304]{1,0:T(8,128)(2,1)S(1)} %get-tuple-element.46.refs_5_), channel_id=1, source_target_pairs={{0,6},{2,4},{4,2},{6,0},{8,14},{10,12},{12,10},{14,8},{16,22},{18,... | collective-permute-start | bytes 884744 | tf_op jit(solution)/shard_map/ppermute | solution.py:506
  62.3 5.5 %load_weights.1 = (bf16[1,2048,768]{2,1,0:T(8,128)(2,1)S(1)}, bf16[1,2048,768]{2,1,0:T(8,128)(2,1)S(1)}, bf16[1,768,2048]{2,1,0:T(8,128)(2,1)}) custom-call(bf16[1,2048,768]{2,1,0:T(8,128)(2,1)} %refs_0_.3, bf16[1,2048,768]{2,1,0:T(8,128)(2,1)} %refs_1_.3, bf16[1,768,2048]{2,1,0:T(8,128)(2,1)} %refs_2_.1, bf16[64,2304]{1,0:T(8,128)(2,1)S(1)} %get-tuple-element.44.refs_3_, ...), custom_call_target="tpu_custom_call" | custom-call | bytes 18874368 | tf_op jit(solution)/shard_map/load_weights/pallas_call | solution.py:183
  67.8 1.6 %copy-done.1 = bf16[1,2048,768]{2,1,0:T(8,128)(2,1)} copy-done((bf16[1,2048,768]{2,1,0:T(8,128)(2,1)}, bf16[1,2048,768]{2,1,0:T(8,128)(2,1)S(1)}, u32[]{:S(2)}) %copy-start.1) | copy-done | bytes 3145752
  69.5 11.0 %experts.1 = (bf16[256,512]{1,0:T(8,128)(2,1)S(1)}, bf16[256,512]{1,0:T(8,128)(2,1)S(1)}, bf16[256,512]{1,0:T(8,128)(2,1)S(1)}, bf16[256,512]{1,0:T(8,128)(2,1)S(1)}) custom-call(bf16[16,2176]{1,0:T(8,128)(2,1)S(1)} %get-tuple-element.40.refs_0_, bf16[16,2176]{1,0:T(8,128)(2,1)S(1)} %collective-permute-done.2.refs_1_, ...), custom_call_target="tpu_custom_call" | custom-call | flops 4831838208 | bytes 18874368 | tf_op jit(solution)/shard_map/experts/pallas_call | solution.py:274
  81.5 2.5 %collective-permute-start.13 = (bf16[256,512]{1,0:T(8,128)(2,1)S(1)}, bf16[256,512]{1,0:T(8,128)(2,1)S(1)}, u32[]{:S(2)}, u32[]{:S(2)}) collective-permute-start(bf16[256,512]{1,0:T(8,128)(2,1)S(1)} %get-tuple-element.56), channel_id=1, source_target_pairs={{0,6},{2,4},{4,2},{6,0},{8,14},{10,12},{12,10},{14,8},{16,22},{18,... | collective-permute-start | bytes 786440 | tf_op jit(solution)/shard_map/ppermute | solution.py:506
  84.0 2.9 %collective-permute-done.11.refs_1_ = bf16[256,512]{1,0:T(8,128)(2,1)S(1)} collective-permute-done((bf16[256,512]{1,0:T(8,128)(2,1)S(1)}, bf16[256,512]{1,0:T(8,128)(2,1)S(1)}, u32[]{:S(2)}, u32[]{:S(2)}) %collective-permute-start.11) | collective-permute-done | bytes 262176 | tf_op jit(solution)/shard_map/ppermute | solution.py:506
  86.9 3.3 %collective-permute-done.12.refs_2_ = bf16[256,512]{1,0:T(8,128)(2,1)S(1)} collective-permute-done((bf16[256,512]{1,0:T(8,128)(2,1)S(1)}, bf16[256,512]{1,0:T(8,128)(2,1)S(1)}, u32[]{:S(2)}, u32[]{:S(2)}) %collective-permute-start.12) | collective-permute-done | bytes 262176 | tf_op jit(solution)/shard_map/ppermute | solution.py:506
  90.3 3.0 %collective-permute-start.14 = (bf16[64,512]{1,0:T(8,128)(2,1)S(1)}, bf16[64,512]{1,0:T(8,128)(2,1)S(1)}, u32[]{:S(2)}, u32[]{:S(2)}) collective-permute-start(bf16[64,512]{1,0:T(8,128)(2,1)S(1)} %get-tuple-element.58), channel_id=1, source_target_pairs={{0,8},{2,10},{4,12},{6,14},{8,0},{10,2},{12,4},{14,6},{16,24},{18,... | collective-permute-start | bytes 196616 | tf_op jit(solution)/shard_map/ppermute | solution.py:506
  93.3 3.2 %collective-permute-start.15 = (bf16[64,512]{1,0:T(8,128)(2,1)S(1)}, bf16[64,512]{1,0:T(8,128)(2,1)S(1)}, u32[]{:S(2)}, u32[]{:S(2)}) collective-permute-start(bf16[64,512]{1,0:T(8,128)(2,1)S(1)} %get-tuple-element.59), channel_id=1, source_target_pairs={{0,16},{2,18},{4,20},{6,22},{8,24},{10,26},{12,28},{14,30},{16,0},... | collective-permute-start | bytes 196616 | tf_op jit(solution)/shard_map/ppermute | solution.py:506
  96.5 3.6 %collective-permute-done.15.refs_2_ = bf16[64,512]{1,0:T(8,128)(2,1)S(1)} collective-permute-done((bf16[64,512]{1,0:T(8,128)(2,1)S(1)}, bf16[64,512]{1,0:T(8,128)(2,1)S(1)}, u32[]{:S(2)}, u32[]{:S(2)}) %collective-permute-start.15) | collective-permute-done | bytes 65568 | tf_op jit(solution)/shard_map/ppermute | solution.py:506
  100.1 2.4 %collective-permute-done.16.refs_3_ = bf16[64,512]{1,0:T(8,128)(2,1)S(1)} collective-permute-done((bf16[64,512]{1,0:T(8,128)(2,1)S(1)}, bf16[64,512]{1,0:T(8,128)(2,1)S(1)}, u32[]{:S(2)}, u32[]{:S(2)}) %collective-permute-start.16) | collective-permute-done | bytes 65568 | tf_op jit(solution)/shard_map/ppermute | solution.py:506
  105.3 4.1 %qkv_projection.1 = (bf16[32,2944]{1,0:T(8,128)(2,1)}, bf16[32,2944]{1,0:T(8,128)(2,1)}, bf16[32,2944]{1,0:T(8,128)(2,1)}, bf16[32,2944]{1,0:T(8,128)(2,1)}) custom-call(bf16[64,640]{1,0:T(8,128)(2,1)} %copy-done.4, bf16[64,640]{1,0:T(8,128)(2,1)} %copy-done.13, bf16[64,512]{1,0:T(8,128)(2,1)} %copy-done.5, bf16[512,2560]{1,0:T(8,128)(2,1)} %all-gather.2.cloned.1.call-done.w_hbm), custom_call_target="tpu_custom_call" | custom-call | flops 335544320 | bytes 2621440 | tf_op jit(solution)/shard_map/qkv_projection/pallas_call | solution.py:409
  109.3 1.7 %collective-permute-start.18 = (bf16[32,2944]{1,0:T(8,128)(2,1)}, bf16[32,2944]{1,0:T(8,128)(2,1)S(1)}, u32[]{:S(2)}, u32[]{:S(2)}) collective-permute-start(bf16[32,2944]{1,0:T(8,128)(2,1)} %get-tuple-element.66), channel_id=1, source_target_pairs={{0,2},{2,0},{4,6},{6,4},{8,10},{10,8},{12,14},{14,12},{16,18},{18,... | collective-permute-start | bytes 565256 | tf_op jit(solution)/shard_map/ppermute | solution.py:506
  111.2 1.7 %collective-permute-start.20 = (bf16[32,2944]{1,0:T(8,128)(2,1)}, bf16[32,2944]{1,0:T(8,128)(2,1)S(1)}, u32[]{:S(2)}, u32[]{:S(2)}) collective-permute-start(bf16[32,2944]{1,0:T(8,128)(2,1)} %get-tuple-element.68), channel_id=1, source_target_pairs={{0,6},{2,4},{4,2},{6,0},{8,14},{10,12},{12,10},{14,8},{16,22},{18,... | collective-permute-start | bytes 565256 | tf_op jit(solution)/shard_map/ppermute | solution.py:506
  112.9 4.3 %collective-permute-done.18.refs_1_ = bf16[32,2944]{1,0:T(8,128)(2,1)S(1)} collective-permute-done((bf16[32,2944]{1,0:T(8,128)(2,1)}, bf16[32,2944]{1,0:T(8,128)(2,1)S(1)}, u32[]{:S(2)}, u32[]{:S(2)}) %collective-permute-start.18) | collective-permute-done | bytes 188448 | tf_op jit(solution)/shard_map/ppermute | solution.py:506
  117.2 4.6 %collective-permute-done.19.refs_2_ = bf16[32,2944]{1,0:T(8,128)(2,1)S(1)} collective-permute-done((bf16[32,2944]{1,0:T(8,128)(2,1)}, bf16[32,2944]{1,0:T(8,128)(2,1)S(1)}, u32[]{:S(2)}, u32[]{:S(2)}) %collective-permute-start.19) | collective-permute-done | bytes 188448 | tf_op jit(solution)/shard_map/ppermute | solution.py:506
  (68 shorter events, 11.5 us)
Async XLA Ops:
  7.2 97.5 %all-gather.2.cloned.1.call-start = ((), (), s32[]{:S(2)}) async-start(), calls=%async_computation | async-start | bytes 3276800 | tf_op jit(solution)/shard_map/all_gather | solution.py:526
  28.9 7.1 %collective-permute-start = (f32[16,512]{1,0:T(8,128)}, f32[16,512]{1,0:T(8,128)S(1)}, u32[]{:S(2)}, u32[]{:S(2)}) collective-permute-start(f32[16,512]{1,0:T(8,128)} %get-tuple-element.38), channel_id=1, source_target_pairs={{0,1},{1,0},{2,3},{3,2},{4,5},{5,4},{6,7},{7,6},{8,9},{9,8},{10,11... | collective-permute-start | bytes 98312 | tf_op jit(solution)/shard_map/ppermute | solution.py:503
  35.4 1.6 %collective-permute-start.1 = (f32[16,1536]{1,0:T(8,128)}, f32[16,1536]{1,0:T(8,128)S(1)}, u32[]{:S(2)}, u32[]{:S(2)}) collective-permute-start(f32[16,1536]{1,0:T(8,128)} %get-tuple-element.39), channel_id=1, source_target_pairs={{0,1},{1,0},{2,3},{3,2},{4,5},{5,4},{6,7},{7,6},{8,9},{9,8},{10,11... | collective-permute-start | bytes 294920 | tf_op jit(solution)/shard_map/ppermute | solution.py:503
  38.0 31.4 %collective-permute-start.10 = (bf16[1,768,2048]{2,1,0:T(8,128)(2,1)S(1)}, bf16[1,768,2048]{2,1,0:T(8,128)(2,1)}, u32[]{:S(2)}, u32[]{:S(2)}) collective-permute-start(bf16[1,768,2048]{2,1,0:T(8,128)(2,1)S(1)} %copy-done.12), channel_id=1, source_target_pairs={{0,1},{1,0},{2,3},{3,2},{4,5},{5,4},{6,7},{7,6},{8,9},{9,8},{10,11... | collective-permute-start | bytes 9437192 | tf_op jit(solution)/shard_map/ppermute | solution.py:503
  38.2 31.2 %collective-permute-start.8 = (bf16[1,2048,768]{2,1,0:T(8,128)(2,1)}, bf16[1,2048,768]{2,1,0:T(8,128)(2,1)}, u32[]{:S(2)}, u32[]{:S(2)}) collective-permute-start(bf16[1,2048,768]{2,1,0:T(8,128)(2,1)} %refs_0_.3), channel_id=1, source_target_pairs={{0,1},{1,0},{2,3},{3,2},{4,5},{5,4},{6,7},{7,6},{8,9},{9,8},{10,11... | collective-permute-start | bytes 9437192 | tf_op jit(solution)/shard_map/ppermute | solution.py:503
  38.6 30.9 %collective-permute-start.9 = (bf16[1,2048,768]{2,1,0:T(8,128)(2,1)}, bf16[1,2048,768]{2,1,0:T(8,128)(2,1)}, u32[]{:S(2)}, u32[]{:S(2)}) collective-permute-start(bf16[1,2048,768]{2,1,0:T(8,128)(2,1)} %refs_1_.3), channel_id=1, source_target_pairs={{0,1},{1,0},{2,3},{3,2},{4,5},{5,4},{6,7},{7,6},{8,9},{9,8},{10,11... | collective-permute-start | bytes 9437192 | tf_op jit(solution)/shard_map/ppermute | solution.py:503
  38.8 5.5 %collective-permute-start.2 = (bf16[16,2176]{1,0:T(8,128)(2,1)S(1)}, bf16[16,2176]{1,0:T(8,128)(2,1)S(1)}, u32[]{:S(2)}, u32[]{:S(2)}) collective-permute-start(bf16[16,2176]{1,0:T(8,128)(2,1)S(1)} %get-tuple-element.40.refs_0_), channel_id=1, source_target_pairs={{0,8},{2,10},{4,12},{6,14},{8,0},{10,2},{12,4},{14,6},{16,24},{18,... | collective-permute-start | bytes 208904 | tf_op jit(solution)/shard_map/ppermute | solution.py:506
  41.7 7.5 %collective-permute-start.3 = (bf16[16,2176]{1,0:T(8,128)(2,1)S(1)}, bf16[16,2176]{1,0:T(8,128)(2,1)S(1)}, u32[]{:S(2)}, u32[]{:S(2)}) collective-permute-start(bf16[16,2176]{1,0:T(8,128)(2,1)S(1)} %get-tuple-element.40.refs_0_), channel_id=1, source_target_pairs={{0,16},{2,18},{4,20},{6,22},{8,24},{10,26},{12,28},{14,30},{16,0},... | collective-permute-start | bytes 208904 | tf_op jit(solution)/shard_map/ppermute | solution.py:506
  44.3 7.8 %collective-permute-start.4 = (bf16[16,2176]{1,0:T(8,128)(2,1)S(1)}, bf16[16,2176]{1,0:T(8,128)(2,1)S(1)}, u32[]{:S(2)}, u32[]{:S(2)}) collective-permute-start(bf16[16,2176]{1,0:T(8,128)(2,1)S(1)} %get-tuple-element.40.refs_0_), channel_id=1, source_target_pairs={{0,24},{2,26},{4,28},{6,30},{8,16},{10,18},{12,20},{14,22},{16,8},... | collective-permute-start | bytes 208904 | tf_op jit(solution)/shard_map/ppermute | solution.py:506
  52.1 7.2 %collective-permute-start.5 = (bf16[64,2304]{1,0:T(8,128)(2,1)S(1)}, bf16[64,2304]{1,0:T(8,128)(2,1)S(1)}, u32[]{:S(2)}, u32[]{:S(2)}) collective-permute-start(bf16[64,2304]{1,0:T(8,128)(2,1)S(1)} %get-tuple-element.44.refs_3_), channel_id=1, source_target_pairs={{0,2},{2,0},{4,6},{6,4},{8,10},{10,8},{12,14},{14,12},{16,18},{18,... | collective-permute-start | bytes 884744 | tf_op jit(solution)/shard_map/ppermute | solution.py:506
  53.4 16.1 %collective-permute-start.6 = (bf16[64,2304]{1,0:T(8,128)(2,1)S(1)}, bf16[64,2304]{1,0:T(8,128)(2,1)S(1)}, u32[]{:S(2)}, u32[]{:S(2)}) collective-permute-start(bf16[64,2304]{1,0:T(8,128)(2,1)S(1)} %get-tuple-element.45.refs_4_), channel_id=1, source_target_pairs={{0,4},{2,6},{4,0},{6,2},{8,12},{10,14},{12,8},{14,10},{16,20},{18,... | collective-permute-start | bytes 884744 | tf_op jit(solution)/shard_map/ppermute | solution.py:506
  59.3 10.2 %collective-permute-start.7 = (bf16[64,2304]{1,0:T(8,128)(2,1)S(1)}, bf16[64,2304]{1,0:T(8,128)(2,1)S(1)}, u32[]{:S(2)}, u32[]{:S(2)}) collective-permute-start(bf16[64,2304]{1,0:T(8,128)(2,1)S(1)} %get-tuple-element.46.refs_5_), channel_id=1, source_target_pairs={{0,6},{2,4},{4,2},{6,0},{8,14},{10,12},{12,10},{14,8},{16,22},{18,... | collective-permute-start | bytes 884744 | tf_op jit(solution)/shard_map/ppermute | solution.py:506
  80.5 41.3 %copy-start.10 = (f32[128]{0:T(128)S(1)}, f32[128]{0:T(128)}, u32[]{:S(2)}) copy-start(f32[128]{0:T(128)} %param.26) | copy-start | bytes 1540
  80.5 41.3 %copy-start.11 = (f32[128]{0:T(128)S(1)}, f32[128]{0:T(128)}, u32[]{:S(2)}) copy-start(f32[128]{0:T(128)} %param.27) | copy-start | bytes 1540
  80.5 6.4 %collective-permute-start.11 = (bf16[256,512]{1,0:T(8,128)(2,1)S(1)}, bf16[256,512]{1,0:T(8,128)(2,1)S(1)}, u32[]{:S(2)}, u32[]{:S(2)}) collective-permute-start(bf16[256,512]{1,0:T(8,128)(2,1)S(1)} %get-tuple-element.54), channel_id=1, source_target_pairs={{0,2},{2,0},{4,6},{6,4},{8,10},{10,8},{12,14},{14,12},{16,18},{18,... | collective-permute-start | bytes 786440 | tf_op jit(solution)/shard_map/ppermute | solution.py:506
  81.0 9.2 %collective-permute-start.12 = (bf16[256,512]{1,0:T(8,128)(2,1)S(1)}, bf16[256,512]{1,0:T(8,128)(2,1)S(1)}, u32[]{:S(2)}, u32[]{:S(2)}) collective-permute-start(bf16[256,512]{1,0:T(8,128)(2,1)S(1)} %get-tuple-element.55), channel_id=1, source_target_pairs={{0,4},{2,6},{4,0},{6,2},{8,12},{10,14},{12,8},{14,10},{16,20},{18,... | collective-permute-start | bytes 786440 | tf_op jit(solution)/shard_map/ppermute | solution.py:506
  81.5 8.7 %collective-permute-start.13 = (bf16[256,512]{1,0:T(8,128)(2,1)S(1)}, bf16[256,512]{1,0:T(8,128)(2,1)S(1)}, u32[]{:S(2)}, u32[]{:S(2)}) collective-permute-start(bf16[256,512]{1,0:T(8,128)(2,1)S(1)} %get-tuple-element.56), channel_id=1, source_target_pairs={{0,6},{2,4},{4,2},{6,0},{8,14},{10,12},{12,10},{14,8},{16,22},{18,... | collective-permute-start | bytes 786440 | tf_op jit(solution)/shard_map/ppermute | solution.py:506
  90.3 6.2 %collective-permute-start.14 = (bf16[64,512]{1,0:T(8,128)(2,1)S(1)}, bf16[64,512]{1,0:T(8,128)(2,1)S(1)}, u32[]{:S(2)}, u32[]{:S(2)}) collective-permute-start(bf16[64,512]{1,0:T(8,128)(2,1)S(1)} %get-tuple-element.58), channel_id=1, source_target_pairs={{0,8},{2,10},{4,12},{6,14},{8,0},{10,2},{12,4},{14,6},{16,24},{18,... | collective-permute-start | bytes 196616 | tf_op jit(solution)/shard_map/ppermute | solution.py:506
  93.3 6.9 %collective-permute-start.15 = (bf16[64,512]{1,0:T(8,128)(2,1)S(1)}, bf16[64,512]{1,0:T(8,128)(2,1)S(1)}, u32[]{:S(2)}, u32[]{:S(2)}) collective-permute-start(bf16[64,512]{1,0:T(8,128)(2,1)S(1)} %get-tuple-element.59), channel_id=1, source_target_pairs={{0,16},{2,18},{4,20},{6,22},{8,24},{10,26},{12,28},{14,30},{16,0},... | collective-permute-start | bytes 196616 | tf_op jit(solution)/shard_map/ppermute | solution.py:506
  96.5 6.1 %collective-permute-start.16 = (bf16[64,512]{1,0:T(8,128)(2,1)S(1)}, bf16[64,512]{1,0:T(8,128)(2,1)S(1)}, u32[]{:S(2)}, u32[]{:S(2)}) collective-permute-start(bf16[64,512]{1,0:T(8,128)(2,1)S(1)} %get-tuple-element.60), channel_id=1, source_target_pairs={{0,24},{2,26},{4,28},{6,30},{8,16},{10,18},{12,20},{14,22},{16,8},... | collective-permute-start | bytes 196616 | tf_op jit(solution)/shard_map/ppermute | solution.py:506
  103.4 1.3 collective-permute-start.17
  109.3 7.8 %collective-permute-start.18 = (bf16[32,2944]{1,0:T(8,128)(2,1)}, bf16[32,2944]{1,0:T(8,128)(2,1)S(1)}, u32[]{:S(2)}, u32[]{:S(2)}) collective-permute-start(bf16[32,2944]{1,0:T(8,128)(2,1)} %get-tuple-element.66), channel_id=1, source_target_pairs={{0,2},{2,0},{4,6},{6,4},{8,10},{10,8},{12,14},{14,12},{16,18},{18,... | collective-permute-start | bytes 565256 | tf_op jit(solution)/shard_map/ppermute | solution.py:506
  111.0 10.8 %collective-permute-start.19 = (bf16[32,2944]{1,0:T(8,128)(2,1)}, bf16[32,2944]{1,0:T(8,128)(2,1)S(1)}, u32[]{:S(2)}, u32[]{:S(2)}) collective-permute-start(bf16[32,2944]{1,0:T(8,128)(2,1)} %get-tuple-element.67), channel_id=1, source_target_pairs={{0,4},{2,6},{4,0},{6,2},{8,12},{10,14},{12,8},{14,10},{16,20},{18,... | collective-permute-start | bytes 565256 | tf_op jit(solution)/shard_map/ppermute | solution.py:506
  111.2 10.5 %collective-permute-start.20 = (bf16[32,2944]{1,0:T(8,128)(2,1)}, bf16[32,2944]{1,0:T(8,128)(2,1)S(1)}, u32[]{:S(2)}, u32[]{:S(2)}) collective-permute-start(bf16[32,2944]{1,0:T(8,128)(2,1)} %get-tuple-element.68), channel_id=1, source_target_pairs={{0,6},{2,4},{4,2},{6,0},{8,14},{10,12},{12,10},{14,8},{16,22},{18,... | collective-permute-start | bytes 565256 | tf_op jit(solution)/shard_map/ppermute | solution.py:506
  (13 other events, 107.6 us)
Sparse Core Ops, SparseCore 0:
  38.9 58.9 all-gather.1

commit v4 on v3

--- a/solution.py
+++ b/solution.py
@@ -15,6 +15,7 @@
 
 EPSILON = 1e-06
 
+SMALL = pl.CostEstimate(flops=0, bytes_accessed=0, transcendentals=0)
 VMEM = pl.BlockSpec(memory_space=pltpu.VMEM)
 HBM = pl.BlockSpec(memory_space=pltpu.HBM)
 
@@ -31,78 +32,63 @@
     return pl.ds(pl.multiple_of(start, size), size)
 
 
-def out_projection_kernel(
-    chunk, start, side_count, a_hbm, w_hbm, *refs
-):
-    side_refs, (mine_ref, theirs_ref) = refs[:side_count], refs[side_count : side_count + 2]
-    joined = refs[side_count + 2 : -5]
-    a_buf, w_buf, a_sem, sems, side_sems = refs[-5:]
-    width = w_buf.shape[1]
-    count = width // chunk
+def in_hbm(value):
+    return pltpu.with_memory_space_constraint(value, pltpu.HBM)
+
+
+def in_vmem(value):
+    return pltpu.with_memory_space_constraint(value, pltpu.VMEM)
+
+
+def out_projection_kernel(chunk, a_hbm, w_hbm, mine_ref, theirs_ref, a_buf, w_buf, a_sem, sems):
+    depth = w_buf.shape[0]
+    count = depth // chunk
     half = mine_ref.shape[0]
     a_copy = pltpu.make_async_copy(a_hbm, a_buf, a_sem)
     a_copy.start()
     copies = []
     for i in range(count):
-        copies.append(
-            pltpu.make_async_copy(
-                w_hbm.at[:, pl.ds(start + i * chunk, chunk)],
-                w_buf.at[:, pl.ds(i * chunk, chunk)],
-                sems.at[i],
-            )
-        )
+        rows = pl.ds(i * chunk, chunk)
+        copies.append(pltpu.make_async_copy(w_hbm.at[rows], w_buf.at[rows], sems.at[i]))
     for copy in copies:
         copy.start()
-    side_copies, at = [], 0
-    for i, ref in enumerate(side_refs):
-        cols = ref.shape[1]
-        side_copies.append(
-            pltpu.make_async_copy(ref, joined[0].at[:, pl.ds(at, cols)], side_sems.at[i])
-        )
-        at += cols
-    for copy in side_copies:
-        copy.start()
     tensor = lax.axis_index("tensor")
+    own = lanes(tensor * half, half)
+    other = lanes((1 - tensor) * half, half)
     a_copy.wait()
-    own = a_buf[lanes(tensor * half, half), :]
-    other = a_buf[lanes((1 - tensor) * half, half), :]
-    both = jnp.concatenate([own, other], axis=0)
     for i in range(count):
         copies[i].wait()
-        cols = pl.ds(i * chunk, chunk)
-        product = jnp.dot(both, w_buf[:, cols], preferred_element_type=jnp.float32)
-        mine_ref[:, cols] = product[:half]
-        theirs_ref[:, cols] = product[half:]
-    for copy in side_copies:
-        copy.wait()
-
-
-def out_projection(attn_out, out_weight, start, width, side=()):
+        at = pl.ds(i * chunk, chunk)
+        both = jnp.concatenate([a_buf[own, at], a_buf[other, at]], axis=0)
+        product = jnp.dot(both, w_buf[at, :], preferred_element_type=jnp.float32)
+        if i == 0:
+            mine_ref[...] = product[:half]
+            theirs_ref[...] = product[half:]
+        else:
+            mine_ref[...] += product[:half]
+            theirs_ref[...] += product[half:]
+
+
+def out_projection(attn_out, out_weight):
     rows, depth = attn_out.shape
+    width = out_weight.shape[1]
     chunk = 256
-    half = jax.ShapeDtypeStruct((rows // 2, width), jnp.float32)
-    joined = ()
-    if side:
-        cols = sum(array.shape[1] for array in side)
-        joined = (jax.ShapeDtypeStruct((side[0].shape[0], cols), side[0].dtype),)
-    return pl.pallas_call(
-        functools.partial(out_projection_kernel, chunk, start, len(side)),
-        out_shape=(half, half) + joined,
-        in_specs=[HBM, HBM] + [HBM] * len(side),
-        out_specs=(VMEM, VMEM) + (HBM,) * len(joined),
+    half = pltpu.VMEM((rows // 2, width), jnp.float32)
+    return pl.pallas_call(
+        functools.partial(out_projection_kernel, chunk),
+        out_shape=(half, half),
+        in_specs=[HBM, HBM],
+        out_specs=(VMEM, VMEM),
         scratch_shapes=[
             pltpu.VMEM((rows, depth), jnp.bfloat16),
             pltpu.VMEM((depth, width), jnp.bfloat16),
             pltpu.SemaphoreType.DMA,
-            pltpu.SemaphoreType.DMA((width // chunk,)),
-            pltpu.SemaphoreType.DMA((2,)),
+            pltpu.SemaphoreType.DMA((depth // chunk,)),
         ],
-        compiler_params=params(60),
-        cost_estimate=pl.CostEstimate(
-            flops=2 * rows * depth * width, bytes_accessed=2 * depth * width, transcendentals=0
-        ),
+        compiler_params=params(14),
+        cost_estimate=SMALL,
         name="out_projection",
-    )(attn_out, out_weight, *side)
+    )(in_hbm(attn_out), in_hbm(out_weight))
 
 
 def first_norm_kernel(depth, count, *refs):
@@ -182,43 +168,24 @@
     size = sum(w.size for w in weights)
     return pl.pallas_call(
         load_kernel,
-        out_shape=tuple(jax.ShapeDtypeStruct(w.shape, w.dtype) for w in weights),
+        out_shape=tuple(pltpu.VMEM(w.shape, w.dtype) for w in weights),
         in_specs=[HBM] * 3 + [pl.BlockSpec(memory_space=pl.ANY)] * len(after),
         out_specs=(VMEM,) * 3,
         scratch_shapes=[pltpu.SemaphoreType.DMA((3,))],
-        compiler_params=params(46),
-        cost_estimate=pl.CostEstimate(flops=0, bytes_accessed=4 * size, transcendentals=0),
+        compiler_params=params(2),
+        cost_estimate=SMALL,
         name="load_weights",
-    )(*weights, *after)
+    )(*map(in_hbm, weights), *after)
 
 
 def expert_kernel(depth, chunk, *refs):
     line, packed = refs[:depth], refs[depth : depth + PLANE - 1]
     at = depth + PLANE - 1
-    own_gate, own_up, own_down, gate_hbm, up_hbm, down_hbm = refs[at : at + 6]
+    sides = (refs[at : at + 3], refs[at + 3 : at + 6])
     out_refs = refs[at + 6 : at + 6 + PLANE]
-    x_buf, gate_buf, up_buf, down_buf, act_buf, sems = refs[at + 6 + PLANE :]
-    width, hidden = gate_buf.shape[1:]
+    x_buf, act_buf = refs[at + 6 + PLANE :]
+    width, hidden = sides[0][0].shape[1:]
     rows, extended = line[0].shape
-    per = hidden // chunk
-    gate_copies = []
-    for i in range(per):
-        cols = pl.ds(i * chunk, chunk)
-        gate_copies.append(
-            (
-                pltpu.make_async_copy(
-                    gate_hbm.at[:, :, cols], gate_buf.at[:, :, cols], sems.at[i]
-                ),
-                pltpu.make_async_copy(
-                    up_hbm.at[:, :, cols], up_buf.at[:, :, cols], sems.at[per + i]
-                ),
-            )
-        )
-    down_copy = pltpu.make_async_copy(down_hbm, down_buf, sems.at[2 * per])
-    for pair in gate_copies:
-        pair[0].start()
-        pair[1].start()
-    down_copy.start()
     group = depth * rows
     for z in range(depth):
         x_buf[z * rows : (z + 1) * rows, :] = line[z][...]
@@ -228,15 +195,11 @@
     lane = lax.broadcasted_iota(jnp.int32, meta.shape, 1)
     chip = lax.axis_index("expert")
     tensor = lax.axis_index("tensor")
-    for side in range(2):
+    for side, (gate_ref, up_ref, _) in enumerate(sides):
         expert = 2 * chip + (tensor if side == 0 else 1 - tensor)
         chosen = (lane == expert) | (lane == expert + META // 2)
         route = jnp.sum(jnp.where(chosen, meta, 0.0), axis=1, keepdims=True)
-        gate_ref, up_ref = (own_gate, own_up) if side == 0 else (gate_buf, up_buf)
-        for i in range(per):
-            if side == 1:
-                gate_copies[i][0].wait()
-                gate_copies[i][1].wait()
+        for i in range(hidden // chunk):
             cols = pl.ds(i * chunk, chunk)
             x = x_buf[:, :width]
             gate = jnp.dot(x, gate_ref[0, :, cols], preferred_element_type=jnp.float32)
@@ -244,14 +207,17 @@
             act = gate / (1.0 + jnp.exp(-gate)) * up * route
             start = side * hidden + i * chunk
             act_buf[:, start : start + chunk] = act.astype(jnp.bfloat16)
-    down_copy.wait()
     sub = width // (PLANE * depth)
     plane = chip % PLANE
     for d in range(PLANE):
         out = 0.0
-        for side, ref in enumerate((own_down, down_buf)):
+        for side in range(2):
+            down_ref = sides[side][2]
             weight = jnp.concatenate(
-                [ref[0, :, lanes((z * PLANE + (plane ^ d)) * sub, sub)] for z in range(depth)],
+                [
+                    down_ref[0, :, lanes((z * PLANE + (plane ^ d)) * sub, sub)]
+                    for z in range(depth)
+                ],
                 axis=1,
             )
             out = out + jnp.dot(
@@ -273,25 +239,17 @@
     total = rows * depth * PLANE
     return pl.pallas_call(
         functools.partial(expert_kernel, depth, chunk),
-        out_shape=(jax.ShapeDtypeStruct((total, width // PLANE), jnp.bfloat16),) * PLANE,
-        in_specs=[VMEM] * (depth + PLANE + 2) + [HBM] * 3,
+        out_shape=(pltpu.VMEM((total, width // PLANE), jnp.bfloat16),) * PLANE,
+        in_specs=[VMEM] * (depth + PLANE + 5),
         out_specs=(VMEM,) * PLANE,
         scratch_shapes=[
             pltpu.VMEM((total, extended), jnp.bfloat16),
-            pltpu.VMEM((1, width, hidden), jnp.bfloat16),
-            pltpu.VMEM((1, width, hidden), jnp.bfloat16),
-            pltpu.VMEM((1, hidden, width), jnp.bfloat16),
             pltpu.VMEM((total, 2 * hidden), jnp.bfloat16),
-            pltpu.SemaphoreType.DMA((2 * (hidden // chunk) + 1,)),
         ],
-        compiler_params=params(46),
-        cost_estimate=pl.CostEstimate(
-            flops=12 * total * width * hidden,
-            bytes_accessed=12 * width * hidden,
-            transcendentals=2 * total * hidden,
-        ),
+        compiler_params=params(16),
+        cost_estimate=SMALL,
         name="experts",
-    )(*line, *packed, *own, *other)
+    )(*line, *packed, *own, *map(in_vmem, other))
 
 
 def plane_sum_kernel(depth, *refs):
@@ -372,9 +330,9 @@
     out_refs, (w_buf, sems) = refs[:PLANE], refs[PLANE:]
     cols = w_buf.shape[1]
     copies = []
-    for i in range(cols // chunk):
-        at = pl.ds(i * chunk, chunk)
-        copies.append(pltpu.make_async_copy(w_hbm.at[:, at], w_buf.at[:, at], sems.at[i]))
+    for i in range(sems.shape[0]):
+        at = lanes(i * META, META)
+        copies.append(pltpu.make_async_copy(w_hbm.at[at], w_buf.at[at], sems.at[i]))
     for copy in copies:
         copy.start()
     rows, extended = mine_ref.shape
@@ -390,8 +348,9 @@
         out_refs[d][:block, cols + META :] = next_ref[at, : part // 2]
         out_refs[d][block:, cols + META :] = next_ref[at, part // 2 :]
     both = jnp.concatenate([mine_ref[:, :part], theirs_ref[:, :part]], axis=0)
+    for copy in copies:
+        copy.wait()
     for i in range(cols // chunk):
-        copies[i].wait()
         at = slice(i * chunk, (i + 1) * chunk)
         product = jnp.dot(both, w_buf[:, at], preferred_element_type=jnp.float32).astype(
             jnp.bfloat16
@@ -405,7 +364,7 @@
     rows, part = following.shape
     cols = weight.shape[1]
     chunk = 512
-    shape = jax.ShapeDtypeStruct((2 * rows // PLANE, cols + META + part // 2), jnp.bfloat16)
+    shape = pltpu.VMEM((2 * rows // PLANE, cols + META + part // 2), jnp.bfloat16)
     return pl.pallas_call(
         functools.partial(projection_kernel, chunk),
         out_shape=(shape,) * PLANE,
@@ -413,14 +372,12 @@
         out_specs=(VMEM,) * PLANE,
         scratch_shapes=[
             pltpu.VMEM((part, cols), jnp.bfloat16),
-            pltpu.SemaphoreType.DMA((cols // chunk,)),
+            pltpu.SemaphoreType.DMA((part // META,)),
         ],
-        compiler_params=params(58),
-        cost_estimate=pl.CostEstimate(
-            flops=4 * rows * part * cols, bytes_accessed=2 * part * cols, transcendentals=0
-        ),
+        compiler_params=params(8),
+        cost_estimate=SMALL,
         name="qkv_projection",
-    )(mine, theirs, following, weight)
+    )(mine, theirs, following, in_hbm(weight))
 
 
 def head_norm_kernel(depth, *refs):
@@ -518,23 +475,23 @@
     high = lax.reduce_precision(dense, 8, 7)
     meta = jnp.concatenate([high, dense - high], axis=1).astype(jnp.bfloat16)
 
-    first_cols = width // 4
-    mine_a, theirs_a, qkv_rows = out_projection(
-        attn_out, out_weight, 0, first_cols, (q_weight, kv_weight)
-    )
     lines = [list(range(i, n_expert, PLANE)) for i in range(PLANE)]
-    qkv = lax.all_gather(qkv_rows, "expert", axis=0, tiled=True, axis_index_groups=lines)
-    mine_b, theirs_b = out_projection(attn_out, out_weight, first_cols, width - first_cols)
-    theirs = (to_core(theirs_a), to_core(theirs_b))
+    qkv = lax.all_gather(
+        jnp.concatenate([q_weight, kv_weight], axis=1),
+        "expert",
+        axis=0,
+        tiled=True,
+        axis_index_groups=lines,
+    )
+    other = [to_core(w_gate), to_core(w_up), to_core(w_down)]
+    mine, theirs = out_projection(attn_out, out_weight)
     tokens, *firsts = first_norm(
-        (mine_a, mine_b), theirs, residual, attn_gain[None, :], meta, depth
-    )
-    own = (w_gate, w_up, w_down)
-    other = [to_core(w) for w in lax.optimization_barrier((*own, tokens))[:3]]
+        (mine,), (to_core(theirs),), residual, attn_gain[None, :], meta, depth
+    )
     line = to_z([tokens] * depth)
     sent = pack(line, firsts[1:])
     packed = to_plane([None, *sent])[1:]
-    own = load(own, sent)
+    own = load((w_gate, w_up, w_down), sent)
     parts = plane_sum(to_plane(experts(line, packed, own, other)), depth)
     scaled, following = second_norm(to_z(parts), firsts[0], packed, input_gain[None, :])
     products = to_plane(projection(scaled, to_core(scaled), following, qkv))

time: 131 us -> 111 us (0.85)
  Pallas kernels: 49.5 us -> 21.4 us
  waiting for transfers between devices: 31 us -> 45.1 us
  local copies, waits for them, and re-layouts: 5.03 us -> 0.34 us
  starting transfers between devices: 30.5 us -> 27.5 us
  other arithmetic: 0.19 us -> 2.21 us
    pallas_call x3 -> x2, Pallas kernels: 33.1 us -> 9.27 us  [the longest x1 5.43 us: out_projection(): pl.pallas_call(functools.partial(out_projection_kernel, chunk), out_shape...]
    ppermute x15, waiting for transfers between devices: 28.7 us -> 40.2 us  [to_expert(): lax.ppermute(value, 'expert', [(i, i ^ offset) for i in range(n_expert)])]
    unnamed x30 -> x14, local copies, waits for them, and re-layouts: 4.74 us -> 0.05 us
    ppermute x15, starting transfers between devices: 29.1 us -> 26.2 us  [to_expert(): lax.ppermute(value, 'expert', [(i, i ^ offset) for i in range(n_expert)])]
    ppermute x6 -> x5, waiting for transfers between devices: 2.26 us -> 4.96 us  [to_core(): return lax.ppermute(value, 'tensor', [(0, 1), (1, 0)])]
    pallas_call x1, Pallas kernels: 11 us -> 8.59 us  [experts(): pl.pallas_call(functools.partial(expert_kernel, depth, chunk), out_shape=...]
    concatenate x0 -> x1, other arithmetic: none -> 2.01 us  [per_device_dense(): jnp.concatenate([q_weight, kv_weight], axis=1)]
    pallas_call x1, Pallas kernels: 4.07 us -> 2.23 us  [projection(): pl.pallas_call(functools.partial(projection_kernel, chunk), out_shape=(sh...]
  transfers between devices with their start and end apart: 22 -> 21, of which waited for: 11 -> 14; matrix products, arithmetic and copies ran while one was open for 0% -> 0% of each run, Pallas kernels for 17% -> 17%
where the time goes in v4:
time: 111 us
  waiting for transfers between devices  45.1 us (41%)
  starting transfers between devices  27.5 us (25%)
  Pallas kernels  21.4 us (19%)
  between operations  14.2 us (13%)
  other arithmetic  2.21 us (2%)
    ppermute x15, waiting for transfers between devices, to_expert(): lax.ppermute(value, 'expert', [(i, i ^ offset) for i in range(n_expert)])  40.2 us
    ppermute x15, starting transfers between devices, to_expert(): lax.ppermute(value, 'expert', [(i, i ^ offset) for i in range(n_expert)])  26.2 us
    pallas_call x1, Pallas kernels, experts(): pl.pallas_call(functools.partial(expert_kernel, depth, chunk), out_shape=...  8.59 us
    pallas_call x1, Pallas kernels, out_projection(): pl.pallas_call(functools.partial(out_projection_kernel, chunk), out_shape...  5.43 us
    ppermute x5, waiting for transfers between devices, to_core(): return lax.ppermute(value, 'tensor', [(0, 1), (1, 0)])  4.96 us
    pallas_call x1, Pallas kernels, load(): pl.pallas_call(load_kernel, out_shape=tuple((pltpu.VMEM(w.shape, w.dtype)...  3.84 us
    pallas_call x1, Pallas kernels, projection(): pl.pallas_call(functools.partial(projection_kernel, chunk), out_shape=(sh...  2.23 us
  transfers between devices with their start and end apart: 21, of which 14 were waited for; matrix products, arithmetic and copies ran while one was open for 0% of the time, Pallas kernels for 17%

profile of v4, /device:TPU:0, one launch (start us, length us, event | category | flops | bytes accessed | tf_op | source)
XLA Modules:
  0.0 110.8 jit_solution(1042935275505036570)
XLA Ops:
  7.2 2.0 %pad_maximum_fusion = bf16[128,2560]{1,0:T(8,128)(2,1)} fusion(bf16[128,512]{1,0:T(8,128)(2,1)} %param.25, bf16[128,2048]{1,0:T(8,128)(2,1)} %param.24), kind=kLoop, calls=%fused_computation | loop fusion | flops 1310720 | bytes 1310720 | tf_op jit(solution)/shard_map/concatenate | solution.py:480
  10.3 5.4 %out_projection.1 = (f32[16,2048]{1,0:T(8,128)S(1)}, f32[16,2048]{1,0:T(8,128)}) custom-call(bf16[32,2048]{1,0:T(8,128)(2,1)} %a_hbm.1, bf16[2048,2048]{1,0:T(8,128)(2,1)} %w_hbm.1), custom_call_target="tpu_custom_call" | custom-call | tf_op jit(solution)/shard_map/out_projection/pallas_call | solution.py:77
  16.4 3.7 %collective-permute-done.refs_1_ = f32[16,2048]{1,0:T(8,128)S(1)} collective-permute-done((f32[16,2048]{1,0:T(8,128)}, f32[16,2048]{1,0:T(8,128)S(1)}, u32[]{:S(2)}, u32[]{:S(2)}) %collective-permute-start) | collective-permute-done | bytes 131104 | tf_op jit(solution)/shard_map/ppermute | solution.py:460
  20.2 2.7 %collective-permute-start.1 = (bf16[16,2176]{1,0:T(8,128)(2,1)S(1)}, bf16[16,2176]{1,0:T(8,128)(2,1)S(1)}, u32[]{:S(2)}, u32[]{:S(2)}) collective-permute-start(bf16[16,2176]{1,0:T(8,128)(2,1)S(1)} %get-tuple-element.32.refs_0_), channel_id=1, source_target_pairs={{0,8},{2,10},{4,12},{6,14},{8,0},{10,2},{12,4},{14,6},{16,24},{18,... | collective-permute-start | bytes 208904 | tf_op jit(solution)/shard_map/ppermute | solution.py:463
  23.0 2.6 %collective-permute-start.2 = (bf16[16,2176]{1,0:T(8,128)(2,1)S(1)}, bf16[16,2176]{1,0:T(8,128)(2,1)S(1)}, u32[]{:S(2)}, u32[]{:S(2)}) collective-permute-start(bf16[16,2176]{1,0:T(8,128)(2,1)S(1)} %get-tuple-element.32.refs_0_), channel_id=1, source_target_pairs={{0,16},{2,18},{4,20},{6,22},{8,24},{10,26},{12,28},{14,30},{16,0},... | collective-permute-start | bytes 208904 | tf_op jit(solution)/shard_map/ppermute | solution.py:463
  25.6 5.3 %collective-permute-done.1.refs_1_ = bf16[16,2176]{1,0:T(8,128)(2,1)S(1)} collective-permute-done((bf16[16,2176]{1,0:T(8,128)(2,1)S(1)}, bf16[16,2176]{1,0:T(8,128)(2,1)S(1)}, u32[]{:S(2)}, u32[]{:S(2)}) %collective-permute-start.1) | collective-permute-done | bytes 69664 | tf_op jit(solution)/shard_map/ppermute | solution.py:463
  30.9 2.5 %collective-permute-start.3 = (bf16[16,2176]{1,0:T(8,128)(2,1)S(1)}, bf16[16,2176]{1,0:T(8,128)(2,1)S(1)}, u32[]{:S(2)}, u32[]{:S(2)}) collective-permute-start(bf16[16,2176]{1,0:T(8,128)(2,1)S(1)} %get-tuple-element.32.refs_0_), channel_id=1, source_target_pairs={{0,24},{2,26},{4,28},{6,30},{8,16},{10,18},{12,20},{14,22},{16,8},... | collective-permute-start | bytes 208904 | tf_op jit(solution)/shard_map/ppermute | solution.py:463
  33.6 5.3 %collective-permute-done.3.refs_3_ = bf16[16,2176]{1,0:T(8,128)(2,1)S(1)} collective-permute-done((bf16[16,2176]{1,0:T(8,128)(2,1)S(1)}, bf16[16,2176]{1,0:T(8,128)(2,1)S(1)}, u32[]{:S(2)}, u32[]{:S(2)}) %collective-permute-start.3) | collective-permute-done | bytes 69664 | tf_op jit(solution)/shard_map/ppermute | solution.py:463
  39.0 1.7 %collective-permute-start.4 = (bf16[64,2304]{1,0:T(8,128)(2,1)S(1)}, bf16[64,2304]{1,0:T(8,128)(2,1)S(1)}, u32[]{:S(2)}, u32[]{:S(2)}) collective-permute-start(bf16[64,2304]{1,0:T(8,128)(2,1)S(1)} %get-tuple-element.36.refs_3_), channel_id=1, source_target_pairs={{0,2},{2,0},{4,6},{6,4},{8,10},{10,8},{12,14},{14,12},{16,18},{18,... | collective-permute-start | bytes 884744 | tf_op jit(solution)/shard_map/ppermute | solution.py:463
  42.2 5.0 %collective-permute-done.4.refs_4_.refs_5_ = bf16[64,2304]{1,0:T(8,128)(2,1)S(1)} collective-permute-done((bf16[64,2304]{1,0:T(8,128)(2,1)S(1)}, bf16[64,2304]{1,0:T(8,128)(2,1)S(1)}, u32[]{:S(2)}, u32[]{:S(2)}) %collective-permute-start.4) | collective-permute-done | bytes 294944 | tf_op jit(solution)/shard_map/ppermute | solution.py:463
  47.2 2.5 %collective-permute-start.6 = (bf16[64,2304]{1,0:T(8,128)(2,1)S(1)}, bf16[64,2304]{1,0:T(8,128)(2,1)S(1)}, u32[]{:S(2)}, u32[]{:S(2)}) collective-permute-start(bf16[64,2304]{1,0:T(8,128)(2,1)S(1)} %get-tuple-element.38.refs_5_), channel_id=1, source_target_pairs={{0,6},{2,4},{4,2},{6,0},{8,14},{10,12},{12,10},{14,8},{16,22},{18,... | collective-permute-start | bytes 884744 | tf_op jit(solution)/shard_map/ppermute | solution.py:463
  49.7 3.8 %load_weights.1 = (bf16[1,2048,768]{2,1,0:T(8,128)(2,1)S(1)}, bf16[1,2048,768]{2,1,0:T(8,128)(2,1)S(1)}, bf16[1,768,2048]{2,1,0:T(8,128)(2,1)S(1)}) custom-call(bf16[1,2048,768]{2,1,0:T(8,128)(2,1)} %refs_0_.1, bf16[1,2048,768]{2,1,0:T(8,128)(2,1)} %refs_1_.1, bf16[1,768,2048]{2,1,0:T(8,128)(2,1)} %refs_2_.3, ...), custom_call_target="tpu_custom_call" | custom-call | tf_op jit(solution)/shard_map/load_weights/pallas_call | solution.py:169
  53.6 1.9 %collective-permute-done.6.refs_6_.refs_7_ = bf16[64,2304]{1,0:T(8,128)(2,1)S(1)} collective-permute-done((bf16[64,2304]{1,0:T(8,128)(2,1)S(1)}, bf16[64,2304]{1,0:T(8,128)(2,1)S(1)}, u32[]{:S(2)}, u32[]{:S(2)}) %collective-permute-start.6) | collective-permute-done | bytes 294944 | tf_op jit(solution)/shard_map/ppermute | solution.py:463
  55.5 8.6 %experts.1 = (bf16[256,512]{1,0:T(8,128)(2,1)S(1)}, bf16[256,512]{1,0:T(8,128)(2,1)S(1)}, bf16[256,512]{1,0:T(8,128)(2,1)S(1)}, bf16[256,512]{1,0:T(8,128)(2,1)S(1)}) custom-call(bf16[16,2176]{1,0:T(8,128)(2,1)S(1)} %get-tuple-element.32.refs_0_, bf16[16,2176]{1,0:T(8,128)(2,1)S(1)} %collective-permute-done.1.refs_1_, ...), custom_call_target="tpu_custom_call" | custom-call | tf_op jit(solution)/shard_map/experts/pallas_call | solution.py:240
  67.7 5.3 %collective-permute-done.10.refs_1_ = bf16[256,512]{1,0:T(8,128)(2,1)S(1)} collective-permute-done((bf16[256,512]{1,0:T(8,128)(2,1)S(1)}, bf16[256,512]{1,0:T(8,128)(2,1)S(1)}, u32[]{:S(2)}, u32[]{:S(2)}) %collective-permute-start.10) | collective-permute-done | bytes 262176 | tf_op jit(solution)/shard_map/ppermute | solution.py:463
  73.0 3.9 %collective-permute-done.11.refs_2_ = bf16[256,512]{1,0:T(8,128)(2,1)S(1)} collective-permute-done((bf16[256,512]{1,0:T(8,128)(2,1)S(1)}, bf16[256,512]{1,0:T(8,128)(2,1)S(1)}, u32[]{:S(2)}, u32[]{:S(2)}) %collective-permute-start.11) | collective-permute-done | bytes 262176 | tf_op jit(solution)/shard_map/ppermute | solution.py:463
  77.0 2.0 %collective-permute-start.13 = (bf16[64,512]{1,0:T(8,128)(2,1)S(1)}, bf16[64,512]{1,0:T(8,128)(2,1)S(1)}, u32[]{:S(2)}, u32[]{:S(2)}) collective-permute-start(bf16[64,512]{1,0:T(8,128)(2,1)S(1)} %get-tuple-element.47), channel_id=1, source_target_pairs={{0,8},{2,10},{4,12},{6,14},{8,0},{10,2},{12,4},{14,6},{16,24},{18,... | collective-permute-start | bytes 196616 | tf_op jit(solution)/shard_map/ppermute | solution.py:463
  79.0 2.1 %collective-permute-start.14 = (bf16[64,512]{1,0:T(8,128)(2,1)S(1)}, bf16[64,512]{1,0:T(8,128)(2,1)S(1)}, u32[]{:S(2)}, u32[]{:S(2)}) collective-permute-start(bf16[64,512]{1,0:T(8,128)(2,1)S(1)} %get-tuple-element.48), channel_id=1, source_target_pairs={{0,16},{2,18},{4,20},{6,22},{8,24},{10,26},{12,28},{14,30},{16,0},... | collective-permute-start | bytes 196616 | tf_op jit(solution)/shard_map/ppermute | solution.py:463
  82.5 1.7 %collective-permute-done.14.refs_2_ = bf16[64,512]{1,0:T(8,128)(2,1)S(1)} collective-permute-done((bf16[64,512]{1,0:T(8,128)(2,1)S(1)}, bf16[64,512]{1,0:T(8,128)(2,1)S(1)}, u32[]{:S(2)}, u32[]{:S(2)}) %collective-permute-start.14) | collective-permute-done | bytes 65568 | tf_op jit(solution)/shard_map/ppermute | solution.py:463
  84.1 3.1 %collective-permute-done.15.refs_3_ = bf16[64,512]{1,0:T(8,128)(2,1)S(1)} collective-permute-done((bf16[64,512]{1,0:T(8,128)(2,1)S(1)}, bf16[64,512]{1,0:T(8,128)(2,1)S(1)}, u32[]{:S(2)}, u32[]{:S(2)}) %collective-permute-start.15) | collective-permute-done | bytes 65568 | tf_op jit(solution)/shard_map/ppermute | solution.py:463
  88.8 2.2 %qkv_projection.1 = (bf16[32,2944]{1,0:T(8,128)(2,1)S(1)}, bf16[32,2944]{1,0:T(8,128)(2,1)S(1)}, bf16[32,2944]{1,0:T(8,128)(2,1)S(1)}, bf16[32,2944]{1,0:T(8,128)(2,1)S(1)}) custom-call(bf16[64,640]{1,0:T(8,128)(2,1)S(1)} %get-tuple-element.51.mine_ref, bf16[64,640]{1,0:T(8,128)(2,1)S(1)} %collective-permute-done.16.theirs_ref, ...), custom_call_target="tpu_custom_call" | custom-call | tf_op jit(solution)/shard_map/qkv_projection/pallas_call | solution.py:368
  94.5 4.1 %collective-permute-done.17.refs_1_ = bf16[32,2944]{1,0:T(8,128)(2,1)S(1)} collective-permute-done((bf16[32,2944]{1,0:T(8,128)(2,1)S(1)}, bf16[32,2944]{1,0:T(8,128)(2,1)S(1)}, u32[]{:S(2)}, u32[]{:S(2)}) %collective-permute-start.17) | collective-permute-done | bytes 188448 | tf_op jit(solution)/shard_map/ppermute | solution.py:463
  98.6 2.7 %collective-permute-done.18.refs_2_ = bf16[32,2944]{1,0:T(8,128)(2,1)S(1)} collective-permute-done((bf16[32,2944]{1,0:T(8,128)(2,1)S(1)}, bf16[32,2944]{1,0:T(8,128)(2,1)S(1)}, u32[]{:S(2)}, u32[]{:S(2)}) %collective-permute-start.18) | collective-permute-done | bytes 188448 | tf_op jit(solution)/shard_map/ppermute | solution.py:463
  101.3 1.8 %collective-permute-done.19.refs_3_ = bf16[32,2944]{1,0:T(8,128)(2,1)S(1)} collective-permute-done((bf16[32,2944]{1,0:T(8,128)(2,1)S(1)}, bf16[32,2944]{1,0:T(8,128)(2,1)S(1)}, u32[]{:S(2)}, u32[]{:S(2)}) %collective-permute-start.19) | collective-permute-done | bytes 188448 | tf_op jit(solution)/shard_map/ppermute | solution.py:463
  (50 shorter events, 14.7 us)
Async XLA Ops:
  7.2 81.6 %all-gather.2.cloned.1.call-start = ((), (), s32[]{:S(2)}) async-start(), calls=%async_computation | async-start | bytes 3276800 | tf_op jit(solution)/shard_map/all_gather | solution.py:479
  9.3 46.2 %collective-permute-start.7 = (bf16[1,2048,768]{2,1,0:T(8,128)(2,1)}, bf16[1,2048,768]{2,1,0:T(8,128)(2,1)S(1)}, u32[]{:S(2)}, u32[]{:S(2)}) collective-permute-start(bf16[1,2048,768]{2,1,0:T(8,128)(2,1)} %refs_0_.1), channel_id=1, source_target_pairs={{0,1},{1,0},{2,3},{3,2},{4,5},{5,4},{6,7},{7,6},{8,9},{9,8},{10,11... | collective-permute-start | bytes 9437192 | tf_op jit(solution)/shard_map/ppermute | solution.py:460
  9.8 45.7 %collective-permute-start.8 = (bf16[1,2048,768]{2,1,0:T(8,128)(2,1)}, bf16[1,2048,768]{2,1,0:T(8,128)(2,1)}, u32[]{:S(2)}, u32[]{:S(2)}) collective-permute-start(bf16[1,2048,768]{2,1,0:T(8,128)(2,1)} %refs_1_.1), channel_id=1, source_target_pairs={{0,1},{1,0},{2,3},{3,2},{4,5},{5,4},{6,7},{7,6},{8,9},{9,8},{10,11... | collective-permute-start | bytes 9437192 | tf_op jit(solution)/shard_map/ppermute | solution.py:460
  9.9 45.6 %collective-permute-start.9 = (bf16[1,768,2048]{2,1,0:T(8,128)(2,1)}, bf16[1,768,2048]{2,1,0:T(8,128)(2,1)}, u32[]{:S(2)}, u32[]{:S(2)}) collective-permute-start(bf16[1,768,2048]{2,1,0:T(8,128)(2,1)} %refs_2_.3), channel_id=1, source_target_pairs={{0,1},{1,0},{2,3},{3,2},{4,5},{5,4},{6,7},{7,6},{8,9},{9,8},{10,11... | collective-permute-start | bytes 9437192 | tf_op jit(solution)/shard_map/ppermute | solution.py:460
  15.8 4.3 %collective-permute-start = (f32[16,2048]{1,0:T(8,128)}, f32[16,2048]{1,0:T(8,128)S(1)}, u32[]{:S(2)}, u32[]{:S(2)}) collective-permute-start(f32[16,2048]{1,0:T(8,128)} %get-tuple-element.31), channel_id=1, source_target_pairs={{0,1},{1,0},{2,3},{3,2},{4,5},{5,4},{6,7},{7,6},{8,9},{9,8},{10,11... | collective-permute-start | bytes 393224 | tf_op jit(solution)/shard_map/ppermute | solution.py:460
  20.2 10.6 %collective-permute-start.1 = (bf16[16,2176]{1,0:T(8,128)(2,1)S(1)}, bf16[16,2176]{1,0:T(8,128)(2,1)S(1)}, u32[]{:S(2)}, u32[]{:S(2)}) collective-permute-start(bf16[16,2176]{1,0:T(8,128)(2,1)S(1)} %get-tuple-element.32.refs_0_), channel_id=1, source_target_pairs={{0,8},{2,10},{4,12},{6,14},{8,0},{10,2},{12,4},{14,6},{16,24},{18,... | collective-permute-start | bytes 208904 | tf_op jit(solution)/shard_map/ppermute | solution.py:463
  23.0 10.6 %collective-permute-start.2 = (bf16[16,2176]{1,0:T(8,128)(2,1)S(1)}, bf16[16,2176]{1,0:T(8,128)(2,1)S(1)}, u32[]{:S(2)}, u32[]{:S(2)}) collective-permute-start(bf16[16,2176]{1,0:T(8,128)(2,1)S(1)} %get-tuple-element.32.refs_0_), channel_id=1, source_target_pairs={{0,16},{2,18},{4,20},{6,22},{8,24},{10,26},{12,28},{14,30},{16,0},... | collective-permute-start | bytes 208904 | tf_op jit(solution)/shard_map/ppermute | solution.py:463
  30.9 8.0 %collective-permute-start.3 = (bf16[16,2176]{1,0:T(8,128)(2,1)S(1)}, bf16[16,2176]{1,0:T(8,128)(2,1)S(1)}, u32[]{:S(2)}, u32[]{:S(2)}) collective-permute-start(bf16[16,2176]{1,0:T(8,128)(2,1)S(1)} %get-tuple-element.32.refs_0_), channel_id=1, source_target_pairs={{0,24},{2,26},{4,28},{6,30},{8,16},{10,18},{12,20},{14,22},{16,8},... | collective-permute-start | bytes 208904 | tf_op jit(solution)/shard_map/ppermute | solution.py:463
  39.0 8.3 %collective-permute-start.4 = (bf16[64,2304]{1,0:T(8,128)(2,1)S(1)}, bf16[64,2304]{1,0:T(8,128)(2,1)S(1)}, u32[]{:S(2)}, u32[]{:S(2)}) collective-permute-start(bf16[64,2304]{1,0:T(8,128)(2,1)S(1)} %get-tuple-element.36.refs_3_), channel_id=1, source_target_pairs={{0,2},{2,0},{4,6},{6,4},{8,10},{10,8},{12,14},{14,12},{16,18},{18,... | collective-permute-start | bytes 884744 | tf_op jit(solution)/shard_map/ppermute | solution.py:463
  40.7 12.9 %collective-permute-start.5 = (bf16[64,2304]{1,0:T(8,128)(2,1)S(1)}, bf16[64,2304]{1,0:T(8,128)(2,1)S(1)}, u32[]{:S(2)}, u32[]{:S(2)}) collective-permute-start(bf16[64,2304]{1,0:T(8,128)(2,1)S(1)} %get-tuple-element.37.refs_4_), channel_id=1, source_target_pairs={{0,4},{2,6},{4,0},{6,2},{8,12},{10,14},{12,8},{14,10},{16,20},{18,... | collective-permute-start | bytes 884744 | tf_op jit(solution)/shard_map/ppermute | solution.py:463
  47.2 8.3 %collective-permute-start.6 = (bf16[64,2304]{1,0:T(8,128)(2,1)S(1)}, bf16[64,2304]{1,0:T(8,128)(2,1)S(1)}, u32[]{:S(2)}, u32[]{:S(2)}) collective-permute-start(bf16[64,2304]{1,0:T(8,128)(2,1)S(1)} %get-tuple-element.38.refs_5_), channel_id=1, source_target_pairs={{0,6},{2,4},{4,2},{6,0},{8,14},{10,12},{12,10},{14,8},{16,22},{18,... | collective-permute-start | bytes 884744 | tf_op jit(solution)/shard_map/ppermute | solution.py:463
  55.5 31.7 %copy-start.2 = (f32[2048]{0:T(1024)S(1)}, f32[2048]{0:T(1024)}, u32[]{:S(2)}) copy-start(f32[2048]{0:T(1024)} %param.23) | copy-start | bytes 24580
  64.1 39.0 %copy-start.4 = (f32[128]{0:T(128)S(1)}, f32[128]{0:T(128)}, u32[]{:S(2)}) copy-start(f32[128]{0:T(128)} %param.26) | copy-start | bytes 1540
  64.1 38.9 %copy-start.5 = (f32[128]{0:T(128)S(1)}, f32[128]{0:T(128)}, u32[]{:S(2)}) copy-start(f32[128]{0:T(128)} %param.27) | copy-start | bytes 1540
  64.1 8.8 %collective-permute-start.10 = (bf16[256,512]{1,0:T(8,128)(2,1)S(1)}, bf16[256,512]{1,0:T(8,128)(2,1)S(1)}, u32[]{:S(2)}, u32[]{:S(2)}) collective-permute-start(bf16[256,512]{1,0:T(8,128)(2,1)S(1)} %get-tuple-element.43), channel_id=1, source_target_pairs={{0,2},{2,0},{4,6},{6,4},{8,10},{10,8},{12,14},{14,12},{16,18},{18,... | collective-permute-start | bytes 786440 | tf_op jit(solution)/shard_map/ppermute | solution.py:463
  65.7 11.2 %collective-permute-start.11 = (bf16[256,512]{1,0:T(8,128)(2,1)S(1)}, bf16[256,512]{1,0:T(8,128)(2,1)S(1)}, u32[]{:S(2)}, u32[]{:S(2)}) collective-permute-start(bf16[256,512]{1,0:T(8,128)(2,1)S(1)} %get-tuple-element.44), channel_id=1, source_target_pairs={{0,4},{2,6},{4,0},{6,2},{8,12},{10,14},{12,8},{14,10},{16,20},{18,... | collective-permute-start | bytes 786440 | tf_op jit(solution)/shard_map/ppermute | solution.py:463
  67.3 9.6 %collective-permute-start.12 = (bf16[256,512]{1,0:T(8,128)(2,1)S(1)}, bf16[256,512]{1,0:T(8,128)(2,1)S(1)}, u32[]{:S(2)}, u32[]{:S(2)}) collective-permute-start(bf16[256,512]{1,0:T(8,128)(2,1)S(1)} %get-tuple-element.45), channel_id=1, source_target_pairs={{0,6},{2,4},{4,2},{6,0},{8,14},{10,12},{12,10},{14,8},{16,22},{18,... | collective-permute-start | bytes 786440 | tf_op jit(solution)/shard_map/ppermute | solution.py:463
  77.0 5.5 %collective-permute-start.13 = (bf16[64,512]{1,0:T(8,128)(2,1)S(1)}, bf16[64,512]{1,0:T(8,128)(2,1)S(1)}, u32[]{:S(2)}, u32[]{:S(2)}) collective-permute-start(bf16[64,512]{1,0:T(8,128)(2,1)S(1)} %get-tuple-element.47), channel_id=1, source_target_pairs={{0,8},{2,10},{4,12},{6,14},{8,0},{10,2},{12,4},{14,6},{16,24},{18,... | collective-permute-start | bytes 196616 | tf_op jit(solution)/shard_map/ppermute | solution.py:463
  79.0 5.2 %collective-permute-start.14 = (bf16[64,512]{1,0:T(8,128)(2,1)S(1)}, bf16[64,512]{1,0:T(8,128)(2,1)S(1)}, u32[]{:S(2)}, u32[]{:S(2)}) collective-permute-start(bf16[64,512]{1,0:T(8,128)(2,1)S(1)} %get-tuple-element.48), channel_id=1, source_target_pairs={{0,16},{2,18},{4,20},{6,22},{8,24},{10,26},{12,28},{14,30},{16,0},... | collective-permute-start | bytes 196616 | tf_op jit(solution)/shard_map/ppermute | solution.py:463
  81.1 6.2 %collective-permute-start.15 = (bf16[64,512]{1,0:T(8,128)(2,1)S(1)}, bf16[64,512]{1,0:T(8,128)(2,1)S(1)}, u32[]{:S(2)}, u32[]{:S(2)}) collective-permute-start(bf16[64,512]{1,0:T(8,128)(2,1)S(1)} %get-tuple-element.49), channel_id=1, source_target_pairs={{0,24},{2,26},{4,28},{6,30},{8,16},{10,18},{12,20},{14,22},{16,8},... | collective-permute-start | bytes 196616 | tf_op jit(solution)/shard_map/ppermute | solution.py:463
  87.4 1.3 %collective-permute-start.16 = (bf16[64,640]{1,0:T(8,128)(2,1)S(1)}, bf16[64,640]{1,0:T(8,128)(2,1)S(1)}, u32[]{:S(2)}, u32[]{:S(2)}) collective-permute-start(bf16[64,640]{1,0:T(8,128)(2,1)S(1)} %get-tuple-element.51.mine_ref), channel_id=1, source_target_pairs={{0,1},{1,0},{2,3},{3,2},{4,5},{5,4},{6,7},{7,6},{8,9},{9,8},{10,11... | collective-permute-start | bytes 245768 | tf_op jit(solution)/shard_map/ppermute | solution.py:460
  91.0 7.6 %collective-permute-start.17 = (bf16[32,2944]{1,0:T(8,128)(2,1)S(1)}, bf16[32,2944]{1,0:T(8,128)(2,1)S(1)}, u32[]{:S(2)}, u32[]{:S(2)}) collective-permute-start(bf16[32,2944]{1,0:T(8,128)(2,1)S(1)} %get-tuple-element.54), channel_id=1, source_target_pairs={{0,2},{2,0},{4,6},{6,4},{8,10},{10,8},{12,14},{14,12},{16,18},{18,... | collective-permute-start | bytes 565256 | tf_op jit(solution)/shard_map/ppermute | solution.py:463
  92.5 8.8 %collective-permute-start.18 = (bf16[32,2944]{1,0:T(8,128)(2,1)S(1)}, bf16[32,2944]{1,0:T(8,128)(2,1)S(1)}, u32[]{:S(2)}, u32[]{:S(2)}) collective-permute-start(bf16[32,2944]{1,0:T(8,128)(2,1)S(1)} %get-tuple-element.55), channel_id=1, source_target_pairs={{0,4},{2,6},{4,0},{6,2},{8,12},{10,14},{12,8},{14,10},{16,20},{18,... | collective-permute-start | bytes 565256 | tf_op jit(solution)/shard_map/ppermute | solution.py:463
  93.2 9.9 %collective-permute-start.19 = (bf16[32,2944]{1,0:T(8,128)(2,1)S(1)}, bf16[32,2944]{1,0:T(8,128)(2,1)S(1)}, u32[]{:S(2)}, u32[]{:S(2)}) collective-permute-start(bf16[32,2944]{1,0:T(8,128)(2,1)S(1)} %get-tuple-element.56), channel_id=1, source_target_pairs={{0,6},{2,4},{4,2},{6,0},{8,14},{10,12},{12,10},{14,8},{16,22},{18,... | collective-permute-start | bytes 565256 | tf_op jit(solution)/shard_map/ppermute | solution.py:463
  (4 other events, 37.2 us)
Sparse Core Ops, SparseCore 0:
  9.6 63.3 all-gather.1

commit v5 on v4

--- a/solution.py
+++ b/solution.py
@@ -130,7 +130,7 @@
 
 
 def pack_kernel(depth, *refs):
-    line, pieces, out_refs = refs[:depth], refs[depth : depth + PLANE - 1], refs[depth + PLANE - 1 :]
+    line, pieces, out_refs = refs[:depth], refs[depth : depth + PLANE], refs[depth + PLANE :]
     rows, extended = line[0].shape
     for ref, piece in zip(out_refs, pieces):
         for z in range(depth):
@@ -141,12 +141,12 @@
 def pack(line, pieces):
     depth = len(line)
     rows, extended = line[0].shape
-    shape = jax.ShapeDtypeStruct((depth * rows, extended + pieces[0].shape[1]), jnp.bfloat16)
+    shape = pltpu.VMEM((depth * rows, extended + pieces[0].shape[1]), jnp.bfloat16)
     return pl.pallas_call(
         functools.partial(pack_kernel, depth),
-        out_shape=(shape,) * (PLANE - 1),
-        in_specs=[VMEM] * (depth + PLANE - 1),
-        out_specs=(VMEM,) * (PLANE - 1),
+        out_shape=(shape,) * PLANE,
+        in_specs=[VMEM] * (depth + PLANE),
+        out_specs=(VMEM,) * PLANE,
         compiler_params=params(2),
         name="pack_tokens",
     )(*line, *pieces)
@@ -178,111 +178,120 @@
     )(*map(in_hbm, weights), *after)
 
 
-def expert_kernel(depth, chunk, *refs):
-    line, packed = refs[:depth], refs[depth : depth + PLANE - 1]
-    at = depth + PLANE - 1
-    sides = (refs[at : at + 3], refs[at + 3 : at + 6])
-    out_refs = refs[at + 6 : at + 6 + PLANE]
-    x_buf, act_buf = refs[at + 6 + PLANE :]
-    width, hidden = sides[0][0].shape[1:]
-    rows, extended = line[0].shape
-    group = depth * rows
-    for z in range(depth):
-        x_buf[z * rows : (z + 1) * rows, :] = line[z][...]
-    for d in range(1, PLANE):
-        x_buf[d * group : (d + 1) * group, :] = packed[d - 1][:, :extended]
+def expert_kernel(depth, chunk, count, *refs):
+    block_refs, (gate_ref, up_ref, down_ref) = refs[:count], refs[count : count + 3]
+    mine_ref, theirs_ref, x_buf, act_buf = refs[count + 3 :]
+    width, hidden = gate_ref.shape[1:]
+    extended = x_buf.shape[1]
+    start = 0
+    for ref in block_refs:
+        rows = ref.shape[0]
+        x_buf[start : start + rows, :] = ref[:, :extended]
+        start += rows
     meta = x_buf[:, width:].astype(jnp.float32)
     lane = lax.broadcasted_iota(jnp.int32, meta.shape, 1)
     chip = lax.axis_index("expert")
-    tensor = lax.axis_index("tensor")
-    for side, (gate_ref, up_ref, _) in enumerate(sides):
-        expert = 2 * chip + (tensor if side == 0 else 1 - tensor)
-        chosen = (lane == expert) | (lane == expert + META // 2)
-        route = jnp.sum(jnp.where(chosen, meta, 0.0), axis=1, keepdims=True)
-        for i in range(hidden // chunk):
-            cols = pl.ds(i * chunk, chunk)
-            x = x_buf[:, :width]
-            gate = jnp.dot(x, gate_ref[0, :, cols], preferred_element_type=jnp.float32)
-            up = jnp.dot(x, up_ref[0, :, cols], preferred_element_type=jnp.float32)
-            act = gate / (1.0 + jnp.exp(-gate)) * up * route
-            start = side * hidden + i * chunk
-            act_buf[:, start : start + chunk] = act.astype(jnp.bfloat16)
+    expert = 2 * chip + lax.axis_index("tensor")
+    chosen = (lane == expert) | (lane == expert + META // 2)
+    route = 0.5 * jnp.sum(jnp.where(chosen, meta, 0.0), axis=1, keepdims=True)
+    for i in range(hidden // chunk):
+        cols = pl.ds(i * chunk, chunk)
+        x = x_buf[:, :width]
+        gate = jnp.dot(x, gate_ref[0, :, cols], preferred_element_type=jnp.float32)
+        up = jnp.dot(x, up_ref[0, :, cols], preferred_element_type=jnp.float32)
+        act = gate * (1.0 + jnp.tanh(0.5 * gate)) * (up * route)
+        act_buf[:, i * chunk : (i + 1) * chunk] = act.astype(jnp.bfloat16)
     sub = width // (PLANE * depth)
+    part = sub * depth
+    half = mine_ref.shape[0]
     plane = chip % PLANE
     for d in range(PLANE):
-        out = 0.0
-        for side in range(2):
-            down_ref = sides[side][2]
-            weight = jnp.concatenate(
-                [
-                    down_ref[0, :, lanes((z * PLANE + (plane ^ d)) * sub, sub)]
-                    for z in range(depth)
-                ],
-                axis=1,
-            )
-            out = out + jnp.dot(
-                act_buf[:, side * hidden : (side + 1) * hidden],
-                weight,
-                preferred_element_type=jnp.float32,
-            )
-        for k in range(PLANE):
-            out_refs[d][k * group : (k + 1) * group, :] = out[
-                (d ^ k) * group : ((d ^ k) + 1) * group
-            ].astype(jnp.bfloat16)
-
-
-def experts(line, packed, own, other):
-    depth = len(line)
-    rows, extended = line[0].shape
-    width, hidden = own[0].shape[1:]
+        weight = jnp.concatenate(
+            [down_ref[0, :, lanes((z * PLANE + (plane ^ d)) * sub, sub)] for z in range(depth)],
+            axis=1,
+        )
+        out = jnp.dot(act_buf[...], weight, preferred_element_type=jnp.float32)
+        cols = slice(d * part, (d + 1) * part)
+        mine_ref[:, cols] = out[:half].astype(jnp.bfloat16)
+        theirs_ref[:, cols] = out[half:].astype(jnp.bfloat16)
+
+
+def experts(blocks, weights, depth):
+    width, hidden = weights[0].shape[1:]
     chunk = 256
-    total = rows * depth * PLANE
-    return pl.pallas_call(
-        functools.partial(expert_kernel, depth, chunk),
-        out_shape=(pltpu.VMEM((total, width // PLANE), jnp.bfloat16),) * PLANE,
-        in_specs=[VMEM] * (depth + PLANE + 5),
-        out_specs=(VMEM,) * PLANE,
+    extended = width + META
+    total = sum(block.shape[0] for block in blocks)
+    half = pltpu.VMEM((total // 2, width), jnp.bfloat16)
+    return pl.pallas_call(
+        functools.partial(expert_kernel, depth, chunk, len(blocks)),
+        out_shape=(half, half),
+        in_specs=[VMEM] * (len(blocks) + 3),
+        out_specs=(VMEM, VMEM),
         scratch_shapes=[
             pltpu.VMEM((total, extended), jnp.bfloat16),
-            pltpu.VMEM((total, 2 * hidden), jnp.bfloat16),
+            pltpu.VMEM((total, hidden), jnp.bfloat16),
         ],
         compiler_params=params(16),
-        cost_estimate=SMALL,
+        cost_estimate=pl.CostEstimate(
+            flops=6 * total * width * hidden, bytes_accessed=0, transcendentals=0
+        ),
         name="experts",
-    )(*line, *packed, *own, *map(in_vmem, other))
+    )(*blocks, *weights)
+
+
+def chip_sum_kernel(mine_ref, theirs_ref, *out_refs):
+    part = out_refs[0].shape[1]
+    for d, ref in enumerate(out_refs):
+        at = slice(d * part, (d + 1) * part)
+        total = mine_ref[:, at].astype(jnp.float32) + theirs_ref[:, at].astype(jnp.float32)
+        ref[...] = total.astype(jnp.bfloat16)
+
+
+def chip_sum(mine, theirs):
+    rows, width = mine.shape
+    return pl.pallas_call(
+        chip_sum_kernel,
+        out_shape=(pltpu.VMEM((rows, width // PLANE), jnp.bfloat16),) * PLANE,
+        in_specs=[VMEM] * 2,
+        out_specs=(VMEM,) * PLANE,
+        compiler_params=params(2),
+        name="chip_sum",
+    )(mine, theirs)
 
 
 def plane_sum_kernel(depth, *refs):
-    in_refs, out_refs = refs[:PLANE], refs[PLANE:]
-    rows = in_refs[0].shape[0] // (PLANE * depth)
-    for d in range(PLANE):
+    halves, out_refs = (refs[:PLANE], refs[PLANE : 2 * PLANE]), refs[2 * PLANE :]
+    group = halves[0][0].shape[0] // 2
+    rows = group // depth
+    for k in range(PLANE):
         for z in range(depth):
-            start = (d * depth + z) * rows
-            at = slice(start, start + rows)
-            total = in_refs[0][at, :].astype(jnp.float32)
-            for ref in in_refs[1:]:
-                total = total + ref[at, :].astype(jnp.float32)
-            out_refs[z][d * rows : (d + 1) * rows, :] = total.astype(jnp.bfloat16)
-
-
-def plane_sum(parts, depth):
-    rows, part = parts[0].shape
+            total = 0.0
+            for d in range(PLANE):
+                block = k ^ d
+                start = block % 2 * group + z * rows
+                part = halves[block // 2][d][start : start + rows, :]
+                total = total + part.astype(jnp.float32)
+            out_refs[z][k * rows : (k + 1) * rows, :] = total.astype(jnp.bfloat16)
+
+
+def plane_sum(first, second, depth):
+    rows, part = first[0].shape
     return pl.pallas_call(
         functools.partial(plane_sum_kernel, depth),
-        out_shape=(jax.ShapeDtypeStruct((rows // depth, part), jnp.bfloat16),) * depth,
-        in_specs=[VMEM] * PLANE,
+        out_shape=(pltpu.VMEM((2 * rows // depth, part), jnp.bfloat16),) * depth,
+        in_specs=[VMEM] * (2 * PLANE),
         out_specs=(VMEM,) * depth,
         compiler_params=params(4),
         name="plane_sum",
-    )(*parts)
+    )(*first, *second)
 
 
 def second_norm_kernel(depth, *refs):
-    parts, first_ref, packed = refs[:depth], refs[depth], refs[depth + 1 : depth + PLANE]
+    parts, packed = refs[:depth], refs[depth : depth + PLANE]
     gain_ref, scaled_ref, next_ref = refs[depth + PLANE :]
-    rows = first_ref.shape[0] // depth
-    sub = first_ref.shape[1]
-    part = depth * sub
+    rows = packed[0].shape[0] // depth
+    part = parts[0].shape[1]
+    sub = part // depth
     lane = lax.broadcasted_iota(jnp.int32, (rows, META), 1)
     plane = lax.axis_index("expert") % PLANE
     gain = jnp.concatenate(
@@ -293,7 +302,7 @@
         total = parts[0][at, :].astype(jnp.float32)
         for ref in parts[1:]:
             total = total + ref[at, :].astype(jnp.float32)
-        source = first_ref if d == 0 else packed[d - 1]
+        source = packed[d]
         skip = source.shape[1] - sub
         first = jnp.concatenate(
             [source[z * rows : (z + 1) * rows, skip:] for z in range(depth)], axis=1
@@ -310,7 +319,7 @@
         ).astype(jnp.bfloat16)
 
 
-def second_norm(parts, first, packed, gain):
+def second_norm(parts, packed, gain):
     depth = len(parts)
     rows, part = parts[0].shape
     return pl.pallas_call(
@@ -323,7 +332,7 @@
         out_specs=(VMEM, VMEM),
         compiler_params=params(4),
         name="second_norm",
-    )(*parts, first, *packed, gain)
+    )(*parts, *packed, gain)
 
 
 def projection_kernel(chunk, mine_ref, theirs_ref, next_ref, w_hbm, *refs):
@@ -483,17 +492,20 @@
         tiled=True,
         axis_index_groups=lines,
     )
-    other = [to_core(w_gate), to_core(w_up), to_core(w_down)]
     mine, theirs = out_projection(attn_out, out_weight)
     tokens, *firsts = first_norm(
         (mine,), (to_core(theirs),), residual, attn_gain[None, :], meta, depth
     )
+    weights = load((w_gate, w_up, w_down), (tokens,))
     line = to_z([tokens] * depth)
-    sent = pack(line, firsts[1:])
-    packed = to_plane([None, *sent])[1:]
-    own = load((w_gate, w_up, w_down), sent)
-    parts = plane_sum(to_plane(experts(line, packed, own, other)), depth)
-    scaled, following = second_norm(to_z(parts), firsts[0], packed, input_gain[None, :])
+    packed = to_plane(pack(line, firsts))
+    near, far = packed[:2], packed[2:]
+    sums = []
+    for blocks in (near, far):
+        mine, theirs = experts((*blocks, *map(to_core, blocks)), weights, depth)
+        sums.append(to_plane(chip_sum(mine, to_core(theirs))))
+    parts = plane_sum(*sums, depth)
+    scaled, following = second_norm(to_z(parts), packed, input_gain[None, :])
     products = to_plane(projection(scaled, to_core(scaled), following, qkv))
     return head_norm(
         products,

time: 111 us -> 109 us (0.982)
  starting transfers between devices: 27.5 us -> 31.8 us
  waiting for transfers between devices: 45.1 us -> 41.6 us
  Pallas kernels: 21.4 us -> 18.4 us
    ppermute x15 -> x18, starting transfers between devices: 26.2 us -> 30 us  [to_expert(): lax.ppermute(value, 'expert', [(i, i ^ offset) for i in range(n_expert)])]
    ppermute x5 -> x8, waiting for transfers between devices: 4.96 us -> 1.76 us  [to_core(): return lax.ppermute(value, 'tensor', [(0, 1), (1, 0)])]
    pallas_call x2 -> x5, Pallas kernels: 8.72 us -> 6.26 us  [the longest x2 5.89 us: experts(): pl.pallas_call(functools.partial(expert_kernel, depth, chunk, len(blocks)...]
    ppermute x15 -> x18, waiting for transfers between devices: 40.2 us -> 39.8 us  [to_expert(): lax.ppermute(value, 'expert', [(i, i ^ offset) for i in range(n_expert)])]
  transfers between devices with their start and end apart: 21 -> 27, of which waited for: 14 -> 13; matrix products, arithmetic and copies ran while one was open for 0% -> 0% of each run, Pallas kernels for 17% -> 14%
where the time goes in v5:
time: 109 us; the launch traced here: 108 us
  waiting for transfers between devices  41.6 us (38%)
  starting transfers between devices  31.8 us (29%)
  Pallas kernels  18.4 us (17%)
  between operations  14.2 us (13%)
  other arithmetic  2.19 us (2%)
    ppermute x18, waiting for transfers between devices, to_expert(): lax.ppermute(value, 'expert', [(i, i ^ offset) for i in range(n_expert)])  39.8 us
    ppermute x18, starting transfers between devices, to_expert(): lax.ppermute(value, 'expert', [(i, i ^ offset) for i in range(n_expert)])  30 us
    pallas_call x2, Pallas kernels, experts(): pl.pallas_call(functools.partial(expert_kernel, depth, chunk, len(blocks)...  5.89 us
    pallas_call x1, Pallas kernels, out_projection(): pl.pallas_call(functools.partial(out_projection_kernel, chunk), out_shape...  4.8 us
    pallas_call x1, Pallas kernels, load(): pl.pallas_call(load_kernel, out_shape=tuple((pltpu.VMEM(w.shape, w.dtype)...  3.84 us
    pallas_call x1, Pallas kernels, projection(): pl.pallas_call(functools.partial(projection_kernel, chunk), out_shape=(sh...  2.23 us
  transfers between devices with their start and end apart: 27, of which 13 were waited for; matrix products, arithmetic and copies ran while one was open for 0% of the time, Pallas kernels for 14%

profile of v5, /device:TPU:0, one launch (start us, length us, event | category | flops | bytes accessed | tf_op | source)
XLA Modules:
  0.0 108.5 jit_solution(9386321238153486662)
XLA Ops:
  7.2 2.0 %pad_maximum_fusion = bf16[128,2560]{1,0:T(8,128)(2,1)} fusion(bf16[128,512]{1,0:T(8,128)(2,1)} %param.25, bf16[128,2048]{1,0:T(8,128)(2,1)} %param.24), kind=kLoop, calls=%fused_computation | loop fusion | flops 1310720 | bytes 1310720 | tf_op jit(solution)/shard_map/concatenate | solution.py:489
  9.3 4.8 %out_projection.1 = (f32[16,2048]{1,0:T(8,128)S(1)}, f32[16,2048]{1,0:T(8,128)S(1)}) custom-call(bf16[32,2048]{1,0:T(8,128)(2,1)} %a_hbm.1, bf16[2048,2048]{1,0:T(8,128)(2,1)} %w_hbm.1), custom_call_target="tpu_custom_call" | custom-call | tf_op jit(solution)/shard_map/out_projection/pallas_call | solution.py:77
  15.7 3.0 %collective-permute-start.1 = (bf16[16,2176]{1,0:T(8,128)(2,1)S(1)}, bf16[16,2176]{1,0:T(8,128)(2,1)S(1)}, u32[]{:S(2)}, u32[]{:S(2)}) collective-permute-start(bf16[16,2176]{1,0:T(8,128)(2,1)S(1)} %get-tuple-element.41.refs_0_.refs_3_), channel_id=1, source_target_pairs={{0,8},{2,10},{4,12},{6,14},{8,0},{10,2},{12,4},{14,6},{16,24},{18,... | collective-permute-start | bytes 208904 | tf_op jit(solution)/shard_map/ppermute | solution.py:472
  18.7 2.6 %collective-permute-start.2 = (bf16[16,2176]{1,0:T(8,128)(2,1)S(1)}, bf16[16,2176]{1,0:T(8,128)(2,1)S(1)}, u32[]{:S(2)}, u32[]{:S(2)}) collective-permute-start(bf16[16,2176]{1,0:T(8,128)(2,1)S(1)} %get-tuple-element.41.refs_0_.refs_3_), channel_id=1, source_target_pairs={{0,16},{2,18},{4,20},{6,22},{8,24},{10,26},{12,28},{14,30},{16,0},... | collective-permute-start | bytes 208904 | tf_op jit(solution)/shard_map/ppermute | solution.py:472
  21.3 8.6 %collective-permute-done.2.refs_2_ = bf16[16,2176]{1,0:T(8,128)(2,1)S(1)} collective-permute-done((bf16[16,2176]{1,0:T(8,128)(2,1)S(1)}, bf16[16,2176]{1,0:T(8,128)(2,1)S(1)}, u32[]{:S(2)}, u32[]{:S(2)}) %collective-permute-start.2) | collective-permute-done | bytes 69664 | tf_op jit(solution)/shard_map/ppermute | solution.py:472
  30.1 1.6 %collective-permute-start.11 = (bf16[64,2304]{1,0:T(8,128)(2,1)S(1)}, bf16[64,2304]{1,0:T(8,128)(2,1)S(1)}, u32[]{:S(2)}, u32[]{:S(2)}) collective-permute-start(bf16[64,2304]{1,0:T(8,128)(2,1)S(1)} %get-tuple-element.57), channel_id=1, source_target_pairs={{0,4},{2,6},{4,0},{6,2},{8,12},{10,14},{12,8},{14,10},{16,20},{18,... | collective-permute-start | bytes 884744 | tf_op jit(solution)/shard_map/ppermute | solution.py:472
  31.7 1.4 %collective-permute-start.12 = (bf16[64,2304]{1,0:T(8,128)(2,1)S(1)}, bf16[64,2304]{1,0:T(8,128)(2,1)S(1)}, u32[]{:S(2)}, u32[]{:S(2)}) collective-permute-start(bf16[64,2304]{1,0:T(8,128)(2,1)S(1)} %get-tuple-element.58), channel_id=1, source_target_pairs={{0,6},{2,4},{4,2},{6,0},{8,14},{10,12},{12,10},{14,8},{16,22},{18,... | collective-permute-start | bytes 884744 | tf_op jit(solution)/shard_map/ppermute | solution.py:472
  33.6 9.2 %collective-permute-done.11.refs_0_.refs_6_ = bf16[64,2304]{1,0:T(8,128)(2,1)S(1)} collective-permute-done((bf16[64,2304]{1,0:T(8,128)(2,1)S(1)}, bf16[64,2304]{1,0:T(8,128)(2,1)S(1)}, u32[]{:S(2)}, u32[]{:S(2)}) %collective-permute-start.11) | collective-permute-done | bytes 294944 | tf_op jit(solution)/shard_map/ppermute | solution.py:472
  44.1 3.8 %load_weights.1 = (bf16[1,2048,768]{2,1,0:T(8,128)(2,1)S(1)}, bf16[1,2048,768]{2,1,0:T(8,128)(2,1)S(1)}, bf16[1,768,2048]{2,1,0:T(8,128)(2,1)S(1)}) custom-call(bf16[1,2048,768]{2,1,0:T(8,128)(2,1)} %refs_0_.1, bf16[1,2048,768]{2,1,0:T(8,128)(2,1)} %refs_1_.1, bf16[1,768,2048]{2,1,0:T(8,128)(2,1)} %refs_2_.3, ...), custom_call_target="tpu_custom_call" | custom-call | tf_op jit(solution)/shard_map/load_weights/pallas_call | solution.py:169
  47.9 2.9 %experts.3 = (bf16[128,2048]{1,0:T(8,128)(2,1)S(1)}, bf16[128,2048]{1,0:T(8,128)(2,1)S(1)}) custom-call(bf16[64,2304]{1,0:T(8,128)(2,1)S(1)} %collective-permute-done.11.refs_0_.refs_6_, bf16[64,2304]{1,0:T(8,128)(2,1)S(1)} %collective-permute-done.12.refs_1_.refs_7_, bf16[64,2304]{1,0:T(8,128)(2,1)S(1)} %collective-permute-done.13.refs_2_, ...), custom_call_target="tpu_custom_call" | custom-call | flops 2415919104 | tf_op jit(solution)/shard_map/experts/pallas_call | solution.py:225
  51.5 2.9 %experts.2 = (bf16[128,2048]{1,0:T(8,128)(2,1)S(1)}, bf16[128,2048]{1,0:T(8,128)(2,1)S(1)}) custom-call(bf16[64,2304]{1,0:T(8,128)(2,1)S(1)} %get-tuple-element.46.refs_0_.refs_4_, bf16[64,2304]{1,0:T(8,128)(2,1)S(1)} %collective-permute-done.4.refs_1_.refs_5_, bf16[64,2304]{1,0:T(8,128)(2,1)S(1)} %collective-permute-done.5.refs_2_, ...), custom_call_target="tpu_custom_call" | custom-call | flops 2415919104 | tf_op jit(solution)/shard_map/experts/pallas_call | solution.py:225
  54.6 1.5 %collective-permute-start.16 = (bf16[128,512]{1,0:T(8,128)(2,1)S(1)}, bf16[128,512]{1,0:T(8,128)(2,1)S(1)}, u32[]{:S(2)}, u32[]{:S(2)}) collective-permute-start(bf16[128,512]{1,0:T(8,128)(2,1)S(1)} %get-tuple-element.62), channel_id=1, source_target_pairs={{0,2},{2,0},{4,6},{6,4},{8,10},{10,8},{12,14},{14,12},{16,18},{18,... | collective-permute-start | bytes 393224 | tf_op jit(solution)/shard_map/ppermute | solution.py:472
  56.2 1.5 %collective-permute-start.17 = (bf16[128,512]{1,0:T(8,128)(2,1)S(1)}, bf16[128,512]{1,0:T(8,128)(2,1)S(1)}, u32[]{:S(2)}, u32[]{:S(2)}) collective-permute-start(bf16[128,512]{1,0:T(8,128)(2,1)S(1)} %get-tuple-element.63), channel_id=1, source_target_pairs={{0,4},{2,6},{4,0},{6,2},{8,12},{10,14},{12,8},{14,10},{16,20},{18,... | collective-permute-start | bytes 393224 | tf_op jit(solution)/shard_map/ppermute | solution.py:472
  58.3 2.5 %collective-permute-start.10 = (bf16[128,512]{1,0:T(8,128)(2,1)S(1)}, bf16[128,512]{1,0:T(8,128)(2,1)S(1)}, u32[]{:S(2)}, u32[]{:S(2)}) collective-permute-start(bf16[128,512]{1,0:T(8,128)(2,1)S(1)} %get-tuple-element.56), channel_id=1, source_target_pairs={{0,6},{2,4},{4,2},{6,0},{8,14},{10,12},{12,10},{14,8},{16,22},{18,... | collective-permute-start | bytes 393224 | tf_op jit(solution)/shard_map/ppermute | solution.py:472
  62.4 4.8 %collective-permute-done.17.refs_6_ = bf16[128,512]{1,0:T(8,128)(2,1)S(1)} collective-permute-done((bf16[128,512]{1,0:T(8,128)(2,1)S(1)}, bf16[128,512]{1,0:T(8,128)(2,1)S(1)}, u32[]{:S(2)}, u32[]{:S(2)}) %collective-permute-start.17) | collective-permute-done | bytes 131104 | tf_op jit(solution)/shard_map/ppermute | solution.py:472
  70.4 5.6 %collective-permute-start.19 = (bf16[64,512]{1,0:T(8,128)(2,1)S(1)}, bf16[64,512]{1,0:T(8,128)(2,1)S(1)}, u32[]{:S(2)}, u32[]{:S(2)}) collective-permute-start(bf16[64,512]{1,0:T(8,128)(2,1)S(1)} %get-tuple-element.66), channel_id=1, source_target_pairs={{0,8},{2,10},{4,12},{6,14},{8,0},{10,2},{12,4},{14,6},{16,24},{18,... | collective-permute-start | bytes 196616 | tf_op jit(solution)/shard_map/ppermute | solution.py:472
  75.9 2.7 %collective-permute-start.20 = (bf16[64,512]{1,0:T(8,128)(2,1)S(1)}, bf16[64,512]{1,0:T(8,128)(2,1)S(1)}, u32[]{:S(2)}, u32[]{:S(2)}) collective-permute-start(bf16[64,512]{1,0:T(8,128)(2,1)S(1)} %get-tuple-element.67), channel_id=1, source_target_pairs={{0,16},{2,18},{4,20},{6,22},{8,24},{10,26},{12,28},{14,30},{16,0},... | collective-permute-start | bytes 196616 | tf_op jit(solution)/shard_map/ppermute | solution.py:472
  78.6 1.4 %collective-permute-start.21 = (bf16[64,512]{1,0:T(8,128)(2,1)S(1)}, bf16[64,512]{1,0:T(8,128)(2,1)S(1)}, u32[]{:S(2)}, u32[]{:S(2)}) collective-permute-start(bf16[64,512]{1,0:T(8,128)(2,1)S(1)} %get-tuple-element.68), channel_id=1, source_target_pairs={{0,24},{2,26},{4,28},{6,30},{8,16},{10,18},{12,20},{14,22},{16,8},... | collective-permute-start | bytes 196616 | tf_op jit(solution)/shard_map/ppermute | solution.py:472
  81.1 3.7 %collective-permute-done.21.refs_3_ = bf16[64,512]{1,0:T(8,128)(2,1)S(1)} collective-permute-done((bf16[64,512]{1,0:T(8,128)(2,1)S(1)}, bf16[64,512]{1,0:T(8,128)(2,1)S(1)}, u32[]{:S(2)}, u32[]{:S(2)}) %collective-permute-start.21) | collective-permute-done | bytes 65568 | tf_op jit(solution)/shard_map/ppermute | solution.py:472
  86.3 2.2 %qkv_projection.1 = (bf16[32,2944]{1,0:T(8,128)(2,1)S(1)}, bf16[32,2944]{1,0:T(8,128)(2,1)S(1)}, bf16[32,2944]{1,0:T(8,128)(2,1)S(1)}, bf16[32,2944]{1,0:T(8,128)(2,1)S(1)}) custom-call(bf16[64,640]{1,0:T(8,128)(2,1)S(1)} %get-tuple-element.69.mine_ref, bf16[64,640]{1,0:T(8,128)(2,1)S(1)} %collective-permute-done.22.theirs_ref, ...), custom_call_target="tpu_custom_call" | custom-call | tf_op jit(solution)/shard_map/qkv_projection/pallas_call | solution.py:377
  88.6 1.6 %collective-permute-start.23 = (bf16[32,2944]{1,0:T(8,128)(2,1)S(1)}, bf16[32,2944]{1,0:T(8,128)(2,1)S(1)}, u32[]{:S(2)}, u32[]{:S(2)}) collective-permute-start(bf16[32,2944]{1,0:T(8,128)(2,1)S(1)} %get-tuple-element.72), channel_id=1, source_target_pairs={{0,2},{2,0},{4,6},{6,4},{8,10},{10,8},{12,14},{14,12},{16,18},{18,... | collective-permute-start | bytes 565256 | tf_op jit(solution)/shard_map/ppermute | solution.py:472
  90.6 1.5 %collective-permute-start.25 = (bf16[32,2944]{1,0:T(8,128)(2,1)S(1)}, bf16[32,2944]{1,0:T(8,128)(2,1)S(1)}, u32[]{:S(2)}, u32[]{:S(2)}) collective-permute-start(bf16[32,2944]{1,0:T(8,128)(2,1)S(1)} %get-tuple-element.74), channel_id=1, source_target_pairs={{0,6},{2,4},{4,2},{6,0},{8,14},{10,12},{12,10},{14,8},{16,22},{18,... | collective-permute-start | bytes 565256 | tf_op jit(solution)/shard_map/ppermute | solution.py:472
  92.1 4.1 %collective-permute-done.23.refs_1_ = bf16[32,2944]{1,0:T(8,128)(2,1)S(1)} collective-permute-done((bf16[32,2944]{1,0:T(8,128)(2,1)S(1)}, bf16[32,2944]{1,0:T(8,128)(2,1)S(1)}, u32[]{:S(2)}, u32[]{:S(2)}) %collective-permute-start.23) | collective-permute-done | bytes 188448 | tf_op jit(solution)/shard_map/ppermute | solution.py:472
  96.2 4.5 %collective-permute-done.24.refs_2_ = bf16[32,2944]{1,0:T(8,128)(2,1)S(1)} collective-permute-done((bf16[32,2944]{1,0:T(8,128)(2,1)S(1)}, bf16[32,2944]{1,0:T(8,128)(2,1)S(1)}, u32[]{:S(2)}, u32[]{:S(2)}) %collective-permute-start.24) | collective-permute-done | bytes 188448 | tf_op jit(solution)/shard_map/ppermute | solution.py:472
  (65 shorter events, 13.6 us)
Async XLA Ops:
  7.2 79.1 %all-gather.2.cloned.1.call-start = ((), (), s32[]{:S(2)}) async-start(), calls=%async_computation | async-start | bytes 3276800 | tf_op jit(solution)/shard_map/all_gather | solution.py:488
  15.7 5.6 %collective-permute-start.1 = (bf16[16,2176]{1,0:T(8,128)(2,1)S(1)}, bf16[16,2176]{1,0:T(8,128)(2,1)S(1)}, u32[]{:S(2)}, u32[]{:S(2)}) collective-permute-start(bf16[16,2176]{1,0:T(8,128)(2,1)S(1)} %get-tuple-element.41.refs_0_.refs_3_), channel_id=1, source_target_pairs={{0,8},{2,10},{4,12},{6,14},{8,0},{10,2},{12,4},{14,6},{16,24},{18,... | collective-permute-start | bytes 208904 | tf_op jit(solution)/shard_map/ppermute | solution.py:472
  18.7 11.2 %collective-permute-start.2 = (bf16[16,2176]{1,0:T(8,128)(2,1)S(1)}, bf16[16,2176]{1,0:T(8,128)(2,1)S(1)}, u32[]{:S(2)}, u32[]{:S(2)}) collective-permute-start(bf16[16,2176]{1,0:T(8,128)(2,1)S(1)} %get-tuple-element.41.refs_0_.refs_3_), channel_id=1, source_target_pairs={{0,16},{2,18},{4,20},{6,22},{8,24},{10,26},{12,28},{14,30},{16,0},... | collective-permute-start | bytes 208904 | tf_op jit(solution)/shard_map/ppermute | solution.py:472
  21.3 8.6 %collective-permute-start.3 = (bf16[16,2176]{1,0:T(8,128)(2,1)S(1)}, bf16[16,2176]{1,0:T(8,128)(2,1)S(1)}, u32[]{:S(2)}, u32[]{:S(2)}) collective-permute-start(bf16[16,2176]{1,0:T(8,128)(2,1)S(1)} %get-tuple-element.41.refs_0_.refs_3_), channel_id=1, source_target_pairs={{0,24},{2,26},{4,28},{6,30},{8,16},{10,18},{12,20},{14,22},{16,8},... | collective-permute-start | bytes 208904 | tf_op jit(solution)/shard_map/ppermute | solution.py:472
  30.1 12.8 %collective-permute-start.11 = (bf16[64,2304]{1,0:T(8,128)(2,1)S(1)}, bf16[64,2304]{1,0:T(8,128)(2,1)S(1)}, u32[]{:S(2)}, u32[]{:S(2)}) collective-permute-start(bf16[64,2304]{1,0:T(8,128)(2,1)S(1)} %get-tuple-element.57), channel_id=1, source_target_pairs={{0,4},{2,6},{4,0},{6,2},{8,12},{10,14},{12,8},{14,10},{16,20},{18,... | collective-permute-start | bytes 884744 | tf_op jit(solution)/shard_map/ppermute | solution.py:472
  31.7 11.2 %collective-permute-start.12 = (bf16[64,2304]{1,0:T(8,128)(2,1)S(1)}, bf16[64,2304]{1,0:T(8,128)(2,1)S(1)}, u32[]{:S(2)}, u32[]{:S(2)}) collective-permute-start(bf16[64,2304]{1,0:T(8,128)(2,1)S(1)} %get-tuple-element.58), channel_id=1, source_target_pairs={{0,6},{2,4},{4,2},{6,0},{8,14},{10,12},{12,10},{14,8},{16,22},{18,... | collective-permute-start | bytes 884744 | tf_op jit(solution)/shard_map/ppermute | solution.py:472
  33.1 11.0 %collective-permute-start.4 = (bf16[64,2304]{1,0:T(8,128)(2,1)S(1)}, bf16[64,2304]{1,0:T(8,128)(2,1)S(1)}, u32[]{:S(2)}, u32[]{:S(2)}) collective-permute-start(bf16[64,2304]{1,0:T(8,128)(2,1)S(1)} %get-tuple-element.47), channel_id=1, source_target_pairs={{0,2},{2,0},{4,6},{6,4},{8,10},{10,8},{12,14},{14,12},{16,18},{18,... | collective-permute-start | bytes 884744 | tf_op jit(solution)/shard_map/ppermute | solution.py:472
  42.8 5.1 %collective-permute-start.13 = (bf16[64,2304]{1,0:T(8,128)(2,1)S(1)}, bf16[64,2304]{1,0:T(8,128)(2,1)S(1)}, u32[]{:S(2)}, u32[]{:S(2)}) collective-permute-start(bf16[64,2304]{1,0:T(8,128)(2,1)S(1)} %collective-permute-done.11.refs_0_.refs_6_), channel_id=1, source_target_pairs={{0,1},{1,0},{2,3},{3,2},{4,5},{5,4},{6,7},{7,6},{8,9},{9,8},{10,11... | collective-permute-start | bytes 884744 | tf_op jit(solution)/shard_map/ppermute | solution.py:469
  42.9 5.1 %collective-permute-start.14 = (bf16[64,2304]{1,0:T(8,128)(2,1)S(1)}, bf16[64,2304]{1,0:T(8,128)(2,1)S(1)}, u32[]{:S(2)}, u32[]{:S(2)}) collective-permute-start(bf16[64,2304]{1,0:T(8,128)(2,1)S(1)} %collective-permute-done.12.refs_1_.refs_7_), channel_id=1, source_target_pairs={{0,1},{1,0},{2,3},{3,2},{4,5},{5,4},{6,7},{7,6},{8,9},{9,8},{10,11... | collective-permute-start | bytes 884744 | tf_op jit(solution)/shard_map/ppermute | solution.py:469
  43.4 8.1 %collective-permute-start.5 = (bf16[64,2304]{1,0:T(8,128)(2,1)S(1)}, bf16[64,2304]{1,0:T(8,128)(2,1)S(1)}, u32[]{:S(2)}, u32[]{:S(2)}) collective-permute-start(bf16[64,2304]{1,0:T(8,128)(2,1)S(1)} %get-tuple-element.46.refs_0_.refs_4_), channel_id=1, source_target_pairs={{0,1},{1,0},{2,3},{3,2},{4,5},{5,4},{6,7},{7,6},{8,9},{9,8},{10,11... | collective-permute-start | bytes 884744 | tf_op jit(solution)/shard_map/ppermute | solution.py:469
  44.1 7.4 %collective-permute-start.6 = (bf16[64,2304]{1,0:T(8,128)(2,1)S(1)}, bf16[64,2304]{1,0:T(8,128)(2,1)S(1)}, u32[]{:S(2)}, u32[]{:S(2)}) collective-permute-start(bf16[64,2304]{1,0:T(8,128)(2,1)S(1)} %collective-permute-done.4.refs_1_.refs_5_), channel_id=1, source_target_pairs={{0,1},{1,0},{2,3},{3,2},{4,5},{5,4},{6,7},{7,6},{8,9},{9,8},{10,11... | collective-permute-start | bytes 884744 | tf_op jit(solution)/shard_map/ppermute | solution.py:469
  54.4 3.8 %collective-permute-start.7 = (bf16[128,2048]{1,0:T(8,128)(2,1)S(1)}, bf16[128,2048]{1,0:T(8,128)(2,1)S(1)}, u32[]{:S(2)}, u32[]{:S(2)}) collective-permute-start(bf16[128,2048]{1,0:T(8,128)(2,1)S(1)} %get-tuple-element.52), channel_id=1, source_target_pairs={{0,1},{1,0},{2,3},{3,2},{4,5},{5,4},{6,7},{7,6},{8,9},{9,8},{10,11... | collective-permute-start | bytes 1572872 | tf_op jit(solution)/shard_map/ppermute | solution.py:469
  54.6 6.7 %collective-permute-start.16 = (bf16[128,512]{1,0:T(8,128)(2,1)S(1)}, bf16[128,512]{1,0:T(8,128)(2,1)S(1)}, u32[]{:S(2)}, u32[]{:S(2)}) collective-permute-start(bf16[128,512]{1,0:T(8,128)(2,1)S(1)} %get-tuple-element.62), channel_id=1, source_target_pairs={{0,2},{2,0},{4,6},{6,4},{8,10},{10,8},{12,14},{14,12},{16,18},{18,... | collective-permute-start | bytes 393224 | tf_op jit(solution)/shard_map/ppermute | solution.py:472
  56.2 11.0 %collective-permute-start.17 = (bf16[128,512]{1,0:T(8,128)(2,1)S(1)}, bf16[128,512]{1,0:T(8,128)(2,1)S(1)}, u32[]{:S(2)}, u32[]{:S(2)}) collective-permute-start(bf16[128,512]{1,0:T(8,128)(2,1)S(1)} %get-tuple-element.63), channel_id=1, source_target_pairs={{0,4},{2,6},{4,0},{6,2},{8,12},{10,14},{12,8},{14,10},{16,20},{18,... | collective-permute-start | bytes 393224 | tf_op jit(solution)/shard_map/ppermute | solution.py:472
  57.7 9.5 %collective-permute-start.18 = (bf16[128,512]{1,0:T(8,128)(2,1)S(1)}, bf16[128,512]{1,0:T(8,128)(2,1)S(1)}, u32[]{:S(2)}, u32[]{:S(2)}) collective-permute-start(bf16[128,512]{1,0:T(8,128)(2,1)S(1)} %get-tuple-element.64), channel_id=1, source_target_pairs={{0,6},{2,4},{4,2},{6,0},{8,14},{10,12},{12,10},{14,8},{16,22},{18,... | collective-permute-start | bytes 393224 | tf_op jit(solution)/shard_map/ppermute | solution.py:472
  58.3 9.5 %collective-permute-start.10 = (bf16[128,512]{1,0:T(8,128)(2,1)S(1)}, bf16[128,512]{1,0:T(8,128)(2,1)S(1)}, u32[]{:S(2)}, u32[]{:S(2)}) collective-permute-start(bf16[128,512]{1,0:T(8,128)(2,1)S(1)} %get-tuple-element.56), channel_id=1, source_target_pairs={{0,6},{2,4},{4,2},{6,0},{8,14},{10,12},{12,10},{14,8},{16,22},{18,... | collective-permute-start | bytes 393224 | tf_op jit(solution)/shard_map/ppermute | solution.py:472
  60.8 8.2 %collective-permute-start.8 = (bf16[128,512]{1,0:T(8,128)(2,1)S(1)}, bf16[128,512]{1,0:T(8,128)(2,1)S(1)}, u32[]{:S(2)}, u32[]{:S(2)}) collective-permute-start(bf16[128,512]{1,0:T(8,128)(2,1)S(1)} %get-tuple-element.54), channel_id=1, source_target_pairs={{0,2},{2,0},{4,6},{6,4},{8,10},{10,8},{12,14},{14,12},{16,18},{18,... | collective-permute-start | bytes 393224 | tf_op jit(solution)/shard_map/ppermute | solution.py:472
  61.3 8.9 %collective-permute-start.9 = (bf16[128,512]{1,0:T(8,128)(2,1)S(1)}, bf16[128,512]{1,0:T(8,128)(2,1)S(1)}, u32[]{:S(2)}, u32[]{:S(2)}) collective-permute-start(bf16[128,512]{1,0:T(8,128)(2,1)S(1)} %get-tuple-element.55), channel_id=1, source_target_pairs={{0,4},{2,6},{4,0},{6,2},{8,12},{10,14},{12,8},{14,10},{16,20},{18,... | collective-permute-start | bytes 393224 | tf_op jit(solution)/shard_map/ppermute | solution.py:472
  70.4 9.6 %collective-permute-start.19 = (bf16[64,512]{1,0:T(8,128)(2,1)S(1)}, bf16[64,512]{1,0:T(8,128)(2,1)S(1)}, u32[]{:S(2)}, u32[]{:S(2)}) collective-permute-start(bf16[64,512]{1,0:T(8,128)(2,1)S(1)} %get-tuple-element.66), channel_id=1, source_target_pairs={{0,8},{2,10},{4,12},{6,14},{8,0},{10,2},{12,4},{14,6},{16,24},{18,... | collective-permute-start | bytes 196616 | tf_op jit(solution)/shard_map/ppermute | solution.py:472
  75.9 5.2 %collective-permute-start.20 = (bf16[64,512]{1,0:T(8,128)(2,1)S(1)}, bf16[64,512]{1,0:T(8,128)(2,1)S(1)}, u32[]{:S(2)}, u32[]{:S(2)}) collective-permute-start(bf16[64,512]{1,0:T(8,128)(2,1)S(1)} %get-tuple-element.67), channel_id=1, source_target_pairs={{0,16},{2,18},{4,20},{6,22},{8,24},{10,26},{12,28},{14,30},{16,0},... | collective-permute-start | bytes 196616 | tf_op jit(solution)/shard_map/ppermute | solution.py:472
  78.6 6.2 %collective-permute-start.21 = (bf16[64,512]{1,0:T(8,128)(2,1)S(1)}, bf16[64,512]{1,0:T(8,128)(2,1)S(1)}, u32[]{:S(2)}, u32[]{:S(2)}) collective-permute-start(bf16[64,512]{1,0:T(8,128)(2,1)S(1)} %get-tuple-element.68), channel_id=1, source_target_pairs={{0,24},{2,26},{4,28},{6,30},{8,16},{10,18},{12,20},{14,22},{16,8},... | collective-permute-start | bytes 196616 | tf_op jit(solution)/shard_map/ppermute | solution.py:472
  88.6 7.6 %collective-permute-start.23 = (bf16[32,2944]{1,0:T(8,128)(2,1)S(1)}, bf16[32,2944]{1,0:T(8,128)(2,1)S(1)}, u32[]{:S(2)}, u32[]{:S(2)}) collective-permute-start(bf16[32,2944]{1,0:T(8,128)(2,1)S(1)} %get-tuple-element.72), channel_id=1, source_target_pairs={{0,2},{2,0},{4,6},{6,4},{8,10},{10,8},{12,14},{14,12},{16,18},{18,... | collective-permute-start | bytes 565256 | tf_op jit(solution)/shard_map/ppermute | solution.py:472
  90.2 10.5 %collective-permute-start.24 = (bf16[32,2944]{1,0:T(8,128)(2,1)S(1)}, bf16[32,2944]{1,0:T(8,128)(2,1)S(1)}, u32[]{:S(2)}, u32[]{:S(2)}) collective-permute-start(bf16[32,2944]{1,0:T(8,128)(2,1)S(1)} %get-tuple-element.73), channel_id=1, source_target_pairs={{0,4},{2,6},{4,0},{6,2},{8,12},{10,14},{12,8},{14,10},{16,20},{18,... | collective-permute-start | bytes 565256 | tf_op jit(solution)/shard_map/ppermute | solution.py:472
  90.6 10.1 %collective-permute-start.25 = (bf16[32,2944]{1,0:T(8,128)(2,1)S(1)}, bf16[32,2944]{1,0:T(8,128)(2,1)S(1)}, u32[]{:S(2)}, u32[]{:S(2)}) collective-permute-start(bf16[32,2944]{1,0:T(8,128)(2,1)S(1)} %get-tuple-element.74), channel_id=1, source_target_pairs={{0,6},{2,4},{4,2},{6,0},{8,14},{10,12},{12,10},{14,8},{16,22},{18,... | collective-permute-start | bytes 565256 | tf_op jit(solution)/shard_map/ppermute | solution.py:472
  (10 other events, 147.6 us)
Sparse Core Ops, SparseCore 0:
  9.6 61.3 all-gather.1

commit v6 on v5

--- a/solution.py
+++ b/solution.py
@@ -132,21 +132,23 @@
 def pack_kernel(depth, *refs):
     line, pieces, out_refs = refs[:depth], refs[depth : depth + PLANE], refs[depth + PLANE :]
     rows, extended = line[0].shape
-    for ref, piece in zip(out_refs, pieces):
+    sub = pieces[0].shape[1]
+    for d, ref in enumerate(out_refs):
         for z in range(depth):
             ref[z * rows : (z + 1) * rows, :extended] = line[z][...]
-        ref[:, extended:] = piece[...]
+        ref[:, extended : extended + sub] = pieces[d][...]
+        ref[:, extended + sub :] = pieces[PLANE - 1][...]
 
 
 def pack(line, pieces):
     depth = len(line)
     rows, extended = line[0].shape
-    shape = pltpu.VMEM((depth * rows, extended + pieces[0].shape[1]), jnp.bfloat16)
+    shape = pltpu.VMEM((depth * rows, extended + 2 * pieces[0].shape[1]), jnp.bfloat16)
     return pl.pallas_call(
         functools.partial(pack_kernel, depth),
-        out_shape=(shape,) * PLANE,
+        out_shape=(shape,) * (PLANE - 1),
         in_specs=[VMEM] * (depth + PLANE),
-        out_specs=(VMEM,) * PLANE,
+        out_specs=(VMEM,) * (PLANE - 1),
         compiler_params=params(2),
         name="pack_tokens",
     )(*line, *pieces)
@@ -180,7 +182,7 @@
 
 def expert_kernel(depth, chunk, count, *refs):
     block_refs, (gate_ref, up_ref, down_ref) = refs[:count], refs[count : count + 3]
-    mine_ref, theirs_ref, x_buf, act_buf = refs[count + 3 :]
+    mine_ref, *theirs_refs, x_buf, act_buf = refs[count + 3 :]
     width, hidden = gate_ref.shape[1:]
     extended = x_buf.shape[1]
     start = 0
@@ -213,20 +215,24 @@
         out = jnp.dot(act_buf[...], weight, preferred_element_type=jnp.float32)
         cols = slice(d * part, (d + 1) * part)
         mine_ref[:, cols] = out[:half].astype(jnp.bfloat16)
-        theirs_ref[:, cols] = out[half:].astype(jnp.bfloat16)
-
-
-def experts(blocks, weights, depth):
+        start = half
+        for ref in theirs_refs:
+            stop = start + ref.shape[0]
+            ref[:, cols] = out[start:stop].astype(jnp.bfloat16)
+            start = stop
+
+
+def experts(blocks, weights, depth, pieces):
     width, hidden = weights[0].shape[1:]
     chunk = 256
     extended = width + META
     total = sum(block.shape[0] for block in blocks)
-    half = pltpu.VMEM((total // 2, width), jnp.bfloat16)
+    rows = [total // 2] + [total // 2 // pieces] * pieces
     return pl.pallas_call(
         functools.partial(expert_kernel, depth, chunk, len(blocks)),
-        out_shape=(half, half),
+        out_shape=tuple(pltpu.VMEM((size, width), jnp.bfloat16) for size in rows),
         in_specs=[VMEM] * (len(blocks) + 3),
-        out_specs=(VMEM, VMEM),
+        out_specs=(VMEM,) * (1 + pieces),
         scratch_shapes=[
             pltpu.VMEM((total, extended), jnp.bfloat16),
             pltpu.VMEM((total, hidden), jnp.bfloat16),
@@ -239,59 +245,65 @@
     )(*blocks, *weights)
 
 
-def chip_sum_kernel(mine_ref, theirs_ref, *out_refs):
+def chip_sum_kernel(count, mine_ref, *refs):
+    theirs, out_refs = refs[:count], refs[count:]
     part = out_refs[0].shape[1]
-    for d, ref in enumerate(out_refs):
-        at = slice(d * part, (d + 1) * part)
-        total = mine_ref[:, at].astype(jnp.float32) + theirs_ref[:, at].astype(jnp.float32)
-        ref[...] = total.astype(jnp.bfloat16)
+    start = 0
+    for theirs_ref in theirs:
+        rows = slice(start, start + theirs_ref.shape[0])
+        start = rows.stop
+        for d, ref in enumerate(out_refs):
+            at = slice(d * part, (d + 1) * part)
+            total = mine_ref[rows, at].astype(jnp.float32) + theirs_ref[:, at].astype(jnp.float32)
+            ref[rows, :] = total.astype(jnp.bfloat16)
 
 
 def chip_sum(mine, theirs):
     rows, width = mine.shape
     return pl.pallas_call(
-        chip_sum_kernel,
+        functools.partial(chip_sum_kernel, len(theirs)),
         out_shape=(pltpu.VMEM((rows, width // PLANE), jnp.bfloat16),) * PLANE,
-        in_specs=[VMEM] * 2,
+        in_specs=[VMEM] * (1 + len(theirs)),
         out_specs=(VMEM,) * PLANE,
         compiler_params=params(2),
         name="chip_sum",
-    )(mine, theirs)
+    )(mine, *theirs)
 
 
 def plane_sum_kernel(depth, *refs):
-    halves, out_refs = (refs[:PLANE], refs[PLANE : 2 * PLANE]), refs[2 * PLANE :]
-    group = halves[0][0].shape[0] // 2
+    near, far, out_refs = refs[:PLANE], refs[PLANE : 2 * PLANE], refs[2 * PLANE :]
+    group = far[0].shape[0]
     rows = group // depth
     for k in range(PLANE):
         for z in range(depth):
             total = 0.0
             for d in range(PLANE):
                 block = k ^ d
-                start = block % 2 * group + z * rows
-                part = halves[block // 2][d][start : start + rows, :]
-                total = total + part.astype(jnp.float32)
+                ref, skip = (far[d], 0) if block == PLANE - 1 else (near[d], block * group)
+                start = skip + z * rows
+                total = total + ref[start : start + rows, :].astype(jnp.float32)
             out_refs[z][k * rows : (k + 1) * rows, :] = total.astype(jnp.bfloat16)
 
 
-def plane_sum(first, second, depth):
-    rows, part = first[0].shape
+def plane_sum(near, far, depth):
+    rows, part = far[0].shape
     return pl.pallas_call(
         functools.partial(plane_sum_kernel, depth),
-        out_shape=(pltpu.VMEM((2 * rows // depth, part), jnp.bfloat16),) * depth,
+        out_shape=(pltpu.VMEM((PLANE * rows // depth, part), jnp.bfloat16),) * depth,
         in_specs=[VMEM] * (2 * PLANE),
         out_specs=(VMEM,) * depth,
         compiler_params=params(4),
         name="plane_sum",
-    )(*first, *second)
+    )(*near, *far)
 
 
 def second_norm_kernel(depth, *refs):
-    parts, packed = refs[:depth], refs[depth : depth + PLANE]
-    gain_ref, scaled_ref, next_ref = refs[depth + PLANE :]
+    parts, packed = refs[:depth], refs[depth : depth + PLANE + 1]
+    gain_ref, scaled_ref, next_ref = refs[depth + PLANE + 1 :]
     rows = packed[0].shape[0] // depth
     part = parts[0].shape[1]
     sub = part // depth
+    skip = packed[0].shape[1] - 2 * sub
     lane = lax.broadcasted_iota(jnp.int32, (rows, META), 1)
     plane = lax.axis_index("expert") % PLANE
     gain = jnp.concatenate(
@@ -302,11 +314,11 @@
         total = parts[0][at, :].astype(jnp.float32)
         for ref in parts[1:]:
             total = total + ref[at, :].astype(jnp.float32)
-        source = packed[d]
-        skip = source.shape[1] - sub
-        first = jnp.concatenate(
-            [source[z * rows : (z + 1) * rows, skip:] for z in range(depth)], axis=1
-        )
+        if d < PLANE - 1:
+            first = packed[d][:, skip : skip + sub]
+        else:
+            first = jnp.concatenate([ref[:, skip + sub :] for ref in packed[d:]], axis=0)
+        first = jnp.concatenate([first[z * rows : (z + 1) * rows] for z in range(depth)], axis=1)
         following = (first.astype(jnp.float32) + total).astype(jnp.bfloat16)
         next_ref[at, :] = following
         wide = following.astype(jnp.float32)
@@ -328,7 +340,7 @@
             jax.ShapeDtypeStruct((rows, part + META), jnp.bfloat16),
             jax.ShapeDtypeStruct((rows, part), jnp.bfloat16),
         ),
-        in_specs=[VMEM] * (depth + PLANE + 1),
+        in_specs=[VMEM] * (depth + PLANE + 2),
         out_specs=(VMEM, VMEM),
         compiler_params=params(4),
         name="second_norm",
@@ -498,14 +510,21 @@
     )
     weights = load((w_gate, w_up, w_down), (tokens,))
     line = to_z([tokens] * depth)
-    packed = to_plane(pack(line, firsts))
-    near, far = packed[:2], packed[2:]
-    sums = []
-    for blocks in (near, far):
-        mine, theirs = experts((*blocks, *map(to_core, blocks)), weights, depth)
-        sums.append(to_plane(chip_sum(mine, to_core(theirs))))
-    parts = plane_sum(*sums, depth)
-    scaled, following = second_norm(to_z(parts), packed, input_gain[None, :])
+    *line, gate, up, down = lax.optimization_barrier((*line, *weights))
+    weights = (gate, up, down)
+    near = to_plane(pack(line, firsts))
+    cut = near[0].shape[0] // 2
+    one, two = near[1][:cut], near[2][cut:]
+    far = [to_expert(one, 2), to_expert(two, 1)]
+    mine, *theirs = experts((*near, *map(to_core, near)), weights, depth, len(near))
+    near_sum = chip_sum(mine, list(map(to_core, theirs)))
+    far_both = [*far, *map(to_core, far)]
+    tied = lax.optimization_barrier((*near_sum, *far_both))
+    near_sum, far_both = tied[:PLANE], tied[PLANE:]
+    mine, *theirs = experts(far_both, weights, depth, 1)
+    far_sum = chip_sum(mine, list(map(to_core, theirs)))
+    parts = plane_sum(to_plane(near_sum), to_plane(far_sum), depth)
+    scaled, following = second_norm(to_z(parts), (*near, *far), input_gain[None, :])
     products = to_plane(projection(scaled, to_core(scaled), following, qkv))
     return head_norm(
         products,

time: 109 us -> 103 us (0.945)
  waiting for transfers between devices: 41.6 us -> 34.8 us
  starting transfers between devices: 31.8 us -> 33.1 us
    ppermute x18 -> x19, waiting for transfers between devices: 39.8 us -> 31.8 us  [to_expert(): lax.ppermute(value, 'expert', [(i, i ^ offset) for i in range(n_expert)])]
    ppermute x8 -> x11, waiting for transfers between devices: 1.76 us -> 2.95 us  [to_core(): return lax.ppermute(value, 'tensor', [(0, 1), (1, 0)])]
    ppermute x18 -> x19, starting transfers between devices: 30 us -> 31.1 us  [to_expert(): lax.ppermute(value, 'expert', [(i, i ^ offset) for i in range(n_expert)])]
  transfers between devices with their start and end apart: 27 -> 31, of which waited for: 13 -> 16; matrix products, arithmetic and copies ran while one was open for 0% -> 0% of each run, Pallas kernels for 14% -> 15%
where the time goes in v6:
time: 103 us
  waiting for transfers between devices  34.8 us (34%)
  starting transfers between devices  33.1 us (32%)
  Pallas kernels  18.5 us (18%)
  between operations  14.2 us (14%)
  other arithmetic  2.21 us (2%)
    ppermute x19, waiting for transfers between devices, to_expert(): lax.ppermute(value, 'expert', [(i, i ^ offset) for i in range(n_expert)])  31.8 us
    ppermute x19, starting transfers between devices, to_expert(): lax.ppermute(value, 'expert', [(i, i ^ offset) for i in range(n_expert)])  31.1 us
    pallas_call x2, Pallas kernels, experts(): pl.pallas_call(functools.partial(expert_kernel, depth, chunk, len(blocks)...  6.05 us
    pallas_call x1, Pallas kernels, out_projection(): pl.pallas_call(functools.partial(out_projection_kernel, chunk), out_shape...  4.8 us
    pallas_call x1, Pallas kernels, load(): pl.pallas_call(load_kernel, out_shape=tuple((pltpu.VMEM(w.shape, w.dtype)...  3.78 us
    ppermute x11, waiting for transfers between devices, to_core(): return lax.ppermute(value, 'tensor', [(0, 1), (1, 0)])  2.95 us
    pallas_call x1, Pallas kernels, projection(): pl.pallas_call(functools.partial(projection_kernel, chunk), out_shape=(sh...  2.22 us
  transfers between devices with their start and end apart: 31, of which 16 were waited for; matrix products, arithmetic and copies ran while one was open for 0% of the time, Pallas kernels for 15%

profile of v6, /device:TPU:0, one launch (start us, length us, event | category | flops | bytes accessed | tf_op | source)
XLA Modules:
  0.0 103.1 jit_solution(4856237790314502069)
XLA Ops:
  7.2 2.0 %pad_maximum_fusion = bf16[128,2560]{1,0:T(8,128)(2,1)} fusion(bf16[128,512]{1,0:T(8,128)(2,1)} %param.25, bf16[128,2048]{1,0:T(8,128)(2,1)} %param.24), kind=kLoop, calls=%fused_computation | loop fusion | flops 1310720 | bytes 1310720 | tf_op jit(solution)/shard_map/concatenate | solution.py:501
  9.3 4.8 %out_projection.1 = (f32[16,2048]{1,0:T(8,128)S(1)}, f32[16,2048]{1,0:T(8,128)S(1)}) custom-call(bf16[32,2048]{1,0:T(8,128)(2,1)} %a_hbm.1, bf16[2048,2048]{1,0:T(8,128)(2,1)} %w_hbm.1), custom_call_target="tpu_custom_call" | custom-call | tf_op jit(solution)/shard_map/out_projection/pallas_call | solution.py:77
  15.8 3.0 %collective-permute-start.1 = (bf16[16,2176]{1,0:T(8,128)(2,1)S(1)}, bf16[16,2176]{1,0:T(8,128)(2,1)S(1)}, u32[]{:S(2)}, u32[]{:S(2)}) collective-permute-start(bf16[16,2176]{1,0:T(8,128)(2,1)S(1)} %get-tuple-element.61.refs_3_.refs_0_), channel_id=1, source_target_pairs={{0,8},{2,10},{4,12},{6,14},{8,0},{10,2},{12,4},{14,6},{16,24},{18,... | collective-permute-start | bytes 208904 | tf_op jit(solution)/shard_map/ppermute | solution.py:484
  18.8 2.6 %collective-permute-start.2 = (bf16[16,2176]{1,0:T(8,128)(2,1)S(1)}, bf16[16,2176]{1,0:T(8,128)(2,1)S(1)}, u32[]{:S(2)}, u32[]{:S(2)}) collective-permute-start(bf16[16,2176]{1,0:T(8,128)(2,1)S(1)} %get-tuple-element.61.refs_3_.refs_0_), channel_id=1, source_target_pairs={{0,16},{2,18},{4,20},{6,22},{8,24},{10,26},{12,28},{14,30},{16,0},... | collective-permute-start | bytes 208904 | tf_op jit(solution)/shard_map/ppermute | solution.py:484
  21.3 3.8 %load_weights.1 = (bf16[1,2048,768]{2,1,0:T(8,128)(2,1)S(1)}, bf16[1,2048,768]{2,1,0:T(8,128)(2,1)S(1)}, bf16[1,768,2048]{2,1,0:T(8,128)(2,1)S(1)}) custom-call(bf16[1,2048,768]{2,1,0:T(8,128)(2,1)} %refs_0_.1, bf16[1,2048,768]{2,1,0:T(8,128)(2,1)} %refs_1_.1, bf16[1,768,2048]{2,1,0:T(8,128)(2,1)} %refs_2_.3, ...), custom_call_target="tpu_custom_call" | custom-call | tf_op jit(solution)/shard_map/load_weights/pallas_call | solution.py:171
  25.1 4.8 %collective-permute-done.2.refs_2_ = bf16[16,2176]{1,0:T(8,128)(2,1)S(1)} collective-permute-done((bf16[16,2176]{1,0:T(8,128)(2,1)S(1)}, bf16[16,2176]{1,0:T(8,128)(2,1)S(1)}, u32[]{:S(2)}, u32[]{:S(2)}) %collective-permute-start.2) | collective-permute-done | bytes 69664 | tf_op jit(solution)/shard_map/ppermute | solution.py:484
  30.1 1.6 %collective-permute-start.4 = (bf16[64,2432]{1,0:T(8,128)(2,1)S(1)}, bf16[64,2432]{1,0:T(8,128)(2,1)S(1)}, u32[]{:S(2)}, u32[]{:S(2)}) collective-permute-start(bf16[64,2432]{1,0:T(8,128)(2,1)S(1)} %get-tuple-element.70), channel_id=1, source_target_pairs={{0,2},{2,0},{4,6},{6,4},{8,10},{10,8},{12,14},{14,12},{16,18},{18,... | collective-permute-start | bytes 933896 | tf_op jit(solution)/shard_map/ppermute | solution.py:484
  31.6 1.5 %collective-permute-start.5 = (bf16[64,2432]{1,0:T(8,128)(2,1)S(1)}, bf16[64,2432]{1,0:T(8,128)(2,1)S(1)}, u32[]{:S(2)}, u32[]{:S(2)}) collective-permute-start(bf16[64,2432]{1,0:T(8,128)(2,1)S(1)} %get-tuple-element.71), channel_id=1, source_target_pairs={{0,4},{2,6},{4,0},{6,2},{8,12},{10,14},{12,8},{14,10},{16,20},{18,... | collective-permute-start | bytes 933896 | tf_op jit(solution)/shard_map/ppermute | solution.py:484
  33.2 3.8 %collective-permute-done.4.refs_1_.refs_5_ = bf16[64,2432]{1,0:T(8,128)(2,1)S(1)} collective-permute-done((bf16[64,2432]{1,0:T(8,128)(2,1)S(1)}, bf16[64,2432]{1,0:T(8,128)(2,1)S(1)}, u32[]{:S(2)}, u32[]{:S(2)}) %collective-permute-start.4) | collective-permute-done | bytes 311328 | tf_op jit(solution)/shard_map/ppermute | solution.py:484
  37.0 1.5 %collective-permute-done.5.refs_2_.refs_6_ = bf16[64,2432]{1,0:T(8,128)(2,1)S(1)} collective-permute-done((bf16[64,2432]{1,0:T(8,128)(2,1)S(1)}, bf16[64,2432]{1,0:T(8,128)(2,1)S(1)}, u32[]{:S(2)}, u32[]{:S(2)}) %collective-permute-start.5) | collective-permute-done | bytes 311328 | tf_op jit(solution)/shard_map/ppermute | solution.py:484
  38.5 1.6 %collective-permute-start.12 = (bf16[32,2432]{1,0:T(8,128)(2,1)S(1)}, bf16[32,2432]{1,0:T(8,128)(2,1)S(1)}, u32[]{:S(2)}, u32[]{:S(2)}) collective-permute-start(bf16[32,2432]{1,0:T(8,128)(2,1)S(1)} %slice.8), channel_id=1, source_target_pairs={{0,4},{2,6},{4,0},{6,2},{8,12},{10,14},{12,8},{14,10},{16,20},{18,... | collective-permute-start | bytes 466952 | tf_op jit(solution)/shard_map/ppermute | solution.py:484
  40.8 4.1 %experts.2 = (bf16[192,2048]{1,0:T(8,128)(2,1)S(1)}, bf16[64,2048]{1,0:T(8,128)(2,1)S(1)}, bf16[64,2048]{1,0:T(8,128)(2,1)S(1)}, bf16[64,2048]{1,0:T(8,128)(2,1)S(1)}) custom-call(bf16[64,2432]{1,0:T(8,128)(2,1)S(1)} %get-tuple-element.69.refs_0_.refs_4_, bf16[64,2432]{1,0:T(8,128)(2,1)S(1)} %collective-permute-done.4.refs_1_.refs_5_, ...), custom_call_target="tpu_custom_call" | custom-call | flops 3623878656 | tf_op jit(solution)/shard_map/experts/pallas_call | solution.py:231
  47.8 2.0 %experts.3 = (bf16[64,2048]{1,0:T(8,128)(2,1)S(1)}, bf16[64,2048]{1,0:T(8,128)(2,1)S(1)}) custom-call(bf16[32,2432]{1,0:T(8,128)(2,1)S(1)} %collective-permute-done.12.refs_0_.refs_7_, bf16[32,2432]{1,0:T(8,128)(2,1)S(1)} %collective-permute-done.13.refs_1_.refs_8_, bf16[32,2432]{1,0:T(8,128)(2,1)S(1)} %collective-permute-done.14.refs_2_, ...), custom_call_target="tpu_custom_call" | custom-call | flops 1207959552 | tf_op jit(solution)/shard_map/experts/pallas_call | solution.py:231
  51.9 1.6 %collective-permute-start.18 = (bf16[192,512]{1,0:T(8,128)(2,1)S(1)}, bf16[192,512]{1,0:T(8,128)(2,1)S(1)}, u32[]{:S(2)}, u32[]{:S(2)}) collective-permute-start(bf16[192,512]{1,0:T(8,128)(2,1)S(1)} %get-tuple-element.86), channel_id=1, source_target_pairs={{0,6},{2,4},{4,2},{6,0},{8,14},{10,12},{12,10},{14,8},{16,22},{18,... | collective-permute-start | bytes 589832 | tf_op jit(solution)/shard_map/ppermute | solution.py:484
  53.6 1.4 %collective-permute-start.20 = (bf16[64,512]{1,0:T(8,128)(2,1)S(1)}, bf16[64,512]{1,0:T(8,128)(2,1)S(1)}, u32[]{:S(2)}, u32[]{:S(2)}) collective-permute-start(bf16[64,512]{1,0:T(8,128)(2,1)S(1)} %get-tuple-element.94), channel_id=1, source_target_pairs={{0,2},{2,0},{4,6},{6,4},{8,10},{10,8},{12,14},{14,12},{16,18},{18,... | collective-permute-start | bytes 196616 | tf_op jit(solution)/shard_map/ppermute | solution.py:484
  55.5 2.2 %collective-permute-done.16.refs_1_ = bf16[192,512]{1,0:T(8,128)(2,1)S(1)} collective-permute-done((bf16[192,512]{1,0:T(8,128)(2,1)S(1)}, bf16[192,512]{1,0:T(8,128)(2,1)S(1)}, u32[]{:S(2)}, u32[]{:S(2)}) %collective-permute-start.16) | collective-permute-done | bytes 196640 | tf_op jit(solution)/shard_map/ppermute | solution.py:484
  59.0 5.5 %collective-permute-done.17.refs_2_ = bf16[192,512]{1,0:T(8,128)(2,1)S(1)} collective-permute-done((bf16[192,512]{1,0:T(8,128)(2,1)S(1)}, bf16[192,512]{1,0:T(8,128)(2,1)S(1)}, u32[]{:S(2)}, u32[]{:S(2)}) %collective-permute-start.17) | collective-permute-done | bytes 196640 | tf_op jit(solution)/shard_map/ppermute | solution.py:484
  65.4 6.5 %collective-permute-start.23 = (bf16[64,512]{1,0:T(8,128)(2,1)S(1)}, bf16[64,512]{1,0:T(8,128)(2,1)S(1)}, u32[]{:S(2)}, u32[]{:S(2)}) collective-permute-start(bf16[64,512]{1,0:T(8,128)(2,1)S(1)} %get-tuple-element.98), channel_id=1, source_target_pairs={{0,8},{2,10},{4,12},{6,14},{8,0},{10,2},{12,4},{14,6},{16,24},{18,... | collective-permute-start | bytes 196616 | tf_op jit(solution)/shard_map/ppermute | solution.py:484
  71.9 2.1 %collective-permute-start.24 = (bf16[64,512]{1,0:T(8,128)(2,1)S(1)}, bf16[64,512]{1,0:T(8,128)(2,1)S(1)}, u32[]{:S(2)}, u32[]{:S(2)}) collective-permute-start(bf16[64,512]{1,0:T(8,128)(2,1)S(1)} %get-tuple-element.99), channel_id=1, source_target_pairs={{0,16},{2,18},{4,20},{6,22},{8,24},{10,26},{12,28},{14,30},{16,0},... | collective-permute-start | bytes 196616 | tf_op jit(solution)/shard_map/ppermute | solution.py:484
  75.4 5.0 %collective-permute-done.24.refs_2_ = bf16[64,512]{1,0:T(8,128)(2,1)S(1)} collective-permute-done((bf16[64,512]{1,0:T(8,128)(2,1)S(1)}, bf16[64,512]{1,0:T(8,128)(2,1)S(1)}, u32[]{:S(2)}, u32[]{:S(2)}) %collective-permute-start.24) | collective-permute-done | bytes 65568 | tf_op jit(solution)/shard_map/ppermute | solution.py:484
  81.8 2.2 %qkv_projection.1 = (bf16[32,2944]{1,0:T(8,128)(2,1)S(1)}, bf16[32,2944]{1,0:T(8,128)(2,1)S(1)}, bf16[32,2944]{1,0:T(8,128)(2,1)S(1)}, bf16[32,2944]{1,0:T(8,128)(2,1)S(1)}) custom-call(bf16[64,640]{1,0:T(8,128)(2,1)S(1)} %get-tuple-element.101.mine_ref, bf16[64,640]{1,0:T(8,128)(2,1)S(1)} %collective-permute-done.26.theirs_ref, ...), custom_call_target="tpu_custom_call" | custom-call | tf_op jit(solution)/shard_map/qkv_projection/pallas_call | solution.py:389
  86.2 1.5 %collective-permute-start.29 = (bf16[32,2944]{1,0:T(8,128)(2,1)S(1)}, bf16[32,2944]{1,0:T(8,128)(2,1)S(1)}, u32[]{:S(2)}, u32[]{:S(2)}) collective-permute-start(bf16[32,2944]{1,0:T(8,128)(2,1)S(1)} %get-tuple-element.106), channel_id=1, source_target_pairs={{0,6},{2,4},{4,2},{6,0},{8,14},{10,12},{12,10},{14,8},{16,22},{18,... | collective-permute-start | bytes 565256 | tf_op jit(solution)/shard_map/ppermute | solution.py:484
  87.6 4.1 %collective-permute-done.27.refs_1_ = bf16[32,2944]{1,0:T(8,128)(2,1)S(1)} collective-permute-done((bf16[32,2944]{1,0:T(8,128)(2,1)S(1)}, bf16[32,2944]{1,0:T(8,128)(2,1)S(1)}, u32[]{:S(2)}, u32[]{:S(2)}) %collective-permute-start.27) | collective-permute-done | bytes 188448 | tf_op jit(solution)/shard_map/ppermute | solution.py:484
  91.7 3.7 %collective-permute-done.28.refs_2_ = bf16[32,2944]{1,0:T(8,128)(2,1)S(1)} collective-permute-done((bf16[32,2944]{1,0:T(8,128)(2,1)S(1)}, bf16[32,2944]{1,0:T(8,128)(2,1)S(1)}, u32[]{:S(2)}, u32[]{:S(2)}) %collective-permute-start.28) | collective-permute-done | bytes 188448 | tf_op jit(solution)/shard_map/ppermute | solution.py:484
  (75 shorter events, 16.0 us)
Async XLA Ops:
  7.2 74.7 %all-gather.2.cloned.1.call-start = ((), (), s32[]{:S(2)}) async-start(), calls=%async_computation | async-start | bytes 3276800 | tf_op jit(solution)/shard_map/all_gather | solution.py:500
  15.8 9.4 %collective-permute-start.1 = (bf16[16,2176]{1,0:T(8,128)(2,1)S(1)}, bf16[16,2176]{1,0:T(8,128)(2,1)S(1)}, u32[]{:S(2)}, u32[]{:S(2)}) collective-permute-start(bf16[16,2176]{1,0:T(8,128)(2,1)S(1)} %get-tuple-element.61.refs_3_.refs_0_), channel_id=1, source_target_pairs={{0,8},{2,10},{4,12},{6,14},{8,0},{10,2},{12,4},{14,6},{16,24},{18,... | collective-permute-start | bytes 208904 | tf_op jit(solution)/shard_map/ppermute | solution.py:484
  18.8 11.2 %collective-permute-start.2 = (bf16[16,2176]{1,0:T(8,128)(2,1)S(1)}, bf16[16,2176]{1,0:T(8,128)(2,1)S(1)}, u32[]{:S(2)}, u32[]{:S(2)}) collective-permute-start(bf16[16,2176]{1,0:T(8,128)(2,1)S(1)} %get-tuple-element.61.refs_3_.refs_0_), channel_id=1, source_target_pairs={{0,16},{2,18},{4,20},{6,22},{8,24},{10,26},{12,28},{14,30},{16,0},... | collective-permute-start | bytes 208904 | tf_op jit(solution)/shard_map/ppermute | solution.py:484
  21.3 8.6 %collective-permute-start.3 = (bf16[16,2176]{1,0:T(8,128)(2,1)S(1)}, bf16[16,2176]{1,0:T(8,128)(2,1)S(1)}, u32[]{:S(2)}, u32[]{:S(2)}) collective-permute-start(bf16[16,2176]{1,0:T(8,128)(2,1)S(1)} %get-tuple-element.61.refs_3_.refs_0_), channel_id=1, source_target_pairs={{0,24},{2,26},{4,28},{6,30},{8,16},{10,18},{12,20},{14,22},{16,8},... | collective-permute-start | bytes 208904 | tf_op jit(solution)/shard_map/ppermute | solution.py:484
  30.1 7.0 %collective-permute-start.4 = (bf16[64,2432]{1,0:T(8,128)(2,1)S(1)}, bf16[64,2432]{1,0:T(8,128)(2,1)S(1)}, u32[]{:S(2)}, u32[]{:S(2)}) collective-permute-start(bf16[64,2432]{1,0:T(8,128)(2,1)S(1)} %get-tuple-element.70), channel_id=1, source_target_pairs={{0,2},{2,0},{4,6},{6,4},{8,10},{10,8},{12,14},{14,12},{16,18},{18,... | collective-permute-start | bytes 933896 | tf_op jit(solution)/shard_map/ppermute | solution.py:484
  31.6 6.9 %collective-permute-start.5 = (bf16[64,2432]{1,0:T(8,128)(2,1)S(1)}, bf16[64,2432]{1,0:T(8,128)(2,1)S(1)}, u32[]{:S(2)}, u32[]{:S(2)}) collective-permute-start(bf16[64,2432]{1,0:T(8,128)(2,1)S(1)} %get-tuple-element.71), channel_id=1, source_target_pairs={{0,4},{2,6},{4,0},{6,2},{8,12},{10,14},{12,8},{14,10},{16,20},{18,... | collective-permute-start | bytes 933896 | tf_op jit(solution)/shard_map/ppermute | solution.py:484
  33.2 7.6 %collective-permute-start.6 = (bf16[64,2432]{1,0:T(8,128)(2,1)S(1)}, bf16[64,2432]{1,0:T(8,128)(2,1)S(1)}, u32[]{:S(2)}, u32[]{:S(2)}) collective-permute-start(bf16[64,2432]{1,0:T(8,128)(2,1)S(1)} %get-tuple-element.69.refs_0_.refs_4_), channel_id=1, source_target_pairs={{0,1},{1,0},{2,3},{3,2},{4,5},{5,4},{6,7},{7,6},{8,9},{9,8},{10,11... | collective-permute-start | bytes 933896 | tf_op jit(solution)/shard_map/ppermute | solution.py:481
  37.0 3.8 %collective-permute-start.7 = (bf16[64,2432]{1,0:T(8,128)(2,1)S(1)}, bf16[64,2432]{1,0:T(8,128)(2,1)S(1)}, u32[]{:S(2)}, u32[]{:S(2)}) collective-permute-start(bf16[64,2432]{1,0:T(8,128)(2,1)S(1)} %collective-permute-done.4.refs_1_.refs_5_), channel_id=1, source_target_pairs={{0,1},{1,0},{2,3},{3,2},{4,5},{5,4},{6,7},{7,6},{8,9},{9,8},{10,11... | collective-permute-start | bytes 933896 | tf_op jit(solution)/shard_map/ppermute | solution.py:481
  38.5 2.3 %collective-permute-start.8 = (bf16[64,2432]{1,0:T(8,128)(2,1)S(1)}, bf16[64,2432]{1,0:T(8,128)(2,1)S(1)}, u32[]{:S(2)}, u32[]{:S(2)}) collective-permute-start(bf16[64,2432]{1,0:T(8,128)(2,1)S(1)} %collective-permute-done.5.refs_2_.refs_6_), channel_id=1, source_target_pairs={{0,1},{1,0},{2,3},{3,2},{4,5},{5,4},{6,7},{7,6},{8,9},{9,8},{10,11... | collective-permute-start | bytes 933896 | tf_op jit(solution)/shard_map/ppermute | solution.py:481
  38.5 7.0 %collective-permute-start.12 = (bf16[32,2432]{1,0:T(8,128)(2,1)S(1)}, bf16[32,2432]{1,0:T(8,128)(2,1)S(1)}, u32[]{:S(2)}, u32[]{:S(2)}) collective-permute-start(bf16[32,2432]{1,0:T(8,128)(2,1)S(1)} %slice.8), channel_id=1, source_target_pairs={{0,4},{2,6},{4,0},{6,2},{8,12},{10,14},{12,8},{14,10},{16,20},{18,... | collective-permute-start | bytes 466952 | tf_op jit(solution)/shard_map/ppermute | solution.py:484
  40.2 6.2 %collective-permute-start.13 = (bf16[32,2432]{1,0:T(8,128)(2,1)S(1)}, bf16[32,2432]{1,0:T(8,128)(2,1)S(1)}, u32[]{:S(2)}, u32[]{:S(2)}) collective-permute-start(bf16[32,2432]{1,0:T(8,128)(2,1)S(1)} %slice.9), channel_id=1, source_target_pairs={{0,2},{2,0},{4,6},{6,4},{8,10},{10,8},{12,14},{14,12},{16,18},{18,... | collective-permute-start | bytes 466952 | tf_op jit(solution)/shard_map/ppermute | solution.py:484
  49.8 3.7 %collective-permute-start.19 = (bf16[64,2048]{1,0:T(8,128)(2,1)S(1)}, bf16[64,2048]{1,0:T(8,128)(2,1)S(1)}, u32[]{:S(2)}, u32[]{:S(2)}) collective-permute-start(bf16[64,2048]{1,0:T(8,128)(2,1)S(1)} %get-tuple-element.92), channel_id=1, source_target_pairs={{0,1},{1,0},{2,3},{3,2},{4,5},{5,4},{6,7},{7,6},{8,9},{9,8},{10,11... | collective-permute-start | bytes 786440 | tf_op jit(solution)/shard_map/ppermute | solution.py:481
  50.0 7.7 %collective-permute-start.16 = (bf16[192,512]{1,0:T(8,128)(2,1)S(1)}, bf16[192,512]{1,0:T(8,128)(2,1)S(1)}, u32[]{:S(2)}, u32[]{:S(2)}) collective-permute-start(bf16[192,512]{1,0:T(8,128)(2,1)S(1)} %get-tuple-element.84), channel_id=1, source_target_pairs={{0,2},{2,0},{4,6},{6,4},{8,10},{10,8},{12,14},{14,12},{16,18},{18,... | collective-permute-start | bytes 589832 | tf_op jit(solution)/shard_map/ppermute | solution.py:484
  51.4 13.2 %collective-permute-start.17 = (bf16[192,512]{1,0:T(8,128)(2,1)S(1)}, bf16[192,512]{1,0:T(8,128)(2,1)S(1)}, u32[]{:S(2)}, u32[]{:S(2)}) collective-permute-start(bf16[192,512]{1,0:T(8,128)(2,1)S(1)} %get-tuple-element.85), channel_id=1, source_target_pairs={{0,4},{2,6},{4,0},{6,2},{8,12},{10,14},{12,8},{14,10},{16,20},{18,... | collective-permute-start | bytes 589832 | tf_op jit(solution)/shard_map/ppermute | solution.py:484
  51.9 12.7 %collective-permute-start.18 = (bf16[192,512]{1,0:T(8,128)(2,1)S(1)}, bf16[192,512]{1,0:T(8,128)(2,1)S(1)}, u32[]{:S(2)}, u32[]{:S(2)}) collective-permute-start(bf16[192,512]{1,0:T(8,128)(2,1)S(1)} %get-tuple-element.86), channel_id=1, source_target_pairs={{0,6},{2,4},{4,2},{6,0},{8,14},{10,12},{12,10},{14,8},{16,22},{18,... | collective-permute-start | bytes 589832 | tf_op jit(solution)/shard_map/ppermute | solution.py:484
  53.6 11.0 %collective-permute-start.20 = (bf16[64,512]{1,0:T(8,128)(2,1)S(1)}, bf16[64,512]{1,0:T(8,128)(2,1)S(1)}, u32[]{:S(2)}, u32[]{:S(2)}) collective-permute-start(bf16[64,512]{1,0:T(8,128)(2,1)S(1)} %get-tuple-element.94), channel_id=1, source_target_pairs={{0,2},{2,0},{4,6},{6,4},{8,10},{10,8},{12,14},{14,12},{16,18},{18,... | collective-permute-start | bytes 196616 | tf_op jit(solution)/shard_map/ppermute | solution.py:484
  55.0 10.3 %collective-permute-start.21 = (bf16[64,512]{1,0:T(8,128)(2,1)S(1)}, bf16[64,512]{1,0:T(8,128)(2,1)S(1)}, u32[]{:S(2)}, u32[]{:S(2)}) collective-permute-start(bf16[64,512]{1,0:T(8,128)(2,1)S(1)} %get-tuple-element.95), channel_id=1, source_target_pairs={{0,4},{2,6},{4,0},{6,2},{8,12},{10,14},{12,8},{14,10},{16,20},{18,... | collective-permute-start | bytes 196616 | tf_op jit(solution)/shard_map/ppermute | solution.py:484
  57.7 7.5 %collective-permute-start.22 = (bf16[64,512]{1,0:T(8,128)(2,1)S(1)}, bf16[64,512]{1,0:T(8,128)(2,1)S(1)}, u32[]{:S(2)}, u32[]{:S(2)}) collective-permute-start(bf16[64,512]{1,0:T(8,128)(2,1)S(1)} %get-tuple-element.96), channel_id=1, source_target_pairs={{0,6},{2,4},{4,2},{6,0},{8,14},{10,12},{12,10},{14,8},{16,22},{18,... | collective-permute-start | bytes 196616 | tf_op jit(solution)/shard_map/ppermute | solution.py:484
  65.4 10.0 %collective-permute-start.23 = (bf16[64,512]{1,0:T(8,128)(2,1)S(1)}, bf16[64,512]{1,0:T(8,128)(2,1)S(1)}, u32[]{:S(2)}, u32[]{:S(2)}) collective-permute-start(bf16[64,512]{1,0:T(8,128)(2,1)S(1)} %get-tuple-element.98), channel_id=1, source_target_pairs={{0,8},{2,10},{4,12},{6,14},{8,0},{10,2},{12,4},{14,6},{16,24},{18,... | collective-permute-start | bytes 196616 | tf_op jit(solution)/shard_map/ppermute | solution.py:484
  71.9 8.5 %collective-permute-start.24 = (bf16[64,512]{1,0:T(8,128)(2,1)S(1)}, bf16[64,512]{1,0:T(8,128)(2,1)S(1)}, u32[]{:S(2)}, u32[]{:S(2)}) collective-permute-start(bf16[64,512]{1,0:T(8,128)(2,1)S(1)} %get-tuple-element.99), channel_id=1, source_target_pairs={{0,16},{2,18},{4,20},{6,22},{8,24},{10,26},{12,28},{14,30},{16,0},... | collective-permute-start | bytes 196616 | tf_op jit(solution)/shard_map/ppermute | solution.py:484
  74.0 6.4 %collective-permute-start.25 = (bf16[64,512]{1,0:T(8,128)(2,1)S(1)}, bf16[64,512]{1,0:T(8,128)(2,1)S(1)}, u32[]{:S(2)}, u32[]{:S(2)}) collective-permute-start(bf16[64,512]{1,0:T(8,128)(2,1)S(1)} %get-tuple-element.100), channel_id=1, source_target_pairs={{0,24},{2,26},{4,28},{6,30},{8,16},{10,18},{12,20},{14,22},{16,8},... | collective-permute-start | bytes 196616 | tf_op jit(solution)/shard_map/ppermute | solution.py:484
  84.1 7.6 %collective-permute-start.27 = (bf16[32,2944]{1,0:T(8,128)(2,1)S(1)}, bf16[32,2944]{1,0:T(8,128)(2,1)S(1)}, u32[]{:S(2)}, u32[]{:S(2)}) collective-permute-start(bf16[32,2944]{1,0:T(8,128)(2,1)S(1)} %get-tuple-element.104), channel_id=1, source_target_pairs={{0,2},{2,0},{4,6},{6,4},{8,10},{10,8},{12,14},{14,12},{16,18},{18,... | collective-permute-start | bytes 565256 | tf_op jit(solution)/shard_map/ppermute | solution.py:484
  84.8 10.5 %collective-permute-start.28 = (bf16[32,2944]{1,0:T(8,128)(2,1)S(1)}, bf16[32,2944]{1,0:T(8,128)(2,1)S(1)}, u32[]{:S(2)}, u32[]{:S(2)}) collective-permute-start(bf16[32,2944]{1,0:T(8,128)(2,1)S(1)} %get-tuple-element.105), channel_id=1, source_target_pairs={{0,4},{2,6},{4,0},{6,2},{8,12},{10,14},{12,8},{14,10},{16,20},{18,... | collective-permute-start | bytes 565256 | tf_op jit(solution)/shard_map/ppermute | solution.py:484
  86.2 9.2 %collective-permute-start.29 = (bf16[32,2944]{1,0:T(8,128)(2,1)S(1)}, bf16[32,2944]{1,0:T(8,128)(2,1)S(1)}, u32[]{:S(2)}, u32[]{:S(2)}) collective-permute-start(bf16[32,2944]{1,0:T(8,128)(2,1)S(1)} %get-tuple-element.106), channel_id=1, source_target_pairs={{0,6},{2,4},{4,2},{6,0},{8,14},{10,12},{12,10},{14,8},{16,22},{18,... | collective-permute-start | bytes 565256 | tf_op jit(solution)/shard_map/ppermute | solution.py:484
  (14 other events, 160.8 us)
Sparse Core Ops, SparseCore 0:
  9.6 61.3 all-gather.1

commit v7 on v6

--- a/solution.py
+++ b/solution.py
@@ -497,20 +497,15 @@
     meta = jnp.concatenate([high, dense - high], axis=1).astype(jnp.bfloat16)
 
     lines = [list(range(i, n_expert, PLANE)) for i in range(PLANE)]
-    qkv = lax.all_gather(
-        jnp.concatenate([q_weight, kv_weight], axis=1),
-        "expert",
-        axis=0,
-        tiled=True,
-        axis_index_groups=lines,
-    )
+    joined = jnp.concatenate([q_weight, kv_weight], axis=1)
     mine, theirs = out_projection(attn_out, out_weight)
     tokens, *firsts = first_norm(
         (mine,), (to_core(theirs),), residual, attn_gain[None, :], meta, depth
     )
-    weights = load((w_gate, w_up, w_down), (tokens,))
+    weights = load((w_gate, w_up, w_down), (tokens, joined))
     line = to_z([tokens] * depth)
-    *line, gate, up, down = lax.optimization_barrier((*line, *weights))
+    *line, joined, gate, up, down = lax.optimization_barrier((*line, joined, *weights))
+    qkv = lax.all_gather(joined, "expert", axis=0, tiled=True, axis_index_groups=lines)
     weights = (gate, up, down)
     near = to_plane(pack(line, firsts))
     cut = near[0].shape[0] // 2

time: 103 us -> 112 us (1.087)
  local copies, waits for them, and re-layouts: 0.36 us -> 11.1 us
  starting transfers between devices: 33.1 us -> 27.9 us
  waiting for transfers between devices: 34.8 us -> 40 us
  other arithmetic: 2.21 us -> 0.19 us
    unnamed x14 -> x39, local copies, waits for them, and re-layouts: 0.04 us -> 10.8 us
    ppermute x19, starting transfers between devices: 31.1 us -> 25.9 us  [to_expert(): lax.ppermute(value, 'expert', [(i, i ^ offset) for i in range(n_expert)])]
    all_gather x1, waiting for transfers between devices: 0.01 us -> 4.53 us  [per_device_dense(): lax.all_gather(joined, 'expert', axis=0, tiled=True, axis_index_groups=li...]
    concatenate x1 -> x0, other arithmetic: 2.01 us -> none  [per_device_dense(): jnp.concatenate([q_weight, kv_weight], axis=1)]
  transfers between devices with their start and end apart: 31 -> 31, of which waited for: 16 -> 16; matrix products, arithmetic and copies ran while one was open for 0% -> 0% of each run, Pallas kernels for 15% -> 9%
where the time goes in v7:
time: 112 us
  waiting for transfers between devices  40 us (36%)
  starting transfers between devices  27.9 us (25%)
  Pallas kernels  18.7 us (17%)
  between operations  14.3 us (13%)
  local copies, waits for them, and re-layouts  11.1 us (10%)
    ppermute x19, waiting for transfers between devices, to_expert(): lax.ppermute(value, 'expert', [(i, i ^ offset) for i in range(n_expert)])  32.3 us
    ppermute x19, starting transfers between devices, to_expert(): lax.ppermute(value, 'expert', [(i, i ^ offset) for i in range(n_expert)])  25.9 us
    unnamed x39, local copies, waits for them, and re-layouts  10.8 us
    pallas_call x2, Pallas kernels, experts(): pl.pallas_call(functools.partial(expert_kernel, depth, chunk, len(blocks)...  6.04 us
    pallas_call x1, Pallas kernels, out_projection(): pl.pallas_call(functools.partial(out_projection_kernel, chunk), out_shape...  4.83 us
    all_gather x1, waiting for transfers between devices, per_device_dense(): lax.all_gather(joined, 'expert', axis=0, tiled=True, axis_index_groups=li...  4.53 us
    pallas_call x1, Pallas kernels, load(): pl.pallas_call(load_kernel, out_shape=tuple((pltpu.VMEM(w.shape, w.dtype)...  4.01 us
    ppermute x11, waiting for transfers between devices, to_core(): return lax.ppermute(value, 'tensor', [(0, 1), (1, 0)])  3.15 us
  transfers between devices with their start and end apart: 31, of which 16 were waited for; matrix products, arithmetic and copies ran while one was open for 0% of the time, Pallas kernels for 9%

profile of v7, /device:TPU:0, one launch (start us, length us, event | category | flops | bytes accessed | tf_op | source)
XLA Modules:
  0.0 112.2 jit_solution(8408184883228127228)
XLA Ops:
  7.3 4.8 %out_projection.1 = (f32[16,2048]{1,0:T(8,128)S(1)}, f32[16,2048]{1,0:T(8,128)S(1)}) custom-call(bf16[32,2048]{1,0:T(8,128)(2,1)} %a_hbm.1, bf16[2048,2048]{1,0:T(8,128)(2,1)} %w_hbm.1), custom_call_target="tpu_custom_call" | custom-call | tf_op jit(solution)/shard_map/out_projection/pallas_call | solution.py:77
  13.8 3.0 %collective-permute-start.1 = (bf16[16,2176]{1,0:T(8,128)(2,1)S(1)}, bf16[16,2176]{1,0:T(8,128)(2,1)S(1)}, u32[]{:S(2)}, u32[]{:S(2)}) collective-permute-start(bf16[16,2176]{1,0:T(8,128)(2,1)S(1)} %get-tuple-element.62.refs_3_.refs_0_), channel_id=1, source_target_pairs={{0,8},{2,10},{4,12},{6,14},{8,0},{10,2},{12,4},{14,6},{16,24},{18,... | collective-permute-start | bytes 208904 | tf_op jit(solution)/shard_map/ppermute | solution.py:484
  16.8 2.6 %collective-permute-start.2 = (bf16[16,2176]{1,0:T(8,128)(2,1)S(1)}, bf16[16,2176]{1,0:T(8,128)(2,1)S(1)}, u32[]{:S(2)}, u32[]{:S(2)}) collective-permute-start(bf16[16,2176]{1,0:T(8,128)(2,1)S(1)} %get-tuple-element.62.refs_3_.refs_0_), channel_id=1, source_target_pairs={{0,16},{2,18},{4,20},{6,22},{8,24},{10,26},{12,28},{14,30},{16,0},... | collective-permute-start | bytes 208904 | tf_op jit(solution)/shard_map/ppermute | solution.py:484
  19.4 4.0 %load_weights.1 = (bf16[1,2048,768]{2,1,0:T(8,128)(2,1)S(1)}, bf16[1,2048,768]{2,1,0:T(8,128)(2,1)S(1)}, bf16[1,768,2048]{2,1,0:T(8,128)(2,1)S(1)}) custom-call(bf16[1,2048,768]{2,1,0:T(8,128)(2,1)} %refs_0_.1, bf16[1,2048,768]{2,1,0:T(8,128)(2,1)} %refs_1_.1, bf16[1,768,2048]{2,1,0:T(8,128)(2,1)} %refs_2_.3, ...), custom_call_target="tpu_custom_call" | custom-call | tf_op jit(solution)/shard_map/load_weights/pallas_call | solution.py:171
  23.4 1.6 %copy-done.2 = bf16[1,2048,768]{2,1,0:T(8,128)(2,1)} copy-done((bf16[1,2048,768]{2,1,0:T(8,128)(2,1)}, bf16[1,2048,768]{2,1,0:T(8,128)(2,1)S(1)}, u32[]{:S(2)}) %copy-start.2) | copy-done | bytes 3145752
  25.0 1.7 %copy-done.5 = bf16[1,2048,768]{2,1,0:T(8,128)(2,1)} copy-done((bf16[1,2048,768]{2,1,0:T(8,128)(2,1)}, bf16[1,2048,768]{2,1,0:T(8,128)(2,1)S(1)}, u32[]{:S(2)}) %copy-start.5) | copy-done | bytes 3145752
  26.7 1.7 %copy-done.8 = bf16[1,768,2048]{2,1,0:T(8,128)(2,1)} copy-done((bf16[1,768,2048]{2,1,0:T(8,128)(2,1)}, bf16[1,768,2048]{2,1,0:T(8,128)(2,1)S(1)}, u32[]{:S(2)}) %copy-start.8) | copy-done | bytes 3145752
  28.5 1.8 %collective-permute-start.4 = (bf16[64,2432]{1,0:T(8,128)(2,1)S(1)}, bf16[64,2432]{1,0:T(8,128)(2,1)S(1)}, u32[]{:S(2)}, u32[]{:S(2)}) collective-permute-start(bf16[64,2432]{1,0:T(8,128)(2,1)S(1)} %get-tuple-element.71), channel_id=1, source_target_pairs={{0,2},{2,0},{4,6},{6,4},{8,10},{10,8},{12,14},{14,12},{16,18},{18,... | collective-permute-start | bytes 933896 | tf_op jit(solution)/shard_map/ppermute | solution.py:484
  31.8 5.6 %collective-permute-done.4.refs_1_.refs_5_ = bf16[64,2432]{1,0:T(8,128)(2,1)S(1)} collective-permute-done((bf16[64,2432]{1,0:T(8,128)(2,1)S(1)}, bf16[64,2432]{1,0:T(8,128)(2,1)S(1)}, u32[]{:S(2)}, u32[]{:S(2)}) %collective-permute-start.4) | collective-permute-done | bytes 311328 | tf_op jit(solution)/shard_map/ppermute | solution.py:484
  41.2 1.9 %copy-done.3 = bf16[1,2048,768]{2,1,0:T(8,128)(2,1)S(1)} copy-done((bf16[1,2048,768]{2,1,0:T(8,128)(2,1)S(1)}, bf16[1,2048,768]{2,1,0:T(8,128)(2,1)}, u32[]{:S(2)}) %copy-start.3) | copy-done | bytes 3145752
  43.0 1.9 %copy-done.6 = bf16[1,2048,768]{2,1,0:T(8,128)(2,1)S(1)} copy-done((bf16[1,2048,768]{2,1,0:T(8,128)(2,1)S(1)}, bf16[1,2048,768]{2,1,0:T(8,128)(2,1)}, u32[]{:S(2)}) %copy-start.6) | copy-done | bytes 3145752
  44.9 1.9 %copy-done.9 = bf16[1,768,2048]{2,1,0:T(8,128)(2,1)S(1)} copy-done((bf16[1,768,2048]{2,1,0:T(8,128)(2,1)S(1)}, bf16[1,768,2048]{2,1,0:T(8,128)(2,1)}, u32[]{:S(2)}) %copy-start.9) | copy-done | bytes 3145752
  46.8 4.0 %experts.2 = (bf16[192,2048]{1,0:T(8,128)(2,1)S(1)}, bf16[64,2048]{1,0:T(8,128)(2,1)S(1)}, bf16[64,2048]{1,0:T(8,128)(2,1)S(1)}, bf16[64,2048]{1,0:T(8,128)(2,1)S(1)}) custom-call(bf16[64,2432]{1,0:T(8,128)(2,1)S(1)} %get-tuple-element.70.refs_0_.refs_4_, bf16[64,2432]{1,0:T(8,128)(2,1)S(1)} %collective-permute-done.4.refs_1_.refs_5_, ...), custom_call_target="tpu_custom_call" | custom-call | flops 3623878656 | tf_op jit(solution)/shard_map/experts/pallas_call | solution.py:231
  53.7 2.0 %experts.3 = (bf16[64,2048]{1,0:T(8,128)(2,1)S(1)}, bf16[64,2048]{1,0:T(8,128)(2,1)S(1)}) custom-call(bf16[32,2432]{1,0:T(8,128)(2,1)S(1)} %collective-permute-done.12.refs_0_.refs_7_, bf16[32,2432]{1,0:T(8,128)(2,1)S(1)} %collective-permute-done.13.refs_1_.refs_8_, bf16[32,2432]{1,0:T(8,128)(2,1)S(1)} %collective-permute-done.14.refs_2_, ...), custom_call_target="tpu_custom_call" | custom-call | flops 1207959552 | tf_op jit(solution)/shard_map/experts/pallas_call | solution.py:231
  57.7 1.7 %collective-permute-start.18 = (bf16[192,512]{1,0:T(8,128)(2,1)S(1)}, bf16[192,512]{1,0:T(8,128)(2,1)S(1)}, u32[]{:S(2)}, u32[]{:S(2)}) collective-permute-start(bf16[192,512]{1,0:T(8,128)(2,1)S(1)} %get-tuple-element.87), channel_id=1, source_target_pairs={{0,6},{2,4},{4,2},{6,0},{8,14},{10,12},{12,10},{14,8},{16,22},{18,... | collective-permute-start | bytes 589832 | tf_op jit(solution)/shard_map/ppermute | solution.py:484
  61.4 2.3 %collective-permute-done.16.refs_1_ = bf16[192,512]{1,0:T(8,128)(2,1)S(1)} collective-permute-done((bf16[192,512]{1,0:T(8,128)(2,1)S(1)}, bf16[192,512]{1,0:T(8,128)(2,1)S(1)}, u32[]{:S(2)}, u32[]{:S(2)}) %collective-permute-start.16) | collective-permute-done | bytes 196640 | tf_op jit(solution)/shard_map/ppermute | solution.py:484
  64.9 5.5 %collective-permute-done.17.refs_2_ = bf16[192,512]{1,0:T(8,128)(2,1)S(1)} collective-permute-done((bf16[192,512]{1,0:T(8,128)(2,1)S(1)}, bf16[192,512]{1,0:T(8,128)(2,1)S(1)}, u32[]{:S(2)}, u32[]{:S(2)}) %collective-permute-start.17) | collective-permute-done | bytes 196640 | tf_op jit(solution)/shard_map/ppermute | solution.py:484
  72.0 3.5 %collective-permute-start.24 = (bf16[64,512]{1,0:T(8,128)(2,1)S(1)}, bf16[64,512]{1,0:T(8,128)(2,1)S(1)}, u32[]{:S(2)}, u32[]{:S(2)}) collective-permute-start(bf16[64,512]{1,0:T(8,128)(2,1)S(1)} %get-tuple-element.100), channel_id=1, source_target_pairs={{0,16},{2,18},{4,20},{6,22},{8,24},{10,26},{12,28},{14,30},{16,0},... | collective-permute-start | bytes 196616 | tf_op jit(solution)/shard_map/ppermute | solution.py:484
  75.7 4.8 %collective-permute-done.23.refs_1_ = bf16[64,512]{1,0:T(8,128)(2,1)S(1)} collective-permute-done((bf16[64,512]{1,0:T(8,128)(2,1)S(1)}, bf16[64,512]{1,0:T(8,128)(2,1)S(1)}, u32[]{:S(2)}, u32[]{:S(2)}) %collective-permute-start.23) | collective-permute-done | bytes 65568 | tf_op jit(solution)/shard_map/ppermute | solution.py:484
  80.5 4.0 %collective-permute-done.24.refs_2_ = bf16[64,512]{1,0:T(8,128)(2,1)S(1)} collective-permute-done((bf16[64,512]{1,0:T(8,128)(2,1)S(1)}, bf16[64,512]{1,0:T(8,128)(2,1)S(1)}, u32[]{:S(2)}, u32[]{:S(2)}) %collective-permute-start.24) | collective-permute-done | bytes 65568 | tf_op jit(solution)/shard_map/ppermute | solution.py:484
  85.9 4.5 %all-gather.2.cloned.1.call-done.w_hbm = bf16[512,2560]{1,0:T(8,128)(2,1)} async-done(((bf16[128,2560]{1,0:T(8,128)(2,1)}), bf16[512,2560]{1,0:T(8,128)(2,1)}) %all-gather.2.cloned.1.call-update) | async-done | bytes 2621456 | tf_op jit(solution)/shard_map/all_gather | solution.py:508
  90.5 2.2 %qkv_projection.1 = (bf16[32,2944]{1,0:T(8,128)(2,1)S(1)}, bf16[32,2944]{1,0:T(8,128)(2,1)S(1)}, bf16[32,2944]{1,0:T(8,128)(2,1)S(1)}, bf16[32,2944]{1,0:T(8,128)(2,1)S(1)}) custom-call(bf16[64,640]{1,0:T(8,128)(2,1)S(1)} %get-tuple-element.102.mine_ref, bf16[64,640]{1,0:T(8,128)(2,1)S(1)} %collective-permute-done.26.theirs_ref, ...), custom_call_target="tpu_custom_call" | custom-call | tf_op jit(solution)/shard_map/qkv_projection/pallas_call | solution.py:389
  96.2 4.1 %collective-permute-done.27.refs_1_ = bf16[32,2944]{1,0:T(8,128)(2,1)S(1)} collective-permute-done((bf16[32,2944]{1,0:T(8,128)(2,1)S(1)}, bf16[32,2944]{1,0:T(8,128)(2,1)S(1)}, u32[]{:S(2)}, u32[]{:S(2)}) %collective-permute-start.27) | collective-permute-done | bytes 188448 | tf_op jit(solution)/shard_map/ppermute | solution.py:484
  100.4 4.0 %collective-permute-done.28.refs_2_ = bf16[32,2944]{1,0:T(8,128)(2,1)S(1)} collective-permute-done((bf16[32,2944]{1,0:T(8,128)(2,1)S(1)}, bf16[32,2944]{1,0:T(8,128)(2,1)S(1)}, u32[]{:S(2)}, u32[]{:S(2)}) %collective-permute-start.28) | collective-permute-done | bytes 188448 | tf_op jit(solution)/shard_map/ppermute | solution.py:484
  (100 shorter events, 22.7 us)
Async XLA Ops:
  7.2 83.2 %all-gather.2.cloned.1.call-start = ((), (), s32[]{:S(2)}) async-start(), calls=%async_computation | async-start | bytes 3276800 | tf_op jit(solution)/shard_map/all_gather | solution.py:508
  13.8 14.7 %collective-permute-start.1 = (bf16[16,2176]{1,0:T(8,128)(2,1)S(1)}, bf16[16,2176]{1,0:T(8,128)(2,1)S(1)}, u32[]{:S(2)}, u32[]{:S(2)}) collective-permute-start(bf16[16,2176]{1,0:T(8,128)(2,1)S(1)} %get-tuple-element.62.refs_3_.refs_0_), channel_id=1, source_target_pairs={{0,8},{2,10},{4,12},{6,14},{8,0},{10,2},{12,4},{14,6},{16,24},{18,... | collective-permute-start | bytes 208904 | tf_op jit(solution)/shard_map/ppermute | solution.py:484
  16.8 11.7 %collective-permute-start.2 = (bf16[16,2176]{1,0:T(8,128)(2,1)S(1)}, bf16[16,2176]{1,0:T(8,128)(2,1)S(1)}, u32[]{:S(2)}, u32[]{:S(2)}) collective-permute-start(bf16[16,2176]{1,0:T(8,128)(2,1)S(1)} %get-tuple-element.62.refs_3_.refs_0_), channel_id=1, source_target_pairs={{0,16},{2,18},{4,20},{6,22},{8,24},{10,26},{12,28},{14,30},{16,0},... | collective-permute-start | bytes 208904 | tf_op jit(solution)/shard_map/ppermute | solution.py:484
  19.3 9.1 %collective-permute-start.3 = (bf16[16,2176]{1,0:T(8,128)(2,1)S(1)}, bf16[16,2176]{1,0:T(8,128)(2,1)S(1)}, u32[]{:S(2)}, u32[]{:S(2)}) collective-permute-start(bf16[16,2176]{1,0:T(8,128)(2,1)S(1)} %get-tuple-element.62.refs_3_.refs_0_), channel_id=1, source_target_pairs={{0,24},{2,26},{4,28},{6,30},{8,16},{10,18},{12,20},{14,22},{16,8},... | collective-permute-start | bytes 208904 | tf_op jit(solution)/shard_map/ppermute | solution.py:484
  28.5 8.9 %collective-permute-start.4 = (bf16[64,2432]{1,0:T(8,128)(2,1)S(1)}, bf16[64,2432]{1,0:T(8,128)(2,1)S(1)}, u32[]{:S(2)}, u32[]{:S(2)}) collective-permute-start(bf16[64,2432]{1,0:T(8,128)(2,1)S(1)} %get-tuple-element.71), channel_id=1, source_target_pairs={{0,2},{2,0},{4,6},{6,4},{8,10},{10,8},{12,14},{14,12},{16,18},{18,... | collective-permute-start | bytes 933896 | tf_op jit(solution)/shard_map/ppermute | solution.py:484
  30.3 8.4 %collective-permute-start.5 = (bf16[64,2432]{1,0:T(8,128)(2,1)S(1)}, bf16[64,2432]{1,0:T(8,128)(2,1)S(1)}, u32[]{:S(2)}, u32[]{:S(2)}) collective-permute-start(bf16[64,2432]{1,0:T(8,128)(2,1)S(1)} %get-tuple-element.72), channel_id=1, source_target_pairs={{0,4},{2,6},{4,0},{6,2},{8,12},{10,14},{12,8},{14,10},{16,20},{18,... | collective-permute-start | bytes 933896 | tf_op jit(solution)/shard_map/ppermute | solution.py:484
  31.8 9.3 %collective-permute-start.6 = (bf16[64,2432]{1,0:T(8,128)(2,1)S(1)}, bf16[64,2432]{1,0:T(8,128)(2,1)S(1)}, u32[]{:S(2)}, u32[]{:S(2)}) collective-permute-start(bf16[64,2432]{1,0:T(8,128)(2,1)S(1)} %get-tuple-element.70.refs_0_.refs_4_), channel_id=1, source_target_pairs={{0,1},{1,0},{2,3},{3,2},{4,5},{5,4},{6,7},{7,6},{8,9},{9,8},{10,11... | collective-permute-start | bytes 933896 | tf_op jit(solution)/shard_map/ppermute | solution.py:481
  37.4 3.7 %collective-permute-start.7 = (bf16[64,2432]{1,0:T(8,128)(2,1)S(1)}, bf16[64,2432]{1,0:T(8,128)(2,1)S(1)}, u32[]{:S(2)}, u32[]{:S(2)}) collective-permute-start(bf16[64,2432]{1,0:T(8,128)(2,1)S(1)} %collective-permute-done.4.refs_1_.refs_5_), channel_id=1, source_target_pairs={{0,1},{1,0},{2,3},{3,2},{4,5},{5,4},{6,7},{7,6},{8,9},{9,8},{10,11... | collective-permute-start | bytes 933896 | tf_op jit(solution)/shard_map/ppermute | solution.py:481
  38.7 2.5 %collective-permute-start.8 = (bf16[64,2432]{1,0:T(8,128)(2,1)S(1)}, bf16[64,2432]{1,0:T(8,128)(2,1)S(1)}, u32[]{:S(2)}, u32[]{:S(2)}) collective-permute-start(bf16[64,2432]{1,0:T(8,128)(2,1)S(1)} %collective-permute-done.5.refs_2_.refs_6_), channel_id=1, source_target_pairs={{0,1},{1,0},{2,3},{3,2},{4,5},{5,4},{6,7},{7,6},{8,9},{9,8},{10,11... | collective-permute-start | bytes 933896 | tf_op jit(solution)/shard_map/ppermute | solution.py:481
  38.7 12.9 %collective-permute-start.12 = (bf16[32,2432]{1,0:T(8,128)(2,1)S(1)}, bf16[32,2432]{1,0:T(8,128)(2,1)S(1)}, u32[]{:S(2)}, u32[]{:S(2)}) collective-permute-start(bf16[32,2432]{1,0:T(8,128)(2,1)S(1)} %slice.8), channel_id=1, source_target_pairs={{0,4},{2,6},{4,0},{6,2},{8,12},{10,14},{12,8},{14,10},{16,20},{18,... | collective-permute-start | bytes 466952 | tf_op jit(solution)/shard_map/ppermute | solution.py:484
  40.3 11.7 %collective-permute-start.13 = (bf16[32,2432]{1,0:T(8,128)(2,1)S(1)}, bf16[32,2432]{1,0:T(8,128)(2,1)S(1)}, u32[]{:S(2)}, u32[]{:S(2)}) collective-permute-start(bf16[32,2432]{1,0:T(8,128)(2,1)S(1)} %slice.9), channel_id=1, source_target_pairs={{0,2},{2,0},{4,6},{6,4},{8,10},{10,8},{12,14},{14,12},{16,18},{18,... | collective-permute-start | bytes 466952 | tf_op jit(solution)/shard_map/ppermute | solution.py:484
  55.7 3.7 %collective-permute-start.19 = (bf16[64,2048]{1,0:T(8,128)(2,1)S(1)}, bf16[64,2048]{1,0:T(8,128)(2,1)S(1)}, u32[]{:S(2)}, u32[]{:S(2)}) collective-permute-start(bf16[64,2048]{1,0:T(8,128)(2,1)S(1)} %get-tuple-element.93), channel_id=1, source_target_pairs={{0,1},{1,0},{2,3},{3,2},{4,5},{5,4},{6,7},{7,6},{8,9},{9,8},{10,11... | collective-permute-start | bytes 786440 | tf_op jit(solution)/shard_map/ppermute | solution.py:481
  55.9 7.7 %collective-permute-start.16 = (bf16[192,512]{1,0:T(8,128)(2,1)S(1)}, bf16[192,512]{1,0:T(8,128)(2,1)S(1)}, u32[]{:S(2)}, u32[]{:S(2)}) collective-permute-start(bf16[192,512]{1,0:T(8,128)(2,1)S(1)} %get-tuple-element.85), channel_id=1, source_target_pairs={{0,2},{2,0},{4,6},{6,4},{8,10},{10,8},{12,14},{14,12},{16,18},{18,... | collective-permute-start | bytes 589832 | tf_op jit(solution)/shard_map/ppermute | solution.py:484
  57.2 13.2 %collective-permute-start.17 = (bf16[192,512]{1,0:T(8,128)(2,1)S(1)}, bf16[192,512]{1,0:T(8,128)(2,1)S(1)}, u32[]{:S(2)}, u32[]{:S(2)}) collective-permute-start(bf16[192,512]{1,0:T(8,128)(2,1)S(1)} %get-tuple-element.86), channel_id=1, source_target_pairs={{0,4},{2,6},{4,0},{6,2},{8,12},{10,14},{12,8},{14,10},{16,20},{18,... | collective-permute-start | bytes 589832 | tf_op jit(solution)/shard_map/ppermute | solution.py:484
  57.7 12.7 %collective-permute-start.18 = (bf16[192,512]{1,0:T(8,128)(2,1)S(1)}, bf16[192,512]{1,0:T(8,128)(2,1)S(1)}, u32[]{:S(2)}, u32[]{:S(2)}) collective-permute-start(bf16[192,512]{1,0:T(8,128)(2,1)S(1)} %get-tuple-element.87), channel_id=1, source_target_pairs={{0,6},{2,4},{4,2},{6,0},{8,14},{10,12},{12,10},{14,8},{16,22},{18,... | collective-permute-start | bytes 589832 | tf_op jit(solution)/shard_map/ppermute | solution.py:484
  59.5 10.9 %collective-permute-start.20 = (bf16[64,512]{1,0:T(8,128)(2,1)S(1)}, bf16[64,512]{1,0:T(8,128)(2,1)S(1)}, u32[]{:S(2)}, u32[]{:S(2)}) collective-permute-start(bf16[64,512]{1,0:T(8,128)(2,1)S(1)} %get-tuple-element.95), channel_id=1, source_target_pairs={{0,2},{2,0},{4,6},{6,4},{8,10},{10,8},{12,14},{14,12},{16,18},{18,... | collective-permute-start | bytes 196616 | tf_op jit(solution)/shard_map/ppermute | solution.py:484
  60.8 10.3 %collective-permute-start.21 = (bf16[64,512]{1,0:T(8,128)(2,1)S(1)}, bf16[64,512]{1,0:T(8,128)(2,1)S(1)}, u32[]{:S(2)}, u32[]{:S(2)}) collective-permute-start(bf16[64,512]{1,0:T(8,128)(2,1)S(1)} %get-tuple-element.96), channel_id=1, source_target_pairs={{0,4},{2,6},{4,0},{6,2},{8,12},{10,14},{12,8},{14,10},{16,20},{18,... | collective-permute-start | bytes 196616 | tf_op jit(solution)/shard_map/ppermute | solution.py:484
  63.7 7.4 %collective-permute-start.22 = (bf16[64,512]{1,0:T(8,128)(2,1)S(1)}, bf16[64,512]{1,0:T(8,128)(2,1)S(1)}, u32[]{:S(2)}, u32[]{:S(2)}) collective-permute-start(bf16[64,512]{1,0:T(8,128)(2,1)S(1)} %get-tuple-element.97), channel_id=1, source_target_pairs={{0,6},{2,4},{4,2},{6,0},{8,14},{10,12},{12,10},{14,8},{16,22},{18,... | collective-permute-start | bytes 196616 | tf_op jit(solution)/shard_map/ppermute | solution.py:484
  71.2 9.2 %collective-permute-start.23 = (bf16[64,512]{1,0:T(8,128)(2,1)S(1)}, bf16[64,512]{1,0:T(8,128)(2,1)S(1)}, u32[]{:S(2)}, u32[]{:S(2)}) collective-permute-start(bf16[64,512]{1,0:T(8,128)(2,1)S(1)} %get-tuple-element.99), channel_id=1, source_target_pairs={{0,8},{2,10},{4,12},{6,14},{8,0},{10,2},{12,4},{14,6},{16,24},{18,... | collective-permute-start | bytes 196616 | tf_op jit(solution)/shard_map/ppermute | solution.py:484
  72.0 12.5 %collective-permute-start.24 = (bf16[64,512]{1,0:T(8,128)(2,1)S(1)}, bf16[64,512]{1,0:T(8,128)(2,1)S(1)}, u32[]{:S(2)}, u32[]{:S(2)}) collective-permute-start(bf16[64,512]{1,0:T(8,128)(2,1)S(1)} %get-tuple-element.100), channel_id=1, source_target_pairs={{0,16},{2,18},{4,20},{6,22},{8,24},{10,26},{12,28},{14,30},{16,0},... | collective-permute-start | bytes 196616 | tf_op jit(solution)/shard_map/ppermute | solution.py:484
  75.4 9.0 %collective-permute-start.25 = (bf16[64,512]{1,0:T(8,128)(2,1)S(1)}, bf16[64,512]{1,0:T(8,128)(2,1)S(1)}, u32[]{:S(2)}, u32[]{:S(2)}) collective-permute-start(bf16[64,512]{1,0:T(8,128)(2,1)S(1)} %get-tuple-element.101), channel_id=1, source_target_pairs={{0,24},{2,26},{4,28},{6,30},{8,16},{10,18},{12,20},{14,22},{16,8},... | collective-permute-start | bytes 196616 | tf_op jit(solution)/shard_map/ppermute | solution.py:484
  92.7 7.7 %collective-permute-start.27 = (bf16[32,2944]{1,0:T(8,128)(2,1)S(1)}, bf16[32,2944]{1,0:T(8,128)(2,1)S(1)}, u32[]{:S(2)}, u32[]{:S(2)}) collective-permute-start(bf16[32,2944]{1,0:T(8,128)(2,1)S(1)} %get-tuple-element.106), channel_id=1, source_target_pairs={{0,2},{2,0},{4,6},{6,4},{8,10},{10,8},{12,14},{14,12},{16,18},{18,... | collective-permute-start | bytes 565256 | tf_op jit(solution)/shard_map/ppermute | solution.py:484
  94.2 10.2 %collective-permute-start.28 = (bf16[32,2944]{1,0:T(8,128)(2,1)S(1)}, bf16[32,2944]{1,0:T(8,128)(2,1)S(1)}, u32[]{:S(2)}, u32[]{:S(2)}) collective-permute-start(bf16[32,2944]{1,0:T(8,128)(2,1)S(1)} %get-tuple-element.107), channel_id=1, source_target_pairs={{0,4},{2,6},{4,0},{6,2},{8,12},{10,14},{12,8},{14,10},{16,20},{18,... | collective-permute-start | bytes 565256 | tf_op jit(solution)/shard_map/ppermute | solution.py:484
  95.7 8.7 %collective-permute-start.29 = (bf16[32,2944]{1,0:T(8,128)(2,1)S(1)}, bf16[32,2944]{1,0:T(8,128)(2,1)S(1)}, u32[]{:S(2)}, u32[]{:S(2)}) collective-permute-start(bf16[32,2944]{1,0:T(8,128)(2,1)S(1)} %get-tuple-element.108), channel_id=1, source_target_pairs={{0,6},{2,4},{4,2},{6,0},{8,14},{10,12},{12,10},{14,8},{16,22},{18,... | collective-permute-start | bytes 565256 | tf_op jit(solution)/shard_map/ppermute | solution.py:484
  (26 other events, 216.9 us)
Sparse Core Ops, SparseCore 0:
  28.6 61.8 all-gather.1

commit v8 on v7

--- a/solution.py
+++ b/solution.py
@@ -497,15 +497,17 @@
     meta = jnp.concatenate([high, dense - high], axis=1).astype(jnp.bfloat16)
 
     lines = [list(range(i, n_expert, PLANE)) for i in range(PLANE)]
-    joined = jnp.concatenate([q_weight, kv_weight], axis=1)
     mine, theirs = out_projection(attn_out, out_weight)
+    mine, q_own, kv_own = lax.optimization_barrier((mine, q_weight, kv_weight))
+    joined = jnp.concatenate([q_own, kv_own], axis=1)
     tokens, *firsts = first_norm(
         (mine,), (to_core(theirs),), residual, attn_gain[None, :], meta, depth
     )
-    weights = load((w_gate, w_up, w_down), (tokens, joined))
+    tokens, joined = lax.optimization_barrier((tokens, joined))
+    qkv = lax.all_gather(joined, "expert", axis=0, tiled=True, axis_index_groups=lines)
+    weights = load((w_gate, w_up, w_down), (tokens,))
     line = to_z([tokens] * depth)
-    *line, joined, gate, up, down = lax.optimization_barrier((*line, joined, *weights))
-    qkv = lax.all_gather(joined, "expert", axis=0, tiled=True, axis_index_groups=lines)
+    *line, gate, up, down = lax.optimization_barrier((*line, *weights))
     weights = (gate, up, down)
     near = to_plane(pack(line, firsts))
     cut = near[0].shape[0] // 2

time: 112 us -> 99.1 us (0.88)
  local copies, waits for them, and re-layouts: 11.1 us -> 0.36 us
  waiting for transfers between devices: 40 us -> 37 us
    unnamed x39 -> x18, local copies, waits for them, and re-layouts: 10.8 us -> 0.05 us
    all_gather x1, waiting for transfers between devices: 4.53 us -> 0.01 us  [per_device_dense(): lax.all_gather(joined, 'expert', axis=0, tiled=True, axis_index_groups=li...]
    ppermute x19, waiting for transfers between devices: 32.3 us -> 34.4 us  [to_expert(): lax.ppermute(value, 'expert', [(i, i ^ offset) for i in range(n_expert)])]
  transfers between devices with their start and end apart: 31 -> 31, of which waited for: 16 -> 17; matrix products, arithmetic and copies ran while one was open for 0% -> 1% of each run, Pallas kernels for 9% -> 11%
where the time goes in v8:
time: 99.1 us; the launch traced here: 98.9 us
  waiting for transfers between devices  37 us (37%)
  starting transfers between devices  27.7 us (28%)
  Pallas kernels  18.5 us (19%)
  between operations  14.3 us (14%)
  other arithmetic  1.09 us (1%)
    ppermute x19, waiting for transfers between devices, to_expert(): lax.ppermute(value, 'expert', [(i, i ^ offset) for i in range(n_expert)])  34.4 us
    ppermute x19, starting transfers between devices, to_expert(): lax.ppermute(value, 'expert', [(i, i ^ offset) for i in range(n_expert)])  25.8 us
    pallas_call x2, Pallas kernels, experts(): pl.pallas_call(functools.partial(expert_kernel, depth, chunk, len(blocks)...  6.04 us
    pallas_call x1, Pallas kernels, out_projection(): pl.pallas_call(functools.partial(out_projection_kernel, chunk), out_shape...  4.83 us
    pallas_call x1, Pallas kernels, load(): pl.pallas_call(load_kernel, out_shape=tuple((pltpu.VMEM(w.shape, w.dtype)...  3.8 us
    ppermute x11, waiting for transfers between devices, to_core(): return lax.ppermute(value, 'tensor', [(0, 1), (1, 0)])  2.59 us
    pallas_call x1, Pallas kernels, projection(): pl.pallas_call(functools.partial(projection_kernel, chunk), out_shape=(sh...  2.23 us
  transfers between devices with their start and end apart: 31, of which 17 were waited for; matrix products, arithmetic and copies ran while one was open for 1% of the time, Pallas kernels for 11%

profile of v8, /device:TPU:0, one launch (start us, length us, event | category | flops | bytes accessed | tf_op | source)
XLA Modules:
  0.0 98.9 jit_solution(8581742131172503190)
XLA Ops:
  7.3 4.8 %out_projection.1 = (f32[16,2048]{1,0:T(8,128)S(1)}, f32[16,2048]{1,0:T(8,128)S(1)}) custom-call(bf16[32,2048]{1,0:T(8,128)(2,1)} %a_hbm.1, bf16[2048,2048]{1,0:T(8,128)(2,1)} %w_hbm.1), custom_call_target="tpu_custom_call" | custom-call | tf_op jit(solution)/shard_map/out_projection/pallas_call | solution.py:77
  14.2 2.7 %collective-permute-start.1 = (bf16[16,2176]{1,0:T(8,128)(2,1)S(1)}, bf16[16,2176]{1,0:T(8,128)(2,1)S(1)}, u32[]{:S(2)}, u32[]{:S(2)}) collective-permute-start(bf16[16,2176]{1,0:T(8,128)(2,1)S(1)} %get-tuple-element.70.refs_3_.refs_0_), channel_id=1, source_target_pairs={{0,8},{2,10},{4,12},{6,14},{8,0},{10,2},{12,4},{14,6},{16,24},{18,... | collective-permute-start | bytes 208904 | tf_op jit(solution)/shard_map/ppermute | solution.py:484
  16.9 2.6 %collective-permute-start.2 = (bf16[16,2176]{1,0:T(8,128)(2,1)S(1)}, bf16[16,2176]{1,0:T(8,128)(2,1)S(1)}, u32[]{:S(2)}, u32[]{:S(2)}) collective-permute-start(bf16[16,2176]{1,0:T(8,128)(2,1)S(1)} %get-tuple-element.70.refs_3_.refs_0_), channel_id=1, source_target_pairs={{0,16},{2,18},{4,20},{6,22},{8,24},{10,26},{12,28},{14,30},{16,0},... | collective-permute-start | bytes 208904 | tf_op jit(solution)/shard_map/ppermute | solution.py:484
  19.5 3.8 %load_weights.1 = (bf16[1,2048,768]{2,1,0:T(8,128)(2,1)S(1)}, bf16[1,2048,768]{2,1,0:T(8,128)(2,1)S(1)}, bf16[1,768,2048]{2,1,0:T(8,128)(2,1)S(1)}) custom-call(bf16[1,2048,768]{2,1,0:T(8,128)(2,1)} %refs_0_.1, bf16[1,2048,768]{2,1,0:T(8,128)(2,1)} %refs_1_.1, bf16[1,768,2048]{2,1,0:T(8,128)(2,1)} %refs_2_.3, ...), custom_call_target="tpu_custom_call" | custom-call | tf_op jit(solution)/shard_map/load_weights/pallas_call | solution.py:171
  23.3 1.5 %collective-permute-done.2.refs_2_ = bf16[16,2176]{1,0:T(8,128)(2,1)S(1)} collective-permute-done((bf16[16,2176]{1,0:T(8,128)(2,1)S(1)}, bf16[16,2176]{1,0:T(8,128)(2,1)S(1)}, u32[]{:S(2)}, u32[]{:S(2)}) %collective-permute-start.2) | collective-permute-done | bytes 69664 | tf_op jit(solution)/shard_map/ppermute | solution.py:484
  25.7 1.6 %collective-permute-start.4 = (bf16[64,2432]{1,0:T(8,128)(2,1)S(1)}, bf16[64,2432]{1,0:T(8,128)(2,1)S(1)}, u32[]{:S(2)}, u32[]{:S(2)}) collective-permute-start(bf16[64,2432]{1,0:T(8,128)(2,1)S(1)} %get-tuple-element.79), channel_id=1, source_target_pairs={{0,2},{2,0},{4,6},{6,4},{8,10},{10,8},{12,14},{14,12},{16,18},{18,... | collective-permute-start | bytes 933896 | tf_op jit(solution)/shard_map/ppermute | solution.py:484
  27.3 1.5 %collective-permute-start.5 = (bf16[64,2432]{1,0:T(8,128)(2,1)S(1)}, bf16[64,2432]{1,0:T(8,128)(2,1)S(1)}, u32[]{:S(2)}, u32[]{:S(2)}) collective-permute-start(bf16[64,2432]{1,0:T(8,128)(2,1)S(1)} %get-tuple-element.80), channel_id=1, source_target_pairs={{0,4},{2,6},{4,0},{6,2},{8,12},{10,14},{12,8},{14,10},{16,20},{18,... | collective-permute-start | bytes 933896 | tf_op jit(solution)/shard_map/ppermute | solution.py:484
  28.8 5.0 %collective-permute-done.4.refs_1_.refs_5_ = bf16[64,2432]{1,0:T(8,128)(2,1)S(1)} collective-permute-done((bf16[64,2432]{1,0:T(8,128)(2,1)S(1)}, bf16[64,2432]{1,0:T(8,128)(2,1)S(1)}, u32[]{:S(2)}, u32[]{:S(2)}) %collective-permute-start.4) | collective-permute-done | bytes 311328 | tf_op jit(solution)/shard_map/ppermute | solution.py:484
  35.0 1.6 %collective-permute-start.12 = (bf16[32,2432]{1,0:T(8,128)(2,1)S(1)}, bf16[32,2432]{1,0:T(8,128)(2,1)S(1)}, u32[]{:S(2)}, u32[]{:S(2)}) collective-permute-start(bf16[32,2432]{1,0:T(8,128)(2,1)S(1)} %slice.8), channel_id=1, source_target_pairs={{0,4},{2,6},{4,0},{6,2},{8,12},{10,14},{12,8},{14,10},{16,20},{18,... | collective-permute-start | bytes 466952 | tf_op jit(solution)/shard_map/ppermute | solution.py:484
  37.5 4.0 %experts.2 = (bf16[192,2048]{1,0:T(8,128)(2,1)S(1)}, bf16[64,2048]{1,0:T(8,128)(2,1)S(1)}, bf16[64,2048]{1,0:T(8,128)(2,1)S(1)}, bf16[64,2048]{1,0:T(8,128)(2,1)S(1)}) custom-call(bf16[64,2432]{1,0:T(8,128)(2,1)S(1)} %get-tuple-element.78.refs_0_.refs_4_, bf16[64,2432]{1,0:T(8,128)(2,1)S(1)} %collective-permute-done.4.refs_1_.refs_5_, ...), custom_call_target="tpu_custom_call" | custom-call | flops 3623878656 | tf_op jit(solution)/shard_map/experts/pallas_call | solution.py:231
  44.3 2.0 %experts.3 = (bf16[64,2048]{1,0:T(8,128)(2,1)S(1)}, bf16[64,2048]{1,0:T(8,128)(2,1)S(1)}) custom-call(bf16[32,2432]{1,0:T(8,128)(2,1)S(1)} %collective-permute-done.12.refs_0_.refs_7_, bf16[32,2432]{1,0:T(8,128)(2,1)S(1)} %collective-permute-done.13.refs_1_.refs_8_, bf16[32,2432]{1,0:T(8,128)(2,1)S(1)} %collective-permute-done.14.refs_2_, ...), custom_call_target="tpu_custom_call" | custom-call | flops 1207959552 | tf_op jit(solution)/shard_map/experts/pallas_call | solution.py:231
  48.3 1.7 %collective-permute-start.18 = (bf16[192,512]{1,0:T(8,128)(2,1)S(1)}, bf16[192,512]{1,0:T(8,128)(2,1)S(1)}, u32[]{:S(2)}, u32[]{:S(2)}) collective-permute-start(bf16[192,512]{1,0:T(8,128)(2,1)S(1)} %get-tuple-element.95), channel_id=1, source_target_pairs={{0,6},{2,4},{4,2},{6,0},{8,14},{10,12},{12,10},{14,8},{16,22},{18,... | collective-permute-start | bytes 589832 | tf_op jit(solution)/shard_map/ppermute | solution.py:484
  50.1 1.3 %collective-permute-start.20 = (bf16[64,512]{1,0:T(8,128)(2,1)S(1)}, bf16[64,512]{1,0:T(8,128)(2,1)S(1)}, u32[]{:S(2)}, u32[]{:S(2)}) collective-permute-start(bf16[64,512]{1,0:T(8,128)(2,1)S(1)} %get-tuple-element.103), channel_id=1, source_target_pairs={{0,2},{2,0},{4,6},{6,4},{8,10},{10,8},{12,14},{14,12},{16,18},{18,... | collective-permute-start | bytes 196616 | tf_op jit(solution)/shard_map/ppermute | solution.py:484
  51.9 2.3 %collective-permute-done.16.refs_1_ = bf16[192,512]{1,0:T(8,128)(2,1)S(1)} collective-permute-done((bf16[192,512]{1,0:T(8,128)(2,1)S(1)}, bf16[192,512]{1,0:T(8,128)(2,1)S(1)}, u32[]{:S(2)}, u32[]{:S(2)}) %collective-permute-start.16) | collective-permute-done | bytes 196640 | tf_op jit(solution)/shard_map/ppermute | solution.py:484
  55.5 5.5 %collective-permute-done.17.refs_2_ = bf16[192,512]{1,0:T(8,128)(2,1)S(1)} collective-permute-done((bf16[192,512]{1,0:T(8,128)(2,1)S(1)}, bf16[192,512]{1,0:T(8,128)(2,1)S(1)}, u32[]{:S(2)}, u32[]{:S(2)}) %collective-permute-start.17) | collective-permute-done | bytes 196640 | tf_op jit(solution)/shard_map/ppermute | solution.py:484
  61.8 2.5 %collective-permute-start.23 = (bf16[64,512]{1,0:T(8,128)(2,1)S(1)}, bf16[64,512]{1,0:T(8,128)(2,1)S(1)}, u32[]{:S(2)}, u32[]{:S(2)}) collective-permute-start(bf16[64,512]{1,0:T(8,128)(2,1)S(1)} %get-tuple-element.107), channel_id=1, source_target_pairs={{0,8},{2,10},{4,12},{6,14},{8,0},{10,2},{12,4},{14,6},{16,24},{18,... | collective-permute-start | bytes 196616 | tf_op jit(solution)/shard_map/ppermute | solution.py:484
  65.1 1.7 %collective-permute-start.25 = (bf16[64,512]{1,0:T(8,128)(2,1)S(1)}, bf16[64,512]{1,0:T(8,128)(2,1)S(1)}, u32[]{:S(2)}, u32[]{:S(2)}) collective-permute-start(bf16[64,512]{1,0:T(8,128)(2,1)S(1)} %get-tuple-element.109), channel_id=1, source_target_pairs={{0,24},{2,26},{4,28},{6,30},{8,16},{10,18},{12,20},{14,22},{16,8},... | collective-permute-start | bytes 196616 | tf_op jit(solution)/shard_map/ppermute | solution.py:484
  66.8 4.1 %collective-permute-done.23.refs_1_ = bf16[64,512]{1,0:T(8,128)(2,1)S(1)} collective-permute-done((bf16[64,512]{1,0:T(8,128)(2,1)S(1)}, bf16[64,512]{1,0:T(8,128)(2,1)S(1)}, u32[]{:S(2)}, u32[]{:S(2)}) %collective-permute-start.23) | collective-permute-done | bytes 65568 | tf_op jit(solution)/shard_map/ppermute | solution.py:484
  70.9 4.9 %collective-permute-done.24.refs_2_ = bf16[64,512]{1,0:T(8,128)(2,1)S(1)} collective-permute-done((bf16[64,512]{1,0:T(8,128)(2,1)S(1)}, bf16[64,512]{1,0:T(8,128)(2,1)S(1)}, u32[]{:S(2)}, u32[]{:S(2)}) %collective-permute-start.24) | collective-permute-done | bytes 65568 | tf_op jit(solution)/shard_map/ppermute | solution.py:484
  76.1 1.3 %collective-permute-done.26.theirs_ref = bf16[64,640]{1,0:T(8,128)(2,1)S(1)} collective-permute-done((bf16[64,640]{1,0:T(8,128)(2,1)S(1)}, bf16[64,640]{1,0:T(8,128)(2,1)S(1)}, u32[]{:S(2)}, u32[]{:S(2)}) %collective-permute-start.26) | collective-permute-done | bytes 81952 | tf_op jit(solution)/shard_map/ppermute | solution.py:481
  77.4 2.2 %qkv_projection.1 = (bf16[32,2944]{1,0:T(8,128)(2,1)S(1)}, bf16[32,2944]{1,0:T(8,128)(2,1)S(1)}, bf16[32,2944]{1,0:T(8,128)(2,1)S(1)}, bf16[32,2944]{1,0:T(8,128)(2,1)S(1)}) custom-call(bf16[64,640]{1,0:T(8,128)(2,1)S(1)} %get-tuple-element.110.mine_ref, bf16[64,640]{1,0:T(8,128)(2,1)S(1)} %collective-permute-done.26.theirs_ref, ...), custom_call_target="tpu_custom_call" | custom-call | tf_op jit(solution)/shard_map/qkv_projection/pallas_call | solution.py:389
  80.6 1.6 %collective-permute-start.28 = (bf16[32,2944]{1,0:T(8,128)(2,1)S(1)}, bf16[32,2944]{1,0:T(8,128)(2,1)S(1)}, u32[]{:S(2)}, u32[]{:S(2)}) collective-permute-start(bf16[32,2944]{1,0:T(8,128)(2,1)S(1)} %get-tuple-element.115), channel_id=1, source_target_pairs={{0,4},{2,6},{4,0},{6,2},{8,12},{10,14},{12,8},{14,10},{16,20},{18,... | collective-permute-start | bytes 565256 | tf_op jit(solution)/shard_map/ppermute | solution.py:484
  83.2 4.1 %collective-permute-done.27.refs_1_ = bf16[32,2944]{1,0:T(8,128)(2,1)S(1)} collective-permute-done((bf16[32,2944]{1,0:T(8,128)(2,1)S(1)}, bf16[32,2944]{1,0:T(8,128)(2,1)S(1)}, u32[]{:S(2)}, u32[]{:S(2)}) %collective-permute-start.27) | collective-permute-done | bytes 188448 | tf_op jit(solution)/shard_map/ppermute | solution.py:484
  87.2 3.9 %collective-permute-done.28.refs_2_ = bf16[32,2944]{1,0:T(8,128)(2,1)S(1)} collective-permute-done((bf16[32,2944]{1,0:T(8,128)(2,1)S(1)}, bf16[32,2944]{1,0:T(8,128)(2,1)S(1)}, u32[]{:S(2)}, u32[]{:S(2)}) %collective-permute-start.28) | collective-permute-done | bytes 188448 | tf_op jit(solution)/shard_map/ppermute | solution.py:484
  (79 shorter events, 16.4 us)
Async XLA Ops:
  7.2 70.1 %all-gather.2.cloned.1.call-start = ((), (), s32[]{:S(2)}) async-start(), calls=%async_computation | async-start | bytes 3276800 | tf_op jit(solution)/shard_map/all_gather | solution.py:507
  14.2 9.1 %collective-permute-start.1 = (bf16[16,2176]{1,0:T(8,128)(2,1)S(1)}, bf16[16,2176]{1,0:T(8,128)(2,1)S(1)}, u32[]{:S(2)}, u32[]{:S(2)}) collective-permute-start(bf16[16,2176]{1,0:T(8,128)(2,1)S(1)} %get-tuple-element.70.refs_3_.refs_0_), channel_id=1, source_target_pairs={{0,8},{2,10},{4,12},{6,14},{8,0},{10,2},{12,4},{14,6},{16,24},{18,... | collective-permute-start | bytes 208904 | tf_op jit(solution)/shard_map/ppermute | solution.py:484
  16.9 7.9 %collective-permute-start.2 = (bf16[16,2176]{1,0:T(8,128)(2,1)S(1)}, bf16[16,2176]{1,0:T(8,128)(2,1)S(1)}, u32[]{:S(2)}, u32[]{:S(2)}) collective-permute-start(bf16[16,2176]{1,0:T(8,128)(2,1)S(1)} %get-tuple-element.70.refs_3_.refs_0_), channel_id=1, source_target_pairs={{0,16},{2,18},{4,20},{6,22},{8,24},{10,26},{12,28},{14,30},{16,0},... | collective-permute-start | bytes 208904 | tf_op jit(solution)/shard_map/ppermute | solution.py:484
  19.5 6.2 %collective-permute-start.3 = (bf16[16,2176]{1,0:T(8,128)(2,1)S(1)}, bf16[16,2176]{1,0:T(8,128)(2,1)S(1)}, u32[]{:S(2)}, u32[]{:S(2)}) collective-permute-start(bf16[16,2176]{1,0:T(8,128)(2,1)S(1)} %get-tuple-element.70.refs_3_.refs_0_), channel_id=1, source_target_pairs={{0,24},{2,26},{4,28},{6,30},{8,16},{10,18},{12,20},{14,22},{16,8},... | collective-permute-start | bytes 208904 | tf_op jit(solution)/shard_map/ppermute | solution.py:484
  25.7 8.0 %collective-permute-start.4 = (bf16[64,2432]{1,0:T(8,128)(2,1)S(1)}, bf16[64,2432]{1,0:T(8,128)(2,1)S(1)}, u32[]{:S(2)}, u32[]{:S(2)}) collective-permute-start(bf16[64,2432]{1,0:T(8,128)(2,1)S(1)} %get-tuple-element.79), channel_id=1, source_target_pairs={{0,2},{2,0},{4,6},{6,4},{8,10},{10,8},{12,14},{14,12},{16,18},{18,... | collective-permute-start | bytes 933896 | tf_op jit(solution)/shard_map/ppermute | solution.py:484
  27.3 7.7 %collective-permute-start.5 = (bf16[64,2432]{1,0:T(8,128)(2,1)S(1)}, bf16[64,2432]{1,0:T(8,128)(2,1)S(1)}, u32[]{:S(2)}, u32[]{:S(2)}) collective-permute-start(bf16[64,2432]{1,0:T(8,128)(2,1)S(1)} %get-tuple-element.80), channel_id=1, source_target_pairs={{0,4},{2,6},{4,0},{6,2},{8,12},{10,14},{12,8},{14,10},{16,20},{18,... | collective-permute-start | bytes 933896 | tf_op jit(solution)/shard_map/ppermute | solution.py:484
  28.8 8.7 %collective-permute-start.6 = (bf16[64,2432]{1,0:T(8,128)(2,1)S(1)}, bf16[64,2432]{1,0:T(8,128)(2,1)S(1)}, u32[]{:S(2)}, u32[]{:S(2)}) collective-permute-start(bf16[64,2432]{1,0:T(8,128)(2,1)S(1)} %get-tuple-element.78.refs_0_.refs_4_), channel_id=1, source_target_pairs={{0,1},{1,0},{2,3},{3,2},{4,5},{5,4},{6,7},{7,6},{8,9},{9,8},{10,11... | collective-permute-start | bytes 933896 | tf_op jit(solution)/shard_map/ppermute | solution.py:481
  33.8 3.7 %collective-permute-start.7 = (bf16[64,2432]{1,0:T(8,128)(2,1)S(1)}, bf16[64,2432]{1,0:T(8,128)(2,1)S(1)}, u32[]{:S(2)}, u32[]{:S(2)}) collective-permute-start(bf16[64,2432]{1,0:T(8,128)(2,1)S(1)} %collective-permute-done.4.refs_1_.refs_5_), channel_id=1, source_target_pairs={{0,1},{1,0},{2,3},{3,2},{4,5},{5,4},{6,7},{7,6},{8,9},{9,8},{10,11... | collective-permute-start | bytes 933896 | tf_op jit(solution)/shard_map/ppermute | solution.py:481
  35.0 2.5 %collective-permute-start.8 = (bf16[64,2432]{1,0:T(8,128)(2,1)S(1)}, bf16[64,2432]{1,0:T(8,128)(2,1)S(1)}, u32[]{:S(2)}, u32[]{:S(2)}) collective-permute-start(bf16[64,2432]{1,0:T(8,128)(2,1)S(1)} %collective-permute-done.5.refs_2_.refs_6_), channel_id=1, source_target_pairs={{0,1},{1,0},{2,3},{3,2},{4,5},{5,4},{6,7},{7,6},{8,9},{9,8},{10,11... | collective-permute-start | bytes 933896 | tf_op jit(solution)/shard_map/ppermute | solution.py:481
  35.0 7.2 %collective-permute-start.12 = (bf16[32,2432]{1,0:T(8,128)(2,1)S(1)}, bf16[32,2432]{1,0:T(8,128)(2,1)S(1)}, u32[]{:S(2)}, u32[]{:S(2)}) collective-permute-start(bf16[32,2432]{1,0:T(8,128)(2,1)S(1)} %slice.8), channel_id=1, source_target_pairs={{0,4},{2,6},{4,0},{6,2},{8,12},{10,14},{12,8},{14,10},{16,20},{18,... | collective-permute-start | bytes 466952 | tf_op jit(solution)/shard_map/ppermute | solution.py:484
  36.6 6.2 %collective-permute-start.13 = (bf16[32,2432]{1,0:T(8,128)(2,1)S(1)}, bf16[32,2432]{1,0:T(8,128)(2,1)S(1)}, u32[]{:S(2)}, u32[]{:S(2)}) collective-permute-start(bf16[32,2432]{1,0:T(8,128)(2,1)S(1)} %slice.9), channel_id=1, source_target_pairs={{0,2},{2,0},{4,6},{6,4},{8,10},{10,8},{12,14},{14,12},{16,18},{18,... | collective-permute-start | bytes 466952 | tf_op jit(solution)/shard_map/ppermute | solution.py:484
  46.3 3.7 %collective-permute-start.19 = (bf16[64,2048]{1,0:T(8,128)(2,1)S(1)}, bf16[64,2048]{1,0:T(8,128)(2,1)S(1)}, u32[]{:S(2)}, u32[]{:S(2)}) collective-permute-start(bf16[64,2048]{1,0:T(8,128)(2,1)S(1)} %get-tuple-element.101), channel_id=1, source_target_pairs={{0,1},{1,0},{2,3},{3,2},{4,5},{5,4},{6,7},{7,6},{8,9},{9,8},{10,11... | collective-permute-start | bytes 786440 | tf_op jit(solution)/shard_map/ppermute | solution.py:481
  46.5 7.7 %collective-permute-start.16 = (bf16[192,512]{1,0:T(8,128)(2,1)S(1)}, bf16[192,512]{1,0:T(8,128)(2,1)S(1)}, u32[]{:S(2)}, u32[]{:S(2)}) collective-permute-start(bf16[192,512]{1,0:T(8,128)(2,1)S(1)} %get-tuple-element.93), channel_id=1, source_target_pairs={{0,2},{2,0},{4,6},{6,4},{8,10},{10,8},{12,14},{14,12},{16,18},{18,... | collective-permute-start | bytes 589832 | tf_op jit(solution)/shard_map/ppermute | solution.py:484
  47.8 13.2 %collective-permute-start.17 = (bf16[192,512]{1,0:T(8,128)(2,1)S(1)}, bf16[192,512]{1,0:T(8,128)(2,1)S(1)}, u32[]{:S(2)}, u32[]{:S(2)}) collective-permute-start(bf16[192,512]{1,0:T(8,128)(2,1)S(1)} %get-tuple-element.94), channel_id=1, source_target_pairs={{0,4},{2,6},{4,0},{6,2},{8,12},{10,14},{12,8},{14,10},{16,20},{18,... | collective-permute-start | bytes 589832 | tf_op jit(solution)/shard_map/ppermute | solution.py:484
  48.3 12.7 %collective-permute-start.18 = (bf16[192,512]{1,0:T(8,128)(2,1)S(1)}, bf16[192,512]{1,0:T(8,128)(2,1)S(1)}, u32[]{:S(2)}, u32[]{:S(2)}) collective-permute-start(bf16[192,512]{1,0:T(8,128)(2,1)S(1)} %get-tuple-element.95), channel_id=1, source_target_pairs={{0,6},{2,4},{4,2},{6,0},{8,14},{10,12},{12,10},{14,8},{16,22},{18,... | collective-permute-start | bytes 589832 | tf_op jit(solution)/shard_map/ppermute | solution.py:484
  50.1 10.9 %collective-permute-start.20 = (bf16[64,512]{1,0:T(8,128)(2,1)S(1)}, bf16[64,512]{1,0:T(8,128)(2,1)S(1)}, u32[]{:S(2)}, u32[]{:S(2)}) collective-permute-start(bf16[64,512]{1,0:T(8,128)(2,1)S(1)} %get-tuple-element.103), channel_id=1, source_target_pairs={{0,2},{2,0},{4,6},{6,4},{8,10},{10,8},{12,14},{14,12},{16,18},{18,... | collective-permute-start | bytes 196616 | tf_op jit(solution)/shard_map/ppermute | solution.py:484
  51.4 10.3 %collective-permute-start.21 = (bf16[64,512]{1,0:T(8,128)(2,1)S(1)}, bf16[64,512]{1,0:T(8,128)(2,1)S(1)}, u32[]{:S(2)}, u32[]{:S(2)}) collective-permute-start(bf16[64,512]{1,0:T(8,128)(2,1)S(1)} %get-tuple-element.104), channel_id=1, source_target_pairs={{0,4},{2,6},{4,0},{6,2},{8,12},{10,14},{12,8},{14,10},{16,20},{18,... | collective-permute-start | bytes 196616 | tf_op jit(solution)/shard_map/ppermute | solution.py:484
  54.3 7.4 %collective-permute-start.22 = (bf16[64,512]{1,0:T(8,128)(2,1)S(1)}, bf16[64,512]{1,0:T(8,128)(2,1)S(1)}, u32[]{:S(2)}, u32[]{:S(2)}) collective-permute-start(bf16[64,512]{1,0:T(8,128)(2,1)S(1)} %get-tuple-element.105), channel_id=1, source_target_pairs={{0,6},{2,4},{4,2},{6,0},{8,14},{10,12},{12,10},{14,8},{16,22},{18,... | collective-permute-start | bytes 196616 | tf_op jit(solution)/shard_map/ppermute | solution.py:484
  61.8 9.1 %collective-permute-start.23 = (bf16[64,512]{1,0:T(8,128)(2,1)S(1)}, bf16[64,512]{1,0:T(8,128)(2,1)S(1)}, u32[]{:S(2)}, u32[]{:S(2)}) collective-permute-start(bf16[64,512]{1,0:T(8,128)(2,1)S(1)} %get-tuple-element.107), channel_id=1, source_target_pairs={{0,8},{2,10},{4,12},{6,14},{8,0},{10,2},{12,4},{14,6},{16,24},{18,... | collective-permute-start | bytes 196616 | tf_op jit(solution)/shard_map/ppermute | solution.py:484
  64.4 11.5 %collective-permute-start.24 = (bf16[64,512]{1,0:T(8,128)(2,1)S(1)}, bf16[64,512]{1,0:T(8,128)(2,1)S(1)}, u32[]{:S(2)}, u32[]{:S(2)}) collective-permute-start(bf16[64,512]{1,0:T(8,128)(2,1)S(1)} %get-tuple-element.108), channel_id=1, source_target_pairs={{0,16},{2,18},{4,20},{6,22},{8,24},{10,26},{12,28},{14,30},{16,0},... | collective-permute-start | bytes 196616 | tf_op jit(solution)/shard_map/ppermute | solution.py:484
  65.1 10.7 %collective-permute-start.25 = (bf16[64,512]{1,0:T(8,128)(2,1)S(1)}, bf16[64,512]{1,0:T(8,128)(2,1)S(1)}, u32[]{:S(2)}, u32[]{:S(2)}) collective-permute-start(bf16[64,512]{1,0:T(8,128)(2,1)S(1)} %get-tuple-element.109), channel_id=1, source_target_pairs={{0,24},{2,26},{4,28},{6,30},{8,16},{10,18},{12,20},{14,22},{16,8},... | collective-permute-start | bytes 196616 | tf_op jit(solution)/shard_map/ppermute | solution.py:484
  79.6 7.6 %collective-permute-start.27 = (bf16[32,2944]{1,0:T(8,128)(2,1)S(1)}, bf16[32,2944]{1,0:T(8,128)(2,1)S(1)}, u32[]{:S(2)}, u32[]{:S(2)}) collective-permute-start(bf16[32,2944]{1,0:T(8,128)(2,1)S(1)} %get-tuple-element.114), channel_id=1, source_target_pairs={{0,2},{2,0},{4,6},{6,4},{8,10},{10,8},{12,14},{14,12},{16,18},{18,... | collective-permute-start | bytes 565256 | tf_op jit(solution)/shard_map/ppermute | solution.py:484
  80.6 10.5 %collective-permute-start.28 = (bf16[32,2944]{1,0:T(8,128)(2,1)S(1)}, bf16[32,2944]{1,0:T(8,128)(2,1)S(1)}, u32[]{:S(2)}, u32[]{:S(2)}) collective-permute-start(bf16[32,2944]{1,0:T(8,128)(2,1)S(1)} %get-tuple-element.115), channel_id=1, source_target_pairs={{0,4},{2,6},{4,0},{6,2},{8,12},{10,14},{12,8},{14,10},{16,20},{18,... | collective-permute-start | bytes 565256 | tf_op jit(solution)/shard_map/ppermute | solution.py:484
  82.2 9.0 %collective-permute-start.29 = (bf16[32,2944]{1,0:T(8,128)(2,1)S(1)}, bf16[32,2944]{1,0:T(8,128)(2,1)S(1)}, u32[]{:S(2)}, u32[]{:S(2)}) collective-permute-start(bf16[32,2944]{1,0:T(8,128)(2,1)S(1)} %get-tuple-element.116), channel_id=1, source_target_pairs={{0,6},{2,4},{4,2},{6,0},{8,14},{10,12},{12,10},{14,8},{16,22},{18,... | collective-permute-start | bytes 565256 | tf_op jit(solution)/shard_map/ppermute | solution.py:484
  (16 other events, 169.7 us)
Sparse Core Ops, SparseCore 0:
  14.3 62.2 all-gather.1

commit v9 on v8

--- a/solution.py
+++ b/solution.py
@@ -347,13 +347,15 @@
     )(*parts, *packed, gain)
 
 
-def projection_kernel(chunk, mine_ref, theirs_ref, next_ref, w_hbm, *refs):
-    out_refs, (w_buf, sems) = refs[:PLANE], refs[PLANE:]
+def projection_kernel(chunk, mine_ref, theirs_ref, next_ref, *refs):
+    halves, out_refs, (w_buf, sems) = refs[:2], refs[2 : 2 + PLANE], refs[2 + PLANE :]
     cols = w_buf.shape[1]
     copies = []
+    piece = w_buf.shape[0] // sems.shape[0]
     for i in range(sems.shape[0]):
-        at = lanes(i * META, META)
-        copies.append(pltpu.make_async_copy(w_hbm.at[at], w_buf.at[at], sems.at[i]))
+        source = halves[i % 2].at[pl.ds(i // 2 * piece, piece)]
+        target = w_buf.at[pl.ds(i * piece, piece)]
+        copies.append(pltpu.make_async_copy(source, target, sems.at[i]))
     for copy in copies:
         copy.start()
     rows, extended = mine_ref.shape
@@ -381,24 +383,24 @@
             out_refs[d][other, at] = product[rows + d * block : rows + (d + 1) * block]
 
 
-def projection(mine, theirs, following, weight):
+def projection(mine, theirs, following, weight, depth):
     rows, part = following.shape
-    cols = weight.shape[1]
+    cols = weight[0].shape[1]
     chunk = 512
     shape = pltpu.VMEM((2 * rows // PLANE, cols + META + part // 2), jnp.bfloat16)
     return pl.pallas_call(
         functools.partial(projection_kernel, chunk),
         out_shape=(shape,) * PLANE,
-        in_specs=[VMEM] * 3 + [HBM],
+        in_specs=[VMEM] * 3 + [HBM] * 2,
         out_specs=(VMEM,) * PLANE,
         scratch_shapes=[
             pltpu.VMEM((part, cols), jnp.bfloat16),
-            pltpu.SemaphoreType.DMA((part // META,)),
+            pltpu.SemaphoreType.DMA((2 * depth,)),
         ],
         compiler_params=params(8),
         cost_estimate=SMALL,
         name="qkv_projection",
-    )(mine, theirs, following, in_hbm(weight))
+    )(mine, theirs, following, *map(in_hbm, weight))
 
 
 def head_norm_kernel(depth, *refs):
@@ -499,12 +501,19 @@
     lines = [list(range(i, n_expert, PLANE)) for i in range(PLANE)]
     mine, theirs = out_projection(attn_out, out_weight)
     mine, q_own, kv_own = lax.optimization_barrier((mine, q_weight, kv_weight))
-    joined = jnp.concatenate([q_own, kv_own], axis=1)
+    middle = q_own.shape[0] // 2
+    joined = [
+        jnp.concatenate([q_own[at], kv_own[at]], axis=1)
+        for at in (slice(None, middle), slice(middle, None))
+    ]
     tokens, *firsts = first_norm(
         (mine,), (to_core(theirs),), residual, attn_gain[None, :], meta, depth
     )
-    tokens, joined = lax.optimization_barrier((tokens, joined))
-    qkv = lax.all_gather(joined, "expert", axis=0, tiled=True, axis_index_groups=lines)
+    tokens, *joined = lax.optimization_barrier((tokens, *joined))
+    qkv = [
+        lax.all_gather(rows, "expert", axis=0, tiled=True, axis_index_groups=lines)
+        for rows in joined
+    ]
     weights = load((w_gate, w_up, w_down), (tokens,))
     line = to_z([tokens] * depth)
     *line, gate, up, down = lax.optimization_barrier((*line, *weights))
@@ -522,7 +531,7 @@
     far_sum = chip_sum(mine, list(map(to_core, theirs)))
     parts = plane_sum(to_plane(near_sum), to_plane(far_sum), depth)
     scaled, following = second_norm(to_z(parts), (*near, *far), input_gain[None, :])
-    products = to_plane(projection(scaled, to_core(scaled), following, qkv))
+    products = to_plane(projection(scaled, to_core(scaled), following, qkv, depth))
     return head_norm(
         products,
         q_gain[None, :],

time: 99.1 us -> 111 us (1.12)
  waiting for transfers between devices: 37 us -> 48 us
    all_gather x1 -> x2, waiting for transfers between devices: 0.01 us -> 10 us  [per_device_dense(): lax.all_gather(rows, 'expert', axis=0, tiled=True, axis_index_groups=lines)]
  transfers between devices with their start and end apart: 31 -> 32, of which waited for: 17 -> 19; matrix products, arithmetic and copies ran while one was open for 1% -> 1% of each run, Pallas kernels for 11% -> 9%
where the time goes in v9:
time: 111 us
  waiting for transfers between devices  48 us (43%)
  starting transfers between devices  28.4 us (26%)
  Pallas kernels  18.6 us (17%)
  between operations  14.3 us (13%)
    ppermute x19, waiting for transfers between devices, to_expert(): lax.ppermute(value, 'expert', [(i, i ^ offset) for i in range(n_expert)])  34.6 us
    ppermute x19, starting transfers between devices, to_expert(): lax.ppermute(value, 'expert', [(i, i ^ offset) for i in range(n_expert)])  26.4 us
    all_gather x2, waiting for transfers between devices, per_device_dense(): lax.all_gather(rows, 'expert', axis=0, tiled=True, axis_index_groups=lines)  10 us
    pallas_call x2, Pallas kernels, experts(): pl.pallas_call(functools.partial(expert_kernel, depth, chunk, len(blocks)...  6.04 us
    pallas_call x1, Pallas kernels, out_projection(): pl.pallas_call(functools.partial(out_projection_kernel, chunk), out_shape...  4.83 us
    pallas_call x1, Pallas kernels, load(): pl.pallas_call(load_kernel, out_shape=tuple((pltpu.VMEM(w.shape, w.dtype)...  3.88 us
    ppermute x11, waiting for transfers between devices, to_core(): return lax.ppermute(value, 'tensor', [(0, 1), (1, 0)])  2.59 us
    pallas_call x1, Pallas kernels, projection(): pl.pallas_call(functools.partial(projection_kernel, chunk), out_shape=(sh...  2.24 us
  transfers between devices with their start and end apart: 32, of which 19 were waited for; matrix products, arithmetic and copies ran while one was open for 1% of the time, Pallas kernels for 9%

profile of v9, /device:TPU:0, one launch (start us, length us, event | category | flops | bytes accessed | tf_op | source)
XLA Modules:
  0.0 110.7 jit_solution(14211584159082710647)
XLA Ops:
  7.3 4.8 %out_projection.1 = (f32[16,2048]{1,0:T(8,128)S(1)}, f32[16,2048]{1,0:T(8,128)S(1)}) custom-call(bf16[32,2048]{1,0:T(8,128)(2,1)} %a_hbm.1, bf16[2048,2048]{1,0:T(8,128)(2,1)} %w_hbm.1), custom_call_target="tpu_custom_call" | custom-call | tf_op jit(solution)/shard_map/out_projection/pallas_call | solution.py:77
  15.0 2.7 %collective-permute-start.1 = (bf16[16,2176]{1,0:T(8,128)(2,1)S(1)}, bf16[16,2176]{1,0:T(8,128)(2,1)S(1)}, u32[]{:S(2)}, u32[]{:S(2)}) collective-permute-start(bf16[16,2176]{1,0:T(8,128)(2,1)S(1)} %get-tuple-element.71.refs_3_.refs_0_), channel_id=1, source_target_pairs={{0,8},{2,10},{4,12},{6,14},{8,0},{10,2},{12,4},{14,6},{16,24},{18,... | collective-permute-start | bytes 208904 | tf_op jit(solution)/shard_map/ppermute | solution.py:486
  17.7 2.6 %collective-permute-start.2 = (bf16[16,2176]{1,0:T(8,128)(2,1)S(1)}, bf16[16,2176]{1,0:T(8,128)(2,1)S(1)}, u32[]{:S(2)}, u32[]{:S(2)}) collective-permute-start(bf16[16,2176]{1,0:T(8,128)(2,1)S(1)} %get-tuple-element.71.refs_3_.refs_0_), channel_id=1, source_target_pairs={{0,16},{2,18},{4,20},{6,22},{8,24},{10,26},{12,28},{14,30},{16,0},... | collective-permute-start | bytes 208904 | tf_op jit(solution)/shard_map/ppermute | solution.py:486
  20.3 3.9 %load_weights.1 = (bf16[1,2048,768]{2,1,0:T(8,128)(2,1)S(1)}, bf16[1,2048,768]{2,1,0:T(8,128)(2,1)S(1)}, bf16[1,768,2048]{2,1,0:T(8,128)(2,1)S(1)}) custom-call(bf16[1,2048,768]{2,1,0:T(8,128)(2,1)} %refs_0_.1, bf16[1,2048,768]{2,1,0:T(8,128)(2,1)} %refs_1_.1, bf16[1,768,2048]{2,1,0:T(8,128)(2,1)} %refs_2_.3, ...), custom_call_target="tpu_custom_call" | custom-call | tf_op jit(solution)/shard_map/load_weights/pallas_call | solution.py:171
  26.5 1.6 %collective-permute-start.4 = (bf16[64,2432]{1,0:T(8,128)(2,1)S(1)}, bf16[64,2432]{1,0:T(8,128)(2,1)S(1)}, u32[]{:S(2)}, u32[]{:S(2)}) collective-permute-start(bf16[64,2432]{1,0:T(8,128)(2,1)S(1)} %get-tuple-element.80), channel_id=1, source_target_pairs={{0,2},{2,0},{4,6},{6,4},{8,10},{10,8},{12,14},{14,12},{16,18},{18,... | collective-permute-start | bytes 933896 | tf_op jit(solution)/shard_map/ppermute | solution.py:486
  28.1 1.5 %collective-permute-start.5 = (bf16[64,2432]{1,0:T(8,128)(2,1)S(1)}, bf16[64,2432]{1,0:T(8,128)(2,1)S(1)}, u32[]{:S(2)}, u32[]{:S(2)}) collective-permute-start(bf16[64,2432]{1,0:T(8,128)(2,1)S(1)} %get-tuple-element.81), channel_id=1, source_target_pairs={{0,4},{2,6},{4,0},{6,2},{8,12},{10,14},{12,8},{14,10},{16,20},{18,... | collective-permute-start | bytes 933896 | tf_op jit(solution)/shard_map/ppermute | solution.py:486
  29.6 5.0 %collective-permute-done.4.refs_1_.refs_5_ = bf16[64,2432]{1,0:T(8,128)(2,1)S(1)} collective-permute-done((bf16[64,2432]{1,0:T(8,128)(2,1)S(1)}, bf16[64,2432]{1,0:T(8,128)(2,1)S(1)}, u32[]{:S(2)}, u32[]{:S(2)}) %collective-permute-start.4) | collective-permute-done | bytes 311328 | tf_op jit(solution)/shard_map/ppermute | solution.py:486
  35.8 1.6 %collective-permute-start.12 = (bf16[32,2432]{1,0:T(8,128)(2,1)S(1)}, bf16[32,2432]{1,0:T(8,128)(2,1)S(1)}, u32[]{:S(2)}, u32[]{:S(2)}) collective-permute-start(bf16[32,2432]{1,0:T(8,128)(2,1)S(1)} %slice.24), channel_id=1, source_target_pairs={{0,4},{2,6},{4,0},{6,2},{8,12},{10,14},{12,8},{14,10},{16,20},{18,... | collective-permute-start | bytes 466952 | tf_op jit(solution)/shard_map/ppermute | solution.py:486
  38.3 4.0 %experts.2 = (bf16[192,2048]{1,0:T(8,128)(2,1)S(1)}, bf16[64,2048]{1,0:T(8,128)(2,1)S(1)}, bf16[64,2048]{1,0:T(8,128)(2,1)S(1)}, bf16[64,2048]{1,0:T(8,128)(2,1)S(1)}) custom-call(bf16[64,2432]{1,0:T(8,128)(2,1)S(1)} %get-tuple-element.79.refs_0_.refs_4_, bf16[64,2432]{1,0:T(8,128)(2,1)S(1)} %collective-permute-done.4.refs_1_.refs_5_, ...), custom_call_target="tpu_custom_call" | custom-call | flops 3623878656 | tf_op jit(solution)/shard_map/experts/pallas_call | solution.py:231
  45.1 2.0 %experts.3 = (bf16[64,2048]{1,0:T(8,128)(2,1)S(1)}, bf16[64,2048]{1,0:T(8,128)(2,1)S(1)}) custom-call(bf16[32,2432]{1,0:T(8,128)(2,1)S(1)} %collective-permute-done.12.refs_0_.refs_7_, bf16[32,2432]{1,0:T(8,128)(2,1)S(1)} %collective-permute-done.13.refs_1_.refs_8_, bf16[32,2432]{1,0:T(8,128)(2,1)S(1)} %collective-permute-done.14.refs_2_, ...), custom_call_target="tpu_custom_call" | custom-call | flops 1207959552 | tf_op jit(solution)/shard_map/experts/pallas_call | solution.py:231
  49.1 1.7 %collective-permute-start.18 = (bf16[192,512]{1,0:T(8,128)(2,1)S(1)}, bf16[192,512]{1,0:T(8,128)(2,1)S(1)}, u32[]{:S(2)}, u32[]{:S(2)}) collective-permute-start(bf16[192,512]{1,0:T(8,128)(2,1)S(1)} %get-tuple-element.96), channel_id=1, source_target_pairs={{0,6},{2,4},{4,2},{6,0},{8,14},{10,12},{12,10},{14,8},{16,22},{18,... | collective-permute-start | bytes 589832 | tf_op jit(solution)/shard_map/ppermute | solution.py:486
  52.8 2.3 %collective-permute-done.16.refs_1_ = bf16[192,512]{1,0:T(8,128)(2,1)S(1)} collective-permute-done((bf16[192,512]{1,0:T(8,128)(2,1)S(1)}, bf16[192,512]{1,0:T(8,128)(2,1)S(1)}, u32[]{:S(2)}, u32[]{:S(2)}) %collective-permute-start.16) | collective-permute-done | bytes 196640 | tf_op jit(solution)/shard_map/ppermute | solution.py:486
  56.3 5.5 %collective-permute-done.17.refs_2_ = bf16[192,512]{1,0:T(8,128)(2,1)S(1)} collective-permute-done((bf16[192,512]{1,0:T(8,128)(2,1)S(1)}, bf16[192,512]{1,0:T(8,128)(2,1)S(1)}, u32[]{:S(2)}, u32[]{:S(2)}) %collective-permute-start.17) | collective-permute-done | bytes 196640 | tf_op jit(solution)/shard_map/ppermute | solution.py:486
  62.7 2.5 %collective-permute-start.23 = (bf16[64,512]{1,0:T(8,128)(2,1)S(1)}, bf16[64,512]{1,0:T(8,128)(2,1)S(1)}, u32[]{:S(2)}, u32[]{:S(2)}) collective-permute-start(bf16[64,512]{1,0:T(8,128)(2,1)S(1)} %get-tuple-element.108), channel_id=1, source_target_pairs={{0,8},{2,10},{4,12},{6,14},{8,0},{10,2},{12,4},{14,6},{16,24},{18,... | collective-permute-start | bytes 196616 | tf_op jit(solution)/shard_map/ppermute | solution.py:486
  65.2 1.6 %collective-permute-start.24 = (bf16[64,512]{1,0:T(8,128)(2,1)S(1)}, bf16[64,512]{1,0:T(8,128)(2,1)S(1)}, u32[]{:S(2)}, u32[]{:S(2)}) collective-permute-start(bf16[64,512]{1,0:T(8,128)(2,1)S(1)} %get-tuple-element.109), channel_id=1, source_target_pairs={{0,16},{2,18},{4,20},{6,22},{8,24},{10,26},{12,28},{14,30},{16,0},... | collective-permute-start | bytes 196616 | tf_op jit(solution)/shard_map/ppermute | solution.py:486
  66.8 1.4 %collective-permute-start.25 = (bf16[64,512]{1,0:T(8,128)(2,1)S(1)}, bf16[64,512]{1,0:T(8,128)(2,1)S(1)}, u32[]{:S(2)}, u32[]{:S(2)}) collective-permute-start(bf16[64,512]{1,0:T(8,128)(2,1)S(1)} %get-tuple-element.110), channel_id=1, source_target_pairs={{0,24},{2,26},{4,28},{6,30},{8,16},{10,18},{12,20},{14,22},{16,8},... | collective-permute-start | bytes 196616 | tf_op jit(solution)/shard_map/ppermute | solution.py:486
  68.2 3.8 %collective-permute-done.23.refs_1_ = bf16[64,512]{1,0:T(8,128)(2,1)S(1)} collective-permute-done((bf16[64,512]{1,0:T(8,128)(2,1)S(1)}, bf16[64,512]{1,0:T(8,128)(2,1)S(1)}, u32[]{:S(2)}, u32[]{:S(2)}) %collective-permute-start.23) | collective-permute-done | bytes 65568 | tf_op jit(solution)/shard_map/ppermute | solution.py:486
  72.0 4.8 %collective-permute-done.24.refs_2_ = bf16[64,512]{1,0:T(8,128)(2,1)S(1)} collective-permute-done((bf16[64,512]{1,0:T(8,128)(2,1)S(1)}, bf16[64,512]{1,0:T(8,128)(2,1)S(1)}, u32[]{:S(2)}, u32[]{:S(2)}) %collective-permute-start.24) | collective-permute-done | bytes 65568 | tf_op jit(solution)/shard_map/ppermute | solution.py:486
  78.9 10.0 %all-gather.5.cloned.1.call-done.refs_1_ = bf16[256,2560]{1,0:T(8,128)(2,1)} async-done(((bf16[64,2560]{1,0:T(8,128)(2,1)}), bf16[256,2560]{1,0:T(8,128)(2,1)}) %all-gather.5.cloned.1.call-update) | async-done | bytes 1310736 | tf_op jit(solution)/shard_map/all_gather | solution.py:514
  88.9 2.2 %qkv_projection.1 = (bf16[32,2944]{1,0:T(8,128)(2,1)S(1)}, bf16[32,2944]{1,0:T(8,128)(2,1)S(1)}, bf16[32,2944]{1,0:T(8,128)(2,1)S(1)}, bf16[32,2944]{1,0:T(8,128)(2,1)S(1)}) custom-call(bf16[64,640]{1,0:T(8,128)(2,1)S(1)} %get-tuple-element.111.mine_ref, bf16[64,640]{1,0:T(8,128)(2,1)S(1)} %collective-permute-done.26.theirs_ref, ...), custom_call_target="tpu_custom_call" | custom-call | tf_op jit(solution)/shard_map/qkv_projection/pallas_call | solution.py:391
  91.2 1.5 %collective-permute-start.27 = (bf16[32,2944]{1,0:T(8,128)(2,1)S(1)}, bf16[32,2944]{1,0:T(8,128)(2,1)S(1)}, u32[]{:S(2)}, u32[]{:S(2)}) collective-permute-start(bf16[32,2944]{1,0:T(8,128)(2,1)S(1)} %get-tuple-element.116), channel_id=1, source_target_pairs={{0,2},{2,0},{4,6},{6,4},{8,10},{10,8},{12,14},{14,12},{16,18},{18,... | collective-permute-start | bytes 565256 | tf_op jit(solution)/shard_map/ppermute | solution.py:486
  92.7 1.5 %collective-permute-start.28 = (bf16[32,2944]{1,0:T(8,128)(2,1)S(1)}, bf16[32,2944]{1,0:T(8,128)(2,1)S(1)}, u32[]{:S(2)}, u32[]{:S(2)}) collective-permute-start(bf16[32,2944]{1,0:T(8,128)(2,1)S(1)} %get-tuple-element.117), channel_id=1, source_target_pairs={{0,4},{2,6},{4,0},{6,2},{8,12},{10,14},{12,8},{14,10},{16,20},{18,... | collective-permute-start | bytes 565256 | tf_op jit(solution)/shard_map/ppermute | solution.py:486
  94.7 4.1 %collective-permute-done.27.refs_1_ = bf16[32,2944]{1,0:T(8,128)(2,1)S(1)} collective-permute-done((bf16[32,2944]{1,0:T(8,128)(2,1)S(1)}, bf16[32,2944]{1,0:T(8,128)(2,1)S(1)}, u32[]{:S(2)}, u32[]{:S(2)}) %collective-permute-start.27) | collective-permute-done | bytes 188448 | tf_op jit(solution)/shard_map/ppermute | solution.py:486
  98.9 4.1 %collective-permute-done.28.refs_2_ = bf16[32,2944]{1,0:T(8,128)(2,1)S(1)} collective-permute-done((bf16[32,2944]{1,0:T(8,128)(2,1)S(1)}, bf16[32,2944]{1,0:T(8,128)(2,1)S(1)}, u32[]{:S(2)}, u32[]{:S(2)}) %collective-permute-start.28) | collective-permute-done | bytes 188448 | tf_op jit(solution)/shard_map/ppermute | solution.py:486
  (84 shorter events, 19.6 us)
Async XLA Ops:
  7.2 71.7 %all-gather.3.cloned.1.call-start = ((), (), s32[]{:S(2)}) async-start(), calls=%async_computation | async-start | bytes 1638400 | tf_op jit(solution)/shard_map/all_gather | solution.py:514
  14.3 74.7 %all-gather.5.cloned.1.call-start = ((), (), s32[]{:S(2)}) async-start(), calls=%async_computation.1 | async-start | bytes 1638400 | tf_op jit(solution)/shard_map/all_gather | solution.py:514
  15.0 9.2 %collective-permute-start.1 = (bf16[16,2176]{1,0:T(8,128)(2,1)S(1)}, bf16[16,2176]{1,0:T(8,128)(2,1)S(1)}, u32[]{:S(2)}, u32[]{:S(2)}) collective-permute-start(bf16[16,2176]{1,0:T(8,128)(2,1)S(1)} %get-tuple-element.71.refs_3_.refs_0_), channel_id=1, source_target_pairs={{0,8},{2,10},{4,12},{6,14},{8,0},{10,2},{12,4},{14,6},{16,24},{18,... | collective-permute-start | bytes 208904 | tf_op jit(solution)/shard_map/ppermute | solution.py:486
  17.7 7.9 %collective-permute-start.2 = (bf16[16,2176]{1,0:T(8,128)(2,1)S(1)}, bf16[16,2176]{1,0:T(8,128)(2,1)S(1)}, u32[]{:S(2)}, u32[]{:S(2)}) collective-permute-start(bf16[16,2176]{1,0:T(8,128)(2,1)S(1)} %get-tuple-element.71.refs_3_.refs_0_), channel_id=1, source_target_pairs={{0,16},{2,18},{4,20},{6,22},{8,24},{10,26},{12,28},{14,30},{16,0},... | collective-permute-start | bytes 208904 | tf_op jit(solution)/shard_map/ppermute | solution.py:486
  20.3 6.2 %collective-permute-start.3 = (bf16[16,2176]{1,0:T(8,128)(2,1)S(1)}, bf16[16,2176]{1,0:T(8,128)(2,1)S(1)}, u32[]{:S(2)}, u32[]{:S(2)}) collective-permute-start(bf16[16,2176]{1,0:T(8,128)(2,1)S(1)} %get-tuple-element.71.refs_3_.refs_0_), channel_id=1, source_target_pairs={{0,24},{2,26},{4,28},{6,30},{8,16},{10,18},{12,20},{14,22},{16,8},... | collective-permute-start | bytes 208904 | tf_op jit(solution)/shard_map/ppermute | solution.py:486
  26.5 8.0 %collective-permute-start.4 = (bf16[64,2432]{1,0:T(8,128)(2,1)S(1)}, bf16[64,2432]{1,0:T(8,128)(2,1)S(1)}, u32[]{:S(2)}, u32[]{:S(2)}) collective-permute-start(bf16[64,2432]{1,0:T(8,128)(2,1)S(1)} %get-tuple-element.80), channel_id=1, source_target_pairs={{0,2},{2,0},{4,6},{6,4},{8,10},{10,8},{12,14},{14,12},{16,18},{18,... | collective-permute-start | bytes 933896 | tf_op jit(solution)/shard_map/ppermute | solution.py:486
  28.1 7.7 %collective-permute-start.5 = (bf16[64,2432]{1,0:T(8,128)(2,1)S(1)}, bf16[64,2432]{1,0:T(8,128)(2,1)S(1)}, u32[]{:S(2)}, u32[]{:S(2)}) collective-permute-start(bf16[64,2432]{1,0:T(8,128)(2,1)S(1)} %get-tuple-element.81), channel_id=1, source_target_pairs={{0,4},{2,6},{4,0},{6,2},{8,12},{10,14},{12,8},{14,10},{16,20},{18,... | collective-permute-start | bytes 933896 | tf_op jit(solution)/shard_map/ppermute | solution.py:486
  29.6 8.7 %collective-permute-start.6 = (bf16[64,2432]{1,0:T(8,128)(2,1)S(1)}, bf16[64,2432]{1,0:T(8,128)(2,1)S(1)}, u32[]{:S(2)}, u32[]{:S(2)}) collective-permute-start(bf16[64,2432]{1,0:T(8,128)(2,1)S(1)} %get-tuple-element.79.refs_0_.refs_4_), channel_id=1, source_target_pairs={{0,1},{1,0},{2,3},{3,2},{4,5},{5,4},{6,7},{7,6},{8,9},{9,8},{10,11... | collective-permute-start | bytes 933896 | tf_op jit(solution)/shard_map/ppermute | solution.py:483
  34.6 3.7 %collective-permute-start.7 = (bf16[64,2432]{1,0:T(8,128)(2,1)S(1)}, bf16[64,2432]{1,0:T(8,128)(2,1)S(1)}, u32[]{:S(2)}, u32[]{:S(2)}) collective-permute-start(bf16[64,2432]{1,0:T(8,128)(2,1)S(1)} %collective-permute-done.4.refs_1_.refs_5_), channel_id=1, source_target_pairs={{0,1},{1,0},{2,3},{3,2},{4,5},{5,4},{6,7},{7,6},{8,9},{9,8},{10,11... | collective-permute-start | bytes 933896 | tf_op jit(solution)/shard_map/ppermute | solution.py:483
  35.8 7.2 %collective-permute-start.12 = (bf16[32,2432]{1,0:T(8,128)(2,1)S(1)}, bf16[32,2432]{1,0:T(8,128)(2,1)S(1)}, u32[]{:S(2)}, u32[]{:S(2)}) collective-permute-start(bf16[32,2432]{1,0:T(8,128)(2,1)S(1)} %slice.24), channel_id=1, source_target_pairs={{0,4},{2,6},{4,0},{6,2},{8,12},{10,14},{12,8},{14,10},{16,20},{18,... | collective-permute-start | bytes 466952 | tf_op jit(solution)/shard_map/ppermute | solution.py:486
  37.4 6.2 %collective-permute-start.13 = (bf16[32,2432]{1,0:T(8,128)(2,1)S(1)}, bf16[32,2432]{1,0:T(8,128)(2,1)S(1)}, u32[]{:S(2)}, u32[]{:S(2)}) collective-permute-start(bf16[32,2432]{1,0:T(8,128)(2,1)S(1)} %slice.25), channel_id=1, source_target_pairs={{0,2},{2,0},{4,6},{6,4},{8,10},{10,8},{12,14},{14,12},{16,18},{18,... | collective-permute-start | bytes 466952 | tf_op jit(solution)/shard_map/ppermute | solution.py:486
  47.2 3.7 %collective-permute-start.19 = (bf16[64,2048]{1,0:T(8,128)(2,1)S(1)}, bf16[64,2048]{1,0:T(8,128)(2,1)S(1)}, u32[]{:S(2)}, u32[]{:S(2)}) collective-permute-start(bf16[64,2048]{1,0:T(8,128)(2,1)S(1)} %get-tuple-element.102), channel_id=1, source_target_pairs={{0,1},{1,0},{2,3},{3,2},{4,5},{5,4},{6,7},{7,6},{8,9},{9,8},{10,11... | collective-permute-start | bytes 786440 | tf_op jit(solution)/shard_map/ppermute | solution.py:483
  47.4 7.7 %collective-permute-start.16 = (bf16[192,512]{1,0:T(8,128)(2,1)S(1)}, bf16[192,512]{1,0:T(8,128)(2,1)S(1)}, u32[]{:S(2)}, u32[]{:S(2)}) collective-permute-start(bf16[192,512]{1,0:T(8,128)(2,1)S(1)} %get-tuple-element.94), channel_id=1, source_target_pairs={{0,2},{2,0},{4,6},{6,4},{8,10},{10,8},{12,14},{14,12},{16,18},{18,... | collective-permute-start | bytes 589832 | tf_op jit(solution)/shard_map/ppermute | solution.py:486
  48.6 13.2 %collective-permute-start.17 = (bf16[192,512]{1,0:T(8,128)(2,1)S(1)}, bf16[192,512]{1,0:T(8,128)(2,1)S(1)}, u32[]{:S(2)}, u32[]{:S(2)}) collective-permute-start(bf16[192,512]{1,0:T(8,128)(2,1)S(1)} %get-tuple-element.95), channel_id=1, source_target_pairs={{0,4},{2,6},{4,0},{6,2},{8,12},{10,14},{12,8},{14,10},{16,20},{18,... | collective-permute-start | bytes 589832 | tf_op jit(solution)/shard_map/ppermute | solution.py:486
  49.1 12.7 %collective-permute-start.18 = (bf16[192,512]{1,0:T(8,128)(2,1)S(1)}, bf16[192,512]{1,0:T(8,128)(2,1)S(1)}, u32[]{:S(2)}, u32[]{:S(2)}) collective-permute-start(bf16[192,512]{1,0:T(8,128)(2,1)S(1)} %get-tuple-element.96), channel_id=1, source_target_pairs={{0,6},{2,4},{4,2},{6,0},{8,14},{10,12},{12,10},{14,8},{16,22},{18,... | collective-permute-start | bytes 589832 | tf_op jit(solution)/shard_map/ppermute | solution.py:486
  50.9 10.9 %collective-permute-start.20 = (bf16[64,512]{1,0:T(8,128)(2,1)S(1)}, bf16[64,512]{1,0:T(8,128)(2,1)S(1)}, u32[]{:S(2)}, u32[]{:S(2)}) collective-permute-start(bf16[64,512]{1,0:T(8,128)(2,1)S(1)} %get-tuple-element.104), channel_id=1, source_target_pairs={{0,2},{2,0},{4,6},{6,4},{8,10},{10,8},{12,14},{14,12},{16,18},{18,... | collective-permute-start | bytes 196616 | tf_op jit(solution)/shard_map/ppermute | solution.py:486
  52.2 10.3 %collective-permute-start.21 = (bf16[64,512]{1,0:T(8,128)(2,1)S(1)}, bf16[64,512]{1,0:T(8,128)(2,1)S(1)}, u32[]{:S(2)}, u32[]{:S(2)}) collective-permute-start(bf16[64,512]{1,0:T(8,128)(2,1)S(1)} %get-tuple-element.105), channel_id=1, source_target_pairs={{0,4},{2,6},{4,0},{6,2},{8,12},{10,14},{12,8},{14,10},{16,20},{18,... | collective-permute-start | bytes 196616 | tf_op jit(solution)/shard_map/ppermute | solution.py:486
  55.1 7.4 %collective-permute-start.22 = (bf16[64,512]{1,0:T(8,128)(2,1)S(1)}, bf16[64,512]{1,0:T(8,128)(2,1)S(1)}, u32[]{:S(2)}, u32[]{:S(2)}) collective-permute-start(bf16[64,512]{1,0:T(8,128)(2,1)S(1)} %get-tuple-element.106), channel_id=1, source_target_pairs={{0,6},{2,4},{4,2},{6,0},{8,14},{10,12},{12,10},{14,8},{16,22},{18,... | collective-permute-start | bytes 196616 | tf_op jit(solution)/shard_map/ppermute | solution.py:486
  62.7 9.4 %collective-permute-start.23 = (bf16[64,512]{1,0:T(8,128)(2,1)S(1)}, bf16[64,512]{1,0:T(8,128)(2,1)S(1)}, u32[]{:S(2)}, u32[]{:S(2)}) collective-permute-start(bf16[64,512]{1,0:T(8,128)(2,1)S(1)} %get-tuple-element.108), channel_id=1, source_target_pairs={{0,8},{2,10},{4,12},{6,14},{8,0},{10,2},{12,4},{14,6},{16,24},{18,... | collective-permute-start | bytes 196616 | tf_op jit(solution)/shard_map/ppermute | solution.py:486
  65.2 11.6 %collective-permute-start.24 = (bf16[64,512]{1,0:T(8,128)(2,1)S(1)}, bf16[64,512]{1,0:T(8,128)(2,1)S(1)}, u32[]{:S(2)}, u32[]{:S(2)}) collective-permute-start(bf16[64,512]{1,0:T(8,128)(2,1)S(1)} %get-tuple-element.109), channel_id=1, source_target_pairs={{0,16},{2,18},{4,20},{6,22},{8,24},{10,26},{12,28},{14,30},{16,0},... | collective-permute-start | bytes 196616 | tf_op jit(solution)/shard_map/ppermute | solution.py:486
  66.8 10.6 %collective-permute-start.25 = (bf16[64,512]{1,0:T(8,128)(2,1)S(1)}, bf16[64,512]{1,0:T(8,128)(2,1)S(1)}, u32[]{:S(2)}, u32[]{:S(2)}) collective-permute-start(bf16[64,512]{1,0:T(8,128)(2,1)S(1)} %get-tuple-element.110), channel_id=1, source_target_pairs={{0,24},{2,26},{4,28},{6,30},{8,16},{10,18},{12,20},{14,22},{16,8},... | collective-permute-start | bytes 196616 | tf_op jit(solution)/shard_map/ppermute | solution.py:486
  91.2 7.7 %collective-permute-start.27 = (bf16[32,2944]{1,0:T(8,128)(2,1)S(1)}, bf16[32,2944]{1,0:T(8,128)(2,1)S(1)}, u32[]{:S(2)}, u32[]{:S(2)}) collective-permute-start(bf16[32,2944]{1,0:T(8,128)(2,1)S(1)} %get-tuple-element.116), channel_id=1, source_target_pairs={{0,2},{2,0},{4,6},{6,4},{8,10},{10,8},{12,14},{14,12},{16,18},{18,... | collective-permute-start | bytes 565256 | tf_op jit(solution)/shard_map/ppermute | solution.py:486
  92.7 10.2 %collective-permute-start.28 = (bf16[32,2944]{1,0:T(8,128)(2,1)S(1)}, bf16[32,2944]{1,0:T(8,128)(2,1)S(1)}, u32[]{:S(2)}, u32[]{:S(2)}) collective-permute-start(bf16[32,2944]{1,0:T(8,128)(2,1)S(1)} %get-tuple-element.117), channel_id=1, source_target_pairs={{0,4},{2,6},{4,0},{6,2},{8,12},{10,14},{12,8},{14,10},{16,20},{18,... | collective-permute-start | bytes 565256 | tf_op jit(solution)/shard_map/ppermute | solution.py:486
  94.2 8.8 %collective-permute-start.29 = (bf16[32,2944]{1,0:T(8,128)(2,1)S(1)}, bf16[32,2944]{1,0:T(8,128)(2,1)S(1)}, u32[]{:S(2)}, u32[]{:S(2)}) collective-permute-start(bf16[32,2944]{1,0:T(8,128)(2,1)S(1)} %get-tuple-element.118), channel_id=1, source_target_pairs={{0,6},{2,4},{4,2},{6,0},{8,14},{10,12},{12,10},{14,8},{16,22},{18,... | collective-permute-start | bytes 565256 | tf_op jit(solution)/shard_map/ppermute | solution.py:486
  (17 other events, 194.8 us)
Sparse Core Ops, SparseCore 0:
  14.4 35.0 all-gather.2
  51.1 37.7 all-gather.4

commit v10 on v8

--- a/solution.py
+++ b/solution.py
@@ -40,7 +40,9 @@
     return pltpu.with_memory_space_constraint(value, pltpu.VMEM)
 
 
-def out_projection_kernel(chunk, a_hbm, w_hbm, mine_ref, theirs_ref, a_buf, w_buf, a_sem, sems):
+def out_projection_kernel(
+    chunk, a_hbm, w_hbm, mine_ref, left_ref, right_ref, a_buf, w_buf, a_sem, sems
+):
     depth = w_buf.shape[0]
     count = depth // chunk
     half = mine_ref.shape[0]
@@ -61,12 +63,15 @@
         at = pl.ds(i * chunk, chunk)
         both = jnp.concatenate([a_buf[own, at], a_buf[other, at]], axis=0)
         product = jnp.dot(both, w_buf[at, :], preferred_element_type=jnp.float32)
+        middle = left_ref.shape[1]
         if i == 0:
             mine_ref[...] = product[:half]
-            theirs_ref[...] = product[half:]
+            left_ref[...] = product[half:, :middle]
+            right_ref[...] = product[half:, middle:]
         else:
             mine_ref[...] += product[:half]
-            theirs_ref[...] += product[half:]
+            left_ref[...] += product[half:, :middle]
+            right_ref[...] += product[half:, middle:]
 
 
 def out_projection(attn_out, out_weight):
@@ -74,11 +79,12 @@
     width = out_weight.shape[1]
     chunk = 256
     half = pltpu.VMEM((rows // 2, width), jnp.float32)
+    quarter = pltpu.VMEM((rows // 2, width // 2), jnp.float32)
     return pl.pallas_call(
         functools.partial(out_projection_kernel, chunk),
-        out_shape=(half, half),
+        out_shape=(half, quarter, quarter),
         in_specs=[HBM, HBM],
-        out_specs=(VMEM, VMEM),
+        out_specs=(VMEM,) * 3,
         scratch_shapes=[
             pltpu.VMEM((rows, depth), jnp.bfloat16),
             pltpu.VMEM((depth, width), jnp.bfloat16),
@@ -91,18 +97,15 @@
     )(in_hbm(attn_out), in_hbm(out_weight))
 
 
-def first_norm_kernel(depth, count, *refs):
-    mine, theirs = refs[:count], refs[count : 2 * count]
-    residual_ref, gain_ref, meta_ref, tokens_ref = refs[2 * count : 2 * count + 4]
-    slice_refs, first_ref = refs[2 * count + 4 : -1], refs[-1]
+def first_norm_kernel(depth, mine_ref, left_ref, right_ref, *refs):
+    residual_ref, gain_ref, meta_ref, tokens_ref = refs[:4]
+    slice_refs, first_ref = refs[4:-1], refs[-1]
     rows, width = residual_ref.shape
     sub = width // (PLANE * depth)
-    start = 0
-    for mine_ref, theirs_ref in zip(mine, theirs):
-        cols = slice(start, start + mine_ref.shape[1])
-        start += mine_ref.shape[1]
+    middle = left_ref.shape[1]
+    for ref, cols in ((left_ref, slice(None, middle)), (right_ref, slice(middle, None))):
         first_ref[:, cols] = (
-            residual_ref[:, cols].astype(jnp.float32) + (mine_ref[...] + theirs_ref[...])
+            residual_ref[:, cols].astype(jnp.float32) + (mine_ref[:, cols] + ref[...])
         ).astype(jnp.bfloat16)
     first = first_ref[...]
     tokens_ref[:, :width] = normalize(first.astype(jnp.float32), gain_ref[...]).astype(jnp.bfloat16)
@@ -115,18 +118,18 @@
             ]
 
 
-def first_norm(mine, theirs, residual, gain, meta, depth):
+def first_norm(mine, left, right, residual, gain, meta, depth):
     rows, width = residual.shape
     piece = jax.ShapeDtypeStruct((depth * rows, width // (PLANE * depth)), jnp.bfloat16)
     return pl.pallas_call(
-        functools.partial(first_norm_kernel, depth, len(mine)),
+        functools.partial(first_norm_kernel, depth),
         out_shape=(jax.ShapeDtypeStruct((rows, width + META), jnp.bfloat16),) + (piece,) * PLANE,
-        in_specs=[VMEM] * (2 * len(mine) + 3),
+        in_specs=[VMEM] * 6,
         out_specs=(VMEM,) * (1 + PLANE),
         scratch_shapes=[pltpu.VMEM((rows, width), jnp.bfloat16)],
         compiler_params=params(2),
         name="first_norm",
-    )(*mine, *theirs, residual, gain, meta)
+    )(mine, left, right, residual, gain, meta)
 
 
 def pack_kernel(depth, *refs):
@@ -347,17 +350,24 @@
     )(*parts, *packed, gain)
 
 
-def projection_kernel(chunk, mine_ref, theirs_ref, next_ref, w_hbm, *refs):
-    out_refs, (w_buf, sems) = refs[:PLANE], refs[PLANE:]
-    cols = w_buf.shape[1]
+def projection_kernel(chunk, mine_ref, theirs_ref, next_ref, q_hbm, *refs):
+    kv_refs, out_refs = refs[: q_hbm.shape[0] // META], refs[-PLANE - 3 : -3]
+    q_buf, kv_buf, sems = refs[-3:]
+    depth = len(kv_refs)
+    rows, extended = mine_ref.shape
+    part = extended - META
+    sub = part // depth
+    q_cols, kv_cols = q_buf.shape[1], kv_buf.shape[1]
+    cols = q_cols + kv_cols
     copies = []
-    for i in range(sems.shape[0]):
-        at = lanes(i * META, META)
-        copies.append(pltpu.make_async_copy(w_hbm.at[at], w_buf.at[at], sems.at[i]))
+    for i in range(depth):
+        at = lanes(i * sub, sub)
+        copies.append(pltpu.make_async_copy(q_hbm.at[at], q_buf.at[at], sems.at[i]))
     for copy in copies:
         copy.start()
-    rows, extended = mine_ref.shape
-    part = extended - META
+    line = lax.axis_index("expert") // PLANE
+    for d, ref in enumerate(kv_refs):
+        kv_buf[lanes((line ^ d) * sub, sub), :] = ref[...]
     block = rows // PLANE
     tensor = lax.axis_index("tensor")
     own = lanes(tensor * block, block)
@@ -369,36 +379,40 @@
         out_refs[d][:block, cols + META :] = next_ref[at, : part // 2]
         out_refs[d][block:, cols + META :] = next_ref[at, part // 2 :]
     both = jnp.concatenate([mine_ref[:, :part], theirs_ref[:, :part]], axis=0)
-    for copy in copies:
-        copy.wait()
-    for i in range(cols // chunk):
-        at = slice(i * chunk, (i + 1) * chunk)
-        product = jnp.dot(both, w_buf[:, at], preferred_element_type=jnp.float32).astype(
-            jnp.bfloat16
-        )
+
+    def multiply(weight, target):
+        product = jnp.dot(both, weight, preferred_element_type=jnp.float32).astype(jnp.bfloat16)
+        at = slice(target, target + weight.shape[1])
         for d in range(PLANE):
             out_refs[d][own, at] = product[d * block : (d + 1) * block]
             out_refs[d][other, at] = product[rows + d * block : rows + (d + 1) * block]
 
-
-def projection(mine, theirs, following, weight):
+    multiply(kv_buf[...], q_cols)
+    for copy in copies:
+        copy.wait()
+    for start in range(0, q_cols, chunk):
+        multiply(q_buf[:, start : start + chunk], start)
+
+
+def projection(mine, theirs, following, q_weight, kv_weights):
     rows, part = following.shape
-    cols = weight.shape[1]
+    q_cols, kv_cols = q_weight.shape[1], kv_weights[0].shape[1]
     chunk = 512
-    shape = pltpu.VMEM((2 * rows // PLANE, cols + META + part // 2), jnp.bfloat16)
+    shape = pltpu.VMEM((2 * rows // PLANE, q_cols + kv_cols + META + part // 2), jnp.bfloat16)
     return pl.pallas_call(
         functools.partial(projection_kernel, chunk),
         out_shape=(shape,) * PLANE,
-        in_specs=[VMEM] * 3 + [HBM],
+        in_specs=[VMEM] * 3 + [HBM] + [VMEM] * len(kv_weights),
         out_specs=(VMEM,) * PLANE,
         scratch_shapes=[
-            pltpu.VMEM((part, cols), jnp.bfloat16),
-            pltpu.SemaphoreType.DMA((part // META,)),
+            pltpu.VMEM((part, q_cols), jnp.bfloat16),
+            pltpu.VMEM((part, kv_cols), jnp.bfloat16),
+            pltpu.SemaphoreType.DMA((len(kv_weights),)),
         ],
         compiler_params=params(8),
         cost_estimate=SMALL,
         name="qkv_projection",
-    )(mine, theirs, following, in_hbm(weight))
+    )(mine, theirs, following, in_hbm(q_weight), *kv_weights)
 
 
 def head_norm_kernel(depth, *refs):
@@ -497,17 +511,20 @@
     meta = jnp.concatenate([high, dense - high], axis=1).astype(jnp.bfloat16)
 
     lines = [list(range(i, n_expert, PLANE)) for i in range(PLANE)]
-    mine, theirs = out_projection(attn_out, out_weight)
-    mine, q_own, kv_own = lax.optimization_barrier((mine, q_weight, kv_weight))
-    joined = jnp.concatenate([q_own, kv_own], axis=1)
+    kv_rows = [kv_weight, to_expert(kv_weight, PLANE), to_expert(kv_weight, 2 * PLANE)]
+    mine, left, right = out_projection(attn_out, out_weight)
+    mine, left, right, *kv_rows = lax.optimization_barrier(
+        (mine, to_core(left), to_core(right), *kv_rows)
+    )
     tokens, *firsts = first_norm(
-        (mine,), (to_core(theirs),), residual, attn_gain[None, :], meta, depth
-    )
-    tokens, joined = lax.optimization_barrier((tokens, joined))
-    qkv = lax.all_gather(joined, "expert", axis=0, tiled=True, axis_index_groups=lines)
+        mine, left, right, residual, attn_gain[None, :], meta, depth
+    )
+    tokens, q_own = lax.optimization_barrier((tokens, q_weight))
+    q_rows = lax.all_gather(q_own, "expert", axis=0, tiled=True, axis_index_groups=lines)
+    kv_rows.append(to_expert(kv_rows[2], PLANE))
     weights = load((w_gate, w_up, w_down), (tokens,))
     line = to_z([tokens] * depth)
-    *line, gate, up, down = lax.optimization_barrier((*line, *weights))
+    *line, kv_rows[3], gate, up, down = lax.optimization_barrier((*line, kv_rows[3], *weights))
     weights = (gate, up, down)
     near = to_plane(pack(line, firsts))
     cut = near[0].shape[0] // 2
@@ -518,11 +535,14 @@
     far_both = [*far, *map(to_core, far)]
     tied = lax.optimization_barrier((*near_sum, *far_both))
     near_sum, far_both = tied[:PLANE], tied[PLANE:]
-    mine, *theirs = experts(far_both, weights, depth, 1)
-    far_sum = chip_sum(mine, list(map(to_core, theirs)))
-    parts = plane_sum(to_plane(near_sum), to_plane(far_sum), depth)
+    near_parts = to_plane(near_sum)
+    mine, *theirs = experts(far_both, weights, depth, 2)
+    tied = lax.optimization_barrier((mine, *map(to_core, theirs), *near_parts))
+    mine, theirs, near_parts = tied[0], tied[1:-PLANE], tied[-PLANE:]
+    far_sum = chip_sum(mine, theirs)
+    parts = plane_sum(near_parts, to_plane(far_sum), depth)
     scaled, following = second_norm(to_z(parts), (*near, *far), input_gain[None, :])
-    products = to_plane(projection(scaled, to_core(scaled), following, qkv))
+    products = to_plane(projection(scaled, to_core(scaled), following, q_rows, kv_rows))
     return head_norm(
         products,
         q_gain[None, :],

time: 99.1 us -> 101 us (1.019)
  starting transfers between devices: 27.7 us -> 35.6 us
  waiting for transfers between devices: 37 us -> 32.2 us
    ppermute x19 -> x22, starting transfers between devices: 25.8 us -> 33.2 us  [to_expert(): lax.ppermute(value, 'expert', [(i, i ^ offset) for i in range(n_expert)])]
    ppermute x19 -> x22, waiting for transfers between devices: 34.4 us -> 28.2 us  [to_expert(): lax.ppermute(value, 'expert', [(i, i ^ offset) for i in range(n_expert)])]
    ppermute x11 -> x13, waiting for transfers between devices: 2.59 us -> 4 us  [to_core(): return lax.ppermute(value, 'tensor', [(0, 1), (1, 0)])]
    ppermute x11 -> x13, starting transfers between devices: 1.88 us -> 2.3 us  [to_core(): return lax.ppermute(value, 'tensor', [(0, 1), (1, 0)])]
  transfers between devices with their start and end apart: 31 -> 36, of which waited for: 17 -> 24; matrix products, arithmetic and copies ran while one was open for 1% -> 1% of each run, Pallas kernels for 11% -> 15%
where the time goes in v10:
time: 101 us
  starting transfers between devices  35.6 us (35%)
  waiting for transfers between devices  32.2 us (32%)
  Pallas kernels  18.7 us (19%)
  between operations  14.3 us (14%)
    ppermute x22, starting transfers between devices, to_expert(): lax.ppermute(value, 'expert', [(i, i ^ offset) for i in range(n_expert)])  33.2 us
    ppermute x22, waiting for transfers between devices, to_expert(): lax.ppermute(value, 'expert', [(i, i ^ offset) for i in range(n_expert)])  28.2 us
    pallas_call x2, Pallas kernels, experts(): pl.pallas_call(functools.partial(expert_kernel, depth, chunk, len(blocks)...  6.04 us
    pallas_call x1, Pallas kernels, out_projection(): pl.pallas_call(functools.partial(out_projection_kernel, chunk), out_shape...  4.77 us
    pallas_call x1, Pallas kernels, load(): pl.pallas_call(load_kernel, out_shape=tuple((pltpu.VMEM(w.shape, w.dtype)...  4.15 us
    ppermute x13, waiting for transfers between devices, to_core(): return lax.ppermute(value, 'tensor', [(0, 1), (1, 0)])  4 us
    ppermute x13, starting transfers between devices, to_core(): return lax.ppermute(value, 'tensor', [(0, 1), (1, 0)])  2.3 us
    pallas_call x1, Pallas kernels, projection(): pl.pallas_call(functools.partial(projection_kernel, chunk), out_shape=(sh...  2.12 us
  transfers between devices with their start and end apart: 36, of which 24 were waited for; matrix products, arithmetic and copies ran while one was open for 1% of the time, Pallas kernels for 15%

profile of v10, /device:TPU:0, one launch (start us, length us, event | category | flops | bytes accessed | tf_op | source)
XLA Modules:
  0.0 101.3 jit_solution(3461326237001075953)
XLA Ops:
  7.3 3.1 %collective-permute-start.2 = (bf16[128,512]{1,0:T(8,128)(2,1)}, bf16[128,512]{1,0:T(8,128)(2,1)S(1)}, u32[]{:S(2)}, u32[]{:S(2)}) collective-permute-start(bf16[128,512]{1,0:T(8,128)(2,1)} %refs_0_.4), channel_id=1, source_target_pairs={{0,8},{2,10},{4,12},{6,14},{8,0},{10,2},{12,4},{14,6},{16,24},{18,... | collective-permute-start | bytes 393224 | tf_op jit(solution)/shard_map/ppermute | solution.py:498
  10.3 2.6 %collective-permute-start.3 = (bf16[128,512]{1,0:T(8,128)(2,1)}, bf16[128,512]{1,0:T(8,128)(2,1)S(1)}, u32[]{:S(2)}, u32[]{:S(2)}) collective-permute-start(bf16[128,512]{1,0:T(8,128)(2,1)} %refs_0_.4), channel_id=1, source_target_pairs={{0,16},{2,18},{4,20},{6,22},{8,24},{10,26},{12,28},{14,30},{16,0},... | collective-permute-start | bytes 393224 | tf_op jit(solution)/shard_map/ppermute | solution.py:498
  12.9 4.8 %out_projection.1 = (f32[16,2048]{1,0:T(8,128)S(1)}, f32[16,1024]{1,0:T(8,128)S(1)}, f32[16,1024]{1,0:T(8,128)S(1)}) custom-call(bf16[32,2048]{1,0:T(8,128)(2,1)} %a_hbm.1, bf16[2048,2048]{1,0:T(8,128)(2,1)} %w_hbm.1), custom_call_target="tpu_custom_call" | custom-call | tf_op jit(solution)/shard_map/out_projection/pallas_call | solution.py:83
  19.9 1.6 %collective-permute-start.4 = (bf16[16,2176]{1,0:T(8,128)(2,1)S(1)}, bf16[16,2176]{1,0:T(8,128)(2,1)S(1)}, u32[]{:S(2)}, u32[]{:S(2)}) collective-permute-start(bf16[16,2176]{1,0:T(8,128)(2,1)S(1)} %get-tuple-element.85.refs_3_.refs_0_), channel_id=1, source_target_pairs={{0,8},{2,10},{4,12},{6,14},{8,0},{10,2},{12,4},{14,6},{16,24},{18,... | collective-permute-start | bytes 208904 | tf_op jit(solution)/shard_map/ppermute | solution.py:498
  22.6 1.7 %collective-permute-start.6 = (bf16[16,2176]{1,0:T(8,128)(2,1)S(1)}, bf16[16,2176]{1,0:T(8,128)(2,1)S(1)}, u32[]{:S(2)}, u32[]{:S(2)}) collective-permute-start(bf16[16,2176]{1,0:T(8,128)(2,1)S(1)} %get-tuple-element.85.refs_3_.refs_0_), channel_id=1, source_target_pairs={{0,24},{2,26},{4,28},{6,30},{8,16},{10,18},{12,20},{14,22},{16,8},... | collective-permute-start | bytes 208904 | tf_op jit(solution)/shard_map/ppermute | solution.py:498
  24.3 4.1 %load_weights.1 = (bf16[1,2048,768]{2,1,0:T(8,128)(2,1)S(1)}, bf16[1,2048,768]{2,1,0:T(8,128)(2,1)S(1)}, bf16[1,768,2048]{2,1,0:T(8,128)(2,1)S(1)}) custom-call(bf16[1,2048,768]{2,1,0:T(8,128)(2,1)} %refs_0_.3, bf16[1,2048,768]{2,1,0:T(8,128)(2,1)} %refs_1_.1, bf16[1,768,2048]{2,1,0:T(8,128)(2,1)} %refs_2_.1, ...), custom_call_target="tpu_custom_call" | custom-call | tf_op jit(solution)/shard_map/load_weights/pallas_call | solution.py:174
  30.1 1.6 %collective-permute-start.8 = (bf16[64,2432]{1,0:T(8,128)(2,1)S(1)}, bf16[64,2432]{1,0:T(8,128)(2,1)S(1)}, u32[]{:S(2)}, u32[]{:S(2)}) collective-permute-start(bf16[64,2432]{1,0:T(8,128)(2,1)S(1)} %get-tuple-element.94), channel_id=1, source_target_pairs={{0,2},{2,0},{4,6},{6,4},{8,10},{10,8},{12,14},{14,12},{16,18},{18,... | collective-permute-start | bytes 933896 | tf_op jit(solution)/shard_map/ppermute | solution.py:498
  31.6 1.5 %collective-permute-start.9 = (bf16[64,2432]{1,0:T(8,128)(2,1)S(1)}, bf16[64,2432]{1,0:T(8,128)(2,1)S(1)}, u32[]{:S(2)}, u32[]{:S(2)}) collective-permute-start(bf16[64,2432]{1,0:T(8,128)(2,1)S(1)} %get-tuple-element.95), channel_id=1, source_target_pairs={{0,4},{2,6},{4,0},{6,2},{8,12},{10,14},{12,8},{14,10},{16,20},{18,... | collective-permute-start | bytes 933896 | tf_op jit(solution)/shard_map/ppermute | solution.py:498
  33.1 4.3 %collective-permute-done.8.refs_1_.refs_5_ = bf16[64,2432]{1,0:T(8,128)(2,1)S(1)} collective-permute-done((bf16[64,2432]{1,0:T(8,128)(2,1)S(1)}, bf16[64,2432]{1,0:T(8,128)(2,1)S(1)}, u32[]{:S(2)}, u32[]{:S(2)}) %collective-permute-start.8) | collective-permute-done | bytes 311328 | tf_op jit(solution)/shard_map/ppermute | solution.py:498
  38.7 1.6 %collective-permute-start.16 = (bf16[32,2432]{1,0:T(8,128)(2,1)S(1)}, bf16[32,2432]{1,0:T(8,128)(2,1)S(1)}, u32[]{:S(2)}, u32[]{:S(2)}) collective-permute-start(bf16[32,2432]{1,0:T(8,128)(2,1)S(1)} %slice.8), channel_id=1, source_target_pairs={{0,4},{2,6},{4,0},{6,2},{8,12},{10,14},{12,8},{14,10},{16,20},{18,... | collective-permute-start | bytes 466952 | tf_op jit(solution)/shard_map/ppermute | solution.py:498
  41.1 4.0 %experts.2 = (bf16[192,2048]{1,0:T(8,128)(2,1)S(1)}, bf16[64,2048]{1,0:T(8,128)(2,1)S(1)}, bf16[64,2048]{1,0:T(8,128)(2,1)S(1)}, bf16[64,2048]{1,0:T(8,128)(2,1)S(1)}) custom-call(bf16[64,2432]{1,0:T(8,128)(2,1)S(1)} %get-tuple-element.93.refs_0_.refs_4_, bf16[64,2432]{1,0:T(8,128)(2,1)S(1)} %collective-permute-done.8.refs_1_.refs_5_, ...), custom_call_target="tpu_custom_call" | custom-call | flops 3623878656 | tf_op jit(solution)/shard_map/experts/pallas_call | solution.py:234
  49.7 1.7 %collective-permute-start.24 = (bf16[192,512]{1,0:T(8,128)(2,1)S(1)}, bf16[192,512]{1,0:T(8,128)(2,1)S(1)}, u32[]{:S(2)}, u32[]{:S(2)}) collective-permute-start(bf16[192,512]{1,0:T(8,128)(2,1)S(1)} %get-tuple-element.117), channel_id=1, source_target_pairs={{0,6},{2,4},{4,2},{6,0},{8,14},{10,12},{12,10},{14,8},{16,22},{18,... | collective-permute-start | bytes 589832 | tf_op jit(solution)/shard_map/ppermute | solution.py:498
  51.5 2.0 %experts.3 = (bf16[64,2048]{1,0:T(8,128)(2,1)S(1)}, bf16[32,2048]{1,0:T(8,128)(2,1)S(1)}, bf16[32,2048]{1,0:T(8,128)(2,1)S(1)}) custom-call(bf16[32,2432]{1,0:T(8,128)(2,1)S(1)} %collective-permute-done.16.refs_0_.refs_7_, bf16[32,2432]{1,0:T(8,128)(2,1)S(1)} %collective-permute-done.17.refs_1_.refs_8_, ...), custom_call_target="tpu_custom_call" | custom-call | flops 1207959552 | tf_op jit(solution)/shard_map/experts/pallas_call | solution.py:234
  55.7 4.4 %collective-permute-done.23.refs_2_ = bf16[192,512]{1,0:T(8,128)(2,1)S(1)} collective-permute-done((bf16[192,512]{1,0:T(8,128)(2,1)S(1)}, bf16[192,512]{1,0:T(8,128)(2,1)S(1)}, u32[]{:S(2)}, u32[]{:S(2)}) %collective-permute-start.23) | collective-permute-done | bytes 196640 | tf_op jit(solution)/shard_map/ppermute | solution.py:498
  62.0 1.8 %collective-permute-start.27 = (bf16[64,512]{1,0:T(8,128)(2,1)S(1)}, bf16[64,512]{1,0:T(8,128)(2,1)S(1)}, u32[]{:S(2)}, u32[]{:S(2)}) collective-permute-start(bf16[64,512]{1,0:T(8,128)(2,1)S(1)} %get-tuple-element.128), channel_id=1, source_target_pairs={{0,6},{2,4},{4,2},{6,0},{8,14},{10,12},{12,10},{14,8},{16,22},{18,... | collective-permute-start | bytes 196616 | tf_op jit(solution)/shard_map/ppermute | solution.py:498
  67.3 2.3 %collective-permute-start.28 = (bf16[64,512]{1,0:T(8,128)(2,1)S(1)}, bf16[64,512]{1,0:T(8,128)(2,1)S(1)}, u32[]{:S(2)}, u32[]{:S(2)}) collective-permute-start(bf16[64,512]{1,0:T(8,128)(2,1)S(1)} %get-tuple-element.130), channel_id=1, source_target_pairs={{0,8},{2,10},{4,12},{6,14},{8,0},{10,2},{12,4},{14,6},{16,24},{18,... | collective-permute-start | bytes 196616 | tf_op jit(solution)/shard_map/ppermute | solution.py:498
  69.6 2.8 %collective-permute-start.29 = (bf16[64,512]{1,0:T(8,128)(2,1)S(1)}, bf16[64,512]{1,0:T(8,128)(2,1)S(1)}, u32[]{:S(2)}, u32[]{:S(2)}) collective-permute-start(bf16[64,512]{1,0:T(8,128)(2,1)S(1)} %get-tuple-element.131), channel_id=1, source_target_pairs={{0,16},{2,18},{4,20},{6,22},{8,24},{10,26},{12,28},{14,30},{16,0},... | collective-permute-start | bytes 196616 | tf_op jit(solution)/shard_map/ppermute | solution.py:498
  72.4 1.4 %collective-permute-start.30 = (bf16[64,512]{1,0:T(8,128)(2,1)S(1)}, bf16[64,512]{1,0:T(8,128)(2,1)S(1)}, u32[]{:S(2)}, u32[]{:S(2)}) collective-permute-start(bf16[64,512]{1,0:T(8,128)(2,1)S(1)} %get-tuple-element.132), channel_id=1, source_target_pairs={{0,24},{2,26},{4,28},{6,30},{8,16},{10,18},{12,20},{14,22},{16,8},... | collective-permute-start | bytes 196616 | tf_op jit(solution)/shard_map/ppermute | solution.py:498
  73.8 1.3 %collective-permute-done.29.refs_2_ = bf16[64,512]{1,0:T(8,128)(2,1)S(1)} collective-permute-done((bf16[64,512]{1,0:T(8,128)(2,1)S(1)}, bf16[64,512]{1,0:T(8,128)(2,1)S(1)}, u32[]{:S(2)}, u32[]{:S(2)}) %collective-permute-start.29) | collective-permute-done | bytes 65568 | tf_op jit(solution)/shard_map/ppermute | solution.py:498
  75.2 3.5 %collective-permute-done.30.refs_3_ = bf16[64,512]{1,0:T(8,128)(2,1)S(1)} collective-permute-done((bf16[64,512]{1,0:T(8,128)(2,1)S(1)}, bf16[64,512]{1,0:T(8,128)(2,1)S(1)}, u32[]{:S(2)}, u32[]{:S(2)}) %collective-permute-start.30) | collective-permute-done | bytes 65568 | tf_op jit(solution)/shard_map/ppermute | solution.py:498
  80.1 2.1 %qkv_projection.1 = (bf16[32,2944]{1,0:T(8,128)(2,1)S(1)}, bf16[32,2944]{1,0:T(8,128)(2,1)S(1)}, bf16[32,2944]{1,0:T(8,128)(2,1)S(1)}, bf16[32,2944]{1,0:T(8,128)(2,1)S(1)}) custom-call(bf16[64,640]{1,0:T(8,128)(2,1)S(1)} %get-tuple-element.133.mine_ref, bf16[64,640]{1,0:T(8,128)(2,1)S(1)} %collective-permute-done.31.theirs_ref, ...), custom_call_target="tpu_custom_call" | custom-call | tf_op jit(solution)/shard_map/qkv_projection/pallas_call | solution.py:402
  84.0 1.8 %collective-permute-start.34 = (bf16[32,2944]{1,0:T(8,128)(2,1)S(1)}, bf16[32,2944]{1,0:T(8,128)(2,1)S(1)}, u32[]{:S(2)}, u32[]{:S(2)}) collective-permute-start(bf16[32,2944]{1,0:T(8,128)(2,1)S(1)} %get-tuple-element.142), channel_id=1, source_target_pairs={{0,6},{2,4},{4,2},{6,0},{8,14},{10,12},{12,10},{14,8},{16,22},{18,... | collective-permute-start | bytes 565256 | tf_op jit(solution)/shard_map/ppermute | solution.py:498
  85.8 4.1 %collective-permute-done.32.refs_1_ = bf16[32,2944]{1,0:T(8,128)(2,1)S(1)} collective-permute-done((bf16[32,2944]{1,0:T(8,128)(2,1)S(1)}, bf16[32,2944]{1,0:T(8,128)(2,1)S(1)}, u32[]{:S(2)}, u32[]{:S(2)}) %collective-permute-start.32) | collective-permute-done | bytes 188448 | tf_op jit(solution)/shard_map/ppermute | solution.py:498
  89.9 3.6 %collective-permute-done.33.refs_2_ = bf16[32,2944]{1,0:T(8,128)(2,1)S(1)} collective-permute-done((bf16[32,2944]{1,0:T(8,128)(2,1)S(1)}, bf16[32,2944]{1,0:T(8,128)(2,1)S(1)}, u32[]{:S(2)}, u32[]{:S(2)}) %collective-permute-start.33) | collective-permute-done | bytes 188448 | tf_op jit(solution)/shard_map/ppermute | solution.py:498
  (86 shorter events, 23.3 us)
Async XLA Ops:
  7.2 72.9 %all-gather.2.cloned.1.call-start = ((), (), s32[]{:S(2)}) async-start(), calls=%async_computation | async-start | bytes 2621440 | tf_op jit(solution)/shard_map/all_gather | solution.py:523
  7.3 11.9 %collective-permute-start.2 = (bf16[128,512]{1,0:T(8,128)(2,1)}, bf16[128,512]{1,0:T(8,128)(2,1)S(1)}, u32[]{:S(2)}, u32[]{:S(2)}) collective-permute-start(bf16[128,512]{1,0:T(8,128)(2,1)} %refs_0_.4), channel_id=1, source_target_pairs={{0,8},{2,10},{4,12},{6,14},{8,0},{10,2},{12,4},{14,6},{16,24},{18,... | collective-permute-start | bytes 393224 | tf_op jit(solution)/shard_map/ppermute | solution.py:498
  10.3 8.9 %collective-permute-start.3 = (bf16[128,512]{1,0:T(8,128)(2,1)}, bf16[128,512]{1,0:T(8,128)(2,1)S(1)}, u32[]{:S(2)}, u32[]{:S(2)}) collective-permute-start(bf16[128,512]{1,0:T(8,128)(2,1)} %refs_0_.4), channel_id=1, source_target_pairs={{0,16},{2,18},{4,20},{6,22},{8,24},{10,26},{12,28},{14,30},{16,0},... | collective-permute-start | bytes 393224 | tf_op jit(solution)/shard_map/ppermute | solution.py:498
  19.4 10.5 %collective-permute-start.7 = (bf16[128,512]{1,0:T(8,128)(2,1)S(1)}, bf16[128,512]{1,0:T(8,128)(2,1)S(1)}, u32[]{:S(2)}, u32[]{:S(2)}) collective-permute-start(bf16[128,512]{1,0:T(8,128)(2,1)S(1)} %collective-permute-done.3.refs_2_), channel_id=1, source_target_pairs={{0,8},{2,10},{4,12},{6,14},{8,0},{10,2},{12,4},{14,6},{16,24},{18,... | collective-permute-start | bytes 393224 | tf_op jit(solution)/shard_map/ppermute | solution.py:498
  19.9 8.7 %collective-permute-start.4 = (bf16[16,2176]{1,0:T(8,128)(2,1)S(1)}, bf16[16,2176]{1,0:T(8,128)(2,1)S(1)}, u32[]{:S(2)}, u32[]{:S(2)}) collective-permute-start(bf16[16,2176]{1,0:T(8,128)(2,1)S(1)} %get-tuple-element.85.refs_3_.refs_0_), channel_id=1, source_target_pairs={{0,8},{2,10},{4,12},{6,14},{8,0},{10,2},{12,4},{14,6},{16,24},{18,... | collective-permute-start | bytes 208904 | tf_op jit(solution)/shard_map/ppermute | solution.py:498
  21.5 8.4 %collective-permute-start.5 = (bf16[16,2176]{1,0:T(8,128)(2,1)S(1)}, bf16[16,2176]{1,0:T(8,128)(2,1)S(1)}, u32[]{:S(2)}, u32[]{:S(2)}) collective-permute-start(bf16[16,2176]{1,0:T(8,128)(2,1)S(1)} %get-tuple-element.85.refs_3_.refs_0_), channel_id=1, source_target_pairs={{0,16},{2,18},{4,20},{6,22},{8,24},{10,26},{12,28},{14,30},{16,0},... | collective-permute-start | bytes 208904 | tf_op jit(solution)/shard_map/ppermute | solution.py:498
  22.6 7.4 %collective-permute-start.6 = (bf16[16,2176]{1,0:T(8,128)(2,1)S(1)}, bf16[16,2176]{1,0:T(8,128)(2,1)S(1)}, u32[]{:S(2)}, u32[]{:S(2)}) collective-permute-start(bf16[16,2176]{1,0:T(8,128)(2,1)S(1)} %get-tuple-element.85.refs_3_.refs_0_), channel_id=1, source_target_pairs={{0,24},{2,26},{4,28},{6,30},{8,16},{10,18},{12,20},{14,22},{16,8},... | collective-permute-start | bytes 208904 | tf_op jit(solution)/shard_map/ppermute | solution.py:498
  30.1 7.4 %collective-permute-start.8 = (bf16[64,2432]{1,0:T(8,128)(2,1)S(1)}, bf16[64,2432]{1,0:T(8,128)(2,1)S(1)}, u32[]{:S(2)}, u32[]{:S(2)}) collective-permute-start(bf16[64,2432]{1,0:T(8,128)(2,1)S(1)} %get-tuple-element.94), channel_id=1, source_target_pairs={{0,2},{2,0},{4,6},{6,4},{8,10},{10,8},{12,14},{14,12},{16,18},{18,... | collective-permute-start | bytes 933896 | tf_op jit(solution)/shard_map/ppermute | solution.py:498
  31.6 7.0 %collective-permute-start.9 = (bf16[64,2432]{1,0:T(8,128)(2,1)S(1)}, bf16[64,2432]{1,0:T(8,128)(2,1)S(1)}, u32[]{:S(2)}, u32[]{:S(2)}) collective-permute-start(bf16[64,2432]{1,0:T(8,128)(2,1)S(1)} %get-tuple-element.95), channel_id=1, source_target_pairs={{0,4},{2,6},{4,0},{6,2},{8,12},{10,14},{12,8},{14,10},{16,20},{18,... | collective-permute-start | bytes 933896 | tf_op jit(solution)/shard_map/ppermute | solution.py:498
  33.1 8.0 %collective-permute-start.10 = (bf16[64,2432]{1,0:T(8,128)(2,1)S(1)}, bf16[64,2432]{1,0:T(8,128)(2,1)S(1)}, u32[]{:S(2)}, u32[]{:S(2)}) collective-permute-start(bf16[64,2432]{1,0:T(8,128)(2,1)S(1)} %get-tuple-element.93.refs_0_.refs_4_), channel_id=1, source_target_pairs={{0,1},{1,0},{2,3},{3,2},{4,5},{5,4},{6,7},{7,6},{8,9},{9,8},{10,11... | collective-permute-start | bytes 933896 | tf_op jit(solution)/shard_map/ppermute | solution.py:495
  38.7 7.2 %collective-permute-start.16 = (bf16[32,2432]{1,0:T(8,128)(2,1)S(1)}, bf16[32,2432]{1,0:T(8,128)(2,1)S(1)}, u32[]{:S(2)}, u32[]{:S(2)}) collective-permute-start(bf16[32,2432]{1,0:T(8,128)(2,1)S(1)} %slice.8), channel_id=1, source_target_pairs={{0,4},{2,6},{4,0},{6,2},{8,12},{10,14},{12,8},{14,10},{16,20},{18,... | collective-permute-start | bytes 466952 | tf_op jit(solution)/shard_map/ppermute | solution.py:498
  40.3 6.2 %collective-permute-start.17 = (bf16[32,2432]{1,0:T(8,128)(2,1)S(1)}, bf16[32,2432]{1,0:T(8,128)(2,1)S(1)}, u32[]{:S(2)}, u32[]{:S(2)}) collective-permute-start(bf16[32,2432]{1,0:T(8,128)(2,1)S(1)} %slice.9), channel_id=1, source_target_pairs={{0,2},{2,0},{4,6},{6,4},{8,10},{10,8},{12,14},{14,12},{16,18},{18,... | collective-permute-start | bytes 466952 | tf_op jit(solution)/shard_map/ppermute | solution.py:498
  48.0 7.7 %collective-permute-start.22 = (bf16[192,512]{1,0:T(8,128)(2,1)S(1)}, bf16[192,512]{1,0:T(8,128)(2,1)S(1)}, u32[]{:S(2)}, u32[]{:S(2)}) collective-permute-start(bf16[192,512]{1,0:T(8,128)(2,1)S(1)} %get-tuple-element.115), channel_id=1, source_target_pairs={{0,2},{2,0},{4,6},{6,4},{8,10},{10,8},{12,14},{14,12},{16,18},{18,... | collective-permute-start | bytes 589832 | tf_op jit(solution)/shard_map/ppermute | solution.py:498
  49.2 10.9 %collective-permute-start.23 = (bf16[192,512]{1,0:T(8,128)(2,1)S(1)}, bf16[192,512]{1,0:T(8,128)(2,1)S(1)}, u32[]{:S(2)}, u32[]{:S(2)}) collective-permute-start(bf16[192,512]{1,0:T(8,128)(2,1)S(1)} %get-tuple-element.116), channel_id=1, source_target_pairs={{0,4},{2,6},{4,0},{6,2},{8,12},{10,14},{12,8},{14,10},{16,20},{18,... | collective-permute-start | bytes 589832 | tf_op jit(solution)/shard_map/ppermute | solution.py:498
  49.7 10.4 %collective-permute-start.24 = (bf16[192,512]{1,0:T(8,128)(2,1)S(1)}, bf16[192,512]{1,0:T(8,128)(2,1)S(1)}, u32[]{:S(2)}, u32[]{:S(2)}) collective-permute-start(bf16[192,512]{1,0:T(8,128)(2,1)S(1)} %get-tuple-element.117), channel_id=1, source_target_pairs={{0,6},{2,4},{4,2},{6,0},{8,14},{10,12},{12,10},{14,8},{16,22},{18,... | collective-permute-start | bytes 589832 | tf_op jit(solution)/shard_map/ppermute | solution.py:498
  60.2 4.6 %collective-permute-start.25 = (bf16[64,512]{1,0:T(8,128)(2,1)S(1)}, bf16[64,512]{1,0:T(8,128)(2,1)S(1)}, u32[]{:S(2)}, u32[]{:S(2)}) collective-permute-start(bf16[64,512]{1,0:T(8,128)(2,1)S(1)} %get-tuple-element.126), channel_id=1, source_target_pairs={{0,2},{2,0},{4,6},{6,4},{8,10},{10,8},{12,14},{14,12},{16,18},{18,... | collective-permute-start | bytes 196616 | tf_op jit(solution)/shard_map/ppermute | solution.py:498
  61.0 4.8 %collective-permute-start.26 = (bf16[64,512]{1,0:T(8,128)(2,1)S(1)}, bf16[64,512]{1,0:T(8,128)(2,1)S(1)}, u32[]{:S(2)}, u32[]{:S(2)}) collective-permute-start(bf16[64,512]{1,0:T(8,128)(2,1)S(1)} %get-tuple-element.127), channel_id=1, source_target_pairs={{0,4},{2,6},{4,0},{6,2},{8,12},{10,14},{12,8},{14,10},{16,20},{18,... | collective-permute-start | bytes 196616 | tf_op jit(solution)/shard_map/ppermute | solution.py:498
  62.0 5.2 %collective-permute-start.27 = (bf16[64,512]{1,0:T(8,128)(2,1)S(1)}, bf16[64,512]{1,0:T(8,128)(2,1)S(1)}, u32[]{:S(2)}, u32[]{:S(2)}) collective-permute-start(bf16[64,512]{1,0:T(8,128)(2,1)S(1)} %get-tuple-element.128), channel_id=1, source_target_pairs={{0,6},{2,4},{4,2},{6,0},{8,14},{10,12},{12,10},{14,8},{16,22},{18,... | collective-permute-start | bytes 196616 | tf_op jit(solution)/shard_map/ppermute | solution.py:498
  67.3 6.6 %collective-permute-start.28 = (bf16[64,512]{1,0:T(8,128)(2,1)S(1)}, bf16[64,512]{1,0:T(8,128)(2,1)S(1)}, u32[]{:S(2)}, u32[]{:S(2)}) collective-permute-start(bf16[64,512]{1,0:T(8,128)(2,1)S(1)} %get-tuple-element.130), channel_id=1, source_target_pairs={{0,8},{2,10},{4,12},{6,14},{8,0},{10,2},{12,4},{14,6},{16,24},{18,... | collective-permute-start | bytes 196616 | tf_op jit(solution)/shard_map/ppermute | solution.py:498
  69.6 5.6 %collective-permute-start.29 = (bf16[64,512]{1,0:T(8,128)(2,1)S(1)}, bf16[64,512]{1,0:T(8,128)(2,1)S(1)}, u32[]{:S(2)}, u32[]{:S(2)}) collective-permute-start(bf16[64,512]{1,0:T(8,128)(2,1)S(1)} %get-tuple-element.131), channel_id=1, source_target_pairs={{0,16},{2,18},{4,20},{6,22},{8,24},{10,26},{12,28},{14,30},{16,0},... | collective-permute-start | bytes 196616 | tf_op jit(solution)/shard_map/ppermute | solution.py:498
  72.4 6.2 %collective-permute-start.30 = (bf16[64,512]{1,0:T(8,128)(2,1)S(1)}, bf16[64,512]{1,0:T(8,128)(2,1)S(1)}, u32[]{:S(2)}, u32[]{:S(2)}) collective-permute-start(bf16[64,512]{1,0:T(8,128)(2,1)S(1)} %get-tuple-element.132), channel_id=1, source_target_pairs={{0,24},{2,26},{4,28},{6,30},{8,16},{10,18},{12,20},{14,22},{16,8},... | collective-permute-start | bytes 196616 | tf_op jit(solution)/shard_map/ppermute | solution.py:498
  82.2 7.6 %collective-permute-start.32 = (bf16[32,2944]{1,0:T(8,128)(2,1)S(1)}, bf16[32,2944]{1,0:T(8,128)(2,1)S(1)}, u32[]{:S(2)}, u32[]{:S(2)}) collective-permute-start(bf16[32,2944]{1,0:T(8,128)(2,1)S(1)} %get-tuple-element.140), channel_id=1, source_target_pairs={{0,2},{2,0},{4,6},{6,4},{8,10},{10,8},{12,14},{14,12},{16,18},{18,... | collective-permute-start | bytes 565256 | tf_op jit(solution)/shard_map/ppermute | solution.py:498
  83.0 10.5 %collective-permute-start.33 = (bf16[32,2944]{1,0:T(8,128)(2,1)S(1)}, bf16[32,2944]{1,0:T(8,128)(2,1)S(1)}, u32[]{:S(2)}, u32[]{:S(2)}) collective-permute-start(bf16[32,2944]{1,0:T(8,128)(2,1)S(1)} %get-tuple-element.141), channel_id=1, source_target_pairs={{0,4},{2,6},{4,0},{6,2},{8,12},{10,14},{12,8},{14,10},{16,20},{18,... | collective-permute-start | bytes 565256 | tf_op jit(solution)/shard_map/ppermute | solution.py:498
  84.0 9.5 %collective-permute-start.34 = (bf16[32,2944]{1,0:T(8,128)(2,1)S(1)}, bf16[32,2944]{1,0:T(8,128)(2,1)S(1)}, u32[]{:S(2)}, u32[]{:S(2)}) collective-permute-start(bf16[32,2944]{1,0:T(8,128)(2,1)S(1)} %get-tuple-element.142), channel_id=1, source_target_pairs={{0,6},{2,4},{4,2},{6,0},{8,14},{10,12},{12,10},{14,8},{16,22},{18,... | collective-permute-start | bytes 565256 | tf_op jit(solution)/shard_map/ppermute | solution.py:498
  (20 other events, 205.7 us)
Sparse Core Ops, SparseCore 0:
  19.6 46.0 all-gather.1

commit v11 on v8

--- a/solution.py
+++ b/solution.py
@@ -154,8 +154,8 @@
     )(*line, *pieces)
 
 
-def load_kernel(*refs):
-    sources, targets, sems = refs[:3], refs[-4:-1], refs[-1]
+def load_kernel(count, *refs):
+    sources, targets, sems = refs[:count], refs[-count - 1 : -1], refs[-1]
     copies = [
         pltpu.make_async_copy(source, target, sems.at[i])
         for i, (source, target) in enumerate(zip(sources, targets))
@@ -167,13 +167,13 @@
 
 
 def load(weights, after):
-    size = sum(w.size for w in weights)
-    return pl.pallas_call(
-        load_kernel,
+    count = len(weights)
+    return pl.pallas_call(
+        functools.partial(load_kernel, count),
         out_shape=tuple(pltpu.VMEM(w.shape, w.dtype) for w in weights),
-        in_specs=[HBM] * 3 + [pl.BlockSpec(memory_space=pl.ANY)] * len(after),
-        out_specs=(VMEM,) * 3,
-        scratch_shapes=[pltpu.SemaphoreType.DMA((3,))],
+        in_specs=[HBM] * count + [pl.BlockSpec(memory_space=pl.ANY)] * len(after),
+        out_specs=(VMEM,) * count,
+        scratch_shapes=[pltpu.SemaphoreType.DMA((count,))],
         compiler_params=params(2),
         cost_estimate=SMALL,
         name="load_weights",
@@ -347,17 +347,17 @@
     )(*parts, *packed, gain)
 
 
-def projection_kernel(chunk, mine_ref, theirs_ref, next_ref, w_hbm, *refs):
-    out_refs, (w_buf, sems) = refs[:PLANE], refs[PLANE:]
-    cols = w_buf.shape[1]
-    copies = []
-    for i in range(sems.shape[0]):
-        at = lanes(i * META, META)
-        copies.append(pltpu.make_async_copy(w_hbm.at[at], w_buf.at[at], sems.at[i]))
-    for copy in copies:
-        copy.start()
+def projection_kernel(chunk, mine_ref, theirs_ref, next_ref, q_ref, *refs):
+    kv_refs, out_refs, kv_buf = refs[: -PLANE - 1], refs[-PLANE - 1 : -1], refs[-1]
+    depth = len(kv_refs)
     rows, extended = mine_ref.shape
     part = extended - META
+    sub = part // depth
+    q_cols, kv_cols = q_ref.shape[1], kv_buf.shape[1]
+    cols = q_cols + kv_cols
+    line = lax.axis_index("expert") // PLANE
+    for d, ref in enumerate(kv_refs):
+        kv_buf[lanes((line ^ d) * sub, sub), :] = ref[...]
     block = rows // PLANE
     tensor = lax.axis_index("tensor")
     own = lanes(tensor * block, block)
@@ -369,36 +369,34 @@
         out_refs[d][:block, cols + META :] = next_ref[at, : part // 2]
         out_refs[d][block:, cols + META :] = next_ref[at, part // 2 :]
     both = jnp.concatenate([mine_ref[:, :part], theirs_ref[:, :part]], axis=0)
-    for copy in copies:
-        copy.wait()
-    for i in range(cols // chunk):
-        at = slice(i * chunk, (i + 1) * chunk)
-        product = jnp.dot(both, w_buf[:, at], preferred_element_type=jnp.float32).astype(
-            jnp.bfloat16
-        )
+
+    def multiply(weight, target):
+        product = jnp.dot(both, weight, preferred_element_type=jnp.float32).astype(jnp.bfloat16)
+        at = slice(target, target + weight.shape[1])
         for d in range(PLANE):
             out_refs[d][own, at] = product[d * block : (d + 1) * block]
             out_refs[d][other, at] = product[rows + d * block : rows + (d + 1) * block]
 
-
-def projection(mine, theirs, following, weight):
+    multiply(kv_buf[...], q_cols)
+    for start in range(0, q_cols, chunk):
+        multiply(q_ref[:, start : start + chunk], start)
+
+
+def projection(mine, theirs, following, q_weight, kv_weights):
     rows, part = following.shape
-    cols = weight.shape[1]
+    q_cols, kv_cols = q_weight.shape[1], kv_weights[0].shape[1]
     chunk = 512
-    shape = pltpu.VMEM((2 * rows // PLANE, cols + META + part // 2), jnp.bfloat16)
+    shape = pltpu.VMEM((2 * rows // PLANE, q_cols + kv_cols + META + part // 2), jnp.bfloat16)
     return pl.pallas_call(
         functools.partial(projection_kernel, chunk),
         out_shape=(shape,) * PLANE,
-        in_specs=[VMEM] * 3 + [HBM],
+        in_specs=[VMEM] * (4 + len(kv_weights)),
         out_specs=(VMEM,) * PLANE,
-        scratch_shapes=[
-            pltpu.VMEM((part, cols), jnp.bfloat16),
-            pltpu.SemaphoreType.DMA((part // META,)),
-        ],
+        scratch_shapes=[pltpu.VMEM((part, kv_cols), jnp.bfloat16)],
         compiler_params=params(8),
         cost_estimate=SMALL,
         name="qkv_projection",
-    )(mine, theirs, following, in_hbm(weight))
+    )(mine, theirs, following, q_weight, *kv_weights)
 
 
 def head_norm_kernel(depth, *refs):
@@ -498,13 +496,11 @@
 
     lines = [list(range(i, n_expert, PLANE)) for i in range(PLANE)]
     mine, theirs = out_projection(attn_out, out_weight)
-    mine, q_own, kv_own = lax.optimization_barrier((mine, q_weight, kv_weight))
-    joined = jnp.concatenate([q_own, kv_own], axis=1)
     tokens, *firsts = first_norm(
         (mine,), (to_core(theirs),), residual, attn_gain[None, :], meta, depth
     )
-    tokens, joined = lax.optimization_barrier((tokens, joined))
-    qkv = lax.all_gather(joined, "expert", axis=0, tiled=True, axis_index_groups=lines)
+    tokens, q_own = lax.optimization_barrier((tokens, q_weight))
+    q_rows = lax.all_gather(q_own, "expert", axis=0, tiled=True, axis_index_groups=lines)
     weights = load((w_gate, w_up, w_down), (tokens,))
     line = to_z([tokens] * depth)
     *line, gate, up, down = lax.optimization_barrier((*line, *weights))
@@ -520,9 +516,17 @@
     near_sum, far_both = tied[:PLANE], tied[PLANE:]
     mine, *theirs = experts(far_both, weights, depth, 1)
     far_sum = chip_sum(mine, list(map(to_core, theirs)))
-    parts = plane_sum(to_plane(near_sum), to_plane(far_sum), depth)
-    scaled, following = second_norm(to_z(parts), (*near, *far), input_gain[None, :])
-    products = to_plane(projection(scaled, to_core(scaled), following, qkv))
+    *far_sum, kv_own = lax.optimization_barrier((*far_sum, kv_weight))
+    kv_rows = [kv_own, to_expert(kv_own, PLANE), to_expert(kv_own, 2 * PLANE)]
+    *parts, kv_rows[2] = lax.optimization_barrier(
+        (*plane_sum(to_plane(near_sum), to_plane(far_sum), depth), kv_rows[2])
+    )
+    kv_rows.append(to_expert(kv_rows[2], PLANE))
+    (q_rows,) = load((q_rows,), parts)
+    parts = to_z(parts)
+    *parts, q_rows = lax.optimization_barrier((*parts, q_rows))
+    scaled, following = second_norm(parts, (*near, *far), input_gain[None, :])
+    products = to_plane(projection(scaled, to_core(scaled), following, q_rows, kv_rows))
     return head_norm(
         products,
         q_gain[None, :],

time: 99.1 us -> 98.2 us (level)
  starting transfers between devices: 27.7 us -> 30.9 us
  waiting for transfers between devices: 37 us -> 33.9 us
    ppermute x19 -> x22, starting transfers between devices: 25.8 us -> 29 us  [to_expert(): lax.ppermute(value, 'expert', [(i, i ^ offset) for i in range(n_expert)])]
    ppermute x19 -> x22, waiting for transfers between devices: 34.4 us -> 32 us  [to_expert(): lax.ppermute(value, 'expert', [(i, i ^ offset) for i in range(n_expert)])]
    pallas_call x1, Pallas kernels: 2.23 us -> 0.56 us  [projection(): pl.pallas_call(functools.partial(projection_kernel, chunk), out_shape=(sh...]
    pallas_call x1 -> x2, Pallas kernels: 3.8 us -> 5.42 us  [load(): pl.pallas_call(functools.partial(load_kernel, count), out_shape=tuple((pl...]
  transfers between devices with their start and end apart: 31 -> 34, of which waited for: 17 -> 20; matrix products, arithmetic and copies ran while one was open for 1% -> 1% of each run, Pallas kernels for 11% -> 12%
where the time goes in v11:
time: 98.2 us; the launch traced here: 98.1 us
  waiting for transfers between devices  33.9 us (35%)
  starting transfers between devices  30.9 us (31%)
  Pallas kernels  18.4 us (19%)
  between operations  14.3 us (15%)
    ppermute x22, waiting for transfers between devices, to_expert(): lax.ppermute(value, 'expert', [(i, i ^ offset) for i in range(n_expert)])  32 us
    ppermute x22, starting transfers between devices, to_expert(): lax.ppermute(value, 'expert', [(i, i ^ offset) for i in range(n_expert)])  29 us
    pallas_call x2, Pallas kernels, experts(): pl.pallas_call(functools.partial(expert_kernel, depth, chunk, len(blocks)...  6.06 us
    pallas_call x2, Pallas kernels, load(): pl.pallas_call(functools.partial(load_kernel, count), out_shape=tuple((pl...  5.42 us
    pallas_call x1, Pallas kernels, out_projection(): pl.pallas_call(functools.partial(out_projection_kernel, chunk), out_shape...  4.77 us
  transfers between devices with their start and end apart: 34, of which 20 were waited for; matrix products, arithmetic and copies ran while one was open for 1% of the time, Pallas kernels for 12%

profile of v11, /device:TPU:0, one launch (start us, length us, event | category | flops | bytes accessed | tf_op | source)
XLA Modules:
  0.0 98.1 jit_solution(1474315655986402965)
XLA Ops:
  7.3 4.8 %out_projection.1 = (f32[16,2048]{1,0:T(8,128)S(1)}, f32[16,2048]{1,0:T(8,128)S(1)}) custom-call(bf16[32,2048]{1,0:T(8,128)(2,1)} %a_hbm.1, bf16[2048,2048]{1,0:T(8,128)(2,1)} %w_hbm.1), custom_call_target="tpu_custom_call" | custom-call | tf_op jit(solution)/shard_map/out_projection/pallas_call | solution.py:77
  13.7 3.0 %collective-permute-start.1 = (bf16[16,2176]{1,0:T(8,128)(2,1)S(1)}, bf16[16,2176]{1,0:T(8,128)(2,1)S(1)}, u32[]{:S(2)}, u32[]{:S(2)}) collective-permute-start(bf16[16,2176]{1,0:T(8,128)(2,1)S(1)} %get-tuple-element.79.refs_3_.refs_0_), channel_id=1, source_target_pairs={{0,8},{2,10},{4,12},{6,14},{8,0},{10,2},{12,4},{14,6},{16,24},{18,... | collective-permute-start | bytes 208904 | tf_op jit(solution)/shard_map/ppermute | solution.py:482
  16.7 2.6 %collective-permute-start.2 = (bf16[16,2176]{1,0:T(8,128)(2,1)S(1)}, bf16[16,2176]{1,0:T(8,128)(2,1)S(1)}, u32[]{:S(2)}, u32[]{:S(2)}) collective-permute-start(bf16[16,2176]{1,0:T(8,128)(2,1)S(1)} %get-tuple-element.79.refs_3_.refs_0_), channel_id=1, source_target_pairs={{0,16},{2,18},{4,20},{6,22},{8,24},{10,26},{12,28},{14,30},{16,0},... | collective-permute-start | bytes 208904 | tf_op jit(solution)/shard_map/ppermute | solution.py:482
  19.3 3.8 %load_weights.2 = (bf16[1,2048,768]{2,1,0:T(8,128)(2,1)S(1)}, bf16[1,2048,768]{2,1,0:T(8,128)(2,1)S(1)}, bf16[1,768,2048]{2,1,0:T(8,128)(2,1)S(1)}) custom-call(bf16[1,2048,768]{2,1,0:T(8,128)(2,1)} %refs_0_.1, bf16[1,2048,768]{2,1,0:T(8,128)(2,1)} %refs_1_.1, bf16[1,768,2048]{2,1,0:T(8,128)(2,1)} %refs_2_.3, ...), custom_call_target="tpu_custom_call" | custom-call | tf_op jit(solution)/shard_map/load_weights/pallas_call | solution.py:171
  23.1 1.4 %collective-permute-done.2.refs_2_ = bf16[16,2176]{1,0:T(8,128)(2,1)S(1)} collective-permute-done((bf16[16,2176]{1,0:T(8,128)(2,1)S(1)}, bf16[16,2176]{1,0:T(8,128)(2,1)S(1)}, u32[]{:S(2)}, u32[]{:S(2)}) %collective-permute-start.2) | collective-permute-done | bytes 69664 | tf_op jit(solution)/shard_map/ppermute | solution.py:482
  25.6 1.6 %collective-permute-start.4 = (bf16[64,2432]{1,0:T(8,128)(2,1)S(1)}, bf16[64,2432]{1,0:T(8,128)(2,1)S(1)}, u32[]{:S(2)}, u32[]{:S(2)}) collective-permute-start(bf16[64,2432]{1,0:T(8,128)(2,1)S(1)} %get-tuple-element.88), channel_id=1, source_target_pairs={{0,2},{2,0},{4,6},{6,4},{8,10},{10,8},{12,14},{14,12},{16,18},{18,... | collective-permute-start | bytes 933896 | tf_op jit(solution)/shard_map/ppermute | solution.py:482
  27.1 1.5 %collective-permute-start.5 = (bf16[64,2432]{1,0:T(8,128)(2,1)S(1)}, bf16[64,2432]{1,0:T(8,128)(2,1)S(1)}, u32[]{:S(2)}, u32[]{:S(2)}) collective-permute-start(bf16[64,2432]{1,0:T(8,128)(2,1)S(1)} %get-tuple-element.89), channel_id=1, source_target_pairs={{0,4},{2,6},{4,0},{6,2},{8,12},{10,14},{12,8},{14,10},{16,20},{18,... | collective-permute-start | bytes 933896 | tf_op jit(solution)/shard_map/ppermute | solution.py:482
  28.7 4.6 %collective-permute-done.4.refs_1_.refs_5_ = bf16[64,2432]{1,0:T(8,128)(2,1)S(1)} collective-permute-done((bf16[64,2432]{1,0:T(8,128)(2,1)S(1)}, bf16[64,2432]{1,0:T(8,128)(2,1)S(1)}, u32[]{:S(2)}, u32[]{:S(2)}) %collective-permute-start.4) | collective-permute-done | bytes 311328 | tf_op jit(solution)/shard_map/ppermute | solution.py:482
  34.5 1.6 %collective-permute-start.12 = (bf16[32,2432]{1,0:T(8,128)(2,1)S(1)}, bf16[32,2432]{1,0:T(8,128)(2,1)S(1)}, u32[]{:S(2)}, u32[]{:S(2)}) collective-permute-start(bf16[32,2432]{1,0:T(8,128)(2,1)S(1)} %slice.8), channel_id=1, source_target_pairs={{0,4},{2,6},{4,0},{6,2},{8,12},{10,14},{12,8},{14,10},{16,20},{18,... | collective-permute-start | bytes 466952 | tf_op jit(solution)/shard_map/ppermute | solution.py:482
  37.0 4.1 %experts.2 = (bf16[192,2048]{1,0:T(8,128)(2,1)S(1)}, bf16[64,2048]{1,0:T(8,128)(2,1)S(1)}, bf16[64,2048]{1,0:T(8,128)(2,1)S(1)}, bf16[64,2048]{1,0:T(8,128)(2,1)S(1)}) custom-call(bf16[64,2432]{1,0:T(8,128)(2,1)S(1)} %get-tuple-element.87.refs_0_.refs_4_, bf16[64,2432]{1,0:T(8,128)(2,1)S(1)} %collective-permute-done.4.refs_1_.refs_5_, ...), custom_call_target="tpu_custom_call" | custom-call | flops 3623878656 | tf_op jit(solution)/shard_map/experts/pallas_call | solution.py:231
  43.8 2.0 %experts.3 = (bf16[64,2048]{1,0:T(8,128)(2,1)S(1)}, bf16[64,2048]{1,0:T(8,128)(2,1)S(1)}) custom-call(bf16[32,2432]{1,0:T(8,128)(2,1)S(1)} %collective-permute-done.12.refs_0_.refs_7_, bf16[32,2432]{1,0:T(8,128)(2,1)S(1)} %collective-permute-done.13.refs_1_.refs_8_, bf16[32,2432]{1,0:T(8,128)(2,1)S(1)} %collective-permute-done.14.refs_2_, ...), custom_call_target="tpu_custom_call" | custom-call | flops 1207959552 | tf_op jit(solution)/shard_map/experts/pallas_call | solution.py:231
  47.8 1.7 %collective-permute-start.18 = (bf16[192,512]{1,0:T(8,128)(2,1)S(1)}, bf16[192,512]{1,0:T(8,128)(2,1)S(1)}, u32[]{:S(2)}, u32[]{:S(2)}) collective-permute-start(bf16[192,512]{1,0:T(8,128)(2,1)S(1)} %get-tuple-element.104), channel_id=1, source_target_pairs={{0,6},{2,4},{4,2},{6,0},{8,14},{10,12},{12,10},{14,8},{16,22},{18,... | collective-permute-start | bytes 589832 | tf_op jit(solution)/shard_map/ppermute | solution.py:482
  49.6 2.5 %collective-permute-start.23 = (bf16[128,512]{1,0:T(8,128)(2,1)S(1)}, bf16[128,512]{1,0:T(8,128)(2,1)S(1)}, u32[]{:S(2)}, u32[]{:S(2)}) collective-permute-start(bf16[128,512]{1,0:T(8,128)(2,1)S(1)} %copy-done.1), channel_id=1, source_target_pairs={{0,16},{2,18},{4,20},{6,22},{8,24},{10,26},{12,28},{14,30},{16,0},... | collective-permute-start | bytes 393224 | tf_op jit(solution)/shard_map/ppermute | solution.py:482
  54.4 5.4 %collective-permute-done.17.refs_2_ = bf16[192,512]{1,0:T(8,128)(2,1)S(1)} collective-permute-done((bf16[192,512]{1,0:T(8,128)(2,1)S(1)}, bf16[192,512]{1,0:T(8,128)(2,1)S(1)}, u32[]{:S(2)}, u32[]{:S(2)}) %collective-permute-start.17) | collective-permute-done | bytes 196640 | tf_op jit(solution)/shard_map/ppermute | solution.py:482
  60.5 4.5 %collective-permute-done.22.refs_7_ = bf16[64,512]{1,0:T(8,128)(2,1)S(1)} collective-permute-done((bf16[64,512]{1,0:T(8,128)(2,1)S(1)}, bf16[64,512]{1,0:T(8,128)(2,1)S(1)}, u32[]{:S(2)}, u32[]{:S(2)}) %collective-permute-start.22) | collective-permute-done | bytes 65568 | tf_op jit(solution)/shard_map/ppermute | solution.py:482
  66.7 1.4 %collective-permute-start.25 = (bf16[64,512]{1,0:T(8,128)(2,1)S(1)}, bf16[64,512]{1,0:T(8,128)(2,1)S(1)}, u32[]{:S(2)}, u32[]{:S(2)}) collective-permute-start(bf16[64,512]{1,0:T(8,128)(2,1)S(1)} %get-tuple-element.126.refs_3_), channel_id=1, source_target_pairs={{0,16},{2,18},{4,20},{6,22},{8,24},{10,26},{12,28},{14,30},{16,0},... | collective-permute-start | bytes 196616 | tf_op jit(solution)/shard_map/ppermute | solution.py:482
  68.1 2.4 %collective-permute-start.26 = (bf16[64,512]{1,0:T(8,128)(2,1)S(1)}, bf16[64,512]{1,0:T(8,128)(2,1)S(1)}, u32[]{:S(2)}, u32[]{:S(2)}) collective-permute-start(bf16[64,512]{1,0:T(8,128)(2,1)S(1)} %get-tuple-element.127.refs_4_), channel_id=1, source_target_pairs={{0,24},{2,26},{4,28},{6,30},{8,16},{10,18},{12,20},{14,22},{16,8},... | collective-permute-start | bytes 196616 | tf_op jit(solution)/shard_map/ppermute | solution.py:482
  70.5 2.0 %collective-permute-start.29 = (bf16[128,512]{1,0:T(8,128)(2,1)S(1)}, bf16[128,512]{1,0:T(8,128)(2,1)S(1)}, u32[]{:S(2)}, u32[]{:S(2)}) collective-permute-start(bf16[128,512]{1,0:T(8,128)(2,1)S(1)} %collective-permute-done.23.refs_2_), channel_id=1, source_target_pairs={{0,8},{2,10},{4,12},{6,14},{8,0},{10,2},{12,4},{14,6},{16,24},{18,... | collective-permute-start | bytes 393224 | tf_op jit(solution)/shard_map/ppermute | solution.py:482
  72.5 1.6 %load_weights.3.q_ref = bf16[512,2048]{1,0:T(8,128)(2,1)S(1)} custom-call(bf16[512,2048]{1,0:T(8,128)(2,1)} %all-gather.2.cloned.1.call-done.refs_0_, bf16[64,512]{1,0:T(8,128)(2,1)S(1)} %get-tuple-element.129.refs_1_.refs_0_, bf16[64,512]{1,0:T(8,128)(2,1)S(1)} %get-tuple-element.125.refs_2_, bf16[64,512]{1,0:T(8,128)(2,1)S(1)} %get-tuple-element.126.refs_3_, ...), custom_call_target="tpu_custom_call" | custom-call | tf_op jit(solution)/shard_map/load_weights/pallas_call | solution.py:171
  75.2 2.2 %collective-permute-done.28.refs_1_ = bf16[128,512]{1,0:T(8,128)(2,1)S(1)} collective-permute-done((bf16[128,512]{1,0:T(8,128)(2,1)S(1)}, bf16[128,512]{1,0:T(8,128)(2,1)S(1)}, u32[]{:S(2)}, u32[]{:S(2)}) %collective-permute-start.28) | collective-permute-done | bytes 131104 | tf_op jit(solution)/shard_map/ppermute | solution.py:482
  77.4 1.5 %collective-permute-done.29.refs_3_ = bf16[128,512]{1,0:T(8,128)(2,1)S(1)} collective-permute-done((bf16[128,512]{1,0:T(8,128)(2,1)S(1)}, bf16[128,512]{1,0:T(8,128)(2,1)S(1)}, u32[]{:S(2)}, u32[]{:S(2)}) %collective-permute-start.29) | collective-permute-done | bytes 131104 | tf_op jit(solution)/shard_map/ppermute | solution.py:482
  80.8 1.4 %collective-permute-start.31 = (bf16[32,2944]{1,0:T(8,128)(2,1)S(1)}, bf16[32,2944]{1,0:T(8,128)(2,1)S(1)}, u32[]{:S(2)}, u32[]{:S(2)}) collective-permute-start(bf16[32,2944]{1,0:T(8,128)(2,1)S(1)} %get-tuple-element.139), channel_id=1, source_target_pairs={{0,4},{2,6},{4,0},{6,2},{8,12},{10,14},{12,8},{14,10},{16,20},{18,... | collective-permute-start | bytes 565256 | tf_op jit(solution)/shard_map/ppermute | solution.py:482
  83.0 4.1 %collective-permute-done.30.refs_1_ = bf16[32,2944]{1,0:T(8,128)(2,1)S(1)} collective-permute-done((bf16[32,2944]{1,0:T(8,128)(2,1)S(1)}, bf16[32,2944]{1,0:T(8,128)(2,1)S(1)}, u32[]{:S(2)}, u32[]{:S(2)}) %collective-permute-start.30) | collective-permute-done | bytes 188448 | tf_op jit(solution)/shard_map/ppermute | solution.py:482
  87.1 3.2 %collective-permute-done.31.refs_2_ = bf16[32,2944]{1,0:T(8,128)(2,1)S(1)} collective-permute-done((bf16[32,2944]{1,0:T(8,128)(2,1)S(1)}, bf16[32,2944]{1,0:T(8,128)(2,1)S(1)}, u32[]{:S(2)}, u32[]{:S(2)}) %collective-permute-start.31) | collective-permute-done | bytes 188448 | tf_op jit(solution)/shard_map/ppermute | solution.py:482
  (83 shorter events, 19.0 us)
Async XLA Ops:
  7.2 65.3 %all-gather.2.cloned.1.call-start = ((), (), s32[]{:S(2)}) async-start(), calls=%async_computation | async-start | bytes 2621440 | tf_op jit(solution)/shard_map/all_gather | solution.py:503
  13.7 9.4 %collective-permute-start.1 = (bf16[16,2176]{1,0:T(8,128)(2,1)S(1)}, bf16[16,2176]{1,0:T(8,128)(2,1)S(1)}, u32[]{:S(2)}, u32[]{:S(2)}) collective-permute-start(bf16[16,2176]{1,0:T(8,128)(2,1)S(1)} %get-tuple-element.79.refs_3_.refs_0_), channel_id=1, source_target_pairs={{0,8},{2,10},{4,12},{6,14},{8,0},{10,2},{12,4},{14,6},{16,24},{18,... | collective-permute-start | bytes 208904 | tf_op jit(solution)/shard_map/ppermute | solution.py:482
  16.7 7.8 %collective-permute-start.2 = (bf16[16,2176]{1,0:T(8,128)(2,1)S(1)}, bf16[16,2176]{1,0:T(8,128)(2,1)S(1)}, u32[]{:S(2)}, u32[]{:S(2)}) collective-permute-start(bf16[16,2176]{1,0:T(8,128)(2,1)S(1)} %get-tuple-element.79.refs_3_.refs_0_), channel_id=1, source_target_pairs={{0,16},{2,18},{4,20},{6,22},{8,24},{10,26},{12,28},{14,30},{16,0},... | collective-permute-start | bytes 208904 | tf_op jit(solution)/shard_map/ppermute | solution.py:482
  19.3 6.2 %collective-permute-start.3 = (bf16[16,2176]{1,0:T(8,128)(2,1)S(1)}, bf16[16,2176]{1,0:T(8,128)(2,1)S(1)}, u32[]{:S(2)}, u32[]{:S(2)}) collective-permute-start(bf16[16,2176]{1,0:T(8,128)(2,1)S(1)} %get-tuple-element.79.refs_3_.refs_0_), channel_id=1, source_target_pairs={{0,24},{2,26},{4,28},{6,30},{8,16},{10,18},{12,20},{14,22},{16,8},... | collective-permute-start | bytes 208904 | tf_op jit(solution)/shard_map/ppermute | solution.py:482
  25.6 7.7 %collective-permute-start.4 = (bf16[64,2432]{1,0:T(8,128)(2,1)S(1)}, bf16[64,2432]{1,0:T(8,128)(2,1)S(1)}, u32[]{:S(2)}, u32[]{:S(2)}) collective-permute-start(bf16[64,2432]{1,0:T(8,128)(2,1)S(1)} %get-tuple-element.88), channel_id=1, source_target_pairs={{0,2},{2,0},{4,6},{6,4},{8,10},{10,8},{12,14},{14,12},{16,18},{18,... | collective-permute-start | bytes 933896 | tf_op jit(solution)/shard_map/ppermute | solution.py:482
  27.1 7.3 %collective-permute-start.5 = (bf16[64,2432]{1,0:T(8,128)(2,1)S(1)}, bf16[64,2432]{1,0:T(8,128)(2,1)S(1)}, u32[]{:S(2)}, u32[]{:S(2)}) collective-permute-start(bf16[64,2432]{1,0:T(8,128)(2,1)S(1)} %get-tuple-element.89), channel_id=1, source_target_pairs={{0,4},{2,6},{4,0},{6,2},{8,12},{10,14},{12,8},{14,10},{16,20},{18,... | collective-permute-start | bytes 933896 | tf_op jit(solution)/shard_map/ppermute | solution.py:482
  28.7 8.3 %collective-permute-start.6 = (bf16[64,2432]{1,0:T(8,128)(2,1)S(1)}, bf16[64,2432]{1,0:T(8,128)(2,1)S(1)}, u32[]{:S(2)}, u32[]{:S(2)}) collective-permute-start(bf16[64,2432]{1,0:T(8,128)(2,1)S(1)} %get-tuple-element.87.refs_0_.refs_4_), channel_id=1, source_target_pairs={{0,1},{1,0},{2,3},{3,2},{4,5},{5,4},{6,7},{7,6},{8,9},{9,8},{10,11... | collective-permute-start | bytes 933896 | tf_op jit(solution)/shard_map/ppermute | solution.py:479
  34.5 7.2 %collective-permute-start.12 = (bf16[32,2432]{1,0:T(8,128)(2,1)S(1)}, bf16[32,2432]{1,0:T(8,128)(2,1)S(1)}, u32[]{:S(2)}, u32[]{:S(2)}) collective-permute-start(bf16[32,2432]{1,0:T(8,128)(2,1)S(1)} %slice.8), channel_id=1, source_target_pairs={{0,4},{2,6},{4,0},{6,2},{8,12},{10,14},{12,8},{14,10},{16,20},{18,... | collective-permute-start | bytes 466952 | tf_op jit(solution)/shard_map/ppermute | solution.py:482
  36.1 6.2 %collective-permute-start.13 = (bf16[32,2432]{1,0:T(8,128)(2,1)S(1)}, bf16[32,2432]{1,0:T(8,128)(2,1)S(1)}, u32[]{:S(2)}, u32[]{:S(2)}) collective-permute-start(bf16[32,2432]{1,0:T(8,128)(2,1)S(1)} %slice.9), channel_id=1, source_target_pairs={{0,2},{2,0},{4,6},{6,4},{8,10},{10,8},{12,14},{14,12},{16,18},{18,... | collective-permute-start | bytes 466952 | tf_op jit(solution)/shard_map/ppermute | solution.py:482
  46.0 7.7 %collective-permute-start.16 = (bf16[192,512]{1,0:T(8,128)(2,1)S(1)}, bf16[192,512]{1,0:T(8,128)(2,1)S(1)}, u32[]{:S(2)}, u32[]{:S(2)}) collective-permute-start(bf16[192,512]{1,0:T(8,128)(2,1)S(1)} %get-tuple-element.102), channel_id=1, source_target_pairs={{0,2},{2,0},{4,6},{6,4},{8,10},{10,8},{12,14},{14,12},{16,18},{18,... | collective-permute-start | bytes 589832 | tf_op jit(solution)/shard_map/ppermute | solution.py:482
  47.3 12.5 %collective-permute-start.17 = (bf16[192,512]{1,0:T(8,128)(2,1)S(1)}, bf16[192,512]{1,0:T(8,128)(2,1)S(1)}, u32[]{:S(2)}, u32[]{:S(2)}) collective-permute-start(bf16[192,512]{1,0:T(8,128)(2,1)S(1)} %get-tuple-element.103), channel_id=1, source_target_pairs={{0,4},{2,6},{4,0},{6,2},{8,12},{10,14},{12,8},{14,10},{16,20},{18,... | collective-permute-start | bytes 589832 | tf_op jit(solution)/shard_map/ppermute | solution.py:482
  47.8 12.0 %collective-permute-start.18 = (bf16[192,512]{1,0:T(8,128)(2,1)S(1)}, bf16[192,512]{1,0:T(8,128)(2,1)S(1)}, u32[]{:S(2)}, u32[]{:S(2)}) collective-permute-start(bf16[192,512]{1,0:T(8,128)(2,1)S(1)} %get-tuple-element.104), channel_id=1, source_target_pairs={{0,6},{2,4},{4,2},{6,0},{8,14},{10,12},{12,10},{14,8},{16,22},{18,... | collective-permute-start | bytes 589832 | tf_op jit(solution)/shard_map/ppermute | solution.py:482
  49.6 16.5 %collective-permute-start.23 = (bf16[128,512]{1,0:T(8,128)(2,1)S(1)}, bf16[128,512]{1,0:T(8,128)(2,1)S(1)}, u32[]{:S(2)}, u32[]{:S(2)}) collective-permute-start(bf16[128,512]{1,0:T(8,128)(2,1)S(1)} %copy-done.1), channel_id=1, source_target_pairs={{0,16},{2,18},{4,20},{6,22},{8,24},{10,26},{12,28},{14,30},{16,0},... | collective-permute-start | bytes 393224 | tf_op jit(solution)/shard_map/ppermute | solution.py:482
  52.2 7.6 %collective-permute-start.20 = (bf16[64,512]{1,0:T(8,128)(2,1)S(1)}, bf16[64,512]{1,0:T(8,128)(2,1)S(1)}, u32[]{:S(2)}, u32[]{:S(2)}) collective-permute-start(bf16[64,512]{1,0:T(8,128)(2,1)S(1)} %get-tuple-element.116), channel_id=1, source_target_pairs={{0,2},{2,0},{4,6},{6,4},{8,10},{10,8},{12,14},{14,12},{16,18},{18,... | collective-permute-start | bytes 196616 | tf_op jit(solution)/shard_map/ppermute | solution.py:482
  53.8 6.7 %collective-permute-start.21 = (bf16[64,512]{1,0:T(8,128)(2,1)S(1)}, bf16[64,512]{1,0:T(8,128)(2,1)S(1)}, u32[]{:S(2)}, u32[]{:S(2)}) collective-permute-start(bf16[64,512]{1,0:T(8,128)(2,1)S(1)} %get-tuple-element.117), channel_id=1, source_target_pairs={{0,4},{2,6},{4,0},{6,2},{8,12},{10,14},{12,8},{14,10},{16,20},{18,... | collective-permute-start | bytes 196616 | tf_op jit(solution)/shard_map/ppermute | solution.py:482
  59.8 5.2 %collective-permute-start.22 = (bf16[64,512]{1,0:T(8,128)(2,1)S(1)}, bf16[64,512]{1,0:T(8,128)(2,1)S(1)}, u32[]{:S(2)}, u32[]{:S(2)}) collective-permute-start(bf16[64,512]{1,0:T(8,128)(2,1)S(1)} %get-tuple-element.118), channel_id=1, source_target_pairs={{0,6},{2,4},{4,2},{6,0},{8,14},{10,12},{12,10},{14,8},{16,22},{18,... | collective-permute-start | bytes 196616 | tf_op jit(solution)/shard_map/ppermute | solution.py:482
  66.1 8.1 %collective-permute-start.24 = (bf16[64,512]{1,0:T(8,128)(2,1)S(1)}, bf16[64,512]{1,0:T(8,128)(2,1)S(1)}, u32[]{:S(2)}, u32[]{:S(2)}) collective-permute-start(bf16[64,512]{1,0:T(8,128)(2,1)S(1)} %get-tuple-element.125.refs_2_), channel_id=1, source_target_pairs={{0,8},{2,10},{4,12},{6,14},{8,0},{10,2},{12,4},{14,6},{16,24},{18,... | collective-permute-start | bytes 196616 | tf_op jit(solution)/shard_map/ppermute | solution.py:482
  66.7 7.5 %collective-permute-start.25 = (bf16[64,512]{1,0:T(8,128)(2,1)S(1)}, bf16[64,512]{1,0:T(8,128)(2,1)S(1)}, u32[]{:S(2)}, u32[]{:S(2)}) collective-permute-start(bf16[64,512]{1,0:T(8,128)(2,1)S(1)} %get-tuple-element.126.refs_3_), channel_id=1, source_target_pairs={{0,16},{2,18},{4,20},{6,22},{8,24},{10,26},{12,28},{14,30},{16,0},... | collective-permute-start | bytes 196616 | tf_op jit(solution)/shard_map/ppermute | solution.py:482
  68.1 6.8 %collective-permute-start.26 = (bf16[64,512]{1,0:T(8,128)(2,1)S(1)}, bf16[64,512]{1,0:T(8,128)(2,1)S(1)}, u32[]{:S(2)}, u32[]{:S(2)}) collective-permute-start(bf16[64,512]{1,0:T(8,128)(2,1)S(1)} %get-tuple-element.127.refs_4_), channel_id=1, source_target_pairs={{0,24},{2,26},{4,28},{6,30},{8,16},{10,18},{12,20},{14,22},{16,8},... | collective-permute-start | bytes 196616 | tf_op jit(solution)/shard_map/ppermute | solution.py:482
  70.5 6.9 %collective-permute-start.28 = (bf16[128,512]{1,0:T(8,128)(2,1)S(1)}, bf16[128,512]{1,0:T(8,128)(2,1)S(1)}, u32[]{:S(2)}, u32[]{:S(2)}) collective-permute-start(bf16[128,512]{1,0:T(8,128)(2,1)S(1)} %copy-done.1), channel_id=1, source_target_pairs={{0,8},{2,10},{4,12},{6,14},{8,0},{10,2},{12,4},{14,6},{16,24},{18,... | collective-permute-start | bytes 393224 | tf_op jit(solution)/shard_map/ppermute | solution.py:482
  70.5 8.4 %collective-permute-start.29 = (bf16[128,512]{1,0:T(8,128)(2,1)S(1)}, bf16[128,512]{1,0:T(8,128)(2,1)S(1)}, u32[]{:S(2)}, u32[]{:S(2)}) collective-permute-start(bf16[128,512]{1,0:T(8,128)(2,1)S(1)} %collective-permute-done.23.refs_2_), channel_id=1, source_target_pairs={{0,8},{2,10},{4,12},{6,14},{8,0},{10,2},{12,4},{14,6},{16,24},{18,... | collective-permute-start | bytes 393224 | tf_op jit(solution)/shard_map/ppermute | solution.py:482
  79.5 7.6 %collective-permute-start.30 = (bf16[32,2944]{1,0:T(8,128)(2,1)S(1)}, bf16[32,2944]{1,0:T(8,128)(2,1)S(1)}, u32[]{:S(2)}, u32[]{:S(2)}) collective-permute-start(bf16[32,2944]{1,0:T(8,128)(2,1)S(1)} %get-tuple-element.138), channel_id=1, source_target_pairs={{0,2},{2,0},{4,6},{6,4},{8,10},{10,8},{12,14},{14,12},{16,18},{18,... | collective-permute-start | bytes 565256 | tf_op jit(solution)/shard_map/ppermute | solution.py:482
  80.8 9.5 %collective-permute-start.31 = (bf16[32,2944]{1,0:T(8,128)(2,1)S(1)}, bf16[32,2944]{1,0:T(8,128)(2,1)S(1)}, u32[]{:S(2)}, u32[]{:S(2)}) collective-permute-start(bf16[32,2944]{1,0:T(8,128)(2,1)S(1)} %get-tuple-element.139), channel_id=1, source_target_pairs={{0,4},{2,6},{4,0},{6,2},{8,12},{10,14},{12,8},{14,10},{16,20},{18,... | collective-permute-start | bytes 565256 | tf_op jit(solution)/shard_map/ppermute | solution.py:482
  82.2 8.1 %collective-permute-start.32 = (bf16[32,2944]{1,0:T(8,128)(2,1)S(1)}, bf16[32,2944]{1,0:T(8,128)(2,1)S(1)}, u32[]{:S(2)}, u32[]{:S(2)}) collective-permute-start(bf16[32,2944]{1,0:T(8,128)(2,1)S(1)} %get-tuple-element.140), channel_id=1, source_target_pairs={{0,6},{2,4},{4,2},{6,0},{8,14},{10,12},{12,10},{14,8},{16,22},{18,... | collective-permute-start | bytes 565256 | tf_op jit(solution)/shard_map/ppermute | solution.py:482
  (18 other events, 114.7 us)
Sparse Core Ops, SparseCore 0:
  13.8 54.1 all-gather.1

commit v12 on v11

--- a/solution.py
+++ b/solution.py
@@ -245,56 +245,58 @@
     )(*blocks, *weights)
 
 
-def chip_sum_kernel(count, mine_ref, *refs):
-    theirs, out_refs = refs[:count], refs[count:]
+def chip_sum_kernel(count, *refs):
+    mine, theirs, out_refs = refs[:2], refs[2 : 2 + count], refs[2 + count :]
     part = out_refs[0].shape[1]
     start = 0
-    for theirs_ref in theirs:
-        rows = slice(start, start + theirs_ref.shape[0])
-        start = rows.stop
-        for d, ref in enumerate(out_refs):
-            at = slice(d * part, (d + 1) * part)
-            total = mine_ref[rows, at].astype(jnp.float32) + theirs_ref[:, at].astype(jnp.float32)
-            ref[rows, :] = total.astype(jnp.bfloat16)
+    for own_ref in mine:
+        first = start
+        while start < first + own_ref.shape[0]:
+            ref, theirs = theirs[0], theirs[1:]
+            size = ref.shape[0]
+            own = slice(start - first, start - first + size)
+            for d, out_ref in enumerate(out_refs):
+                at = slice(d * part, (d + 1) * part)
+                total = own_ref[own, at].astype(jnp.float32) + ref[:, at].astype(jnp.float32)
+                out_ref[start : start + size, :] = total.astype(jnp.bfloat16)
+            start += size
 
 
 def chip_sum(mine, theirs):
-    rows, width = mine.shape
+    rows, width = sum(value.shape[0] for value in mine), mine[0].shape[1]
     return pl.pallas_call(
         functools.partial(chip_sum_kernel, len(theirs)),
         out_shape=(pltpu.VMEM((rows, width // PLANE), jnp.bfloat16),) * PLANE,
-        in_specs=[VMEM] * (1 + len(theirs)),
+        in_specs=[VMEM] * (2 + len(theirs)),
         out_specs=(VMEM,) * PLANE,
-        compiler_params=params(2),
+        compiler_params=params(4),
         name="chip_sum",
-    )(mine, *theirs)
+    )(*mine, *theirs)
 
 
 def plane_sum_kernel(depth, *refs):
-    near, far, out_refs = refs[:PLANE], refs[PLANE : 2 * PLANE], refs[2 * PLANE :]
-    group = far[0].shape[0]
+    in_refs, out_refs = refs[:PLANE], refs[PLANE:]
+    group = in_refs[0].shape[0] // PLANE
     rows = group // depth
     for k in range(PLANE):
         for z in range(depth):
             total = 0.0
             for d in range(PLANE):
-                block = k ^ d
-                ref, skip = (far[d], 0) if block == PLANE - 1 else (near[d], block * group)
-                start = skip + z * rows
-                total = total + ref[start : start + rows, :].astype(jnp.float32)
+                start = (k ^ d) * group + z * rows
+                total = total + in_refs[d][start : start + rows, :].astype(jnp.float32)
             out_refs[z][k * rows : (k + 1) * rows, :] = total.astype(jnp.bfloat16)
 
 
-def plane_sum(near, far, depth):
-    rows, part = far[0].shape
+def plane_sum(parts, depth):
+    rows, part = parts[0].shape
     return pl.pallas_call(
         functools.partial(plane_sum_kernel, depth),
-        out_shape=(pltpu.VMEM((PLANE * rows // depth, part), jnp.bfloat16),) * depth,
-        in_specs=[VMEM] * (2 * PLANE),
+        out_shape=(pltpu.VMEM((rows // depth, part), jnp.bfloat16),) * depth,
+        in_specs=[VMEM] * PLANE,
         out_specs=(VMEM,) * depth,
         compiler_params=params(4),
         name="plane_sum",
-    )(*near, *far)
+    )(*parts)
 
 
 def second_norm_kernel(depth, *refs):
@@ -499,28 +501,27 @@
     tokens, *firsts = first_norm(
         (mine,), (to_core(theirs),), residual, attn_gain[None, :], meta, depth
     )
-    tokens, q_own = lax.optimization_barrier((tokens, q_weight))
+    tokens, q_own, kv_own = lax.optimization_barrier((tokens, q_weight, kv_weight))
     q_rows = lax.all_gather(q_own, "expert", axis=0, tiled=True, axis_index_groups=lines)
     weights = load((w_gate, w_up, w_down), (tokens,))
     line = to_z([tokens] * depth)
-    *line, gate, up, down = lax.optimization_barrier((*line, *weights))
+    *line, gate, up, down, kv_own = lax.optimization_barrier((*line, *weights, kv_own))
     weights = (gate, up, down)
+    kv_rows = [kv_own, to_expert(kv_own, PLANE)]
     near = to_plane(pack(line, firsts))
+    near[2], kv_rows[1] = lax.optimization_barrier((near[2], kv_rows[1]))
     cut = near[0].shape[0] // 2
     one, two = near[1][:cut], near[2][cut:]
     far = [to_expert(one, 2), to_expert(two, 1)]
-    mine, *theirs = experts((*near, *map(to_core, near)), weights, depth, len(near))
-    near_sum = chip_sum(mine, list(map(to_core, theirs)))
+    near_mine, *near_theirs = experts((*near, *map(to_core, near)), weights, depth, len(near))
+    theirs = list(map(to_core, near_theirs))
+    near_mine, *far = lax.optimization_barrier((near_mine, *far))
     far_both = [*far, *map(to_core, far)]
-    tied = lax.optimization_barrier((*near_sum, *far_both))
-    near_sum, far_both = tied[:PLANE], tied[PLANE:]
-    mine, *theirs = experts(far_both, weights, depth, 1)
-    far_sum = chip_sum(mine, list(map(to_core, theirs)))
-    *far_sum, kv_own = lax.optimization_barrier((*far_sum, kv_weight))
-    kv_rows = [kv_own, to_expert(kv_own, PLANE), to_expert(kv_own, 2 * PLANE)]
-    *parts, kv_rows[2] = lax.optimization_barrier(
-        (*plane_sum(to_plane(near_sum), to_plane(far_sum), depth), kv_rows[2])
-    )
+    far_mine, *far_theirs = experts(far_both, weights, depth, 1)
+    theirs += map(to_core, far_theirs)
+    parts = to_plane(chip_sum((near_mine, far_mine), theirs))
+    kv_rows.append(to_expert(kv_own, 2 * PLANE))
+    *parts, kv_rows[2] = lax.optimization_barrier((*plane_sum(parts, depth), kv_rows[2]))
     kv_rows.append(to_expert(kv_rows[2], PLANE))
     (q_rows,) = load((q_rows,), parts)
     parts = to_z(parts)

time: 98.2 us -> 103 us (1.049)
  waiting for transfers between devices: 33.9 us -> 43.7 us
  starting transfers between devices: 30.9 us -> 26.1 us
    ppermute x22 -> x19, waiting for transfers between devices: 32 us -> 40.3 us  [to_expert(): lax.ppermute(value, 'expert', [(i, i ^ offset) for i in range(n_expert)])]
    ppermute x22 -> x19, starting transfers between devices: 29 us -> 23.6 us  [to_expert(): lax.ppermute(value, 'expert', [(i, i ^ offset) for i in range(n_expert)])]
    ppermute x11, waiting for transfers between devices: 1.81 us -> 3.34 us  [to_core(): return lax.ppermute(value, 'tensor', [(0, 1), (1, 0)])]
  transfers between devices with their start and end apart: 34 -> 31, of which waited for: 20 -> 16; matrix products, arithmetic and copies ran while one was open for 1% -> 0% of each run, Pallas kernels for 12% -> 12%
where the time goes in v12:
time: 103 us
  waiting for transfers between devices  43.7 us (42%)
  starting transfers between devices  26.1 us (25%)
  Pallas kernels  18.4 us (18%)
  between operations  14.3 us (14%)
    ppermute x19, waiting for transfers between devices, to_expert(): lax.ppermute(value, 'expert', [(i, i ^ offset) for i in range(n_expert)])  40.3 us
    ppermute x19, starting transfers between devices, to_expert(): lax.ppermute(value, 'expert', [(i, i ^ offset) for i in range(n_expert)])  23.6 us
    pallas_call x2, Pallas kernels, experts(): pl.pallas_call(functools.partial(expert_kernel, depth, chunk, len(blocks)...  6.05 us
    pallas_call x2, Pallas kernels, load(): pl.pallas_call(functools.partial(load_kernel, count), out_shape=tuple((pl...  5.42 us
    pallas_call x1, Pallas kernels, out_projection(): pl.pallas_call(functools.partial(out_projection_kernel, chunk), out_shape...  4.77 us
    ppermute x11, waiting for transfers between devices, to_core(): return lax.ppermute(value, 'tensor', [(0, 1), (1, 0)])  3.34 us
    ppermute x11, starting transfers between devices, to_core(): return lax.ppermute(value, 'tensor', [(0, 1), (1, 0)])  2.47 us
  transfers between devices with their start and end apart: 31, of which 16 were waited for; matrix products, arithmetic and copies ran while one was open for 0% of the time, Pallas kernels for 12%

profile of v12, /device:TPU:0, one launch (start us, length us, event | category | flops | bytes accessed | tf_op | source)
XLA Modules:
  0.0 103.1 jit_solution(6648891696777156833)
XLA Ops:
  7.3 4.8 %out_projection.1 = (f32[16,2048]{1,0:T(8,128)S(1)}, f32[16,2048]{1,0:T(8,128)S(1)}) custom-call(bf16[32,2048]{1,0:T(8,128)(2,1)} %a_hbm.1, bf16[2048,2048]{1,0:T(8,128)(2,1)} %w_hbm.1), custom_call_target="tpu_custom_call" | custom-call | tf_op jit(solution)/shard_map/out_projection/pallas_call | solution.py:77
  13.7 3.0 %collective-permute-start.1 = (bf16[16,2176]{1,0:T(8,128)(2,1)S(1)}, bf16[16,2176]{1,0:T(8,128)(2,1)S(1)}, u32[]{:S(2)}, u32[]{:S(2)}) collective-permute-start(bf16[16,2176]{1,0:T(8,128)(2,1)S(1)} %get-tuple-element.70.refs_3_.refs_0_), channel_id=1, source_target_pairs={{0,8},{2,10},{4,12},{6,14},{8,0},{10,2},{12,4},{14,6},{16,24},{18,... | collective-permute-start | bytes 208904 | tf_op jit(solution)/shard_map/ppermute | solution.py:484
  16.7 2.6 %collective-permute-start.2 = (bf16[16,2176]{1,0:T(8,128)(2,1)S(1)}, bf16[16,2176]{1,0:T(8,128)(2,1)S(1)}, u32[]{:S(2)}, u32[]{:S(2)}) collective-permute-start(bf16[16,2176]{1,0:T(8,128)(2,1)S(1)} %get-tuple-element.70.refs_3_.refs_0_), channel_id=1, source_target_pairs={{0,16},{2,18},{4,20},{6,22},{8,24},{10,26},{12,28},{14,30},{16,0},... | collective-permute-start | bytes 208904 | tf_op jit(solution)/shard_map/ppermute | solution.py:484
  19.3 3.8 %load_weights.2 = (bf16[1,2048,768]{2,1,0:T(8,128)(2,1)S(1)}, bf16[1,2048,768]{2,1,0:T(8,128)(2,1)S(1)}, bf16[1,768,2048]{2,1,0:T(8,128)(2,1)S(1)}) custom-call(bf16[1,2048,768]{2,1,0:T(8,128)(2,1)} %refs_0_.1, bf16[1,2048,768]{2,1,0:T(8,128)(2,1)} %refs_1_.1, bf16[1,768,2048]{2,1,0:T(8,128)(2,1)} %refs_2_.3, ...), custom_call_target="tpu_custom_call" | custom-call | tf_op jit(solution)/shard_map/load_weights/pallas_call | solution.py:171
  23.2 1.4 %collective-permute-done.2.refs_2_ = bf16[16,2176]{1,0:T(8,128)(2,1)S(1)} collective-permute-done((bf16[16,2176]{1,0:T(8,128)(2,1)S(1)}, bf16[16,2176]{1,0:T(8,128)(2,1)S(1)}, u32[]{:S(2)}, u32[]{:S(2)}) %collective-permute-start.2) | collective-permute-done | bytes 69664 | tf_op jit(solution)/shard_map/ppermute | solution.py:484
  25.6 1.6 %collective-permute-start.5 = (bf16[64,2432]{1,0:T(8,128)(2,1)S(1)}, bf16[64,2432]{1,0:T(8,128)(2,1)S(1)}, u32[]{:S(2)}, u32[]{:S(2)}) collective-permute-start(bf16[64,2432]{1,0:T(8,128)(2,1)S(1)} %get-tuple-element.80), channel_id=1, source_target_pairs={{0,4},{2,6},{4,0},{6,2},{8,12},{10,14},{12,8},{14,10},{16,20},{18,... | collective-permute-start | bytes 933896 | tf_op jit(solution)/shard_map/ppermute | solution.py:484
  27.2 1.5 %collective-permute-start.4 = (bf16[64,2432]{1,0:T(8,128)(2,1)S(1)}, bf16[64,2432]{1,0:T(8,128)(2,1)S(1)}, u32[]{:S(2)}, u32[]{:S(2)}) collective-permute-start(bf16[64,2432]{1,0:T(8,128)(2,1)S(1)} %get-tuple-element.79), channel_id=1, source_target_pairs={{0,2},{2,0},{4,6},{6,4},{8,10},{10,8},{12,14},{14,12},{16,18},{18,... | collective-permute-start | bytes 933896 | tf_op jit(solution)/shard_map/ppermute | solution.py:484
  28.7 1.2 %collective-permute-start.6 = (bf16[128,512]{1,0:T(8,128)(2,1)S(1)}, bf16[128,512]{1,0:T(8,128)(2,1)S(1)}, u32[]{:S(2)}, u32[]{:S(2)}) collective-permute-start(bf16[128,512]{1,0:T(8,128)(2,1)S(1)} %copy-done.1), channel_id=1, source_target_pairs={{0,8},{2,10},{4,12},{6,14},{8,0},{10,2},{12,4},{14,6},{16,24},{18,... | collective-permute-start | bytes 393224 | tf_op jit(solution)/shard_map/ppermute | solution.py:484
  29.8 14.1 %collective-permute-done.6.refs_1_ = bf16[128,512]{1,0:T(8,128)(2,1)S(1)} collective-permute-done((bf16[128,512]{1,0:T(8,128)(2,1)S(1)}, bf16[128,512]{1,0:T(8,128)(2,1)S(1)}, u32[]{:S(2)}, u32[]{:S(2)}) %collective-permute-start.6) | collective-permute-done | bytes 131104 | tf_op jit(solution)/shard_map/ppermute | solution.py:484
  44.5 1.2 %collective-permute-start.10 = (bf16[32,2432]{1,0:T(8,128)(2,1)S(1)}, bf16[32,2432]{1,0:T(8,128)(2,1)S(1)}, u32[]{:S(2)}, u32[]{:S(2)}) collective-permute-start(bf16[32,2432]{1,0:T(8,128)(2,1)S(1)} %slice.8), channel_id=1, source_target_pairs={{0,4},{2,6},{4,0},{6,2},{8,12},{10,14},{12,8},{14,10},{16,20},{18,... | collective-permute-start | bytes 466952 | tf_op jit(solution)/shard_map/ppermute | solution.py:484
  46.8 4.1 %experts.2 = (bf16[192,2048]{1,0:T(8,128)(2,1)S(1)}, bf16[64,2048]{1,0:T(8,128)(2,1)S(1)}, bf16[64,2048]{1,0:T(8,128)(2,1)S(1)}, bf16[64,2048]{1,0:T(8,128)(2,1)S(1)}) custom-call(bf16[64,2432]{1,0:T(8,128)(2,1)S(1)} %get-tuple-element.78.refs_0_.refs_4_, bf16[64,2432]{1,0:T(8,128)(2,1)S(1)} %collective-permute-done.4.refs_1_.refs_5_, ...), custom_call_target="tpu_custom_call" | custom-call | flops 3623878656 | tf_op jit(solution)/shard_map/experts/pallas_call | solution.py:231
  53.1 2.0 %experts.3 = (bf16[64,2048]{1,0:T(8,128)(2,1)S(1)}, bf16[64,2048]{1,0:T(8,128)(2,1)S(1)}) custom-call(bf16[32,2432]{1,0:T(8,128)(2,1)S(1)} %collective-permute-done.10.refs_0_.refs_7_, bf16[32,2432]{1,0:T(8,128)(2,1)S(1)} %collective-permute-done.11.refs_1_.refs_8_, bf16[32,2432]{1,0:T(8,128)(2,1)S(1)} %collective-permute-done.12.refs_2_, ...), custom_call_target="tpu_custom_call" | custom-call | flops 1207959552 | tf_op jit(solution)/shard_map/experts/pallas_call | solution.py:231
  55.4 1.2 %collective-permute-done.17.refs_5_ = bf16[64,2048]{1,0:T(8,128)(2,1)S(1)} collective-permute-done((bf16[64,2048]{1,0:T(8,128)(2,1)S(1)}, bf16[64,2048]{1,0:T(8,128)(2,1)S(1)}, u32[]{:S(2)}, u32[]{:S(2)}) %collective-permute-start.17) | collective-permute-done | bytes 262176 | tf_op jit(solution)/shard_map/ppermute | solution.py:481
  59.0 1.4 %collective-permute-start.20 = (bf16[256,512]{1,0:T(8,128)(2,1)S(1)}, bf16[256,512]{1,0:T(8,128)(2,1)S(1)}, u32[]{:S(2)}, u32[]{:S(2)}) collective-permute-start(bf16[256,512]{1,0:T(8,128)(2,1)S(1)} %get-tuple-element.98), channel_id=1, source_target_pairs={{0,6},{2,4},{4,2},{6,0},{8,14},{10,12},{12,10},{14,8},{16,22},{18,... | collective-permute-start | bytes 786440 | tf_op jit(solution)/shard_map/ppermute | solution.py:484
  60.5 5.6 %collective-permute-done.18.refs_1_ = bf16[256,512]{1,0:T(8,128)(2,1)S(1)} collective-permute-done((bf16[256,512]{1,0:T(8,128)(2,1)S(1)}, bf16[256,512]{1,0:T(8,128)(2,1)S(1)}, u32[]{:S(2)}, u32[]{:S(2)}) %collective-permute-start.18) | collective-permute-done | bytes 262176 | tf_op jit(solution)/shard_map/ppermute | solution.py:484
  66.1 5.7 %collective-permute-done.19.refs_2_ = bf16[256,512]{1,0:T(8,128)(2,1)S(1)} collective-permute-done((bf16[256,512]{1,0:T(8,128)(2,1)S(1)}, bf16[256,512]{1,0:T(8,128)(2,1)S(1)}, u32[]{:S(2)}, u32[]{:S(2)}) %collective-permute-start.19) | collective-permute-done | bytes 262176 | tf_op jit(solution)/shard_map/ppermute | solution.py:484
  72.1 3.0 %collective-permute-start.23 = (bf16[64,512]{1,0:T(8,128)(2,1)S(1)}, bf16[64,512]{1,0:T(8,128)(2,1)S(1)}, u32[]{:S(2)}, u32[]{:S(2)}) collective-permute-start(bf16[64,512]{1,0:T(8,128)(2,1)S(1)} %get-tuple-element.105.refs_3_), channel_id=1, source_target_pairs={{0,16},{2,18},{4,20},{6,22},{8,24},{10,26},{12,28},{14,30},{16,0},... | collective-permute-start | bytes 196616 | tf_op jit(solution)/shard_map/ppermute | solution.py:484
  75.1 1.3 %collective-permute-start.24 = (bf16[64,512]{1,0:T(8,128)(2,1)S(1)}, bf16[64,512]{1,0:T(8,128)(2,1)S(1)}, u32[]{:S(2)}, u32[]{:S(2)}) collective-permute-start(bf16[64,512]{1,0:T(8,128)(2,1)S(1)} %get-tuple-element.106.refs_4_), channel_id=1, source_target_pairs={{0,24},{2,26},{4,28},{6,30},{8,16},{10,18},{12,20},{14,22},{16,8},... | collective-permute-start | bytes 196616 | tf_op jit(solution)/shard_map/ppermute | solution.py:484
  76.5 1.6 %load_weights.3.q_ref = bf16[512,2048]{1,0:T(8,128)(2,1)S(1)} custom-call(bf16[512,2048]{1,0:T(8,128)(2,1)} %all-gather.2.cloned.1.call-done.refs_0_, bf16[64,512]{1,0:T(8,128)(2,1)S(1)} %get-tuple-element.108.refs_1_.refs_0_, bf16[64,512]{1,0:T(8,128)(2,1)S(1)} %get-tuple-element.104.refs_2_, bf16[64,512]{1,0:T(8,128)(2,1)S(1)} %get-tuple-element.105.refs_3_, ...), custom_call_target="tpu_custom_call" | custom-call | tf_op jit(solution)/shard_map/load_weights/pallas_call | solution.py:171
  78.1 1.4 %collective-permute-done.23.refs_2_ = bf16[64,512]{1,0:T(8,128)(2,1)S(1)} collective-permute-done((bf16[64,512]{1,0:T(8,128)(2,1)S(1)}, bf16[64,512]{1,0:T(8,128)(2,1)S(1)}, u32[]{:S(2)}, u32[]{:S(2)}) %collective-permute-start.23) | collective-permute-done | bytes 65568 | tf_op jit(solution)/shard_map/ppermute | solution.py:484
  79.5 2.1 %collective-permute-done.24.refs_3_ = bf16[64,512]{1,0:T(8,128)(2,1)S(1)} collective-permute-done((bf16[64,512]{1,0:T(8,128)(2,1)S(1)}, bf16[64,512]{1,0:T(8,128)(2,1)S(1)}, u32[]{:S(2)}, u32[]{:S(2)}) %collective-permute-start.24) | collective-permute-done | bytes 65568 | tf_op jit(solution)/shard_map/ppermute | solution.py:484
  85.7 1.5 %collective-permute-start.29 = (bf16[32,2944]{1,0:T(8,128)(2,1)S(1)}, bf16[32,2944]{1,0:T(8,128)(2,1)S(1)}, u32[]{:S(2)}, u32[]{:S(2)}) collective-permute-start(bf16[32,2944]{1,0:T(8,128)(2,1)S(1)} %get-tuple-element.120), channel_id=1, source_target_pairs={{0,6},{2,4},{4,2},{6,0},{8,14},{10,12},{12,10},{14,8},{16,22},{18,... | collective-permute-start | bytes 565256 | tf_op jit(solution)/shard_map/ppermute | solution.py:484
  87.3 4.1 %collective-permute-done.27.refs_1_ = bf16[32,2944]{1,0:T(8,128)(2,1)S(1)} collective-permute-done((bf16[32,2944]{1,0:T(8,128)(2,1)S(1)}, bf16[32,2944]{1,0:T(8,128)(2,1)S(1)}, u32[]{:S(2)}, u32[]{:S(2)}) %collective-permute-start.27) | collective-permute-done | bytes 188448 | tf_op jit(solution)/shard_map/ppermute | solution.py:484
  91.4 4.0 %collective-permute-done.28.refs_2_ = bf16[32,2944]{1,0:T(8,128)(2,1)S(1)} collective-permute-done((bf16[32,2944]{1,0:T(8,128)(2,1)S(1)}, bf16[32,2944]{1,0:T(8,128)(2,1)S(1)}, u32[]{:S(2)}, u32[]{:S(2)}) %collective-permute-start.28) | collective-permute-done | bytes 188448 | tf_op jit(solution)/shard_map/ppermute | solution.py:484
  (76 shorter events, 14.5 us)
Async XLA Ops:
  7.2 69.2 %all-gather.2.cloned.1.call-start = ((), (), s32[]{:S(2)}) async-start(), calls=%async_computation | async-start | bytes 2621440 | tf_op jit(solution)/shard_map/all_gather | solution.py:505
  13.7 9.4 %collective-permute-start.1 = (bf16[16,2176]{1,0:T(8,128)(2,1)S(1)}, bf16[16,2176]{1,0:T(8,128)(2,1)S(1)}, u32[]{:S(2)}, u32[]{:S(2)}) collective-permute-start(bf16[16,2176]{1,0:T(8,128)(2,1)S(1)} %get-tuple-element.70.refs_3_.refs_0_), channel_id=1, source_target_pairs={{0,8},{2,10},{4,12},{6,14},{8,0},{10,2},{12,4},{14,6},{16,24},{18,... | collective-permute-start | bytes 208904 | tf_op jit(solution)/shard_map/ppermute | solution.py:484
  16.7 7.8 %collective-permute-start.2 = (bf16[16,2176]{1,0:T(8,128)(2,1)S(1)}, bf16[16,2176]{1,0:T(8,128)(2,1)S(1)}, u32[]{:S(2)}, u32[]{:S(2)}) collective-permute-start(bf16[16,2176]{1,0:T(8,128)(2,1)S(1)} %get-tuple-element.70.refs_3_.refs_0_), channel_id=1, source_target_pairs={{0,16},{2,18},{4,20},{6,22},{8,24},{10,26},{12,28},{14,30},{16,0},... | collective-permute-start | bytes 208904 | tf_op jit(solution)/shard_map/ppermute | solution.py:484
  19.3 6.2 %collective-permute-start.3 = (bf16[16,2176]{1,0:T(8,128)(2,1)S(1)}, bf16[16,2176]{1,0:T(8,128)(2,1)S(1)}, u32[]{:S(2)}, u32[]{:S(2)}) collective-permute-start(bf16[16,2176]{1,0:T(8,128)(2,1)S(1)} %get-tuple-element.70.refs_3_.refs_0_), channel_id=1, source_target_pairs={{0,24},{2,26},{4,28},{6,30},{8,16},{10,18},{12,20},{14,22},{16,8},... | collective-permute-start | bytes 208904 | tf_op jit(solution)/shard_map/ppermute | solution.py:484
  25.6 18.4 %collective-permute-start.5 = (bf16[64,2432]{1,0:T(8,128)(2,1)S(1)}, bf16[64,2432]{1,0:T(8,128)(2,1)S(1)}, u32[]{:S(2)}, u32[]{:S(2)}) collective-permute-start(bf16[64,2432]{1,0:T(8,128)(2,1)S(1)} %get-tuple-element.80), channel_id=1, source_target_pairs={{0,4},{2,6},{4,0},{6,2},{8,12},{10,14},{12,8},{14,10},{16,20},{18,... | collective-permute-start | bytes 933896 | tf_op jit(solution)/shard_map/ppermute | solution.py:484
  27.2 16.8 %collective-permute-start.4 = (bf16[64,2432]{1,0:T(8,128)(2,1)S(1)}, bf16[64,2432]{1,0:T(8,128)(2,1)S(1)}, u32[]{:S(2)}, u32[]{:S(2)}) collective-permute-start(bf16[64,2432]{1,0:T(8,128)(2,1)S(1)} %get-tuple-element.79), channel_id=1, source_target_pairs={{0,2},{2,0},{4,6},{6,4},{8,10},{10,8},{12,14},{14,12},{16,18},{18,... | collective-permute-start | bytes 933896 | tf_op jit(solution)/shard_map/ppermute | solution.py:484
  28.7 15.3 %collective-permute-start.6 = (bf16[128,512]{1,0:T(8,128)(2,1)S(1)}, bf16[128,512]{1,0:T(8,128)(2,1)S(1)}, u32[]{:S(2)}, u32[]{:S(2)}) collective-permute-start(bf16[128,512]{1,0:T(8,128)(2,1)S(1)} %copy-done.1), channel_id=1, source_target_pairs={{0,8},{2,10},{4,12},{6,14},{8,0},{10,2},{12,4},{14,6},{16,24},{18,... | collective-permute-start | bytes 393224 | tf_op jit(solution)/shard_map/ppermute | solution.py:484
  29.8 16.9 %collective-permute-start.7 = (bf16[64,2432]{1,0:T(8,128)(2,1)S(1)}, bf16[64,2432]{1,0:T(8,128)(2,1)S(1)}, u32[]{:S(2)}, u32[]{:S(2)}) collective-permute-start(bf16[64,2432]{1,0:T(8,128)(2,1)S(1)} %get-tuple-element.78.refs_0_.refs_4_), channel_id=1, source_target_pairs={{0,1},{1,0},{2,3},{3,2},{4,5},{5,4},{6,7},{7,6},{8,9},{9,8},{10,11... | collective-permute-start | bytes 933896 | tf_op jit(solution)/shard_map/ppermute | solution.py:481
  44.5 6.3 %collective-permute-start.10 = (bf16[32,2432]{1,0:T(8,128)(2,1)S(1)}, bf16[32,2432]{1,0:T(8,128)(2,1)S(1)}, u32[]{:S(2)}, u32[]{:S(2)}) collective-permute-start(bf16[32,2432]{1,0:T(8,128)(2,1)S(1)} %slice.8), channel_id=1, source_target_pairs={{0,4},{2,6},{4,0},{6,2},{8,12},{10,14},{12,8},{14,10},{16,20},{18,... | collective-permute-start | bytes 466952 | tf_op jit(solution)/shard_map/ppermute | solution.py:484
  45.7 5.7 %collective-permute-start.11 = (bf16[32,2432]{1,0:T(8,128)(2,1)S(1)}, bf16[32,2432]{1,0:T(8,128)(2,1)S(1)}, u32[]{:S(2)}, u32[]{:S(2)}) collective-permute-start(bf16[32,2432]{1,0:T(8,128)(2,1)S(1)} %slice.7), channel_id=1, source_target_pairs={{0,2},{2,0},{4,6},{6,4},{8,10},{10,8},{12,14},{14,12},{16,18},{18,... | collective-permute-start | bytes 466952 | tf_op jit(solution)/shard_map/ppermute | solution.py:484
  52.0 3.5 %collective-permute-start.14 = (bf16[64,2048]{1,0:T(8,128)(2,1)S(1)}, bf16[64,2048]{1,0:T(8,128)(2,1)S(1)}, u32[]{:S(2)}, u32[]{:S(2)}) collective-permute-start(bf16[64,2048]{1,0:T(8,128)(2,1)S(1)} %get-tuple-element.91), channel_id=1, source_target_pairs={{0,1},{1,0},{2,3},{3,2},{4,5},{5,4},{6,7},{7,6},{8,9},{9,8},{10,11... | collective-permute-start | bytes 786440 | tf_op jit(solution)/shard_map/ppermute | solution.py:481
  52.0 3.5 %collective-permute-start.15 = (bf16[64,2048]{1,0:T(8,128)(2,1)S(1)}, bf16[64,2048]{1,0:T(8,128)(2,1)S(1)}, u32[]{:S(2)}, u32[]{:S(2)}) collective-permute-start(bf16[64,2048]{1,0:T(8,128)(2,1)S(1)} %get-tuple-element.92), channel_id=1, source_target_pairs={{0,1},{1,0},{2,3},{3,2},{4,5},{5,4},{6,7},{7,6},{8,9},{9,8},{10,11... | collective-permute-start | bytes 786440 | tf_op jit(solution)/shard_map/ppermute | solution.py:481
  52.5 3.0 %collective-permute-start.16 = (bf16[64,2048]{1,0:T(8,128)(2,1)S(1)}, bf16[64,2048]{1,0:T(8,128)(2,1)S(1)}, u32[]{:S(2)}, u32[]{:S(2)}) collective-permute-start(bf16[64,2048]{1,0:T(8,128)(2,1)S(1)} %get-tuple-element.93), channel_id=1, source_target_pairs={{0,1},{1,0},{2,3},{3,2},{4,5},{5,4},{6,7},{7,6},{8,9},{9,8},{10,11... | collective-permute-start | bytes 786440 | tf_op jit(solution)/shard_map/ppermute | solution.py:481
  56.9 9.2 %collective-permute-start.18 = (bf16[256,512]{1,0:T(8,128)(2,1)S(1)}, bf16[256,512]{1,0:T(8,128)(2,1)S(1)}, u32[]{:S(2)}, u32[]{:S(2)}) collective-permute-start(bf16[256,512]{1,0:T(8,128)(2,1)S(1)} %get-tuple-element.96), channel_id=1, source_target_pairs={{0,2},{2,0},{4,6},{6,4},{8,10},{10,8},{12,14},{14,12},{16,18},{18,... | collective-permute-start | bytes 786440 | tf_op jit(solution)/shard_map/ppermute | solution.py:484
  58.0 13.8 %collective-permute-start.19 = (bf16[256,512]{1,0:T(8,128)(2,1)S(1)}, bf16[256,512]{1,0:T(8,128)(2,1)S(1)}, u32[]{:S(2)}, u32[]{:S(2)}) collective-permute-start(bf16[256,512]{1,0:T(8,128)(2,1)S(1)} %get-tuple-element.97), channel_id=1, source_target_pairs={{0,4},{2,6},{4,0},{6,2},{8,12},{10,14},{12,8},{14,10},{16,20},{18,... | collective-permute-start | bytes 786440 | tf_op jit(solution)/shard_map/ppermute | solution.py:484
  59.0 12.8 %collective-permute-start.20 = (bf16[256,512]{1,0:T(8,128)(2,1)S(1)}, bf16[256,512]{1,0:T(8,128)(2,1)S(1)}, u32[]{:S(2)}, u32[]{:S(2)}) collective-permute-start(bf16[256,512]{1,0:T(8,128)(2,1)S(1)} %get-tuple-element.98), channel_id=1, source_target_pairs={{0,6},{2,4},{4,2},{6,0},{8,14},{10,12},{12,10},{14,8},{16,22},{18,... | collective-permute-start | bytes 786440 | tf_op jit(solution)/shard_map/ppermute | solution.py:484
  60.5 11.5 %collective-permute-start.21 = (bf16[128,512]{1,0:T(8,128)(2,1)S(1)}, bf16[128,512]{1,0:T(8,128)(2,1)S(1)}, u32[]{:S(2)}, u32[]{:S(2)}) collective-permute-start(bf16[128,512]{1,0:T(8,128)(2,1)S(1)} %copy-done.1), channel_id=1, source_target_pairs={{0,16},{2,18},{4,20},{6,22},{8,24},{10,26},{12,28},{14,30},{16,0},... | collective-permute-start | bytes 393224 | tf_op jit(solution)/shard_map/ppermute | solution.py:484
  72.0 6.1 %collective-permute-start.22 = (bf16[64,512]{1,0:T(8,128)(2,1)S(1)}, bf16[64,512]{1,0:T(8,128)(2,1)S(1)}, u32[]{:S(2)}, u32[]{:S(2)}) collective-permute-start(bf16[64,512]{1,0:T(8,128)(2,1)S(1)} %get-tuple-element.104.refs_2_), channel_id=1, source_target_pairs={{0,8},{2,10},{4,12},{6,14},{8,0},{10,2},{12,4},{14,6},{16,24},{18,... | collective-permute-start | bytes 196616 | tf_op jit(solution)/shard_map/ppermute | solution.py:484
  72.1 7.5 %collective-permute-start.23 = (bf16[64,512]{1,0:T(8,128)(2,1)S(1)}, bf16[64,512]{1,0:T(8,128)(2,1)S(1)}, u32[]{:S(2)}, u32[]{:S(2)}) collective-permute-start(bf16[64,512]{1,0:T(8,128)(2,1)S(1)} %get-tuple-element.105.refs_3_), channel_id=1, source_target_pairs={{0,16},{2,18},{4,20},{6,22},{8,24},{10,26},{12,28},{14,30},{16,0},... | collective-permute-start | bytes 196616 | tf_op jit(solution)/shard_map/ppermute | solution.py:484
  75.1 6.5 %collective-permute-start.24 = (bf16[64,512]{1,0:T(8,128)(2,1)S(1)}, bf16[64,512]{1,0:T(8,128)(2,1)S(1)}, u32[]{:S(2)}, u32[]{:S(2)}) collective-permute-start(bf16[64,512]{1,0:T(8,128)(2,1)S(1)} %get-tuple-element.106.refs_4_), channel_id=1, source_target_pairs={{0,24},{2,26},{4,28},{6,30},{8,16},{10,18},{12,20},{14,22},{16,8},... | collective-permute-start | bytes 196616 | tf_op jit(solution)/shard_map/ppermute | solution.py:484
  76.4 5.7 %collective-permute-start.26 = (bf16[128,512]{1,0:T(8,128)(2,1)S(1)}, bf16[128,512]{1,0:T(8,128)(2,1)S(1)}, u32[]{:S(2)}, u32[]{:S(2)}) collective-permute-start(bf16[128,512]{1,0:T(8,128)(2,1)S(1)} %collective-permute-done.21.refs_2_), channel_id=1, source_target_pairs={{0,8},{2,10},{4,12},{6,14},{8,0},{10,2},{12,4},{14,6},{16,24},{18,... | collective-permute-start | bytes 393224 | tf_op jit(solution)/shard_map/ppermute | solution.py:484
  83.7 7.6 %collective-permute-start.27 = (bf16[32,2944]{1,0:T(8,128)(2,1)S(1)}, bf16[32,2944]{1,0:T(8,128)(2,1)S(1)}, u32[]{:S(2)}, u32[]{:S(2)}) collective-permute-start(bf16[32,2944]{1,0:T(8,128)(2,1)S(1)} %get-tuple-element.118), channel_id=1, source_target_pairs={{0,2},{2,0},{4,6},{6,4},{8,10},{10,8},{12,14},{14,12},{16,18},{18,... | collective-permute-start | bytes 565256 | tf_op jit(solution)/shard_map/ppermute | solution.py:484
  84.8 10.5 %collective-permute-start.28 = (bf16[32,2944]{1,0:T(8,128)(2,1)S(1)}, bf16[32,2944]{1,0:T(8,128)(2,1)S(1)}, u32[]{:S(2)}, u32[]{:S(2)}) collective-permute-start(bf16[32,2944]{1,0:T(8,128)(2,1)S(1)} %get-tuple-element.119), channel_id=1, source_target_pairs={{0,4},{2,6},{4,0},{6,2},{8,12},{10,14},{12,8},{14,10},{16,20},{18,... | collective-permute-start | bytes 565256 | tf_op jit(solution)/shard_map/ppermute | solution.py:484
  85.7 9.6 %collective-permute-start.29 = (bf16[32,2944]{1,0:T(8,128)(2,1)S(1)}, bf16[32,2944]{1,0:T(8,128)(2,1)S(1)}, u32[]{:S(2)}, u32[]{:S(2)}) collective-permute-start(bf16[32,2944]{1,0:T(8,128)(2,1)S(1)} %get-tuple-element.120), channel_id=1, source_target_pairs={{0,6},{2,4},{4,2},{6,0},{8,14},{10,12},{12,10},{14,8},{16,22},{18,... | collective-permute-start | bytes 565256 | tf_op jit(solution)/shard_map/ppermute | solution.py:484
  (15 other events, 110.9 us)
Sparse Core Ops, SparseCore 0:
  13.8 49.9 all-gather.1

commit v13 on v12

--- a/solution.py
+++ b/solution.py
@@ -501,15 +501,13 @@
     tokens, *firsts = first_norm(
         (mine,), (to_core(theirs),), residual, attn_gain[None, :], meta, depth
     )
-    tokens, q_own, kv_own = lax.optimization_barrier((tokens, q_weight, kv_weight))
+    tokens, q_own = lax.optimization_barrier((tokens, q_weight))
     q_rows = lax.all_gather(q_own, "expert", axis=0, tiled=True, axis_index_groups=lines)
     weights = load((w_gate, w_up, w_down), (tokens,))
     line = to_z([tokens] * depth)
-    *line, gate, up, down, kv_own = lax.optimization_barrier((*line, *weights, kv_own))
+    *line, gate, up, down = lax.optimization_barrier((*line, *weights))
     weights = (gate, up, down)
-    kv_rows = [kv_own, to_expert(kv_own, PLANE)]
     near = to_plane(pack(line, firsts))
-    near[2], kv_rows[1] = lax.optimization_barrier((near[2], kv_rows[1]))
     cut = near[0].shape[0] // 2
     one, two = near[1][:cut], near[2][cut:]
     far = [to_expert(one, 2), to_expert(two, 1)]
@@ -519,9 +517,12 @@
     far_both = [*far, *map(to_core, far)]
     far_mine, *far_theirs = experts(far_both, weights, depth, 1)
     theirs += map(to_core, far_theirs)
-    parts = to_plane(chip_sum((near_mine, far_mine), theirs))
-    kv_rows.append(to_expert(kv_own, 2 * PLANE))
-    *parts, kv_rows[2] = lax.optimization_barrier((*plane_sum(parts, depth), kv_rows[2]))
+    *sums, kv_own = lax.optimization_barrier((*chip_sum((near_mine, far_mine), theirs), kv_weight))
+    parts = to_plane(sums)
+    kv_rows = [kv_own, to_expert(kv_own, PLANE), to_expert(kv_own, 2 * PLANE)]
+    *parts, kv_rows[1], kv_rows[2] = lax.optimization_barrier(
+        (*plane_sum(parts, depth), *kv_rows[1:])
+    )
     kv_rows.append(to_expert(kv_rows[2], PLANE))
     (q_rows,) = load((q_rows,), parts)
     parts = to_z(parts)

time: 103 us -> 97.7 us (0.949)
  waiting for transfers between devices: 43.7 us -> 36.8 us
  starting transfers between devices: 26.1 us -> 27.6 us
    ppermute x19, waiting for transfers between devices: 40.3 us -> 34 us  [to_expert(): lax.ppermute(value, 'expert', [(i, i ^ offset) for i in range(n_expert)])]
    ppermute x19, starting transfers between devices: 23.6 us -> 25.6 us  [to_expert(): lax.ppermute(value, 'expert', [(i, i ^ offset) for i in range(n_expert)])]
  transfers between devices with their start and end apart: 31 -> 31, of which waited for: 16 -> 20; matrix products, arithmetic and copies ran while one was open for 0% -> 1% of each run, Pallas kernels for 12% -> 12%
where the time goes in v13:
time: 97.7 us; the launch traced here: 97.6 us
  waiting for transfers between devices  36.8 us (38%)
  starting transfers between devices  27.6 us (28%)
  Pallas kernels  18.4 us (19%)
  between operations  14.2 us (15%)
    ppermute x19, waiting for transfers between devices, to_expert(): lax.ppermute(value, 'expert', [(i, i ^ offset) for i in range(n_expert)])  34 us
    ppermute x19, starting transfers between devices, to_expert(): lax.ppermute(value, 'expert', [(i, i ^ offset) for i in range(n_expert)])  25.6 us
    pallas_call x2, Pallas kernels, experts(): pl.pallas_call(functools.partial(expert_kernel, depth, chunk, len(blocks)...  6.05 us
    pallas_call x2, Pallas kernels, load(): pl.pallas_call(functools.partial(load_kernel, count), out_shape=tuple((pl...  5.42 us
    pallas_call x1, Pallas kernels, out_projection(): pl.pallas_call(functools.partial(out_projection_kernel, chunk), out_shape...  4.77 us
    ppermute x11, waiting for transfers between devices, to_core(): return lax.ppermute(value, 'tensor', [(0, 1), (1, 0)])  2.79 us
    ppermute x11, starting transfers between devices, to_core(): return lax.ppermute(value, 'tensor', [(0, 1), (1, 0)])  1.97 us
  transfers between devices with their start and end apart: 31, of which 20 were waited for; matrix products, arithmetic and copies ran while one was open for 1% of the time, Pallas kernels for 12%

profile of v13, /device:TPU:0, one launch (start us, length us, event | category | flops | bytes accessed | tf_op | source)
XLA Modules:
  0.0 97.6 jit_solution(1048344545196248555)
XLA Ops:
  7.3 4.8 %out_projection.1 = (f32[16,2048]{1,0:T(8,128)S(1)}, f32[16,2048]{1,0:T(8,128)S(1)}) custom-call(bf16[32,2048]{1,0:T(8,128)(2,1)} %a_hbm.1, bf16[2048,2048]{1,0:T(8,128)(2,1)} %w_hbm.1), custom_call_target="tpu_custom_call" | custom-call | tf_op jit(solution)/shard_map/out_projection/pallas_call | solution.py:77
  13.7 3.0 %collective-permute-start.1 = (bf16[16,2176]{1,0:T(8,128)(2,1)S(1)}, bf16[16,2176]{1,0:T(8,128)(2,1)S(1)}, u32[]{:S(2)}, u32[]{:S(2)}) collective-permute-start(bf16[16,2176]{1,0:T(8,128)(2,1)S(1)} %get-tuple-element.71.refs_3_.refs_0_), channel_id=1, source_target_pairs={{0,8},{2,10},{4,12},{6,14},{8,0},{10,2},{12,4},{14,6},{16,24},{18,... | collective-permute-start | bytes 208904 | tf_op jit(solution)/shard_map/ppermute | solution.py:484
  16.7 2.6 %collective-permute-start.2 = (bf16[16,2176]{1,0:T(8,128)(2,1)S(1)}, bf16[16,2176]{1,0:T(8,128)(2,1)S(1)}, u32[]{:S(2)}, u32[]{:S(2)}) collective-permute-start(bf16[16,2176]{1,0:T(8,128)(2,1)S(1)} %get-tuple-element.71.refs_3_.refs_0_), channel_id=1, source_target_pairs={{0,16},{2,18},{4,20},{6,22},{8,24},{10,26},{12,28},{14,30},{16,0},... | collective-permute-start | bytes 208904 | tf_op jit(solution)/shard_map/ppermute | solution.py:484
  19.3 3.8 %load_weights.2 = (bf16[1,2048,768]{2,1,0:T(8,128)(2,1)S(1)}, bf16[1,2048,768]{2,1,0:T(8,128)(2,1)S(1)}, bf16[1,768,2048]{2,1,0:T(8,128)(2,1)S(1)}) custom-call(bf16[1,2048,768]{2,1,0:T(8,128)(2,1)} %refs_0_.1, bf16[1,2048,768]{2,1,0:T(8,128)(2,1)} %refs_1_.1, bf16[1,768,2048]{2,1,0:T(8,128)(2,1)} %refs_2_.3, ...), custom_call_target="tpu_custom_call" | custom-call | tf_op jit(solution)/shard_map/load_weights/pallas_call | solution.py:171
  23.1 1.4 %collective-permute-done.2.refs_2_ = bf16[16,2176]{1,0:T(8,128)(2,1)S(1)} collective-permute-done((bf16[16,2176]{1,0:T(8,128)(2,1)S(1)}, bf16[16,2176]{1,0:T(8,128)(2,1)S(1)}, u32[]{:S(2)}, u32[]{:S(2)}) %collective-permute-start.2) | collective-permute-done | bytes 69664 | tf_op jit(solution)/shard_map/ppermute | solution.py:484
  25.6 1.6 %collective-permute-start.4 = (bf16[64,2432]{1,0:T(8,128)(2,1)S(1)}, bf16[64,2432]{1,0:T(8,128)(2,1)S(1)}, u32[]{:S(2)}, u32[]{:S(2)}) collective-permute-start(bf16[64,2432]{1,0:T(8,128)(2,1)S(1)} %get-tuple-element.80), channel_id=1, source_target_pairs={{0,2},{2,0},{4,6},{6,4},{8,10},{10,8},{12,14},{14,12},{16,18},{18,... | collective-permute-start | bytes 933896 | tf_op jit(solution)/shard_map/ppermute | solution.py:484
  27.1 1.5 %collective-permute-start.5 = (bf16[64,2432]{1,0:T(8,128)(2,1)S(1)}, bf16[64,2432]{1,0:T(8,128)(2,1)S(1)}, u32[]{:S(2)}, u32[]{:S(2)}) collective-permute-start(bf16[64,2432]{1,0:T(8,128)(2,1)S(1)} %get-tuple-element.81), channel_id=1, source_target_pairs={{0,4},{2,6},{4,0},{6,2},{8,12},{10,14},{12,8},{14,10},{16,20},{18,... | collective-permute-start | bytes 933896 | tf_op jit(solution)/shard_map/ppermute | solution.py:484
  28.7 4.6 %collective-permute-done.4.refs_1_.refs_5_ = bf16[64,2432]{1,0:T(8,128)(2,1)S(1)} collective-permute-done((bf16[64,2432]{1,0:T(8,128)(2,1)S(1)}, bf16[64,2432]{1,0:T(8,128)(2,1)S(1)}, u32[]{:S(2)}, u32[]{:S(2)}) %collective-permute-start.4) | collective-permute-done | bytes 311328 | tf_op jit(solution)/shard_map/ppermute | solution.py:484
  34.5 1.6 %collective-permute-start.9 = (bf16[32,2432]{1,0:T(8,128)(2,1)S(1)}, bf16[32,2432]{1,0:T(8,128)(2,1)S(1)}, u32[]{:S(2)}, u32[]{:S(2)}) collective-permute-start(bf16[32,2432]{1,0:T(8,128)(2,1)S(1)} %slice.8), channel_id=1, source_target_pairs={{0,4},{2,6},{4,0},{6,2},{8,12},{10,14},{12,8},{14,10},{16,20},{18,... | collective-permute-start | bytes 466952 | tf_op jit(solution)/shard_map/ppermute | solution.py:484
  37.0 4.1 %experts.2 = (bf16[192,2048]{1,0:T(8,128)(2,1)S(1)}, bf16[64,2048]{1,0:T(8,128)(2,1)S(1)}, bf16[64,2048]{1,0:T(8,128)(2,1)S(1)}, bf16[64,2048]{1,0:T(8,128)(2,1)S(1)}) custom-call(bf16[64,2432]{1,0:T(8,128)(2,1)S(1)} %get-tuple-element.79.refs_0_.refs_4_, bf16[64,2432]{1,0:T(8,128)(2,1)S(1)} %collective-permute-done.4.refs_1_.refs_5_, ...), custom_call_target="tpu_custom_call" | custom-call | flops 3623878656 | tf_op jit(solution)/shard_map/experts/pallas_call | solution.py:231
  43.9 2.0 %experts.3 = (bf16[64,2048]{1,0:T(8,128)(2,1)S(1)}, bf16[64,2048]{1,0:T(8,128)(2,1)S(1)}) custom-call(bf16[32,2432]{1,0:T(8,128)(2,1)S(1)} %collective-permute-done.9.refs_0_.refs_7_, bf16[32,2432]{1,0:T(8,128)(2,1)S(1)} %collective-permute-done.10.refs_1_.refs_8_, bf16[32,2432]{1,0:T(8,128)(2,1)S(1)} %collective-permute-done.11.refs_2_, ...), custom_call_target="tpu_custom_call" | custom-call | flops 1207959552 | tf_op jit(solution)/shard_map/experts/pallas_call | solution.py:231
  48.9 2.4 %collective-permute-start.19 = (bf16[256,512]{1,0:T(8,128)(2,1)S(1)}, bf16[256,512]{1,0:T(8,128)(2,1)S(1)}, u32[]{:S(2)}, u32[]{:S(2)}) collective-permute-start(bf16[256,512]{1,0:T(8,128)(2,1)S(1)} %get-tuple-element.101), channel_id=1, source_target_pairs={{0,6},{2,4},{4,2},{6,0},{8,14},{10,12},{12,10},{14,8},{16,22},{18,... | collective-permute-start | bytes 786440 | tf_op jit(solution)/shard_map/ppermute | solution.py:484
  51.3 1.5 %collective-permute-start.20 = (bf16[128,512]{1,0:T(8,128)(2,1)S(1)}, bf16[128,512]{1,0:T(8,128)(2,1)S(1)}, u32[]{:S(2)}, u32[]{:S(2)}) collective-permute-start(bf16[128,512]{1,0:T(8,128)(2,1)S(1)} %copy-done.1), channel_id=1, source_target_pairs={{0,8},{2,10},{4,12},{6,14},{8,0},{10,2},{12,4},{14,6},{16,24},{18,... | collective-permute-start | bytes 393224 | tf_op jit(solution)/shard_map/ppermute | solution.py:484
  52.9 1.4 %collective-permute-start.21 = (bf16[128,512]{1,0:T(8,128)(2,1)S(1)}, bf16[128,512]{1,0:T(8,128)(2,1)S(1)}, u32[]{:S(2)}, u32[]{:S(2)}) collective-permute-start(bf16[128,512]{1,0:T(8,128)(2,1)S(1)} %copy-done.1), channel_id=1, source_target_pairs={{0,16},{2,18},{4,20},{6,22},{8,24},{10,26},{12,28},{14,30},{16,0},... | collective-permute-start | bytes 393224 | tf_op jit(solution)/shard_map/ppermute | solution.py:484
  54.3 2.7 %collective-permute-done.17.refs_1_ = bf16[256,512]{1,0:T(8,128)(2,1)S(1)} collective-permute-done((bf16[256,512]{1,0:T(8,128)(2,1)S(1)}, bf16[256,512]{1,0:T(8,128)(2,1)S(1)}, u32[]{:S(2)}, u32[]{:S(2)}) %collective-permute-start.17) | collective-permute-done | bytes 262176 | tf_op jit(solution)/shard_map/ppermute | solution.py:484
  57.0 5.2 %collective-permute-done.18.refs_2_ = bf16[256,512]{1,0:T(8,128)(2,1)S(1)} collective-permute-done((bf16[256,512]{1,0:T(8,128)(2,1)S(1)}, bf16[256,512]{1,0:T(8,128)(2,1)S(1)}, u32[]{:S(2)}, u32[]{:S(2)}) %collective-permute-start.18) | collective-permute-done | bytes 262176 | tf_op jit(solution)/shard_map/ppermute | solution.py:484
  62.3 2.9 %collective-permute-done.20.refs_1_ = bf16[128,512]{1,0:T(8,128)(2,1)S(1)} collective-permute-done((bf16[128,512]{1,0:T(8,128)(2,1)S(1)}, bf16[128,512]{1,0:T(8,128)(2,1)S(1)}, u32[]{:S(2)}, u32[]{:S(2)}) %collective-permute-start.20) | collective-permute-done | bytes 131104 | tf_op jit(solution)/shard_map/ppermute | solution.py:484
  65.3 2.4 %collective-permute-done.21.refs_2_ = bf16[128,512]{1,0:T(8,128)(2,1)S(1)} collective-permute-done((bf16[128,512]{1,0:T(8,128)(2,1)S(1)}, bf16[128,512]{1,0:T(8,128)(2,1)S(1)}, u32[]{:S(2)}, u32[]{:S(2)}) %collective-permute-start.21) | collective-permute-done | bytes 131104 | tf_op jit(solution)/shard_map/ppermute | solution.py:484
  69.3 2.7 %collective-permute-start.24 = (bf16[64,512]{1,0:T(8,128)(2,1)S(1)}, bf16[64,512]{1,0:T(8,128)(2,1)S(1)}, u32[]{:S(2)}, u32[]{:S(2)}) collective-permute-start(bf16[64,512]{1,0:T(8,128)(2,1)S(1)} %get-tuple-element.110.refs_4_), channel_id=1, source_target_pairs={{0,24},{2,26},{4,28},{6,30},{8,16},{10,18},{12,20},{14,22},{16,8},... | collective-permute-start | bytes 196616 | tf_op jit(solution)/shard_map/ppermute | solution.py:484
  72.0 1.6 %load_weights.3.q_ref = bf16[512,2048]{1,0:T(8,128)(2,1)S(1)} custom-call(bf16[512,2048]{1,0:T(8,128)(2,1)} %all-gather.2.cloned.1.call-done.refs_0_, bf16[64,512]{1,0:T(8,128)(2,1)S(1)} %get-tuple-element.112.refs_1_.refs_0_, bf16[64,512]{1,0:T(8,128)(2,1)S(1)} %get-tuple-element.108.refs_2_, bf16[64,512]{1,0:T(8,128)(2,1)S(1)} %get-tuple-element.109.refs_3_, ...), custom_call_target="tpu_custom_call" | custom-call | tf_op jit(solution)/shard_map/load_weights/pallas_call | solution.py:171
  74.4 1.9 %collective-permute-done.24.refs_3_ = bf16[64,512]{1,0:T(8,128)(2,1)S(1)} collective-permute-done((bf16[64,512]{1,0:T(8,128)(2,1)S(1)}, bf16[64,512]{1,0:T(8,128)(2,1)S(1)}, u32[]{:S(2)}, u32[]{:S(2)}) %collective-permute-start.24) | collective-permute-done | bytes 65568 | tf_op jit(solution)/shard_map/ppermute | solution.py:484
  80.2 1.7 %collective-permute-start.29 = (bf16[32,2944]{1,0:T(8,128)(2,1)S(1)}, bf16[32,2944]{1,0:T(8,128)(2,1)S(1)}, u32[]{:S(2)}, u32[]{:S(2)}) collective-permute-start(bf16[32,2944]{1,0:T(8,128)(2,1)S(1)} %get-tuple-element.124), channel_id=1, source_target_pairs={{0,6},{2,4},{4,2},{6,0},{8,14},{10,12},{12,10},{14,8},{16,22},{18,... | collective-permute-start | bytes 565256 | tf_op jit(solution)/shard_map/ppermute | solution.py:484
  82.0 4.1 %collective-permute-done.27.refs_1_ = bf16[32,2944]{1,0:T(8,128)(2,1)S(1)} collective-permute-done((bf16[32,2944]{1,0:T(8,128)(2,1)S(1)}, bf16[32,2944]{1,0:T(8,128)(2,1)S(1)}, u32[]{:S(2)}, u32[]{:S(2)}) %collective-permute-start.27) | collective-permute-done | bytes 188448 | tf_op jit(solution)/shard_map/ppermute | solution.py:484
  86.0 3.8 %collective-permute-done.28.refs_2_ = bf16[32,2944]{1,0:T(8,128)(2,1)S(1)} collective-permute-done((bf16[32,2944]{1,0:T(8,128)(2,1)S(1)}, bf16[32,2944]{1,0:T(8,128)(2,1)S(1)}, u32[]{:S(2)}, u32[]{:S(2)}) %collective-permute-start.28) | collective-permute-done | bytes 188448 | tf_op jit(solution)/shard_map/ppermute | solution.py:484
  (76 shorter events, 18.0 us)
Async XLA Ops:
  7.2 64.8 %all-gather.2.cloned.1.call-start = ((), (), s32[]{:S(2)}) async-start(), calls=%async_computation | async-start | bytes 2621440 | tf_op jit(solution)/shard_map/all_gather | solution.py:505
  13.7 9.4 %collective-permute-start.1 = (bf16[16,2176]{1,0:T(8,128)(2,1)S(1)}, bf16[16,2176]{1,0:T(8,128)(2,1)S(1)}, u32[]{:S(2)}, u32[]{:S(2)}) collective-permute-start(bf16[16,2176]{1,0:T(8,128)(2,1)S(1)} %get-tuple-element.71.refs_3_.refs_0_), channel_id=1, source_target_pairs={{0,8},{2,10},{4,12},{6,14},{8,0},{10,2},{12,4},{14,6},{16,24},{18,... | collective-permute-start | bytes 208904 | tf_op jit(solution)/shard_map/ppermute | solution.py:484
  16.7 7.8 %collective-permute-start.2 = (bf16[16,2176]{1,0:T(8,128)(2,1)S(1)}, bf16[16,2176]{1,0:T(8,128)(2,1)S(1)}, u32[]{:S(2)}, u32[]{:S(2)}) collective-permute-start(bf16[16,2176]{1,0:T(8,128)(2,1)S(1)} %get-tuple-element.71.refs_3_.refs_0_), channel_id=1, source_target_pairs={{0,16},{2,18},{4,20},{6,22},{8,24},{10,26},{12,28},{14,30},{16,0},... | collective-permute-start | bytes 208904 | tf_op jit(solution)/shard_map/ppermute | solution.py:484
  19.3 6.2 %collective-permute-start.3 = (bf16[16,2176]{1,0:T(8,128)(2,1)S(1)}, bf16[16,2176]{1,0:T(8,128)(2,1)S(1)}, u32[]{:S(2)}, u32[]{:S(2)}) collective-permute-start(bf16[16,2176]{1,0:T(8,128)(2,1)S(1)} %get-tuple-element.71.refs_3_.refs_0_), channel_id=1, source_target_pairs={{0,24},{2,26},{4,28},{6,30},{8,16},{10,18},{12,20},{14,22},{16,8},... | collective-permute-start | bytes 208904 | tf_op jit(solution)/shard_map/ppermute | solution.py:484
  25.6 7.7 %collective-permute-start.4 = (bf16[64,2432]{1,0:T(8,128)(2,1)S(1)}, bf16[64,2432]{1,0:T(8,128)(2,1)S(1)}, u32[]{:S(2)}, u32[]{:S(2)}) collective-permute-start(bf16[64,2432]{1,0:T(8,128)(2,1)S(1)} %get-tuple-element.80), channel_id=1, source_target_pairs={{0,2},{2,0},{4,6},{6,4},{8,10},{10,8},{12,14},{14,12},{16,18},{18,... | collective-permute-start | bytes 933896 | tf_op jit(solution)/shard_map/ppermute | solution.py:484
  27.1 7.3 %collective-permute-start.5 = (bf16[64,2432]{1,0:T(8,128)(2,1)S(1)}, bf16[64,2432]{1,0:T(8,128)(2,1)S(1)}, u32[]{:S(2)}, u32[]{:S(2)}) collective-permute-start(bf16[64,2432]{1,0:T(8,128)(2,1)S(1)} %get-tuple-element.81), channel_id=1, source_target_pairs={{0,4},{2,6},{4,0},{6,2},{8,12},{10,14},{12,8},{14,10},{16,20},{18,... | collective-permute-start | bytes 933896 | tf_op jit(solution)/shard_map/ppermute | solution.py:484
  28.7 8.3 %collective-permute-start.6 = (bf16[64,2432]{1,0:T(8,128)(2,1)S(1)}, bf16[64,2432]{1,0:T(8,128)(2,1)S(1)}, u32[]{:S(2)}, u32[]{:S(2)}) collective-permute-start(bf16[64,2432]{1,0:T(8,128)(2,1)S(1)} %get-tuple-element.79.refs_0_.refs_4_), channel_id=1, source_target_pairs={{0,1},{1,0},{2,3},{3,2},{4,5},{5,4},{6,7},{7,6},{8,9},{9,8},{10,11... | collective-permute-start | bytes 933896 | tf_op jit(solution)/shard_map/ppermute | solution.py:481
  33.2 3.7 %collective-permute-start.7 = (bf16[64,2432]{1,0:T(8,128)(2,1)S(1)}, bf16[64,2432]{1,0:T(8,128)(2,1)S(1)}, u32[]{:S(2)}, u32[]{:S(2)}) collective-permute-start(bf16[64,2432]{1,0:T(8,128)(2,1)S(1)} %collective-permute-done.4.refs_1_.refs_5_), channel_id=1, source_target_pairs={{0,1},{1,0},{2,3},{3,2},{4,5},{5,4},{6,7},{7,6},{8,9},{9,8},{10,11... | collective-permute-start | bytes 933896 | tf_op jit(solution)/shard_map/ppermute | solution.py:481
  34.5 6.5 %collective-permute-start.9 = (bf16[32,2432]{1,0:T(8,128)(2,1)S(1)}, bf16[32,2432]{1,0:T(8,128)(2,1)S(1)}, u32[]{:S(2)}, u32[]{:S(2)}) collective-permute-start(bf16[32,2432]{1,0:T(8,128)(2,1)S(1)} %slice.8), channel_id=1, source_target_pairs={{0,4},{2,6},{4,0},{6,2},{8,12},{10,14},{12,8},{14,10},{16,20},{18,... | collective-permute-start | bytes 466952 | tf_op jit(solution)/shard_map/ppermute | solution.py:484
  36.1 6.2 %collective-permute-start.10 = (bf16[32,2432]{1,0:T(8,128)(2,1)S(1)}, bf16[32,2432]{1,0:T(8,128)(2,1)S(1)}, u32[]{:S(2)}, u32[]{:S(2)}) collective-permute-start(bf16[32,2432]{1,0:T(8,128)(2,1)S(1)} %slice.9), channel_id=1, source_target_pairs={{0,2},{2,0},{4,6},{6,4},{8,10},{10,8},{12,14},{14,12},{16,18},{18,... | collective-permute-start | bytes 466952 | tf_op jit(solution)/shard_map/ppermute | solution.py:484
  42.8 3.5 %collective-permute-start.13 = (bf16[64,2048]{1,0:T(8,128)(2,1)S(1)}, bf16[64,2048]{1,0:T(8,128)(2,1)S(1)}, u32[]{:S(2)}, u32[]{:S(2)}) collective-permute-start(bf16[64,2048]{1,0:T(8,128)(2,1)S(1)} %get-tuple-element.90), channel_id=1, source_target_pairs={{0,1},{1,0},{2,3},{3,2},{4,5},{5,4},{6,7},{7,6},{8,9},{9,8},{10,11... | collective-permute-start | bytes 786440 | tf_op jit(solution)/shard_map/ppermute | solution.py:481
  42.8 3.5 %collective-permute-start.14 = (bf16[64,2048]{1,0:T(8,128)(2,1)S(1)}, bf16[64,2048]{1,0:T(8,128)(2,1)S(1)}, u32[]{:S(2)}, u32[]{:S(2)}) collective-permute-start(bf16[64,2048]{1,0:T(8,128)(2,1)S(1)} %get-tuple-element.91), channel_id=1, source_target_pairs={{0,1},{1,0},{2,3},{3,2},{4,5},{5,4},{6,7},{7,6},{8,9},{9,8},{10,11... | collective-permute-start | bytes 786440 | tf_op jit(solution)/shard_map/ppermute | solution.py:481
  47.8 9.2 %collective-permute-start.17 = (bf16[256,512]{1,0:T(8,128)(2,1)S(1)}, bf16[256,512]{1,0:T(8,128)(2,1)S(1)}, u32[]{:S(2)}, u32[]{:S(2)}) collective-permute-start(bf16[256,512]{1,0:T(8,128)(2,1)S(1)} %get-tuple-element.99), channel_id=1, source_target_pairs={{0,2},{2,0},{4,6},{6,4},{8,10},{10,8},{12,14},{14,12},{16,18},{18,... | collective-permute-start | bytes 786440 | tf_op jit(solution)/shard_map/ppermute | solution.py:484
  48.4 13.8 %collective-permute-start.18 = (bf16[256,512]{1,0:T(8,128)(2,1)S(1)}, bf16[256,512]{1,0:T(8,128)(2,1)S(1)}, u32[]{:S(2)}, u32[]{:S(2)}) collective-permute-start(bf16[256,512]{1,0:T(8,128)(2,1)S(1)} %get-tuple-element.100), channel_id=1, source_target_pairs={{0,4},{2,6},{4,0},{6,2},{8,12},{10,14},{12,8},{14,10},{16,20},{18,... | collective-permute-start | bytes 786440 | tf_op jit(solution)/shard_map/ppermute | solution.py:484
  48.9 13.3 %collective-permute-start.19 = (bf16[256,512]{1,0:T(8,128)(2,1)S(1)}, bf16[256,512]{1,0:T(8,128)(2,1)S(1)}, u32[]{:S(2)}, u32[]{:S(2)}) collective-permute-start(bf16[256,512]{1,0:T(8,128)(2,1)S(1)} %get-tuple-element.101), channel_id=1, source_target_pairs={{0,6},{2,4},{4,2},{6,0},{8,14},{10,12},{12,10},{14,8},{16,22},{18,... | collective-permute-start | bytes 786440 | tf_op jit(solution)/shard_map/ppermute | solution.py:484
  51.3 13.9 %collective-permute-start.20 = (bf16[128,512]{1,0:T(8,128)(2,1)S(1)}, bf16[128,512]{1,0:T(8,128)(2,1)S(1)}, u32[]{:S(2)}, u32[]{:S(2)}) collective-permute-start(bf16[128,512]{1,0:T(8,128)(2,1)S(1)} %copy-done.1), channel_id=1, source_target_pairs={{0,8},{2,10},{4,12},{6,14},{8,0},{10,2},{12,4},{14,6},{16,24},{18,... | collective-permute-start | bytes 393224 | tf_op jit(solution)/shard_map/ppermute | solution.py:484
  52.9 14.8 %collective-permute-start.21 = (bf16[128,512]{1,0:T(8,128)(2,1)S(1)}, bf16[128,512]{1,0:T(8,128)(2,1)S(1)}, u32[]{:S(2)}, u32[]{:S(2)}) collective-permute-start(bf16[128,512]{1,0:T(8,128)(2,1)S(1)} %copy-done.1), channel_id=1, source_target_pairs={{0,16},{2,18},{4,20},{6,22},{8,24},{10,26},{12,28},{14,30},{16,0},... | collective-permute-start | bytes 393224 | tf_op jit(solution)/shard_map/ppermute | solution.py:484
  67.6 6.1 %collective-permute-start.22 = (bf16[64,512]{1,0:T(8,128)(2,1)S(1)}, bf16[64,512]{1,0:T(8,128)(2,1)S(1)}, u32[]{:S(2)}, u32[]{:S(2)}) collective-permute-start(bf16[64,512]{1,0:T(8,128)(2,1)S(1)} %get-tuple-element.108.refs_2_), channel_id=1, source_target_pairs={{0,8},{2,10},{4,12},{6,14},{8,0},{10,2},{12,4},{14,6},{16,24},{18,... | collective-permute-start | bytes 196616 | tf_op jit(solution)/shard_map/ppermute | solution.py:484
  68.1 6.3 %collective-permute-start.23 = (bf16[64,512]{1,0:T(8,128)(2,1)S(1)}, bf16[64,512]{1,0:T(8,128)(2,1)S(1)}, u32[]{:S(2)}, u32[]{:S(2)}) collective-permute-start(bf16[64,512]{1,0:T(8,128)(2,1)S(1)} %get-tuple-element.109.refs_3_), channel_id=1, source_target_pairs={{0,16},{2,18},{4,20},{6,22},{8,24},{10,26},{12,28},{14,30},{16,0},... | collective-permute-start | bytes 196616 | tf_op jit(solution)/shard_map/ppermute | solution.py:484
  69.3 7.0 %collective-permute-start.24 = (bf16[64,512]{1,0:T(8,128)(2,1)S(1)}, bf16[64,512]{1,0:T(8,128)(2,1)S(1)}, u32[]{:S(2)}, u32[]{:S(2)}) collective-permute-start(bf16[64,512]{1,0:T(8,128)(2,1)S(1)} %get-tuple-element.110.refs_4_), channel_id=1, source_target_pairs={{0,24},{2,26},{4,28},{6,30},{8,16},{10,18},{12,20},{14,22},{16,8},... | collective-permute-start | bytes 196616 | tf_op jit(solution)/shard_map/ppermute | solution.py:484
  72.0 5.3 %collective-permute-start.26 = (bf16[128,512]{1,0:T(8,128)(2,1)S(1)}, bf16[128,512]{1,0:T(8,128)(2,1)S(1)}, u32[]{:S(2)}, u32[]{:S(2)}) collective-permute-start(bf16[128,512]{1,0:T(8,128)(2,1)S(1)} %collective-permute-done.21.refs_2_), channel_id=1, source_target_pairs={{0,8},{2,10},{4,12},{6,14},{8,0},{10,2},{12,4},{14,6},{16,24},{18,... | collective-permute-start | bytes 393224 | tf_op jit(solution)/shard_map/ppermute | solution.py:484
  78.4 7.6 %collective-permute-start.27 = (bf16[32,2944]{1,0:T(8,128)(2,1)S(1)}, bf16[32,2944]{1,0:T(8,128)(2,1)S(1)}, u32[]{:S(2)}, u32[]{:S(2)}) collective-permute-start(bf16[32,2944]{1,0:T(8,128)(2,1)S(1)} %get-tuple-element.122), channel_id=1, source_target_pairs={{0,2},{2,0},{4,6},{6,4},{8,10},{10,8},{12,14},{14,12},{16,18},{18,... | collective-permute-start | bytes 565256 | tf_op jit(solution)/shard_map/ppermute | solution.py:484
  79.3 10.5 %collective-permute-start.28 = (bf16[32,2944]{1,0:T(8,128)(2,1)S(1)}, bf16[32,2944]{1,0:T(8,128)(2,1)S(1)}, u32[]{:S(2)}, u32[]{:S(2)}) collective-permute-start(bf16[32,2944]{1,0:T(8,128)(2,1)S(1)} %get-tuple-element.123), channel_id=1, source_target_pairs={{0,4},{2,6},{4,0},{6,2},{8,12},{10,14},{12,8},{14,10},{16,20},{18,... | collective-permute-start | bytes 565256 | tf_op jit(solution)/shard_map/ppermute | solution.py:484
  80.2 9.6 %collective-permute-start.29 = (bf16[32,2944]{1,0:T(8,128)(2,1)S(1)}, bf16[32,2944]{1,0:T(8,128)(2,1)S(1)}, u32[]{:S(2)}, u32[]{:S(2)}) collective-permute-start(bf16[32,2944]{1,0:T(8,128)(2,1)S(1)} %get-tuple-element.124), channel_id=1, source_target_pairs={{0,6},{2,4},{4,2},{6,0},{8,14},{10,12},{12,10},{14,8},{16,22},{18,... | collective-permute-start | bytes 565256 | tf_op jit(solution)/shard_map/ppermute | solution.py:484
  (15 other events, 105.4 us)
Sparse Core Ops, SparseCore 0:
  13.8 54.0 all-gather.1

commit v14 on v13

--- a/solution.py
+++ b/solution.py
@@ -498,11 +498,11 @@
 
     lines = [list(range(i, n_expert, PLANE)) for i in range(PLANE)]
     mine, theirs = out_projection(attn_out, out_weight)
+    mine, q_own = lax.optimization_barrier((mine, q_weight))
+    q_rows = lax.all_gather(q_own, "expert", axis=0, tiled=True, axis_index_groups=lines)
     tokens, *firsts = first_norm(
         (mine,), (to_core(theirs),), residual, attn_gain[None, :], meta, depth
     )
-    tokens, q_own = lax.optimization_barrier((tokens, q_weight))
-    q_rows = lax.all_gather(q_own, "expert", axis=0, tiled=True, axis_index_groups=lines)
     weights = load((w_gate, w_up, w_down), (tokens,))
     line = to_z([tokens] * depth)
     *line, gate, up, down = lax.optimization_barrier((*line, *weights))
@@ -520,9 +520,7 @@
     *sums, kv_own = lax.optimization_barrier((*chip_sum((near_mine, far_mine), theirs), kv_weight))
     parts = to_plane(sums)
     kv_rows = [kv_own, to_expert(kv_own, PLANE), to_expert(kv_own, 2 * PLANE)]
-    *parts, kv_rows[1], kv_rows[2] = lax.optimization_barrier(
-        (*plane_sum(parts, depth), *kv_rows[1:])
-    )
+    parts = plane_sum(parts, depth)
     kv_rows.append(to_expert(kv_rows[2], PLANE))
     (q_rows,) = load((q_rows,), parts)
     parts = to_z(parts)

time: 97.7 us -> 98 us (level)
  waiting for transfers between devices: 36.8 us -> 28.5 us
  starting transfers between devices: 27.6 us -> 35.7 us
    ppermute x19, starting transfers between devices: 25.6 us -> 33.7 us  [to_expert(): lax.ppermute(value, 'expert', [(i, i ^ offset) for i in range(n_expert)])]
    ppermute x19, waiting for transfers between devices: 34 us -> 26.2 us  [to_expert(): lax.ppermute(value, 'expert', [(i, i ^ offset) for i in range(n_expert)])]
  transfers between devices with their start and end apart: 31 -> 31, of which waited for: 20 -> 16; matrix products, arithmetic and copies ran while one was open for 1% -> 1% of each run, Pallas kernels for 12% -> 13%
where the time goes in v14:
time: 98 us; the launch traced here: 97.8 us
  starting transfers between devices  35.7 us (36%)
  waiting for transfers between devices  28.5 us (29%)
  Pallas kernels  18.7 us (19%)
  between operations  14.3 us (15%)
    ppermute x19, starting transfers between devices, to_expert(): lax.ppermute(value, 'expert', [(i, i ^ offset) for i in range(n_expert)])  33.7 us
    ppermute x19, waiting for transfers between devices, to_expert(): lax.ppermute(value, 'expert', [(i, i ^ offset) for i in range(n_expert)])  26.2 us
    pallas_call x2, Pallas kernels, experts(): pl.pallas_call(functools.partial(expert_kernel, depth, chunk, len(blocks)...  6.05 us
    pallas_call x2, Pallas kernels, load(): pl.pallas_call(functools.partial(load_kernel, count), out_shape=tuple((pl...  5.73 us
    pallas_call x1, Pallas kernels, out_projection(): pl.pallas_call(functools.partial(out_projection_kernel, chunk), out_shape...  4.77 us
    ppermute x11, waiting for transfers between devices, to_core(): return lax.ppermute(value, 'tensor', [(0, 1), (1, 0)])  2.3 us
    ppermute x11, starting transfers between devices, to_core(): return lax.ppermute(value, 'tensor', [(0, 1), (1, 0)])  1.98 us
  transfers between devices with their start and end apart: 31, of which 16 were waited for; matrix products, arithmetic and copies ran while one was open for 1% of the time, Pallas kernels for 13%

profile of v14, /device:TPU:0, one launch (start us, length us, event | category | flops | bytes accessed | tf_op | source)
XLA Modules:
  0.0 97.8 jit_solution(5072672862511933339)
XLA Ops:
  7.3 4.8 %out_projection.1 = (f32[16,2048]{1,0:T(8,128)S(1)}, f32[16,2048]{1,0:T(8,128)S(1)}) custom-call(bf16[32,2048]{1,0:T(8,128)(2,1)} %a_hbm.1, bf16[2048,2048]{1,0:T(8,128)(2,1)} %w_hbm.1), custom_call_target="tpu_custom_call" | custom-call | tf_op jit(solution)/shard_map/out_projection/pallas_call | solution.py:77
  13.7 3.0 %collective-permute-start.1 = (bf16[16,2176]{1,0:T(8,128)(2,1)S(1)}, bf16[16,2176]{1,0:T(8,128)(2,1)S(1)}, u32[]{:S(2)}, u32[]{:S(2)}) collective-permute-start(bf16[16,2176]{1,0:T(8,128)(2,1)S(1)} %get-tuple-element.65.refs_3_.refs_0_), channel_id=1, source_target_pairs={{0,8},{2,10},{4,12},{6,14},{8,0},{10,2},{12,4},{14,6},{16,24},{18,... | collective-permute-start | bytes 208904 | tf_op jit(solution)/shard_map/ppermute | solution.py:484
  16.7 2.6 %collective-permute-start.2 = (bf16[16,2176]{1,0:T(8,128)(2,1)S(1)}, bf16[16,2176]{1,0:T(8,128)(2,1)S(1)}, u32[]{:S(2)}, u32[]{:S(2)}) collective-permute-start(bf16[16,2176]{1,0:T(8,128)(2,1)S(1)} %get-tuple-element.65.refs_3_.refs_0_), channel_id=1, source_target_pairs={{0,16},{2,18},{4,20},{6,22},{8,24},{10,26},{12,28},{14,30},{16,0},... | collective-permute-start | bytes 208904 | tf_op jit(solution)/shard_map/ppermute | solution.py:484
  19.3 4.1 %load_weights.2 = (bf16[1,2048,768]{2,1,0:T(8,128)(2,1)S(1)}, bf16[1,2048,768]{2,1,0:T(8,128)(2,1)S(1)}, bf16[1,768,2048]{2,1,0:T(8,128)(2,1)S(1)}) custom-call(bf16[1,2048,768]{2,1,0:T(8,128)(2,1)} %refs_0_.1, bf16[1,2048,768]{2,1,0:T(8,128)(2,1)} %refs_1_.1, bf16[1,768,2048]{2,1,0:T(8,128)(2,1)} %refs_2_.3, ...), custom_call_target="tpu_custom_call" | custom-call | tf_op jit(solution)/shard_map/load_weights/pallas_call | solution.py:171
  25.6 1.6 %collective-permute-start.4 = (bf16[64,2432]{1,0:T(8,128)(2,1)S(1)}, bf16[64,2432]{1,0:T(8,128)(2,1)S(1)}, u32[]{:S(2)}, u32[]{:S(2)}) collective-permute-start(bf16[64,2432]{1,0:T(8,128)(2,1)S(1)} %get-tuple-element.74), channel_id=1, source_target_pairs={{0,2},{2,0},{4,6},{6,4},{8,10},{10,8},{12,14},{14,12},{16,18},{18,... | collective-permute-start | bytes 933896 | tf_op jit(solution)/shard_map/ppermute | solution.py:484
  27.1 1.5 %collective-permute-start.5 = (bf16[64,2432]{1,0:T(8,128)(2,1)S(1)}, bf16[64,2432]{1,0:T(8,128)(2,1)S(1)}, u32[]{:S(2)}, u32[]{:S(2)}) collective-permute-start(bf16[64,2432]{1,0:T(8,128)(2,1)S(1)} %get-tuple-element.75), channel_id=1, source_target_pairs={{0,4},{2,6},{4,0},{6,2},{8,12},{10,14},{12,8},{14,10},{16,20},{18,... | collective-permute-start | bytes 933896 | tf_op jit(solution)/shard_map/ppermute | solution.py:484
  28.7 4.6 %collective-permute-done.4.refs_1_.refs_5_ = bf16[64,2432]{1,0:T(8,128)(2,1)S(1)} collective-permute-done((bf16[64,2432]{1,0:T(8,128)(2,1)S(1)}, bf16[64,2432]{1,0:T(8,128)(2,1)S(1)}, u32[]{:S(2)}, u32[]{:S(2)}) %collective-permute-start.4) | collective-permute-done | bytes 311328 | tf_op jit(solution)/shard_map/ppermute | solution.py:484
  34.5 1.6 %collective-permute-start.9 = (bf16[32,2432]{1,0:T(8,128)(2,1)S(1)}, bf16[32,2432]{1,0:T(8,128)(2,1)S(1)}, u32[]{:S(2)}, u32[]{:S(2)}) collective-permute-start(bf16[32,2432]{1,0:T(8,128)(2,1)S(1)} %slice.8), channel_id=1, source_target_pairs={{0,4},{2,6},{4,0},{6,2},{8,12},{10,14},{12,8},{14,10},{16,20},{18,... | collective-permute-start | bytes 466952 | tf_op jit(solution)/shard_map/ppermute | solution.py:484
  36.9 4.1 %experts.2 = (bf16[192,2048]{1,0:T(8,128)(2,1)S(1)}, bf16[64,2048]{1,0:T(8,128)(2,1)S(1)}, bf16[64,2048]{1,0:T(8,128)(2,1)S(1)}, bf16[64,2048]{1,0:T(8,128)(2,1)S(1)}) custom-call(bf16[64,2432]{1,0:T(8,128)(2,1)S(1)} %get-tuple-element.73.refs_0_.refs_4_, bf16[64,2432]{1,0:T(8,128)(2,1)S(1)} %collective-permute-done.4.refs_1_.refs_5_, ...), custom_call_target="tpu_custom_call" | custom-call | flops 3623878656 | tf_op jit(solution)/shard_map/experts/pallas_call | solution.py:231
  43.9 2.0 %experts.3 = (bf16[64,2048]{1,0:T(8,128)(2,1)S(1)}, bf16[64,2048]{1,0:T(8,128)(2,1)S(1)}) custom-call(bf16[32,2432]{1,0:T(8,128)(2,1)S(1)} %collective-permute-done.9.refs_0_.refs_7_, bf16[32,2432]{1,0:T(8,128)(2,1)S(1)} %collective-permute-done.10.refs_1_.refs_8_, bf16[32,2432]{1,0:T(8,128)(2,1)S(1)} %collective-permute-done.11.refs_2_, ...), custom_call_target="tpu_custom_call" | custom-call | flops 1207959552 | tf_op jit(solution)/shard_map/experts/pallas_call | solution.py:231
  48.9 2.4 %collective-permute-start.19 = (bf16[256,512]{1,0:T(8,128)(2,1)S(1)}, bf16[256,512]{1,0:T(8,128)(2,1)S(1)}, u32[]{:S(2)}, u32[]{:S(2)}) collective-permute-start(bf16[256,512]{1,0:T(8,128)(2,1)S(1)} %get-tuple-element.95), channel_id=1, source_target_pairs={{0,6},{2,4},{4,2},{6,0},{8,14},{10,12},{12,10},{14,8},{16,22},{18,... | collective-permute-start | bytes 786440 | tf_op jit(solution)/shard_map/ppermute | solution.py:484
  51.3 6.0 %collective-permute-start.25 = (bf16[128,512]{1,0:T(8,128)(2,1)S(1)}, bf16[128,512]{1,0:T(8,128)(2,1)S(1)}, u32[]{:S(2)}, u32[]{:S(2)}) collective-permute-start(bf16[128,512]{1,0:T(8,128)(2,1)S(1)} %copy-done.1), channel_id=1, source_target_pairs={{0,16},{2,18},{4,20},{6,22},{8,24},{10,26},{12,28},{14,30},{16,0},... | collective-permute-start | bytes 393224 | tf_op jit(solution)/shard_map/ppermute | solution.py:484
  57.3 4.9 %collective-permute-done.18.refs_2_ = bf16[256,512]{1,0:T(8,128)(2,1)S(1)} collective-permute-done((bf16[256,512]{1,0:T(8,128)(2,1)S(1)}, bf16[256,512]{1,0:T(8,128)(2,1)S(1)}, u32[]{:S(2)}, u32[]{:S(2)}) %collective-permute-start.18) | collective-permute-done | bytes 262176 | tf_op jit(solution)/shard_map/ppermute | solution.py:484
  62.3 3.8 %collective-permute-start.20 = (bf16[64,512]{1,0:T(8,128)(2,1)S(1)}, bf16[64,512]{1,0:T(8,128)(2,1)S(1)}, u32[]{:S(2)}, u32[]{:S(2)}) collective-permute-start(bf16[64,512]{1,0:T(8,128)(2,1)S(1)} %get-tuple-element.97.refs_2_), channel_id=1, source_target_pairs={{0,8},{2,10},{4,12},{6,14},{8,0},{10,2},{12,4},{14,6},{16,24},{18,... | collective-permute-start | bytes 196616 | tf_op jit(solution)/shard_map/ppermute | solution.py:484
  66.1 2.3 %collective-permute-start.21 = (bf16[64,512]{1,0:T(8,128)(2,1)S(1)}, bf16[64,512]{1,0:T(8,128)(2,1)S(1)}, u32[]{:S(2)}, u32[]{:S(2)}) collective-permute-start(bf16[64,512]{1,0:T(8,128)(2,1)S(1)} %get-tuple-element.98.refs_3_), channel_id=1, source_target_pairs={{0,16},{2,18},{4,20},{6,22},{8,24},{10,26},{12,28},{14,30},{16,0},... | collective-permute-start | bytes 196616 | tf_op jit(solution)/shard_map/ppermute | solution.py:484
  68.4 1.4 %collective-permute-start.22 = (bf16[64,512]{1,0:T(8,128)(2,1)S(1)}, bf16[64,512]{1,0:T(8,128)(2,1)S(1)}, u32[]{:S(2)}, u32[]{:S(2)}) collective-permute-start(bf16[64,512]{1,0:T(8,128)(2,1)S(1)} %get-tuple-element.99.refs_4_), channel_id=1, source_target_pairs={{0,24},{2,26},{4,28},{6,30},{8,16},{10,18},{12,20},{14,22},{16,8},... | collective-permute-start | bytes 196616 | tf_op jit(solution)/shard_map/ppermute | solution.py:484
  70.4 1.5 %collective-permute-start.26 = (bf16[128,512]{1,0:T(8,128)(2,1)S(1)}, bf16[128,512]{1,0:T(8,128)(2,1)S(1)}, u32[]{:S(2)}, u32[]{:S(2)}) collective-permute-start(bf16[128,512]{1,0:T(8,128)(2,1)S(1)} %collective-permute-done.25.refs_2_), channel_id=1, source_target_pairs={{0,8},{2,10},{4,12},{6,14},{8,0},{10,2},{12,4},{14,6},{16,24},{18,... | collective-permute-start | bytes 393224 | tf_op jit(solution)/shard_map/ppermute | solution.py:484
  71.9 1.6 %load_weights.3.q_ref = bf16[512,2048]{1,0:T(8,128)(2,1)S(1)} custom-call(bf16[512,2048]{1,0:T(8,128)(2,1)} %all-gather.2.cloned.1.call-done.refs_0_, bf16[64,512]{1,0:T(8,128)(2,1)S(1)} %get-tuple-element.101.refs_1_.refs_0_, bf16[64,512]{1,0:T(8,128)(2,1)S(1)} %get-tuple-element.97.refs_2_, bf16[64,512]{1,0:T(8,128)(2,1)S(1)} %get-tuple-element.98.refs_3_, ...), custom_call_target="tpu_custom_call" | custom-call | tf_op jit(solution)/shard_map/load_weights/pallas_call | solution.py:171
  73.5 1.8 %collective-permute-done.22.refs_3_ = bf16[64,512]{1,0:T(8,128)(2,1)S(1)} collective-permute-done((bf16[64,512]{1,0:T(8,128)(2,1)S(1)}, bf16[64,512]{1,0:T(8,128)(2,1)S(1)}, u32[]{:S(2)}, u32[]{:S(2)}) %collective-permute-start.22) | collective-permute-done | bytes 65568 | tf_op jit(solution)/shard_map/ppermute | solution.py:484
  75.5 1.4 %collective-permute-done.24.refs_1_ = bf16[128,512]{1,0:T(8,128)(2,1)S(1)} collective-permute-done((bf16[128,512]{1,0:T(8,128)(2,1)S(1)}, bf16[128,512]{1,0:T(8,128)(2,1)S(1)}, u32[]{:S(2)}, u32[]{:S(2)}) %collective-permute-start.24) | collective-permute-done | bytes 131104 | tf_op jit(solution)/shard_map/ppermute | solution.py:484
  77.0 1.7 %collective-permute-done.26.refs_3_ = bf16[128,512]{1,0:T(8,128)(2,1)S(1)} collective-permute-done((bf16[128,512]{1,0:T(8,128)(2,1)S(1)}, bf16[128,512]{1,0:T(8,128)(2,1)S(1)}, u32[]{:S(2)}, u32[]{:S(2)}) %collective-permute-start.26) | collective-permute-done | bytes 131104 | tf_op jit(solution)/shard_map/ppermute | solution.py:484
  82.8 4.2 %collective-permute-done.27.refs_1_ = bf16[32,2944]{1,0:T(8,128)(2,1)S(1)} collective-permute-done((bf16[32,2944]{1,0:T(8,128)(2,1)S(1)}, bf16[32,2944]{1,0:T(8,128)(2,1)S(1)}, u32[]{:S(2)}, u32[]{:S(2)}) %collective-permute-start.27) | collective-permute-done | bytes 188448 | tf_op jit(solution)/shard_map/ppermute | solution.py:484
  87.0 1.4 %collective-permute-done.28.refs_2_ = bf16[32,2944]{1,0:T(8,128)(2,1)S(1)} collective-permute-done((bf16[32,2944]{1,0:T(8,128)(2,1)S(1)}, bf16[32,2944]{1,0:T(8,128)(2,1)S(1)}, u32[]{:S(2)}, u32[]{:S(2)}) %collective-permute-start.28) | collective-permute-done | bytes 188448 | tf_op jit(solution)/shard_map/ppermute | solution.py:484
  88.4 1.7 %collective-permute-done.29.refs_3_ = bf16[32,2944]{1,0:T(8,128)(2,1)S(1)} collective-permute-done((bf16[32,2944]{1,0:T(8,128)(2,1)S(1)}, bf16[32,2944]{1,0:T(8,128)(2,1)S(1)}, u32[]{:S(2)}, u32[]{:S(2)}) %collective-permute-start.29) | collective-permute-done | bytes 188448 | tf_op jit(solution)/shard_map/ppermute | solution.py:484
  (76 shorter events, 17.7 us)
Async XLA Ops:
  7.2 64.6 %all-gather.2.cloned.1.call-start = ((), (), s32[]{:S(2)}) async-start(), calls=%async_computation | async-start | bytes 2621440 | tf_op jit(solution)/shard_map/all_gather | solution.py:502
  13.7 9.7 %collective-permute-start.1 = (bf16[16,2176]{1,0:T(8,128)(2,1)S(1)}, bf16[16,2176]{1,0:T(8,128)(2,1)S(1)}, u32[]{:S(2)}, u32[]{:S(2)}) collective-permute-start(bf16[16,2176]{1,0:T(8,128)(2,1)S(1)} %get-tuple-element.65.refs_3_.refs_0_), channel_id=1, source_target_pairs={{0,8},{2,10},{4,12},{6,14},{8,0},{10,2},{12,4},{14,6},{16,24},{18,... | collective-permute-start | bytes 208904 | tf_op jit(solution)/shard_map/ppermute | solution.py:484
  16.7 7.8 %collective-permute-start.2 = (bf16[16,2176]{1,0:T(8,128)(2,1)S(1)}, bf16[16,2176]{1,0:T(8,128)(2,1)S(1)}, u32[]{:S(2)}, u32[]{:S(2)}) collective-permute-start(bf16[16,2176]{1,0:T(8,128)(2,1)S(1)} %get-tuple-element.65.refs_3_.refs_0_), channel_id=1, source_target_pairs={{0,16},{2,18},{4,20},{6,22},{8,24},{10,26},{12,28},{14,30},{16,0},... | collective-permute-start | bytes 208904 | tf_op jit(solution)/shard_map/ppermute | solution.py:484
  19.3 6.2 %collective-permute-start.3 = (bf16[16,2176]{1,0:T(8,128)(2,1)S(1)}, bf16[16,2176]{1,0:T(8,128)(2,1)S(1)}, u32[]{:S(2)}, u32[]{:S(2)}) collective-permute-start(bf16[16,2176]{1,0:T(8,128)(2,1)S(1)} %get-tuple-element.65.refs_3_.refs_0_), channel_id=1, source_target_pairs={{0,24},{2,26},{4,28},{6,30},{8,16},{10,18},{12,20},{14,22},{16,8},... | collective-permute-start | bytes 208904 | tf_op jit(solution)/shard_map/ppermute | solution.py:484
  25.6 7.7 %collective-permute-start.4 = (bf16[64,2432]{1,0:T(8,128)(2,1)S(1)}, bf16[64,2432]{1,0:T(8,128)(2,1)S(1)}, u32[]{:S(2)}, u32[]{:S(2)}) collective-permute-start(bf16[64,2432]{1,0:T(8,128)(2,1)S(1)} %get-tuple-element.74), channel_id=1, source_target_pairs={{0,2},{2,0},{4,6},{6,4},{8,10},{10,8},{12,14},{14,12},{16,18},{18,... | collective-permute-start | bytes 933896 | tf_op jit(solution)/shard_map/ppermute | solution.py:484
  27.1 7.3 %collective-permute-start.5 = (bf16[64,2432]{1,0:T(8,128)(2,1)S(1)}, bf16[64,2432]{1,0:T(8,128)(2,1)S(1)}, u32[]{:S(2)}, u32[]{:S(2)}) collective-permute-start(bf16[64,2432]{1,0:T(8,128)(2,1)S(1)} %get-tuple-element.75), channel_id=1, source_target_pairs={{0,4},{2,6},{4,0},{6,2},{8,12},{10,14},{12,8},{14,10},{16,20},{18,... | collective-permute-start | bytes 933896 | tf_op jit(solution)/shard_map/ppermute | solution.py:484
  28.7 8.3 %collective-permute-start.6 = (bf16[64,2432]{1,0:T(8,128)(2,1)S(1)}, bf16[64,2432]{1,0:T(8,128)(2,1)S(1)}, u32[]{:S(2)}, u32[]{:S(2)}) collective-permute-start(bf16[64,2432]{1,0:T(8,128)(2,1)S(1)} %get-tuple-element.73.refs_0_.refs_4_), channel_id=1, source_target_pairs={{0,1},{1,0},{2,3},{3,2},{4,5},{5,4},{6,7},{7,6},{8,9},{9,8},{10,11... | collective-permute-start | bytes 933896 | tf_op jit(solution)/shard_map/ppermute | solution.py:481
  33.2 3.7 %collective-permute-start.7 = (bf16[64,2432]{1,0:T(8,128)(2,1)S(1)}, bf16[64,2432]{1,0:T(8,128)(2,1)S(1)}, u32[]{:S(2)}, u32[]{:S(2)}) collective-permute-start(bf16[64,2432]{1,0:T(8,128)(2,1)S(1)} %collective-permute-done.4.refs_1_.refs_5_), channel_id=1, source_target_pairs={{0,1},{1,0},{2,3},{3,2},{4,5},{5,4},{6,7},{7,6},{8,9},{9,8},{10,11... | collective-permute-start | bytes 933896 | tf_op jit(solution)/shard_map/ppermute | solution.py:481
  34.5 6.5 %collective-permute-start.9 = (bf16[32,2432]{1,0:T(8,128)(2,1)S(1)}, bf16[32,2432]{1,0:T(8,128)(2,1)S(1)}, u32[]{:S(2)}, u32[]{:S(2)}) collective-permute-start(bf16[32,2432]{1,0:T(8,128)(2,1)S(1)} %slice.8), channel_id=1, source_target_pairs={{0,4},{2,6},{4,0},{6,2},{8,12},{10,14},{12,8},{14,10},{16,20},{18,... | collective-permute-start | bytes 466952 | tf_op jit(solution)/shard_map/ppermute | solution.py:484
  36.1 6.2 %collective-permute-start.10 = (bf16[32,2432]{1,0:T(8,128)(2,1)S(1)}, bf16[32,2432]{1,0:T(8,128)(2,1)S(1)}, u32[]{:S(2)}, u32[]{:S(2)}) collective-permute-start(bf16[32,2432]{1,0:T(8,128)(2,1)S(1)} %slice.9), channel_id=1, source_target_pairs={{0,2},{2,0},{4,6},{6,4},{8,10},{10,8},{12,14},{14,12},{16,18},{18,... | collective-permute-start | bytes 466952 | tf_op jit(solution)/shard_map/ppermute | solution.py:484
  42.8 3.5 %collective-permute-start.13 = (bf16[64,2048]{1,0:T(8,128)(2,1)S(1)}, bf16[64,2048]{1,0:T(8,128)(2,1)S(1)}, u32[]{:S(2)}, u32[]{:S(2)}) collective-permute-start(bf16[64,2048]{1,0:T(8,128)(2,1)S(1)} %get-tuple-element.84), channel_id=1, source_target_pairs={{0,1},{1,0},{2,3},{3,2},{4,5},{5,4},{6,7},{7,6},{8,9},{9,8},{10,11... | collective-permute-start | bytes 786440 | tf_op jit(solution)/shard_map/ppermute | solution.py:481
  42.8 3.5 %collective-permute-start.14 = (bf16[64,2048]{1,0:T(8,128)(2,1)S(1)}, bf16[64,2048]{1,0:T(8,128)(2,1)S(1)}, u32[]{:S(2)}, u32[]{:S(2)}) collective-permute-start(bf16[64,2048]{1,0:T(8,128)(2,1)S(1)} %get-tuple-element.85), channel_id=1, source_target_pairs={{0,1},{1,0},{2,3},{3,2},{4,5},{5,4},{6,7},{7,6},{8,9},{9,8},{10,11... | collective-permute-start | bytes 786440 | tf_op jit(solution)/shard_map/ppermute | solution.py:481
  47.8 9.6 %collective-permute-start.17 = (bf16[256,512]{1,0:T(8,128)(2,1)S(1)}, bf16[256,512]{1,0:T(8,128)(2,1)S(1)}, u32[]{:S(2)}, u32[]{:S(2)}) collective-permute-start(bf16[256,512]{1,0:T(8,128)(2,1)S(1)} %get-tuple-element.93), channel_id=1, source_target_pairs={{0,2},{2,0},{4,6},{6,4},{8,10},{10,8},{12,14},{14,12},{16,18},{18,... | collective-permute-start | bytes 786440 | tf_op jit(solution)/shard_map/ppermute | solution.py:484
  48.4 13.8 %collective-permute-start.18 = (bf16[256,512]{1,0:T(8,128)(2,1)S(1)}, bf16[256,512]{1,0:T(8,128)(2,1)S(1)}, u32[]{:S(2)}, u32[]{:S(2)}) collective-permute-start(bf16[256,512]{1,0:T(8,128)(2,1)S(1)} %get-tuple-element.94), channel_id=1, source_target_pairs={{0,4},{2,6},{4,0},{6,2},{8,12},{10,14},{12,8},{14,10},{16,20},{18,... | collective-permute-start | bytes 786440 | tf_op jit(solution)/shard_map/ppermute | solution.py:484
  48.9 13.3 %collective-permute-start.19 = (bf16[256,512]{1,0:T(8,128)(2,1)S(1)}, bf16[256,512]{1,0:T(8,128)(2,1)S(1)}, u32[]{:S(2)}, u32[]{:S(2)}) collective-permute-start(bf16[256,512]{1,0:T(8,128)(2,1)S(1)} %get-tuple-element.95), channel_id=1, source_target_pairs={{0,6},{2,4},{4,2},{6,0},{8,14},{10,12},{12,10},{14,8},{16,22},{18,... | collective-permute-start | bytes 786440 | tf_op jit(solution)/shard_map/ppermute | solution.py:484
  51.3 19.1 %collective-permute-start.25 = (bf16[128,512]{1,0:T(8,128)(2,1)S(1)}, bf16[128,512]{1,0:T(8,128)(2,1)S(1)}, u32[]{:S(2)}, u32[]{:S(2)}) collective-permute-start(bf16[128,512]{1,0:T(8,128)(2,1)S(1)} %copy-done.1), channel_id=1, source_target_pairs={{0,16},{2,18},{4,20},{6,22},{8,24},{10,26},{12,28},{14,30},{16,0},... | collective-permute-start | bytes 393224 | tf_op jit(solution)/shard_map/ppermute | solution.py:484
  62.3 11.1 %collective-permute-start.20 = (bf16[64,512]{1,0:T(8,128)(2,1)S(1)}, bf16[64,512]{1,0:T(8,128)(2,1)S(1)}, u32[]{:S(2)}, u32[]{:S(2)}) collective-permute-start(bf16[64,512]{1,0:T(8,128)(2,1)S(1)} %get-tuple-element.97.refs_2_), channel_id=1, source_target_pairs={{0,8},{2,10},{4,12},{6,14},{8,0},{10,2},{12,4},{14,6},{16,24},{18,... | collective-permute-start | bytes 196616 | tf_op jit(solution)/shard_map/ppermute | solution.py:484
  66.1 7.4 %collective-permute-start.21 = (bf16[64,512]{1,0:T(8,128)(2,1)S(1)}, bf16[64,512]{1,0:T(8,128)(2,1)S(1)}, u32[]{:S(2)}, u32[]{:S(2)}) collective-permute-start(bf16[64,512]{1,0:T(8,128)(2,1)S(1)} %get-tuple-element.98.refs_3_), channel_id=1, source_target_pairs={{0,16},{2,18},{4,20},{6,22},{8,24},{10,26},{12,28},{14,30},{16,0},... | collective-permute-start | bytes 196616 | tf_op jit(solution)/shard_map/ppermute | solution.py:484
  68.4 6.9 %collective-permute-start.22 = (bf16[64,512]{1,0:T(8,128)(2,1)S(1)}, bf16[64,512]{1,0:T(8,128)(2,1)S(1)}, u32[]{:S(2)}, u32[]{:S(2)}) collective-permute-start(bf16[64,512]{1,0:T(8,128)(2,1)S(1)} %get-tuple-element.99.refs_4_), channel_id=1, source_target_pairs={{0,24},{2,26},{4,28},{6,30},{8,16},{10,18},{12,20},{14,22},{16,8},... | collective-permute-start | bytes 196616 | tf_op jit(solution)/shard_map/ppermute | solution.py:484
  69.8 7.2 %collective-permute-start.24 = (bf16[128,512]{1,0:T(8,128)(2,1)S(1)}, bf16[128,512]{1,0:T(8,128)(2,1)S(1)}, u32[]{:S(2)}, u32[]{:S(2)}) collective-permute-start(bf16[128,512]{1,0:T(8,128)(2,1)S(1)} %copy-done.1), channel_id=1, source_target_pairs={{0,8},{2,10},{4,12},{6,14},{8,0},{10,2},{12,4},{14,6},{16,24},{18,... | collective-permute-start | bytes 393224 | tf_op jit(solution)/shard_map/ppermute | solution.py:484
  70.4 8.3 %collective-permute-start.26 = (bf16[128,512]{1,0:T(8,128)(2,1)S(1)}, bf16[128,512]{1,0:T(8,128)(2,1)S(1)}, u32[]{:S(2)}, u32[]{:S(2)}) collective-permute-start(bf16[128,512]{1,0:T(8,128)(2,1)S(1)} %collective-permute-done.25.refs_2_), channel_id=1, source_target_pairs={{0,8},{2,10},{4,12},{6,14},{8,0},{10,2},{12,4},{14,6},{16,24},{18,... | collective-permute-start | bytes 393224 | tf_op jit(solution)/shard_map/ppermute | solution.py:484
  79.2 7.7 %collective-permute-start.27 = (bf16[32,2944]{1,0:T(8,128)(2,1)S(1)}, bf16[32,2944]{1,0:T(8,128)(2,1)S(1)}, u32[]{:S(2)}, u32[]{:S(2)}) collective-permute-start(bf16[32,2944]{1,0:T(8,128)(2,1)S(1)} %get-tuple-element.110), channel_id=1, source_target_pairs={{0,2},{2,0},{4,6},{6,4},{8,10},{10,8},{12,14},{14,12},{16,18},{18,... | collective-permute-start | bytes 565256 | tf_op jit(solution)/shard_map/ppermute | solution.py:484
  80.4 8.0 %collective-permute-start.28 = (bf16[32,2944]{1,0:T(8,128)(2,1)S(1)}, bf16[32,2944]{1,0:T(8,128)(2,1)S(1)}, u32[]{:S(2)}, u32[]{:S(2)}) collective-permute-start(bf16[32,2944]{1,0:T(8,128)(2,1)S(1)} %get-tuple-element.111), channel_id=1, source_target_pairs={{0,4},{2,6},{4,0},{6,2},{8,12},{10,14},{12,8},{14,10},{16,20},{18,... | collective-permute-start | bytes 565256 | tf_op jit(solution)/shard_map/ppermute | solution.py:484
  81.4 8.6 %collective-permute-start.29 = (bf16[32,2944]{1,0:T(8,128)(2,1)S(1)}, bf16[32,2944]{1,0:T(8,128)(2,1)S(1)}, u32[]{:S(2)}, u32[]{:S(2)}) collective-permute-start(bf16[32,2944]{1,0:T(8,128)(2,1)S(1)} %get-tuple-element.112), channel_id=1, source_target_pairs={{0,6},{2,4},{4,2},{6,0},{8,14},{10,12},{12,10},{14,8},{16,22},{18,... | collective-permute-start | bytes 565256 | tf_op jit(solution)/shard_map/ppermute | solution.py:484
  (15 other events, 107.2 us)
Sparse Core Ops, SparseCore 0:
  12.2 53.0 all-gather.1

commit v15 on v12

--- a/solution.py
+++ b/solution.py
@@ -502,14 +502,13 @@
         (mine,), (to_core(theirs),), residual, attn_gain[None, :], meta, depth
     )
     tokens, q_own, kv_own = lax.optimization_barrier((tokens, q_weight, kv_weight))
+    kv_rows = [kv_own, to_expert(kv_own, PLANE)]
     q_rows = lax.all_gather(q_own, "expert", axis=0, tiled=True, axis_index_groups=lines)
     weights = load((w_gate, w_up, w_down), (tokens,))
     line = to_z([tokens] * depth)
-    *line, gate, up, down, kv_own = lax.optimization_barrier((*line, *weights, kv_own))
+    *line, gate, up, down, kv_rows[1] = lax.optimization_barrier((*line, *weights, kv_rows[1]))
     weights = (gate, up, down)
-    kv_rows = [kv_own, to_expert(kv_own, PLANE)]
     near = to_plane(pack(line, firsts))
-    near[2], kv_rows[1] = lax.optimization_barrier((near[2], kv_rows[1]))
     cut = near[0].shape[0] // 2
     one, two = near[1][:cut], near[2][cut:]
     far = [to_expert(one, 2), to_expert(two, 1)]
@@ -519,9 +518,10 @@
     far_both = [*far, *map(to_core, far)]
     far_mine, *far_theirs = experts(far_both, weights, depth, 1)
     theirs += map(to_core, far_theirs)
-    parts = to_plane(chip_sum((near_mine, far_mine), theirs))
+    *sums, kv_own = lax.optimization_barrier((*chip_sum((near_mine, far_mine), theirs), kv_own))
+    parts = to_plane(sums)
     kv_rows.append(to_expert(kv_own, 2 * PLANE))
-    *parts, kv_rows[2] = lax.optimization_barrier((*plane_sum(parts, depth), kv_rows[2]))
+    parts = plane_sum(parts, depth)
     kv_rows.append(to_expert(kv_rows[2], PLANE))
     (q_rows,) = load((q_rows,), parts)
     parts = to_z(parts)

time: 103 us -> 98.5 us (0.956)
  waiting for transfers between devices: 43.7 us -> 32.1 us
  starting transfers between devices: 26.1 us -> 32.6 us
    ppermute x19, waiting for transfers between devices: 40.3 us -> 28.7 us  [to_expert(): lax.ppermute(value, 'expert', [(i, i ^ offset) for i in range(n_expert)])]
    ppermute x19, starting transfers between devices: 23.6 us -> 30.6 us  [to_expert(): lax.ppermute(value, 'expert', [(i, i ^ offset) for i in range(n_expert)])]
  transfers between devices with their start and end apart: 31 -> 31, of which waited for: 16 -> 15; matrix products, arithmetic and copies ran while one was open for 0% -> 1% of each run, Pallas kernels for 12% -> 13%
where the time goes in v15:
time: 98.5 us; the launch traced here: 98.4 us
  starting transfers between devices  32.6 us (33%)
  waiting for transfers between devices  32.1 us (33%)
  Pallas kernels  18.8 us (19%)
  between operations  14.3 us (15%)
    ppermute x19, starting transfers between devices, to_expert(): lax.ppermute(value, 'expert', [(i, i ^ offset) for i in range(n_expert)])  30.6 us
    ppermute x19, waiting for transfers between devices, to_expert(): lax.ppermute(value, 'expert', [(i, i ^ offset) for i in range(n_expert)])  28.7 us
    pallas_call x2, Pallas kernels, experts(): pl.pallas_call(functools.partial(expert_kernel, depth, chunk, len(blocks)...  6.05 us
    pallas_call x2, Pallas kernels, load(): pl.pallas_call(functools.partial(load_kernel, count), out_shape=tuple((pl...  5.74 us
    pallas_call x1, Pallas kernels, out_projection(): pl.pallas_call(functools.partial(out_projection_kernel, chunk), out_shape...  4.82 us
    ppermute x11, waiting for transfers between devices, to_core(): return lax.ppermute(value, 'tensor', [(0, 1), (1, 0)])  3.43 us
    ppermute x11, starting transfers between devices, to_core(): return lax.ppermute(value, 'tensor', [(0, 1), (1, 0)])  1.98 us
  transfers between devices with their start and end apart: 31, of which 15 were waited for; matrix products, arithmetic and copies ran while one was open for 1% of the time, Pallas kernels for 13%

profile of v15, /device:TPU:0, one launch (start us, length us, event | category | flops | bytes accessed | tf_op | source)
XLA Modules:
  0.0 98.4 jit_solution(10451924358815416648)
XLA Ops:
  7.3 4.8 %out_projection.1 = (f32[16,2048]{1,0:T(8,128)S(1)}, f32[16,2048]{1,0:T(8,128)S(1)}) custom-call(bf16[32,2048]{1,0:T(8,128)(2,1)} %a_hbm.1, bf16[2048,2048]{1,0:T(8,128)(2,1)} %w_hbm.1), custom_call_target="tpu_custom_call" | custom-call | tf_op jit(solution)/shard_map/out_projection/pallas_call | solution.py:77
  13.8 3.0 %collective-permute-start.4 = (bf16[128,512]{1,0:T(8,128)(2,1)S(1)}, bf16[128,512]{1,0:T(8,128)(2,1)S(1)}, u32[]{:S(2)}, u32[]{:S(2)}) collective-permute-start(bf16[128,512]{1,0:T(8,128)(2,1)S(1)} %copy-done.1), channel_id=1, source_target_pairs={{0,8},{2,10},{4,12},{6,14},{8,0},{10,2},{12,4},{14,6},{16,24},{18,... | collective-permute-start | bytes 393224 | tf_op jit(solution)/shard_map/ppermute | solution.py:484
  16.8 3.0 %collective-permute-start.2 = (bf16[16,2176]{1,0:T(8,128)(2,1)S(1)}, bf16[16,2176]{1,0:T(8,128)(2,1)S(1)}, u32[]{:S(2)}, u32[]{:S(2)}) collective-permute-start(bf16[16,2176]{1,0:T(8,128)(2,1)S(1)} %get-tuple-element.68.refs_3_.refs_0_), channel_id=1, source_target_pairs={{0,16},{2,18},{4,20},{6,22},{8,24},{10,26},{12,28},{14,30},{16,0},... | collective-permute-start | bytes 208904 | tf_op jit(solution)/shard_map/ppermute | solution.py:484
  19.8 1.3 %collective-permute-start.3 = (bf16[16,2176]{1,0:T(8,128)(2,1)S(1)}, bf16[16,2176]{1,0:T(8,128)(2,1)S(1)}, u32[]{:S(2)}, u32[]{:S(2)}) collective-permute-start(bf16[16,2176]{1,0:T(8,128)(2,1)S(1)} %get-tuple-element.68.refs_3_.refs_0_), channel_id=1, source_target_pairs={{0,24},{2,26},{4,28},{6,30},{8,16},{10,18},{12,20},{14,22},{16,8},... | collective-permute-start | bytes 208904 | tf_op jit(solution)/shard_map/ppermute | solution.py:484
  21.2 4.1 %load_weights.2 = (bf16[1,2048,768]{2,1,0:T(8,128)(2,1)S(1)}, bf16[1,2048,768]{2,1,0:T(8,128)(2,1)S(1)}, bf16[1,768,2048]{2,1,0:T(8,128)(2,1)S(1)}) custom-call(bf16[1,2048,768]{2,1,0:T(8,128)(2,1)} %refs_0_.1, bf16[1,2048,768]{2,1,0:T(8,128)(2,1)} %refs_1_.1, bf16[1,768,2048]{2,1,0:T(8,128)(2,1)} %refs_2_.3, ...), custom_call_target="tpu_custom_call" | custom-call | tf_op jit(solution)/shard_map/load_weights/pallas_call | solution.py:171
  25.3 2.1 %collective-permute-done.3.refs_3_ = bf16[16,2176]{1,0:T(8,128)(2,1)S(1)} collective-permute-done((bf16[16,2176]{1,0:T(8,128)(2,1)S(1)}, bf16[16,2176]{1,0:T(8,128)(2,1)S(1)}, u32[]{:S(2)}, u32[]{:S(2)}) %collective-permute-start.3) | collective-permute-done | bytes 69664 | tf_op jit(solution)/shard_map/ppermute | solution.py:484
  27.5 1.6 %collective-permute-start.5 = (bf16[64,2432]{1,0:T(8,128)(2,1)S(1)}, bf16[64,2432]{1,0:T(8,128)(2,1)S(1)}, u32[]{:S(2)}, u32[]{:S(2)}) collective-permute-start(bf16[64,2432]{1,0:T(8,128)(2,1)S(1)} %get-tuple-element.77), channel_id=1, source_target_pairs={{0,2},{2,0},{4,6},{6,4},{8,10},{10,8},{12,14},{14,12},{16,18},{18,... | collective-permute-start | bytes 933896 | tf_op jit(solution)/shard_map/ppermute | solution.py:484
  29.0 1.5 %collective-permute-start.6 = (bf16[64,2432]{1,0:T(8,128)(2,1)S(1)}, bf16[64,2432]{1,0:T(8,128)(2,1)S(1)}, u32[]{:S(2)}, u32[]{:S(2)}) collective-permute-start(bf16[64,2432]{1,0:T(8,128)(2,1)S(1)} %get-tuple-element.78), channel_id=1, source_target_pairs={{0,4},{2,6},{4,0},{6,2},{8,12},{10,14},{12,8},{14,10},{16,20},{18,... | collective-permute-start | bytes 933896 | tf_op jit(solution)/shard_map/ppermute | solution.py:484
  30.6 5.2 %collective-permute-done.5.refs_1_.refs_5_ = bf16[64,2432]{1,0:T(8,128)(2,1)S(1)} collective-permute-done((bf16[64,2432]{1,0:T(8,128)(2,1)S(1)}, bf16[64,2432]{1,0:T(8,128)(2,1)S(1)}, u32[]{:S(2)}, u32[]{:S(2)}) %collective-permute-start.5) | collective-permute-done | bytes 311328 | tf_op jit(solution)/shard_map/ppermute | solution.py:484
  37.0 1.6 %collective-permute-start.10 = (bf16[32,2432]{1,0:T(8,128)(2,1)S(1)}, bf16[32,2432]{1,0:T(8,128)(2,1)S(1)}, u32[]{:S(2)}, u32[]{:S(2)}) collective-permute-start(bf16[32,2432]{1,0:T(8,128)(2,1)S(1)} %slice.8), channel_id=1, source_target_pairs={{0,4},{2,6},{4,0},{6,2},{8,12},{10,14},{12,8},{14,10},{16,20},{18,... | collective-permute-start | bytes 466952 | tf_op jit(solution)/shard_map/ppermute | solution.py:484
  39.5 4.1 %experts.2 = (bf16[192,2048]{1,0:T(8,128)(2,1)S(1)}, bf16[64,2048]{1,0:T(8,128)(2,1)S(1)}, bf16[64,2048]{1,0:T(8,128)(2,1)S(1)}, bf16[64,2048]{1,0:T(8,128)(2,1)S(1)}) custom-call(bf16[64,2432]{1,0:T(8,128)(2,1)S(1)} %get-tuple-element.76.refs_0_.refs_4_, bf16[64,2432]{1,0:T(8,128)(2,1)S(1)} %collective-permute-done.5.refs_1_.refs_5_, ...), custom_call_target="tpu_custom_call" | custom-call | flops 3623878656 | tf_op jit(solution)/shard_map/experts/pallas_call | solution.py:231
  46.4 2.0 %experts.3 = (bf16[64,2048]{1,0:T(8,128)(2,1)S(1)}, bf16[64,2048]{1,0:T(8,128)(2,1)S(1)}) custom-call(bf16[32,2432]{1,0:T(8,128)(2,1)S(1)} %collective-permute-done.10.refs_0_.refs_7_, bf16[32,2432]{1,0:T(8,128)(2,1)S(1)} %collective-permute-done.11.refs_1_.refs_8_, bf16[32,2432]{1,0:T(8,128)(2,1)S(1)} %collective-permute-done.12.refs_2_, ...), custom_call_target="tpu_custom_call" | custom-call | flops 1207959552 | tf_op jit(solution)/shard_map/experts/pallas_call | solution.py:231
  51.4 2.4 %collective-permute-start.20 = (bf16[256,512]{1,0:T(8,128)(2,1)S(1)}, bf16[256,512]{1,0:T(8,128)(2,1)S(1)}, u32[]{:S(2)}, u32[]{:S(2)}) collective-permute-start(bf16[256,512]{1,0:T(8,128)(2,1)S(1)} %get-tuple-element.98), channel_id=1, source_target_pairs={{0,6},{2,4},{4,2},{6,0},{8,14},{10,12},{12,10},{14,8},{16,22},{18,... | collective-permute-start | bytes 786440 | tf_op jit(solution)/shard_map/ppermute | solution.py:484
  53.8 4.3 %collective-permute-start.25 = (bf16[128,512]{1,0:T(8,128)(2,1)S(1)}, bf16[128,512]{1,0:T(8,128)(2,1)S(1)}, u32[]{:S(2)}, u32[]{:S(2)}) collective-permute-start(bf16[128,512]{1,0:T(8,128)(2,1)S(1)} %copy-done.1), channel_id=1, source_target_pairs={{0,16},{2,18},{4,20},{6,22},{8,24},{10,26},{12,28},{14,30},{16,0},... | collective-permute-start | bytes 393224 | tf_op jit(solution)/shard_map/ppermute | solution.py:484
  59.5 5.2 %collective-permute-done.19.refs_2_ = bf16[256,512]{1,0:T(8,128)(2,1)S(1)} collective-permute-done((bf16[256,512]{1,0:T(8,128)(2,1)S(1)}, bf16[256,512]{1,0:T(8,128)(2,1)S(1)}, u32[]{:S(2)}, u32[]{:S(2)}) %collective-permute-start.19) | collective-permute-done | bytes 262176 | tf_op jit(solution)/shard_map/ppermute | solution.py:484
  64.9 1.5 %collective-permute-start.21 = (bf16[64,512]{1,0:T(8,128)(2,1)S(1)}, bf16[64,512]{1,0:T(8,128)(2,1)S(1)}, u32[]{:S(2)}, u32[]{:S(2)}) collective-permute-start(bf16[64,512]{1,0:T(8,128)(2,1)S(1)} %get-tuple-element.100.refs_2_), channel_id=1, source_target_pairs={{0,8},{2,10},{4,12},{6,14},{8,0},{10,2},{12,4},{14,6},{16,24},{18,... | collective-permute-start | bytes 196616 | tf_op jit(solution)/shard_map/ppermute | solution.py:484
  66.4 2.9 %collective-permute-start.22 = (bf16[64,512]{1,0:T(8,128)(2,1)S(1)}, bf16[64,512]{1,0:T(8,128)(2,1)S(1)}, u32[]{:S(2)}, u32[]{:S(2)}) collective-permute-start(bf16[64,512]{1,0:T(8,128)(2,1)S(1)} %get-tuple-element.101.refs_3_), channel_id=1, source_target_pairs={{0,16},{2,18},{4,20},{6,22},{8,24},{10,26},{12,28},{14,30},{16,0},... | collective-permute-start | bytes 196616 | tf_op jit(solution)/shard_map/ppermute | solution.py:484
  69.2 1.4 %collective-permute-start.23 = (bf16[64,512]{1,0:T(8,128)(2,1)S(1)}, bf16[64,512]{1,0:T(8,128)(2,1)S(1)}, u32[]{:S(2)}, u32[]{:S(2)}) collective-permute-start(bf16[64,512]{1,0:T(8,128)(2,1)S(1)} %get-tuple-element.102.refs_4_), channel_id=1, source_target_pairs={{0,24},{2,26},{4,28},{6,30},{8,16},{10,18},{12,20},{14,22},{16,8},... | collective-permute-start | bytes 196616 | tf_op jit(solution)/shard_map/ppermute | solution.py:484
  71.2 1.6 %load_weights.3.q_ref = bf16[512,2048]{1,0:T(8,128)(2,1)S(1)} custom-call(bf16[512,2048]{1,0:T(8,128)(2,1)} %all-gather.2.cloned.1.call-done.refs_0_, bf16[64,512]{1,0:T(8,128)(2,1)S(1)} %get-tuple-element.104.refs_1_.refs_0_, bf16[64,512]{1,0:T(8,128)(2,1)S(1)} %get-tuple-element.100.refs_2_, bf16[64,512]{1,0:T(8,128)(2,1)S(1)} %get-tuple-element.101.refs_3_, ...), custom_call_target="tpu_custom_call" | custom-call | tf_op jit(solution)/shard_map/load_weights/pallas_call | solution.py:171
  72.9 3.2 %collective-permute-done.23.refs_3_ = bf16[64,512]{1,0:T(8,128)(2,1)S(1)} collective-permute-done((bf16[64,512]{1,0:T(8,128)(2,1)S(1)}, bf16[64,512]{1,0:T(8,128)(2,1)S(1)}, u32[]{:S(2)}, u32[]{:S(2)}) %collective-permute-start.23) | collective-permute-done | bytes 65568 | tf_op jit(solution)/shard_map/ppermute | solution.py:484
  78.1 2.0 %collective-permute-start.27 = (bf16[32,2944]{1,0:T(8,128)(2,1)S(1)}, bf16[32,2944]{1,0:T(8,128)(2,1)S(1)}, u32[]{:S(2)}, u32[]{:S(2)}) collective-permute-start(bf16[32,2944]{1,0:T(8,128)(2,1)S(1)} %get-tuple-element.114), channel_id=1, source_target_pairs={{0,2},{2,0},{4,6},{6,4},{8,10},{10,8},{12,14},{14,12},{16,18},{18,... | collective-permute-start | bytes 565256 | tf_op jit(solution)/shard_map/ppermute | solution.py:484
  80.1 1.6 %collective-permute-start.29 = (bf16[32,2944]{1,0:T(8,128)(2,1)S(1)}, bf16[32,2944]{1,0:T(8,128)(2,1)S(1)}, u32[]{:S(2)}, u32[]{:S(2)}) collective-permute-start(bf16[32,2944]{1,0:T(8,128)(2,1)S(1)} %get-tuple-element.116), channel_id=1, source_target_pairs={{0,6},{2,4},{4,2},{6,0},{8,14},{10,12},{12,10},{14,8},{16,22},{18,... | collective-permute-start | bytes 565256 | tf_op jit(solution)/shard_map/ppermute | solution.py:484
  81.7 4.1 %collective-permute-done.27.refs_1_ = bf16[32,2944]{1,0:T(8,128)(2,1)S(1)} collective-permute-done((bf16[32,2944]{1,0:T(8,128)(2,1)S(1)}, bf16[32,2944]{1,0:T(8,128)(2,1)S(1)}, u32[]{:S(2)}, u32[]{:S(2)}) %collective-permute-start.27) | collective-permute-done | bytes 188448 | tf_op jit(solution)/shard_map/ppermute | solution.py:484
  85.7 4.9 %collective-permute-done.28.refs_2_ = bf16[32,2944]{1,0:T(8,128)(2,1)S(1)} collective-permute-done((bf16[32,2944]{1,0:T(8,128)(2,1)S(1)}, bf16[32,2944]{1,0:T(8,128)(2,1)S(1)}, u32[]{:S(2)}, u32[]{:S(2)}) %collective-permute-start.28) | collective-permute-done | bytes 188448 | tf_op jit(solution)/shard_map/ppermute | solution.py:484
  (76 shorter events, 14.8 us)
Async XLA Ops:
  7.2 64.0 %all-gather.2.cloned.1.call-start = ((), (), s32[]{:S(2)}) async-start(), calls=%async_computation | async-start | bytes 2621440 | tf_op jit(solution)/shard_map/all_gather | solution.py:506
  13.8 13.6 %collective-permute-start.4 = (bf16[128,512]{1,0:T(8,128)(2,1)S(1)}, bf16[128,512]{1,0:T(8,128)(2,1)S(1)}, u32[]{:S(2)}, u32[]{:S(2)}) collective-permute-start(bf16[128,512]{1,0:T(8,128)(2,1)S(1)} %copy-done.1), channel_id=1, source_target_pairs={{0,8},{2,10},{4,12},{6,14},{8,0},{10,2},{12,4},{14,6},{16,24},{18,... | collective-permute-start | bytes 393224 | tf_op jit(solution)/shard_map/ppermute | solution.py:484
  16.8 8.5 %collective-permute-start.1 = (bf16[16,2176]{1,0:T(8,128)(2,1)S(1)}, bf16[16,2176]{1,0:T(8,128)(2,1)S(1)}, u32[]{:S(2)}, u32[]{:S(2)}) collective-permute-start(bf16[16,2176]{1,0:T(8,128)(2,1)S(1)} %get-tuple-element.68.refs_3_.refs_0_), channel_id=1, source_target_pairs={{0,8},{2,10},{4,12},{6,14},{8,0},{10,2},{12,4},{14,6},{16,24},{18,... | collective-permute-start | bytes 208904 | tf_op jit(solution)/shard_map/ppermute | solution.py:484
  16.8 8.5 %collective-permute-start.2 = (bf16[16,2176]{1,0:T(8,128)(2,1)S(1)}, bf16[16,2176]{1,0:T(8,128)(2,1)S(1)}, u32[]{:S(2)}, u32[]{:S(2)}) collective-permute-start(bf16[16,2176]{1,0:T(8,128)(2,1)S(1)} %get-tuple-element.68.refs_3_.refs_0_), channel_id=1, source_target_pairs={{0,16},{2,18},{4,20},{6,22},{8,24},{10,26},{12,28},{14,30},{16,0},... | collective-permute-start | bytes 208904 | tf_op jit(solution)/shard_map/ppermute | solution.py:484
  19.8 7.6 %collective-permute-start.3 = (bf16[16,2176]{1,0:T(8,128)(2,1)S(1)}, bf16[16,2176]{1,0:T(8,128)(2,1)S(1)}, u32[]{:S(2)}, u32[]{:S(2)}) collective-permute-start(bf16[16,2176]{1,0:T(8,128)(2,1)S(1)} %get-tuple-element.68.refs_3_.refs_0_), channel_id=1, source_target_pairs={{0,24},{2,26},{4,28},{6,30},{8,16},{10,18},{12,20},{14,22},{16,8},... | collective-permute-start | bytes 208904 | tf_op jit(solution)/shard_map/ppermute | solution.py:484
  27.5 8.3 %collective-permute-start.5 = (bf16[64,2432]{1,0:T(8,128)(2,1)S(1)}, bf16[64,2432]{1,0:T(8,128)(2,1)S(1)}, u32[]{:S(2)}, u32[]{:S(2)}) collective-permute-start(bf16[64,2432]{1,0:T(8,128)(2,1)S(1)} %get-tuple-element.77), channel_id=1, source_target_pairs={{0,2},{2,0},{4,6},{6,4},{8,10},{10,8},{12,14},{14,12},{16,18},{18,... | collective-permute-start | bytes 933896 | tf_op jit(solution)/shard_map/ppermute | solution.py:484
  29.0 8.0 %collective-permute-start.6 = (bf16[64,2432]{1,0:T(8,128)(2,1)S(1)}, bf16[64,2432]{1,0:T(8,128)(2,1)S(1)}, u32[]{:S(2)}, u32[]{:S(2)}) collective-permute-start(bf16[64,2432]{1,0:T(8,128)(2,1)S(1)} %get-tuple-element.78), channel_id=1, source_target_pairs={{0,4},{2,6},{4,0},{6,2},{8,12},{10,14},{12,8},{14,10},{16,20},{18,... | collective-permute-start | bytes 933896 | tf_op jit(solution)/shard_map/ppermute | solution.py:484
  30.6 8.9 %collective-permute-start.7 = (bf16[64,2432]{1,0:T(8,128)(2,1)S(1)}, bf16[64,2432]{1,0:T(8,128)(2,1)S(1)}, u32[]{:S(2)}, u32[]{:S(2)}) collective-permute-start(bf16[64,2432]{1,0:T(8,128)(2,1)S(1)} %get-tuple-element.76.refs_0_.refs_4_), channel_id=1, source_target_pairs={{0,1},{1,0},{2,3},{3,2},{4,5},{5,4},{6,7},{7,6},{8,9},{9,8},{10,11... | collective-permute-start | bytes 933896 | tf_op jit(solution)/shard_map/ppermute | solution.py:481
  35.8 3.7 %collective-permute-start.8 = (bf16[64,2432]{1,0:T(8,128)(2,1)S(1)}, bf16[64,2432]{1,0:T(8,128)(2,1)S(1)}, u32[]{:S(2)}, u32[]{:S(2)}) collective-permute-start(bf16[64,2432]{1,0:T(8,128)(2,1)S(1)} %collective-permute-done.5.refs_1_.refs_5_), channel_id=1, source_target_pairs={{0,1},{1,0},{2,3},{3,2},{4,5},{5,4},{6,7},{7,6},{8,9},{9,8},{10,11... | collective-permute-start | bytes 933896 | tf_op jit(solution)/shard_map/ppermute | solution.py:481
  37.0 6.5 %collective-permute-start.10 = (bf16[32,2432]{1,0:T(8,128)(2,1)S(1)}, bf16[32,2432]{1,0:T(8,128)(2,1)S(1)}, u32[]{:S(2)}, u32[]{:S(2)}) collective-permute-start(bf16[32,2432]{1,0:T(8,128)(2,1)S(1)} %slice.8), channel_id=1, source_target_pairs={{0,4},{2,6},{4,0},{6,2},{8,12},{10,14},{12,8},{14,10},{16,20},{18,... | collective-permute-start | bytes 466952 | tf_op jit(solution)/shard_map/ppermute | solution.py:484
  38.6 6.2 %collective-permute-start.11 = (bf16[32,2432]{1,0:T(8,128)(2,1)S(1)}, bf16[32,2432]{1,0:T(8,128)(2,1)S(1)}, u32[]{:S(2)}, u32[]{:S(2)}) collective-permute-start(bf16[32,2432]{1,0:T(8,128)(2,1)S(1)} %slice.9), channel_id=1, source_target_pairs={{0,2},{2,0},{4,6},{6,4},{8,10},{10,8},{12,14},{14,12},{16,18},{18,... | collective-permute-start | bytes 466952 | tf_op jit(solution)/shard_map/ppermute | solution.py:484
  45.3 3.5 %collective-permute-start.14 = (bf16[64,2048]{1,0:T(8,128)(2,1)S(1)}, bf16[64,2048]{1,0:T(8,128)(2,1)S(1)}, u32[]{:S(2)}, u32[]{:S(2)}) collective-permute-start(bf16[64,2048]{1,0:T(8,128)(2,1)S(1)} %get-tuple-element.87), channel_id=1, source_target_pairs={{0,1},{1,0},{2,3},{3,2},{4,5},{5,4},{6,7},{7,6},{8,9},{9,8},{10,11... | collective-permute-start | bytes 786440 | tf_op jit(solution)/shard_map/ppermute | solution.py:481
  45.3 3.5 %collective-permute-start.15 = (bf16[64,2048]{1,0:T(8,128)(2,1)S(1)}, bf16[64,2048]{1,0:T(8,128)(2,1)S(1)}, u32[]{:S(2)}, u32[]{:S(2)}) collective-permute-start(bf16[64,2048]{1,0:T(8,128)(2,1)S(1)} %get-tuple-element.88), channel_id=1, source_target_pairs={{0,1},{1,0},{2,3},{3,2},{4,5},{5,4},{6,7},{7,6},{8,9},{9,8},{10,11... | collective-permute-start | bytes 786440 | tf_op jit(solution)/shard_map/ppermute | solution.py:481
  50.3 9.2 %collective-permute-start.18 = (bf16[256,512]{1,0:T(8,128)(2,1)S(1)}, bf16[256,512]{1,0:T(8,128)(2,1)S(1)}, u32[]{:S(2)}, u32[]{:S(2)}) collective-permute-start(bf16[256,512]{1,0:T(8,128)(2,1)S(1)} %get-tuple-element.96), channel_id=1, source_target_pairs={{0,2},{2,0},{4,6},{6,4},{8,10},{10,8},{12,14},{14,12},{16,18},{18,... | collective-permute-start | bytes 786440 | tf_op jit(solution)/shard_map/ppermute | solution.py:484
  50.9 13.8 %collective-permute-start.19 = (bf16[256,512]{1,0:T(8,128)(2,1)S(1)}, bf16[256,512]{1,0:T(8,128)(2,1)S(1)}, u32[]{:S(2)}, u32[]{:S(2)}) collective-permute-start(bf16[256,512]{1,0:T(8,128)(2,1)S(1)} %get-tuple-element.97), channel_id=1, source_target_pairs={{0,4},{2,6},{4,0},{6,2},{8,12},{10,14},{12,8},{14,10},{16,20},{18,... | collective-permute-start | bytes 786440 | tf_op jit(solution)/shard_map/ppermute | solution.py:484
  51.4 13.3 %collective-permute-start.20 = (bf16[256,512]{1,0:T(8,128)(2,1)S(1)}, bf16[256,512]{1,0:T(8,128)(2,1)S(1)}, u32[]{:S(2)}, u32[]{:S(2)}) collective-permute-start(bf16[256,512]{1,0:T(8,128)(2,1)S(1)} %get-tuple-element.98), channel_id=1, source_target_pairs={{0,6},{2,4},{4,2},{6,0},{8,14},{10,12},{12,10},{14,8},{16,22},{18,... | collective-permute-start | bytes 786440 | tf_op jit(solution)/shard_map/ppermute | solution.py:484
  53.8 16.8 %collective-permute-start.25 = (bf16[128,512]{1,0:T(8,128)(2,1)S(1)}, bf16[128,512]{1,0:T(8,128)(2,1)S(1)}, u32[]{:S(2)}, u32[]{:S(2)}) collective-permute-start(bf16[128,512]{1,0:T(8,128)(2,1)S(1)} %copy-done.1), channel_id=1, source_target_pairs={{0,16},{2,18},{4,20},{6,22},{8,24},{10,26},{12,28},{14,30},{16,0},... | collective-permute-start | bytes 393224 | tf_op jit(solution)/shard_map/ppermute | solution.py:484
  64.9 7.9 %collective-permute-start.21 = (bf16[64,512]{1,0:T(8,128)(2,1)S(1)}, bf16[64,512]{1,0:T(8,128)(2,1)S(1)}, u32[]{:S(2)}, u32[]{:S(2)}) collective-permute-start(bf16[64,512]{1,0:T(8,128)(2,1)S(1)} %get-tuple-element.100.refs_2_), channel_id=1, source_target_pairs={{0,8},{2,10},{4,12},{6,14},{8,0},{10,2},{12,4},{14,6},{16,24},{18,... | collective-permute-start | bytes 196616 | tf_op jit(solution)/shard_map/ppermute | solution.py:484
  66.4 6.5 %collective-permute-start.22 = (bf16[64,512]{1,0:T(8,128)(2,1)S(1)}, bf16[64,512]{1,0:T(8,128)(2,1)S(1)}, u32[]{:S(2)}, u32[]{:S(2)}) collective-permute-start(bf16[64,512]{1,0:T(8,128)(2,1)S(1)} %get-tuple-element.101.refs_3_), channel_id=1, source_target_pairs={{0,16},{2,18},{4,20},{6,22},{8,24},{10,26},{12,28},{14,30},{16,0},... | collective-permute-start | bytes 196616 | tf_op jit(solution)/shard_map/ppermute | solution.py:484
  69.2 6.8 %collective-permute-start.23 = (bf16[64,512]{1,0:T(8,128)(2,1)S(1)}, bf16[64,512]{1,0:T(8,128)(2,1)S(1)}, u32[]{:S(2)}, u32[]{:S(2)}) collective-permute-start(bf16[64,512]{1,0:T(8,128)(2,1)S(1)} %get-tuple-element.102.refs_4_), channel_id=1, source_target_pairs={{0,24},{2,26},{4,28},{6,30},{8,16},{10,18},{12,20},{14,22},{16,8},... | collective-permute-start | bytes 196616 | tf_op jit(solution)/shard_map/ppermute | solution.py:484
  70.6 5.8 %collective-permute-start.26 = (bf16[128,512]{1,0:T(8,128)(2,1)S(1)}, bf16[128,512]{1,0:T(8,128)(2,1)S(1)}, u32[]{:S(2)}, u32[]{:S(2)}) collective-permute-start(bf16[128,512]{1,0:T(8,128)(2,1)S(1)} %collective-permute-done.25.refs_2_), channel_id=1, source_target_pairs={{0,8},{2,10},{4,12},{6,14},{8,0},{10,2},{12,4},{14,6},{16,24},{18,... | collective-permute-start | bytes 393224 | tf_op jit(solution)/shard_map/ppermute | solution.py:484
  78.1 7.6 %collective-permute-start.27 = (bf16[32,2944]{1,0:T(8,128)(2,1)S(1)}, bf16[32,2944]{1,0:T(8,128)(2,1)S(1)}, u32[]{:S(2)}, u32[]{:S(2)}) collective-permute-start(bf16[32,2944]{1,0:T(8,128)(2,1)S(1)} %get-tuple-element.114), channel_id=1, source_target_pairs={{0,2},{2,0},{4,6},{6,4},{8,10},{10,8},{12,14},{14,12},{16,18},{18,... | collective-permute-start | bytes 565256 | tf_op jit(solution)/shard_map/ppermute | solution.py:484
  80.1 10.5 %collective-permute-start.28 = (bf16[32,2944]{1,0:T(8,128)(2,1)S(1)}, bf16[32,2944]{1,0:T(8,128)(2,1)S(1)}, u32[]{:S(2)}, u32[]{:S(2)}) collective-permute-start(bf16[32,2944]{1,0:T(8,128)(2,1)S(1)} %get-tuple-element.115), channel_id=1, source_target_pairs={{0,4},{2,6},{4,0},{6,2},{8,12},{10,14},{12,8},{14,10},{16,20},{18,... | collective-permute-start | bytes 565256 | tf_op jit(solution)/shard_map/ppermute | solution.py:484
  80.1 10.5 %collective-permute-start.29 = (bf16[32,2944]{1,0:T(8,128)(2,1)S(1)}, bf16[32,2944]{1,0:T(8,128)(2,1)S(1)}, u32[]{:S(2)}, u32[]{:S(2)}) collective-permute-start(bf16[32,2944]{1,0:T(8,128)(2,1)S(1)} %get-tuple-element.116), channel_id=1, source_target_pairs={{0,6},{2,4},{4,2},{6,0},{8,14},{10,12},{12,10},{14,8},{16,22},{18,... | collective-permute-start | bytes 565256 | tf_op jit(solution)/shard_map/ppermute | solution.py:484
  (15 other events, 104.7 us)
Sparse Core Ops, SparseCore 0:
  13.9 53.9 all-gather.1

commit v16 on v14

--- a/solution.py
+++ b/solution.py
@@ -349,17 +349,18 @@
     )(*parts, *packed, gain)
 
 
-def projection_kernel(chunk, mine_ref, theirs_ref, next_ref, q_ref, *refs):
-    kv_refs, out_refs, kv_buf = refs[: -PLANE - 1], refs[-PLANE - 1 : -1], refs[-1]
-    depth = len(kv_refs)
+def projection_kernel(chunk, count, mine_ref, theirs_ref, next_ref, *refs):
+    weight_refs, out_refs, order_buf = refs[:count], refs[count:-1], refs[-1]
     rows, extended = mine_ref.shape
     part = extended - META
-    sub = part // depth
-    q_cols, kv_cols = q_ref.shape[1], kv_buf.shape[1]
-    cols = q_cols + kv_cols
+    sub = part // count
+    cols = weight_refs[0].shape[1]
     line = lax.axis_index("expert") // PLANE
-    for d, ref in enumerate(kv_refs):
-        kv_buf[lanes((line ^ d) * sub, sub), :] = ref[...]
+    for d in range(count):
+        at = lanes((line ^ d) * sub, sub)
+        here = slice(d * sub, (d + 1) * sub)
+        order_buf[:rows, here] = mine_ref[:, at]
+        order_buf[rows:, here] = theirs_ref[:, at]
     block = rows // PLANE
     tensor = lax.axis_index("tensor")
     own = lanes(tensor * block, block)
@@ -370,35 +371,31 @@
         out_refs[d][other, cols : cols + META] = theirs_ref[at, part:]
         out_refs[d][:block, cols + META :] = next_ref[at, : part // 2]
         out_refs[d][block:, cols + META :] = next_ref[at, part // 2 :]
-    both = jnp.concatenate([mine_ref[:, :part], theirs_ref[:, :part]], axis=0)
-
-    def multiply(weight, target):
-        product = jnp.dot(both, weight, preferred_element_type=jnp.float32).astype(jnp.bfloat16)
-        at = slice(target, target + weight.shape[1])
+    for start in range(0, cols, chunk):
+        at = slice(start, start + chunk)
+        weight = jnp.concatenate([ref[:, at] for ref in weight_refs], axis=0)
+        product = jnp.dot(order_buf[...], weight, preferred_element_type=jnp.float32)
+        product = product.astype(jnp.bfloat16)
         for d in range(PLANE):
             out_refs[d][own, at] = product[d * block : (d + 1) * block]
             out_refs[d][other, at] = product[rows + d * block : rows + (d + 1) * block]
 
-    multiply(kv_buf[...], q_cols)
-    for start in range(0, q_cols, chunk):
-        multiply(q_ref[:, start : start + chunk], start)
-
-
-def projection(mine, theirs, following, q_weight, kv_weights):
+
+def projection(mine, theirs, following, weights):
     rows, part = following.shape
-    q_cols, kv_cols = q_weight.shape[1], kv_weights[0].shape[1]
+    cols = weights[0].shape[1]
     chunk = 512
-    shape = pltpu.VMEM((2 * rows // PLANE, q_cols + kv_cols + META + part // 2), jnp.bfloat16)
-    return pl.pallas_call(
-        functools.partial(projection_kernel, chunk),
+    shape = pltpu.VMEM((2 * rows // PLANE, cols + META + part // 2), jnp.bfloat16)
+    return pl.pallas_call(
+        functools.partial(projection_kernel, chunk, len(weights)),
         out_shape=(shape,) * PLANE,
-        in_specs=[VMEM] * (4 + len(kv_weights)),
+        in_specs=[VMEM] * (3 + len(weights)),
         out_specs=(VMEM,) * PLANE,
-        scratch_shapes=[pltpu.VMEM((part, kv_cols), jnp.bfloat16)],
+        scratch_shapes=[pltpu.VMEM((2 * rows, part), jnp.bfloat16)],
         compiler_params=params(8),
         cost_estimate=SMALL,
         name="qkv_projection",
-    )(mine, theirs, following, q_weight, *kv_weights)
+    )(mine, theirs, following, *map(in_vmem, weights))
 
 
 def head_norm_kernel(depth, *refs):
@@ -496,13 +493,17 @@
     high = lax.reduce_precision(dense, 8, 7)
     meta = jnp.concatenate([high, dense - high], axis=1).astype(jnp.bfloat16)
 
-    lines = [list(range(i, n_expert, PLANE)) for i in range(PLANE)]
     mine, theirs = out_projection(attn_out, out_weight)
-    mine, q_own = lax.optimization_barrier((mine, q_weight))
-    q_rows = lax.all_gather(q_own, "expert", axis=0, tiled=True, axis_index_groups=lines)
+    mine, q_own, kv_own = lax.optimization_barrier((mine, q_weight, kv_weight))
+    joined = jnp.concatenate([q_own, kv_own], axis=1)
     tokens, *firsts = first_norm(
         (mine,), (to_core(theirs),), residual, attn_gain[None, :], meta, depth
     )
+    tokens, joined = lax.optimization_barrier((tokens, joined))
+    far_line = n_expert // 2
+    pairs = [[i, i + far_line] for i in range(far_line)]
+    pair_rows = lax.all_gather(joined, "expert", axis=0, axis_index_groups=pairs)
+    rows_of = [joined, to_expert(joined, PLANE)]
     weights = load((w_gate, w_up, w_down), (tokens,))
     line = to_z([tokens] * depth)
     *line, gate, up, down = lax.optimization_barrier((*line, *weights))
@@ -513,20 +514,18 @@
     far = [to_expert(one, 2), to_expert(two, 1)]
     near_mine, *near_theirs = experts((*near, *map(to_core, near)), weights, depth, len(near))
     theirs = list(map(to_core, near_theirs))
-    near_mine, *far = lax.optimization_barrier((near_mine, *far))
+    near_mine, rows_of[1], *far = lax.optimization_barrier((near_mine, rows_of[1], *far))
     far_both = [*far, *map(to_core, far)]
     far_mine, *far_theirs = experts(far_both, weights, depth, 1)
     theirs += map(to_core, far_theirs)
-    *sums, kv_own = lax.optimization_barrier((*chip_sum((near_mine, far_mine), theirs), kv_weight))
-    parts = to_plane(sums)
-    kv_rows = [kv_own, to_expert(kv_own, PLANE), to_expert(kv_own, 2 * PLANE)]
-    parts = plane_sum(parts, depth)
-    kv_rows.append(to_expert(kv_rows[2], PLANE))
-    (q_rows,) = load((q_rows,), parts)
-    parts = to_z(parts)
-    *parts, q_rows = lax.optimization_barrier((*parts, q_rows))
+    parts = to_plane(chip_sum((near_mine, far_mine), theirs))
+    parts[0], pair_rows = lax.optimization_barrier((parts[0], pair_rows))
+    other_half = 1 - lax.axis_index("expert").astype(jnp.int32) // far_line
+    rows_of.append(lax.dynamic_index_in_dim(pair_rows, other_half, 0, keepdims=False))
+    rows_of.append(to_expert(rows_of[2], PLANE))
+    parts = to_z(plane_sum(parts, depth))
     scaled, following = second_norm(parts, (*near, *far), input_gain[None, :])
-    products = to_plane(projection(scaled, to_core(scaled), following, q_rows, kv_rows))
+    products = to_plane(projection(scaled, to_core(scaled), following, rows_of))
     return head_norm(
         products,
         q_gain[None, :],

time: 98 us -> 118 us (1.20)
  local copies, waits for them, and re-layouts: 0.36 us -> 17.6 us
  waiting for transfers between devices: 28.5 us -> 40.1 us
  starting transfers between devices: 35.7 us -> 25.4 us
    unnamed x16 -> x52, local copies, waits for them, and re-layouts: 0.04 us -> 16.1 us
    ppermute x19 -> x18, starting transfers between devices: 33.7 us -> 23.4 us  [to_expert(): lax.ppermute(value, 'expert', [(i, i ^ offset) for i in range(n_expert)])]
    ppermute x19 -> x18, waiting for transfers between devices: 26.2 us -> 32.5 us  [to_expert(): lax.ppermute(value, 'expert', [(i, i ^ offset) for i in range(n_expert)])]
    all_gather x1, waiting for transfers between devices: 0.01 us -> 4.11 us  [per_device_dense(): lax.all_gather(joined, 'expert', axis=0, axis_index_groups=pairs)]
    pallas_call x2 -> x1, Pallas kernels: 5.73 us -> 3.78 us  [load(): pl.pallas_call(functools.partial(load_kernel, count), out_shape=tuple((pl...]
    pallas_call x2, Pallas kernels: 6.05 us -> 7.67 us  [experts(): pl.pallas_call(functools.partial(expert_kernel, depth, chunk, len(blocks)...]
    pallas_call x1, Pallas kernels: 0.24 us -> 1.45 us  [chip_sum(): pl.pallas_call(functools.partial(chip_sum_kernel, len(theirs)), out_shape...]
  transfers between devices with their start and end apart: 31 -> 30, of which waited for: 16 -> 14; matrix products, arithmetic and copies ran while one was open for 1% -> 1% of each run, Pallas kernels for 13% -> 11%
where the time goes in v16:
time: 118 us
  waiting for transfers between devices  40.1 us (34%)
  starting transfers between devices  25.4 us (22%)
  Pallas kernels  19.6 us (17%)
  local copies, waits for them, and re-layouts  17.6 us (15%)
  between operations  14.3 us (12%)
    ppermute x18, waiting for transfers between devices, to_expert(): lax.ppermute(value, 'expert', [(i, i ^ offset) for i in range(n_expert)])  32.5 us
    ppermute x18, starting transfers between devices, to_expert(): lax.ppermute(value, 'expert', [(i, i ^ offset) for i in range(n_expert)])  23.4 us
    unnamed x52, local copies, waits for them, and re-layouts  16.1 us
    pallas_call x2, Pallas kernels, experts(): pl.pallas_call(functools.partial(expert_kernel, depth, chunk, len(blocks)...  7.67 us
    pallas_call x1, Pallas kernels, out_projection(): pl.pallas_call(functools.partial(out_projection_kernel, chunk), out_shape...  4.83 us
    all_gather x1, waiting for transfers between devices, per_device_dense(): lax.all_gather(joined, 'expert', axis=0, axis_index_groups=pairs)  4.11 us
    pallas_call x1, Pallas kernels, load(): pl.pallas_call(functools.partial(load_kernel, count), out_shape=tuple((pl...  3.78 us
    ppermute x11, waiting for transfers between devices, to_core(): return lax.ppermute(value, 'tensor', [(0, 1), (1, 0)])  3.46 us
  transfers between devices with their start and end apart: 30, of which 14 were waited for; matrix products, arithmetic and copies ran while one was open for 1% of the time, Pallas kernels for 11%

profile of v16, /device:TPU:0, one launch (start us, length us, event | category | flops | bytes accessed | tf_op | source)
XLA Modules:
  0.0 118.0 jit_solution(17935353605878222448)
XLA Ops:
  7.3 4.8 %out_projection.1 = (f32[16,2048]{1,0:T(8,128)S(1)}, f32[16,2048]{1,0:T(8,128)S(1)}) custom-call(bf16[32,2048]{1,0:T(8,128)(2,1)} %a_hbm.1, bf16[2048,2048]{1,0:T(8,128)(2,1)} %w_hbm.1), custom_call_target="tpu_custom_call" | custom-call | tf_op jit(solution)/shard_map/out_projection/pallas_call | solution.py:77
  14.2 2.7 %collective-permute-start.1 = (bf16[16,2176]{1,0:T(8,128)(2,1)S(1)}, bf16[16,2176]{1,0:T(8,128)(2,1)S(1)}, u32[]{:S(2)}, u32[]{:S(2)}) collective-permute-start(bf16[16,2176]{1,0:T(8,128)(2,1)S(1)} %get-tuple-element.64.refs_3_.refs_0_), channel_id=1, source_target_pairs={{0,8},{2,10},{4,12},{6,14},{8,0},{10,2},{12,4},{14,6},{16,24},{18,... | collective-permute-start | bytes 208904 | tf_op jit(solution)/shard_map/ppermute | solution.py:481
  16.9 2.6 %collective-permute-start.2 = (bf16[16,2176]{1,0:T(8,128)(2,1)S(1)}, bf16[16,2176]{1,0:T(8,128)(2,1)S(1)}, u32[]{:S(2)}, u32[]{:S(2)}) collective-permute-start(bf16[16,2176]{1,0:T(8,128)(2,1)S(1)} %get-tuple-element.64.refs_3_.refs_0_), channel_id=1, source_target_pairs={{0,16},{2,18},{4,20},{6,22},{8,24},{10,26},{12,28},{14,30},{16,0},... | collective-permute-start | bytes 208904 | tf_op jit(solution)/shard_map/ppermute | solution.py:481
  19.5 3.8 %load_weights.1 = (bf16[1,2048,768]{2,1,0:T(8,128)(2,1)S(1)}, bf16[1,2048,768]{2,1,0:T(8,128)(2,1)S(1)}, bf16[1,768,2048]{2,1,0:T(8,128)(2,1)S(1)}) custom-call(bf16[1,2048,768]{2,1,0:T(8,128)(2,1)} %refs_0_.1, bf16[1,2048,768]{2,1,0:T(8,128)(2,1)} %refs_1_.1, bf16[1,768,2048]{2,1,0:T(8,128)(2,1)} %refs_2_.3, ...), custom_call_target="tpu_custom_call" | custom-call | tf_op jit(solution)/shard_map/load_weights/pallas_call | solution.py:171
  23.3 1.6 %copy-done.2 = bf16[1,2048,768]{2,1,0:T(8,128)(2,1)} copy-done((bf16[1,2048,768]{2,1,0:T(8,128)(2,1)}, bf16[1,2048,768]{2,1,0:T(8,128)(2,1)S(1)}, u32[]{:S(2)}) %copy-start.2) | copy-done | bytes 3145752
  24.9 1.7 %copy-done.5 = bf16[1,2048,768]{2,1,0:T(8,128)(2,1)} copy-done((bf16[1,2048,768]{2,1,0:T(8,128)(2,1)}, bf16[1,2048,768]{2,1,0:T(8,128)(2,1)S(1)}, u32[]{:S(2)}) %copy-start.5) | copy-done | bytes 3145752
  26.6 1.7 %copy-done.8 = bf16[1,768,2048]{2,1,0:T(8,128)(2,1)} copy-done((bf16[1,768,2048]{2,1,0:T(8,128)(2,1)}, bf16[1,768,2048]{2,1,0:T(8,128)(2,1)S(1)}, u32[]{:S(2)}) %copy-start.8) | copy-done | bytes 3145752
  28.4 1.8 %collective-permute-start.4 = (bf16[64,2432]{1,0:T(8,128)(2,1)S(1)}, bf16[64,2432]{1,0:T(8,128)(2,1)S(1)}, u32[]{:S(2)}, u32[]{:S(2)}) collective-permute-start(bf16[64,2432]{1,0:T(8,128)(2,1)S(1)} %get-tuple-element.73), channel_id=1, source_target_pairs={{0,2},{2,0},{4,6},{6,4},{8,10},{10,8},{12,14},{14,12},{16,18},{18,... | collective-permute-start | bytes 933896 | tf_op jit(solution)/shard_map/ppermute | solution.py:481
  32.4 5.2 %collective-permute-done.4.refs_1_.refs_5_ = bf16[64,2432]{1,0:T(8,128)(2,1)S(1)} collective-permute-done((bf16[64,2432]{1,0:T(8,128)(2,1)S(1)}, bf16[64,2432]{1,0:T(8,128)(2,1)S(1)}, u32[]{:S(2)}, u32[]{:S(2)}) %collective-permute-start.4) | collective-permute-done | bytes 311328 | tf_op jit(solution)/shard_map/ppermute | solution.py:481
  38.8 1.6 %collective-permute-start.10 = (bf16[32,2432]{1,0:T(8,128)(2,1)S(1)}, bf16[32,2432]{1,0:T(8,128)(2,1)S(1)}, u32[]{:S(2)}, u32[]{:S(2)}) collective-permute-start(bf16[32,2432]{1,0:T(8,128)(2,1)S(1)} %slice.8), channel_id=1, source_target_pairs={{0,4},{2,6},{4,0},{6,2},{8,12},{10,14},{12,8},{14,10},{16,20},{18,... | collective-permute-start | bytes 466952 | tf_op jit(solution)/shard_map/ppermute | solution.py:481
  41.3 1.9 %copy-done.3 = bf16[1,2048,768]{2,1,0:T(8,128)(2,1)S(1)} copy-done((bf16[1,2048,768]{2,1,0:T(8,128)(2,1)S(1)}, bf16[1,2048,768]{2,1,0:T(8,128)(2,1)}, u32[]{:S(2)}) %copy-start.3) | copy-done | bytes 3145752
  43.2 1.9 %copy-done.6 = bf16[1,2048,768]{2,1,0:T(8,128)(2,1)S(1)} copy-done((bf16[1,2048,768]{2,1,0:T(8,128)(2,1)S(1)}, bf16[1,2048,768]{2,1,0:T(8,128)(2,1)}, u32[]{:S(2)}) %copy-start.6) | copy-done | bytes 3145752
  45.1 1.9 %copy-done.9 = bf16[1,768,2048]{2,1,0:T(8,128)(2,1)S(1)} copy-done((bf16[1,768,2048]{2,1,0:T(8,128)(2,1)S(1)}, bf16[1,768,2048]{2,1,0:T(8,128)(2,1)}, u32[]{:S(2)}) %copy-start.9) | copy-done | bytes 3145752
  47.0 5.0 %experts.2 = (bf16[192,2048]{1,0:T(8,128)(2,1)S(1)}, bf16[64,2048]{1,0:T(8,128)(2,1)}, bf16[64,2048]{1,0:T(8,128)(2,1)}, bf16[64,2048]{1,0:T(8,128)(2,1)}) custom-call(bf16[64,2432]{1,0:T(8,128)(2,1)S(1)} %get-tuple-element.72.refs_0_.refs_4_, bf16[64,2432]{1,0:T(8,128)(2,1)S(1)} %collective-permute-done.4.refs_1_.refs_5_, ...), custom_call_target="tpu_custom_call" | custom-call | flops 3623878656 | tf_op jit(solution)/shard_map/experts/pallas_call | solution.py:231
  52.0 2.2 %collective-permute-done.9.refs_1_ = bf16[128,2560]{1,0:T(8,128)(2,1)S(1)} collective-permute-done((bf16[128,2560]{1,0:T(8,128)(2,1)S(1)}, bf16[128,2560]{1,0:T(8,128)(2,1)S(1)}, u32[]{:S(2)}, u32[]{:S(2)}) %collective-permute-start.9) | collective-permute-done | bytes 655392 | tf_op jit(solution)/shard_map/ppermute | solution.py:481
  55.9 2.7 %experts.3 = (bf16[64,2048]{1,0:T(8,128)(2,1)S(1)}, bf16[64,2048]{1,0:T(8,128)(2,1)}) custom-call(bf16[32,2432]{1,0:T(8,128)(2,1)S(1)} %collective-permute-done.10.refs_0_.refs_7_, bf16[32,2432]{1,0:T(8,128)(2,1)S(1)} %collective-permute-done.11.refs_1_.refs_8_, bf16[32,2432]{1,0:T(8,128)(2,1)S(1)} %collective-permute-done.12.refs_2_, ...), custom_call_target="tpu_custom_call" | custom-call | flops 1207959552 | tf_op jit(solution)/shard_map/experts/pallas_call | solution.py:231
  66.4 4.1 %all-gather.3.cloned.1.call-done = bf16[256,2560]{1,0:T(8,128)(2,1)} async-done(((bf16[128,2560]{1,0:T(8,128)(2,1)}), bf16[256,2560]{1,0:T(8,128)(2,1)}) %all-gather.3.cloned.1.call-update) | async-done | bytes 1310736 | tf_op jit(solution)/shard_map/all_gather | solution.py:505
  75.3 5.9 %collective-permute-done.18.refs_1_ = bf16[256,512]{1,0:T(8,128)(2,1)S(1)} collective-permute-done((bf16[256,512]{1,0:T(8,128)(2,1)}, bf16[256,512]{1,0:T(8,128)(2,1)S(1)}, u32[]{:S(2)}, u32[]{:S(2)}) %collective-permute-start.18) | collective-permute-done | bytes 262176 | tf_op jit(solution)/shard_map/ppermute | solution.py:481
  81.2 5.7 %collective-permute-done.19.refs_2_ = bf16[256,512]{1,0:T(8,128)(2,1)S(1)} collective-permute-done((bf16[256,512]{1,0:T(8,128)(2,1)}, bf16[256,512]{1,0:T(8,128)(2,1)S(1)}, u32[]{:S(2)}, u32[]{:S(2)}) %collective-permute-start.19) | collective-permute-done | bytes 262176 | tf_op jit(solution)/shard_map/ppermute | solution.py:481
  87.9 1.7 %collective-permute-start.21 = (bf16[64,512]{1,0:T(8,128)(2,1)S(1)}, bf16[64,512]{1,0:T(8,128)(2,1)S(1)}, u32[]{:S(2)}, u32[]{:S(2)}) collective-permute-start(bf16[64,512]{1,0:T(8,128)(2,1)S(1)} %get-tuple-element.94), channel_id=1, source_target_pairs={{0,8},{2,10},{4,12},{6,14},{8,0},{10,2},{12,4},{14,6},{16,24},{18,... | collective-permute-start | bytes 196616 | tf_op jit(solution)/shard_map/ppermute | solution.py:481
  90.1 2.3 %collective-permute-start.23 = (bf16[64,512]{1,0:T(8,128)(2,1)S(1)}, bf16[64,512]{1,0:T(8,128)(2,1)S(1)}, u32[]{:S(2)}, u32[]{:S(2)}) collective-permute-start(bf16[64,512]{1,0:T(8,128)(2,1)S(1)} %get-tuple-element.96), channel_id=1, source_target_pairs={{0,24},{2,26},{4,28},{6,30},{8,16},{10,18},{12,20},{14,22},{16,8},... | collective-permute-start | bytes 196616 | tf_op jit(solution)/shard_map/ppermute | solution.py:481
  92.4 3.1 %collective-permute-done.22.refs_2_ = bf16[64,512]{1,0:T(8,128)(2,1)S(1)} collective-permute-done((bf16[64,512]{1,0:T(8,128)(2,1)S(1)}, bf16[64,512]{1,0:T(8,128)(2,1)S(1)}, u32[]{:S(2)}, u32[]{:S(2)}) %collective-permute-start.22) | collective-permute-done | bytes 65568 | tf_op jit(solution)/shard_map/ppermute | solution.py:481
  101.8 4.1 %collective-permute-done.26.refs_1_ = bf16[32,2944]{1,0:T(8,128)(2,1)S(1)} collective-permute-done((bf16[32,2944]{1,0:T(8,128)(2,1)S(1)}, bf16[32,2944]{1,0:T(8,128)(2,1)S(1)}, u32[]{:S(2)}, u32[]{:S(2)}) %collective-permute-start.26) | collective-permute-done | bytes 188448 | tf_op jit(solution)/shard_map/ppermute | solution.py:481
  105.9 4.4 %collective-permute-done.27.refs_2_ = bf16[32,2944]{1,0:T(8,128)(2,1)S(1)} collective-permute-done((bf16[32,2944]{1,0:T(8,128)(2,1)S(1)}, bf16[32,2944]{1,0:T(8,128)(2,1)S(1)}, u32[]{:S(2)}, u32[]{:S(2)}) %collective-permute-start.27) | collective-permute-done | bytes 188448 | tf_op jit(solution)/shard_map/ppermute | solution.py:481
  (111 shorter events, 29.5 us)
Async XLA Ops:
  7.2 63.2 %all-gather.3.cloned.1.call-start = ((), (), s32[]{:S(2)}) async-start(), calls=%async_computation | async-start | bytes 1966080 | tf_op jit(solution)/shard_map/all_gather | solution.py:505
  14.2 14.1 %collective-permute-start.1 = (bf16[16,2176]{1,0:T(8,128)(2,1)S(1)}, bf16[16,2176]{1,0:T(8,128)(2,1)S(1)}, u32[]{:S(2)}, u32[]{:S(2)}) collective-permute-start(bf16[16,2176]{1,0:T(8,128)(2,1)S(1)} %get-tuple-element.64.refs_3_.refs_0_), channel_id=1, source_target_pairs={{0,8},{2,10},{4,12},{6,14},{8,0},{10,2},{12,4},{14,6},{16,24},{18,... | collective-permute-start | bytes 208904 | tf_op jit(solution)/shard_map/ppermute | solution.py:481
  16.9 11.4 %collective-permute-start.2 = (bf16[16,2176]{1,0:T(8,128)(2,1)S(1)}, bf16[16,2176]{1,0:T(8,128)(2,1)S(1)}, u32[]{:S(2)}, u32[]{:S(2)}) collective-permute-start(bf16[16,2176]{1,0:T(8,128)(2,1)S(1)} %get-tuple-element.64.refs_3_.refs_0_), channel_id=1, source_target_pairs={{0,16},{2,18},{4,20},{6,22},{8,24},{10,26},{12,28},{14,30},{16,0},... | collective-permute-start | bytes 208904 | tf_op jit(solution)/shard_map/ppermute | solution.py:481
  19.5 8.8 %collective-permute-start.3 = (bf16[16,2176]{1,0:T(8,128)(2,1)S(1)}, bf16[16,2176]{1,0:T(8,128)(2,1)S(1)}, u32[]{:S(2)}, u32[]{:S(2)}) collective-permute-start(bf16[16,2176]{1,0:T(8,128)(2,1)S(1)} %get-tuple-element.64.refs_3_.refs_0_), channel_id=1, source_target_pairs={{0,24},{2,26},{4,28},{6,30},{8,16},{10,18},{12,20},{14,22},{16,8},... | collective-permute-start | bytes 208904 | tf_op jit(solution)/shard_map/ppermute | solution.py:481
  28.4 9.2 %collective-permute-start.4 = (bf16[64,2432]{1,0:T(8,128)(2,1)S(1)}, bf16[64,2432]{1,0:T(8,128)(2,1)S(1)}, u32[]{:S(2)}, u32[]{:S(2)}) collective-permute-start(bf16[64,2432]{1,0:T(8,128)(2,1)S(1)} %get-tuple-element.73), channel_id=1, source_target_pairs={{0,2},{2,0},{4,6},{6,4},{8,10},{10,8},{12,14},{14,12},{16,18},{18,... | collective-permute-start | bytes 933896 | tf_op jit(solution)/shard_map/ppermute | solution.py:481
  30.1 8.7 %collective-permute-start.5 = (bf16[64,2432]{1,0:T(8,128)(2,1)S(1)}, bf16[64,2432]{1,0:T(8,128)(2,1)S(1)}, u32[]{:S(2)}, u32[]{:S(2)}) collective-permute-start(bf16[64,2432]{1,0:T(8,128)(2,1)S(1)} %get-tuple-element.74), channel_id=1, source_target_pairs={{0,4},{2,6},{4,0},{6,2},{8,12},{10,14},{12,8},{14,10},{16,20},{18,... | collective-permute-start | bytes 933896 | tf_op jit(solution)/shard_map/ppermute | solution.py:481
  31.7 22.5 %collective-permute-start.9 = (bf16[128,2560]{1,0:T(8,128)(2,1)S(1)}, bf16[128,2560]{1,0:T(8,128)(2,1)S(1)}, u32[]{:S(2)}, u32[]{:S(2)}) collective-permute-start(bf16[128,2560]{1,0:T(8,128)(2,1)S(1)} %copy-done.1), channel_id=1, source_target_pairs={{0,8},{2,10},{4,12},{6,14},{8,0},{10,2},{12,4},{14,6},{16,24},{18,... | collective-permute-start | bytes 1966088 | tf_op jit(solution)/shard_map/ppermute | solution.py:481
  32.4 8.0 %collective-permute-start.6 = (bf16[64,2432]{1,0:T(8,128)(2,1)S(1)}, bf16[64,2432]{1,0:T(8,128)(2,1)S(1)}, u32[]{:S(2)}, u32[]{:S(2)}) collective-permute-start(bf16[64,2432]{1,0:T(8,128)(2,1)S(1)} %get-tuple-element.72.refs_0_.refs_4_), channel_id=1, source_target_pairs={{0,1},{1,0},{2,3},{3,2},{4,5},{5,4},{6,7},{7,6},{8,9},{9,8},{10,11... | collective-permute-start | bytes 933896 | tf_op jit(solution)/shard_map/ppermute | solution.py:478
  37.6 3.7 %collective-permute-start.7 = (bf16[64,2432]{1,0:T(8,128)(2,1)S(1)}, bf16[64,2432]{1,0:T(8,128)(2,1)S(1)}, u32[]{:S(2)}, u32[]{:S(2)}) collective-permute-start(bf16[64,2432]{1,0:T(8,128)(2,1)S(1)} %collective-permute-done.4.refs_1_.refs_5_), channel_id=1, source_target_pairs={{0,1},{1,0},{2,3},{3,2},{4,5},{5,4},{6,7},{7,6},{8,9},{9,8},{10,11... | collective-permute-start | bytes 933896 | tf_op jit(solution)/shard_map/ppermute | solution.py:478
  38.8 13.1 %collective-permute-start.10 = (bf16[32,2432]{1,0:T(8,128)(2,1)S(1)}, bf16[32,2432]{1,0:T(8,128)(2,1)S(1)}, u32[]{:S(2)}, u32[]{:S(2)}) collective-permute-start(bf16[32,2432]{1,0:T(8,128)(2,1)S(1)} %slice.8), channel_id=1, source_target_pairs={{0,4},{2,6},{4,0},{6,2},{8,12},{10,14},{12,8},{14,10},{16,20},{18,... | collective-permute-start | bytes 466952 | tf_op jit(solution)/shard_map/ppermute | solution.py:481
  40.4 11.5 %collective-permute-start.11 = (bf16[32,2432]{1,0:T(8,128)(2,1)S(1)}, bf16[32,2432]{1,0:T(8,128)(2,1)S(1)}, u32[]{:S(2)}, u32[]{:S(2)}) collective-permute-start(bf16[32,2432]{1,0:T(8,128)(2,1)S(1)} %slice.9), channel_id=1, source_target_pairs={{0,2},{2,0},{4,6},{6,4},{8,10},{10,8},{12,14},{14,12},{16,18},{18,... | collective-permute-start | bytes 466952 | tf_op jit(solution)/shard_map/ppermute | solution.py:481
  54.7 5.0 %collective-permute-start.14 = (bf16[64,2048]{1,0:T(8,128)(2,1)}, bf16[64,2048]{1,0:T(8,128)(2,1)}, u32[]{:S(2)}, u32[]{:S(2)}) collective-permute-start(bf16[64,2048]{1,0:T(8,128)(2,1)} %get-tuple-element.84), channel_id=1, source_target_pairs={{0,1},{1,0},{2,3},{3,2},{4,5},{5,4},{6,7},{7,6},{8,9},{9,8},{10,11... | collective-permute-start | bytes 786440 | tf_op jit(solution)/shard_map/ppermute | solution.py:478
  54.7 5.0 %collective-permute-start.15 = (bf16[64,2048]{1,0:T(8,128)(2,1)}, bf16[64,2048]{1,0:T(8,128)(2,1)}, u32[]{:S(2)}, u32[]{:S(2)}) collective-permute-start(bf16[64,2048]{1,0:T(8,128)(2,1)} %get-tuple-element.85), channel_id=1, source_target_pairs={{0,1},{1,0},{2,3},{3,2},{4,5},{5,4},{6,7},{7,6},{8,9},{9,8},{10,11... | collective-permute-start | bytes 786440 | tf_op jit(solution)/shard_map/ppermute | solution.py:478
  55.2 4.5 %collective-permute-start.16 = (bf16[64,2048]{1,0:T(8,128)(2,1)}, bf16[64,2048]{1,0:T(8,128)(2,1)}, u32[]{:S(2)}, u32[]{:S(2)}) collective-permute-start(bf16[64,2048]{1,0:T(8,128)(2,1)} %get-tuple-element.86), channel_id=1, source_target_pairs={{0,1},{1,0},{2,3},{3,2},{4,5},{5,4},{6,7},{7,6},{8,9},{9,8},{10,11... | collective-permute-start | bytes 786440 | tf_op jit(solution)/shard_map/ppermute | solution.py:478
  71.6 26.1 %collective-permute-start.25 = (bf16[128,2560]{1,0:T(8,128)(2,1)S(1)}, bf16[128,2560]{1,0:T(8,128)(2,1)S(1)}, u32[]{:S(2)}, u32[]{:S(2)}) collective-permute-start(bf16[128,2560]{1,0:T(8,128)(2,1)S(1)} %dynamic-slice_bitcast_fusion.refs_2_), channel_id=1, source_target_pairs={{0,8},{2,10},{4,12},{6,14},{8,0},{10,2},{12,4},{14,6},{16,24},{18,... | collective-permute-start | bytes 1966088 | tf_op jit(solution)/shard_map/ppermute | solution.py:481
  71.7 9.5 %collective-permute-start.18 = (bf16[256,512]{1,0:T(8,128)(2,1)}, bf16[256,512]{1,0:T(8,128)(2,1)S(1)}, u32[]{:S(2)}, u32[]{:S(2)}) collective-permute-start(bf16[256,512]{1,0:T(8,128)(2,1)} %copy-done.22), channel_id=1, source_target_pairs={{0,2},{2,0},{4,6},{6,4},{8,10},{10,8},{12,14},{14,12},{16,18},{18,... | collective-permute-start | bytes 786440 | tf_op jit(solution)/shard_map/ppermute | solution.py:481
  73.3 13.6 %collective-permute-start.19 = (bf16[256,512]{1,0:T(8,128)(2,1)}, bf16[256,512]{1,0:T(8,128)(2,1)S(1)}, u32[]{:S(2)}, u32[]{:S(2)}) collective-permute-start(bf16[256,512]{1,0:T(8,128)(2,1)} %copy-done.21), channel_id=1, source_target_pairs={{0,4},{2,6},{4,0},{6,2},{8,12},{10,14},{12,8},{14,10},{16,20},{18,... | collective-permute-start | bytes 786440 | tf_op jit(solution)/shard_map/ppermute | solution.py:481
  74.7 12.1 %collective-permute-start.20 = (bf16[256,512]{1,0:T(8,128)(2,1)}, bf16[256,512]{1,0:T(8,128)(2,1)S(1)}, u32[]{:S(2)}, u32[]{:S(2)}) collective-permute-start(bf16[256,512]{1,0:T(8,128)(2,1)} %copy-done.20), channel_id=1, source_target_pairs={{0,6},{2,4},{4,2},{6,0},{8,14},{10,12},{12,10},{14,8},{16,22},{18,... | collective-permute-start | bytes 786440 | tf_op jit(solution)/shard_map/ppermute | solution.py:481
  87.9 4.5 %collective-permute-start.21 = (bf16[64,512]{1,0:T(8,128)(2,1)S(1)}, bf16[64,512]{1,0:T(8,128)(2,1)S(1)}, u32[]{:S(2)}, u32[]{:S(2)}) collective-permute-start(bf16[64,512]{1,0:T(8,128)(2,1)S(1)} %get-tuple-element.94), channel_id=1, source_target_pairs={{0,8},{2,10},{4,12},{6,14},{8,0},{10,2},{12,4},{14,6},{16,24},{18,... | collective-permute-start | bytes 196616 | tf_op jit(solution)/shard_map/ppermute | solution.py:481
  89.7 5.9 %collective-permute-start.22 = (bf16[64,512]{1,0:T(8,128)(2,1)S(1)}, bf16[64,512]{1,0:T(8,128)(2,1)S(1)}, u32[]{:S(2)}, u32[]{:S(2)}) collective-permute-start(bf16[64,512]{1,0:T(8,128)(2,1)S(1)} %get-tuple-element.95), channel_id=1, source_target_pairs={{0,16},{2,18},{4,20},{6,22},{8,24},{10,26},{12,28},{14,30},{16,0},... | collective-permute-start | bytes 196616 | tf_op jit(solution)/shard_map/ppermute | solution.py:481
  90.1 6.2 %collective-permute-start.23 = (bf16[64,512]{1,0:T(8,128)(2,1)S(1)}, bf16[64,512]{1,0:T(8,128)(2,1)S(1)}, u32[]{:S(2)}, u32[]{:S(2)}) collective-permute-start(bf16[64,512]{1,0:T(8,128)(2,1)S(1)} %get-tuple-element.96), channel_id=1, source_target_pairs={{0,24},{2,26},{4,28},{6,30},{8,16},{10,18},{12,20},{14,22},{16,8},... | collective-permute-start | bytes 196616 | tf_op jit(solution)/shard_map/ppermute | solution.py:481
  98.3 7.6 %collective-permute-start.26 = (bf16[32,2944]{1,0:T(8,128)(2,1)S(1)}, bf16[32,2944]{1,0:T(8,128)(2,1)S(1)}, u32[]{:S(2)}, u32[]{:S(2)}) collective-permute-start(bf16[32,2944]{1,0:T(8,128)(2,1)S(1)} %get-tuple-element.102), channel_id=1, source_target_pairs={{0,2},{2,0},{4,6},{6,4},{8,10},{10,8},{12,14},{14,12},{16,18},{18,... | collective-permute-start | bytes 565256 | tf_op jit(solution)/shard_map/ppermute | solution.py:481
  99.7 10.5 %collective-permute-start.27 = (bf16[32,2944]{1,0:T(8,128)(2,1)S(1)}, bf16[32,2944]{1,0:T(8,128)(2,1)S(1)}, u32[]{:S(2)}, u32[]{:S(2)}) collective-permute-start(bf16[32,2944]{1,0:T(8,128)(2,1)S(1)} %get-tuple-element.103), channel_id=1, source_target_pairs={{0,4},{2,6},{4,0},{6,2},{8,12},{10,14},{12,8},{14,10},{16,20},{18,... | collective-permute-start | bytes 565256 | tf_op jit(solution)/shard_map/ppermute | solution.py:481
  100.4 9.9 %collective-permute-start.28 = (bf16[32,2944]{1,0:T(8,128)(2,1)S(1)}, bf16[32,2944]{1,0:T(8,128)(2,1)S(1)}, u32[]{:S(2)}, u32[]{:S(2)}) collective-permute-start(bf16[32,2944]{1,0:T(8,128)(2,1)S(1)} %get-tuple-element.104), channel_id=1, source_target_pairs={{0,6},{2,4},{4,2},{6,0},{8,14},{10,12},{12,10},{14,8},{16,22},{18,... | collective-permute-start | bytes 565256 | tf_op jit(solution)/shard_map/ppermute | solution.py:481
  (32 other events, 224.0 us)
Sparse Core Ops, SparseCore 0:
  31.8 38.6 all-gather.2

commit v17 on v13

--- a/solution.py
+++ b/solution.py
@@ -91,67 +91,49 @@
     )(in_hbm(attn_out), in_hbm(out_weight))
 
 
-def first_norm_kernel(depth, count, *refs):
-    mine, theirs = refs[:count], refs[count : 2 * count]
-    residual_ref, gain_ref, meta_ref, tokens_ref = refs[2 * count : 2 * count + 4]
-    slice_refs, first_ref = refs[2 * count + 4 : -1], refs[-1]
-    rows, width = residual_ref.shape
-    sub = width // (PLANE * depth)
-    start = 0
-    for mine_ref, theirs_ref in zip(mine, theirs):
-        cols = slice(start, start + mine_ref.shape[1])
-        start += mine_ref.shape[1]
-        first_ref[:, cols] = (
-            residual_ref[:, cols].astype(jnp.float32) + (mine_ref[...] + theirs_ref[...])
-        ).astype(jnp.bfloat16)
-    first = first_ref[...]
+def first_norm_kernel(mine_ref, theirs_ref, residual_ref, gain_ref, meta_ref, tokens_ref, first_ref):
+    width = residual_ref.shape[1]
+    first = (residual_ref[...].astype(jnp.float32) + (mine_ref[...] + theirs_ref[...])).astype(
+        jnp.bfloat16
+    )
+    first_ref[...] = first
     tokens_ref[:, :width] = normalize(first.astype(jnp.float32), gain_ref[...]).astype(jnp.bfloat16)
     tokens_ref[:, width:] = meta_ref[...]
-    plane = lax.axis_index("expert") % PLANE
-    for d in range(PLANE):
-        for z in range(depth):
-            slice_refs[d][z * rows : (z + 1) * rows, :] = first_ref[
-                :, lanes((z * PLANE + (plane ^ d)) * sub, sub)
-            ]
-
-
-def first_norm(mine, theirs, residual, gain, meta, depth):
+
+
+def first_norm(mine, theirs, residual, gain, meta):
     rows, width = residual.shape
-    piece = jax.ShapeDtypeStruct((depth * rows, width // (PLANE * depth)), jnp.bfloat16)
-    return pl.pallas_call(
-        functools.partial(first_norm_kernel, depth, len(mine)),
-        out_shape=(jax.ShapeDtypeStruct((rows, width + META), jnp.bfloat16),) + (piece,) * PLANE,
-        in_specs=[VMEM] * (2 * len(mine) + 3),
-        out_specs=(VMEM,) * (1 + PLANE),
-        scratch_shapes=[pltpu.VMEM((rows, width), jnp.bfloat16)],
+    return pl.pallas_call(
+        first_norm_kernel,
+        out_shape=(
+            pltpu.VMEM((rows, width + META), jnp.bfloat16),
+            pltpu.VMEM((rows, width), jnp.bfloat16),
+        ),
+        in_specs=[VMEM] * 5,
+        out_specs=(VMEM, VMEM),
         compiler_params=params(2),
         name="first_norm",
-    )(*mine, *theirs, residual, gain, meta)
+    )(mine, theirs, residual, gain, meta)
 
 
 def pack_kernel(depth, *refs):
-    line, pieces, out_refs = refs[:depth], refs[depth : depth + PLANE], refs[depth + PLANE :]
-    rows, extended = line[0].shape
-    sub = pieces[0].shape[1]
-    for d, ref in enumerate(out_refs):
-        for z in range(depth):
-            ref[z * rows : (z + 1) * rows, :extended] = line[z][...]
-        ref[:, extended : extended + sub] = pieces[d][...]
-        ref[:, extended + sub :] = pieces[PLANE - 1][...]
-
-
-def pack(line, pieces):
+    line, out_ref = refs[:depth], refs[depth]
+    rows = line[0].shape[0]
+    for z in range(depth):
+        out_ref[z * rows : (z + 1) * rows, :] = line[z][...]
+
+
+def pack(line):
     depth = len(line)
     rows, extended = line[0].shape
-    shape = pltpu.VMEM((depth * rows, extended + 2 * pieces[0].shape[1]), jnp.bfloat16)
     return pl.pallas_call(
         functools.partial(pack_kernel, depth),
-        out_shape=(shape,) * (PLANE - 1),
-        in_specs=[VMEM] * (depth + PLANE),
-        out_specs=(VMEM,) * (PLANE - 1),
+        out_shape=pltpu.VMEM((depth * rows, extended), jnp.bfloat16),
+        in_specs=[VMEM] * depth,
+        out_specs=VMEM,
         compiler_params=params(2),
         name="pack_tokens",
-    )(*line, *pieces)
+    )(*line)
 
 
 def load_kernel(count, *refs):
@@ -245,9 +227,12 @@
     )(*blocks, *weights)
 
 
-def chip_sum_kernel(count, *refs):
+def chip_sum_kernel(depth, count, first_ref, *refs):
     mine, theirs, out_refs = refs[:2], refs[2 : 2 + count], refs[2 + count :]
     part = out_refs[0].shape[1]
+    sub = part // depth
+    held = first_ref.shape[0]
+    plane = lax.axis_index("expert") % PLANE
     start = 0
     for own_ref in mine:
         first = start
@@ -258,20 +243,30 @@
             for d, out_ref in enumerate(out_refs):
                 at = slice(d * part, (d + 1) * part)
                 total = own_ref[own, at].astype(jnp.float32) + ref[:, at].astype(jnp.float32)
+                if start == 0:
+                    residual = jnp.concatenate(
+                        [
+                            first_ref[:, lanes((z * PLANE + (plane ^ d)) * sub, sub)]
+                            for z in range(depth)
+                        ],
+                        axis=1,
+                    )
+                    with_first = total[:held] + residual.astype(jnp.float32)
+                    total = jnp.concatenate([with_first, total[held:]], axis=0)
                 out_ref[start : start + size, :] = total.astype(jnp.bfloat16)
             start += size
 
 
-def chip_sum(mine, theirs):
+def chip_sum(mine, theirs, first, depth):
     rows, width = sum(value.shape[0] for value in mine), mine[0].shape[1]
     return pl.pallas_call(
-        functools.partial(chip_sum_kernel, len(theirs)),
+        functools.partial(chip_sum_kernel, depth, len(theirs)),
         out_shape=(pltpu.VMEM((rows, width // PLANE), jnp.bfloat16),) * PLANE,
-        in_specs=[VMEM] * (2 + len(theirs)),
+        in_specs=[VMEM] * (3 + len(theirs)),
         out_specs=(VMEM,) * PLANE,
         compiler_params=params(4),
         name="chip_sum",
-    )(*mine, *theirs)
+    )(first, *mine, *theirs)
 
 
 def plane_sum_kernel(depth, *refs):
@@ -300,53 +295,42 @@
 
 
 def second_norm_kernel(depth, *refs):
-    parts, packed = refs[:depth], refs[depth : depth + PLANE + 1]
-    gain_ref, scaled_ref, next_ref = refs[depth + PLANE + 1 :]
-    rows = packed[0].shape[0] // depth
-    part = parts[0].shape[1]
+    parts, (gain_ref, scaled_ref, next_ref) = refs[:depth], refs[depth:]
+    rows, part = next_ref.shape
     sub = part // depth
-    skip = packed[0].shape[1] - 2 * sub
-    lane = lax.broadcasted_iota(jnp.int32, (rows, META), 1)
     plane = lax.axis_index("expert") % PLANE
     gain = jnp.concatenate(
         [gain_ref[:, lanes((z * PLANE + plane) * sub, sub)] for z in range(depth)], axis=1
     )
-    for d in range(PLANE):
-        at = slice(d * rows, (d + 1) * rows)
-        total = parts[0][at, :].astype(jnp.float32)
-        for ref in parts[1:]:
-            total = total + ref[at, :].astype(jnp.float32)
-        if d < PLANE - 1:
-            first = packed[d][:, skip : skip + sub]
-        else:
-            first = jnp.concatenate([ref[:, skip + sub :] for ref in packed[d:]], axis=0)
-        first = jnp.concatenate([first[z * rows : (z + 1) * rows] for z in range(depth)], axis=1)
-        following = (first.astype(jnp.float32) + total).astype(jnp.bfloat16)
-        next_ref[at, :] = following
-        wide = following.astype(jnp.float32)
-        scaled_ref[at, :part] = (wide * gain).astype(jnp.bfloat16)
-        squares = jnp.sum(wide * wide, axis=1, keepdims=True)
-        high = squares.astype(jnp.bfloat16).astype(jnp.float32)
-        low = squares - high
-        scaled_ref[at, part:] = jnp.where(
-            lane == 0, high, jnp.where(lane == 1, low, 0.0)
-        ).astype(jnp.bfloat16)
-
-
-def second_norm(parts, packed, gain):
+    total = parts[0][...].astype(jnp.float32)
+    for ref in parts[1:]:
+        total = total + ref[...].astype(jnp.float32)
+    following = total.astype(jnp.bfloat16)
+    next_ref[...] = following
+    wide = following.astype(jnp.float32)
+    scaled_ref[:, :part] = (wide * gain).astype(jnp.bfloat16)
+    squares = jnp.sum(wide * wide, axis=1, keepdims=True)
+    high = squares.astype(jnp.bfloat16).astype(jnp.float32)
+    lane = lax.broadcasted_iota(jnp.int32, (rows, META), 1)
+    scaled_ref[:, part:] = jnp.where(
+        lane == 0, high, jnp.where(lane == 1, squares - high, 0.0)
+    ).astype(jnp.bfloat16)
+
+
+def second_norm(parts, gain):
     depth = len(parts)
     rows, part = parts[0].shape
     return pl.pallas_call(
         functools.partial(second_norm_kernel, depth),
         out_shape=(
-            jax.ShapeDtypeStruct((rows, part + META), jnp.bfloat16),
-            jax.ShapeDtypeStruct((rows, part), jnp.bfloat16),
+            pltpu.VMEM((rows, part + META), jnp.bfloat16),
+            pltpu.VMEM((rows, part), jnp.bfloat16),
         ),
-        in_specs=[VMEM] * (depth + PLANE + 2),
+        in_specs=[VMEM] * (depth + 1),
         out_specs=(VMEM, VMEM),
         compiler_params=params(4),
         name="second_norm",
-    )(*parts, *packed, gain)
+    )(*parts, gain)
 
 
 def projection_kernel(chunk, mine_ref, theirs_ref, next_ref, q_ref, *refs):
@@ -498,16 +482,14 @@
 
     lines = [list(range(i, n_expert, PLANE)) for i in range(PLANE)]
     mine, theirs = out_projection(attn_out, out_weight)
-    tokens, *firsts = first_norm(
-        (mine,), (to_core(theirs),), residual, attn_gain[None, :], meta, depth
-    )
+    tokens, first = first_norm(mine, to_core(theirs), residual, attn_gain[None, :], meta)
     tokens, q_own = lax.optimization_barrier((tokens, q_weight))
     q_rows = lax.all_gather(q_own, "expert", axis=0, tiled=True, axis_index_groups=lines)
     weights = load((w_gate, w_up, w_down), (tokens,))
     line = to_z([tokens] * depth)
     *line, gate, up, down = lax.optimization_barrier((*line, *weights))
     weights = (gate, up, down)
-    near = to_plane(pack(line, firsts))
+    near = to_plane([pack(line)] * (PLANE - 1))
     cut = near[0].shape[0] // 2
     one, two = near[1][:cut], near[2][cut:]
     far = [to_expert(one, 2), to_expert(two, 1)]
@@ -517,7 +499,7 @@
     far_both = [*far, *map(to_core, far)]
     far_mine, *far_theirs = experts(far_both, weights, depth, 1)
     theirs += map(to_core, far_theirs)
-    *sums, kv_own = lax.optimization_barrier((*chip_sum((near_mine, far_mine), theirs), kv_weight))
+    *sums, kv_own = lax.optimization_barrier((*chip_sum((near_mine, far_mine), theirs, first, depth), kv_weight))
     parts = to_plane(sums)
     kv_rows = [kv_own, to_expert(kv_own, PLANE), to_expert(kv_own, 2 * PLANE)]
     *parts, kv_rows[1], kv_rows[2] = lax.optimization_barrier(
@@ -527,7 +509,7 @@
     (q_rows,) = load((q_rows,), parts)
     parts = to_z(parts)
     *parts, q_rows = lax.optimization_barrier((*parts, q_rows))
-    scaled, following = second_norm(parts, (*near, *far), input_gain[None, :])
+    scaled, following = second_norm(parts, input_gain[None, :])
     products = to_plane(projection(scaled, to_core(scaled), following, q_rows, kv_rows))
     return head_norm(
         products,

time: 97.7 us -> 97.1 us (level)
  transfers between devices with their start and end apart: 31 -> 31, of which waited for: 20 -> 19; matrix products, arithmetic and copies ran while one was open for 1% -> 1% of each run, Pallas kernels for 12% -> 12%
where the time goes in v17:
time: 97.1 us; the launch traced here: 96.9 us
  waiting for transfers between devices  36.2 us (37%)
  starting transfers between devices  27.6 us (28%)
  Pallas kernels  18.4 us (19%)
  between operations  14.2 us (15%)
    ppermute x19, waiting for transfers between devices, to_expert(): lax.ppermute(value, 'expert', [(i, i ^ offset) for i in range(n_expert)])  33.8 us
    ppermute x19, starting transfers between devices, to_expert(): lax.ppermute(value, 'expert', [(i, i ^ offset) for i in range(n_expert)])  25.6 us
    pallas_call x2, Pallas kernels, experts(): pl.pallas_call(functools.partial(expert_kernel, depth, chunk, len(blocks)...  6.05 us
    pallas_call x2, Pallas kernels, load(): pl.pallas_call(functools.partial(load_kernel, count), out_shape=tuple((pl...  5.42 us
    pallas_call x1, Pallas kernels, out_projection(): pl.pallas_call(functools.partial(out_projection_kernel, chunk), out_shape...  4.77 us
    ppermute x11, waiting for transfers between devices, to_core(): return lax.ppermute(value, 'tensor', [(0, 1), (1, 0)])  2.33 us
    ppermute x11, starting transfers between devices, to_core(): return lax.ppermute(value, 'tensor', [(0, 1), (1, 0)])  2 us
  transfers between devices with their start and end apart: 31, of which 19 were waited for; matrix products, arithmetic and copies ran while one was open for 1% of the time, Pallas kernels for 12%

profile of v17, /device:TPU:0, one launch (start us, length us, event | category | flops | bytes accessed | tf_op | source)
XLA Modules:
  0.0 96.9 jit_solution(4129399213302931858)
XLA Ops:
  7.3 4.8 %out_projection.1 = (f32[16,2048]{1,0:T(8,128)S(1)}, f32[16,2048]{1,0:T(8,128)S(1)}) custom-call(bf16[32,2048]{1,0:T(8,128)(2,1)} %a_hbm.1, bf16[2048,2048]{1,0:T(8,128)(2,1)} %w_hbm.1), custom_call_target="tpu_custom_call" | custom-call | tf_op jit(solution)/shard_map/out_projection/pallas_call | solution.py:77
  13.7 3.0 %collective-permute-start.1 = (bf16[16,2176]{1,0:T(8,128)(2,1)S(1)}, bf16[16,2176]{1,0:T(8,128)(2,1)S(1)}, u32[]{:S(2)}, u32[]{:S(2)}) collective-permute-start(bf16[16,2176]{1,0:T(8,128)(2,1)S(1)} %get-tuple-element.66.refs_3_.refs_0_), channel_id=1, source_target_pairs={{0,8},{2,10},{4,12},{6,14},{8,0},{10,2},{12,4},{14,6},{16,24},{18,... | collective-permute-start | bytes 208904 | tf_op jit(solution)/shard_map/ppermute | solution.py:468
  16.7 2.6 %collective-permute-start.2 = (bf16[16,2176]{1,0:T(8,128)(2,1)S(1)}, bf16[16,2176]{1,0:T(8,128)(2,1)S(1)}, u32[]{:S(2)}, u32[]{:S(2)}) collective-permute-start(bf16[16,2176]{1,0:T(8,128)(2,1)S(1)} %get-tuple-element.66.refs_3_.refs_0_), channel_id=1, source_target_pairs={{0,16},{2,18},{4,20},{6,22},{8,24},{10,26},{12,28},{14,30},{16,0},... | collective-permute-start | bytes 208904 | tf_op jit(solution)/shard_map/ppermute | solution.py:468
  19.3 3.8 %load_weights.2 = (bf16[1,2048,768]{2,1,0:T(8,128)(2,1)S(1)}, bf16[1,2048,768]{2,1,0:T(8,128)(2,1)S(1)}, bf16[1,768,2048]{2,1,0:T(8,128)(2,1)S(1)}) custom-call(bf16[1,2048,768]{2,1,0:T(8,128)(2,1)} %refs_0_.1, bf16[1,2048,768]{2,1,0:T(8,128)(2,1)} %refs_1_.1, bf16[1,768,2048]{2,1,0:T(8,128)(2,1)} %refs_2_.1, ...), custom_call_target="tpu_custom_call" | custom-call | tf_op jit(solution)/shard_map/load_weights/pallas_call | solution.py:153
  23.1 1.4 %collective-permute-done.2.refs_2_ = bf16[16,2176]{1,0:T(8,128)(2,1)S(1)} collective-permute-done((bf16[16,2176]{1,0:T(8,128)(2,1)S(1)}, bf16[16,2176]{1,0:T(8,128)(2,1)S(1)}, u32[]{:S(2)}, u32[]{:S(2)}) %collective-permute-start.2) | collective-permute-done | bytes 69664 | tf_op jit(solution)/shard_map/ppermute | solution.py:468
  25.5 1.6 %collective-permute-start.4 = (bf16[64,2176]{1,0:T(8,128)(2,1)S(1)}, bf16[64,2176]{1,0:T(8,128)(2,1)S(1)}, u32[]{:S(2)}, u32[]{:S(2)}) collective-permute-start(bf16[64,2176]{1,0:T(8,128)(2,1)S(1)} %pack_tokens.1.refs_0_), channel_id=1, source_target_pairs={{0,2},{2,0},{4,6},{6,4},{8,10},{10,8},{12,14},{14,12},{16,18},{18,... | collective-permute-start | bytes 835592 | tf_op jit(solution)/shard_map/ppermute | solution.py:468
  27.1 1.5 %collective-permute-start.5 = (bf16[64,2176]{1,0:T(8,128)(2,1)S(1)}, bf16[64,2176]{1,0:T(8,128)(2,1)S(1)}, u32[]{:S(2)}, u32[]{:S(2)}) collective-permute-start(bf16[64,2176]{1,0:T(8,128)(2,1)S(1)} %pack_tokens.1.refs_0_), channel_id=1, source_target_pairs={{0,4},{2,6},{4,0},{6,2},{8,12},{10,14},{12,8},{14,10},{16,20},{18,... | collective-permute-start | bytes 835592 | tf_op jit(solution)/shard_map/ppermute | solution.py:468
  28.6 3.9 %collective-permute-done.4.refs_1_ = bf16[64,2176]{1,0:T(8,128)(2,1)S(1)} collective-permute-done((bf16[64,2176]{1,0:T(8,128)(2,1)S(1)}, bf16[64,2176]{1,0:T(8,128)(2,1)S(1)}, u32[]{:S(2)}, u32[]{:S(2)}) %collective-permute-start.4) | collective-permute-done | bytes 278560 | tf_op jit(solution)/shard_map/ppermute | solution.py:468
  33.7 1.6 %collective-permute-start.9 = (bf16[32,2176]{1,0:T(8,128)(2,1)S(1)}, bf16[32,2176]{1,0:T(8,128)(2,1)S(1)}, u32[]{:S(2)}, u32[]{:S(2)}) collective-permute-start(bf16[32,2176]{1,0:T(8,128)(2,1)S(1)} %slice.8), channel_id=1, source_target_pairs={{0,4},{2,6},{4,0},{6,2},{8,12},{10,14},{12,8},{14,10},{16,20},{18,... | collective-permute-start | bytes 417800 | tf_op jit(solution)/shard_map/ppermute | solution.py:468
  36.2 4.1 %experts.2 = (bf16[192,2048]{1,0:T(8,128)(2,1)S(1)}, bf16[64,2048]{1,0:T(8,128)(2,1)S(1)}, bf16[64,2048]{1,0:T(8,128)(2,1)S(1)}, bf16[64,2048]{1,0:T(8,128)(2,1)S(1)}) custom-call(bf16[64,2176]{1,0:T(8,128)(2,1)S(1)} %pack_tokens.1.refs_0_, bf16[64,2176]{1,0:T(8,128)(2,1)S(1)} %collective-permute-done.4.refs_1_, ...), custom_call_target="tpu_custom_call" | custom-call | flops 3623878656 | tf_op jit(solution)/shard_map/experts/pallas_call | solution.py:213
  42.8 2.0 %experts.3 = (bf16[64,2048]{1,0:T(8,128)(2,1)S(1)}, bf16[64,2048]{1,0:T(8,128)(2,1)S(1)}) custom-call(bf16[32,2176]{1,0:T(8,128)(2,1)S(1)} %collective-permute-done.9.refs_0_, bf16[32,2176]{1,0:T(8,128)(2,1)S(1)} %collective-permute-done.10.refs_1_, bf16[32,2176]{1,0:T(8,128)(2,1)S(1)} %collective-permute-done.11.refs_2_, ...), custom_call_target="tpu_custom_call" | custom-call | flops 1207959552 | tf_op jit(solution)/shard_map/experts/pallas_call | solution.py:213
  47.7 2.4 %collective-permute-start.19 = (bf16[256,512]{1,0:T(8,128)(2,1)S(1)}, bf16[256,512]{1,0:T(8,128)(2,1)S(1)}, u32[]{:S(2)}, u32[]{:S(2)}) collective-permute-start(bf16[256,512]{1,0:T(8,128)(2,1)S(1)} %get-tuple-element.89), channel_id=1, source_target_pairs={{0,6},{2,4},{4,2},{6,0},{8,14},{10,12},{12,10},{14,8},{16,22},{18,... | collective-permute-start | bytes 786440 | tf_op jit(solution)/shard_map/ppermute | solution.py:468
  50.2 1.6 %collective-permute-start.20 = (bf16[128,512]{1,0:T(8,128)(2,1)S(1)}, bf16[128,512]{1,0:T(8,128)(2,1)S(1)}, u32[]{:S(2)}, u32[]{:S(2)}) collective-permute-start(bf16[128,512]{1,0:T(8,128)(2,1)S(1)} %copy-done.1), channel_id=1, source_target_pairs={{0,8},{2,10},{4,12},{6,14},{8,0},{10,2},{12,4},{14,6},{16,24},{18,... | collective-permute-start | bytes 393224 | tf_op jit(solution)/shard_map/ppermute | solution.py:468
  51.7 1.4 %collective-permute-start.21 = (bf16[128,512]{1,0:T(8,128)(2,1)S(1)}, bf16[128,512]{1,0:T(8,128)(2,1)S(1)}, u32[]{:S(2)}, u32[]{:S(2)}) collective-permute-start(bf16[128,512]{1,0:T(8,128)(2,1)S(1)} %copy-done.1), channel_id=1, source_target_pairs={{0,16},{2,18},{4,20},{6,22},{8,24},{10,26},{12,28},{14,30},{16,0},... | collective-permute-start | bytes 393224 | tf_op jit(solution)/shard_map/ppermute | solution.py:468
  53.2 2.7 %collective-permute-done.17.refs_1_ = bf16[256,512]{1,0:T(8,128)(2,1)S(1)} collective-permute-done((bf16[256,512]{1,0:T(8,128)(2,1)S(1)}, bf16[256,512]{1,0:T(8,128)(2,1)S(1)}, u32[]{:S(2)}, u32[]{:S(2)}) %collective-permute-start.17) | collective-permute-done | bytes 262176 | tf_op jit(solution)/shard_map/ppermute | solution.py:468
  55.8 5.3 %collective-permute-done.18.refs_2_ = bf16[256,512]{1,0:T(8,128)(2,1)S(1)} collective-permute-done((bf16[256,512]{1,0:T(8,128)(2,1)S(1)}, bf16[256,512]{1,0:T(8,128)(2,1)S(1)}, u32[]{:S(2)}, u32[]{:S(2)}) %collective-permute-start.18) | collective-permute-done | bytes 262176 | tf_op jit(solution)/shard_map/ppermute | solution.py:468
  61.2 3.9 %collective-permute-done.20.refs_1_ = bf16[128,512]{1,0:T(8,128)(2,1)S(1)} collective-permute-done((bf16[128,512]{1,0:T(8,128)(2,1)S(1)}, bf16[128,512]{1,0:T(8,128)(2,1)S(1)}, u32[]{:S(2)}, u32[]{:S(2)}) %collective-permute-start.20) | collective-permute-done | bytes 131104 | tf_op jit(solution)/shard_map/ppermute | solution.py:468
  65.1 2.2 %collective-permute-done.21.refs_2_ = bf16[128,512]{1,0:T(8,128)(2,1)S(1)} collective-permute-done((bf16[128,512]{1,0:T(8,128)(2,1)S(1)}, bf16[128,512]{1,0:T(8,128)(2,1)S(1)}, u32[]{:S(2)}, u32[]{:S(2)}) %collective-permute-start.21) | collective-permute-done | bytes 131104 | tf_op jit(solution)/shard_map/ppermute | solution.py:468
  67.3 2.0 %collective-permute-start.23 = (bf16[64,512]{1,0:T(8,128)(2,1)S(1)}, bf16[64,512]{1,0:T(8,128)(2,1)S(1)}, u32[]{:S(2)}, u32[]{:S(2)}) collective-permute-start(bf16[64,512]{1,0:T(8,128)(2,1)S(1)} %get-tuple-element.97.refs_3_), channel_id=1, source_target_pairs={{0,16},{2,18},{4,20},{6,22},{8,24},{10,26},{12,28},{14,30},{16,0},... | collective-permute-start | bytes 196616 | tf_op jit(solution)/shard_map/ppermute | solution.py:468
  69.3 2.4 %collective-permute-start.24 = (bf16[64,512]{1,0:T(8,128)(2,1)S(1)}, bf16[64,512]{1,0:T(8,128)(2,1)S(1)}, u32[]{:S(2)}, u32[]{:S(2)}) collective-permute-start(bf16[64,512]{1,0:T(8,128)(2,1)S(1)} %get-tuple-element.98.refs_4_), channel_id=1, source_target_pairs={{0,24},{2,26},{4,28},{6,30},{8,16},{10,18},{12,20},{14,22},{16,8},... | collective-permute-start | bytes 196616 | tf_op jit(solution)/shard_map/ppermute | solution.py:468
  71.7 1.6 %load_weights.3.q_ref = bf16[512,2048]{1,0:T(8,128)(2,1)S(1)} custom-call(bf16[512,2048]{1,0:T(8,128)(2,1)} %all-gather.2.cloned.1.call-done.refs_0_, bf16[64,512]{1,0:T(8,128)(2,1)S(1)} %get-tuple-element.100.refs_1_.refs_0_, bf16[64,512]{1,0:T(8,128)(2,1)S(1)} %get-tuple-element.96.refs_2_, bf16[64,512]{1,0:T(8,128)(2,1)S(1)} %get-tuple-element.97.refs_3_, ...), custom_call_target="tpu_custom_call" | custom-call | tf_op jit(solution)/shard_map/load_weights/pallas_call | solution.py:153
  73.5 1.9 %collective-permute-done.24.refs_3_ = bf16[64,512]{1,0:T(8,128)(2,1)S(1)} collective-permute-done((bf16[64,512]{1,0:T(8,128)(2,1)S(1)}, bf16[64,512]{1,0:T(8,128)(2,1)S(1)}, u32[]{:S(2)}, u32[]{:S(2)}) %collective-permute-start.24) | collective-permute-done | bytes 65568 | tf_op jit(solution)/shard_map/ppermute | solution.py:468
  81.0 4.1 %collective-permute-done.27.refs_1_ = bf16[32,2944]{1,0:T(8,128)(2,1)S(1)} collective-permute-done((bf16[32,2944]{1,0:T(8,128)(2,1)S(1)}, bf16[32,2944]{1,0:T(8,128)(2,1)S(1)}, u32[]{:S(2)}, u32[]{:S(2)}) %collective-permute-start.27) | collective-permute-done | bytes 188448 | tf_op jit(solution)/shard_map/ppermute | solution.py:468
  85.1 4.1 %collective-permute-done.28.refs_2_ = bf16[32,2944]{1,0:T(8,128)(2,1)S(1)} collective-permute-done((bf16[32,2944]{1,0:T(8,128)(2,1)S(1)}, bf16[32,2944]{1,0:T(8,128)(2,1)S(1)}, u32[]{:S(2)}, u32[]{:S(2)}) %collective-permute-start.28) | collective-permute-done | bytes 188448 | tf_op jit(solution)/shard_map/ppermute | solution.py:468
  (76 shorter events, 17.1 us)
Async XLA Ops:
  7.2 64.4 %all-gather.2.cloned.1.call-start = ((), (), s32[]{:S(2)}) async-start(), calls=%async_computation | async-start | bytes 2621440 | tf_op jit(solution)/shard_map/all_gather | solution.py:487
  13.7 9.4 %collective-permute-start.1 = (bf16[16,2176]{1,0:T(8,128)(2,1)S(1)}, bf16[16,2176]{1,0:T(8,128)(2,1)S(1)}, u32[]{:S(2)}, u32[]{:S(2)}) collective-permute-start(bf16[16,2176]{1,0:T(8,128)(2,1)S(1)} %get-tuple-element.66.refs_3_.refs_0_), channel_id=1, source_target_pairs={{0,8},{2,10},{4,12},{6,14},{8,0},{10,2},{12,4},{14,6},{16,24},{18,... | collective-permute-start | bytes 208904 | tf_op jit(solution)/shard_map/ppermute | solution.py:468
  16.7 7.8 %collective-permute-start.2 = (bf16[16,2176]{1,0:T(8,128)(2,1)S(1)}, bf16[16,2176]{1,0:T(8,128)(2,1)S(1)}, u32[]{:S(2)}, u32[]{:S(2)}) collective-permute-start(bf16[16,2176]{1,0:T(8,128)(2,1)S(1)} %get-tuple-element.66.refs_3_.refs_0_), channel_id=1, source_target_pairs={{0,16},{2,18},{4,20},{6,22},{8,24},{10,26},{12,28},{14,30},{16,0},... | collective-permute-start | bytes 208904 | tf_op jit(solution)/shard_map/ppermute | solution.py:468
  19.3 6.2 %collective-permute-start.3 = (bf16[16,2176]{1,0:T(8,128)(2,1)S(1)}, bf16[16,2176]{1,0:T(8,128)(2,1)S(1)}, u32[]{:S(2)}, u32[]{:S(2)}) collective-permute-start(bf16[16,2176]{1,0:T(8,128)(2,1)S(1)} %get-tuple-element.66.refs_3_.refs_0_), channel_id=1, source_target_pairs={{0,24},{2,26},{4,28},{6,30},{8,16},{10,18},{12,20},{14,22},{16,8},... | collective-permute-start | bytes 208904 | tf_op jit(solution)/shard_map/ppermute | solution.py:468
  25.5 7.0 %collective-permute-start.4 = (bf16[64,2176]{1,0:T(8,128)(2,1)S(1)}, bf16[64,2176]{1,0:T(8,128)(2,1)S(1)}, u32[]{:S(2)}, u32[]{:S(2)}) collective-permute-start(bf16[64,2176]{1,0:T(8,128)(2,1)S(1)} %pack_tokens.1.refs_0_), channel_id=1, source_target_pairs={{0,2},{2,0},{4,6},{6,4},{8,10},{10,8},{12,14},{14,12},{16,18},{18,... | collective-permute-start | bytes 835592 | tf_op jit(solution)/shard_map/ppermute | solution.py:468
  27.1 6.6 %collective-permute-start.5 = (bf16[64,2176]{1,0:T(8,128)(2,1)S(1)}, bf16[64,2176]{1,0:T(8,128)(2,1)S(1)}, u32[]{:S(2)}, u32[]{:S(2)}) collective-permute-start(bf16[64,2176]{1,0:T(8,128)(2,1)S(1)} %pack_tokens.1.refs_0_), channel_id=1, source_target_pairs={{0,4},{2,6},{4,0},{6,2},{8,12},{10,14},{12,8},{14,10},{16,20},{18,... | collective-permute-start | bytes 835592 | tf_op jit(solution)/shard_map/ppermute | solution.py:468
  28.6 7.6 %collective-permute-start.6 = (bf16[64,2176]{1,0:T(8,128)(2,1)S(1)}, bf16[64,2176]{1,0:T(8,128)(2,1)S(1)}, u32[]{:S(2)}, u32[]{:S(2)}) collective-permute-start(bf16[64,2176]{1,0:T(8,128)(2,1)S(1)} %pack_tokens.1.refs_0_), channel_id=1, source_target_pairs={{0,1},{1,0},{2,3},{3,2},{4,5},{5,4},{6,7},{7,6},{8,9},{9,8},{10,11... | collective-permute-start | bytes 835592 | tf_op jit(solution)/shard_map/ppermute | solution.py:465
  32.5 3.7 %collective-permute-start.7 = (bf16[64,2176]{1,0:T(8,128)(2,1)S(1)}, bf16[64,2176]{1,0:T(8,128)(2,1)S(1)}, u32[]{:S(2)}, u32[]{:S(2)}) collective-permute-start(bf16[64,2176]{1,0:T(8,128)(2,1)S(1)} %collective-permute-done.4.refs_1_), channel_id=1, source_target_pairs={{0,1},{1,0},{2,3},{3,2},{4,5},{5,4},{6,7},{7,6},{8,9},{9,8},{10,11... | collective-permute-start | bytes 835592 | tf_op jit(solution)/shard_map/ppermute | solution.py:465
  33.7 6.5 %collective-permute-start.9 = (bf16[32,2176]{1,0:T(8,128)(2,1)S(1)}, bf16[32,2176]{1,0:T(8,128)(2,1)S(1)}, u32[]{:S(2)}, u32[]{:S(2)}) collective-permute-start(bf16[32,2176]{1,0:T(8,128)(2,1)S(1)} %slice.8), channel_id=1, source_target_pairs={{0,4},{2,6},{4,0},{6,2},{8,12},{10,14},{12,8},{14,10},{16,20},{18,... | collective-permute-start | bytes 417800 | tf_op jit(solution)/shard_map/ppermute | solution.py:468
  35.3 5.9 %collective-permute-start.10 = (bf16[32,2176]{1,0:T(8,128)(2,1)S(1)}, bf16[32,2176]{1,0:T(8,128)(2,1)S(1)}, u32[]{:S(2)}, u32[]{:S(2)}) collective-permute-start(bf16[32,2176]{1,0:T(8,128)(2,1)S(1)} %slice.9), channel_id=1, source_target_pairs={{0,2},{2,0},{4,6},{6,4},{8,10},{10,8},{12,14},{14,12},{16,18},{18,... | collective-permute-start | bytes 417800 | tf_op jit(solution)/shard_map/ppermute | solution.py:468
  41.7 3.4 %collective-permute-start.13 = (bf16[64,2048]{1,0:T(8,128)(2,1)S(1)}, bf16[64,2048]{1,0:T(8,128)(2,1)S(1)}, u32[]{:S(2)}, u32[]{:S(2)}) collective-permute-start(bf16[64,2048]{1,0:T(8,128)(2,1)S(1)} %get-tuple-element.78), channel_id=1, source_target_pairs={{0,1},{1,0},{2,3},{3,2},{4,5},{5,4},{6,7},{7,6},{8,9},{9,8},{10,11... | collective-permute-start | bytes 786440 | tf_op jit(solution)/shard_map/ppermute | solution.py:465
  41.7 3.4 %collective-permute-start.14 = (bf16[64,2048]{1,0:T(8,128)(2,1)S(1)}, bf16[64,2048]{1,0:T(8,128)(2,1)S(1)}, u32[]{:S(2)}, u32[]{:S(2)}) collective-permute-start(bf16[64,2048]{1,0:T(8,128)(2,1)S(1)} %get-tuple-element.79), channel_id=1, source_target_pairs={{0,1},{1,0},{2,3},{3,2},{4,5},{5,4},{6,7},{7,6},{8,9},{9,8},{10,11... | collective-permute-start | bytes 786440 | tf_op jit(solution)/shard_map/ppermute | solution.py:465
  46.6 9.2 %collective-permute-start.17 = (bf16[256,512]{1,0:T(8,128)(2,1)S(1)}, bf16[256,512]{1,0:T(8,128)(2,1)S(1)}, u32[]{:S(2)}, u32[]{:S(2)}) collective-permute-start(bf16[256,512]{1,0:T(8,128)(2,1)S(1)} %get-tuple-element.87), channel_id=1, source_target_pairs={{0,2},{2,0},{4,6},{6,4},{8,10},{10,8},{12,14},{14,12},{16,18},{18,... | collective-permute-start | bytes 786440 | tf_op jit(solution)/shard_map/ppermute | solution.py:468
  47.2 13.9 %collective-permute-start.18 = (bf16[256,512]{1,0:T(8,128)(2,1)S(1)}, bf16[256,512]{1,0:T(8,128)(2,1)S(1)}, u32[]{:S(2)}, u32[]{:S(2)}) collective-permute-start(bf16[256,512]{1,0:T(8,128)(2,1)S(1)} %get-tuple-element.88), channel_id=1, source_target_pairs={{0,4},{2,6},{4,0},{6,2},{8,12},{10,14},{12,8},{14,10},{16,20},{18,... | collective-permute-start | bytes 786440 | tf_op jit(solution)/shard_map/ppermute | solution.py:468
  47.7 13.3 %collective-permute-start.19 = (bf16[256,512]{1,0:T(8,128)(2,1)S(1)}, bf16[256,512]{1,0:T(8,128)(2,1)S(1)}, u32[]{:S(2)}, u32[]{:S(2)}) collective-permute-start(bf16[256,512]{1,0:T(8,128)(2,1)S(1)} %get-tuple-element.89), channel_id=1, source_target_pairs={{0,6},{2,4},{4,2},{6,0},{8,14},{10,12},{12,10},{14,8},{16,22},{18,... | collective-permute-start | bytes 786440 | tf_op jit(solution)/shard_map/ppermute | solution.py:468
  50.2 14.9 %collective-permute-start.20 = (bf16[128,512]{1,0:T(8,128)(2,1)S(1)}, bf16[128,512]{1,0:T(8,128)(2,1)S(1)}, u32[]{:S(2)}, u32[]{:S(2)}) collective-permute-start(bf16[128,512]{1,0:T(8,128)(2,1)S(1)} %copy-done.1), channel_id=1, source_target_pairs={{0,8},{2,10},{4,12},{6,14},{8,0},{10,2},{12,4},{14,6},{16,24},{18,... | collective-permute-start | bytes 393224 | tf_op jit(solution)/shard_map/ppermute | solution.py:468
  51.7 15.5 %collective-permute-start.21 = (bf16[128,512]{1,0:T(8,128)(2,1)S(1)}, bf16[128,512]{1,0:T(8,128)(2,1)S(1)}, u32[]{:S(2)}, u32[]{:S(2)}) collective-permute-start(bf16[128,512]{1,0:T(8,128)(2,1)S(1)} %copy-done.1), channel_id=1, source_target_pairs={{0,16},{2,18},{4,20},{6,22},{8,24},{10,26},{12,28},{14,30},{16,0},... | collective-permute-start | bytes 393224 | tf_op jit(solution)/shard_map/ppermute | solution.py:468
  67.3 6.2 %collective-permute-start.22 = (bf16[64,512]{1,0:T(8,128)(2,1)S(1)}, bf16[64,512]{1,0:T(8,128)(2,1)S(1)}, u32[]{:S(2)}, u32[]{:S(2)}) collective-permute-start(bf16[64,512]{1,0:T(8,128)(2,1)S(1)} %get-tuple-element.96.refs_2_), channel_id=1, source_target_pairs={{0,8},{2,10},{4,12},{6,14},{8,0},{10,2},{12,4},{14,6},{16,24},{18,... | collective-permute-start | bytes 196616 | tf_op jit(solution)/shard_map/ppermute | solution.py:468
  67.3 6.2 %collective-permute-start.23 = (bf16[64,512]{1,0:T(8,128)(2,1)S(1)}, bf16[64,512]{1,0:T(8,128)(2,1)S(1)}, u32[]{:S(2)}, u32[]{:S(2)}) collective-permute-start(bf16[64,512]{1,0:T(8,128)(2,1)S(1)} %get-tuple-element.97.refs_3_), channel_id=1, source_target_pairs={{0,16},{2,18},{4,20},{6,22},{8,24},{10,26},{12,28},{14,30},{16,0},... | collective-permute-start | bytes 196616 | tf_op jit(solution)/shard_map/ppermute | solution.py:468
  69.3 6.1 %collective-permute-start.24 = (bf16[64,512]{1,0:T(8,128)(2,1)S(1)}, bf16[64,512]{1,0:T(8,128)(2,1)S(1)}, u32[]{:S(2)}, u32[]{:S(2)}) collective-permute-start(bf16[64,512]{1,0:T(8,128)(2,1)S(1)} %get-tuple-element.98.refs_4_), channel_id=1, source_target_pairs={{0,24},{2,26},{4,28},{6,30},{8,16},{10,18},{12,20},{14,22},{16,8},... | collective-permute-start | bytes 196616 | tf_op jit(solution)/shard_map/ppermute | solution.py:468
  71.7 5.1 %collective-permute-start.26 = (bf16[128,512]{1,0:T(8,128)(2,1)S(1)}, bf16[128,512]{1,0:T(8,128)(2,1)S(1)}, u32[]{:S(2)}, u32[]{:S(2)}) collective-permute-start(bf16[128,512]{1,0:T(8,128)(2,1)S(1)} %collective-permute-done.21.refs_2_), channel_id=1, source_target_pairs={{0,8},{2,10},{4,12},{6,14},{8,0},{10,2},{12,4},{14,6},{16,24},{18,... | collective-permute-start | bytes 393224 | tf_op jit(solution)/shard_map/ppermute | solution.py:468
  77.4 7.6 %collective-permute-start.27 = (bf16[32,2944]{1,0:T(8,128)(2,1)S(1)}, bf16[32,2944]{1,0:T(8,128)(2,1)S(1)}, u32[]{:S(2)}, u32[]{:S(2)}) collective-permute-start(bf16[32,2944]{1,0:T(8,128)(2,1)S(1)} %get-tuple-element.110), channel_id=1, source_target_pairs={{0,2},{2,0},{4,6},{6,4},{8,10},{10,8},{12,14},{14,12},{16,18},{18,... | collective-permute-start | bytes 565256 | tf_op jit(solution)/shard_map/ppermute | solution.py:468
  78.6 10.5 %collective-permute-start.28 = (bf16[32,2944]{1,0:T(8,128)(2,1)S(1)}, bf16[32,2944]{1,0:T(8,128)(2,1)S(1)}, u32[]{:S(2)}, u32[]{:S(2)}) collective-permute-start(bf16[32,2944]{1,0:T(8,128)(2,1)S(1)} %get-tuple-element.111), channel_id=1, source_target_pairs={{0,4},{2,6},{4,0},{6,2},{8,12},{10,14},{12,8},{14,10},{16,20},{18,... | collective-permute-start | bytes 565256 | tf_op jit(solution)/shard_map/ppermute | solution.py:468
  79.8 9.3 %collective-permute-start.29 = (bf16[32,2944]{1,0:T(8,128)(2,1)S(1)}, bf16[32,2944]{1,0:T(8,128)(2,1)S(1)}, u32[]{:S(2)}, u32[]{:S(2)}) collective-permute-start(bf16[32,2944]{1,0:T(8,128)(2,1)S(1)} %get-tuple-element.112), channel_id=1, source_target_pairs={{0,6},{2,4},{4,2},{6,0},{8,14},{10,12},{12,10},{14,8},{16,22},{18,... | collective-permute-start | bytes 565256 | tf_op jit(solution)/shard_map/ppermute | solution.py:468
  (15 other events, 117.0 us)
Sparse Core Ops, SparseCore 0:
  13.8 54.1 all-gather.1

commit v18 on v17

--- a/solution.py
+++ b/solution.py
@@ -26,6 +26,10 @@
 
 def params(mebibytes):
     return pltpu.CompilerParams(vmem_limit_bytes=mebibytes << 20)
+
+
+def far_first(values):
+    return [values[0], *reversed(values[1:])]
 
 
 def lanes(start, size):
@@ -117,7 +121,7 @@
 
 
 def pack_kernel(depth, *refs):
-    line, out_ref = refs[:depth], refs[depth]
+    line, out_ref = far_first(refs[:depth]), refs[depth]
     rows = line[0].shape[0]
     for z in range(depth):
         out_ref[z * rows : (z + 1) * rows, :] = line[z][...]
@@ -133,7 +137,7 @@
         out_specs=VMEM,
         compiler_params=params(2),
         name="pack_tokens",
-    )(*line)
+    )(*far_first(line))
 
 
 def load_kernel(count, *refs):
@@ -270,7 +274,7 @@
 
 
 def plane_sum_kernel(depth, *refs):
-    in_refs, out_refs = refs[:PLANE], refs[PLANE:]
+    in_refs, out_refs = far_first(refs[:PLANE]), refs[PLANE:]
     group = in_refs[0].shape[0] // PLANE
     rows = group // depth
     for k in range(PLANE):
@@ -291,7 +295,7 @@
         out_specs=(VMEM,) * depth,
         compiler_params=params(4),
         name="plane_sum",
-    )(*parts)
+    )(*far_first(parts))
 
 
 def second_norm_kernel(depth, *refs):
@@ -330,7 +334,7 @@
         out_specs=(VMEM, VMEM),
         compiler_params=params(4),
         name="second_norm",
-    )(*parts, gain)
+    )(*far_first(parts), gain)
 
 
 def projection_kernel(chunk, mine_ref, theirs_ref, next_ref, q_ref, *refs):
@@ -386,7 +390,7 @@
 
 
 def head_norm_kernel(depth, *refs):
-    parts, q_gain_ref, k_gain_ref = refs[:PLANE], refs[PLANE], refs[PLANE + 1]
+    parts, q_gain_ref, k_gain_ref = far_first(refs[:PLANE]), refs[PLANE], refs[PLANE + 1]
     next_ref, q_ref, kv_ref = refs[PLANE + 2 :]
     width = next_ref.shape[1]
     q_cols, kv_cols = q_ref.shape[1], kv_ref.shape[1]
@@ -437,7 +441,7 @@
         out_specs=(VMEM, VMEM, VMEM),
         compiler_params=params(4),
         name="head_norm",
-    )(*parts, q_gain, k_gain)
+    )(*far_first(parts), q_gain, k_gain)
 
 
 def per_device_dense(

time: 97.1 us -> 97.2 us (level)
  no operation moved by 1% of the time
where the time goes in v18:
time: 97.2 us; the launch traced here: 97 us
  waiting for transfers between devices  36.2 us (37%)
  starting transfers between devices  27.6 us (28%)
  Pallas kernels  18.4 us (19%)
  between operations  14.2 us (15%)
    ppermute x19, waiting for transfers between devices, to_expert(): lax.ppermute(value, 'expert', [(i, i ^ offset) for i in range(n_expert)])  33.9 us
    ppermute x19, starting transfers between devices, to_expert(): lax.ppermute(value, 'expert', [(i, i ^ offset) for i in range(n_expert)])  25.6 us
    pallas_call x2, Pallas kernels, experts(): pl.pallas_call(functools.partial(expert_kernel, depth, chunk, len(blocks)...  6.05 us
    pallas_call x2, Pallas kernels, load(): pl.pallas_call(functools.partial(load_kernel, count), out_shape=tuple((pl...  5.42 us
    pallas_call x1, Pallas kernels, out_projection(): pl.pallas_call(functools.partial(out_projection_kernel, chunk), out_shape...  4.77 us
    ppermute x11, waiting for transfers between devices, to_core(): return lax.ppermute(value, 'tensor', [(0, 1), (1, 0)])  2.33 us
    ppermute x11, starting transfers between devices, to_core(): return lax.ppermute(value, 'tensor', [(0, 1), (1, 0)])  2 us
  transfers between devices with their start and end apart: 31, of which 19 were waited for; matrix products, arithmetic and copies ran while one was open for 1% of the time, Pallas kernels for 12%

profile of v18, /device:TPU:0, one launch (start us, length us, event | category | flops | bytes accessed | tf_op | source)
XLA Modules:
  0.0 97.0 jit_solution(9547302478752360371)
XLA Ops:
  7.3 4.8 %out_projection.1 = (f32[16,2048]{1,0:T(8,128)S(1)}, f32[16,2048]{1,0:T(8,128)S(1)}) custom-call(bf16[32,2048]{1,0:T(8,128)(2,1)} %a_hbm.1, bf16[2048,2048]{1,0:T(8,128)(2,1)} %w_hbm.1), custom_call_target="tpu_custom_call" | custom-call | tf_op jit(solution)/shard_map/out_projection/pallas_call | solution.py:81
  13.7 3.0 %collective-permute-start.1 = (bf16[16,2176]{1,0:T(8,128)(2,1)S(1)}, bf16[16,2176]{1,0:T(8,128)(2,1)S(1)}, u32[]{:S(2)}, u32[]{:S(2)}) collective-permute-start(bf16[16,2176]{1,0:T(8,128)(2,1)S(1)} %get-tuple-element.66.refs_3_.refs_0_), channel_id=1, source_target_pairs={{0,8},{2,10},{4,12},{6,14},{8,0},{10,2},{12,4},{14,6},{16,24},{18,... | collective-permute-start | bytes 208904 | tf_op jit(solution)/shard_map/ppermute | solution.py:472
  16.7 2.6 %collective-permute-start.2 = (bf16[16,2176]{1,0:T(8,128)(2,1)S(1)}, bf16[16,2176]{1,0:T(8,128)(2,1)S(1)}, u32[]{:S(2)}, u32[]{:S(2)}) collective-permute-start(bf16[16,2176]{1,0:T(8,128)(2,1)S(1)} %get-tuple-element.66.refs_3_.refs_0_), channel_id=1, source_target_pairs={{0,16},{2,18},{4,20},{6,22},{8,24},{10,26},{12,28},{14,30},{16,0},... | collective-permute-start | bytes 208904 | tf_op jit(solution)/shard_map/ppermute | solution.py:472
  19.3 3.8 %load_weights.2 = (bf16[1,2048,768]{2,1,0:T(8,128)(2,1)S(1)}, bf16[1,2048,768]{2,1,0:T(8,128)(2,1)S(1)}, bf16[1,768,2048]{2,1,0:T(8,128)(2,1)S(1)}) custom-call(bf16[1,2048,768]{2,1,0:T(8,128)(2,1)} %refs_0_.1, bf16[1,2048,768]{2,1,0:T(8,128)(2,1)} %refs_1_.1, bf16[1,768,2048]{2,1,0:T(8,128)(2,1)} %refs_2_.1, ...), custom_call_target="tpu_custom_call" | custom-call | tf_op jit(solution)/shard_map/load_weights/pallas_call | solution.py:157
  25.5 1.6 %collective-permute-start.4 = (bf16[64,2176]{1,0:T(8,128)(2,1)S(1)}, bf16[64,2176]{1,0:T(8,128)(2,1)S(1)}, u32[]{:S(2)}, u32[]{:S(2)}) collective-permute-start(bf16[64,2176]{1,0:T(8,128)(2,1)S(1)} %pack_tokens.1.refs_0_), channel_id=1, source_target_pairs={{0,2},{2,0},{4,6},{6,4},{8,10},{10,8},{12,14},{14,12},{16,18},{18,... | collective-permute-start | bytes 835592 | tf_op jit(solution)/shard_map/ppermute | solution.py:472
  27.1 1.5 %collective-permute-start.5 = (bf16[64,2176]{1,0:T(8,128)(2,1)S(1)}, bf16[64,2176]{1,0:T(8,128)(2,1)S(1)}, u32[]{:S(2)}, u32[]{:S(2)}) collective-permute-start(bf16[64,2176]{1,0:T(8,128)(2,1)S(1)} %pack_tokens.1.refs_0_), channel_id=1, source_target_pairs={{0,4},{2,6},{4,0},{6,2},{8,12},{10,14},{12,8},{14,10},{16,20},{18,... | collective-permute-start | bytes 835592 | tf_op jit(solution)/shard_map/ppermute | solution.py:472
  28.6 3.9 %collective-permute-done.4.refs_1_ = bf16[64,2176]{1,0:T(8,128)(2,1)S(1)} collective-permute-done((bf16[64,2176]{1,0:T(8,128)(2,1)S(1)}, bf16[64,2176]{1,0:T(8,128)(2,1)S(1)}, u32[]{:S(2)}, u32[]{:S(2)}) %collective-permute-start.4) | collective-permute-done | bytes 278560 | tf_op jit(solution)/shard_map/ppermute | solution.py:472
  33.7 1.6 %collective-permute-start.9 = (bf16[32,2176]{1,0:T(8,128)(2,1)S(1)}, bf16[32,2176]{1,0:T(8,128)(2,1)S(1)}, u32[]{:S(2)}, u32[]{:S(2)}) collective-permute-start(bf16[32,2176]{1,0:T(8,128)(2,1)S(1)} %slice.8), channel_id=1, source_target_pairs={{0,4},{2,6},{4,0},{6,2},{8,12},{10,14},{12,8},{14,10},{16,20},{18,... | collective-permute-start | bytes 417800 | tf_op jit(solution)/shard_map/ppermute | solution.py:472
  36.2 4.1 %experts.2 = (bf16[192,2048]{1,0:T(8,128)(2,1)S(1)}, bf16[64,2048]{1,0:T(8,128)(2,1)S(1)}, bf16[64,2048]{1,0:T(8,128)(2,1)S(1)}, bf16[64,2048]{1,0:T(8,128)(2,1)S(1)}) custom-call(bf16[64,2176]{1,0:T(8,128)(2,1)S(1)} %pack_tokens.1.refs_0_, bf16[64,2176]{1,0:T(8,128)(2,1)S(1)} %collective-permute-done.4.refs_1_, ...), custom_call_target="tpu_custom_call" | custom-call | flops 3623878656 | tf_op jit(solution)/shard_map/experts/pallas_call | solution.py:217
  42.8 2.0 %experts.3 = (bf16[64,2048]{1,0:T(8,128)(2,1)S(1)}, bf16[64,2048]{1,0:T(8,128)(2,1)S(1)}) custom-call(bf16[32,2176]{1,0:T(8,128)(2,1)S(1)} %collective-permute-done.9.refs_0_, bf16[32,2176]{1,0:T(8,128)(2,1)S(1)} %collective-permute-done.10.refs_1_, bf16[32,2176]{1,0:T(8,128)(2,1)S(1)} %collective-permute-done.11.refs_2_, ...), custom_call_target="tpu_custom_call" | custom-call | flops 1207959552 | tf_op jit(solution)/shard_map/experts/pallas_call | solution.py:217
  47.2 1.5 %collective-permute-start.18 = (bf16[256,512]{1,0:T(8,128)(2,1)S(1)}, bf16[256,512]{1,0:T(8,128)(2,1)S(1)}, u32[]{:S(2)}, u32[]{:S(2)}) collective-permute-start(bf16[256,512]{1,0:T(8,128)(2,1)S(1)} %get-tuple-element.88), channel_id=1, source_target_pairs={{0,4},{2,6},{4,0},{6,2},{8,12},{10,14},{12,8},{14,10},{16,20},{18,... | collective-permute-start | bytes 786440 | tf_op jit(solution)/shard_map/ppermute | solution.py:472
  48.7 1.5 %collective-permute-start.19 = (bf16[256,512]{1,0:T(8,128)(2,1)S(1)}, bf16[256,512]{1,0:T(8,128)(2,1)S(1)}, u32[]{:S(2)}, u32[]{:S(2)}) collective-permute-start(bf16[256,512]{1,0:T(8,128)(2,1)S(1)} %get-tuple-element.89), channel_id=1, source_target_pairs={{0,2},{2,0},{4,6},{6,4},{8,10},{10,8},{12,14},{14,12},{16,18},{18,... | collective-permute-start | bytes 786440 | tf_op jit(solution)/shard_map/ppermute | solution.py:472
  50.2 1.6 %collective-permute-start.20 = (bf16[128,512]{1,0:T(8,128)(2,1)S(1)}, bf16[128,512]{1,0:T(8,128)(2,1)S(1)}, u32[]{:S(2)}, u32[]{:S(2)}) collective-permute-start(bf16[128,512]{1,0:T(8,128)(2,1)S(1)} %copy-done.1), channel_id=1, source_target_pairs={{0,8},{2,10},{4,12},{6,14},{8,0},{10,2},{12,4},{14,6},{16,24},{18,... | collective-permute-start | bytes 393224 | tf_op jit(solution)/shard_map/ppermute | solution.py:472
  53.2 3.6 %collective-permute-done.17.refs_1_ = bf16[256,512]{1,0:T(8,128)(2,1)S(1)} collective-permute-done((bf16[256,512]{1,0:T(8,128)(2,1)S(1)}, bf16[256,512]{1,0:T(8,128)(2,1)S(1)}, u32[]{:S(2)}, u32[]{:S(2)}) %collective-permute-start.17) | collective-permute-done | bytes 262176 | tf_op jit(solution)/shard_map/ppermute | solution.py:472
  56.8 4.3 %collective-permute-done.18.refs_2_ = bf16[256,512]{1,0:T(8,128)(2,1)S(1)} collective-permute-done((bf16[256,512]{1,0:T(8,128)(2,1)S(1)}, bf16[256,512]{1,0:T(8,128)(2,1)S(1)}, u32[]{:S(2)}, u32[]{:S(2)}) %collective-permute-start.18) | collective-permute-done | bytes 262176 | tf_op jit(solution)/shard_map/ppermute | solution.py:472
  61.2 3.9 %collective-permute-done.20.refs_1_ = bf16[128,512]{1,0:T(8,128)(2,1)S(1)} collective-permute-done((bf16[128,512]{1,0:T(8,128)(2,1)S(1)}, bf16[128,512]{1,0:T(8,128)(2,1)S(1)}, u32[]{:S(2)}, u32[]{:S(2)}) %collective-permute-start.20) | collective-permute-done | bytes 131104 | tf_op jit(solution)/shard_map/ppermute | solution.py:472
  65.1 2.2 %collective-permute-done.21.refs_2_ = bf16[128,512]{1,0:T(8,128)(2,1)S(1)} collective-permute-done((bf16[128,512]{1,0:T(8,128)(2,1)S(1)}, bf16[128,512]{1,0:T(8,128)(2,1)S(1)}, u32[]{:S(2)}, u32[]{:S(2)}) %collective-permute-start.21) | collective-permute-done | bytes 131104 | tf_op jit(solution)/shard_map/ppermute | solution.py:472
  67.3 2.0 %collective-permute-start.23 = (bf16[64,512]{1,0:T(8,128)(2,1)S(1)}, bf16[64,512]{1,0:T(8,128)(2,1)S(1)}, u32[]{:S(2)}, u32[]{:S(2)}) collective-permute-start(bf16[64,512]{1,0:T(8,128)(2,1)S(1)} %get-tuple-element.97.refs_3_), channel_id=1, source_target_pairs={{0,16},{2,18},{4,20},{6,22},{8,24},{10,26},{12,28},{14,30},{16,0},... | collective-permute-start | bytes 196616 | tf_op jit(solution)/shard_map/ppermute | solution.py:472
  69.3 2.4 %collective-permute-start.24 = (bf16[64,512]{1,0:T(8,128)(2,1)S(1)}, bf16[64,512]{1,0:T(8,128)(2,1)S(1)}, u32[]{:S(2)}, u32[]{:S(2)}) collective-permute-start(bf16[64,512]{1,0:T(8,128)(2,1)S(1)} %get-tuple-element.98.refs_4_), channel_id=1, source_target_pairs={{0,24},{2,26},{4,28},{6,30},{8,16},{10,18},{12,20},{14,22},{16,8},... | collective-permute-start | bytes 196616 | tf_op jit(solution)/shard_map/ppermute | solution.py:472
  71.7 1.6 %load_weights.3.q_ref = bf16[512,2048]{1,0:T(8,128)(2,1)S(1)} custom-call(bf16[512,2048]{1,0:T(8,128)(2,1)} %all-gather.2.cloned.1.call-done.refs_0_, bf16[64,512]{1,0:T(8,128)(2,1)S(1)} %get-tuple-element.100.refs_1_.refs_0_, bf16[64,512]{1,0:T(8,128)(2,1)S(1)} %get-tuple-element.96.refs_2_, bf16[64,512]{1,0:T(8,128)(2,1)S(1)} %get-tuple-element.97.refs_3_, ...), custom_call_target="tpu_custom_call" | custom-call | tf_op jit(solution)/shard_map/load_weights/pallas_call | solution.py:157
  73.5 1.9 %collective-permute-done.24.refs_1_ = bf16[64,512]{1,0:T(8,128)(2,1)S(1)} collective-permute-done((bf16[64,512]{1,0:T(8,128)(2,1)S(1)}, bf16[64,512]{1,0:T(8,128)(2,1)S(1)}, u32[]{:S(2)}, u32[]{:S(2)}) %collective-permute-start.24) | collective-permute-done | bytes 65568 | tf_op jit(solution)/shard_map/ppermute | solution.py:472
  77.4 1.8 %collective-permute-start.27 = (bf16[32,2944]{1,0:T(8,128)(2,1)S(1)}, bf16[32,2944]{1,0:T(8,128)(2,1)S(1)}, u32[]{:S(2)}, u32[]{:S(2)}) collective-permute-start(bf16[32,2944]{1,0:T(8,128)(2,1)S(1)} %get-tuple-element.110), channel_id=1, source_target_pairs={{0,6},{2,4},{4,2},{6,0},{8,14},{10,12},{12,10},{14,8},{16,22},{18,... | collective-permute-start | bytes 565256 | tf_op jit(solution)/shard_map/ppermute | solution.py:472
  81.0 5.0 %collective-permute-done.27.refs_1_ = bf16[32,2944]{1,0:T(8,128)(2,1)S(1)} collective-permute-done((bf16[32,2944]{1,0:T(8,128)(2,1)S(1)}, bf16[32,2944]{1,0:T(8,128)(2,1)S(1)}, u32[]{:S(2)}, u32[]{:S(2)}) %collective-permute-start.27) | collective-permute-done | bytes 188448 | tf_op jit(solution)/shard_map/ppermute | solution.py:472
  86.0 3.2 %collective-permute-done.28.refs_2_ = bf16[32,2944]{1,0:T(8,128)(2,1)S(1)} collective-permute-done((bf16[32,2944]{1,0:T(8,128)(2,1)S(1)}, bf16[32,2944]{1,0:T(8,128)(2,1)S(1)}, u32[]{:S(2)}, u32[]{:S(2)}) %collective-permute-start.28) | collective-permute-done | bytes 188448 | tf_op jit(solution)/shard_map/ppermute | solution.py:472
  (76 shorter events, 17.5 us)
Async XLA Ops:
  7.2 64.4 %all-gather.2.cloned.1.call-start = ((), (), s32[]{:S(2)}) async-start(), calls=%async_computation | async-start | bytes 2621440 | tf_op jit(solution)/shard_map/all_gather | solution.py:491
  13.7 9.4 %collective-permute-start.1 = (bf16[16,2176]{1,0:T(8,128)(2,1)S(1)}, bf16[16,2176]{1,0:T(8,128)(2,1)S(1)}, u32[]{:S(2)}, u32[]{:S(2)}) collective-permute-start(bf16[16,2176]{1,0:T(8,128)(2,1)S(1)} %get-tuple-element.66.refs_3_.refs_0_), channel_id=1, source_target_pairs={{0,8},{2,10},{4,12},{6,14},{8,0},{10,2},{12,4},{14,6},{16,24},{18,... | collective-permute-start | bytes 208904 | tf_op jit(solution)/shard_map/ppermute | solution.py:472
  16.7 7.8 %collective-permute-start.2 = (bf16[16,2176]{1,0:T(8,128)(2,1)S(1)}, bf16[16,2176]{1,0:T(8,128)(2,1)S(1)}, u32[]{:S(2)}, u32[]{:S(2)}) collective-permute-start(bf16[16,2176]{1,0:T(8,128)(2,1)S(1)} %get-tuple-element.66.refs_3_.refs_0_), channel_id=1, source_target_pairs={{0,16},{2,18},{4,20},{6,22},{8,24},{10,26},{12,28},{14,30},{16,0},... | collective-permute-start | bytes 208904 | tf_op jit(solution)/shard_map/ppermute | solution.py:472
  19.3 6.2 %collective-permute-start.3 = (bf16[16,2176]{1,0:T(8,128)(2,1)S(1)}, bf16[16,2176]{1,0:T(8,128)(2,1)S(1)}, u32[]{:S(2)}, u32[]{:S(2)}) collective-permute-start(bf16[16,2176]{1,0:T(8,128)(2,1)S(1)} %get-tuple-element.66.refs_3_.refs_0_), channel_id=1, source_target_pairs={{0,24},{2,26},{4,28},{6,30},{8,16},{10,18},{12,20},{14,22},{16,8},... | collective-permute-start | bytes 208904 | tf_op jit(solution)/shard_map/ppermute | solution.py:472
  25.5 7.0 %collective-permute-start.4 = (bf16[64,2176]{1,0:T(8,128)(2,1)S(1)}, bf16[64,2176]{1,0:T(8,128)(2,1)S(1)}, u32[]{:S(2)}, u32[]{:S(2)}) collective-permute-start(bf16[64,2176]{1,0:T(8,128)(2,1)S(1)} %pack_tokens.1.refs_0_), channel_id=1, source_target_pairs={{0,2},{2,0},{4,6},{6,4},{8,10},{10,8},{12,14},{14,12},{16,18},{18,... | collective-permute-start | bytes 835592 | tf_op jit(solution)/shard_map/ppermute | solution.py:472
  27.1 6.6 %collective-permute-start.5 = (bf16[64,2176]{1,0:T(8,128)(2,1)S(1)}, bf16[64,2176]{1,0:T(8,128)(2,1)S(1)}, u32[]{:S(2)}, u32[]{:S(2)}) collective-permute-start(bf16[64,2176]{1,0:T(8,128)(2,1)S(1)} %pack_tokens.1.refs_0_), channel_id=1, source_target_pairs={{0,4},{2,6},{4,0},{6,2},{8,12},{10,14},{12,8},{14,10},{16,20},{18,... | collective-permute-start | bytes 835592 | tf_op jit(solution)/shard_map/ppermute | solution.py:472
  28.6 7.6 %collective-permute-start.6 = (bf16[64,2176]{1,0:T(8,128)(2,1)S(1)}, bf16[64,2176]{1,0:T(8,128)(2,1)S(1)}, u32[]{:S(2)}, u32[]{:S(2)}) collective-permute-start(bf16[64,2176]{1,0:T(8,128)(2,1)S(1)} %pack_tokens.1.refs_0_), channel_id=1, source_target_pairs={{0,1},{1,0},{2,3},{3,2},{4,5},{5,4},{6,7},{7,6},{8,9},{9,8},{10,11... | collective-permute-start | bytes 835592 | tf_op jit(solution)/shard_map/ppermute | solution.py:469
  32.5 3.7 %collective-permute-start.7 = (bf16[64,2176]{1,0:T(8,128)(2,1)S(1)}, bf16[64,2176]{1,0:T(8,128)(2,1)S(1)}, u32[]{:S(2)}, u32[]{:S(2)}) collective-permute-start(bf16[64,2176]{1,0:T(8,128)(2,1)S(1)} %collective-permute-done.4.refs_1_), channel_id=1, source_target_pairs={{0,1},{1,0},{2,3},{3,2},{4,5},{5,4},{6,7},{7,6},{8,9},{9,8},{10,11... | collective-permute-start | bytes 835592 | tf_op jit(solution)/shard_map/ppermute | solution.py:469
  33.7 6.5 %collective-permute-start.9 = (bf16[32,2176]{1,0:T(8,128)(2,1)S(1)}, bf16[32,2176]{1,0:T(8,128)(2,1)S(1)}, u32[]{:S(2)}, u32[]{:S(2)}) collective-permute-start(bf16[32,2176]{1,0:T(8,128)(2,1)S(1)} %slice.8), channel_id=1, source_target_pairs={{0,4},{2,6},{4,0},{6,2},{8,12},{10,14},{12,8},{14,10},{16,20},{18,... | collective-permute-start | bytes 417800 | tf_op jit(solution)/shard_map/ppermute | solution.py:472
  35.3 5.9 %collective-permute-start.10 = (bf16[32,2176]{1,0:T(8,128)(2,1)S(1)}, bf16[32,2176]{1,0:T(8,128)(2,1)S(1)}, u32[]{:S(2)}, u32[]{:S(2)}) collective-permute-start(bf16[32,2176]{1,0:T(8,128)(2,1)S(1)} %slice.9), channel_id=1, source_target_pairs={{0,2},{2,0},{4,6},{6,4},{8,10},{10,8},{12,14},{14,12},{16,18},{18,... | collective-permute-start | bytes 417800 | tf_op jit(solution)/shard_map/ppermute | solution.py:472
  41.7 3.4 %collective-permute-start.13 = (bf16[64,2048]{1,0:T(8,128)(2,1)S(1)}, bf16[64,2048]{1,0:T(8,128)(2,1)S(1)}, u32[]{:S(2)}, u32[]{:S(2)}) collective-permute-start(bf16[64,2048]{1,0:T(8,128)(2,1)S(1)} %get-tuple-element.78), channel_id=1, source_target_pairs={{0,1},{1,0},{2,3},{3,2},{4,5},{5,4},{6,7},{7,6},{8,9},{9,8},{10,11... | collective-permute-start | bytes 786440 | tf_op jit(solution)/shard_map/ppermute | solution.py:469
  41.7 3.4 %collective-permute-start.14 = (bf16[64,2048]{1,0:T(8,128)(2,1)S(1)}, bf16[64,2048]{1,0:T(8,128)(2,1)S(1)}, u32[]{:S(2)}, u32[]{:S(2)}) collective-permute-start(bf16[64,2048]{1,0:T(8,128)(2,1)S(1)} %get-tuple-element.79), channel_id=1, source_target_pairs={{0,1},{1,0},{2,3},{3,2},{4,5},{5,4},{6,7},{7,6},{8,9},{9,8},{10,11... | collective-permute-start | bytes 786440 | tf_op jit(solution)/shard_map/ppermute | solution.py:469
  46.6 10.1 %collective-permute-start.17 = (bf16[256,512]{1,0:T(8,128)(2,1)S(1)}, bf16[256,512]{1,0:T(8,128)(2,1)S(1)}, u32[]{:S(2)}, u32[]{:S(2)}) collective-permute-start(bf16[256,512]{1,0:T(8,128)(2,1)S(1)} %get-tuple-element.87), channel_id=1, source_target_pairs={{0,6},{2,4},{4,2},{6,0},{8,14},{10,12},{12,10},{14,8},{16,22},{18,... | collective-permute-start | bytes 786440 | tf_op jit(solution)/shard_map/ppermute | solution.py:472
  47.2 13.9 %collective-permute-start.18 = (bf16[256,512]{1,0:T(8,128)(2,1)S(1)}, bf16[256,512]{1,0:T(8,128)(2,1)S(1)}, u32[]{:S(2)}, u32[]{:S(2)}) collective-permute-start(bf16[256,512]{1,0:T(8,128)(2,1)S(1)} %get-tuple-element.88), channel_id=1, source_target_pairs={{0,4},{2,6},{4,0},{6,2},{8,12},{10,14},{12,8},{14,10},{16,20},{18,... | collective-permute-start | bytes 786440 | tf_op jit(solution)/shard_map/ppermute | solution.py:472
  48.7 12.4 %collective-permute-start.19 = (bf16[256,512]{1,0:T(8,128)(2,1)S(1)}, bf16[256,512]{1,0:T(8,128)(2,1)S(1)}, u32[]{:S(2)}, u32[]{:S(2)}) collective-permute-start(bf16[256,512]{1,0:T(8,128)(2,1)S(1)} %get-tuple-element.89), channel_id=1, source_target_pairs={{0,2},{2,0},{4,6},{6,4},{8,10},{10,8},{12,14},{14,12},{16,18},{18,... | collective-permute-start | bytes 786440 | tf_op jit(solution)/shard_map/ppermute | solution.py:472
  50.2 14.9 %collective-permute-start.20 = (bf16[128,512]{1,0:T(8,128)(2,1)S(1)}, bf16[128,512]{1,0:T(8,128)(2,1)S(1)}, u32[]{:S(2)}, u32[]{:S(2)}) collective-permute-start(bf16[128,512]{1,0:T(8,128)(2,1)S(1)} %copy-done.1), channel_id=1, source_target_pairs={{0,8},{2,10},{4,12},{6,14},{8,0},{10,2},{12,4},{14,6},{16,24},{18,... | collective-permute-start | bytes 393224 | tf_op jit(solution)/shard_map/ppermute | solution.py:472
  51.7 15.5 %collective-permute-start.21 = (bf16[128,512]{1,0:T(8,128)(2,1)S(1)}, bf16[128,512]{1,0:T(8,128)(2,1)S(1)}, u32[]{:S(2)}, u32[]{:S(2)}) collective-permute-start(bf16[128,512]{1,0:T(8,128)(2,1)S(1)} %copy-done.1), channel_id=1, source_target_pairs={{0,16},{2,18},{4,20},{6,22},{8,24},{10,26},{12,28},{14,30},{16,0},... | collective-permute-start | bytes 393224 | tf_op jit(solution)/shard_map/ppermute | solution.py:472
  67.3 6.2 %collective-permute-start.22 = (bf16[64,512]{1,0:T(8,128)(2,1)S(1)}, bf16[64,512]{1,0:T(8,128)(2,1)S(1)}, u32[]{:S(2)}, u32[]{:S(2)}) collective-permute-start(bf16[64,512]{1,0:T(8,128)(2,1)S(1)} %get-tuple-element.96.refs_2_), channel_id=1, source_target_pairs={{0,8},{2,10},{4,12},{6,14},{8,0},{10,2},{12,4},{14,6},{16,24},{18,... | collective-permute-start | bytes 196616 | tf_op jit(solution)/shard_map/ppermute | solution.py:472
  67.3 6.2 %collective-permute-start.23 = (bf16[64,512]{1,0:T(8,128)(2,1)S(1)}, bf16[64,512]{1,0:T(8,128)(2,1)S(1)}, u32[]{:S(2)}, u32[]{:S(2)}) collective-permute-start(bf16[64,512]{1,0:T(8,128)(2,1)S(1)} %get-tuple-element.97.refs_3_), channel_id=1, source_target_pairs={{0,16},{2,18},{4,20},{6,22},{8,24},{10,26},{12,28},{14,30},{16,0},... | collective-permute-start | bytes 196616 | tf_op jit(solution)/shard_map/ppermute | solution.py:472
  69.3 6.1 %collective-permute-start.24 = (bf16[64,512]{1,0:T(8,128)(2,1)S(1)}, bf16[64,512]{1,0:T(8,128)(2,1)S(1)}, u32[]{:S(2)}, u32[]{:S(2)}) collective-permute-start(bf16[64,512]{1,0:T(8,128)(2,1)S(1)} %get-tuple-element.98.refs_4_), channel_id=1, source_target_pairs={{0,24},{2,26},{4,28},{6,30},{8,16},{10,18},{12,20},{14,22},{16,8},... | collective-permute-start | bytes 196616 | tf_op jit(solution)/shard_map/ppermute | solution.py:472
  71.7 5.1 %collective-permute-start.26 = (bf16[128,512]{1,0:T(8,128)(2,1)S(1)}, bf16[128,512]{1,0:T(8,128)(2,1)S(1)}, u32[]{:S(2)}, u32[]{:S(2)}) collective-permute-start(bf16[128,512]{1,0:T(8,128)(2,1)S(1)} %collective-permute-done.21.refs_2_), channel_id=1, source_target_pairs={{0,8},{2,10},{4,12},{6,14},{8,0},{10,2},{12,4},{14,6},{16,24},{18,... | collective-permute-start | bytes 393224 | tf_op jit(solution)/shard_map/ppermute | solution.py:472
  77.4 8.6 %collective-permute-start.27 = (bf16[32,2944]{1,0:T(8,128)(2,1)S(1)}, bf16[32,2944]{1,0:T(8,128)(2,1)S(1)}, u32[]{:S(2)}, u32[]{:S(2)}) collective-permute-start(bf16[32,2944]{1,0:T(8,128)(2,1)S(1)} %get-tuple-element.110), channel_id=1, source_target_pairs={{0,6},{2,4},{4,2},{6,0},{8,14},{10,12},{12,10},{14,8},{16,22},{18,... | collective-permute-start | bytes 565256 | tf_op jit(solution)/shard_map/ppermute | solution.py:472
  79.3 10.0 %collective-permute-start.28 = (bf16[32,2944]{1,0:T(8,128)(2,1)S(1)}, bf16[32,2944]{1,0:T(8,128)(2,1)S(1)}, u32[]{:S(2)}, u32[]{:S(2)}) collective-permute-start(bf16[32,2944]{1,0:T(8,128)(2,1)S(1)} %get-tuple-element.111), channel_id=1, source_target_pairs={{0,4},{2,6},{4,0},{6,2},{8,12},{10,14},{12,8},{14,10},{16,20},{18,... | collective-permute-start | bytes 565256 | tf_op jit(solution)/shard_map/ppermute | solution.py:472
  80.1 9.2 %collective-permute-start.29 = (bf16[32,2944]{1,0:T(8,128)(2,1)S(1)}, bf16[32,2944]{1,0:T(8,128)(2,1)S(1)}, u32[]{:S(2)}, u32[]{:S(2)}) collective-permute-start(bf16[32,2944]{1,0:T(8,128)(2,1)S(1)} %get-tuple-element.112), channel_id=1, source_target_pairs={{0,2},{2,0},{4,6},{6,4},{8,10},{10,8},{12,14},{14,12},{16,18},{18,... | collective-permute-start | bytes 565256 | tf_op jit(solution)/shard_map/ppermute | solution.py:472
  (15 other events, 117.1 us)
Sparse Core Ops, SparseCore 0:
  13.8 54.1 all-gather.1

commit v19 on v17

--- a/solution.py
+++ b/solution.py
@@ -502,11 +502,9 @@
     *sums, kv_own = lax.optimization_barrier((*chip_sum((near_mine, far_mine), theirs, first, depth), kv_weight))
     parts = to_plane(sums)
     kv_rows = [kv_own, to_expert(kv_own, PLANE), to_expert(kv_own, 2 * PLANE)]
-    *parts, kv_rows[1], kv_rows[2] = lax.optimization_barrier(
-        (*plane_sum(parts, depth), *kv_rows[1:])
-    )
+    parts = plane_sum(parts, depth)
     kv_rows.append(to_expert(kv_rows[2], PLANE))
-    (q_rows,) = load((q_rows,), parts)
+    (q_rows,) = load((q_rows,), (*parts, *kv_rows[1:3]))
     parts = to_z(parts)
     *parts, q_rows = lax.optimization_barrier((*parts, q_rows))
     scaled, following = second_norm(parts, input_gain[None, :])

time: 97.1 us -> 94.9 us (0.977)
  waiting for transfers between devices: 36.2 us -> 33.2 us
    ppermute x19, waiting for transfers between devices: 33.8 us -> 27 us  [to_expert(): lax.ppermute(value, 'expert', [(i, i ^ offset) for i in range(n_expert)])]
    all_gather x1, waiting for transfers between devices: 0.01 us -> 3.04 us  [per_device_dense(): lax.all_gather(q_own, 'expert', axis=0, tiled=True, axis_index_groups=lines)]
  transfers between devices with their start and end apart: 31 -> 31, of which waited for: 19 -> 17; matrix products, arithmetic and copies ran while one was open for 1% -> 1% of each run, Pallas kernels for 12% -> 13%
where the time goes in v19:
time: 94.9 us; the launch traced here: 94.7 us
  waiting for transfers between devices  33.2 us (35%)
  starting transfers between devices  28.3 us (30%)
  Pallas kernels  18.4 us (19%)
  between operations  14.2 us (15%)
    ppermute x19, waiting for transfers between devices, to_expert(): lax.ppermute(value, 'expert', [(i, i ^ offset) for i in range(n_expert)])  27 us
    ppermute x19, starting transfers between devices, to_expert(): lax.ppermute(value, 'expert', [(i, i ^ offset) for i in range(n_expert)])  26.3 us
    pallas_call x2, Pallas kernels, experts(): pl.pallas_call(functools.partial(expert_kernel, depth, chunk, len(blocks)...  6.05 us
    pallas_call x2, Pallas kernels, load(): pl.pallas_call(functools.partial(load_kernel, count), out_shape=tuple((pl...  5.45 us
    pallas_call x1, Pallas kernels, out_projection(): pl.pallas_call(functools.partial(out_projection_kernel, chunk), out_shape...  4.77 us
    ppermute x11, waiting for transfers between devices, to_core(): return lax.ppermute(value, 'tensor', [(0, 1), (1, 0)])  3.2 us
    all_gather x1, waiting for transfers between devices, per_device_dense(): lax.all_gather(q_own, 'expert', axis=0, tiled=True, axis_index_groups=lines)  3.04 us
    ppermute x11, starting transfers between devices, to_core(): return lax.ppermute(value, 'tensor', [(0, 1), (1, 0)])  2 us
  transfers between devices with their start and end apart: 31, of which 17 were waited for; matrix products, arithmetic and copies ran while one was open for 1% of the time, Pallas kernels for 13%

profile of v19, /device:TPU:0, one launch (start us, length us, event | category | flops | bytes accessed | tf_op | source)
XLA Modules:
  0.0 94.7 jit_solution(18218352347147809435)
XLA Ops:
  7.3 4.8 %out_projection.1 = (f32[16,2048]{1,0:T(8,128)S(1)}, f32[16,2048]{1,0:T(8,128)S(1)}) custom-call(bf16[32,2048]{1,0:T(8,128)(2,1)} %a_hbm.1, bf16[2048,2048]{1,0:T(8,128)(2,1)} %w_hbm.1), custom_call_target="tpu_custom_call" | custom-call | tf_op jit(solution)/shard_map/out_projection/pallas_call | solution.py:77
  13.7 3.0 %collective-permute-start.1 = (bf16[16,2176]{1,0:T(8,128)(2,1)S(1)}, bf16[16,2176]{1,0:T(8,128)(2,1)S(1)}, u32[]{:S(2)}, u32[]{:S(2)}) collective-permute-start(bf16[16,2176]{1,0:T(8,128)(2,1)S(1)} %get-tuple-element.60.refs_3_.refs_0_), channel_id=1, source_target_pairs={{0,8},{2,10},{4,12},{6,14},{8,0},{10,2},{12,4},{14,6},{16,24},{18,... | collective-permute-start | bytes 208904 | tf_op jit(solution)/shard_map/ppermute | solution.py:468
  16.7 2.6 %collective-permute-start.2 = (bf16[16,2176]{1,0:T(8,128)(2,1)S(1)}, bf16[16,2176]{1,0:T(8,128)(2,1)S(1)}, u32[]{:S(2)}, u32[]{:S(2)}) collective-permute-start(bf16[16,2176]{1,0:T(8,128)(2,1)S(1)} %get-tuple-element.60.refs_3_.refs_0_), channel_id=1, source_target_pairs={{0,16},{2,18},{4,20},{6,22},{8,24},{10,26},{12,28},{14,30},{16,0},... | collective-permute-start | bytes 208904 | tf_op jit(solution)/shard_map/ppermute | solution.py:468
  19.3 3.8 %load_weights.2 = (bf16[1,2048,768]{2,1,0:T(8,128)(2,1)S(1)}, bf16[1,2048,768]{2,1,0:T(8,128)(2,1)S(1)}, bf16[1,768,2048]{2,1,0:T(8,128)(2,1)S(1)}) custom-call(bf16[1,2048,768]{2,1,0:T(8,128)(2,1)} %refs_0_.1, bf16[1,2048,768]{2,1,0:T(8,128)(2,1)} %refs_1_.1, bf16[1,768,2048]{2,1,0:T(8,128)(2,1)} %refs_2_.1, ...), custom_call_target="tpu_custom_call" | custom-call | tf_op jit(solution)/shard_map/load_weights/pallas_call | solution.py:153
  25.5 1.6 %collective-permute-start.4 = (bf16[64,2176]{1,0:T(8,128)(2,1)S(1)}, bf16[64,2176]{1,0:T(8,128)(2,1)S(1)}, u32[]{:S(2)}, u32[]{:S(2)}) collective-permute-start(bf16[64,2176]{1,0:T(8,128)(2,1)S(1)} %pack_tokens.1.refs_0_), channel_id=1, source_target_pairs={{0,2},{2,0},{4,6},{6,4},{8,10},{10,8},{12,14},{14,12},{16,18},{18,... | collective-permute-start | bytes 835592 | tf_op jit(solution)/shard_map/ppermute | solution.py:468
  27.1 1.5 %collective-permute-start.5 = (bf16[64,2176]{1,0:T(8,128)(2,1)S(1)}, bf16[64,2176]{1,0:T(8,128)(2,1)S(1)}, u32[]{:S(2)}, u32[]{:S(2)}) collective-permute-start(bf16[64,2176]{1,0:T(8,128)(2,1)S(1)} %pack_tokens.1.refs_0_), channel_id=1, source_target_pairs={{0,4},{2,6},{4,0},{6,2},{8,12},{10,14},{12,8},{14,10},{16,20},{18,... | collective-permute-start | bytes 835592 | tf_op jit(solution)/shard_map/ppermute | solution.py:468
  28.6 3.9 %collective-permute-done.4.refs_1_ = bf16[64,2176]{1,0:T(8,128)(2,1)S(1)} collective-permute-done((bf16[64,2176]{1,0:T(8,128)(2,1)S(1)}, bf16[64,2176]{1,0:T(8,128)(2,1)S(1)}, u32[]{:S(2)}, u32[]{:S(2)}) %collective-permute-start.4) | collective-permute-done | bytes 278560 | tf_op jit(solution)/shard_map/ppermute | solution.py:468
  33.7 1.6 %collective-permute-start.9 = (bf16[32,2176]{1,0:T(8,128)(2,1)S(1)}, bf16[32,2176]{1,0:T(8,128)(2,1)S(1)}, u32[]{:S(2)}, u32[]{:S(2)}) collective-permute-start(bf16[32,2176]{1,0:T(8,128)(2,1)S(1)} %slice.8), channel_id=1, source_target_pairs={{0,4},{2,6},{4,0},{6,2},{8,12},{10,14},{12,8},{14,10},{16,20},{18,... | collective-permute-start | bytes 417800 | tf_op jit(solution)/shard_map/ppermute | solution.py:468
  36.2 4.1 %experts.2 = (bf16[192,2048]{1,0:T(8,128)(2,1)S(1)}, bf16[64,2048]{1,0:T(8,128)(2,1)S(1)}, bf16[64,2048]{1,0:T(8,128)(2,1)S(1)}, bf16[64,2048]{1,0:T(8,128)(2,1)S(1)}) custom-call(bf16[64,2176]{1,0:T(8,128)(2,1)S(1)} %pack_tokens.1.refs_0_, bf16[64,2176]{1,0:T(8,128)(2,1)S(1)} %collective-permute-done.4.refs_1_, ...), custom_call_target="tpu_custom_call" | custom-call | flops 3623878656 | tf_op jit(solution)/shard_map/experts/pallas_call | solution.py:213
  42.8 2.0 %experts.3 = (bf16[64,2048]{1,0:T(8,128)(2,1)S(1)}, bf16[64,2048]{1,0:T(8,128)(2,1)S(1)}) custom-call(bf16[32,2176]{1,0:T(8,128)(2,1)S(1)} %collective-permute-done.9.refs_0_, bf16[32,2176]{1,0:T(8,128)(2,1)S(1)} %collective-permute-done.10.refs_1_, bf16[32,2176]{1,0:T(8,128)(2,1)S(1)} %collective-permute-done.11.refs_2_, ...), custom_call_target="tpu_custom_call" | custom-call | flops 1207959552 | tf_op jit(solution)/shard_map/experts/pallas_call | solution.py:213
  47.7 2.4 %collective-permute-start.19 = (bf16[256,512]{1,0:T(8,128)(2,1)S(1)}, bf16[256,512]{1,0:T(8,128)(2,1)S(1)}, u32[]{:S(2)}, u32[]{:S(2)}) collective-permute-start(bf16[256,512]{1,0:T(8,128)(2,1)S(1)} %get-tuple-element.83), channel_id=1, source_target_pairs={{0,6},{2,4},{4,2},{6,0},{8,14},{10,12},{12,10},{14,8},{16,22},{18,... | collective-permute-start | bytes 786440 | tf_op jit(solution)/shard_map/ppermute | solution.py:468
  50.2 2.5 %collective-permute-start.24 = (bf16[128,512]{1,0:T(8,128)(2,1)S(1)}, bf16[128,512]{1,0:T(8,128)(2,1)S(1)}, u32[]{:S(2)}, u32[]{:S(2)}) collective-permute-start(bf16[128,512]{1,0:T(8,128)(2,1)S(1)} %copy-done.1), channel_id=1, source_target_pairs={{0,16},{2,18},{4,20},{6,22},{8,24},{10,26},{12,28},{14,30},{16,0},... | collective-permute-start | bytes 393224 | tf_op jit(solution)/shard_map/ppermute | solution.py:468
  53.2 2.7 %collective-permute-done.17.refs_1_ = bf16[256,512]{1,0:T(8,128)(2,1)S(1)} collective-permute-done((bf16[256,512]{1,0:T(8,128)(2,1)S(1)}, bf16[256,512]{1,0:T(8,128)(2,1)S(1)}, u32[]{:S(2)}, u32[]{:S(2)}) %collective-permute-start.17) | collective-permute-done | bytes 262176 | tf_op jit(solution)/shard_map/ppermute | solution.py:468
  55.8 5.3 %collective-permute-done.18.refs_2_ = bf16[256,512]{1,0:T(8,128)(2,1)S(1)} collective-permute-done((bf16[256,512]{1,0:T(8,128)(2,1)S(1)}, bf16[256,512]{1,0:T(8,128)(2,1)S(1)}, u32[]{:S(2)}, u32[]{:S(2)}) %collective-permute-start.18) | collective-permute-done | bytes 262176 | tf_op jit(solution)/shard_map/ppermute | solution.py:468
  61.2 1.6 %collective-permute-start.20 = (bf16[64,512]{1,0:T(8,128)(2,1)S(1)}, bf16[64,512]{1,0:T(8,128)(2,1)S(1)}, u32[]{:S(2)}, u32[]{:S(2)}) collective-permute-start(bf16[64,512]{1,0:T(8,128)(2,1)S(1)} %get-tuple-element.85.refs_2_), channel_id=1, source_target_pairs={{0,8},{2,10},{4,12},{6,14},{8,0},{10,2},{12,4},{14,6},{16,24},{18,... | collective-permute-start | bytes 196616 | tf_op jit(solution)/shard_map/ppermute | solution.py:468
  62.8 1.4 %collective-permute-start.21 = (bf16[64,512]{1,0:T(8,128)(2,1)S(1)}, bf16[64,512]{1,0:T(8,128)(2,1)S(1)}, u32[]{:S(2)}, u32[]{:S(2)}) collective-permute-start(bf16[64,512]{1,0:T(8,128)(2,1)S(1)} %get-tuple-element.86.refs_3_), channel_id=1, source_target_pairs={{0,16},{2,18},{4,20},{6,22},{8,24},{10,26},{12,28},{14,30},{16,0},... | collective-permute-start | bytes 196616 | tf_op jit(solution)/shard_map/ppermute | solution.py:468
  64.3 1.4 %collective-permute-start.22 = (bf16[64,512]{1,0:T(8,128)(2,1)S(1)}, bf16[64,512]{1,0:T(8,128)(2,1)S(1)}, u32[]{:S(2)}, u32[]{:S(2)}) collective-permute-start(bf16[64,512]{1,0:T(8,128)(2,1)S(1)} %get-tuple-element.87.refs_4_), channel_id=1, source_target_pairs={{0,24},{2,26},{4,28},{6,30},{8,16},{10,18},{12,20},{14,22},{16,8},... | collective-permute-start | bytes 196616 | tf_op jit(solution)/shard_map/ppermute | solution.py:468
  66.3 3.0 %all-gather.2.cloned.1.call-done.refs_0_ = bf16[512,2048]{1,0:T(8,128)(2,1)} async-done(((bf16[128,2048]{1,0:T(8,128)(2,1)}), bf16[512,2048]{1,0:T(8,128)(2,1)}) %all-gather.2.cloned.1.call-update) | async-done | bytes 2097168 | tf_op jit(solution)/shard_map/all_gather | solution.py:487
  69.4 1.6 %load_weights.3.q_ref = bf16[512,2048]{1,0:T(8,128)(2,1)S(1)} custom-call(bf16[512,2048]{1,0:T(8,128)(2,1)} %all-gather.2.cloned.1.call-done.refs_0_, bf16[64,512]{1,0:T(8,128)(2,1)S(1)} %get-tuple-element.90.refs_1_.refs_0_, bf16[64,512]{1,0:T(8,128)(2,1)S(1)} %get-tuple-element.85.refs_2_, bf16[64,512]{1,0:T(8,128)(2,1)S(1)} %get-tuple-element.86.refs_3_, ...), custom_call_target="tpu_custom_call" | custom-call | tf_op jit(solution)/shard_map/load_weights/pallas_call | solution.py:153
  71.0 1.7 %collective-permute-done.22.refs_3_ = bf16[64,512]{1,0:T(8,128)(2,1)S(1)} collective-permute-done((bf16[64,512]{1,0:T(8,128)(2,1)S(1)}, bf16[64,512]{1,0:T(8,128)(2,1)S(1)}, u32[]{:S(2)}, u32[]{:S(2)}) %collective-permute-start.22) | collective-permute-done | bytes 65568 | tf_op jit(solution)/shard_map/ppermute | solution.py:468
  74.8 1.7 %collective-permute-start.27 = (bf16[32,2944]{1,0:T(8,128)(2,1)S(1)}, bf16[32,2944]{1,0:T(8,128)(2,1)S(1)}, u32[]{:S(2)}, u32[]{:S(2)}) collective-permute-start(bf16[32,2944]{1,0:T(8,128)(2,1)S(1)} %get-tuple-element.98), channel_id=1, source_target_pairs={{0,2},{2,0},{4,6},{6,4},{8,10},{10,8},{12,14},{14,12},{16,18},{18,... | collective-permute-start | bytes 565256 | tf_op jit(solution)/shard_map/ppermute | solution.py:468
  76.4 1.4 %collective-permute-start.28 = (bf16[32,2944]{1,0:T(8,128)(2,1)S(1)}, bf16[32,2944]{1,0:T(8,128)(2,1)S(1)}, u32[]{:S(2)}, u32[]{:S(2)}) collective-permute-start(bf16[32,2944]{1,0:T(8,128)(2,1)S(1)} %get-tuple-element.99), channel_id=1, source_target_pairs={{0,4},{2,6},{4,0},{6,2},{8,12},{10,14},{12,8},{14,10},{16,20},{18,... | collective-permute-start | bytes 565256 | tf_op jit(solution)/shard_map/ppermute | solution.py:468
  78.3 4.1 %collective-permute-done.27.refs_1_ = bf16[32,2944]{1,0:T(8,128)(2,1)S(1)} collective-permute-done((bf16[32,2944]{1,0:T(8,128)(2,1)S(1)}, bf16[32,2944]{1,0:T(8,128)(2,1)S(1)}, u32[]{:S(2)}, u32[]{:S(2)}) %collective-permute-start.27) | collective-permute-done | bytes 188448 | tf_op jit(solution)/shard_map/ppermute | solution.py:468
  82.4 4.6 %collective-permute-done.28.refs_2_ = bf16[32,2944]{1,0:T(8,128)(2,1)S(1)} collective-permute-done((bf16[32,2944]{1,0:T(8,128)(2,1)S(1)}, bf16[32,2944]{1,0:T(8,128)(2,1)S(1)}, u32[]{:S(2)}, u32[]{:S(2)}) %collective-permute-start.28) | collective-permute-done | bytes 188448 | tf_op jit(solution)/shard_map/ppermute | solution.py:468
  (76 shorter events, 16.3 us)
Async XLA Ops:
  7.2 62.2 %all-gather.2.cloned.1.call-start = ((), (), s32[]{:S(2)}) async-start(), calls=%async_computation | async-start | bytes 2621440 | tf_op jit(solution)/shard_map/all_gather | solution.py:487
  13.7 9.4 %collective-permute-start.1 = (bf16[16,2176]{1,0:T(8,128)(2,1)S(1)}, bf16[16,2176]{1,0:T(8,128)(2,1)S(1)}, u32[]{:S(2)}, u32[]{:S(2)}) collective-permute-start(bf16[16,2176]{1,0:T(8,128)(2,1)S(1)} %get-tuple-element.60.refs_3_.refs_0_), channel_id=1, source_target_pairs={{0,8},{2,10},{4,12},{6,14},{8,0},{10,2},{12,4},{14,6},{16,24},{18,... | collective-permute-start | bytes 208904 | tf_op jit(solution)/shard_map/ppermute | solution.py:468
  16.7 7.8 %collective-permute-start.2 = (bf16[16,2176]{1,0:T(8,128)(2,1)S(1)}, bf16[16,2176]{1,0:T(8,128)(2,1)S(1)}, u32[]{:S(2)}, u32[]{:S(2)}) collective-permute-start(bf16[16,2176]{1,0:T(8,128)(2,1)S(1)} %get-tuple-element.60.refs_3_.refs_0_), channel_id=1, source_target_pairs={{0,16},{2,18},{4,20},{6,22},{8,24},{10,26},{12,28},{14,30},{16,0},... | collective-permute-start | bytes 208904 | tf_op jit(solution)/shard_map/ppermute | solution.py:468
  19.3 6.2 %collective-permute-start.3 = (bf16[16,2176]{1,0:T(8,128)(2,1)S(1)}, bf16[16,2176]{1,0:T(8,128)(2,1)S(1)}, u32[]{:S(2)}, u32[]{:S(2)}) collective-permute-start(bf16[16,2176]{1,0:T(8,128)(2,1)S(1)} %get-tuple-element.60.refs_3_.refs_0_), channel_id=1, source_target_pairs={{0,24},{2,26},{4,28},{6,30},{8,16},{10,18},{12,20},{14,22},{16,8},... | collective-permute-start | bytes 208904 | tf_op jit(solution)/shard_map/ppermute | solution.py:468
  25.5 7.0 %collective-permute-start.4 = (bf16[64,2176]{1,0:T(8,128)(2,1)S(1)}, bf16[64,2176]{1,0:T(8,128)(2,1)S(1)}, u32[]{:S(2)}, u32[]{:S(2)}) collective-permute-start(bf16[64,2176]{1,0:T(8,128)(2,1)S(1)} %pack_tokens.1.refs_0_), channel_id=1, source_target_pairs={{0,2},{2,0},{4,6},{6,4},{8,10},{10,8},{12,14},{14,12},{16,18},{18,... | collective-permute-start | bytes 835592 | tf_op jit(solution)/shard_map/ppermute | solution.py:468
  27.1 6.6 %collective-permute-start.5 = (bf16[64,2176]{1,0:T(8,128)(2,1)S(1)}, bf16[64,2176]{1,0:T(8,128)(2,1)S(1)}, u32[]{:S(2)}, u32[]{:S(2)}) collective-permute-start(bf16[64,2176]{1,0:T(8,128)(2,1)S(1)} %pack_tokens.1.refs_0_), channel_id=1, source_target_pairs={{0,4},{2,6},{4,0},{6,2},{8,12},{10,14},{12,8},{14,10},{16,20},{18,... | collective-permute-start | bytes 835592 | tf_op jit(solution)/shard_map/ppermute | solution.py:468
  28.6 7.6 %collective-permute-start.6 = (bf16[64,2176]{1,0:T(8,128)(2,1)S(1)}, bf16[64,2176]{1,0:T(8,128)(2,1)S(1)}, u32[]{:S(2)}, u32[]{:S(2)}) collective-permute-start(bf16[64,2176]{1,0:T(8,128)(2,1)S(1)} %pack_tokens.1.refs_0_), channel_id=1, source_target_pairs={{0,1},{1,0},{2,3},{3,2},{4,5},{5,4},{6,7},{7,6},{8,9},{9,8},{10,11... | collective-permute-start | bytes 835592 | tf_op jit(solution)/shard_map/ppermute | solution.py:465
  32.5 3.7 %collective-permute-start.7 = (bf16[64,2176]{1,0:T(8,128)(2,1)S(1)}, bf16[64,2176]{1,0:T(8,128)(2,1)S(1)}, u32[]{:S(2)}, u32[]{:S(2)}) collective-permute-start(bf16[64,2176]{1,0:T(8,128)(2,1)S(1)} %collective-permute-done.4.refs_1_), channel_id=1, source_target_pairs={{0,1},{1,0},{2,3},{3,2},{4,5},{5,4},{6,7},{7,6},{8,9},{9,8},{10,11... | collective-permute-start | bytes 835592 | tf_op jit(solution)/shard_map/ppermute | solution.py:465
  33.7 6.5 %collective-permute-start.9 = (bf16[32,2176]{1,0:T(8,128)(2,1)S(1)}, bf16[32,2176]{1,0:T(8,128)(2,1)S(1)}, u32[]{:S(2)}, u32[]{:S(2)}) collective-permute-start(bf16[32,2176]{1,0:T(8,128)(2,1)S(1)} %slice.8), channel_id=1, source_target_pairs={{0,4},{2,6},{4,0},{6,2},{8,12},{10,14},{12,8},{14,10},{16,20},{18,... | collective-permute-start | bytes 417800 | tf_op jit(solution)/shard_map/ppermute | solution.py:468
  35.3 5.9 %collective-permute-start.10 = (bf16[32,2176]{1,0:T(8,128)(2,1)S(1)}, bf16[32,2176]{1,0:T(8,128)(2,1)S(1)}, u32[]{:S(2)}, u32[]{:S(2)}) collective-permute-start(bf16[32,2176]{1,0:T(8,128)(2,1)S(1)} %slice.9), channel_id=1, source_target_pairs={{0,2},{2,0},{4,6},{6,4},{8,10},{10,8},{12,14},{14,12},{16,18},{18,... | collective-permute-start | bytes 417800 | tf_op jit(solution)/shard_map/ppermute | solution.py:468
  41.7 3.4 %collective-permute-start.13 = (bf16[64,2048]{1,0:T(8,128)(2,1)S(1)}, bf16[64,2048]{1,0:T(8,128)(2,1)S(1)}, u32[]{:S(2)}, u32[]{:S(2)}) collective-permute-start(bf16[64,2048]{1,0:T(8,128)(2,1)S(1)} %get-tuple-element.72), channel_id=1, source_target_pairs={{0,1},{1,0},{2,3},{3,2},{4,5},{5,4},{6,7},{7,6},{8,9},{9,8},{10,11... | collective-permute-start | bytes 786440 | tf_op jit(solution)/shard_map/ppermute | solution.py:465
  41.7 3.4 %collective-permute-start.14 = (bf16[64,2048]{1,0:T(8,128)(2,1)S(1)}, bf16[64,2048]{1,0:T(8,128)(2,1)S(1)}, u32[]{:S(2)}, u32[]{:S(2)}) collective-permute-start(bf16[64,2048]{1,0:T(8,128)(2,1)S(1)} %get-tuple-element.73), channel_id=1, source_target_pairs={{0,1},{1,0},{2,3},{3,2},{4,5},{5,4},{6,7},{7,6},{8,9},{9,8},{10,11... | collective-permute-start | bytes 786440 | tf_op jit(solution)/shard_map/ppermute | solution.py:465
  46.6 9.2 %collective-permute-start.17 = (bf16[256,512]{1,0:T(8,128)(2,1)S(1)}, bf16[256,512]{1,0:T(8,128)(2,1)S(1)}, u32[]{:S(2)}, u32[]{:S(2)}) collective-permute-start(bf16[256,512]{1,0:T(8,128)(2,1)S(1)} %get-tuple-element.81), channel_id=1, source_target_pairs={{0,2},{2,0},{4,6},{6,4},{8,10},{10,8},{12,14},{14,12},{16,18},{18,... | collective-permute-start | bytes 786440 | tf_op jit(solution)/shard_map/ppermute | solution.py:468
  47.2 13.9 %collective-permute-start.18 = (bf16[256,512]{1,0:T(8,128)(2,1)S(1)}, bf16[256,512]{1,0:T(8,128)(2,1)S(1)}, u32[]{:S(2)}, u32[]{:S(2)}) collective-permute-start(bf16[256,512]{1,0:T(8,128)(2,1)S(1)} %get-tuple-element.82), channel_id=1, source_target_pairs={{0,4},{2,6},{4,0},{6,2},{8,12},{10,14},{12,8},{14,10},{16,20},{18,... | collective-permute-start | bytes 786440 | tf_op jit(solution)/shard_map/ppermute | solution.py:468
  47.7 13.3 %collective-permute-start.19 = (bf16[256,512]{1,0:T(8,128)(2,1)S(1)}, bf16[256,512]{1,0:T(8,128)(2,1)S(1)}, u32[]{:S(2)}, u32[]{:S(2)}) collective-permute-start(bf16[256,512]{1,0:T(8,128)(2,1)S(1)} %get-tuple-element.83), channel_id=1, source_target_pairs={{0,6},{2,4},{4,2},{6,0},{8,14},{10,12},{12,10},{14,8},{16,22},{18,... | collective-permute-start | bytes 786440 | tf_op jit(solution)/shard_map/ppermute | solution.py:468
  50.2 15.5 %collective-permute-start.24 = (bf16[128,512]{1,0:T(8,128)(2,1)S(1)}, bf16[128,512]{1,0:T(8,128)(2,1)S(1)}, u32[]{:S(2)}, u32[]{:S(2)}) collective-permute-start(bf16[128,512]{1,0:T(8,128)(2,1)S(1)} %copy-done.1), channel_id=1, source_target_pairs={{0,16},{2,18},{4,20},{6,22},{8,24},{10,26},{12,28},{14,30},{16,0},... | collective-permute-start | bytes 393224 | tf_op jit(solution)/shard_map/ppermute | solution.py:468
  52.7 13.7 %collective-permute-start.23 = (bf16[128,512]{1,0:T(8,128)(2,1)S(1)}, bf16[128,512]{1,0:T(8,128)(2,1)S(1)}, u32[]{:S(2)}, u32[]{:S(2)}) collective-permute-start(bf16[128,512]{1,0:T(8,128)(2,1)S(1)} %copy-done.1), channel_id=1, source_target_pairs={{0,8},{2,10},{4,12},{6,14},{8,0},{10,2},{12,4},{14,6},{16,24},{18,... | collective-permute-start | bytes 393224 | tf_op jit(solution)/shard_map/ppermute | solution.py:468
  61.2 9.8 %collective-permute-start.20 = (bf16[64,512]{1,0:T(8,128)(2,1)S(1)}, bf16[64,512]{1,0:T(8,128)(2,1)S(1)}, u32[]{:S(2)}, u32[]{:S(2)}) collective-permute-start(bf16[64,512]{1,0:T(8,128)(2,1)S(1)} %get-tuple-element.85.refs_2_), channel_id=1, source_target_pairs={{0,8},{2,10},{4,12},{6,14},{8,0},{10,2},{12,4},{14,6},{16,24},{18,... | collective-permute-start | bytes 196616 | tf_op jit(solution)/shard_map/ppermute | solution.py:468
  62.8 8.2 %collective-permute-start.21 = (bf16[64,512]{1,0:T(8,128)(2,1)S(1)}, bf16[64,512]{1,0:T(8,128)(2,1)S(1)}, u32[]{:S(2)}, u32[]{:S(2)}) collective-permute-start(bf16[64,512]{1,0:T(8,128)(2,1)S(1)} %get-tuple-element.86.refs_3_), channel_id=1, source_target_pairs={{0,16},{2,18},{4,20},{6,22},{8,24},{10,26},{12,28},{14,30},{16,0},... | collective-permute-start | bytes 196616 | tf_op jit(solution)/shard_map/ppermute | solution.py:468
  64.3 8.5 %collective-permute-start.22 = (bf16[64,512]{1,0:T(8,128)(2,1)S(1)}, bf16[64,512]{1,0:T(8,128)(2,1)S(1)}, u32[]{:S(2)}, u32[]{:S(2)}) collective-permute-start(bf16[64,512]{1,0:T(8,128)(2,1)S(1)} %get-tuple-element.87.refs_4_), channel_id=1, source_target_pairs={{0,24},{2,26},{4,28},{6,30},{8,16},{10,18},{12,20},{14,22},{16,8},... | collective-permute-start | bytes 196616 | tf_op jit(solution)/shard_map/ppermute | solution.py:468
  65.7 7.6 %collective-permute-start.26 = (bf16[128,512]{1,0:T(8,128)(2,1)S(1)}, bf16[128,512]{1,0:T(8,128)(2,1)S(1)}, u32[]{:S(2)}, u32[]{:S(2)}) collective-permute-start(bf16[128,512]{1,0:T(8,128)(2,1)S(1)} %collective-permute-done.24.refs_6_.refs_2_), channel_id=1, source_target_pairs={{0,8},{2,10},{4,12},{6,14},{8,0},{10,2},{12,4},{14,6},{16,24},{18,... | collective-permute-start | bytes 393224 | tf_op jit(solution)/shard_map/ppermute | solution.py:468
  74.8 7.6 %collective-permute-start.27 = (bf16[32,2944]{1,0:T(8,128)(2,1)S(1)}, bf16[32,2944]{1,0:T(8,128)(2,1)S(1)}, u32[]{:S(2)}, u32[]{:S(2)}) collective-permute-start(bf16[32,2944]{1,0:T(8,128)(2,1)S(1)} %get-tuple-element.98), channel_id=1, source_target_pairs={{0,2},{2,0},{4,6},{6,4},{8,10},{10,8},{12,14},{14,12},{16,18},{18,... | collective-permute-start | bytes 565256 | tf_op jit(solution)/shard_map/ppermute | solution.py:468
  76.4 10.5 %collective-permute-start.28 = (bf16[32,2944]{1,0:T(8,128)(2,1)S(1)}, bf16[32,2944]{1,0:T(8,128)(2,1)S(1)}, u32[]{:S(2)}, u32[]{:S(2)}) collective-permute-start(bf16[32,2944]{1,0:T(8,128)(2,1)S(1)} %get-tuple-element.99), channel_id=1, source_target_pairs={{0,4},{2,6},{4,0},{6,2},{8,12},{10,14},{12,8},{14,10},{16,20},{18,... | collective-permute-start | bytes 565256 | tf_op jit(solution)/shard_map/ppermute | solution.py:468
  77.9 9.1 %collective-permute-start.29 = (bf16[32,2944]{1,0:T(8,128)(2,1)S(1)}, bf16[32,2944]{1,0:T(8,128)(2,1)S(1)}, u32[]{:S(2)}, u32[]{:S(2)}) collective-permute-start(bf16[32,2944]{1,0:T(8,128)(2,1)S(1)} %get-tuple-element.100), channel_id=1, source_target_pairs={{0,6},{2,4},{4,2},{6,0},{8,14},{10,12},{12,10},{14,8},{16,22},{18,... | collective-permute-start | bytes 565256 | tf_op jit(solution)/shard_map/ppermute | solution.py:468
  (15 other events, 105.7 us)
Sparse Core Ops, SparseCore 0:
  13.8 55.5 all-gather.1

commit v20 on v19

--- a/solution.py
+++ b/solution.py
@@ -72,7 +72,7 @@
 def out_projection(attn_out, out_weight):
     rows, depth = attn_out.shape
     width = out_weight.shape[1]
-    chunk = 256
+    chunk = 512
     half = pltpu.VMEM((rows // 2, width), jnp.float32)
     return pl.pallas_call(
         functools.partial(out_projection_kernel, chunk),
@@ -493,7 +493,7 @@
     cut = near[0].shape[0] // 2
     one, two = near[1][:cut], near[2][cut:]
     far = [to_expert(one, 2), to_expert(two, 1)]
-    near_mine, *near_theirs = experts((*near, *map(to_core, near)), weights, depth, len(near))
+    near_mine, *near_theirs = experts((*near, *map(to_core, near)), weights, depth, 2)
     theirs = list(map(to_core, near_theirs))
     near_mine, *far = lax.optimization_barrier((near_mine, *far))
     far_both = [*far, *map(to_core, far)]

time: 94.9 us -> 94.5 us (level)
    ppermute x11 -> x10, waiting for transfers between devices: 3.2 us -> 3.23 us  [to_core(): return lax.ppermute(value, 'tensor', [(0, 1), (1, 0)])]
    ppermute x11 -> x10, starting transfers between devices: 2 us -> 1.99 us  [to_core(): return lax.ppermute(value, 'tensor', [(0, 1), (1, 0)])]
  transfers between devices with their start and end apart: 31 -> 30, of which waited for: 17 -> 17; matrix products, arithmetic and copies ran while one was open for 1% -> 1% of each run, Pallas kernels for 13% -> 13%
where the time goes in v20:
time: 94.5 us; the launch traced here: 94.4 us
  waiting for transfers between devices  33.2 us (35%)
  starting transfers between devices  28.3 us (30%)
  Pallas kernels  18 us (19%)
  between operations  14.2 us (15%)
    ppermute x19, waiting for transfers between devices, to_expert(): lax.ppermute(value, 'expert', [(i, i ^ offset) for i in range(n_expert)])  26.9 us
    ppermute x19, starting transfers between devices, to_expert(): lax.ppermute(value, 'expert', [(i, i ^ offset) for i in range(n_expert)])  26.3 us
    pallas_call x2, Pallas kernels, experts(): pl.pallas_call(functools.partial(expert_kernel, depth, chunk, len(blocks)...  6.05 us
    pallas_call x2, Pallas kernels, load(): pl.pallas_call(functools.partial(load_kernel, count), out_shape=tuple((pl...  5.45 us
    pallas_call x1, Pallas kernels, out_projection(): pl.pallas_call(functools.partial(out_projection_kernel, chunk), out_shape...  4.38 us
    ppermute x10, waiting for transfers between devices, to_core(): return lax.ppermute(value, 'tensor', [(0, 1), (1, 0)])  3.23 us
    all_gather x1, waiting for transfers between devices, per_device_dense(): lax.all_gather(q_own, 'expert', axis=0, tiled=True, axis_index_groups=lines)  3.05 us
    ppermute x10, starting transfers between devices, to_core(): return lax.ppermute(value, 'tensor', [(0, 1), (1, 0)])  1.99 us
  transfers between devices with their start and end apart: 30, of which 17 were waited for; matrix products, arithmetic and copies ran while one was open for 1% of the time, Pallas kernels for 13%

profile of v20, /device:TPU:0, one launch (start us, length us, event | category | flops | bytes accessed | tf_op | source)
XLA Modules:
  0.0 94.4 jit_solution(11208737401855057906)
XLA Ops:
  7.3 4.4 %out_projection.1 = (f32[16,2048]{1,0:T(8,128)S(1)}, f32[16,2048]{1,0:T(8,128)S(1)}) custom-call(bf16[32,2048]{1,0:T(8,128)(2,1)} %a_hbm.1, bf16[2048,2048]{1,0:T(8,128)(2,1)} %w_hbm.1), custom_call_target="tpu_custom_call" | custom-call | tf_op jit(solution)/shard_map/out_projection/pallas_call | solution.py:77
  13.3 3.0 %collective-permute-start.1 = (bf16[16,2176]{1,0:T(8,128)(2,1)S(1)}, bf16[16,2176]{1,0:T(8,128)(2,1)S(1)}, u32[]{:S(2)}, u32[]{:S(2)}) collective-permute-start(bf16[16,2176]{1,0:T(8,128)(2,1)S(1)} %get-tuple-element.59.refs_3_.refs_0_), channel_id=1, source_target_pairs={{0,8},{2,10},{4,12},{6,14},{8,0},{10,2},{12,4},{14,6},{16,24},{18,... | collective-permute-start | bytes 208904 | tf_op jit(solution)/shard_map/ppermute | solution.py:468
  16.3 2.6 %collective-permute-start.2 = (bf16[16,2176]{1,0:T(8,128)(2,1)S(1)}, bf16[16,2176]{1,0:T(8,128)(2,1)S(1)}, u32[]{:S(2)}, u32[]{:S(2)}) collective-permute-start(bf16[16,2176]{1,0:T(8,128)(2,1)S(1)} %get-tuple-element.59.refs_3_.refs_0_), channel_id=1, source_target_pairs={{0,16},{2,18},{4,20},{6,22},{8,24},{10,26},{12,28},{14,30},{16,0},... | collective-permute-start | bytes 208904 | tf_op jit(solution)/shard_map/ppermute | solution.py:468
  18.9 3.8 %load_weights.2 = (bf16[1,2048,768]{2,1,0:T(8,128)(2,1)S(1)}, bf16[1,2048,768]{2,1,0:T(8,128)(2,1)S(1)}, bf16[1,768,2048]{2,1,0:T(8,128)(2,1)S(1)}) custom-call(bf16[1,2048,768]{2,1,0:T(8,128)(2,1)} %refs_0_.1, bf16[1,2048,768]{2,1,0:T(8,128)(2,1)} %refs_1_.1, bf16[1,768,2048]{2,1,0:T(8,128)(2,1)} %refs_2_.1, ...), custom_call_target="tpu_custom_call" | custom-call | tf_op jit(solution)/shard_map/load_weights/pallas_call | solution.py:153
  25.1 1.6 %collective-permute-start.4 = (bf16[64,2176]{1,0:T(8,128)(2,1)S(1)}, bf16[64,2176]{1,0:T(8,128)(2,1)S(1)}, u32[]{:S(2)}, u32[]{:S(2)}) collective-permute-start(bf16[64,2176]{1,0:T(8,128)(2,1)S(1)} %pack_tokens.1.refs_0_), channel_id=1, source_target_pairs={{0,2},{2,0},{4,6},{6,4},{8,10},{10,8},{12,14},{14,12},{16,18},{18,... | collective-permute-start | bytes 835592 | tf_op jit(solution)/shard_map/ppermute | solution.py:468
  26.7 1.5 %collective-permute-start.5 = (bf16[64,2176]{1,0:T(8,128)(2,1)S(1)}, bf16[64,2176]{1,0:T(8,128)(2,1)S(1)}, u32[]{:S(2)}, u32[]{:S(2)}) collective-permute-start(bf16[64,2176]{1,0:T(8,128)(2,1)S(1)} %pack_tokens.1.refs_0_), channel_id=1, source_target_pairs={{0,4},{2,6},{4,0},{6,2},{8,12},{10,14},{12,8},{14,10},{16,20},{18,... | collective-permute-start | bytes 835592 | tf_op jit(solution)/shard_map/ppermute | solution.py:468
  28.2 3.9 %collective-permute-done.4.refs_1_ = bf16[64,2176]{1,0:T(8,128)(2,1)S(1)} collective-permute-done((bf16[64,2176]{1,0:T(8,128)(2,1)S(1)}, bf16[64,2176]{1,0:T(8,128)(2,1)S(1)}, u32[]{:S(2)}, u32[]{:S(2)}) %collective-permute-start.4) | collective-permute-done | bytes 278560 | tf_op jit(solution)/shard_map/ppermute | solution.py:468
  33.3 1.6 %collective-permute-start.9 = (bf16[32,2176]{1,0:T(8,128)(2,1)S(1)}, bf16[32,2176]{1,0:T(8,128)(2,1)S(1)}, u32[]{:S(2)}, u32[]{:S(2)}) collective-permute-start(bf16[32,2176]{1,0:T(8,128)(2,1)S(1)} %slice.8), channel_id=1, source_target_pairs={{0,4},{2,6},{4,0},{6,2},{8,12},{10,14},{12,8},{14,10},{16,20},{18,... | collective-permute-start | bytes 417800 | tf_op jit(solution)/shard_map/ppermute | solution.py:468
  35.8 4.0 %experts.2 = (bf16[192,2048]{1,0:T(8,128)(2,1)S(1)}, bf16[96,2048]{1,0:T(8,128)(2,1)S(1)}, bf16[96,2048]{1,0:T(8,128)(2,1)S(1)}) custom-call(bf16[64,2176]{1,0:T(8,128)(2,1)S(1)} %pack_tokens.1.refs_0_, bf16[64,2176]{1,0:T(8,128)(2,1)S(1)} %collective-permute-done.4.refs_1_, bf16[64,2176]{1,0:T(8,128)(2,1)S(1)} %collective-permute-done.5.refs_2_, ...), custom_call_target="tpu_custom_call" | custom-call | flops 3623878656 | tf_op jit(solution)/shard_map/experts/pallas_call | solution.py:213
  42.4 2.0 %experts.3 = (bf16[64,2048]{1,0:T(8,128)(2,1)S(1)}, bf16[64,2048]{1,0:T(8,128)(2,1)S(1)}) custom-call(bf16[32,2176]{1,0:T(8,128)(2,1)S(1)} %collective-permute-done.9.refs_0_, bf16[32,2176]{1,0:T(8,128)(2,1)S(1)} %collective-permute-done.10.refs_1_, bf16[32,2176]{1,0:T(8,128)(2,1)S(1)} %collective-permute-done.11.refs_2_, ...), custom_call_target="tpu_custom_call" | custom-call | flops 1207959552 | tf_op jit(solution)/shard_map/experts/pallas_call | solution.py:213
  47.4 2.4 %collective-permute-start.18 = (bf16[256,512]{1,0:T(8,128)(2,1)S(1)}, bf16[256,512]{1,0:T(8,128)(2,1)S(1)}, u32[]{:S(2)}, u32[]{:S(2)}) collective-permute-start(bf16[256,512]{1,0:T(8,128)(2,1)S(1)} %get-tuple-element.81), channel_id=1, source_target_pairs={{0,6},{2,4},{4,2},{6,0},{8,14},{10,12},{12,10},{14,8},{16,22},{18,... | collective-permute-start | bytes 786440 | tf_op jit(solution)/shard_map/ppermute | solution.py:468
  49.8 2.5 %collective-permute-start.23 = (bf16[128,512]{1,0:T(8,128)(2,1)S(1)}, bf16[128,512]{1,0:T(8,128)(2,1)S(1)}, u32[]{:S(2)}, u32[]{:S(2)}) collective-permute-start(bf16[128,512]{1,0:T(8,128)(2,1)S(1)} %copy-done.1), channel_id=1, source_target_pairs={{0,16},{2,18},{4,20},{6,22},{8,24},{10,26},{12,28},{14,30},{16,0},... | collective-permute-start | bytes 393224 | tf_op jit(solution)/shard_map/ppermute | solution.py:468
  52.8 2.7 %collective-permute-done.16.refs_1_ = bf16[256,512]{1,0:T(8,128)(2,1)S(1)} collective-permute-done((bf16[256,512]{1,0:T(8,128)(2,1)S(1)}, bf16[256,512]{1,0:T(8,128)(2,1)S(1)}, u32[]{:S(2)}, u32[]{:S(2)}) %collective-permute-start.16) | collective-permute-done | bytes 262176 | tf_op jit(solution)/shard_map/ppermute | solution.py:468
  55.4 5.3 %collective-permute-done.17.refs_2_ = bf16[256,512]{1,0:T(8,128)(2,1)S(1)} collective-permute-done((bf16[256,512]{1,0:T(8,128)(2,1)S(1)}, bf16[256,512]{1,0:T(8,128)(2,1)S(1)}, u32[]{:S(2)}, u32[]{:S(2)}) %collective-permute-start.17) | collective-permute-done | bytes 262176 | tf_op jit(solution)/shard_map/ppermute | solution.py:468
  60.8 1.6 %collective-permute-start.19 = (bf16[64,512]{1,0:T(8,128)(2,1)S(1)}, bf16[64,512]{1,0:T(8,128)(2,1)S(1)}, u32[]{:S(2)}, u32[]{:S(2)}) collective-permute-start(bf16[64,512]{1,0:T(8,128)(2,1)S(1)} %get-tuple-element.83.refs_2_), channel_id=1, source_target_pairs={{0,8},{2,10},{4,12},{6,14},{8,0},{10,2},{12,4},{14,6},{16,24},{18,... | collective-permute-start | bytes 196616 | tf_op jit(solution)/shard_map/ppermute | solution.py:468
  62.5 1.4 %collective-permute-start.20 = (bf16[64,512]{1,0:T(8,128)(2,1)S(1)}, bf16[64,512]{1,0:T(8,128)(2,1)S(1)}, u32[]{:S(2)}, u32[]{:S(2)}) collective-permute-start(bf16[64,512]{1,0:T(8,128)(2,1)S(1)} %get-tuple-element.84.refs_3_), channel_id=1, source_target_pairs={{0,16},{2,18},{4,20},{6,22},{8,24},{10,26},{12,28},{14,30},{16,0},... | collective-permute-start | bytes 196616 | tf_op jit(solution)/shard_map/ppermute | solution.py:468
  63.9 1.4 %collective-permute-start.21 = (bf16[64,512]{1,0:T(8,128)(2,1)S(1)}, bf16[64,512]{1,0:T(8,128)(2,1)S(1)}, u32[]{:S(2)}, u32[]{:S(2)}) collective-permute-start(bf16[64,512]{1,0:T(8,128)(2,1)S(1)} %get-tuple-element.85.refs_4_), channel_id=1, source_target_pairs={{0,24},{2,26},{4,28},{6,30},{8,16},{10,18},{12,20},{14,22},{16,8},... | collective-permute-start | bytes 196616 | tf_op jit(solution)/shard_map/ppermute | solution.py:468
  65.9 3.1 %all-gather.2.cloned.1.call-done.refs_0_ = bf16[512,2048]{1,0:T(8,128)(2,1)} async-done(((bf16[128,2048]{1,0:T(8,128)(2,1)}), bf16[512,2048]{1,0:T(8,128)(2,1)}) %all-gather.2.cloned.1.call-update) | async-done | bytes 2097168 | tf_op jit(solution)/shard_map/all_gather | solution.py:487
  69.0 1.6 %load_weights.3.q_ref = bf16[512,2048]{1,0:T(8,128)(2,1)S(1)} custom-call(bf16[512,2048]{1,0:T(8,128)(2,1)} %all-gather.2.cloned.1.call-done.refs_0_, bf16[64,512]{1,0:T(8,128)(2,1)S(1)} %get-tuple-element.88.refs_1_.refs_0_, bf16[64,512]{1,0:T(8,128)(2,1)S(1)} %get-tuple-element.83.refs_2_, bf16[64,512]{1,0:T(8,128)(2,1)S(1)} %get-tuple-element.84.refs_3_, ...), custom_call_target="tpu_custom_call" | custom-call | tf_op jit(solution)/shard_map/load_weights/pallas_call | solution.py:153
  70.7 1.7 %collective-permute-done.21.refs_3_ = bf16[64,512]{1,0:T(8,128)(2,1)S(1)} collective-permute-done((bf16[64,512]{1,0:T(8,128)(2,1)S(1)}, bf16[64,512]{1,0:T(8,128)(2,1)S(1)}, u32[]{:S(2)}, u32[]{:S(2)}) %collective-permute-start.21) | collective-permute-done | bytes 65568 | tf_op jit(solution)/shard_map/ppermute | solution.py:468
  74.4 1.6 %collective-permute-start.26 = (bf16[32,2944]{1,0:T(8,128)(2,1)S(1)}, bf16[32,2944]{1,0:T(8,128)(2,1)S(1)}, u32[]{:S(2)}, u32[]{:S(2)}) collective-permute-start(bf16[32,2944]{1,0:T(8,128)(2,1)S(1)} %get-tuple-element.96), channel_id=1, source_target_pairs={{0,2},{2,0},{4,6},{6,4},{8,10},{10,8},{12,14},{14,12},{16,18},{18,... | collective-permute-start | bytes 565256 | tf_op jit(solution)/shard_map/ppermute | solution.py:468
  76.0 1.4 %collective-permute-start.27 = (bf16[32,2944]{1,0:T(8,128)(2,1)S(1)}, bf16[32,2944]{1,0:T(8,128)(2,1)S(1)}, u32[]{:S(2)}, u32[]{:S(2)}) collective-permute-start(bf16[32,2944]{1,0:T(8,128)(2,1)S(1)} %get-tuple-element.97), channel_id=1, source_target_pairs={{0,4},{2,6},{4,0},{6,2},{8,12},{10,14},{12,8},{14,10},{16,20},{18,... | collective-permute-start | bytes 565256 | tf_op jit(solution)/shard_map/ppermute | solution.py:468
  78.0 4.1 %collective-permute-done.26.refs_1_ = bf16[32,2944]{1,0:T(8,128)(2,1)S(1)} collective-permute-done((bf16[32,2944]{1,0:T(8,128)(2,1)S(1)}, bf16[32,2944]{1,0:T(8,128)(2,1)S(1)}, u32[]{:S(2)}, u32[]{:S(2)}) %collective-permute-start.26) | collective-permute-done | bytes 188448 | tf_op jit(solution)/shard_map/ppermute | solution.py:468
  82.0 4.5 %collective-permute-done.27.refs_2_ = bf16[32,2944]{1,0:T(8,128)(2,1)S(1)} collective-permute-done((bf16[32,2944]{1,0:T(8,128)(2,1)S(1)}, bf16[32,2944]{1,0:T(8,128)(2,1)S(1)}, u32[]{:S(2)}, u32[]{:S(2)}) %collective-permute-start.27) | collective-permute-done | bytes 188448 | tf_op jit(solution)/shard_map/ppermute | solution.py:468
  (74 shorter events, 16.4 us)
Async XLA Ops:
  7.2 61.8 %all-gather.2.cloned.1.call-start = ((), (), s32[]{:S(2)}) async-start(), calls=%async_computation | async-start | bytes 2621440 | tf_op jit(solution)/shard_map/all_gather | solution.py:487
  13.3 9.4 %collective-permute-start.1 = (bf16[16,2176]{1,0:T(8,128)(2,1)S(1)}, bf16[16,2176]{1,0:T(8,128)(2,1)S(1)}, u32[]{:S(2)}, u32[]{:S(2)}) collective-permute-start(bf16[16,2176]{1,0:T(8,128)(2,1)S(1)} %get-tuple-element.59.refs_3_.refs_0_), channel_id=1, source_target_pairs={{0,8},{2,10},{4,12},{6,14},{8,0},{10,2},{12,4},{14,6},{16,24},{18,... | collective-permute-start | bytes 208904 | tf_op jit(solution)/shard_map/ppermute | solution.py:468
  16.3 7.8 %collective-permute-start.2 = (bf16[16,2176]{1,0:T(8,128)(2,1)S(1)}, bf16[16,2176]{1,0:T(8,128)(2,1)S(1)}, u32[]{:S(2)}, u32[]{:S(2)}) collective-permute-start(bf16[16,2176]{1,0:T(8,128)(2,1)S(1)} %get-tuple-element.59.refs_3_.refs_0_), channel_id=1, source_target_pairs={{0,16},{2,18},{4,20},{6,22},{8,24},{10,26},{12,28},{14,30},{16,0},... | collective-permute-start | bytes 208904 | tf_op jit(solution)/shard_map/ppermute | solution.py:468
  18.9 6.2 %collective-permute-start.3 = (bf16[16,2176]{1,0:T(8,128)(2,1)S(1)}, bf16[16,2176]{1,0:T(8,128)(2,1)S(1)}, u32[]{:S(2)}, u32[]{:S(2)}) collective-permute-start(bf16[16,2176]{1,0:T(8,128)(2,1)S(1)} %get-tuple-element.59.refs_3_.refs_0_), channel_id=1, source_target_pairs={{0,24},{2,26},{4,28},{6,30},{8,16},{10,18},{12,20},{14,22},{16,8},... | collective-permute-start | bytes 208904 | tf_op jit(solution)/shard_map/ppermute | solution.py:468
  25.1 7.0 %collective-permute-start.4 = (bf16[64,2176]{1,0:T(8,128)(2,1)S(1)}, bf16[64,2176]{1,0:T(8,128)(2,1)S(1)}, u32[]{:S(2)}, u32[]{:S(2)}) collective-permute-start(bf16[64,2176]{1,0:T(8,128)(2,1)S(1)} %pack_tokens.1.refs_0_), channel_id=1, source_target_pairs={{0,2},{2,0},{4,6},{6,4},{8,10},{10,8},{12,14},{14,12},{16,18},{18,... | collective-permute-start | bytes 835592 | tf_op jit(solution)/shard_map/ppermute | solution.py:468
  26.7 6.6 %collective-permute-start.5 = (bf16[64,2176]{1,0:T(8,128)(2,1)S(1)}, bf16[64,2176]{1,0:T(8,128)(2,1)S(1)}, u32[]{:S(2)}, u32[]{:S(2)}) collective-permute-start(bf16[64,2176]{1,0:T(8,128)(2,1)S(1)} %pack_tokens.1.refs_0_), channel_id=1, source_target_pairs={{0,4},{2,6},{4,0},{6,2},{8,12},{10,14},{12,8},{14,10},{16,20},{18,... | collective-permute-start | bytes 835592 | tf_op jit(solution)/shard_map/ppermute | solution.py:468
  28.2 7.6 %collective-permute-start.6 = (bf16[64,2176]{1,0:T(8,128)(2,1)S(1)}, bf16[64,2176]{1,0:T(8,128)(2,1)S(1)}, u32[]{:S(2)}, u32[]{:S(2)}) collective-permute-start(bf16[64,2176]{1,0:T(8,128)(2,1)S(1)} %pack_tokens.1.refs_0_), channel_id=1, source_target_pairs={{0,1},{1,0},{2,3},{3,2},{4,5},{5,4},{6,7},{7,6},{8,9},{9,8},{10,11... | collective-permute-start | bytes 835592 | tf_op jit(solution)/shard_map/ppermute | solution.py:465
  32.1 3.7 %collective-permute-start.7 = (bf16[64,2176]{1,0:T(8,128)(2,1)S(1)}, bf16[64,2176]{1,0:T(8,128)(2,1)S(1)}, u32[]{:S(2)}, u32[]{:S(2)}) collective-permute-start(bf16[64,2176]{1,0:T(8,128)(2,1)S(1)} %collective-permute-done.4.refs_1_), channel_id=1, source_target_pairs={{0,1},{1,0},{2,3},{3,2},{4,5},{5,4},{6,7},{7,6},{8,9},{9,8},{10,11... | collective-permute-start | bytes 835592 | tf_op jit(solution)/shard_map/ppermute | solution.py:465
  33.3 6.5 %collective-permute-start.9 = (bf16[32,2176]{1,0:T(8,128)(2,1)S(1)}, bf16[32,2176]{1,0:T(8,128)(2,1)S(1)}, u32[]{:S(2)}, u32[]{:S(2)}) collective-permute-start(bf16[32,2176]{1,0:T(8,128)(2,1)S(1)} %slice.8), channel_id=1, source_target_pairs={{0,4},{2,6},{4,0},{6,2},{8,12},{10,14},{12,8},{14,10},{16,20},{18,... | collective-permute-start | bytes 417800 | tf_op jit(solution)/shard_map/ppermute | solution.py:468
  34.9 5.9 %collective-permute-start.10 = (bf16[32,2176]{1,0:T(8,128)(2,1)S(1)}, bf16[32,2176]{1,0:T(8,128)(2,1)S(1)}, u32[]{:S(2)}, u32[]{:S(2)}) collective-permute-start(bf16[32,2176]{1,0:T(8,128)(2,1)S(1)} %slice.9), channel_id=1, source_target_pairs={{0,2},{2,0},{4,6},{6,4},{8,10},{10,8},{12,14},{14,12},{16,18},{18,... | collective-permute-start | bytes 417800 | tf_op jit(solution)/shard_map/ppermute | solution.py:468
  41.3 3.4 %collective-permute-start.13 = (bf16[96,2048]{1,0:T(8,128)(2,1)S(1)}, bf16[96,2048]{1,0:T(8,128)(2,1)S(1)}, u32[]{:S(2)}, u32[]{:S(2)}) collective-permute-start(bf16[96,2048]{1,0:T(8,128)(2,1)S(1)} %get-tuple-element.71), channel_id=1, source_target_pairs={{0,1},{1,0},{2,3},{3,2},{4,5},{5,4},{6,7},{7,6},{8,9},{9,8},{10,11... | collective-permute-start | bytes 1179656 | tf_op jit(solution)/shard_map/ppermute | solution.py:465
  41.3 3.4 %collective-permute-start.14 = (bf16[96,2048]{1,0:T(8,128)(2,1)S(1)}, bf16[96,2048]{1,0:T(8,128)(2,1)S(1)}, u32[]{:S(2)}, u32[]{:S(2)}) collective-permute-start(bf16[96,2048]{1,0:T(8,128)(2,1)S(1)} %get-tuple-element.72), channel_id=1, source_target_pairs={{0,1},{1,0},{2,3},{3,2},{4,5},{5,4},{6,7},{7,6},{8,9},{9,8},{10,11... | collective-permute-start | bytes 1179656 | tf_op jit(solution)/shard_map/ppermute | solution.py:465
  46.2 9.2 %collective-permute-start.16 = (bf16[256,512]{1,0:T(8,128)(2,1)S(1)}, bf16[256,512]{1,0:T(8,128)(2,1)S(1)}, u32[]{:S(2)}, u32[]{:S(2)}) collective-permute-start(bf16[256,512]{1,0:T(8,128)(2,1)S(1)} %get-tuple-element.79), channel_id=1, source_target_pairs={{0,2},{2,0},{4,6},{6,4},{8,10},{10,8},{12,14},{14,12},{16,18},{18,... | collective-permute-start | bytes 786440 | tf_op jit(solution)/shard_map/ppermute | solution.py:468
  46.8 13.9 %collective-permute-start.17 = (bf16[256,512]{1,0:T(8,128)(2,1)S(1)}, bf16[256,512]{1,0:T(8,128)(2,1)S(1)}, u32[]{:S(2)}, u32[]{:S(2)}) collective-permute-start(bf16[256,512]{1,0:T(8,128)(2,1)S(1)} %get-tuple-element.80), channel_id=1, source_target_pairs={{0,4},{2,6},{4,0},{6,2},{8,12},{10,14},{12,8},{14,10},{16,20},{18,... | collective-permute-start | bytes 786440 | tf_op jit(solution)/shard_map/ppermute | solution.py:468
  47.4 13.3 %collective-permute-start.18 = (bf16[256,512]{1,0:T(8,128)(2,1)S(1)}, bf16[256,512]{1,0:T(8,128)(2,1)S(1)}, u32[]{:S(2)}, u32[]{:S(2)}) collective-permute-start(bf16[256,512]{1,0:T(8,128)(2,1)S(1)} %get-tuple-element.81), channel_id=1, source_target_pairs={{0,6},{2,4},{4,2},{6,0},{8,14},{10,12},{12,10},{14,8},{16,22},{18,... | collective-permute-start | bytes 786440 | tf_op jit(solution)/shard_map/ppermute | solution.py:468
  49.8 15.5 %collective-permute-start.23 = (bf16[128,512]{1,0:T(8,128)(2,1)S(1)}, bf16[128,512]{1,0:T(8,128)(2,1)S(1)}, u32[]{:S(2)}, u32[]{:S(2)}) collective-permute-start(bf16[128,512]{1,0:T(8,128)(2,1)S(1)} %copy-done.1), channel_id=1, source_target_pairs={{0,16},{2,18},{4,20},{6,22},{8,24},{10,26},{12,28},{14,30},{16,0},... | collective-permute-start | bytes 393224 | tf_op jit(solution)/shard_map/ppermute | solution.py:468
  52.3 13.7 %collective-permute-start.22 = (bf16[128,512]{1,0:T(8,128)(2,1)S(1)}, bf16[128,512]{1,0:T(8,128)(2,1)S(1)}, u32[]{:S(2)}, u32[]{:S(2)}) collective-permute-start(bf16[128,512]{1,0:T(8,128)(2,1)S(1)} %copy-done.1), channel_id=1, source_target_pairs={{0,8},{2,10},{4,12},{6,14},{8,0},{10,2},{12,4},{14,6},{16,24},{18,... | collective-permute-start | bytes 393224 | tf_op jit(solution)/shard_map/ppermute | solution.py:468
  60.8 9.8 %collective-permute-start.19 = (bf16[64,512]{1,0:T(8,128)(2,1)S(1)}, bf16[64,512]{1,0:T(8,128)(2,1)S(1)}, u32[]{:S(2)}, u32[]{:S(2)}) collective-permute-start(bf16[64,512]{1,0:T(8,128)(2,1)S(1)} %get-tuple-element.83.refs_2_), channel_id=1, source_target_pairs={{0,8},{2,10},{4,12},{6,14},{8,0},{10,2},{12,4},{14,6},{16,24},{18,... | collective-permute-start | bytes 196616 | tf_op jit(solution)/shard_map/ppermute | solution.py:468
  62.5 8.2 %collective-permute-start.20 = (bf16[64,512]{1,0:T(8,128)(2,1)S(1)}, bf16[64,512]{1,0:T(8,128)(2,1)S(1)}, u32[]{:S(2)}, u32[]{:S(2)}) collective-permute-start(bf16[64,512]{1,0:T(8,128)(2,1)S(1)} %get-tuple-element.84.refs_3_), channel_id=1, source_target_pairs={{0,16},{2,18},{4,20},{6,22},{8,24},{10,26},{12,28},{14,30},{16,0},... | collective-permute-start | bytes 196616 | tf_op jit(solution)/shard_map/ppermute | solution.py:468
  63.9 8.5 %collective-permute-start.21 = (bf16[64,512]{1,0:T(8,128)(2,1)S(1)}, bf16[64,512]{1,0:T(8,128)(2,1)S(1)}, u32[]{:S(2)}, u32[]{:S(2)}) collective-permute-start(bf16[64,512]{1,0:T(8,128)(2,1)S(1)} %get-tuple-element.85.refs_4_), channel_id=1, source_target_pairs={{0,24},{2,26},{4,28},{6,30},{8,16},{10,18},{12,20},{14,22},{16,8},... | collective-permute-start | bytes 196616 | tf_op jit(solution)/shard_map/ppermute | solution.py:468
  65.3 7.6 %collective-permute-start.25 = (bf16[128,512]{1,0:T(8,128)(2,1)S(1)}, bf16[128,512]{1,0:T(8,128)(2,1)S(1)}, u32[]{:S(2)}, u32[]{:S(2)}) collective-permute-start(bf16[128,512]{1,0:T(8,128)(2,1)S(1)} %collective-permute-done.23.refs_6_.refs_2_), channel_id=1, source_target_pairs={{0,8},{2,10},{4,12},{6,14},{8,0},{10,2},{12,4},{14,6},{16,24},{18,... | collective-permute-start | bytes 393224 | tf_op jit(solution)/shard_map/ppermute | solution.py:468
  74.4 7.6 %collective-permute-start.26 = (bf16[32,2944]{1,0:T(8,128)(2,1)S(1)}, bf16[32,2944]{1,0:T(8,128)(2,1)S(1)}, u32[]{:S(2)}, u32[]{:S(2)}) collective-permute-start(bf16[32,2944]{1,0:T(8,128)(2,1)S(1)} %get-tuple-element.96), channel_id=1, source_target_pairs={{0,2},{2,0},{4,6},{6,4},{8,10},{10,8},{12,14},{14,12},{16,18},{18,... | collective-permute-start | bytes 565256 | tf_op jit(solution)/shard_map/ppermute | solution.py:468
  76.0 10.5 %collective-permute-start.27 = (bf16[32,2944]{1,0:T(8,128)(2,1)S(1)}, bf16[32,2944]{1,0:T(8,128)(2,1)S(1)}, u32[]{:S(2)}, u32[]{:S(2)}) collective-permute-start(bf16[32,2944]{1,0:T(8,128)(2,1)S(1)} %get-tuple-element.97), channel_id=1, source_target_pairs={{0,4},{2,6},{4,0},{6,2},{8,12},{10,14},{12,8},{14,10},{16,20},{18,... | collective-permute-start | bytes 565256 | tf_op jit(solution)/shard_map/ppermute | solution.py:468
  77.5 9.1 %collective-permute-start.28 = (bf16[32,2944]{1,0:T(8,128)(2,1)S(1)}, bf16[32,2944]{1,0:T(8,128)(2,1)S(1)}, u32[]{:S(2)}, u32[]{:S(2)}) collective-permute-start(bf16[32,2944]{1,0:T(8,128)(2,1)S(1)} %get-tuple-element.98), channel_id=1, source_target_pairs={{0,6},{2,4},{4,2},{6,0},{8,14},{10,12},{12,10},{14,8},{16,22},{18,... | collective-permute-start | bytes 565256 | tf_op jit(solution)/shard_map/ppermute | solution.py:468
  (14 other events, 101.7 us)
Sparse Core Ops, SparseCore 0:
  13.4 55.5 all-gather.1

commit v21 on v20

--- a/solution.py
+++ b/solution.py
@@ -26,6 +26,10 @@
 
 def params(mebibytes):
     return pltpu.CompilerParams(vmem_limit_bytes=mebibytes << 20)
+
+
+def far_first(values):
+    return [values[0], *reversed(values[1:])]
 
 
 def lanes(start, size):
@@ -117,7 +121,7 @@
 
 
 def pack_kernel(depth, *refs):
-    line, out_ref = refs[:depth], refs[depth]
+    line, out_ref = far_first(refs[:depth]), refs[depth]
     rows = line[0].shape[0]
     for z in range(depth):
         out_ref[z * rows : (z + 1) * rows, :] = line[z][...]
@@ -133,7 +137,7 @@
         out_specs=VMEM,
         compiler_params=params(2),
         name="pack_tokens",
-    )(*line)
+    )(*far_first(line))
 
 
 def load_kernel(count, *refs):
@@ -330,7 +334,7 @@
         out_specs=(VMEM, VMEM),
         compiler_params=params(4),
         name="second_norm",
-    )(*parts, gain)
+    )(*far_first(parts), gain)
 
 
 def projection_kernel(chunk, mine_ref, theirs_ref, next_ref, q_ref, *refs):
@@ -487,8 +491,8 @@
     q_rows = lax.all_gather(q_own, "expert", axis=0, tiled=True, axis_index_groups=lines)
     weights = load((w_gate, w_up, w_down), (tokens,))
     line = to_z([tokens] * depth)
-    *line, gate, up, down = lax.optimization_barrier((*line, *weights))
-    weights = (gate, up, down)
+    tied = lax.optimization_barrier((*far_first(line), *weights))
+    line, weights = far_first(tied[:depth]), tied[depth:]
     near = to_plane([pack(line)] * (PLANE - 1))
     cut = near[0].shape[0] // 2
     one, two = near[1][:cut], near[2][cut:]
@@ -506,7 +510,8 @@
     kv_rows.append(to_expert(kv_rows[2], PLANE))
     (q_rows,) = load((q_rows,), (*parts, *kv_rows[1:3]))
     parts = to_z(parts)
-    *parts, q_rows = lax.optimization_barrier((*parts, q_rows))
+    *parts, q_rows = lax.optimization_barrier((*far_first(parts), q_rows))
+    parts = far_first(parts)
     scaled, following = second_norm(parts, input_gain[None, :])
     products = to_plane(projection(scaled, to_core(scaled), following, q_rows, kv_rows))
     return head_norm(

time: 94.5 us -> 96.2 us (1.018)
  waiting for transfers between devices: 33.2 us -> 34.9 us
    all_gather x1, waiting for transfers between devices: 3.05 us -> 5.78 us  [per_device_dense(): lax.all_gather(q_own, 'expert', axis=0, tiled=True, axis_index_groups=lines)]
    ppermute x19, waiting for transfers between devices: 26.9 us -> 25.8 us  [to_expert(): lax.ppermute(value, 'expert', [(i, i ^ offset) for i in range(n_expert)])]
  transfers between devices with their start and end apart: 30 -> 30, of which waited for: 17 -> 15; matrix products, arithmetic and copies ran while one was open for 1% -> 1% of each run, Pallas kernels for 13% -> 13%
where the time goes in v21:
time: 96.2 us; the launch traced here: 96.1 us
  waiting for transfers between devices  34.9 us (36%)
  starting transfers between devices  28.3 us (29%)
  Pallas kernels  18 us (19%)
  between operations  14.3 us (15%)
    ppermute x19, starting transfers between devices, to_expert(): lax.ppermute(value, 'expert', [(i, i ^ offset) for i in range(n_expert)])  26.3 us
    ppermute x19, waiting for transfers between devices, to_expert(): lax.ppermute(value, 'expert', [(i, i ^ offset) for i in range(n_expert)])  25.8 us
    pallas_call x2, Pallas kernels, experts(): pl.pallas_call(functools.partial(expert_kernel, depth, chunk, len(blocks)...  6.05 us
    all_gather x1, waiting for transfers between devices, per_device_dense(): lax.all_gather(q_own, 'expert', axis=0, tiled=True, axis_index_groups=lines)  5.78 us
    pallas_call x2, Pallas kernels, load(): pl.pallas_call(functools.partial(load_kernel, count), out_shape=tuple((pl...  5.46 us
    pallas_call x1, Pallas kernels, out_projection(): pl.pallas_call(functools.partial(out_projection_kernel, chunk), out_shape...  4.38 us
    ppermute x10, waiting for transfers between devices, to_core(): return lax.ppermute(value, 'tensor', [(0, 1), (1, 0)])  3.35 us
    ppermute x10, starting transfers between devices, to_core(): return lax.ppermute(value, 'tensor', [(0, 1), (1, 0)])  1.99 us
  transfers between devices with their start and end apart: 30, of which 15 were waited for; matrix products, arithmetic and copies ran while one was open for 1% of the time, Pallas kernels for 13%

profile of v21, /device:TPU:0, one launch (start us, length us, event | category | flops | bytes accessed | tf_op | source)
XLA Modules:
  0.0 96.1 jit_solution(17294929889055857203)
XLA Ops:
  7.3 4.4 %out_projection.1 = (f32[16,2048]{1,0:T(8,128)S(1)}, f32[16,2048]{1,0:T(8,128)S(1)}) custom-call(bf16[32,2048]{1,0:T(8,128)(2,1)} %a_hbm.1, bf16[2048,2048]{1,0:T(8,128)(2,1)} %w_hbm.1), custom_call_target="tpu_custom_call" | custom-call | tf_op jit(solution)/shard_map/out_projection/pallas_call | solution.py:81
  13.3 5.0 %collective-permute-start.1 = (bf16[16,2176]{1,0:T(8,128)(2,1)S(1)}, bf16[16,2176]{1,0:T(8,128)(2,1)S(1)}, u32[]{:S(2)}, u32[]{:S(2)}) collective-permute-start(bf16[16,2176]{1,0:T(8,128)(2,1)S(1)} %get-tuple-element.59.refs_3_.refs_0_), channel_id=1, source_target_pairs={{0,24},{2,26},{4,28},{6,30},{8,16},{10,18},{12,20},{14,22},{16,8},... | collective-permute-start | bytes 208904 | tf_op jit(solution)/shard_map/ppermute | solution.py:472
  19.0 3.8 %load_weights.2 = (bf16[1,2048,768]{2,1,0:T(8,128)(2,1)S(1)}, bf16[1,2048,768]{2,1,0:T(8,128)(2,1)S(1)}, bf16[1,768,2048]{2,1,0:T(8,128)(2,1)S(1)}) custom-call(bf16[1,2048,768]{2,1,0:T(8,128)(2,1)} %refs_0_.1, bf16[1,2048,768]{2,1,0:T(8,128)(2,1)} %refs_1_.1, bf16[1,768,2048]{2,1,0:T(8,128)(2,1)} %refs_2_.1, ...), custom_call_target="tpu_custom_call" | custom-call | tf_op jit(solution)/shard_map/load_weights/pallas_call | solution.py:157
  22.8 1.7 %collective-permute-done.2.refs_2_ = bf16[16,2176]{1,0:T(8,128)(2,1)S(1)} collective-permute-done((bf16[16,2176]{1,0:T(8,128)(2,1)S(1)}, bf16[16,2176]{1,0:T(8,128)(2,1)S(1)}, u32[]{:S(2)}, u32[]{:S(2)}) %collective-permute-start.2) | collective-permute-done | bytes 69664 | tf_op jit(solution)/shard_map/ppermute | solution.py:472
  24.6 1.6 %collective-permute-start.4 = (bf16[64,2176]{1,0:T(8,128)(2,1)S(1)}, bf16[64,2176]{1,0:T(8,128)(2,1)S(1)}, u32[]{:S(2)}, u32[]{:S(2)}) collective-permute-start(bf16[64,2176]{1,0:T(8,128)(2,1)S(1)} %pack_tokens.1.refs_0_), channel_id=1, source_target_pairs={{0,2},{2,0},{4,6},{6,4},{8,10},{10,8},{12,14},{14,12},{16,18},{18,... | collective-permute-start | bytes 835592 | tf_op jit(solution)/shard_map/ppermute | solution.py:472
  26.1 1.5 %collective-permute-start.5 = (bf16[64,2176]{1,0:T(8,128)(2,1)S(1)}, bf16[64,2176]{1,0:T(8,128)(2,1)S(1)}, u32[]{:S(2)}, u32[]{:S(2)}) collective-permute-start(bf16[64,2176]{1,0:T(8,128)(2,1)S(1)} %pack_tokens.1.refs_0_), channel_id=1, source_target_pairs={{0,4},{2,6},{4,0},{6,2},{8,12},{10,14},{12,8},{14,10},{16,20},{18,... | collective-permute-start | bytes 835592 | tf_op jit(solution)/shard_map/ppermute | solution.py:472
  27.6 5.1 %collective-permute-done.4.refs_1_ = bf16[64,2176]{1,0:T(8,128)(2,1)S(1)} collective-permute-done((bf16[64,2176]{1,0:T(8,128)(2,1)S(1)}, bf16[64,2176]{1,0:T(8,128)(2,1)S(1)}, u32[]{:S(2)}, u32[]{:S(2)}) %collective-permute-start.4) | collective-permute-done | bytes 278560 | tf_op jit(solution)/shard_map/ppermute | solution.py:472
  32.7 1.2 %collective-permute-done.5.refs_2_ = bf16[64,2176]{1,0:T(8,128)(2,1)S(1)} collective-permute-done((bf16[64,2176]{1,0:T(8,128)(2,1)S(1)}, bf16[64,2176]{1,0:T(8,128)(2,1)S(1)}, u32[]{:S(2)}, u32[]{:S(2)}) %collective-permute-start.5) | collective-permute-done | bytes 278560 | tf_op jit(solution)/shard_map/ppermute | solution.py:472
  33.9 1.6 %collective-permute-start.9 = (bf16[32,2176]{1,0:T(8,128)(2,1)S(1)}, bf16[32,2176]{1,0:T(8,128)(2,1)S(1)}, u32[]{:S(2)}, u32[]{:S(2)}) collective-permute-start(bf16[32,2176]{1,0:T(8,128)(2,1)S(1)} %slice.8), channel_id=1, source_target_pairs={{0,4},{2,6},{4,0},{6,2},{8,12},{10,14},{12,8},{14,10},{16,20},{18,... | collective-permute-start | bytes 417800 | tf_op jit(solution)/shard_map/ppermute | solution.py:472
  36.4 4.1 %experts.2 = (bf16[192,2048]{1,0:T(8,128)(2,1)S(1)}, bf16[96,2048]{1,0:T(8,128)(2,1)S(1)}, bf16[96,2048]{1,0:T(8,128)(2,1)S(1)}) custom-call(bf16[64,2176]{1,0:T(8,128)(2,1)S(1)} %pack_tokens.1.refs_0_, bf16[64,2176]{1,0:T(8,128)(2,1)S(1)} %collective-permute-done.4.refs_1_, bf16[64,2176]{1,0:T(8,128)(2,1)S(1)} %collective-permute-done.5.refs_2_, ...), custom_call_target="tpu_custom_call" | custom-call | flops 3623878656 | tf_op jit(solution)/shard_map/experts/pallas_call | solution.py:217
  43.0 2.0 %experts.3 = (bf16[64,2048]{1,0:T(8,128)(2,1)S(1)}, bf16[64,2048]{1,0:T(8,128)(2,1)S(1)}) custom-call(bf16[32,2176]{1,0:T(8,128)(2,1)S(1)} %collective-permute-done.9.refs_0_, bf16[32,2176]{1,0:T(8,128)(2,1)S(1)} %collective-permute-done.10.refs_1_, bf16[32,2176]{1,0:T(8,128)(2,1)S(1)} %collective-permute-done.11.refs_2_, ...), custom_call_target="tpu_custom_call" | custom-call | flops 1207959552 | tf_op jit(solution)/shard_map/experts/pallas_call | solution.py:217
  45.4 1.2 %collective-permute-done.15.refs_4_ = bf16[64,2048]{1,0:T(8,128)(2,1)S(1)} collective-permute-done((bf16[64,2048]{1,0:T(8,128)(2,1)S(1)}, bf16[64,2048]{1,0:T(8,128)(2,1)S(1)}, u32[]{:S(2)}, u32[]{:S(2)}) %collective-permute-start.15) | collective-permute-done | bytes 262176 | tf_op jit(solution)/shard_map/ppermute | solution.py:469
  48.0 2.4 %collective-permute-start.18 = (bf16[256,512]{1,0:T(8,128)(2,1)S(1)}, bf16[256,512]{1,0:T(8,128)(2,1)S(1)}, u32[]{:S(2)}, u32[]{:S(2)}) collective-permute-start(bf16[256,512]{1,0:T(8,128)(2,1)S(1)} %get-tuple-element.81), channel_id=1, source_target_pairs={{0,6},{2,4},{4,2},{6,0},{8,14},{10,12},{12,10},{14,8},{16,22},{18,... | collective-permute-start | bytes 786440 | tf_op jit(solution)/shard_map/ppermute | solution.py:472
  51.0 2.4 %collective-permute-start.22 = (bf16[128,512]{1,0:T(8,128)(2,1)S(1)}, bf16[128,512]{1,0:T(8,128)(2,1)S(1)}, u32[]{:S(2)}, u32[]{:S(2)}) collective-permute-start(bf16[128,512]{1,0:T(8,128)(2,1)S(1)} %copy-done.1), channel_id=1, source_target_pairs={{0,8},{2,10},{4,12},{6,14},{8,0},{10,2},{12,4},{14,6},{16,24},{18,... | collective-permute-start | bytes 393224 | tf_op jit(solution)/shard_map/ppermute | solution.py:472
  53.4 2.6 %collective-permute-done.16.refs_1_ = bf16[256,512]{1,0:T(8,128)(2,1)S(1)} collective-permute-done((bf16[256,512]{1,0:T(8,128)(2,1)S(1)}, bf16[256,512]{1,0:T(8,128)(2,1)S(1)}, u32[]{:S(2)}, u32[]{:S(2)}) %collective-permute-start.16) | collective-permute-done | bytes 262176 | tf_op jit(solution)/shard_map/ppermute | solution.py:472
  56.0 5.3 %collective-permute-done.17.refs_2_ = bf16[256,512]{1,0:T(8,128)(2,1)S(1)} collective-permute-done((bf16[256,512]{1,0:T(8,128)(2,1)S(1)}, bf16[256,512]{1,0:T(8,128)(2,1)S(1)}, u32[]{:S(2)}, u32[]{:S(2)}) %collective-permute-start.17) | collective-permute-done | bytes 262176 | tf_op jit(solution)/shard_map/ppermute | solution.py:472
  61.4 2.5 %collective-permute-start.19 = (bf16[64,512]{1,0:T(8,128)(2,1)S(1)}, bf16[64,512]{1,0:T(8,128)(2,1)S(1)}, u32[]{:S(2)}, u32[]{:S(2)}) collective-permute-start(bf16[64,512]{1,0:T(8,128)(2,1)S(1)} %get-tuple-element.83.refs_4_), channel_id=1, source_target_pairs={{0,24},{2,26},{4,28},{6,30},{8,16},{10,18},{12,20},{14,22},{16,8},... | collective-permute-start | bytes 196616 | tf_op jit(solution)/shard_map/ppermute | solution.py:472
  63.9 2.0 %collective-permute-start.21 = (bf16[64,512]{1,0:T(8,128)(2,1)S(1)}, bf16[64,512]{1,0:T(8,128)(2,1)S(1)}, u32[]{:S(2)}, u32[]{:S(2)}) collective-permute-start(bf16[64,512]{1,0:T(8,128)(2,1)S(1)} %get-tuple-element.85.refs_2_), channel_id=1, source_target_pairs={{0,8},{2,10},{4,12},{6,14},{8,0},{10,2},{12,4},{14,6},{16,24},{18,... | collective-permute-start | bytes 196616 | tf_op jit(solution)/shard_map/ppermute | solution.py:472
  66.0 5.8 %all-gather.2.cloned.1.call-done.refs_0_ = bf16[512,2048]{1,0:T(8,128)(2,1)} async-done(((bf16[128,2048]{1,0:T(8,128)(2,1)}), bf16[512,2048]{1,0:T(8,128)(2,1)}) %all-gather.2.cloned.1.call-update) | async-done | bytes 2097168 | tf_op jit(solution)/shard_map/all_gather | solution.py:491
  71.8 1.6 %load_weights.3.q_ref = bf16[512,2048]{1,0:T(8,128)(2,1)S(1)} custom-call(bf16[512,2048]{1,0:T(8,128)(2,1)} %all-gather.2.cloned.1.call-done.refs_0_, bf16[64,512]{1,0:T(8,128)(2,1)S(1)} %get-tuple-element.88.refs_1_.refs_0_, bf16[64,512]{1,0:T(8,128)(2,1)S(1)} %get-tuple-element.85.refs_2_, bf16[64,512]{1,0:T(8,128)(2,1)S(1)} %get-tuple-element.84.refs_3_, ...), custom_call_target="tpu_custom_call" | custom-call | tf_op jit(solution)/shard_map/load_weights/pallas_call | solution.py:157
  75.5 2.2 %collective-permute-start.26 = (bf16[32,2944]{1,0:T(8,128)(2,1)S(1)}, bf16[32,2944]{1,0:T(8,128)(2,1)S(1)}, u32[]{:S(2)}, u32[]{:S(2)}) collective-permute-start(bf16[32,2944]{1,0:T(8,128)(2,1)S(1)} %get-tuple-element.96), channel_id=1, source_target_pairs={{0,2},{2,0},{4,6},{6,4},{8,10},{10,8},{12,14},{14,12},{16,18},{18,... | collective-permute-start | bytes 565256 | tf_op jit(solution)/shard_map/ppermute | solution.py:472
  77.7 1.9 %collective-permute-start.27 = (bf16[32,2944]{1,0:T(8,128)(2,1)S(1)}, bf16[32,2944]{1,0:T(8,128)(2,1)S(1)}, u32[]{:S(2)}, u32[]{:S(2)}) collective-permute-start(bf16[32,2944]{1,0:T(8,128)(2,1)S(1)} %get-tuple-element.97), channel_id=1, source_target_pairs={{0,4},{2,6},{4,0},{6,2},{8,12},{10,14},{12,8},{14,10},{16,20},{18,... | collective-permute-start | bytes 565256 | tf_op jit(solution)/shard_map/ppermute | solution.py:472
  79.5 3.6 %collective-permute-done.26.refs_1_ = bf16[32,2944]{1,0:T(8,128)(2,1)S(1)} collective-permute-done((bf16[32,2944]{1,0:T(8,128)(2,1)S(1)}, bf16[32,2944]{1,0:T(8,128)(2,1)S(1)}, u32[]{:S(2)}, u32[]{:S(2)}) %collective-permute-start.26) | collective-permute-done | bytes 188448 | tf_op jit(solution)/shard_map/ppermute | solution.py:472
  83.2 5.2 %collective-permute-done.27.refs_2_ = bf16[32,2944]{1,0:T(8,128)(2,1)S(1)} collective-permute-done((bf16[32,2944]{1,0:T(8,128)(2,1)S(1)}, bf16[32,2944]{1,0:T(8,128)(2,1)S(1)}, u32[]{:S(2)}, u32[]{:S(2)}) %collective-permute-start.27) | collective-permute-done | bytes 188448 | tf_op jit(solution)/shard_map/ppermute | solution.py:472
  (74 shorter events, 11.3 us)
Async XLA Ops:
  7.2 64.5 %all-gather.2.cloned.1.call-start = ((), (), s32[]{:S(2)}) async-start(), calls=%async_computation | async-start | bytes 2621440 | tf_op jit(solution)/shard_map/all_gather | solution.py:491
  13.3 9.5 %collective-permute-start.1 = (bf16[16,2176]{1,0:T(8,128)(2,1)S(1)}, bf16[16,2176]{1,0:T(8,128)(2,1)S(1)}, u32[]{:S(2)}, u32[]{:S(2)}) collective-permute-start(bf16[16,2176]{1,0:T(8,128)(2,1)S(1)} %get-tuple-element.59.refs_3_.refs_0_), channel_id=1, source_target_pairs={{0,24},{2,26},{4,28},{6,30},{8,16},{10,18},{12,20},{14,22},{16,8},... | collective-permute-start | bytes 208904 | tf_op jit(solution)/shard_map/ppermute | solution.py:472
  18.3 6.2 %collective-permute-start.2 = (bf16[16,2176]{1,0:T(8,128)(2,1)S(1)}, bf16[16,2176]{1,0:T(8,128)(2,1)S(1)}, u32[]{:S(2)}, u32[]{:S(2)}) collective-permute-start(bf16[16,2176]{1,0:T(8,128)(2,1)S(1)} %get-tuple-element.59.refs_3_.refs_0_), channel_id=1, source_target_pairs={{0,16},{2,18},{4,20},{6,22},{8,24},{10,26},{12,28},{14,30},{16,0},... | collective-permute-start | bytes 208904 | tf_op jit(solution)/shard_map/ppermute | solution.py:472
  18.3 6.2 %collective-permute-start.3 = (bf16[16,2176]{1,0:T(8,128)(2,1)S(1)}, bf16[16,2176]{1,0:T(8,128)(2,1)S(1)}, u32[]{:S(2)}, u32[]{:S(2)}) collective-permute-start(bf16[16,2176]{1,0:T(8,128)(2,1)S(1)} %get-tuple-element.59.refs_3_.refs_0_), channel_id=1, source_target_pairs={{0,8},{2,10},{4,12},{6,14},{8,0},{10,2},{12,4},{14,6},{16,24},{18,... | collective-permute-start | bytes 208904 | tf_op jit(solution)/shard_map/ppermute | solution.py:472
  24.6 8.1 %collective-permute-start.4 = (bf16[64,2176]{1,0:T(8,128)(2,1)S(1)}, bf16[64,2176]{1,0:T(8,128)(2,1)S(1)}, u32[]{:S(2)}, u32[]{:S(2)}) collective-permute-start(bf16[64,2176]{1,0:T(8,128)(2,1)S(1)} %pack_tokens.1.refs_0_), channel_id=1, source_target_pairs={{0,2},{2,0},{4,6},{6,4},{8,10},{10,8},{12,14},{14,12},{16,18},{18,... | collective-permute-start | bytes 835592 | tf_op jit(solution)/shard_map/ppermute | solution.py:472
  26.1 7.8 %collective-permute-start.5 = (bf16[64,2176]{1,0:T(8,128)(2,1)S(1)}, bf16[64,2176]{1,0:T(8,128)(2,1)S(1)}, u32[]{:S(2)}, u32[]{:S(2)}) collective-permute-start(bf16[64,2176]{1,0:T(8,128)(2,1)S(1)} %pack_tokens.1.refs_0_), channel_id=1, source_target_pairs={{0,4},{2,6},{4,0},{6,2},{8,12},{10,14},{12,8},{14,10},{16,20},{18,... | collective-permute-start | bytes 835592 | tf_op jit(solution)/shard_map/ppermute | solution.py:472
  27.6 8.8 %collective-permute-start.6 = (bf16[64,2176]{1,0:T(8,128)(2,1)S(1)}, bf16[64,2176]{1,0:T(8,128)(2,1)S(1)}, u32[]{:S(2)}, u32[]{:S(2)}) collective-permute-start(bf16[64,2176]{1,0:T(8,128)(2,1)S(1)} %pack_tokens.1.refs_0_), channel_id=1, source_target_pairs={{0,1},{1,0},{2,3},{3,2},{4,5},{5,4},{6,7},{7,6},{8,9},{9,8},{10,11... | collective-permute-start | bytes 835592 | tf_op jit(solution)/shard_map/ppermute | solution.py:469
  32.7 3.7 %collective-permute-start.7 = (bf16[64,2176]{1,0:T(8,128)(2,1)S(1)}, bf16[64,2176]{1,0:T(8,128)(2,1)S(1)}, u32[]{:S(2)}, u32[]{:S(2)}) collective-permute-start(bf16[64,2176]{1,0:T(8,128)(2,1)S(1)} %collective-permute-done.4.refs_1_), channel_id=1, source_target_pairs={{0,1},{1,0},{2,3},{3,2},{4,5},{5,4},{6,7},{7,6},{8,9},{9,8},{10,11... | collective-permute-start | bytes 835592 | tf_op jit(solution)/shard_map/ppermute | solution.py:469
  33.9 6.5 %collective-permute-start.9 = (bf16[32,2176]{1,0:T(8,128)(2,1)S(1)}, bf16[32,2176]{1,0:T(8,128)(2,1)S(1)}, u32[]{:S(2)}, u32[]{:S(2)}) collective-permute-start(bf16[32,2176]{1,0:T(8,128)(2,1)S(1)} %slice.8), channel_id=1, source_target_pairs={{0,4},{2,6},{4,0},{6,2},{8,12},{10,14},{12,8},{14,10},{16,20},{18,... | collective-permute-start | bytes 417800 | tf_op jit(solution)/shard_map/ppermute | solution.py:472
  35.5 5.9 %collective-permute-start.10 = (bf16[32,2176]{1,0:T(8,128)(2,1)S(1)}, bf16[32,2176]{1,0:T(8,128)(2,1)S(1)}, u32[]{:S(2)}, u32[]{:S(2)}) collective-permute-start(bf16[32,2176]{1,0:T(8,128)(2,1)S(1)} %slice.9), channel_id=1, source_target_pairs={{0,2},{2,0},{4,6},{6,4},{8,10},{10,8},{12,14},{14,12},{16,18},{18,... | collective-permute-start | bytes 417800 | tf_op jit(solution)/shard_map/ppermute | solution.py:472
  41.9 3.4 %collective-permute-start.13 = (bf16[96,2048]{1,0:T(8,128)(2,1)S(1)}, bf16[96,2048]{1,0:T(8,128)(2,1)S(1)}, u32[]{:S(2)}, u32[]{:S(2)}) collective-permute-start(bf16[96,2048]{1,0:T(8,128)(2,1)S(1)} %get-tuple-element.71), channel_id=1, source_target_pairs={{0,1},{1,0},{2,3},{3,2},{4,5},{5,4},{6,7},{7,6},{8,9},{9,8},{10,11... | collective-permute-start | bytes 1179656 | tf_op jit(solution)/shard_map/ppermute | solution.py:469
  41.9 3.4 %collective-permute-start.14 = (bf16[96,2048]{1,0:T(8,128)(2,1)S(1)}, bf16[96,2048]{1,0:T(8,128)(2,1)S(1)}, u32[]{:S(2)}, u32[]{:S(2)}) collective-permute-start(bf16[96,2048]{1,0:T(8,128)(2,1)S(1)} %get-tuple-element.72), channel_id=1, source_target_pairs={{0,1},{1,0},{2,3},{3,2},{4,5},{5,4},{6,7},{7,6},{8,9},{9,8},{10,11... | collective-permute-start | bytes 1179656 | tf_op jit(solution)/shard_map/ppermute | solution.py:469
  46.8 9.2 %collective-permute-start.16 = (bf16[256,512]{1,0:T(8,128)(2,1)S(1)}, bf16[256,512]{1,0:T(8,128)(2,1)S(1)}, u32[]{:S(2)}, u32[]{:S(2)}) collective-permute-start(bf16[256,512]{1,0:T(8,128)(2,1)S(1)} %get-tuple-element.79), channel_id=1, source_target_pairs={{0,2},{2,0},{4,6},{6,4},{8,10},{10,8},{12,14},{14,12},{16,18},{18,... | collective-permute-start | bytes 786440 | tf_op jit(solution)/shard_map/ppermute | solution.py:472
  47.4 13.9 %collective-permute-start.17 = (bf16[256,512]{1,0:T(8,128)(2,1)S(1)}, bf16[256,512]{1,0:T(8,128)(2,1)S(1)}, u32[]{:S(2)}, u32[]{:S(2)}) collective-permute-start(bf16[256,512]{1,0:T(8,128)(2,1)S(1)} %get-tuple-element.80), channel_id=1, source_target_pairs={{0,4},{2,6},{4,0},{6,2},{8,12},{10,14},{12,8},{14,10},{16,20},{18,... | collective-permute-start | bytes 786440 | tf_op jit(solution)/shard_map/ppermute | solution.py:472
  48.0 13.3 %collective-permute-start.18 = (bf16[256,512]{1,0:T(8,128)(2,1)S(1)}, bf16[256,512]{1,0:T(8,128)(2,1)S(1)}, u32[]{:S(2)}, u32[]{:S(2)}) collective-permute-start(bf16[256,512]{1,0:T(8,128)(2,1)S(1)} %get-tuple-element.81), channel_id=1, source_target_pairs={{0,6},{2,4},{4,2},{6,0},{8,14},{10,12},{12,10},{14,8},{16,22},{18,... | collective-permute-start | bytes 786440 | tf_op jit(solution)/shard_map/ppermute | solution.py:472
  50.4 15.5 %collective-permute-start.23 = (bf16[128,512]{1,0:T(8,128)(2,1)S(1)}, bf16[128,512]{1,0:T(8,128)(2,1)S(1)}, u32[]{:S(2)}, u32[]{:S(2)}) collective-permute-start(bf16[128,512]{1,0:T(8,128)(2,1)S(1)} %copy-done.1), channel_id=1, source_target_pairs={{0,16},{2,18},{4,20},{6,22},{8,24},{10,26},{12,28},{14,30},{16,0},... | collective-permute-start | bytes 393224 | tf_op jit(solution)/shard_map/ppermute | solution.py:472
  51.0 14.9 %collective-permute-start.22 = (bf16[128,512]{1,0:T(8,128)(2,1)S(1)}, bf16[128,512]{1,0:T(8,128)(2,1)S(1)}, u32[]{:S(2)}, u32[]{:S(2)}) collective-permute-start(bf16[128,512]{1,0:T(8,128)(2,1)S(1)} %copy-done.1), channel_id=1, source_target_pairs={{0,8},{2,10},{4,12},{6,14},{8,0},{10,2},{12,4},{14,6},{16,24},{18,... | collective-permute-start | bytes 393224 | tf_op jit(solution)/shard_map/ppermute | solution.py:472
  61.4 12.0 %collective-permute-start.19 = (bf16[64,512]{1,0:T(8,128)(2,1)S(1)}, bf16[64,512]{1,0:T(8,128)(2,1)S(1)}, u32[]{:S(2)}, u32[]{:S(2)}) collective-permute-start(bf16[64,512]{1,0:T(8,128)(2,1)S(1)} %get-tuple-element.83.refs_4_), channel_id=1, source_target_pairs={{0,24},{2,26},{4,28},{6,30},{8,16},{10,18},{12,20},{14,22},{16,8},... | collective-permute-start | bytes 196616 | tf_op jit(solution)/shard_map/ppermute | solution.py:472
  63.9 9.5 %collective-permute-start.20 = (bf16[64,512]{1,0:T(8,128)(2,1)S(1)}, bf16[64,512]{1,0:T(8,128)(2,1)S(1)}, u32[]{:S(2)}, u32[]{:S(2)}) collective-permute-start(bf16[64,512]{1,0:T(8,128)(2,1)S(1)} %get-tuple-element.84.refs_3_), channel_id=1, source_target_pairs={{0,16},{2,18},{4,20},{6,22},{8,24},{10,26},{12,28},{14,30},{16,0},... | collective-permute-start | bytes 196616 | tf_op jit(solution)/shard_map/ppermute | solution.py:472
  63.9 9.5 %collective-permute-start.21 = (bf16[64,512]{1,0:T(8,128)(2,1)S(1)}, bf16[64,512]{1,0:T(8,128)(2,1)S(1)}, u32[]{:S(2)}, u32[]{:S(2)}) collective-permute-start(bf16[64,512]{1,0:T(8,128)(2,1)S(1)} %get-tuple-element.85.refs_2_), channel_id=1, source_target_pairs={{0,8},{2,10},{4,12},{6,14},{8,0},{10,2},{12,4},{14,6},{16,24},{18,... | collective-permute-start | bytes 196616 | tf_op jit(solution)/shard_map/ppermute | solution.py:472
  65.9 7.9 %collective-permute-start.25 = (bf16[128,512]{1,0:T(8,128)(2,1)S(1)}, bf16[128,512]{1,0:T(8,128)(2,1)S(1)}, u32[]{:S(2)}, u32[]{:S(2)}) collective-permute-start(bf16[128,512]{1,0:T(8,128)(2,1)S(1)} %collective-permute-done.23.refs_6_.refs_2_), channel_id=1, source_target_pairs={{0,8},{2,10},{4,12},{6,14},{8,0},{10,2},{12,4},{14,6},{16,24},{18,... | collective-permute-start | bytes 393224 | tf_op jit(solution)/shard_map/ppermute | solution.py:472
  75.5 7.7 %collective-permute-start.26 = (bf16[32,2944]{1,0:T(8,128)(2,1)S(1)}, bf16[32,2944]{1,0:T(8,128)(2,1)S(1)}, u32[]{:S(2)}, u32[]{:S(2)}) collective-permute-start(bf16[32,2944]{1,0:T(8,128)(2,1)S(1)} %get-tuple-element.96), channel_id=1, source_target_pairs={{0,2},{2,0},{4,6},{6,4},{8,10},{10,8},{12,14},{14,12},{16,18},{18,... | collective-permute-start | bytes 565256 | tf_op jit(solution)/shard_map/ppermute | solution.py:472
  77.7 10.7 %collective-permute-start.27 = (bf16[32,2944]{1,0:T(8,128)(2,1)S(1)}, bf16[32,2944]{1,0:T(8,128)(2,1)S(1)}, u32[]{:S(2)}, u32[]{:S(2)}) collective-permute-start(bf16[32,2944]{1,0:T(8,128)(2,1)S(1)} %get-tuple-element.97), channel_id=1, source_target_pairs={{0,4},{2,6},{4,0},{6,2},{8,12},{10,14},{12,8},{14,10},{16,20},{18,... | collective-permute-start | bytes 565256 | tf_op jit(solution)/shard_map/ppermute | solution.py:472
  79.5 8.8 %collective-permute-start.28 = (bf16[32,2944]{1,0:T(8,128)(2,1)S(1)}, bf16[32,2944]{1,0:T(8,128)(2,1)S(1)}, u32[]{:S(2)}, u32[]{:S(2)}) collective-permute-start(bf16[32,2944]{1,0:T(8,128)(2,1)S(1)} %get-tuple-element.98), channel_id=1, source_target_pairs={{0,6},{2,4},{4,2},{6,0},{8,14},{10,12},{12,10},{14,8},{16,22},{18,... | collective-permute-start | bytes 565256 | tf_op jit(solution)/shard_map/ppermute | solution.py:472
  (14 other events, 100.1 us)
Sparse Core Ops, SparseCore 0:
  13.4 58.2 all-gather.1

commit v22 on v21

--- a/solution.py
+++ b/solution.py
@@ -334,7 +334,7 @@
         out_specs=(VMEM, VMEM),
         compiler_params=params(4),
         name="second_norm",
-    )(*far_first(parts), gain)
+    )(*parts, gain)
 
 
 def projection_kernel(chunk, mine_ref, theirs_ref, next_ref, q_ref, *refs):
@@ -510,8 +510,7 @@
     kv_rows.append(to_expert(kv_rows[2], PLANE))
     (q_rows,) = load((q_rows,), (*parts, *kv_rows[1:3]))
     parts = to_z(parts)
-    *parts, q_rows = lax.optimization_barrier((*far_first(parts), q_rows))
-    parts = far_first(parts)
+    *parts, q_rows = lax.optimization_barrier((*parts, q_rows))
     scaled, following = second_norm(parts, input_gain[None, :])
     products = to_plane(projection(scaled, to_core(scaled), following, q_rows, kv_rows))
     return head_norm(

time: 96.2 us -> 95.1 us (0.989)
    all_gather x1, waiting for transfers between devices: 5.78 us -> 3.27 us  [per_device_dense(): lax.all_gather(q_own, 'expert', axis=0, tiled=True, axis_index_groups=lines)]
    ppermute x19, waiting for transfers between devices: 25.8 us -> 27.4 us  [to_expert(): lax.ppermute(value, 'expert', [(i, i ^ offset) for i in range(n_expert)])]
  transfers between devices with their start and end apart: 30 -> 30, of which waited for: 15 -> 16; matrix products, arithmetic and copies ran while one was open for 1% -> 1% of each run, Pallas kernels for 13% -> 13%
where the time goes in v22:
time: 95.1 us; the launch traced here: 94.9 us
  waiting for transfers between devices  34 us (36%)
  starting transfers between devices  28.1 us (30%)
  Pallas kernels  18 us (19%)
  between operations  14.2 us (15%)
    ppermute x19, waiting for transfers between devices, to_expert(): lax.ppermute(value, 'expert', [(i, i ^ offset) for i in range(n_expert)])  27.4 us
    ppermute x19, starting transfers between devices, to_expert(): lax.ppermute(value, 'expert', [(i, i ^ offset) for i in range(n_expert)])  26.1 us
    pallas_call x2, Pallas kernels, experts(): pl.pallas_call(functools.partial(expert_kernel, depth, chunk, len(blocks)...  6.05 us
    pallas_call x2, Pallas kernels, load(): pl.pallas_call(functools.partial(load_kernel, count), out_shape=tuple((pl...  5.46 us
    pallas_call x1, Pallas kernels, out_projection(): pl.pallas_call(functools.partial(out_projection_kernel, chunk), out_shape...  4.38 us
    ppermute x10, waiting for transfers between devices, to_core(): return lax.ppermute(value, 'tensor', [(0, 1), (1, 0)])  3.3 us
    all_gather x1, waiting for transfers between devices, per_device_dense(): lax.all_gather(q_own, 'expert', axis=0, tiled=True, axis_index_groups=lines)  3.27 us
    ppermute x10, starting transfers between devices, to_core(): return lax.ppermute(value, 'tensor', [(0, 1), (1, 0)])  1.99 us
  transfers between devices with their start and end apart: 30, of which 16 were waited for; matrix products, arithmetic and copies ran while one was open for 1% of the time, Pallas kernels for 13%

profile of v22, /device:TPU:0, one launch (start us, length us, event | category | flops | bytes accessed | tf_op | source)
XLA Modules:
  0.0 94.9 jit_solution(9481075645927383078)
XLA Ops:
  7.3 4.4 %out_projection.1 = (f32[16,2048]{1,0:T(8,128)S(1)}, f32[16,2048]{1,0:T(8,128)S(1)}) custom-call(bf16[32,2048]{1,0:T(8,128)(2,1)} %a_hbm.1, bf16[2048,2048]{1,0:T(8,128)(2,1)} %w_hbm.1), custom_call_target="tpu_custom_call" | custom-call | tf_op jit(solution)/shard_map/out_projection/pallas_call | solution.py:81
  13.3 5.0 %collective-permute-start.1 = (bf16[16,2176]{1,0:T(8,128)(2,1)S(1)}, bf16[16,2176]{1,0:T(8,128)(2,1)S(1)}, u32[]{:S(2)}, u32[]{:S(2)}) collective-permute-start(bf16[16,2176]{1,0:T(8,128)(2,1)S(1)} %get-tuple-element.59.refs_3_.refs_0_), channel_id=1, source_target_pairs={{0,24},{2,26},{4,28},{6,30},{8,16},{10,18},{12,20},{14,22},{16,8},... | collective-permute-start | bytes 208904 | tf_op jit(solution)/shard_map/ppermute | solution.py:472
  19.0 3.8 %load_weights.2 = (bf16[1,2048,768]{2,1,0:T(8,128)(2,1)S(1)}, bf16[1,2048,768]{2,1,0:T(8,128)(2,1)S(1)}, bf16[1,768,2048]{2,1,0:T(8,128)(2,1)S(1)}) custom-call(bf16[1,2048,768]{2,1,0:T(8,128)(2,1)} %refs_0_.1, bf16[1,2048,768]{2,1,0:T(8,128)(2,1)} %refs_1_.1, bf16[1,768,2048]{2,1,0:T(8,128)(2,1)} %refs_2_.1, ...), custom_call_target="tpu_custom_call" | custom-call | tf_op jit(solution)/shard_map/load_weights/pallas_call | solution.py:157
  22.8 1.7 %collective-permute-done.2.refs_2_ = bf16[16,2176]{1,0:T(8,128)(2,1)S(1)} collective-permute-done((bf16[16,2176]{1,0:T(8,128)(2,1)S(1)}, bf16[16,2176]{1,0:T(8,128)(2,1)S(1)}, u32[]{:S(2)}, u32[]{:S(2)}) %collective-permute-start.2) | collective-permute-done | bytes 69664 | tf_op jit(solution)/shard_map/ppermute | solution.py:472
  24.6 1.6 %collective-permute-start.4 = (bf16[64,2176]{1,0:T(8,128)(2,1)S(1)}, bf16[64,2176]{1,0:T(8,128)(2,1)S(1)}, u32[]{:S(2)}, u32[]{:S(2)}) collective-permute-start(bf16[64,2176]{1,0:T(8,128)(2,1)S(1)} %pack_tokens.1.refs_0_), channel_id=1, source_target_pairs={{0,2},{2,0},{4,6},{6,4},{8,10},{10,8},{12,14},{14,12},{16,18},{18,... | collective-permute-start | bytes 835592 | tf_op jit(solution)/shard_map/ppermute | solution.py:472
  26.1 1.5 %collective-permute-start.5 = (bf16[64,2176]{1,0:T(8,128)(2,1)S(1)}, bf16[64,2176]{1,0:T(8,128)(2,1)S(1)}, u32[]{:S(2)}, u32[]{:S(2)}) collective-permute-start(bf16[64,2176]{1,0:T(8,128)(2,1)S(1)} %pack_tokens.1.refs_0_), channel_id=1, source_target_pairs={{0,4},{2,6},{4,0},{6,2},{8,12},{10,14},{12,8},{14,10},{16,20},{18,... | collective-permute-start | bytes 835592 | tf_op jit(solution)/shard_map/ppermute | solution.py:472
  27.6 5.1 %collective-permute-done.4.refs_1_ = bf16[64,2176]{1,0:T(8,128)(2,1)S(1)} collective-permute-done((bf16[64,2176]{1,0:T(8,128)(2,1)S(1)}, bf16[64,2176]{1,0:T(8,128)(2,1)S(1)}, u32[]{:S(2)}, u32[]{:S(2)}) %collective-permute-start.4) | collective-permute-done | bytes 278560 | tf_op jit(solution)/shard_map/ppermute | solution.py:472
  33.9 1.6 %collective-permute-start.9 = (bf16[32,2176]{1,0:T(8,128)(2,1)S(1)}, bf16[32,2176]{1,0:T(8,128)(2,1)S(1)}, u32[]{:S(2)}, u32[]{:S(2)}) collective-permute-start(bf16[32,2176]{1,0:T(8,128)(2,1)S(1)} %slice.8), channel_id=1, source_target_pairs={{0,4},{2,6},{4,0},{6,2},{8,12},{10,14},{12,8},{14,10},{16,20},{18,... | collective-permute-start | bytes 417800 | tf_op jit(solution)/shard_map/ppermute | solution.py:472
  36.4 4.1 %experts.2 = (bf16[192,2048]{1,0:T(8,128)(2,1)S(1)}, bf16[96,2048]{1,0:T(8,128)(2,1)S(1)}, bf16[96,2048]{1,0:T(8,128)(2,1)S(1)}) custom-call(bf16[64,2176]{1,0:T(8,128)(2,1)S(1)} %pack_tokens.1.refs_0_, bf16[64,2176]{1,0:T(8,128)(2,1)S(1)} %collective-permute-done.4.refs_1_, bf16[64,2176]{1,0:T(8,128)(2,1)S(1)} %collective-permute-done.5.refs_2_, ...), custom_call_target="tpu_custom_call" | custom-call | flops 3623878656 | tf_op jit(solution)/shard_map/experts/pallas_call | solution.py:217
  43.0 2.0 %experts.3 = (bf16[64,2048]{1,0:T(8,128)(2,1)S(1)}, bf16[64,2048]{1,0:T(8,128)(2,1)S(1)}) custom-call(bf16[32,2176]{1,0:T(8,128)(2,1)S(1)} %collective-permute-done.9.refs_0_, bf16[32,2176]{1,0:T(8,128)(2,1)S(1)} %collective-permute-done.10.refs_1_, bf16[32,2176]{1,0:T(8,128)(2,1)S(1)} %collective-permute-done.11.refs_2_, ...), custom_call_target="tpu_custom_call" | custom-call | flops 1207959552 | tf_op jit(solution)/shard_map/experts/pallas_call | solution.py:217
  45.4 1.2 %collective-permute-done.15.refs_4_ = bf16[64,2048]{1,0:T(8,128)(2,1)S(1)} collective-permute-done((bf16[64,2048]{1,0:T(8,128)(2,1)S(1)}, bf16[64,2048]{1,0:T(8,128)(2,1)S(1)}, u32[]{:S(2)}, u32[]{:S(2)}) %collective-permute-start.15) | collective-permute-done | bytes 262176 | tf_op jit(solution)/shard_map/ppermute | solution.py:469
  48.0 2.4 %collective-permute-start.18 = (bf16[256,512]{1,0:T(8,128)(2,1)S(1)}, bf16[256,512]{1,0:T(8,128)(2,1)S(1)}, u32[]{:S(2)}, u32[]{:S(2)}) collective-permute-start(bf16[256,512]{1,0:T(8,128)(2,1)S(1)} %get-tuple-element.81), channel_id=1, source_target_pairs={{0,6},{2,4},{4,2},{6,0},{8,14},{10,12},{12,10},{14,8},{16,22},{18,... | collective-permute-start | bytes 786440 | tf_op jit(solution)/shard_map/ppermute | solution.py:472
  51.0 2.4 %collective-permute-start.22 = (bf16[128,512]{1,0:T(8,128)(2,1)S(1)}, bf16[128,512]{1,0:T(8,128)(2,1)S(1)}, u32[]{:S(2)}, u32[]{:S(2)}) collective-permute-start(bf16[128,512]{1,0:T(8,128)(2,1)S(1)} %copy-done.1), channel_id=1, source_target_pairs={{0,8},{2,10},{4,12},{6,14},{8,0},{10,2},{12,4},{14,6},{16,24},{18,... | collective-permute-start | bytes 393224 | tf_op jit(solution)/shard_map/ppermute | solution.py:472
  53.4 2.6 %collective-permute-done.16.refs_1_ = bf16[256,512]{1,0:T(8,128)(2,1)S(1)} collective-permute-done((bf16[256,512]{1,0:T(8,128)(2,1)S(1)}, bf16[256,512]{1,0:T(8,128)(2,1)S(1)}, u32[]{:S(2)}, u32[]{:S(2)}) %collective-permute-start.16) | collective-permute-done | bytes 262176 | tf_op jit(solution)/shard_map/ppermute | solution.py:472
  56.0 5.3 %collective-permute-done.17.refs_2_ = bf16[256,512]{1,0:T(8,128)(2,1)S(1)} collective-permute-done((bf16[256,512]{1,0:T(8,128)(2,1)S(1)}, bf16[256,512]{1,0:T(8,128)(2,1)S(1)}, u32[]{:S(2)}, u32[]{:S(2)}) %collective-permute-start.17) | collective-permute-done | bytes 262176 | tf_op jit(solution)/shard_map/ppermute | solution.py:472
  62.1 2.4 %collective-permute-start.20 = (bf16[64,512]{1,0:T(8,128)(2,1)S(1)}, bf16[64,512]{1,0:T(8,128)(2,1)S(1)}, u32[]{:S(2)}, u32[]{:S(2)}) collective-permute-start(bf16[64,512]{1,0:T(8,128)(2,1)S(1)} %get-tuple-element.84.refs_3_), channel_id=1, source_target_pairs={{0,16},{2,18},{4,20},{6,22},{8,24},{10,26},{12,28},{14,30},{16,0},... | collective-permute-start | bytes 196616 | tf_op jit(solution)/shard_map/ppermute | solution.py:472
  64.5 1.4 %collective-permute-start.21 = (bf16[64,512]{1,0:T(8,128)(2,1)S(1)}, bf16[64,512]{1,0:T(8,128)(2,1)S(1)}, u32[]{:S(2)}, u32[]{:S(2)}) collective-permute-start(bf16[64,512]{1,0:T(8,128)(2,1)S(1)} %get-tuple-element.85.refs_4_), channel_id=1, source_target_pairs={{0,24},{2,26},{4,28},{6,30},{8,16},{10,18},{12,20},{14,22},{16,8},... | collective-permute-start | bytes 196616 | tf_op jit(solution)/shard_map/ppermute | solution.py:472
  65.9 3.3 %all-gather.2.cloned.1.call-done.refs_0_ = bf16[512,2048]{1,0:T(8,128)(2,1)} async-done(((bf16[128,2048]{1,0:T(8,128)(2,1)}), bf16[512,2048]{1,0:T(8,128)(2,1)}) %all-gather.2.cloned.1.call-update) | async-done | bytes 2097168 | tf_op jit(solution)/shard_map/all_gather | solution.py:491
  69.2 1.6 %load_weights.3.q_ref = bf16[512,2048]{1,0:T(8,128)(2,1)S(1)} custom-call(bf16[512,2048]{1,0:T(8,128)(2,1)} %all-gather.2.cloned.1.call-done.refs_0_, bf16[64,512]{1,0:T(8,128)(2,1)S(1)} %get-tuple-element.88.refs_1_.refs_0_, bf16[64,512]{1,0:T(8,128)(2,1)S(1)} %get-tuple-element.83.refs_2_, bf16[64,512]{1,0:T(8,128)(2,1)S(1)} %get-tuple-element.84.refs_3_, ...), custom_call_target="tpu_custom_call" | custom-call | tf_op jit(solution)/shard_map/load_weights/pallas_call | solution.py:157
  70.8 1.6 %collective-permute-done.21.refs_3_ = bf16[64,512]{1,0:T(8,128)(2,1)S(1)} collective-permute-done((bf16[64,512]{1,0:T(8,128)(2,1)S(1)}, bf16[64,512]{1,0:T(8,128)(2,1)S(1)}, u32[]{:S(2)}, u32[]{:S(2)}) %collective-permute-start.21) | collective-permute-done | bytes 65568 | tf_op jit(solution)/shard_map/ppermute | solution.py:472
  74.5 1.4 %collective-permute-start.26 = (bf16[32,2944]{1,0:T(8,128)(2,1)S(1)}, bf16[32,2944]{1,0:T(8,128)(2,1)S(1)}, u32[]{:S(2)}, u32[]{:S(2)}) collective-permute-start(bf16[32,2944]{1,0:T(8,128)(2,1)S(1)} %get-tuple-element.96), channel_id=1, source_target_pairs={{0,2},{2,0},{4,6},{6,4},{8,10},{10,8},{12,14},{14,12},{16,18},{18,... | collective-permute-start | bytes 565256 | tf_op jit(solution)/shard_map/ppermute | solution.py:472
  75.9 2.4 %collective-permute-start.27 = (bf16[32,2944]{1,0:T(8,128)(2,1)S(1)}, bf16[32,2944]{1,0:T(8,128)(2,1)S(1)}, u32[]{:S(2)}, u32[]{:S(2)}) collective-permute-start(bf16[32,2944]{1,0:T(8,128)(2,1)S(1)} %get-tuple-element.97), channel_id=1, source_target_pairs={{0,4},{2,6},{4,0},{6,2},{8,12},{10,14},{12,8},{14,10},{16,20},{18,... | collective-permute-start | bytes 565256 | tf_op jit(solution)/shard_map/ppermute | solution.py:472
  78.4 3.7 %collective-permute-done.26.refs_1_ = bf16[32,2944]{1,0:T(8,128)(2,1)S(1)} collective-permute-done((bf16[32,2944]{1,0:T(8,128)(2,1)S(1)}, bf16[32,2944]{1,0:T(8,128)(2,1)S(1)}, u32[]{:S(2)}, u32[]{:S(2)}) %collective-permute-start.26) | collective-permute-done | bytes 188448 | tf_op jit(solution)/shard_map/ppermute | solution.py:472
  82.1 5.1 %collective-permute-done.27.refs_2_ = bf16[32,2944]{1,0:T(8,128)(2,1)S(1)} collective-permute-done((bf16[32,2944]{1,0:T(8,128)(2,1)S(1)}, bf16[32,2944]{1,0:T(8,128)(2,1)S(1)}, u32[]{:S(2)}, u32[]{:S(2)}) %collective-permute-start.27) | collective-permute-done | bytes 188448 | tf_op jit(solution)/shard_map/ppermute | solution.py:472
  (74 shorter events, 13.1 us)
Async XLA Ops:
  7.2 62.0 %all-gather.2.cloned.1.call-start = ((), (), s32[]{:S(2)}) async-start(), calls=%async_computation | async-start | bytes 2621440 | tf_op jit(solution)/shard_map/all_gather | solution.py:491
  13.3 9.5 %collective-permute-start.1 = (bf16[16,2176]{1,0:T(8,128)(2,1)S(1)}, bf16[16,2176]{1,0:T(8,128)(2,1)S(1)}, u32[]{:S(2)}, u32[]{:S(2)}) collective-permute-start(bf16[16,2176]{1,0:T(8,128)(2,1)S(1)} %get-tuple-element.59.refs_3_.refs_0_), channel_id=1, source_target_pairs={{0,24},{2,26},{4,28},{6,30},{8,16},{10,18},{12,20},{14,22},{16,8},... | collective-permute-start | bytes 208904 | tf_op jit(solution)/shard_map/ppermute | solution.py:472
  18.3 6.2 %collective-permute-start.2 = (bf16[16,2176]{1,0:T(8,128)(2,1)S(1)}, bf16[16,2176]{1,0:T(8,128)(2,1)S(1)}, u32[]{:S(2)}, u32[]{:S(2)}) collective-permute-start(bf16[16,2176]{1,0:T(8,128)(2,1)S(1)} %get-tuple-element.59.refs_3_.refs_0_), channel_id=1, source_target_pairs={{0,16},{2,18},{4,20},{6,22},{8,24},{10,26},{12,28},{14,30},{16,0},... | collective-permute-start | bytes 208904 | tf_op jit(solution)/shard_map/ppermute | solution.py:472
  18.3 6.2 %collective-permute-start.3 = (bf16[16,2176]{1,0:T(8,128)(2,1)S(1)}, bf16[16,2176]{1,0:T(8,128)(2,1)S(1)}, u32[]{:S(2)}, u32[]{:S(2)}) collective-permute-start(bf16[16,2176]{1,0:T(8,128)(2,1)S(1)} %get-tuple-element.59.refs_3_.refs_0_), channel_id=1, source_target_pairs={{0,8},{2,10},{4,12},{6,14},{8,0},{10,2},{12,4},{14,6},{16,24},{18,... | collective-permute-start | bytes 208904 | tf_op jit(solution)/shard_map/ppermute | solution.py:472
  24.6 8.1 %collective-permute-start.4 = (bf16[64,2176]{1,0:T(8,128)(2,1)S(1)}, bf16[64,2176]{1,0:T(8,128)(2,1)S(1)}, u32[]{:S(2)}, u32[]{:S(2)}) collective-permute-start(bf16[64,2176]{1,0:T(8,128)(2,1)S(1)} %pack_tokens.1.refs_0_), channel_id=1, source_target_pairs={{0,2},{2,0},{4,6},{6,4},{8,10},{10,8},{12,14},{14,12},{16,18},{18,... | collective-permute-start | bytes 835592 | tf_op jit(solution)/shard_map/ppermute | solution.py:472
  26.1 7.8 %collective-permute-start.5 = (bf16[64,2176]{1,0:T(8,128)(2,1)S(1)}, bf16[64,2176]{1,0:T(8,128)(2,1)S(1)}, u32[]{:S(2)}, u32[]{:S(2)}) collective-permute-start(bf16[64,2176]{1,0:T(8,128)(2,1)S(1)} %pack_tokens.1.refs_0_), channel_id=1, source_target_pairs={{0,4},{2,6},{4,0},{6,2},{8,12},{10,14},{12,8},{14,10},{16,20},{18,... | collective-permute-start | bytes 835592 | tf_op jit(solution)/shard_map/ppermute | solution.py:472
  27.6 8.8 %collective-permute-start.6 = (bf16[64,2176]{1,0:T(8,128)(2,1)S(1)}, bf16[64,2176]{1,0:T(8,128)(2,1)S(1)}, u32[]{:S(2)}, u32[]{:S(2)}) collective-permute-start(bf16[64,2176]{1,0:T(8,128)(2,1)S(1)} %pack_tokens.1.refs_0_), channel_id=1, source_target_pairs={{0,1},{1,0},{2,3},{3,2},{4,5},{5,4},{6,7},{7,6},{8,9},{9,8},{10,11... | collective-permute-start | bytes 835592 | tf_op jit(solution)/shard_map/ppermute | solution.py:469
  32.7 3.7 %collective-permute-start.7 = (bf16[64,2176]{1,0:T(8,128)(2,1)S(1)}, bf16[64,2176]{1,0:T(8,128)(2,1)S(1)}, u32[]{:S(2)}, u32[]{:S(2)}) collective-permute-start(bf16[64,2176]{1,0:T(8,128)(2,1)S(1)} %collective-permute-done.4.refs_1_), channel_id=1, source_target_pairs={{0,1},{1,0},{2,3},{3,2},{4,5},{5,4},{6,7},{7,6},{8,9},{9,8},{10,11... | collective-permute-start | bytes 835592 | tf_op jit(solution)/shard_map/ppermute | solution.py:469
  33.9 6.5 %collective-permute-start.9 = (bf16[32,2176]{1,0:T(8,128)(2,1)S(1)}, bf16[32,2176]{1,0:T(8,128)(2,1)S(1)}, u32[]{:S(2)}, u32[]{:S(2)}) collective-permute-start(bf16[32,2176]{1,0:T(8,128)(2,1)S(1)} %slice.8), channel_id=1, source_target_pairs={{0,4},{2,6},{4,0},{6,2},{8,12},{10,14},{12,8},{14,10},{16,20},{18,... | collective-permute-start | bytes 417800 | tf_op jit(solution)/shard_map/ppermute | solution.py:472
  35.5 5.9 %collective-permute-start.10 = (bf16[32,2176]{1,0:T(8,128)(2,1)S(1)}, bf16[32,2176]{1,0:T(8,128)(2,1)S(1)}, u32[]{:S(2)}, u32[]{:S(2)}) collective-permute-start(bf16[32,2176]{1,0:T(8,128)(2,1)S(1)} %slice.9), channel_id=1, source_target_pairs={{0,2},{2,0},{4,6},{6,4},{8,10},{10,8},{12,14},{14,12},{16,18},{18,... | collective-permute-start | bytes 417800 | tf_op jit(solution)/shard_map/ppermute | solution.py:472
  41.9 3.4 %collective-permute-start.13 = (bf16[96,2048]{1,0:T(8,128)(2,1)S(1)}, bf16[96,2048]{1,0:T(8,128)(2,1)S(1)}, u32[]{:S(2)}, u32[]{:S(2)}) collective-permute-start(bf16[96,2048]{1,0:T(8,128)(2,1)S(1)} %get-tuple-element.71), channel_id=1, source_target_pairs={{0,1},{1,0},{2,3},{3,2},{4,5},{5,4},{6,7},{7,6},{8,9},{9,8},{10,11... | collective-permute-start | bytes 1179656 | tf_op jit(solution)/shard_map/ppermute | solution.py:469
  41.9 3.4 %collective-permute-start.14 = (bf16[96,2048]{1,0:T(8,128)(2,1)S(1)}, bf16[96,2048]{1,0:T(8,128)(2,1)S(1)}, u32[]{:S(2)}, u32[]{:S(2)}) collective-permute-start(bf16[96,2048]{1,0:T(8,128)(2,1)S(1)} %get-tuple-element.72), channel_id=1, source_target_pairs={{0,1},{1,0},{2,3},{3,2},{4,5},{5,4},{6,7},{7,6},{8,9},{9,8},{10,11... | collective-permute-start | bytes 1179656 | tf_op jit(solution)/shard_map/ppermute | solution.py:469
  46.8 9.2 %collective-permute-start.16 = (bf16[256,512]{1,0:T(8,128)(2,1)S(1)}, bf16[256,512]{1,0:T(8,128)(2,1)S(1)}, u32[]{:S(2)}, u32[]{:S(2)}) collective-permute-start(bf16[256,512]{1,0:T(8,128)(2,1)S(1)} %get-tuple-element.79), channel_id=1, source_target_pairs={{0,2},{2,0},{4,6},{6,4},{8,10},{10,8},{12,14},{14,12},{16,18},{18,... | collective-permute-start | bytes 786440 | tf_op jit(solution)/shard_map/ppermute | solution.py:472
  47.4 13.9 %collective-permute-start.17 = (bf16[256,512]{1,0:T(8,128)(2,1)S(1)}, bf16[256,512]{1,0:T(8,128)(2,1)S(1)}, u32[]{:S(2)}, u32[]{:S(2)}) collective-permute-start(bf16[256,512]{1,0:T(8,128)(2,1)S(1)} %get-tuple-element.80), channel_id=1, source_target_pairs={{0,4},{2,6},{4,0},{6,2},{8,12},{10,14},{12,8},{14,10},{16,20},{18,... | collective-permute-start | bytes 786440 | tf_op jit(solution)/shard_map/ppermute | solution.py:472
  48.0 13.3 %collective-permute-start.18 = (bf16[256,512]{1,0:T(8,128)(2,1)S(1)}, bf16[256,512]{1,0:T(8,128)(2,1)S(1)}, u32[]{:S(2)}, u32[]{:S(2)}) collective-permute-start(bf16[256,512]{1,0:T(8,128)(2,1)S(1)} %get-tuple-element.81), channel_id=1, source_target_pairs={{0,6},{2,4},{4,2},{6,0},{8,14},{10,12},{12,10},{14,8},{16,22},{18,... | collective-permute-start | bytes 786440 | tf_op jit(solution)/shard_map/ppermute | solution.py:472
  50.4 15.5 %collective-permute-start.23 = (bf16[128,512]{1,0:T(8,128)(2,1)S(1)}, bf16[128,512]{1,0:T(8,128)(2,1)S(1)}, u32[]{:S(2)}, u32[]{:S(2)}) collective-permute-start(bf16[128,512]{1,0:T(8,128)(2,1)S(1)} %copy-done.1), channel_id=1, source_target_pairs={{0,16},{2,18},{4,20},{6,22},{8,24},{10,26},{12,28},{14,30},{16,0},... | collective-permute-start | bytes 393224 | tf_op jit(solution)/shard_map/ppermute | solution.py:472
  51.0 14.9 %collective-permute-start.22 = (bf16[128,512]{1,0:T(8,128)(2,1)S(1)}, bf16[128,512]{1,0:T(8,128)(2,1)S(1)}, u32[]{:S(2)}, u32[]{:S(2)}) collective-permute-start(bf16[128,512]{1,0:T(8,128)(2,1)S(1)} %copy-done.1), channel_id=1, source_target_pairs={{0,8},{2,10},{4,12},{6,14},{8,0},{10,2},{12,4},{14,6},{16,24},{18,... | collective-permute-start | bytes 393224 | tf_op jit(solution)/shard_map/ppermute | solution.py:472
  61.4 9.4 %collective-permute-start.19 = (bf16[64,512]{1,0:T(8,128)(2,1)S(1)}, bf16[64,512]{1,0:T(8,128)(2,1)S(1)}, u32[]{:S(2)}, u32[]{:S(2)}) collective-permute-start(bf16[64,512]{1,0:T(8,128)(2,1)S(1)} %get-tuple-element.83.refs_2_), channel_id=1, source_target_pairs={{0,8},{2,10},{4,12},{6,14},{8,0},{10,2},{12,4},{14,6},{16,24},{18,... | collective-permute-start | bytes 196616 | tf_op jit(solution)/shard_map/ppermute | solution.py:472
  62.1 8.7 %collective-permute-start.20 = (bf16[64,512]{1,0:T(8,128)(2,1)S(1)}, bf16[64,512]{1,0:T(8,128)(2,1)S(1)}, u32[]{:S(2)}, u32[]{:S(2)}) collective-permute-start(bf16[64,512]{1,0:T(8,128)(2,1)S(1)} %get-tuple-element.84.refs_3_), channel_id=1, source_target_pairs={{0,16},{2,18},{4,20},{6,22},{8,24},{10,26},{12,28},{14,30},{16,0},... | collective-permute-start | bytes 196616 | tf_op jit(solution)/shard_map/ppermute | solution.py:472
  64.5 7.9 %collective-permute-start.21 = (bf16[64,512]{1,0:T(8,128)(2,1)S(1)}, bf16[64,512]{1,0:T(8,128)(2,1)S(1)}, u32[]{:S(2)}, u32[]{:S(2)}) collective-permute-start(bf16[64,512]{1,0:T(8,128)(2,1)S(1)} %get-tuple-element.85.refs_4_), channel_id=1, source_target_pairs={{0,24},{2,26},{4,28},{6,30},{8,16},{10,18},{12,20},{14,22},{16,8},... | collective-permute-start | bytes 196616 | tf_op jit(solution)/shard_map/ppermute | solution.py:472
  65.9 6.9 %collective-permute-start.25 = (bf16[128,512]{1,0:T(8,128)(2,1)S(1)}, bf16[128,512]{1,0:T(8,128)(2,1)S(1)}, u32[]{:S(2)}, u32[]{:S(2)}) collective-permute-start(bf16[128,512]{1,0:T(8,128)(2,1)S(1)} %collective-permute-done.23.refs_6_.refs_2_), channel_id=1, source_target_pairs={{0,8},{2,10},{4,12},{6,14},{8,0},{10,2},{12,4},{14,6},{16,24},{18,... | collective-permute-start | bytes 393224 | tf_op jit(solution)/shard_map/ppermute | solution.py:472
  74.5 7.6 %collective-permute-start.26 = (bf16[32,2944]{1,0:T(8,128)(2,1)S(1)}, bf16[32,2944]{1,0:T(8,128)(2,1)S(1)}, u32[]{:S(2)}, u32[]{:S(2)}) collective-permute-start(bf16[32,2944]{1,0:T(8,128)(2,1)S(1)} %get-tuple-element.96), channel_id=1, source_target_pairs={{0,2},{2,0},{4,6},{6,4},{8,10},{10,8},{12,14},{14,12},{16,18},{18,... | collective-permute-start | bytes 565256 | tf_op jit(solution)/shard_map/ppermute | solution.py:472
  75.9 11.3 %collective-permute-start.27 = (bf16[32,2944]{1,0:T(8,128)(2,1)S(1)}, bf16[32,2944]{1,0:T(8,128)(2,1)S(1)}, u32[]{:S(2)}, u32[]{:S(2)}) collective-permute-start(bf16[32,2944]{1,0:T(8,128)(2,1)S(1)} %get-tuple-element.97), channel_id=1, source_target_pairs={{0,4},{2,6},{4,0},{6,2},{8,12},{10,14},{12,8},{14,10},{16,20},{18,... | collective-permute-start | bytes 565256 | tf_op jit(solution)/shard_map/ppermute | solution.py:472
  78.4 8.8 %collective-permute-start.28 = (bf16[32,2944]{1,0:T(8,128)(2,1)S(1)}, bf16[32,2944]{1,0:T(8,128)(2,1)S(1)}, u32[]{:S(2)}, u32[]{:S(2)}) collective-permute-start(bf16[32,2944]{1,0:T(8,128)(2,1)S(1)} %get-tuple-element.98), channel_id=1, source_target_pairs={{0,6},{2,4},{4,2},{6,0},{8,14},{10,12},{12,10},{14,8},{16,22},{18,... | collective-permute-start | bytes 565256 | tf_op jit(solution)/shard_map/ppermute | solution.py:472
  (14 other events, 102.0 us)
Sparse Core Ops, SparseCore 0:
  13.4 55.6 all-gather.1

commit v23 on v20

--- a/solution.py
+++ b/solution.py
@@ -503,8 +503,8 @@
     parts = to_plane(sums)
     kv_rows = [kv_own, to_expert(kv_own, PLANE), to_expert(kv_own, 2 * PLANE)]
     parts = plane_sum(parts, depth)
-    kv_rows.append(to_expert(kv_rows[2], PLANE))
-    (q_rows,) = load((q_rows,), (*parts, *kv_rows[1:3]))
+    kv_rows.append(to_expert(kv_own, 3 * PLANE))
+    (q_rows,) = load((q_rows,), (*parts, *kv_rows[1:]))
     parts = to_z(parts)
     *parts, q_rows = lax.optimization_barrier((*parts, q_rows))
     scaled, following = second_norm(parts, input_gain[None, :])

time: 94.5 us -> 99.6 us (1.054)
  starting transfers between devices: 28.3 us -> 31 us
  waiting for transfers between devices: 33.2 us -> 35.6 us
    ppermute x19, waiting for transfers between devices: 26.9 us -> 32 us  [to_expert(): lax.ppermute(value, 'expert', [(i, i ^ offset) for i in range(n_expert)])]
    all_gather x1, waiting for transfers between devices: 3.05 us -> 0.11 us  [per_device_dense(): lax.all_gather(q_own, 'expert', axis=0, tiled=True, axis_index_groups=lines)]
    ppermute x19, starting transfers between devices: 26.3 us -> 29 us  [to_expert(): lax.ppermute(value, 'expert', [(i, i ^ offset) for i in range(n_expert)])]
  transfers between devices with their start and end apart: 30 -> 30, of which waited for: 17 -> 19; matrix products, arithmetic and copies ran while one was open for 1% -> 1% of each run, Pallas kernels for 13% -> 12%
where the time goes in v23:
time: 99.6 us; the launch traced here: 99.4 us
  waiting for transfers between devices  35.6 us (36%)
  starting transfers between devices  31 us (31%)
  Pallas kernels  18 us (18%)
  between operations  14.2 us (14%)
    ppermute x19, waiting for transfers between devices, to_expert(): lax.ppermute(value, 'expert', [(i, i ^ offset) for i in range(n_expert)])  32 us
    ppermute x19, starting transfers between devices, to_expert(): lax.ppermute(value, 'expert', [(i, i ^ offset) for i in range(n_expert)])  29 us
    pallas_call x2, Pallas kernels, experts(): pl.pallas_call(functools.partial(expert_kernel, depth, chunk, len(blocks)...  6.05 us
    pallas_call x2, Pallas kernels, load(): pl.pallas_call(functools.partial(load_kernel, count), out_shape=tuple((pl...  5.45 us
    pallas_call x1, Pallas kernels, out_projection(): pl.pallas_call(functools.partial(out_projection_kernel, chunk), out_shape...  4.38 us
    ppermute x10, waiting for transfers between devices, to_core(): return lax.ppermute(value, 'tensor', [(0, 1), (1, 0)])  3.51 us
    ppermute x10, starting transfers between devices, to_core(): return lax.ppermute(value, 'tensor', [(0, 1), (1, 0)])  1.99 us
  transfers between devices with their start and end apart: 30, of which 19 were waited for; matrix products, arithmetic and copies ran while one was open for 1% of the time, Pallas kernels for 12%

profile of v23, /device:TPU:0, one launch (start us, length us, event | category | flops | bytes accessed | tf_op | source)
XLA Modules:
  0.0 99.4 jit_solution(13488676855941270533)
XLA Ops:
  7.3 4.4 %out_projection.1 = (f32[16,2048]{1,0:T(8,128)S(1)}, f32[16,2048]{1,0:T(8,128)S(1)}) custom-call(bf16[32,2048]{1,0:T(8,128)(2,1)} %a_hbm.1, bf16[2048,2048]{1,0:T(8,128)(2,1)} %w_hbm.1), custom_call_target="tpu_custom_call" | custom-call | tf_op jit(solution)/shard_map/out_projection/pallas_call | solution.py:77
  13.3 3.0 %collective-permute-start.1 = (bf16[16,2176]{1,0:T(8,128)(2,1)S(1)}, bf16[16,2176]{1,0:T(8,128)(2,1)S(1)}, u32[]{:S(2)}, u32[]{:S(2)}) collective-permute-start(bf16[16,2176]{1,0:T(8,128)(2,1)S(1)} %get-tuple-element.59.refs_3_.refs_0_), channel_id=1, source_target_pairs={{0,8},{2,10},{4,12},{6,14},{8,0},{10,2},{12,4},{14,6},{16,24},{18,... | collective-permute-start | bytes 208904 | tf_op jit(solution)/shard_map/ppermute | solution.py:468
  16.3 2.6 %collective-permute-start.2 = (bf16[16,2176]{1,0:T(8,128)(2,1)S(1)}, bf16[16,2176]{1,0:T(8,128)(2,1)S(1)}, u32[]{:S(2)}, u32[]{:S(2)}) collective-permute-start(bf16[16,2176]{1,0:T(8,128)(2,1)S(1)} %get-tuple-element.59.refs_3_.refs_0_), channel_id=1, source_target_pairs={{0,16},{2,18},{4,20},{6,22},{8,24},{10,26},{12,28},{14,30},{16,0},... | collective-permute-start | bytes 208904 | tf_op jit(solution)/shard_map/ppermute | solution.py:468
  18.9 3.8 %load_weights.2 = (bf16[1,2048,768]{2,1,0:T(8,128)(2,1)S(1)}, bf16[1,2048,768]{2,1,0:T(8,128)(2,1)S(1)}, bf16[1,768,2048]{2,1,0:T(8,128)(2,1)S(1)}) custom-call(bf16[1,2048,768]{2,1,0:T(8,128)(2,1)} %refs_0_.1, bf16[1,2048,768]{2,1,0:T(8,128)(2,1)} %refs_1_.1, bf16[1,768,2048]{2,1,0:T(8,128)(2,1)} %refs_2_.1, ...), custom_call_target="tpu_custom_call" | custom-call | tf_op jit(solution)/shard_map/load_weights/pallas_call | solution.py:153
  25.1 1.6 %collective-permute-start.4 = (bf16[64,2176]{1,0:T(8,128)(2,1)S(1)}, bf16[64,2176]{1,0:T(8,128)(2,1)S(1)}, u32[]{:S(2)}, u32[]{:S(2)}) collective-permute-start(bf16[64,2176]{1,0:T(8,128)(2,1)S(1)} %pack_tokens.1.refs_0_), channel_id=1, source_target_pairs={{0,2},{2,0},{4,6},{6,4},{8,10},{10,8},{12,14},{14,12},{16,18},{18,... | collective-permute-start | bytes 835592 | tf_op jit(solution)/shard_map/ppermute | solution.py:468
  26.7 1.5 %collective-permute-start.5 = (bf16[64,2176]{1,0:T(8,128)(2,1)S(1)}, bf16[64,2176]{1,0:T(8,128)(2,1)S(1)}, u32[]{:S(2)}, u32[]{:S(2)}) collective-permute-start(bf16[64,2176]{1,0:T(8,128)(2,1)S(1)} %pack_tokens.1.refs_0_), channel_id=1, source_target_pairs={{0,4},{2,6},{4,0},{6,2},{8,12},{10,14},{12,8},{14,10},{16,20},{18,... | collective-permute-start | bytes 835592 | tf_op jit(solution)/shard_map/ppermute | solution.py:468
  28.2 3.9 %collective-permute-done.4.refs_1_ = bf16[64,2176]{1,0:T(8,128)(2,1)S(1)} collective-permute-done((bf16[64,2176]{1,0:T(8,128)(2,1)S(1)}, bf16[64,2176]{1,0:T(8,128)(2,1)S(1)}, u32[]{:S(2)}, u32[]{:S(2)}) %collective-permute-start.4) | collective-permute-done | bytes 278560 | tf_op jit(solution)/shard_map/ppermute | solution.py:468
  33.3 1.6 %collective-permute-start.9 = (bf16[32,2176]{1,0:T(8,128)(2,1)S(1)}, bf16[32,2176]{1,0:T(8,128)(2,1)S(1)}, u32[]{:S(2)}, u32[]{:S(2)}) collective-permute-start(bf16[32,2176]{1,0:T(8,128)(2,1)S(1)} %slice.8), channel_id=1, source_target_pairs={{0,4},{2,6},{4,0},{6,2},{8,12},{10,14},{12,8},{14,10},{16,20},{18,... | collective-permute-start | bytes 417800 | tf_op jit(solution)/shard_map/ppermute | solution.py:468
  35.8 4.0 %experts.2 = (bf16[192,2048]{1,0:T(8,128)(2,1)S(1)}, bf16[96,2048]{1,0:T(8,128)(2,1)S(1)}, bf16[96,2048]{1,0:T(8,128)(2,1)S(1)}) custom-call(bf16[64,2176]{1,0:T(8,128)(2,1)S(1)} %pack_tokens.1.refs_0_, bf16[64,2176]{1,0:T(8,128)(2,1)S(1)} %collective-permute-done.4.refs_1_, bf16[64,2176]{1,0:T(8,128)(2,1)S(1)} %collective-permute-done.5.refs_2_, ...), custom_call_target="tpu_custom_call" | custom-call | flops 3623878656 | tf_op jit(solution)/shard_map/experts/pallas_call | solution.py:213
  42.4 2.0 %experts.3 = (bf16[64,2048]{1,0:T(8,128)(2,1)S(1)}, bf16[64,2048]{1,0:T(8,128)(2,1)S(1)}) custom-call(bf16[32,2176]{1,0:T(8,128)(2,1)S(1)} %collective-permute-done.9.refs_0_, bf16[32,2176]{1,0:T(8,128)(2,1)S(1)} %collective-permute-done.10.refs_1_, bf16[32,2176]{1,0:T(8,128)(2,1)S(1)} %collective-permute-done.11.refs_2_, ...), custom_call_target="tpu_custom_call" | custom-call | flops 1207959552 | tf_op jit(solution)/shard_map/experts/pallas_call | solution.py:213
  47.4 2.4 %collective-permute-start.18 = (bf16[256,512]{1,0:T(8,128)(2,1)S(1)}, bf16[256,512]{1,0:T(8,128)(2,1)S(1)}, u32[]{:S(2)}, u32[]{:S(2)}) collective-permute-start(bf16[256,512]{1,0:T(8,128)(2,1)S(1)} %get-tuple-element.81), channel_id=1, source_target_pairs={{0,6},{2,4},{4,2},{6,0},{8,14},{10,12},{12,10},{14,8},{16,22},{18,... | collective-permute-start | bytes 786440 | tf_op jit(solution)/shard_map/ppermute | solution.py:468
  49.8 1.6 %collective-permute-start.22 = (bf16[128,512]{1,0:T(8,128)(2,1)S(1)}, bf16[128,512]{1,0:T(8,128)(2,1)S(1)}, u32[]{:S(2)}, u32[]{:S(2)}) collective-permute-start(bf16[128,512]{1,0:T(8,128)(2,1)S(1)} %copy-done.1), channel_id=1, source_target_pairs={{0,8},{2,10},{4,12},{6,14},{8,0},{10,2},{12,4},{14,6},{16,24},{18,... | collective-permute-start | bytes 393224 | tf_op jit(solution)/shard_map/ppermute | solution.py:468
  52.8 2.7 %collective-permute-done.16.refs_1_ = bf16[256,512]{1,0:T(8,128)(2,1)S(1)} collective-permute-done((bf16[256,512]{1,0:T(8,128)(2,1)S(1)}, bf16[256,512]{1,0:T(8,128)(2,1)S(1)}, u32[]{:S(2)}, u32[]{:S(2)}) %collective-permute-start.16) | collective-permute-done | bytes 262176 | tf_op jit(solution)/shard_map/ppermute | solution.py:468
  55.4 2.4 %collective-permute-start.24 = (bf16[128,512]{1,0:T(8,128)(2,1)S(1)}, bf16[128,512]{1,0:T(8,128)(2,1)S(1)}, u32[]{:S(2)}, u32[]{:S(2)}) collective-permute-start(bf16[128,512]{1,0:T(8,128)(2,1)S(1)} %copy-done.1), channel_id=1, source_target_pairs={{0,24},{2,26},{4,28},{6,30},{8,16},{10,18},{12,20},{14,22},{16,8},... | collective-permute-start | bytes 393224 | tf_op jit(solution)/shard_map/ppermute | solution.py:468
  57.8 2.9 %collective-permute-done.17.refs_2_ = bf16[256,512]{1,0:T(8,128)(2,1)S(1)} collective-permute-done((bf16[256,512]{1,0:T(8,128)(2,1)S(1)}, bf16[256,512]{1,0:T(8,128)(2,1)S(1)}, u32[]{:S(2)}, u32[]{:S(2)}) %collective-permute-start.17) | collective-permute-done | bytes 262176 | tf_op jit(solution)/shard_map/ppermute | solution.py:468
  60.8 1.6 %collective-permute-start.19 = (bf16[64,512]{1,0:T(8,128)(2,1)S(1)}, bf16[64,512]{1,0:T(8,128)(2,1)S(1)}, u32[]{:S(2)}, u32[]{:S(2)}) collective-permute-start(bf16[64,512]{1,0:T(8,128)(2,1)S(1)} %get-tuple-element.83.refs_2_), channel_id=1, source_target_pairs={{0,8},{2,10},{4,12},{6,14},{8,0},{10,2},{12,4},{14,6},{16,24},{18,... | collective-permute-start | bytes 196616 | tf_op jit(solution)/shard_map/ppermute | solution.py:468
  64.9 2.3 %collective-permute-start.21 = (bf16[64,512]{1,0:T(8,128)(2,1)S(1)}, bf16[64,512]{1,0:T(8,128)(2,1)S(1)}, u32[]{:S(2)}, u32[]{:S(2)}) collective-permute-start(bf16[64,512]{1,0:T(8,128)(2,1)S(1)} %get-tuple-element.85.refs_4_), channel_id=1, source_target_pairs={{0,24},{2,26},{4,28},{6,30},{8,16},{10,18},{12,20},{14,22},{16,8},... | collective-permute-start | bytes 196616 | tf_op jit(solution)/shard_map/ppermute | solution.py:468
  67.2 1.5 %collective-permute-done.23.refs_6_.refs_2_ = bf16[128,512]{1,0:T(8,128)(2,1)S(1)} collective-permute-done((bf16[128,512]{1,0:T(8,128)(2,1)S(1)}, bf16[128,512]{1,0:T(8,128)(2,1)S(1)}, u32[]{:S(2)}, u32[]{:S(2)}) %collective-permute-start.23) | collective-permute-done | bytes 131104 | tf_op jit(solution)/shard_map/ppermute | solution.py:468
  68.8 2.2 %collective-permute-done.24.refs_7_.refs_3_ = bf16[128,512]{1,0:T(8,128)(2,1)S(1)} collective-permute-done((bf16[128,512]{1,0:T(8,128)(2,1)S(1)}, bf16[128,512]{1,0:T(8,128)(2,1)S(1)}, u32[]{:S(2)}, u32[]{:S(2)}) %collective-permute-start.24) | collective-permute-done | bytes 131104 | tf_op jit(solution)/shard_map/ppermute | solution.py:468
  71.1 1.6 %load_weights.3.q_ref = bf16[512,2048]{1,0:T(8,128)(2,1)S(1)} custom-call(bf16[512,2048]{1,0:T(8,128)(2,1)} %all-gather.2.cloned.1.call-done.refs_0_, bf16[64,512]{1,0:T(8,128)(2,1)S(1)} %get-tuple-element.88.refs_1_.refs_0_, bf16[64,512]{1,0:T(8,128)(2,1)S(1)} %get-tuple-element.83.refs_2_, bf16[64,512]{1,0:T(8,128)(2,1)S(1)} %get-tuple-element.84.refs_3_, ...), custom_call_target="tpu_custom_call" | custom-call | tf_op jit(solution)/shard_map/load_weights/pallas_call | solution.py:153
  72.8 4.6 %collective-permute-done.20.refs_2_ = bf16[64,512]{1,0:T(8,128)(2,1)S(1)} collective-permute-done((bf16[64,512]{1,0:T(8,128)(2,1)S(1)}, bf16[64,512]{1,0:T(8,128)(2,1)S(1)}, u32[]{:S(2)}, u32[]{:S(2)}) %collective-permute-start.20) | collective-permute-done | bytes 65568 | tf_op jit(solution)/shard_map/ppermute | solution.py:468
  79.4 1.7 %collective-permute-start.26 = (bf16[32,2944]{1,0:T(8,128)(2,1)S(1)}, bf16[32,2944]{1,0:T(8,128)(2,1)S(1)}, u32[]{:S(2)}, u32[]{:S(2)}) collective-permute-start(bf16[32,2944]{1,0:T(8,128)(2,1)S(1)} %get-tuple-element.96), channel_id=1, source_target_pairs={{0,2},{2,0},{4,6},{6,4},{8,10},{10,8},{12,14},{14,12},{16,18},{18,... | collective-permute-start | bytes 565256 | tf_op jit(solution)/shard_map/ppermute | solution.py:468
  82.9 4.1 %collective-permute-done.26.refs_1_ = bf16[32,2944]{1,0:T(8,128)(2,1)S(1)} collective-permute-done((bf16[32,2944]{1,0:T(8,128)(2,1)S(1)}, bf16[32,2944]{1,0:T(8,128)(2,1)S(1)}, u32[]{:S(2)}, u32[]{:S(2)}) %collective-permute-start.26) | collective-permute-done | bytes 188448 | tf_op jit(solution)/shard_map/ppermute | solution.py:468
  87.0 4.6 %collective-permute-done.27.refs_2_ = bf16[32,2944]{1,0:T(8,128)(2,1)S(1)} collective-permute-done((bf16[32,2944]{1,0:T(8,128)(2,1)S(1)}, bf16[32,2944]{1,0:T(8,128)(2,1)S(1)}, u32[]{:S(2)}, u32[]{:S(2)}) %collective-permute-start.27) | collective-permute-done | bytes 188448 | tf_op jit(solution)/shard_map/ppermute | solution.py:468
  (74 shorter events, 20.5 us)
Async XLA Ops:
  7.2 63.9 %all-gather.2.cloned.1.call-start = ((), (), s32[]{:S(2)}) async-start(), calls=%async_computation | async-start | bytes 2621440 | tf_op jit(solution)/shard_map/all_gather | solution.py:487
  13.3 9.4 %collective-permute-start.1 = (bf16[16,2176]{1,0:T(8,128)(2,1)S(1)}, bf16[16,2176]{1,0:T(8,128)(2,1)S(1)}, u32[]{:S(2)}, u32[]{:S(2)}) collective-permute-start(bf16[16,2176]{1,0:T(8,128)(2,1)S(1)} %get-tuple-element.59.refs_3_.refs_0_), channel_id=1, source_target_pairs={{0,8},{2,10},{4,12},{6,14},{8,0},{10,2},{12,4},{14,6},{16,24},{18,... | collective-permute-start | bytes 208904 | tf_op jit(solution)/shard_map/ppermute | solution.py:468
  16.3 7.8 %collective-permute-start.2 = (bf16[16,2176]{1,0:T(8,128)(2,1)S(1)}, bf16[16,2176]{1,0:T(8,128)(2,1)S(1)}, u32[]{:S(2)}, u32[]{:S(2)}) collective-permute-start(bf16[16,2176]{1,0:T(8,128)(2,1)S(1)} %get-tuple-element.59.refs_3_.refs_0_), channel_id=1, source_target_pairs={{0,16},{2,18},{4,20},{6,22},{8,24},{10,26},{12,28},{14,30},{16,0},... | collective-permute-start | bytes 208904 | tf_op jit(solution)/shard_map/ppermute | solution.py:468
  18.9 6.2 %collective-permute-start.3 = (bf16[16,2176]{1,0:T(8,128)(2,1)S(1)}, bf16[16,2176]{1,0:T(8,128)(2,1)S(1)}, u32[]{:S(2)}, u32[]{:S(2)}) collective-permute-start(bf16[16,2176]{1,0:T(8,128)(2,1)S(1)} %get-tuple-element.59.refs_3_.refs_0_), channel_id=1, source_target_pairs={{0,24},{2,26},{4,28},{6,30},{8,16},{10,18},{12,20},{14,22},{16,8},... | collective-permute-start | bytes 208904 | tf_op jit(solution)/shard_map/ppermute | solution.py:468
  25.1 7.0 %collective-permute-start.4 = (bf16[64,2176]{1,0:T(8,128)(2,1)S(1)}, bf16[64,2176]{1,0:T(8,128)(2,1)S(1)}, u32[]{:S(2)}, u32[]{:S(2)}) collective-permute-start(bf16[64,2176]{1,0:T(8,128)(2,1)S(1)} %pack_tokens.1.refs_0_), channel_id=1, source_target_pairs={{0,2},{2,0},{4,6},{6,4},{8,10},{10,8},{12,14},{14,12},{16,18},{18,... | collective-permute-start | bytes 835592 | tf_op jit(solution)/shard_map/ppermute | solution.py:468
  26.7 6.6 %collective-permute-start.5 = (bf16[64,2176]{1,0:T(8,128)(2,1)S(1)}, bf16[64,2176]{1,0:T(8,128)(2,1)S(1)}, u32[]{:S(2)}, u32[]{:S(2)}) collective-permute-start(bf16[64,2176]{1,0:T(8,128)(2,1)S(1)} %pack_tokens.1.refs_0_), channel_id=1, source_target_pairs={{0,4},{2,6},{4,0},{6,2},{8,12},{10,14},{12,8},{14,10},{16,20},{18,... | collective-permute-start | bytes 835592 | tf_op jit(solution)/shard_map/ppermute | solution.py:468
  28.2 7.6 %collective-permute-start.6 = (bf16[64,2176]{1,0:T(8,128)(2,1)S(1)}, bf16[64,2176]{1,0:T(8,128)(2,1)S(1)}, u32[]{:S(2)}, u32[]{:S(2)}) collective-permute-start(bf16[64,2176]{1,0:T(8,128)(2,1)S(1)} %pack_tokens.1.refs_0_), channel_id=1, source_target_pairs={{0,1},{1,0},{2,3},{3,2},{4,5},{5,4},{6,7},{7,6},{8,9},{9,8},{10,11... | collective-permute-start | bytes 835592 | tf_op jit(solution)/shard_map/ppermute | solution.py:465
  32.1 3.7 %collective-permute-start.7 = (bf16[64,2176]{1,0:T(8,128)(2,1)S(1)}, bf16[64,2176]{1,0:T(8,128)(2,1)S(1)}, u32[]{:S(2)}, u32[]{:S(2)}) collective-permute-start(bf16[64,2176]{1,0:T(8,128)(2,1)S(1)} %collective-permute-done.4.refs_1_), channel_id=1, source_target_pairs={{0,1},{1,0},{2,3},{3,2},{4,5},{5,4},{6,7},{7,6},{8,9},{9,8},{10,11... | collective-permute-start | bytes 835592 | tf_op jit(solution)/shard_map/ppermute | solution.py:465
  33.3 6.5 %collective-permute-start.9 = (bf16[32,2176]{1,0:T(8,128)(2,1)S(1)}, bf16[32,2176]{1,0:T(8,128)(2,1)S(1)}, u32[]{:S(2)}, u32[]{:S(2)}) collective-permute-start(bf16[32,2176]{1,0:T(8,128)(2,1)S(1)} %slice.8), channel_id=1, source_target_pairs={{0,4},{2,6},{4,0},{6,2},{8,12},{10,14},{12,8},{14,10},{16,20},{18,... | collective-permute-start | bytes 417800 | tf_op jit(solution)/shard_map/ppermute | solution.py:468
  34.9 5.9 %collective-permute-start.10 = (bf16[32,2176]{1,0:T(8,128)(2,1)S(1)}, bf16[32,2176]{1,0:T(8,128)(2,1)S(1)}, u32[]{:S(2)}, u32[]{:S(2)}) collective-permute-start(bf16[32,2176]{1,0:T(8,128)(2,1)S(1)} %slice.9), channel_id=1, source_target_pairs={{0,2},{2,0},{4,6},{6,4},{8,10},{10,8},{12,14},{14,12},{16,18},{18,... | collective-permute-start | bytes 417800 | tf_op jit(solution)/shard_map/ppermute | solution.py:468
  41.3 3.4 %collective-permute-start.13 = (bf16[96,2048]{1,0:T(8,128)(2,1)S(1)}, bf16[96,2048]{1,0:T(8,128)(2,1)S(1)}, u32[]{:S(2)}, u32[]{:S(2)}) collective-permute-start(bf16[96,2048]{1,0:T(8,128)(2,1)S(1)} %get-tuple-element.71), channel_id=1, source_target_pairs={{0,1},{1,0},{2,3},{3,2},{4,5},{5,4},{6,7},{7,6},{8,9},{9,8},{10,11... | collective-permute-start | bytes 1179656 | tf_op jit(solution)/shard_map/ppermute | solution.py:465
  41.3 3.4 %collective-permute-start.14 = (bf16[96,2048]{1,0:T(8,128)(2,1)S(1)}, bf16[96,2048]{1,0:T(8,128)(2,1)S(1)}, u32[]{:S(2)}, u32[]{:S(2)}) collective-permute-start(bf16[96,2048]{1,0:T(8,128)(2,1)S(1)} %get-tuple-element.72), channel_id=1, source_target_pairs={{0,1},{1,0},{2,3},{3,2},{4,5},{5,4},{6,7},{7,6},{8,9},{9,8},{10,11... | collective-permute-start | bytes 1179656 | tf_op jit(solution)/shard_map/ppermute | solution.py:465
  46.2 9.2 %collective-permute-start.16 = (bf16[256,512]{1,0:T(8,128)(2,1)S(1)}, bf16[256,512]{1,0:T(8,128)(2,1)S(1)}, u32[]{:S(2)}, u32[]{:S(2)}) collective-permute-start(bf16[256,512]{1,0:T(8,128)(2,1)S(1)} %get-tuple-element.79), channel_id=1, source_target_pairs={{0,2},{2,0},{4,6},{6,4},{8,10},{10,8},{12,14},{14,12},{16,18},{18,... | collective-permute-start | bytes 786440 | tf_op jit(solution)/shard_map/ppermute | solution.py:468
  46.8 13.9 %collective-permute-start.17 = (bf16[256,512]{1,0:T(8,128)(2,1)S(1)}, bf16[256,512]{1,0:T(8,128)(2,1)S(1)}, u32[]{:S(2)}, u32[]{:S(2)}) collective-permute-start(bf16[256,512]{1,0:T(8,128)(2,1)S(1)} %get-tuple-element.80), channel_id=1, source_target_pairs={{0,4},{2,6},{4,0},{6,2},{8,12},{10,14},{12,8},{14,10},{16,20},{18,... | collective-permute-start | bytes 786440 | tf_op jit(solution)/shard_map/ppermute | solution.py:468
  47.4 13.3 %collective-permute-start.18 = (bf16[256,512]{1,0:T(8,128)(2,1)S(1)}, bf16[256,512]{1,0:T(8,128)(2,1)S(1)}, u32[]{:S(2)}, u32[]{:S(2)}) collective-permute-start(bf16[256,512]{1,0:T(8,128)(2,1)S(1)} %get-tuple-element.81), channel_id=1, source_target_pairs={{0,6},{2,4},{4,2},{6,0},{8,14},{10,12},{12,10},{14,8},{16,22},{18,... | collective-permute-start | bytes 786440 | tf_op jit(solution)/shard_map/ppermute | solution.py:468
  49.8 15.1 %collective-permute-start.22 = (bf16[128,512]{1,0:T(8,128)(2,1)S(1)}, bf16[128,512]{1,0:T(8,128)(2,1)S(1)}, u32[]{:S(2)}, u32[]{:S(2)}) collective-permute-start(bf16[128,512]{1,0:T(8,128)(2,1)S(1)} %copy-done.1), channel_id=1, source_target_pairs={{0,8},{2,10},{4,12},{6,14},{8,0},{10,2},{12,4},{14,6},{16,24},{18,... | collective-permute-start | bytes 393224 | tf_op jit(solution)/shard_map/ppermute | solution.py:468
  51.4 17.4 %collective-permute-start.23 = (bf16[128,512]{1,0:T(8,128)(2,1)S(1)}, bf16[128,512]{1,0:T(8,128)(2,1)S(1)}, u32[]{:S(2)}, u32[]{:S(2)}) collective-permute-start(bf16[128,512]{1,0:T(8,128)(2,1)S(1)} %copy-done.1), channel_id=1, source_target_pairs={{0,16},{2,18},{4,20},{6,22},{8,24},{10,26},{12,28},{14,30},{16,0},... | collective-permute-start | bytes 393224 | tf_op jit(solution)/shard_map/ppermute | solution.py:468
  55.4 15.6 %collective-permute-start.24 = (bf16[128,512]{1,0:T(8,128)(2,1)S(1)}, bf16[128,512]{1,0:T(8,128)(2,1)S(1)}, u32[]{:S(2)}, u32[]{:S(2)}) collective-permute-start(bf16[128,512]{1,0:T(8,128)(2,1)S(1)} %copy-done.1), channel_id=1, source_target_pairs={{0,24},{2,26},{4,28},{6,30},{8,16},{10,18},{12,20},{14,22},{16,8},... | collective-permute-start | bytes 393224 | tf_op jit(solution)/shard_map/ppermute | solution.py:468
  60.8 11.9 %collective-permute-start.19 = (bf16[64,512]{1,0:T(8,128)(2,1)S(1)}, bf16[64,512]{1,0:T(8,128)(2,1)S(1)}, u32[]{:S(2)}, u32[]{:S(2)}) collective-permute-start(bf16[64,512]{1,0:T(8,128)(2,1)S(1)} %get-tuple-element.83.refs_2_), channel_id=1, source_target_pairs={{0,8},{2,10},{4,12},{6,14},{8,0},{10,2},{12,4},{14,6},{16,24},{18,... | collective-permute-start | bytes 196616 | tf_op jit(solution)/shard_map/ppermute | solution.py:468
  62.5 14.9 %collective-permute-start.20 = (bf16[64,512]{1,0:T(8,128)(2,1)S(1)}, bf16[64,512]{1,0:T(8,128)(2,1)S(1)}, u32[]{:S(2)}, u32[]{:S(2)}) collective-permute-start(bf16[64,512]{1,0:T(8,128)(2,1)S(1)} %get-tuple-element.84.refs_3_), channel_id=1, source_target_pairs={{0,16},{2,18},{4,20},{6,22},{8,24},{10,26},{12,28},{14,30},{16,0},... | collective-permute-start | bytes 196616 | tf_op jit(solution)/shard_map/ppermute | solution.py:468
  64.9 12.4 %collective-permute-start.21 = (bf16[64,512]{1,0:T(8,128)(2,1)S(1)}, bf16[64,512]{1,0:T(8,128)(2,1)S(1)}, u32[]{:S(2)}, u32[]{:S(2)}) collective-permute-start(bf16[64,512]{1,0:T(8,128)(2,1)S(1)} %get-tuple-element.85.refs_4_), channel_id=1, source_target_pairs={{0,24},{2,26},{4,28},{6,30},{8,16},{10,18},{12,20},{14,22},{16,8},... | collective-permute-start | bytes 196616 | tf_op jit(solution)/shard_map/ppermute | solution.py:468
  79.4 7.6 %collective-permute-start.26 = (bf16[32,2944]{1,0:T(8,128)(2,1)S(1)}, bf16[32,2944]{1,0:T(8,128)(2,1)S(1)}, u32[]{:S(2)}, u32[]{:S(2)}) collective-permute-start(bf16[32,2944]{1,0:T(8,128)(2,1)S(1)} %get-tuple-element.96), channel_id=1, source_target_pairs={{0,2},{2,0},{4,6},{6,4},{8,10},{10,8},{12,14},{14,12},{16,18},{18,... | collective-permute-start | bytes 565256 | tf_op jit(solution)/shard_map/ppermute | solution.py:468
  81.1 10.6 %collective-permute-start.27 = (bf16[32,2944]{1,0:T(8,128)(2,1)S(1)}, bf16[32,2944]{1,0:T(8,128)(2,1)S(1)}, u32[]{:S(2)}, u32[]{:S(2)}) collective-permute-start(bf16[32,2944]{1,0:T(8,128)(2,1)S(1)} %get-tuple-element.97), channel_id=1, source_target_pairs={{0,4},{2,6},{4,0},{6,2},{8,12},{10,14},{12,8},{14,10},{16,20},{18,... | collective-permute-start | bytes 565256 | tf_op jit(solution)/shard_map/ppermute | solution.py:468
  82.6 9.0 %collective-permute-start.28 = (bf16[32,2944]{1,0:T(8,128)(2,1)S(1)}, bf16[32,2944]{1,0:T(8,128)(2,1)S(1)}, u32[]{:S(2)}, u32[]{:S(2)}) collective-permute-start(bf16[32,2944]{1,0:T(8,128)(2,1)S(1)} %get-tuple-element.98), channel_id=1, source_target_pairs={{0,6},{2,4},{4,2},{6,0},{8,14},{10,12},{12,10},{14,8},{16,22},{18,... | collective-permute-start | bytes 565256 | tf_op jit(solution)/shard_map/ppermute | solution.py:468
  (14 other events, 112.6 us)
Sparse Core Ops, SparseCore 0:
  13.4 57.6 all-gather.1
